TPU v7x, 32 devices: a whole 2x2x4 slice. The times are simulated.
32 devices in a mesh: grp: 2 (over y), wide: 16 (over z, x, core), narrow: 1.
Axes of the slice: x: 2, y: 2, z: 4, core: 2. Of those that a mesh axis runs over, the one named last changes fastest.
Arguments:
- pairwise_state: bfloat16 [256, 128, 128], P(('grp', 'wide'), 'narrow'), parts along dimension 0, may hold values from -6 to 6
- homolog_features: bfloat16 [128, 128, 256], P('grp', 'wide'), parts along dimension 0, may hold values from -6 to 6
- residue_chain_index: int32 [256], P('grp'), parts along dimension 0, may hold values from 0 to 3, as said below
- resolved_residue_mask: int32 [256], P('grp'), parts along dimension 0, may hold values 0 or 1
- alignment_mask: bfloat16 [128, 128], P('grp', 'wide'), parts along dimension 0, may hold values from 0 to 1
- relative_offset_table: bfloat16 [66, 128], replicated, may hold values from -3 to 3
- homolog_to_sides_matrix: bfloat16 [256, 64], replicated, may hold values from -0.375 to 0.375
- outer_mean_output_weight: bfloat16 [1024, 128], replicated, may hold values from -0.1875 to 0.1875
- triangle_projection_weight: bfloat16 [2, 128, 640], replicated, may hold values from -0.5 to 0.5
- triangle_output_weight: bfloat16 [2, 128, 128], replicated, may hold values from -0.5 to 0.5
Outputs:
- new_pair: bfloat16 [256, 128, 128], P(('grp', 'wide'), 'narrow'), parts along dimension 0
There are 2 independent parts, one for each index of `grp`. A program takes and returns all parts, laid end to end along the dimension named above; an argument that names none is the same for every part. Nothing has to cross between parts.
Inputs may be any that keep to these rules, and one draw needn't show every extreme that they name: `residue_chain_index`: chain numbers never fall along the residues, so each chain is one contiguous run; the first residue is in chain 0 and the last in chain 4 - 1; some chains may be empty.
All inputs are finite; a program needn't handle non-finite values.
Results may differ from a plain program's by a relative error of at most 0.009.
Values may be sent and summed in bfloat16 or wider, within the bound.
No kernel may reach another device: no remote copies, remote signals or barrier semaphores. Data moves between devices by JAX's collectives and lax.ppermute only.
A program may use at most 64 MiB of HBM per device.

v0:
```python
import jax
import jax.numpy as jnp
from jax import lax
from jax.sharding import PartitionSpec as P

RELMAX = 32


EPSILON = 1e-05


def apply_layer_norm(values, axis_dim):
    center = values - jnp.mean(values, axis=axis_dim, keepdims=True)
    spread = jnp.mean(center * center, axis=axis_dim, keepdims=True)
    return center * lax.rsqrt(spread + EPSILON)


def split_into_sheets(flat, per_dev, wide_count, core_count, rows, cols):
    shaped = flat.reshape(per_dev, wide_count, core_count, rows, cols)
    return jnp.transpose(shaped, (0, 1, 3, 2, 4)).reshape(
        per_dev, wide_count * rows, core_count * cols
    )


def triangle(stream, pair_live, proj_weight, out_weight, incoming):
    rows = stream.shape[0]
    cols = stream.shape[1]
    width = out_weight.shape[0]
    wide_count = lax.axis_size("wide")
    core_count = lax.axis_size("narrow")
    normed = apply_layer_norm(stream, 2).astype(jnp.bfloat16)
    blocks = [proj_weight[:, index * width : (index + 1) * width] for index in range(4)]

    def project(block):
        return jnp.einsum("ijd,dc->cij", normed, block, preferred_element_type=jnp.float32)

    left_side = (jax.nn.sigmoid(project(blocks[0])) * project(blocks[1]) * pair_live[None]).astype(
        jnp.bfloat16
    )
    right_side = (jax.nn.sigmoid(project(blocks[2])) * project(blocks[3]) * pair_live[None]).astype(
        jnp.bfloat16
    )
    gate = jax.nn.sigmoid(
        jnp.einsum(
            "ijd,dc->ijc", normed, proj_weight[:, 4 * width :], preferred_element_type=jnp.float32
        )
    )
    form = "cki,ckj->cij" if incoming else "cik,cjk->cij"
    flat_left = left_side.reshape(width, rows * cols)
    flat_right = right_side.reshape(width, rows * cols)
    left_flat, right_flat = (
        lax.all_to_all(flat_left, ("wide", "narrow"), split_axis=0, concat_axis=1, tiled=True),
        lax.all_to_all(flat_right, ("wide", "narrow"), split_axis=0, concat_axis=1, tiled=True),
    )
    per_dev = left_flat.shape[0]
    left_full = split_into_sheets(left_flat, per_dev, wide_count, core_count, rows, cols)
    right_full = split_into_sheets(right_flat, per_dev, wide_count, core_count, rows, cols)
    mixed = jnp.einsum(form, left_full, right_full, preferred_element_type=jnp.float32).astype(
        jnp.bfloat16
    )
    spread_out = mixed.reshape(per_dev, wide_count, rows, core_count, cols)
    spread_out = jnp.transpose(spread_out, (1, 3, 0, 2, 4)).reshape(
        wide_count * core_count * per_dev, rows * cols
    )
    returned = lax.all_to_all(
        spread_out, ("wide", "narrow"), split_axis=0, concat_axis=0, tiled=True
    ).reshape(width, rows, cols)
    blended_standardize = apply_layer_norm(returned.astype(jnp.float32), 0).astype(jnp.bfloat16)
    update = jnp.einsum(
        "cij,cd->ijd", blended_standardize, out_weight, preferred_element_type=jnp.float32
    )
    return stream + gate * update


def per_device(
    pairwise_state,
    homolog_features,
    residue_chain_index,
    resolved_residue_mask,
    alignment_mask,
    relative_offset_table,
    homolog_to_sides_matrix,
    outer_mean_output_weight,
    triangle_projection_weight,
    triangle_output_weight,
):
    rows = pairwise_state.shape[0]
    cols = pairwise_state.shape[1]
    row_start = lax.axis_index("wide") * rows
    col_start = lax.axis_index("narrow") * cols
    residue_present = resolved_residue_mask.astype(jnp.float32)
    row_present = lax.dynamic_slice_in_dim(residue_present, row_start, rows)
    col_live = lax.dynamic_slice_in_dim(residue_present, col_start, cols)
    present_flags = alignment_mask.astype(jnp.float32) * row_present[None, :]
    alignment_normed = apply_layer_norm(homolog_features.astype(jnp.float32), 2).astype(
        jnp.bfloat16
    )
    projected_rows = jnp.einsum(
        "tna,ak->tnk", alignment_normed, homolog_to_sides_matrix, preferred_element_type=jnp.float32
    )
    projected_rows = (projected_rows * present_flags[:, :, None]).astype(jnp.bfloat16)
    half_width = projected_rows.shape[2] // 2
    left_proj = projected_rows[:, :, :half_width]
    right_proj = projected_rows[:, :, half_width:]
    live_flags = present_flags.astype(jnp.bfloat16)
    right_all, live_all = (
        lax.all_gather(right_proj, "wide", axis=1, tiled=True),
        lax.all_gather(live_flags, "wide", axis=1, tiled=True),
    )
    right_mine = lax.dynamic_slice_in_dim(right_all, col_start, cols, 1)
    live_mine = lax.dynamic_slice_in_dim(live_all, col_start, cols, 1)
    counts = jnp.dot(live_flags.T, live_mine, preferred_element_type=jnp.float32)

    def opm_row(left_row):
        outer = jnp.einsum("sc,sjd->jcd", left_row, right_mine, preferred_element_type=jnp.float32)
        outer = outer.reshape(cols, half_width * half_width).astype(jnp.bfloat16)
        return jnp.dot(outer, outer_mean_output_weight, preferred_element_type=jnp.float32)

    opm = lax.map(opm_row, jnp.transpose(left_proj, (1, 0, 2)))
    row_pos = row_start + jnp.arange(rows, dtype=jnp.int32)
    col_pos = col_start + jnp.arange(cols, dtype=jnp.int32)
    row_chain = lax.dynamic_slice_in_dim(residue_chain_index, row_start, rows)
    col_chain = lax.dynamic_slice_in_dim(residue_chain_index, col_start, cols)
    offset = jnp.clip(row_pos[:, None] - col_pos[None, :], -RELMAX, RELMAX) + RELMAX
    bin_index = jnp.where(row_chain[:, None] == col_chain[None, :], offset, 2 * RELMAX + 1)
    bin_count = relative_offset_table.shape[0]
    one_hot = (
        bin_index[:, :, None] == jnp.arange(bin_count, dtype=jnp.int32)[None, None, :]
    ).astype(jnp.bfloat16)
    relpos = jnp.einsum(
        "ijb,bc->ijc", one_hot, relative_offset_table, preferred_element_type=jnp.float32
    )
    stream = (
        pairwise_state.astype(jnp.float32) + relpos + opm / jnp.maximum(counts, 1.0)[:, :, None]
    )
    pair_live = row_present[:, None] * col_live[None, :]
    for turn_index in range(2):
        stream = triangle(
            stream,
            pair_live,
            triangle_projection_weight[turn_index],
            triangle_output_weight[turn_index],
            turn_index == 1,
        )
    return stream.astype(jnp.bfloat16)


def solution(mesh):
    return jax.shard_map(
        per_device,
        mesh=mesh,
        in_specs=(
            P(("grp", "wide"), "narrow", None),
            P("grp", "wide", None),
            P("grp"),
            P("grp"),
            P("grp", "wide"),
            P(),
            P(),
            P(),
            P(),
            P(),
        ),
        out_specs=P(("grp", "wide"), "narrow", None),
        check_vma=False,
    )
```

profile of v0, /device:TPU:0, one launch (start us, length us, event | category | flops | bytes accessed | tf_op | source)
XLA Modules:
  0.0 160.9 jit_solution(3228646192383259307)
XLA Ops:
  0.0 0.7 convert_element_type.114
  0.8 0.8 fusion.68
  1.7 1.1 convert_reduce_fusion.2
  2.8 1.2 fusion.52
  4.0 1.3 fusion.41
  5.4 32.3 %all_gather.6 = bf16[64,128,32]{2,1,0:T(8,128)(2,1)S(1)} all-gather(bf16[64,8,32]{2,1,0:T(8,128)(2,1)S(1)} %get-tuple-element.55), channel_id=1, replica_groups=mesh['grp'=2,'wide'=16,'narrow'=1] {'wide'}, dimensions={1}, use_global_device_ids=true | all-gather | bytes 557056 | tf_op jit(solution)/shard_map/all_gather | solution.py:107
  37.7 1.1 copy.48
  39.0 9.9 %while.10 = (s32[]{:T(128)}, f32[8,128,128]{1,2,0:T(8,128)}, bf16[8,64,32]{1,2,0:T(8,128)(2,1)S(1)}, bf16[64,128,32]{1,0,2:T(8,128)(2,1)S(1)}, bf16[1024,128]{1,0:T(8,128)(2,1)S(1)}, /*index=5*/s32[]{:T(128)}) while((s32[]{:T(128)}, f32[8,128,128]{1,2,0:T(8,128)}, bf16[8,64,32]{1,2,0:T(8,128)(2,1)S(1)}, bf16[64,128,32]{1,0,2:T(8,128)(2,1)S(1)}, ...), condition=%wide.region_3.4_spmd, body=%wide.region_2.3_spmd.sunk | while | flops 50462720 | bytes 1909321 | solution.py:119
  39.0 0.2 fusion.101
  39.4 0.9 fusion.102
  40.3 0.2 fusion.101
  40.6 0.9 fusion.102
  41.5 0.2 fusion.101
  41.8 0.9 fusion.102
  42.7 0.2 fusion.101
  43.1 0.9 fusion.102
  44.0 0.2 fusion.101
  44.3 0.9 fusion.102
  45.2 0.2 fusion.101
  45.6 0.9 fusion.102
  46.5 0.2 fusion.101
  46.8 0.9 fusion.102
  47.7 0.2 fusion.101
  48.0 0.9 fusion.102
  49.0 20.1 %all_gather.7 = bf16[64,128]{0,1:T(8,128)(2,1)S(1)} all-gather(bf16[64,8]{0,1:T(8,128)(2,1)S(1)} %get-tuple-element.57), channel_id=1, replica_groups=mesh['grp'=2,'wide'=16,'narrow'=1] {'wide'}, dimensions={1}, use_global_device_ids=true | all-gather | bytes 17408 | tf_op jit(solution)/shard_map/all_gather | solution.py:108
  69.3 0.2 copy.45
  69.6 1.3 fusion.70
  71.3 0.3 fusion.7
  71.6 0.2 fusion.40
  71.8 0.2 copy.66
  72.0 0.8 all_to_all.63
  72.8 3.5 %all-to-all-start.1 = ((bf16[16,8,1024]{2,1,0:T(8,128)(2,1)}), bf16[16,8,1024]{2,1,0:T(8,128)(2,1)S(1)}, u32[]{:S(2)}, u32[]{:S(2)}) async-start(bf16[16,8,1024]{2,1,0:T(8,128)(2,1)} %all_to_all.63), calls=%async_computation.1 | async-start | bytes 524288 | tf_op jit(solution)/shard_map/all_to_all | solution.py:53
  76.3 0.3 fusion.10
  76.6 0.2 fusion.39
  76.9 0.2 copy.58
  77.0 0.8 all_to_all.60
  77.9 8.5 %all-to-all-done.1 = bf16[16,8,1024]{2,1,0:T(8,128)(2,1)S(1)} async-done(((bf16[16,8,1024]{2,1,0:T(8,128)(2,1)}), bf16[16,8,1024]{2,1,0:T(8,128)(2,1)S(1)}, u32[]{:S(2)}, u32[]{:S(2)}) %all-to-all-start.1) | async-done | bytes 262176 | tf_op jit(solution)/shard_map/all_to_all | solution.py:53
  86.3 3.5 %all-to-all-start = ((bf16[16,8,1024]{2,1,0:T(8,128)(2,1)}), bf16[16,8,1024]{2,1,0:T(8,128)(2,1)S(1)}, u32[]{:S(2)}, u32[]{:S(2)}) async-start(bf16[16,8,1024]{2,1,0:T(8,128)(2,1)} %all_to_all.60), calls=%async_computation | async-start | bytes 524288 | tf_op jit(solution)/shard_map/all_to_all | solution.py:52
  90.2 9.7 %all-to-all-done = bf16[16,8,1024]{2,1,0:T(8,128)(2,1)S(1)} async-done(((bf16[16,8,1024]{2,1,0:T(8,128)(2,1)}), bf16[16,8,1024]{2,1,0:T(8,128)(2,1)S(1)}, u32[]{:S(2)}, u32[]{:S(2)}) %all-to-all-start) | async-done | bytes 262176 | tf_op jit(solution)/shard_map/all_to_all | solution.py:52
  100.2 0.3 fusion.35
  100.5 0.9 copy.144
  101.4 3.7 %all-to-all-start.2 = ((bf16[16,8,1024]{2,1,0:T(8,128)(2,1)}), bf16[16,8,1024]{2,1,0:T(8,128)(2,1)S(1)}, u32[]{:S(2)}, u32[]{:S(2)}) async-start(bf16[16,8,1024]{2,1,0:T(8,128)(2,1)} %bitcast.118), calls=%async_computation.2 | async-start | bytes 524288 | tf_op jit(solution)/shard_map/all_to_all | solution.py:65
  105.0 0.3 fusion.13
  105.3 9.7 %all-to-all-done.2 = bf16[16,8,1024]{2,1,0:T(8,128)(2,1)S(1)} async-done(((bf16[16,8,1024]{2,1,0:T(8,128)(2,1)}), bf16[16,8,1024]{2,1,0:T(8,128)(2,1)S(1)}, u32[]{:S(2)}, u32[]{:S(2)}) %all-to-all-start.2) | async-done | bytes 262176 | tf_op jit(solution)/shard_map/all_to_all | solution.py:65
  115.3 0.3 fusion.71
  115.8 0.3 fusion.16
  116.1 0.3 fusion.38
  116.4 0.2 copy.83
  116.6 0.8 all_to_all.71
  117.4 3.5 %all-to-all-start.4 = ((bf16[16,8,1024]{2,1,0:T(8,128)(2,1)}), bf16[16,8,1024]{2,1,0:T(8,128)(2,1)S(1)}, u32[]{:S(2)}, u32[]{:S(2)}) async-start(bf16[16,8,1024]{2,1,0:T(8,128)(2,1)} %all_to_all.71), calls=%async_computation.4 | async-start | bytes 524288 | tf_op jit(solution)/shard_map/all_to_all | solution.py:53
  120.9 0.3 fusion.19
  121.3 0.3 fusion.37
  121.5 0.2 copy.77
  121.7 0.8 all_to_all.68
  122.5 8.4 %all-to-all-done.4 = bf16[16,8,1024]{2,1,0:T(8,128)(2,1)S(1)} async-done(((bf16[16,8,1024]{2,1,0:T(8,128)(2,1)}), bf16[16,8,1024]{2,1,0:T(8,128)(2,1)S(1)}, u32[]{:S(2)}, u32[]{:S(2)}) %all-to-all-start.4) | async-done | bytes 262176 | tf_op jit(solution)/shard_map/all_to_all | solution.py:53
  130.9 3.5 %all-to-all-start.3 = ((bf16[16,8,1024]{2,1,0:T(8,128)(2,1)}), bf16[16,8,1024]{2,1,0:T(8,128)(2,1)S(1)}, u32[]{:S(2)}, u32[]{:S(2)}) async-start(bf16[16,8,1024]{2,1,0:T(8,128)(2,1)} %all_to_all.68), calls=%async_computation.3 | async-start | bytes 524288 | tf_op jit(solution)/shard_map/all_to_all | solution.py:52
  134.7 9.7 %all-to-all-done.3 = bf16[16,8,1024]{2,1,0:T(8,128)(2,1)S(1)} async-done(((bf16[16,8,1024]{2,1,0:T(8,128)(2,1)}), bf16[16,8,1024]{2,1,0:T(8,128)(2,1)S(1)}, u32[]{:S(2)}, u32[]{:S(2)}) %all-to-all-start.3) | async-done | bytes 262176 | tf_op jit(solution)/shard_map/all_to_all | solution.py:52
  144.8 0.3 fusion.36
  145.0 0.9 copy.143
  145.9 3.5 %all-to-all-start.5 = ((bf16[16,8,1024]{2,1,0:T(8,128)(2,1)}), bf16[16,8,1024]{2,1,0:T(8,128)(2,1)S(1)}, u32[]{:S(2)}, u32[]{:S(2)}) async-start(bf16[16,8,1024]{2,1,0:T(8,128)(2,1)} %bitcast.117), calls=%async_computation.5 | async-start | bytes 524288 | tf_op jit(solution)/shard_map/all_to_all | solution.py:65
  149.5 0.3 fusion.22
  149.8 9.7 %all-to-all-done.5 = bf16[16,8,1024]{2,1,0:T(8,128)(2,1)S(1)} async-done(((bf16[16,8,1024]{2,1,0:T(8,128)(2,1)}), bf16[16,8,1024]{2,1,0:T(8,128)(2,1)S(1)}, u32[]{:S(2)}, u32[]{:S(2)}) %all-to-all-start.5) | async-done | bytes 262176 | tf_op jit(solution)/shard_map/all_to_all | solution.py:65
  159.8 0.3 fusion.32
  160.0 0.9 copy.89
  (64 shorter events, 3.7 us)
Async XLA Ops:
  0.0 4.0 %copy-start = (bf16[256,64]{0,1:T(8,128)(2,1)S(1)}, bf16[256,64]{0,1:T(8,128)(2,1)}, u32[]{:S(2)}) copy-start(bf16[256,64]{0,1:T(8,128)(2,1)} %param.18) | copy-start | bytes 98308
  5.4 33.6 %copy-start.1 = (bf16[1024,128]{1,0:T(8,128)(2,1)S(1)}, bf16[1024,128]{1,0:T(8,128)(2,1)}, u32[]{:S(2)}) copy-start(bf16[1024,128]{1,0:T(8,128)(2,1)} %param.19) | copy-start | bytes 786436
  39.0 30.2 %copy-start.5 = (s32[128]{0:T(128)S(1)}, s32[128]{0:T(128)}, u32[]{:S(2)}) copy-start(s32[128]{0:T(128)} %param.14) | copy-start | bytes 1540
  39.0 30.3 %copy-start.3 = (bf16[8,128,128]{2,1,0:T(8,128)(2,1)S(1)}, bf16[8,128,128]{2,1,0:T(8,128)(2,1)}, u32[]{:S(2)}) copy-start(bf16[8,128,128]{2,1,0:T(8,128)(2,1)} %param.12) | copy-start | bytes 786436
  39.0 30.6 %copy-start.6 = (bf16[66,128]{1,0:T(8,128)(2,1)S(1)}, bf16[66,128]{1,0:T(8,128)(2,1)}, u32[]{:S(2)}) copy-start(bf16[66,128]{1,0:T(8,128)(2,1)} %param.17) | copy-start | bytes 50692
  69.2 1.9 %copy-start.2 = (bf16[2,128,640]{2,1,0:T(8,128)(2,1)S(1)}, bf16[2,128,640]{2,1,0:T(8,128)(2,1)}, u32[]{:S(2)}) copy-start(bf16[2,128,640]{2,1,0:T(8,128)(2,1)} %param.20) | copy-start | bytes 983044
  72.8 13.5 %all-to-all-start.1 = ((bf16[16,8,1024]{2,1,0:T(8,128)(2,1)}), bf16[16,8,1024]{2,1,0:T(8,128)(2,1)S(1)}, u32[]{:S(2)}, u32[]{:S(2)}) async-start(bf16[16,8,1024]{2,1,0:T(8,128)(2,1)} %all_to_all.63), calls=%async_computation.1 | async-start | bytes 524288 | tf_op jit(solution)/shard_map/all_to_all | solution.py:53
  86.3 13.5 %all-to-all-start = ((bf16[16,8,1024]{2,1,0:T(8,128)(2,1)}), bf16[16,8,1024]{2,1,0:T(8,128)(2,1)S(1)}, u32[]{:S(2)}, u32[]{:S(2)}) async-start(bf16[16,8,1024]{2,1,0:T(8,128)(2,1)} %all_to_all.60), calls=%async_computation | async-start | bytes 524288 | tf_op jit(solution)/shard_map/all_to_all | solution.py:52
  101.4 14.0 %copy-start.4 = (bf16[2,128,128]{2,1,0:T(8,128)(2,1)S(1)}, bf16[2,128,128]{2,1,0:T(8,128)(2,1)}, u32[]{:S(2)}) copy-start(bf16[2,128,128]{2,1,0:T(8,128)(2,1)} %param.21) | copy-start | bytes 196612
  101.4 13.7 %all-to-all-start.2 = ((bf16[16,8,1024]{2,1,0:T(8,128)(2,1)}), bf16[16,8,1024]{2,1,0:T(8,128)(2,1)S(1)}, u32[]{:S(2)}, u32[]{:S(2)}) async-start(bf16[16,8,1024]{2,1,0:T(8,128)(2,1)} %bitcast.118), calls=%async_computation.2 | async-start | bytes 524288 | tf_op jit(solution)/shard_map/all_to_all | solution.py:65
  117.4 13.5 %all-to-all-start.4 = ((bf16[16,8,1024]{2,1,0:T(8,128)(2,1)}), bf16[16,8,1024]{2,1,0:T(8,128)(2,1)S(1)}, u32[]{:S(2)}, u32[]{:S(2)}) async-start(bf16[16,8,1024]{2,1,0:T(8,128)(2,1)} %all_to_all.71), calls=%async_computation.4 | async-start | bytes 524288 | tf_op jit(solution)/shard_map/all_to_all | solution.py:53
  130.9 13.5 %all-to-all-start.3 = ((bf16[16,8,1024]{2,1,0:T(8,128)(2,1)}), bf16[16,8,1024]{2,1,0:T(8,128)(2,1)S(1)}, u32[]{:S(2)}, u32[]{:S(2)}) async-start(bf16[16,8,1024]{2,1,0:T(8,128)(2,1)} %all_to_all.68), calls=%async_computation.3 | async-start | bytes 524288 | tf_op jit(solution)/shard_map/all_to_all | solution.py:52
  145.9 13.5 %all-to-all-start.5 = ((bf16[16,8,1024]{2,1,0:T(8,128)(2,1)}), bf16[16,8,1024]{2,1,0:T(8,128)(2,1)S(1)}, u32[]{:S(2)}, u32[]{:S(2)}) async-start(bf16[16,8,1024]{2,1,0:T(8,128)(2,1)} %bitcast.117), calls=%async_computation.5 | async-start | bytes 524288 | tf_op jit(solution)/shard_map/all_to_all | solution.py:65
where the time goes:
time: 162 us; the launch traced here: 161 us
  waiting for transfers between devices  55.7 us (34%)
  blocking collectives  52.4 us (32%)
  starting transfers between devices  21.3 us (13%)
  matrix products  15.7 us (10%)
  local copies, waits for them, and re-layouts  10.6 us (7%)
  other arithmetic  4.57 us (3%)
    all_gather x1, blocking collectives, per_device(): lax.all_gather(right_proj, 'wide', axis=1, tiled=True)  32.3 us
    all_gather x1, blocking collectives, per_device(): lax.all_gather(live_flags, 'wide', axis=1, tiled=True)  20.1 us
    all_to_all x2, waiting for transfers between devices, triangle(): lax.all_to_all(flat_left, ('wide', 'narrow'), split_axis=0, concat_axis=1...  19.5 us
    all_to_all x2, waiting for transfers between devices, triangle(): lax.all_to_all(spread_out, ('wide', 'narrow'), split_axis=0, concat_axis=...  19.4 us
    all_to_all x2, waiting for transfers between devices, triangle(): lax.all_to_all(flat_right, ('wide', 'narrow'), split_axis=0, concat_axis=...  16.9 us
    dot_general x8, matrix products, opm_row(): jnp.dot(outer, outer_mean_output_weight, preferred_element_type=jnp.float32)  7.28 us
    all_to_all x2, starting transfers between devices, triangle(): lax.all_to_all(spread_out, ('wide', 'narrow'), split_axis=0, concat_axis=...  7.2 us
    all_to_all x2, starting transfers between devices, triangle(): lax.all_to_all(flat_left, ('wide', 'narrow'), split_axis=0, concat_axis=1...  7.07 us
  transfers between devices with their start and end apart: 6, of which 6 were waited for; matrix products, arithmetic and copies ran while one was open for 2% of the time, Pallas kernels for 0%

commit v1 on v0

--- a/solution.py
+++ b/solution.py
@@ -15,11 +15,29 @@
     return center * lax.rsqrt(spread + EPSILON)
 
 
-def split_into_sheets(flat, per_dev, wide_count, core_count, rows, cols):
-    shaped = flat.reshape(per_dev, wide_count, core_count, rows, cols)
-    return jnp.transpose(shaped, (0, 1, 3, 2, 4)).reshape(
-        per_dev, wide_count * rows, core_count * cols
+def gather_wide(block):
+    n = lax.axis_size("wide")
+    if n % 4 or n < 8:
+        return lax.all_gather(block, "wide", axis=0)
+    outer = n // 4
+    me = lax.axis_index("wide")
+    high, mid, low = me // 4, (me // 2) % 2, me % 2
+    arrived = [block]
+    for shift in range(1, outer):
+        perm = [(w, ((w // 4 + shift) % outer) * 4 + w % 4) for w in range(n)]
+        arrived.append(lax.ppermute(block, "wide", perm))
+    held = jnp.zeros((outer,) + block.shape, block.dtype)
+    for shift, piece in enumerate(arrived):
+        held = lax.dynamic_update_index_in_dim(held, piece, (high - shift + outer) % outer, 0)
+    other = lax.ppermute(held, "wide", [(w, w ^ 2) for w in range(n)])
+    held = jnp.stack(
+        [jnp.where(mid == 0, held, other), jnp.where(mid == 0, other, held)], axis=1
     )
+    other = lax.ppermute(held, "wide", [(w, w ^ 1) for w in range(n)])
+    held = jnp.stack(
+        [jnp.where(low == 0, held, other), jnp.where(low == 0, other, held)], axis=2
+    )
+    return held.reshape((n,) + block.shape)
 
 
 def triangle(stream, pair_live, proj_weight, out_weight, incoming):
@@ -28,6 +46,8 @@
     width = out_weight.shape[0]
     wide_count = lax.axis_size("wide")
     core_count = lax.axis_size("narrow")
+    devices = wide_count * core_count
+    per_dev = width // devices
     normed = apply_layer_norm(stream, 2).astype(jnp.bfloat16)
     blocks = [proj_weight[:, index * width : (index + 1) * width] for index in range(4)]
 
@@ -46,16 +66,19 @@
         )
     )
     form = "cki,ckj->cij" if incoming else "cik,cjk->cij"
-    flat_left = left_side.reshape(width, rows * cols)
-    flat_right = right_side.reshape(width, rows * cols)
-    left_flat, right_flat = (
-        lax.all_to_all(flat_left, ("wide", "narrow"), split_axis=0, concat_axis=1, tiled=True),
-        lax.all_to_all(flat_right, ("wide", "narrow"), split_axis=0, concat_axis=1, tiled=True),
+    both = jnp.stack(
+        [
+            left_side.reshape(devices, per_dev, rows * cols),
+            right_side.reshape(devices, per_dev, rows * cols),
+        ],
+        axis=1,
+    ).reshape(devices, 2 * per_dev, rows * cols)
+    both = lax.all_to_all(both, ("wide", "narrow"), split_axis=0, concat_axis=0, tiled=True)
+    both = both.reshape(wide_count, core_count, 2, per_dev, rows, cols)
+    both = jnp.transpose(both, (2, 3, 0, 4, 1, 5)).reshape(
+        2, per_dev, wide_count * rows, core_count * cols
     )
-    per_dev = left_flat.shape[0]
-    left_full = split_into_sheets(left_flat, per_dev, wide_count, core_count, rows, cols)
-    right_full = split_into_sheets(right_flat, per_dev, wide_count, core_count, rows, cols)
-    mixed = jnp.einsum(form, left_full, right_full, preferred_element_type=jnp.float32).astype(
+    mixed = jnp.einsum(form, both[0], both[1], preferred_element_type=jnp.float32).astype(
         jnp.bfloat16
     )
     spread_out = mixed.reshape(per_dev, wide_count, rows, core_count, cols)
@@ -100,15 +123,20 @@
     )
     projected_rows = (projected_rows * present_flags[:, :, None]).astype(jnp.bfloat16)
     half_width = projected_rows.shape[2] // 2
+    homologs = projected_rows.shape[0]
     left_proj = projected_rows[:, :, :half_width]
     right_proj = projected_rows[:, :, half_width:]
     live_flags = present_flags.astype(jnp.bfloat16)
-    right_all, live_all = (
-        lax.all_gather(right_proj, "wide", axis=1, tiled=True),
-        lax.all_gather(live_flags, "wide", axis=1, tiled=True),
+    packed = jnp.concatenate(
+        [jnp.transpose(right_proj, (1, 0, 2)).reshape(rows, homologs * half_width), live_flags.T],
+        axis=1,
     )
-    right_mine = lax.dynamic_slice_in_dim(right_all, col_start, cols, 1)
-    live_mine = lax.dynamic_slice_in_dim(live_all, col_start, cols, 1)
+    gathered = gather_wide(packed).reshape(-1, packed.shape[1])
+    gathered = lax.dynamic_slice_in_dim(gathered, col_start, cols, 0)
+    right_mine = jnp.transpose(
+        gathered[:, : homologs * half_width].reshape(cols, homologs, half_width), (1, 0, 2)
+    )
+    live_mine = gathered[:, homologs * half_width :].T
     counts = jnp.dot(live_flags.T, live_mine, preferred_element_type=jnp.float32)
 
     def opm_row(left_row):

time: 162 us -> 103 us (0.64)
  waiting for transfers between devices: 55.7 us -> 25.6 us
  blocking collectives: 52.4 us -> 37 us
  matrix products: 15.7 us -> 8.71 us
  starting transfers between devices: 21.3 us -> 16.8 us
    all_gather x2 -> x0, blocking collectives: 52.4 us -> none  [the longest x1 32.3 us: per_device(): lax.all_gather(right_proj, 'wide', axis=1, tiled=True)]
    all_to_all x0 -> x2, blocking collectives: none -> 37 us  [triangle(): lax.all_to_all(both, ('wide', 'narrow'), split_axis=0, concat_axis=0, til...]
    all_to_all x4 -> x0, waiting for transfers between devices: 36.3 us -> none  [the longest x2 19.5 us: triangle(): lax.all_to_all(flat_left, ('wide', 'narrow'), split_axis=0, concat_axis=1...]
    all_to_all x4 -> x0, starting transfers between devices: 14.1 us -> none  [the longest x2 7.07 us: triangle(): lax.all_to_all(flat_left, ('wide', 'narrow'), split_axis=0, concat_axis=1...]
    ppermute x0 -> x5, starting transfers between devices: none -> 8.58 us  [the longest x3 7.01 us: gather_wide(): arrived.append(lax.ppermute(block, 'wide', perm))]
    ppermute x0 -> x5, waiting for transfers between devices: none -> 6.17 us  [the longest x1 3.49 us: gather_wide(): other = lax.ppermute(held, 'wide', [(w, w ^ 2) for w in range(n)])]
    dot_general x8, matrix products: 7.28 us -> 2.27 us  [opm_row(): jnp.dot(outer, outer_mean_output_weight, preferred_element_type=jnp.float32)]
    all_to_all x8 -> x0, local copies, waits for them, and re-layouts: 3.85 us -> none  [the longest x4 1.93 us: triangle(): lax.all_to_all(flat_left, ('wide', 'narrow'), split_axis=0, concat_axis=1...]
  transfers between devices with their start and end apart: 6 -> 7, of which waited for: 6 -> 6; matrix products, arithmetic and copies ran while one was open for 2% -> 1% of each run, Pallas kernels for 0% -> 0%
where the time goes in v1:
time: 103 us; the launch traced here: 102 us
  blocking collectives  37 us (36%)
  waiting for transfers between devices  25.6 us (25%)
  starting transfers between devices  16.8 us (16%)
  local copies, waits for them, and re-layouts  9.25 us (9%)
  matrix products  8.71 us (8%)
  other arithmetic  3.95 us (4%)
    all_to_all x2, blocking collectives, triangle(): lax.all_to_all(both, ('wide', 'narrow'), split_axis=0, concat_axis=0, til...  37 us
    all_to_all x2, waiting for transfers between devices, triangle(): lax.all_to_all(spread_out, ('wide', 'narrow'), split_axis=0, concat_axis=...  19.4 us
    all_to_all x2, starting transfers between devices, triangle(): lax.all_to_all(spread_out, ('wide', 'narrow'), split_axis=0, concat_axis=...  8.19 us
    ppermute x3, starting transfers between devices, gather_wide(): arrived.append(lax.ppermute(block, 'wide', perm))  7.01 us
    ppermute x1, waiting for transfers between devices, gather_wide(): other = lax.ppermute(held, 'wide', [(w, w ^ 2) for w in range(n)])  3.49 us
    unnamed x22, local copies, waits for them, and re-layouts  3.16 us
    ppermute x3, waiting for transfers between devices, gather_wide(): arrived.append(lax.ppermute(block, 'wide', perm))  2.38 us
    dot_general x8, matrix products, opm_row(): jnp.dot(outer, outer_mean_output_weight, preferred_element_type=jnp.float32)  2.27 us
  transfers between devices with their start and end apart: 7, of which 6 were waited for; matrix products, arithmetic and copies ran while one was open for 1% of the time, Pallas kernels for 0%

profile of v1, /device:TPU:0, one launch (start us, length us, event | category | flops | bytes accessed | tf_op | source)
XLA Modules:
  0.0 102.2 jit_solution(11187836860911018108)
XLA Ops:
  0.0 0.7 convert_element_type.114
  0.8 0.8 convert_bitcast_fusion
  1.6 1.1 %convert_reduce_fusion.2 = f32[64,8]{1,0:T(8,128)S(1)} fusion(bf16[64,8,256]{2,1,0:T(8,128)(2,1)} %param.13), kind=kLoop, calls=%fused_computation.66 | loop fusion | flops 261632 | bytes 264192 | tf_op jit(solution)/shard_map/reduce_sum | solution.py:13
  2.7 0.2 fusion.52
  3.0 0.3 fusion.41
  3.7 3.1 %collective-permute-start = (bf16[8,2112]{1,0:T(8,128)(2,1)S(1)}, bf16[8,2112]{1,0:T(8,128)(2,1)S(1)}, u32[]{:S(2)}, u32[]{:S(2)}) collective-permute-start(bf16[8,2112]{1,0:T(8,128)(2,1)S(1)} %pad_maximum_fusion.4), channel_id=1, source_target_pairs={{0,4},{1,5},{2,6},{3,7},{4,8},{5,9},{6,10},{7,11},{8,12},{9,13},{1... | collective-permute-start | bytes 101384 | tf_op jit(solution)/shard_map/ppermute | solution.py:28
  6.7 2.6 %collective-permute-start.1 = (bf16[8,2112]{1,0:T(8,128)(2,1)S(1)}, bf16[8,2112]{1,0:T(8,128)(2,1)S(1)}, u32[]{:S(2)}, u32[]{:S(2)}) collective-permute-start(bf16[8,2112]{1,0:T(8,128)(2,1)S(1)} %pad_maximum_fusion.4), channel_id=1, source_target_pairs={{0,8},{1,9},{2,10},{3,11},{4,12},{5,13},{6,14},{7,15},{8,0},{9,1},... | collective-permute-start | bytes 101384 | tf_op jit(solution)/shard_map/ppermute | solution.py:28
  9.3 1.3 %collective-permute-start.2 = (bf16[8,2112]{1,0:T(8,128)(2,1)S(1)}, bf16[8,2112]{1,0:T(8,128)(2,1)S(1)}, u32[]{:S(2)}, u32[]{:S(2)}) collective-permute-start(bf16[8,2112]{1,0:T(8,128)(2,1)S(1)} %pad_maximum_fusion.4), channel_id=1, source_target_pairs={{0,12},{1,13},{2,14},{3,15},{4,0},{5,1},{6,2},{7,3},{8,4},{9,5},{1... | collective-permute-start | bytes 101384 | tf_op jit(solution)/shard_map/ppermute | solution.py:28
  10.9 1.1 %collective-permute-done.1 = bf16[8,2112]{1,0:T(8,128)(2,1)S(1)} collective-permute-done((bf16[8,2112]{1,0:T(8,128)(2,1)S(1)}, bf16[8,2112]{1,0:T(8,128)(2,1)S(1)}, u32[]{:S(2)}, u32[]{:S(2)}) %collective-permute-start.1) | collective-permute-done | bytes 33824 | tf_op jit(solution)/shard_map/ppermute | solution.py:28
  12.0 1.3 %collective-permute-done.2 = bf16[8,2112]{1,0:T(8,128)(2,1)S(1)} collective-permute-done((bf16[8,2112]{1,0:T(8,128)(2,1)S(1)}, bf16[8,2112]{1,0:T(8,128)(2,1)S(1)}, u32[]{:S(2)}, u32[]{:S(2)}) %collective-permute-start.2) | collective-permute-done | bytes 33824 | tf_op jit(solution)/shard_map/ppermute | solution.py:28
  13.3 1.5 %collective-permute-start.3 = (bf16[4,8,2112]{2,1,0:T(8,128)(2,1)S(1)}, bf16[4,8,2112]{2,1,0:T(8,128)(2,1)S(1)}, u32[]{:S(2)}, u32[]{:S(2)}) collective-permute-start(bf16[4,8,2112]{2,1,0:T(8,128)(2,1)S(1)} %bitcast_dynamic-update-slice_fusion), channel_id=1, source_target_pairs={{0,2},{1,3},{2,0},{3,1},{4,6},{5,7},{6,4},{7,5},{8,10},{9,11},{10,... | collective-permute-start | bytes 405512 | tf_op jit(solution)/shard_map/ppermute | solution.py:32
  14.8 3.5 %collective-permute-done.3 = bf16[4,8,2112]{2,1,0:T(8,128)(2,1)S(1)} collective-permute-done((bf16[4,8,2112]{2,1,0:T(8,128)(2,1)S(1)}, bf16[4,8,2112]{2,1,0:T(8,128)(2,1)S(1)}, u32[]{:S(2)}, u32[]{:S(2)}) %collective-permute-start.3) | collective-permute-done | bytes 135200 | tf_op jit(solution)/shard_map/ppermute | solution.py:32
  18.7 0.5 copy-done.7
  19.3 0.2 copy.92
  19.8 0.3 collective-permute-done.4
  20.3 0.6 copy-done.6
  21.0 0.3 copy.97
  21.4 0.2 copy.99
  21.6 0.7 copy-done.1
  22.3 5.0 %while.10 = (s32[]{:T(128)}, f32[8,128,128]{1,2,0:T(8,128)S(1)}, bf16[8,64,32]{1,2,0:T(8,128)(2,1)S(1)}, bf16[64,128,32]{1,0,2:T(8,128)(2,1)S(1)}, bf16[1024,128]{1,0:T(8,128)(2,1)S(1)}, /*index=5*/s32[]{:T(128)}) while((s32[]{:T(128)}, f32[8,128,128]{1,2,0:T(8,128)S(1)}, bf16[8,64,32]{1,2,0:T(8,128)(2,1)S(1)}, ...), condition=%wide.region_3.4_spmd, body=%wide.region_2.3_spmd.sunk | while | flops 50462720 | bytes 1908813 | solution.py:147
  22.3 0.2 fusion.95
  22.6 0.3 fusion.96
  22.9 0.2 fusion.95
  23.3 0.3 fusion.96
  23.6 0.2 fusion.95
  23.9 0.3 fusion.96
  24.2 0.2 fusion.95
  24.5 0.3 fusion.96
  24.8 0.2 fusion.95
  25.2 0.3 fusion.96
  25.5 0.2 fusion.95
  25.8 0.3 fusion.96
  26.1 0.2 fusion.95
  26.4 0.3 fusion.96
  26.7 0.2 fusion.95
  27.1 0.3 fusion.96
  27.4 0.3 fusion.70
  27.8 0.3 fusion.10
  28.1 0.3 fusion.7
  28.4 0.2 fusion.39
  28.6 0.2 copy.109
  28.9 0.2 fusion.40
  29.2 0.2 copy.116
  29.5 19.7 %all_to_all.28 = bf16[16,16,1024]{2,1,0:T(8,128)(2,1)S(1)} all-to-all(bf16[16,16,1024]{2,1,0:T(8,128)(2,1)S(1)} %copy_bitcast_fusion.3), channel_id=1, replica_groups=mesh['grp'=2,'wide'=16,'narrow'=1] {'wide','narrow'}, dimensions={0} | all-to-all | bytes 1048576 | tf_op jit(solution)/shard_map/all_to_all | solution.py:76
  49.3 0.3 fusion.35
  49.6 0.9 copy.201
  50.5 4.1 %all-to-all-start.1 = ((bf16[16,8,1024]{2,1,0:T(8,128)(2,1)}), bf16[16,8,1024]{2,1,0:T(8,128)(2,1)S(1)}, u32[]{:S(2)}, u32[]{:S(2)}) async-start(bf16[16,8,1024]{2,1,0:T(8,128)(2,1)} %bitcast.160), calls=%async_computation.1 | async-start | bytes 524288 | tf_op jit(solution)/shard_map/all_to_all | solution.py:88
  54.6 0.3 fusion.13
  54.9 9.7 %all-to-all-done.1 = bf16[16,8,1024]{2,1,0:T(8,128)(2,1)S(1)} async-done(((bf16[16,8,1024]{2,1,0:T(8,128)(2,1)}), bf16[16,8,1024]{2,1,0:T(8,128)(2,1)S(1)}, u32[]{:S(2)}, u32[]{:S(2)}) %all-to-all-start.1) | async-done | bytes 262176 | tf_op jit(solution)/shard_map/all_to_all | solution.py:88
  65.0 0.8 copy-done.5
  65.8 0.3 fusion.71
  66.2 0.3 fusion.19
  66.5 0.3 fusion.16
  66.9 0.3 fusion.37
  67.5 0.3 fusion.38
  67.8 0.2 copy.133
  68.1 17.2 %all_to_all.29 = bf16[16,16,1024]{2,1,0:T(8,128)(2,1)S(1)} all-to-all(bf16[16,16,1024]{2,1,0:T(8,128)(2,1)S(1)} %copy_bitcast_fusion.1), channel_id=1, replica_groups=mesh['grp'=2,'wide'=16,'narrow'=1] {'wide','narrow'}, dimensions={0} | all-to-all | bytes 1048576 | tf_op jit(solution)/shard_map/all_to_all | solution.py:76
  85.4 0.3 fusion.36
  85.7 0.9 copy.200
  86.6 4.1 %all-to-all-start.3 = ((bf16[16,8,1024]{2,1,0:T(8,128)(2,1)}), bf16[16,8,1024]{2,1,0:T(8,128)(2,1)S(1)}, u32[]{:S(2)}, u32[]{:S(2)}) async-start(bf16[16,8,1024]{2,1,0:T(8,128)(2,1)} %bitcast.159), calls=%async_computation.3 | async-start | bytes 524288 | tf_op jit(solution)/shard_map/all_to_all | solution.py:88
  90.7 0.3 fusion.22
  91.1 9.7 %all-to-all-done.3 = bf16[16,8,1024]{2,1,0:T(8,128)(2,1)S(1)} async-done(((bf16[16,8,1024]{2,1,0:T(8,128)(2,1)}), bf16[16,8,1024]{2,1,0:T(8,128)(2,1)S(1)}, u32[]{:S(2)}, u32[]{:S(2)}) %all-to-all-start.3) | async-done | bytes 262176 | tf_op jit(solution)/shard_map/all_to_all | solution.py:88
  101.0 0.3 fusion.32
  101.3 0.9 copy.140
  (80 shorter events, 4.2 us)
Async XLA Ops:
  0.0 3.0 %copy-start = (bf16[256,64]{0,1:T(8,128)(2,1)S(1)}, bf16[256,64]{0,1:T(8,128)(2,1)}, u32[]{:S(2)}) copy-start(bf16[256,64]{0,1:T(8,128)(2,1)} %param.18) | copy-start | bytes 98308
  0.0 2.7 %copy-start.2 = (bf16[64,8,256]{2,1,0:T(8,128)(2,1)S(1)}, bf16[64,8,256]{2,1,0:T(8,128)(2,1)}, u32[]{:S(2)}) copy-start(bf16[64,8,256]{2,1,0:T(8,128)(2,1)} %param.13) | copy-start | bytes 786436
  3.4 7.3 %copy-start.3 = (bf16[2,128,640]{2,1,0:T(8,128)(2,1)S(1)}, bf16[2,128,640]{2,1,0:T(8,128)(2,1)}, u32[]{:S(2)}) copy-start(bf16[2,128,640]{2,1,0:T(8,128)(2,1)} %param.20) | copy-start | bytes 983044
  3.7 7.2 %collective-permute-start = (bf16[8,2112]{1,0:T(8,128)(2,1)S(1)}, bf16[8,2112]{1,0:T(8,128)(2,1)S(1)}, u32[]{:S(2)}, u32[]{:S(2)}) collective-permute-start(bf16[8,2112]{1,0:T(8,128)(2,1)S(1)} %pad_maximum_fusion.4), channel_id=1, source_target_pairs={{0,4},{1,5},{2,6},{3,7},{4,8},{5,9},{6,10},{7,11},{8,12},{9,13},{1... | collective-permute-start | bytes 101384 | tf_op jit(solution)/shard_map/ppermute | solution.py:28
  6.7 5.2 %collective-permute-start.1 = (bf16[8,2112]{1,0:T(8,128)(2,1)S(1)}, bf16[8,2112]{1,0:T(8,128)(2,1)S(1)}, u32[]{:S(2)}, u32[]{:S(2)}) collective-permute-start(bf16[8,2112]{1,0:T(8,128)(2,1)S(1)} %pad_maximum_fusion.4), channel_id=1, source_target_pairs={{0,8},{1,9},{2,10},{3,11},{4,12},{5,13},{6,14},{7,15},{8,0},{9,1},... | collective-permute-start | bytes 101384 | tf_op jit(solution)/shard_map/ppermute | solution.py:28
  9.3 3.9 %collective-permute-start.2 = (bf16[8,2112]{1,0:T(8,128)(2,1)S(1)}, bf16[8,2112]{1,0:T(8,128)(2,1)S(1)}, u32[]{:S(2)}, u32[]{:S(2)}) collective-permute-start(bf16[8,2112]{1,0:T(8,128)(2,1)S(1)} %pad_maximum_fusion.4), channel_id=1, source_target_pairs={{0,12},{1,13},{2,14},{3,15},{4,0},{5,1},{6,2},{7,3},{8,4},{9,5},{1... | collective-permute-start | bytes 101384 | tf_op jit(solution)/shard_map/ppermute | solution.py:28
  13.3 5.1 %collective-permute-start.3 = (bf16[4,8,2112]{2,1,0:T(8,128)(2,1)S(1)}, bf16[4,8,2112]{2,1,0:T(8,128)(2,1)S(1)}, u32[]{:S(2)}, u32[]{:S(2)}) collective-permute-start(bf16[4,8,2112]{2,1,0:T(8,128)(2,1)S(1)} %bitcast_dynamic-update-slice_fusion), channel_id=1, source_target_pairs={{0,2},{1,3},{2,0},{3,1},{4,6},{5,7},{6,4},{7,5},{8,10},{9,11},{10,... | collective-permute-start | bytes 405512 | tf_op jit(solution)/shard_map/ppermute | solution.py:32
  18.4 1.0 copy-start.4
  18.4 1.6 %collective-permute-start.4 = (bf16[4,2,8,2112]{3,2,1,0:T(8,128)(2,1)S(1)}, bf16[4,2,8,2112]{3,2,1,0:T(8,128)(2,1)S(1)}, u32[]{:S(2)}, u32[]{:S(2)}) collective-permute-start(bf16[4,2,8,2112]{3,2,1,0:T(8,128)(2,1)S(1)} %pad_maximum_fusion.3), channel_id=1, source_target_pairs={{0,1},{1,0},{2,3},{3,2},{4,5},{5,4},{6,7},{7,6},{8,9},{9,8},{10,11... | collective-permute-start | bytes 811016 | tf_op jit(solution)/shard_map/ppermute | solution.py:36
  18.5 0.7 copy-start.7
  20.2 0.7 copy-start.6
  21.3 1.0 copy-start.1
  22.3 5.1 %copy-start.8 = (bf16[66,128]{1,0:T(8,128)(2,1)S(1)}, bf16[66,128]{1,0:T(8,128)(2,1)}, u32[]{:S(2)}) copy-start(bf16[66,128]{1,0:T(8,128)(2,1)} %param.17) | copy-start | bytes 50692
  50.5 14.1 %all-to-all-start.1 = ((bf16[16,8,1024]{2,1,0:T(8,128)(2,1)}), bf16[16,8,1024]{2,1,0:T(8,128)(2,1)S(1)}, u32[]{:S(2)}, u32[]{:S(2)}) async-start(bf16[16,8,1024]{2,1,0:T(8,128)(2,1)} %bitcast.160), calls=%async_computation.1 | async-start | bytes 524288 | tf_op jit(solution)/shard_map/all_to_all | solution.py:88
  64.9 0.8 copy-start.5
  86.6 14.2 %all-to-all-start.3 = ((bf16[16,8,1024]{2,1,0:T(8,128)(2,1)}), bf16[16,8,1024]{2,1,0:T(8,128)(2,1)S(1)}, u32[]{:S(2)}, u32[]{:S(2)}) async-start(bf16[16,8,1024]{2,1,0:T(8,128)(2,1)} %bitcast.159), calls=%async_computation.3 | async-start | bytes 524288 | tf_op jit(solution)/shard_map/all_to_all | solution.py:88

commit v2 on v1

--- a/solution.py
+++ b/solution.py
@@ -40,32 +40,64 @@
     return held.reshape((n,) + block.shape)
 
 
-def triangle(stream, pair_live, proj_weight, out_weight, incoming):
-    rows = stream.shape[0]
-    cols = stream.shape[1]
-    width = out_weight.shape[0]
+def chip_exchange(blocks):
+    chips = blocks.shape[0]
+    count = lax.axis_size("wide")
+    here = lax.axis_index("wide") // 2
+    held = lax.dynamic_update_index_in_dim(
+        jnp.zeros_like(blocks), lax.dynamic_index_in_dim(blocks, here, 0, False), here, 0
+    )
+    arrived = []
+    for step in range(chips - 1, 0, -1):
+        piece = lax.dynamic_index_in_dim(blocks, here ^ step, 0, False)
+        pairs = [(w, w ^ (2 * step)) for w in range(count)]
+        arrived.append((step, lax.ppermute(piece, "wide", pairs)))
+    for step, piece in arrived:
+        held = lax.dynamic_update_index_in_dim(held, piece, here ^ step, 0)
+    return held
+
+
+def core_swap(block):
+    count = lax.axis_size("wide")
+    return lax.ppermute(block, "wide", [(w, w ^ 1) for w in range(count)])
+
+
+def planes_by_chip(left_side, right_side, incoming):
+    width, rows, cols = left_side.shape
+    chips = lax.axis_size("wide") // 2
+    per_chip = width // chips
+    core = lax.axis_index("wide") % 2
+    both = jnp.stack(
+        [left_side.reshape(chips, per_chip, rows, cols), right_side.reshape(chips, per_chip, rows, cols)],
+        axis=1,
+    )
+    both = jnp.transpose(chip_exchange(both), (1, 2, 0, 3, 4))
+    if incoming:
+        both = both.reshape(2, per_chip, chips * rows, cols)
+        partial = jnp.einsum("cki,ckj->cij", both[0], both[1], preferred_element_type=jnp.float32)
+        partial = partial.reshape(per_chip, chips, 2, rows, cols)
+        mine = jnp.where(core == 0, partial[:, :, 0], partial[:, :, 1])
+        theirs = jnp.where(core == 0, partial[:, :, 1], partial[:, :, 0])
+        mixed = mine + core_swap(theirs)
+    else:
+        left = both[0].reshape(per_chip, chips * rows, cols)
+        mine = both[1]
+        theirs = core_swap(mine)
+        right = jnp.stack(
+            [jnp.where(core == 0, mine, theirs), jnp.where(core == 0, theirs, mine)], axis=2
+        ).reshape(per_chip, 2 * chips * rows, cols)
+        mixed = jnp.einsum("cik,cjk->cij", left, right, preferred_element_type=jnp.float32)
+        mixed = mixed.reshape(per_chip, chips, rows, cols)
+    mixed = jnp.transpose(mixed.astype(jnp.bfloat16), (1, 0, 2, 3))
+    return chip_exchange(mixed).reshape(width, rows, cols)
+
+
+def planes_by_device(left_side, right_side, incoming):
+    width, rows, cols = left_side.shape
     wide_count = lax.axis_size("wide")
     core_count = lax.axis_size("narrow")
     devices = wide_count * core_count
     per_dev = width // devices
-    normed = apply_layer_norm(stream, 2).astype(jnp.bfloat16)
-    blocks = [proj_weight[:, index * width : (index + 1) * width] for index in range(4)]
-
-    def project(block):
-        return jnp.einsum("ijd,dc->cij", normed, block, preferred_element_type=jnp.float32)
-
-    left_side = (jax.nn.sigmoid(project(blocks[0])) * project(blocks[1]) * pair_live[None]).astype(
-        jnp.bfloat16
-    )
-    right_side = (jax.nn.sigmoid(project(blocks[2])) * project(blocks[3]) * pair_live[None]).astype(
-        jnp.bfloat16
-    )
-    gate = jax.nn.sigmoid(
-        jnp.einsum(
-            "ijd,dc->ijc", normed, proj_weight[:, 4 * width :], preferred_element_type=jnp.float32
-        )
-    )
-    form = "cki,ckj->cij" if incoming else "cik,cjk->cij"
     both = jnp.stack(
         [
             left_side.reshape(devices, per_dev, rows * cols),
@@ -78,6 +110,7 @@
     both = jnp.transpose(both, (2, 3, 0, 4, 1, 5)).reshape(
         2, per_dev, wide_count * rows, core_count * cols
     )
+    form = "cki,ckj->cij" if incoming else "cik,cjk->cij"
     mixed = jnp.einsum(form, both[0], both[1], preferred_element_type=jnp.float32).astype(
         jnp.bfloat16
     )
@@ -85,9 +118,34 @@
     spread_out = jnp.transpose(spread_out, (1, 3, 0, 2, 4)).reshape(
         wide_count * core_count * per_dev, rows * cols
     )
-    returned = lax.all_to_all(
+    return lax.all_to_all(
         spread_out, ("wide", "narrow"), split_axis=0, concat_axis=0, tiled=True
     ).reshape(width, rows, cols)
+
+
+def triangle(stream, pair_live, proj_weight, out_weight, incoming):
+    width = out_weight.shape[0]
+    wide_count = lax.axis_size("wide")
+    by_chip = lax.axis_size("narrow") == 1 and wide_count in (4, 8, 16)
+    normed = apply_layer_norm(stream, 2).astype(jnp.bfloat16)
+    blocks = [proj_weight[:, index * width : (index + 1) * width] for index in range(4)]
+
+    def project(block):
+        return jnp.einsum("ijd,dc->cij", normed, block, preferred_element_type=jnp.float32)
+
+    left_side = (jax.nn.sigmoid(project(blocks[0])) * project(blocks[1]) * pair_live[None]).astype(
+        jnp.bfloat16
+    )
+    right_side = (jax.nn.sigmoid(project(blocks[2])) * project(blocks[3]) * pair_live[None]).astype(
+        jnp.bfloat16
+    )
+    gate = jax.nn.sigmoid(
+        jnp.einsum(
+            "ijd,dc->ijc", normed, proj_weight[:, 4 * width :], preferred_element_type=jnp.float32
+        )
+    )
+    planes = planes_by_chip if by_chip else planes_by_device
+    returned = planes(left_side, right_side, incoming)
     blended_standardize = apply_layer_norm(returned.astype(jnp.float32), 0).astype(jnp.bfloat16)
     update = jnp.einsum(
         "cij,cd->ijd", blended_standardize, out_weight, preferred_element_type=jnp.float32

time: 103 us -> 98.5 us (0.956)
  starting transfers between devices: 16.8 us -> 54 us
  blocking collectives: 37 us -> 0 us
  waiting for transfers between devices: 25.6 us -> 21.7 us
  local copies, waits for them, and re-layouts: 9.25 us -> 7.86 us
    ppermute x0 -> x30, starting transfers between devices: none -> 45.5 us  [the longest x28 45.3 us: chip_exchange(): arrived.append((step, lax.ppermute(piece, 'wide', pairs)))]
    all_to_all x2 -> x0, blocking collectives: 37 us -> none  [triangle(): lax.all_to_all(both, ('wide', 'narrow'), split_axis=0, concat_axis=0, til...]
    all_to_all x2 -> x0, waiting for transfers between devices: 19.4 us -> none  [triangle(): lax.all_to_all(spread_out, ('wide', 'narrow'), split_axis=0, concat_axis=...]
    ppermute x0 -> x30, waiting for transfers between devices: none -> 15.6 us  [the longest x28 12.8 us: chip_exchange(): arrived.append((step, lax.ppermute(piece, 'wide', pairs)))]
    all_to_all x2 -> x0, starting transfers between devices: 8.19 us -> none  [triangle(): lax.all_to_all(spread_out, ('wide', 'narrow'), split_axis=0, concat_axis=...]
    transpose x2 -> x0, local copies, waits for them, and re-layouts: 1.76 us -> none  [triangle(): jnp.transpose(spread_out, (1, 3, 0, 2, 4))]
  transfers between devices with their start and end apart: 7 -> 35, of which waited for: 6 -> 20; matrix products, arithmetic and copies ran while one was open for 1% -> 2% of each run, Pallas kernels for 0% -> 0%
where the time goes in v2:
time: 98.5 us; the launch traced here: 98.2 us
  starting transfers between devices  54 us (55%)
  waiting for transfers between devices  21.7 us (22%)
  matrix products  8.96 us (9%)
  local copies, waits for them, and re-layouts  7.86 us (8%)
  other arithmetic  4.44 us (5%)
    ppermute x28, starting transfers between devices, chip_exchange(): arrived.append((step, lax.ppermute(piece, 'wide', pairs)))  45.3 us
    ppermute x28, waiting for transfers between devices, chip_exchange(): arrived.append((step, lax.ppermute(piece, 'wide', pairs)))  12.8 us
    ppermute x3, starting transfers between devices, gather_wide(): arrived.append(lax.ppermute(block, 'wide', perm))  7.01 us
    ppermute x1, waiting for transfers between devices, gather_wide(): other = lax.ppermute(held, 'wide', [(w, w ^ 2) for w in range(n)])  3.49 us
    unnamed x22, local copies, waits for them, and re-layouts  3.36 us
    ppermute x2, waiting for transfers between devices, core_swap(): return lax.ppermute(block, 'wide', [(w, w ^ 1) for w in range(count)])  2.77 us
    ppermute x3, waiting for transfers between devices, gather_wide(): arrived.append(lax.ppermute(block, 'wide', perm))  2.37 us
    dot_general x8, matrix products, opm_row(): jnp.dot(outer, outer_mean_output_weight, preferred_element_type=jnp.float32)  2.26 us
  transfers between devices with their start and end apart: 35, of which 20 were waited for; matrix products, arithmetic and copies ran while one was open for 2% of the time, Pallas kernels for 0%

profile of v2, /device:TPU:0, one launch (start us, length us, event | category | flops | bytes accessed | tf_op | source)
XLA Modules:
  0.0 98.2 jit_solution(3695387376671614232)
XLA Ops:
  0.0 0.7 convert_element_type.89
  0.8 0.8 convert_bitcast_fusion
  1.6 1.1 %convert_reduce_fusion.2 = f32[64,8]{1,0:T(8,128)S(1)} fusion(bf16[64,8,256]{2,1,0:T(8,128)(2,1)} %param.13), kind=kLoop, calls=%fused_computation.60 | loop fusion | flops 261632 | bytes 264192 | tf_op jit(solution)/shard_map/reduce_sum | solution.py:13
  3.0 0.3 fusion.36
  3.7 3.1 %collective-permute-start = (bf16[8,2112]{1,0:T(8,128)(2,1)S(1)}, bf16[8,2112]{1,0:T(8,128)(2,1)S(1)}, u32[]{:S(2)}, u32[]{:S(2)}) collective-permute-start(bf16[8,2112]{1,0:T(8,128)(2,1)S(1)} %pad_maximum_fusion.3), channel_id=1, source_target_pairs={{0,4},{1,5},{2,6},{3,7},{4,8},{5,9},{6,10},{7,11},{8,12},{9,13},{1... | collective-permute-start | bytes 101384 | tf_op jit(solution)/shard_map/ppermute | solution.py:28
  6.7 2.6 %collective-permute-start.1 = (bf16[8,2112]{1,0:T(8,128)(2,1)S(1)}, bf16[8,2112]{1,0:T(8,128)(2,1)S(1)}, u32[]{:S(2)}, u32[]{:S(2)}) collective-permute-start(bf16[8,2112]{1,0:T(8,128)(2,1)S(1)} %pad_maximum_fusion.3), channel_id=1, source_target_pairs={{0,8},{1,9},{2,10},{3,11},{4,12},{5,13},{6,14},{7,15},{8,0},{9,1},... | collective-permute-start | bytes 101384 | tf_op jit(solution)/shard_map/ppermute | solution.py:28
  9.3 1.3 %collective-permute-start.2 = (bf16[8,2112]{1,0:T(8,128)(2,1)S(1)}, bf16[8,2112]{1,0:T(8,128)(2,1)S(1)}, u32[]{:S(2)}, u32[]{:S(2)}) collective-permute-start(bf16[8,2112]{1,0:T(8,128)(2,1)S(1)} %pad_maximum_fusion.3), channel_id=1, source_target_pairs={{0,12},{1,13},{2,14},{3,15},{4,0},{5,1},{6,2},{7,3},{8,4},{9,5},{1... | collective-permute-start | bytes 101384 | tf_op jit(solution)/shard_map/ppermute | solution.py:28
  10.9 1.1 %collective-permute-done.1 = bf16[8,2112]{1,0:T(8,128)(2,1)S(1)} collective-permute-done((bf16[8,2112]{1,0:T(8,128)(2,1)S(1)}, bf16[8,2112]{1,0:T(8,128)(2,1)S(1)}, u32[]{:S(2)}, u32[]{:S(2)}) %collective-permute-start.1) | collective-permute-done | bytes 33824 | tf_op jit(solution)/shard_map/ppermute | solution.py:28
  12.0 1.3 %collective-permute-done.2 = bf16[8,2112]{1,0:T(8,128)(2,1)S(1)} collective-permute-done((bf16[8,2112]{1,0:T(8,128)(2,1)S(1)}, bf16[8,2112]{1,0:T(8,128)(2,1)S(1)}, u32[]{:S(2)}, u32[]{:S(2)}) %collective-permute-start.2) | collective-permute-done | bytes 33824 | tf_op jit(solution)/shard_map/ppermute | solution.py:28
  13.3 1.5 %collective-permute-start.3 = (bf16[4,8,2112]{2,1,0:T(8,128)(2,1)S(1)}, bf16[4,8,2112]{2,1,0:T(8,128)(2,1)S(1)}, u32[]{:S(2)}, u32[]{:S(2)}) collective-permute-start(bf16[4,8,2112]{2,1,0:T(8,128)(2,1)S(1)} %bitcast_dynamic-update-slice_fusion.16), channel_id=1, source_target_pairs={{0,2},{1,3},{2,0},{3,1},{4,6},{5,7},{6,4},{7,5},{8,10},{9,11},{10,... | collective-permute-start | bytes 405512 | tf_op jit(solution)/shard_map/ppermute | solution.py:32
  14.8 3.5 %collective-permute-done.3 = bf16[4,8,2112]{2,1,0:T(8,128)(2,1)S(1)} collective-permute-done((bf16[4,8,2112]{2,1,0:T(8,128)(2,1)S(1)}, bf16[4,8,2112]{2,1,0:T(8,128)(2,1)S(1)}, u32[]{:S(2)}, u32[]{:S(2)}) %collective-permute-start.3) | collective-permute-done | bytes 135200 | tf_op jit(solution)/shard_map/ppermute | solution.py:32
  18.7 0.5 copy-done.7
  20.3 0.6 copy-done.6
  21.6 0.7 copy-done.1
  22.3 5.0 %while.10 = (s32[]{:T(128)}, f32[8,128,128]{1,2,0:T(8,128)S(1)}, bf16[8,64,32]{1,2,0:T(8,128)(2,1)S(1)}, bf16[64,128,32]{1,0,2:T(8,128)(2,1)S(1)}, bf16[1024,128]{1,0:T(8,128)(2,1)S(1)}, /*index=5*/s32[]{:T(128)}) while((s32[]{:T(128)}, f32[8,128,128]{1,2,0:T(8,128)S(1)}, bf16[8,64,32]{1,2,0:T(8,128)(2,1)S(1)}, ...), condition=%wide.region_3.4_spmd, body=%wide.region_2.3_spmd.sunk | while | flops 50462720 | bytes 1908813 | solution.py:205
  27.8 0.3 fusion.7
  29.3 4.1 %collective-permute-start.5 = (bf16[2,16,8,128]{3,2,1,0:T(8,128)(2,1)S(1)}, bf16[2,16,8,128]{3,2,1,0:T(8,128)(2,1)S(1)}, u32[]{:S(2)}, u32[]{:S(2)}) collective-permute-start(bf16[2,16,8,128]{3,2,1,0:T(8,128)(2,1)S(1)} %get-tuple-element.72), channel_id=1, source_target_pairs={{0,14},{1,15},{2,12},{3,13},{4,10},{5,11},{6,8},{7,9},{8,6},{9,7},... | collective-permute-start | bytes 196616 | tf_op jit(solution)/shard_map/ppermute | solution.py:54
  33.4 0.7 collective-permute-start.6
  34.1 2.9 %collective-permute-start.8 = (bf16[2,16,8,128]{3,2,1,0:T(8,128)(2,1)S(1)}, bf16[2,16,8,128]{3,2,1,0:T(8,128)(2,1)S(1)}, u32[]{:S(2)}, u32[]{:S(2)}) collective-permute-start(bf16[2,16,8,128]{3,2,1,0:T(8,128)(2,1)S(1)} %get-tuple-element.69), channel_id=1, source_target_pairs={{0,8},{1,9},{2,10},{3,11},{4,12},{5,13},{6,14},{7,15},{8,0},{9,1},... | collective-permute-start | bytes 196616 | tf_op jit(solution)/shard_map/ppermute | solution.py:54
  37.0 1.7 %collective-permute-start.9 = (bf16[2,16,8,128]{3,2,1,0:T(8,128)(2,1)S(1)}, bf16[2,16,8,128]{3,2,1,0:T(8,128)(2,1)S(1)}, u32[]{:S(2)}, u32[]{:S(2)}) collective-permute-start(bf16[2,16,8,128]{3,2,1,0:T(8,128)(2,1)S(1)} %get-tuple-element.68), channel_id=1, source_target_pairs={{0,6},{1,7},{2,4},{3,5},{4,2},{5,3},{6,0},{7,1},{8,14},{9,15},{10,... | collective-permute-start | bytes 196616 | tf_op jit(solution)/shard_map/ppermute | solution.py:54
  38.9 1.3 %collective-permute-start.10 = (bf16[2,16,8,128]{3,2,1,0:T(8,128)(2,1)S(1)}, bf16[2,16,8,128]{3,2,1,0:T(8,128)(2,1)S(1)}, u32[]{:S(2)}, u32[]{:S(2)}) collective-permute-start(bf16[2,16,8,128]{3,2,1,0:T(8,128)(2,1)S(1)} %get-tuple-element.67), channel_id=1, source_target_pairs={{0,4},{1,5},{2,6},{3,7},{4,0},{5,1},{6,2},{7,3},{8,12},{9,13},{10,... | collective-permute-start | bytes 196616 | tf_op jit(solution)/shard_map/ppermute | solution.py:54
  40.2 0.6 collective-permute-start.11
  40.9 1.9 %collective-permute-done.7 = bf16[2,16,8,128]{3,2,1,0:T(8,128)(2,1)S(1)} collective-permute-done((bf16[2,16,8,128]{3,2,1,0:T(8,128)(2,1)S(1)}, bf16[2,16,8,128]{3,2,1,0:T(8,128)(2,1)S(1)}, u32[]{:S(2)}, u32[]{:S(2)}) %collective-permute-start.7) | collective-permute-done | bytes 65568 | tf_op jit(solution)/shard_map/ppermute | solution.py:54
  42.8 1.5 %collective-permute-done.8 = bf16[2,16,8,128]{3,2,1,0:T(8,128)(2,1)S(1)} collective-permute-done((bf16[2,16,8,128]{3,2,1,0:T(8,128)(2,1)S(1)}, bf16[2,16,8,128]{3,2,1,0:T(8,128)(2,1)S(1)}, u32[]{:S(2)}, u32[]{:S(2)}) %collective-permute-start.8) | collective-permute-done | bytes 65568 | tf_op jit(solution)/shard_map/ppermute | solution.py:54
  44.4 0.5 collective-permute-done.10
  45.4 1.2 %collective-permute-done.12 = bf16[16,8,8,128]{3,2,1,0:T(8,128)(2,1)S(1)} collective-permute-done((bf16[16,8,8,128]{3,2,1,0:T(8,128)(2,1)S(1)}, bf16[16,8,8,128]{3,2,1,0:T(8,128)(2,1)S(1)}, u32[]{:S(2)}, u32[]{:S(2)}) %collective-permute-start.12) | collective-permute-done | bytes 262176 | tf_op jit(solution)/shard_map/ppermute | solution.py:62
  46.7 0.5 fusion.35
  47.3 3.6 %collective-permute-start.13 = (bf16[16,8,128]{2,1,0:T(8,128)(2,1)S(1)}, bf16[16,8,128]{2,1,0:T(8,128)(2,1)S(1)}, u32[]{:S(2)}, u32[]{:S(2)}) collective-permute-start(bf16[16,8,128]{2,1,0:T(8,128)(2,1)S(1)} %get-tuple-element.90), channel_id=1, source_target_pairs={{0,14},{1,15},{2,12},{3,13},{4,10},{5,11},{6,8},{7,9},{8,6},{9,7},... | collective-permute-start | bytes 98312 | tf_op jit(solution)/shard_map/ppermute | solution.py:54
  51.0 0.8 collective-permute-start.14
  51.8 3.3 %collective-permute-start.16 = (bf16[16,8,128]{2,1,0:T(8,128)(2,1)S(1)}, bf16[16,8,128]{2,1,0:T(8,128)(2,1)S(1)}, u32[]{:S(2)}, u32[]{:S(2)}) collective-permute-start(bf16[16,8,128]{2,1,0:T(8,128)(2,1)S(1)} %get-tuple-element.87), channel_id=1, source_target_pairs={{0,8},{1,9},{2,10},{3,11},{4,12},{5,13},{6,14},{7,15},{8,0},{9,1},... | collective-permute-start | bytes 98312 | tf_op jit(solution)/shard_map/ppermute | solution.py:54
  55.1 1.2 %collective-permute-start.17 = (bf16[16,8,128]{2,1,0:T(8,128)(2,1)S(1)}, bf16[16,8,128]{2,1,0:T(8,128)(2,1)S(1)}, u32[]{:S(2)}, u32[]{:S(2)}) collective-permute-start(bf16[16,8,128]{2,1,0:T(8,128)(2,1)S(1)} %get-tuple-element.86), channel_id=1, source_target_pairs={{0,6},{1,7},{2,4},{3,5},{4,2},{5,3},{6,0},{7,1},{8,14},{9,15},{10,... | collective-permute-start | bytes 98312 | tf_op jit(solution)/shard_map/ppermute | solution.py:54
  56.3 1.3 %collective-permute-start.18 = (bf16[16,8,128]{2,1,0:T(8,128)(2,1)S(1)}, bf16[16,8,128]{2,1,0:T(8,128)(2,1)S(1)}, u32[]{:S(2)}, u32[]{:S(2)}) collective-permute-start(bf16[16,8,128]{2,1,0:T(8,128)(2,1)S(1)} %get-tuple-element.85), channel_id=1, source_target_pairs={{0,4},{1,5},{2,6},{3,7},{4,0},{5,1},{6,2},{7,3},{8,12},{9,13},{10,... | collective-permute-start | bytes 98312 | tf_op jit(solution)/shard_map/ppermute | solution.py:54
  57.7 1.0 %collective-permute-start.19 = (bf16[16,8,128]{2,1,0:T(8,128)(2,1)S(1)}, bf16[16,8,128]{2,1,0:T(8,128)(2,1)S(1)}, u32[]{:S(2)}, u32[]{:S(2)}) collective-permute-start(bf16[16,8,128]{2,1,0:T(8,128)(2,1)S(1)} %get-tuple-element.84), channel_id=1, source_target_pairs={{0,2},{1,3},{2,0},{3,1},{4,6},{5,7},{6,4},{7,5},{8,10},{9,11},{10,... | collective-permute-start | bytes 98312 | tf_op jit(solution)/shard_map/ppermute | solution.py:54
  58.8 1.2 %collective-permute-done.17 = bf16[16,8,128]{2,1,0:T(8,128)(2,1)S(1)} collective-permute-done((bf16[16,8,128]{2,1,0:T(8,128)(2,1)S(1)}, bf16[16,8,128]{2,1,0:T(8,128)(2,1)S(1)}, u32[]{:S(2)}, u32[]{:S(2)}) %collective-permute-start.17) | collective-permute-done | bytes 32800 | tf_op jit(solution)/shard_map/ppermute | solution.py:54
  59.9 0.3 collective-permute-done.18
  60.3 1.4 %collective-permute-done.19 = bf16[16,8,128]{2,1,0:T(8,128)(2,1)S(1)} collective-permute-done((bf16[16,8,128]{2,1,0:T(8,128)(2,1)S(1)}, bf16[16,8,128]{2,1,0:T(8,128)(2,1)S(1)}, u32[]{:S(2)}, u32[]{:S(2)}) %collective-permute-start.19) | collective-permute-done | bytes 32800 | tf_op jit(solution)/shard_map/ppermute | solution.py:54
  62.0 0.8 copy-done.5
  63.2 0.3 fusion.16
  63.6 0.3 fusion.19
  64.9 3.8 %collective-permute-start.20 = (bf16[2,16,8,128]{3,2,1,0:T(8,128)(2,1)S(1)}, bf16[2,16,8,128]{3,2,1,0:T(8,128)(2,1)S(1)}, u32[]{:S(2)}, u32[]{:S(2)}) collective-permute-start(bf16[2,16,8,128]{3,2,1,0:T(8,128)(2,1)S(1)} %get-tuple-element.65), channel_id=1, source_target_pairs={{0,14},{1,15},{2,12},{3,13},{4,10},{5,11},{6,8},{7,9},{8,6},{9,7},... | collective-permute-start | bytes 196616 | tf_op jit(solution)/shard_map/ppermute | solution.py:54
  68.7 0.5 collective-permute-start.21
  69.2 0.3 collective-permute-start.22
  69.5 3.1 %collective-permute-start.23 = (bf16[2,16,8,128]{3,2,1,0:T(8,128)(2,1)S(1)}, bf16[2,16,8,128]{3,2,1,0:T(8,128)(2,1)S(1)}, u32[]{:S(2)}, u32[]{:S(2)}) collective-permute-start(bf16[2,16,8,128]{3,2,1,0:T(8,128)(2,1)S(1)} %get-tuple-element.62), channel_id=1, source_target_pairs={{0,8},{1,9},{2,10},{3,11},{4,12},{5,13},{6,14},{7,15},{8,0},{9,1},... | collective-permute-start | bytes 196616 | tf_op jit(solution)/shard_map/ppermute | solution.py:54
  72.6 1.4 %collective-permute-start.24 = (bf16[2,16,8,128]{3,2,1,0:T(8,128)(2,1)S(1)}, bf16[2,16,8,128]{3,2,1,0:T(8,128)(2,1)S(1)}, u32[]{:S(2)}, u32[]{:S(2)}) collective-permute-start(bf16[2,16,8,128]{3,2,1,0:T(8,128)(2,1)S(1)} %get-tuple-element.61), channel_id=1, source_target_pairs={{0,6},{1,7},{2,4},{3,5},{4,2},{5,3},{6,0},{7,1},{8,14},{9,15},{10,... | collective-permute-start | bytes 196616 | tf_op jit(solution)/shard_map/ppermute | solution.py:54
  74.2 1.1 %collective-permute-start.25 = (bf16[2,16,8,128]{3,2,1,0:T(8,128)(2,1)S(1)}, bf16[2,16,8,128]{3,2,1,0:T(8,128)(2,1)S(1)}, u32[]{:S(2)}, u32[]{:S(2)}) collective-permute-start(bf16[2,16,8,128]{3,2,1,0:T(8,128)(2,1)S(1)} %get-tuple-element.60), channel_id=1, source_target_pairs={{0,4},{1,5},{2,6},{3,7},{4,0},{5,1},{6,2},{7,3},{8,12},{9,13},{10,... | collective-permute-start | bytes 196616 | tf_op jit(solution)/shard_map/ppermute | solution.py:54
  75.3 1.1 %collective-permute-start.26 = (bf16[2,16,8,128]{3,2,1,0:T(8,128)(2,1)S(1)}, bf16[2,16,8,128]{3,2,1,0:T(8,128)(2,1)S(1)}, u32[]{:S(2)}, u32[]{:S(2)}) collective-permute-start(bf16[2,16,8,128]{3,2,1,0:T(8,128)(2,1)S(1)} %get-tuple-element.59), channel_id=1, source_target_pairs={{0,2},{1,3},{2,0},{3,1},{4,6},{5,7},{6,4},{7,5},{8,10},{9,11},{10,... | collective-permute-start | bytes 196616 | tf_op jit(solution)/shard_map/ppermute | solution.py:54
  76.5 0.9 collective-permute-done.22
  77.4 1.2 %collective-permute-done.23 = bf16[2,16,8,128]{3,2,1,0:T(8,128)(2,1)S(1)} collective-permute-done((bf16[2,16,8,128]{3,2,1,0:T(8,128)(2,1)S(1)}, bf16[2,16,8,128]{3,2,1,0:T(8,128)(2,1)S(1)}, u32[]{:S(2)}, u32[]{:S(2)}) %collective-permute-start.23) | collective-permute-done | bytes 65568 | tf_op jit(solution)/shard_map/ppermute | solution.py:54
  78.7 0.5 collective-permute-done.25
  79.2 0.4 collective-permute-done.26
  79.7 0.4 fusion.51
  80.3 0.3 fusion.22
  80.7 1.5 %collective-permute-done.27 = f32[16,8,8,128]{3,2,0,1:T(8,128)S(1)} collective-permute-done((f32[16,8,8,128]{3,2,0,1:T(8,128)S(1)}, f32[16,8,8,128]{3,2,0,1:T(8,128)S(1)}, u32[]{:S(2)}, u32[]{:S(2)}) %collective-permute-start.27) | collective-permute-done | bytes 524320 | tf_op jit(solution)/shard_map/ppermute | solution.py:62
  82.3 3.6 %collective-permute-start.28 = (bf16[16,8,128]{2,1,0:T(8,128)(2,1)S(1)}, bf16[16,8,128]{2,1,0:T(8,128)(2,1)S(1)}, u32[]{:S(2)}, u32[]{:S(2)}) collective-permute-start(bf16[16,8,128]{2,1,0:T(8,128)(2,1)S(1)} %get-tuple-element.83), channel_id=1, source_target_pairs={{0,14},{1,15},{2,12},{3,13},{4,10},{5,11},{6,8},{7,9},{8,6},{9,7},... | collective-permute-start | bytes 98312 | tf_op jit(solution)/shard_map/ppermute | solution.py:54
  86.0 0.8 collective-permute-start.29
  86.8 0.5 collective-permute-start.30
  87.3 2.8 %collective-permute-start.31 = (bf16[16,8,128]{2,1,0:T(8,128)(2,1)S(1)}, bf16[16,8,128]{2,1,0:T(8,128)(2,1)S(1)}, u32[]{:S(2)}, u32[]{:S(2)}) collective-permute-start(bf16[16,8,128]{2,1,0:T(8,128)(2,1)S(1)} %get-tuple-element.80), channel_id=1, source_target_pairs={{0,8},{1,9},{2,10},{3,11},{4,12},{5,13},{6,14},{7,15},{8,0},{9,1},... | collective-permute-start | bytes 98312 | tf_op jit(solution)/shard_map/ppermute | solution.py:54
  90.2 1.2 %collective-permute-start.32 = (bf16[16,8,128]{2,1,0:T(8,128)(2,1)S(1)}, bf16[16,8,128]{2,1,0:T(8,128)(2,1)S(1)}, u32[]{:S(2)}, u32[]{:S(2)}) collective-permute-start(bf16[16,8,128]{2,1,0:T(8,128)(2,1)S(1)} %get-tuple-element.79), channel_id=1, source_target_pairs={{0,6},{1,7},{2,4},{3,5},{4,2},{5,3},{6,0},{7,1},{8,14},{9,15},{10,... | collective-permute-start | bytes 98312 | tf_op jit(solution)/shard_map/ppermute | solution.py:54
  91.4 1.3 %collective-permute-start.33 = (bf16[16,8,128]{2,1,0:T(8,128)(2,1)S(1)}, bf16[16,8,128]{2,1,0:T(8,128)(2,1)S(1)}, u32[]{:S(2)}, u32[]{:S(2)}) collective-permute-start(bf16[16,8,128]{2,1,0:T(8,128)(2,1)S(1)} %get-tuple-element.78), channel_id=1, source_target_pairs={{0,4},{1,5},{2,6},{3,7},{4,0},{5,1},{6,2},{7,3},{8,12},{9,13},{10,... | collective-permute-start | bytes 98312 | tf_op jit(solution)/shard_map/ppermute | solution.py:54
  92.7 1.0 %collective-permute-start.34 = (bf16[16,8,128]{2,1,0:T(8,128)(2,1)S(1)}, bf16[16,8,128]{2,1,0:T(8,128)(2,1)S(1)}, u32[]{:S(2)}, u32[]{:S(2)}) collective-permute-start(bf16[16,8,128]{2,1,0:T(8,128)(2,1)S(1)} %get-tuple-element.77), channel_id=1, source_target_pairs={{0,2},{1,3},{2,0},{3,1},{4,6},{5,7},{6,4},{7,5},{8,10},{9,11},{10,... | collective-permute-start | bytes 98312 | tf_op jit(solution)/shard_map/ppermute | solution.py:54
  93.8 1.2 %collective-permute-done.32 = bf16[16,8,128]{2,1,0:T(8,128)(2,1)S(1)} collective-permute-done((bf16[16,8,128]{2,1,0:T(8,128)(2,1)S(1)}, bf16[16,8,128]{2,1,0:T(8,128)(2,1)S(1)}, u32[]{:S(2)}, u32[]{:S(2)}) %collective-permute-start.32) | collective-permute-done | bytes 32800 | tf_op jit(solution)/shard_map/ppermute | solution.py:54
  95.0 0.3 collective-permute-done.33
  95.3 1.4 %collective-permute-done.34 = bf16[16,8,128]{2,1,0:T(8,128)(2,1)S(1)} collective-permute-done((bf16[16,8,128]{2,1,0:T(8,128)(2,1)S(1)}, bf16[16,8,128]{2,1,0:T(8,128)(2,1)S(1)}, u32[]{:S(2)}, u32[]{:S(2)}) %collective-permute-start.34) | collective-permute-done | bytes 32800 | tf_op jit(solution)/shard_map/ppermute | solution.py:54
  97.4 0.9 copy.104
  (168 shorter events, 13.4 us)
Async XLA Ops:
  0.0 3.0 %copy-start = (bf16[256,64]{0,1:T(8,128)(2,1)S(1)}, bf16[256,64]{0,1:T(8,128)(2,1)}, u32[]{:S(2)}) copy-start(bf16[256,64]{0,1:T(8,128)(2,1)} %param.18) | copy-start | bytes 98308
  0.0 2.7 %copy-start.2 = (bf16[64,8,256]{2,1,0:T(8,128)(2,1)S(1)}, bf16[64,8,256]{2,1,0:T(8,128)(2,1)}, u32[]{:S(2)}) copy-start(bf16[64,8,256]{2,1,0:T(8,128)(2,1)} %param.13) | copy-start | bytes 786436
  3.4 7.3 %copy-start.3 = (bf16[2,128,640]{2,1,0:T(8,128)(2,1)S(1)}, bf16[2,128,640]{2,1,0:T(8,128)(2,1)}, u32[]{:S(2)}) copy-start(bf16[2,128,640]{2,1,0:T(8,128)(2,1)} %param.20) | copy-start | bytes 983044
  3.7 7.2 %collective-permute-start = (bf16[8,2112]{1,0:T(8,128)(2,1)S(1)}, bf16[8,2112]{1,0:T(8,128)(2,1)S(1)}, u32[]{:S(2)}, u32[]{:S(2)}) collective-permute-start(bf16[8,2112]{1,0:T(8,128)(2,1)S(1)} %pad_maximum_fusion.3), channel_id=1, source_target_pairs={{0,4},{1,5},{2,6},{3,7},{4,8},{5,9},{6,10},{7,11},{8,12},{9,13},{1... | collective-permute-start | bytes 101384 | tf_op jit(solution)/shard_map/ppermute | solution.py:28
  6.7 5.2 %collective-permute-start.1 = (bf16[8,2112]{1,0:T(8,128)(2,1)S(1)}, bf16[8,2112]{1,0:T(8,128)(2,1)S(1)}, u32[]{:S(2)}, u32[]{:S(2)}) collective-permute-start(bf16[8,2112]{1,0:T(8,128)(2,1)S(1)} %pad_maximum_fusion.3), channel_id=1, source_target_pairs={{0,8},{1,9},{2,10},{3,11},{4,12},{5,13},{6,14},{7,15},{8,0},{9,1},... | collective-permute-start | bytes 101384 | tf_op jit(solution)/shard_map/ppermute | solution.py:28
  9.3 3.9 %collective-permute-start.2 = (bf16[8,2112]{1,0:T(8,128)(2,1)S(1)}, bf16[8,2112]{1,0:T(8,128)(2,1)S(1)}, u32[]{:S(2)}, u32[]{:S(2)}) collective-permute-start(bf16[8,2112]{1,0:T(8,128)(2,1)S(1)} %pad_maximum_fusion.3), channel_id=1, source_target_pairs={{0,12},{1,13},{2,14},{3,15},{4,0},{5,1},{6,2},{7,3},{8,4},{9,5},{1... | collective-permute-start | bytes 101384 | tf_op jit(solution)/shard_map/ppermute | solution.py:28
  13.3 5.1 %collective-permute-start.3 = (bf16[4,8,2112]{2,1,0:T(8,128)(2,1)S(1)}, bf16[4,8,2112]{2,1,0:T(8,128)(2,1)S(1)}, u32[]{:S(2)}, u32[]{:S(2)}) collective-permute-start(bf16[4,8,2112]{2,1,0:T(8,128)(2,1)S(1)} %bitcast_dynamic-update-slice_fusion.16), channel_id=1, source_target_pairs={{0,2},{1,3},{2,0},{3,1},{4,6},{5,7},{6,4},{7,5},{8,10},{9,11},{10,... | collective-permute-start | bytes 405512 | tf_op jit(solution)/shard_map/ppermute | solution.py:32
  18.4 1.0 copy-start.4
  18.4 1.6 %collective-permute-start.4 = (bf16[4,2,8,2112]{3,2,1,0:T(8,128)(2,1)S(1)}, bf16[4,2,8,2112]{3,2,1,0:T(8,128)(2,1)S(1)}, u32[]{:S(2)}, u32[]{:S(2)}) collective-permute-start(bf16[4,2,8,2112]{3,2,1,0:T(8,128)(2,1)S(1)} %pad_maximum_fusion.2), channel_id=1, source_target_pairs={{0,1},{1,0},{2,3},{3,2},{4,5},{5,4},{6,7},{7,6},{8,9},{9,8},{10,11... | collective-permute-start | bytes 811016 | tf_op jit(solution)/shard_map/ppermute | solution.py:36
  18.6 0.7 copy-start.7
  20.2 0.7 copy-start.6
  21.3 1.0 copy-start.1
  22.3 5.1 %copy-start.8 = (bf16[66,128]{1,0:T(8,128)(2,1)S(1)}, bf16[66,128]{1,0:T(8,128)(2,1)}, u32[]{:S(2)}) copy-start(bf16[66,128]{1,0:T(8,128)(2,1)} %param.17) | copy-start | bytes 50692
  29.3 9.6 %collective-permute-start.5 = (bf16[2,16,8,128]{3,2,1,0:T(8,128)(2,1)S(1)}, bf16[2,16,8,128]{3,2,1,0:T(8,128)(2,1)S(1)}, u32[]{:S(2)}, u32[]{:S(2)}) collective-permute-start(bf16[2,16,8,128]{3,2,1,0:T(8,128)(2,1)S(1)} %get-tuple-element.72), channel_id=1, source_target_pairs={{0,14},{1,15},{2,12},{3,13},{4,10},{5,11},{6,8},{7,9},{8,6},{9,7},... | collective-permute-start | bytes 196616 | tf_op jit(solution)/shard_map/ppermute | solution.py:54
  33.4 6.8 %collective-permute-start.6 = (bf16[2,16,8,128]{3,2,1,0:T(8,128)(2,1)S(1)}, bf16[2,16,8,128]{3,2,1,0:T(8,128)(2,1)S(1)}, u32[]{:S(2)}, u32[]{:S(2)}) collective-permute-start(bf16[2,16,8,128]{3,2,1,0:T(8,128)(2,1)S(1)} %get-tuple-element.71), channel_id=1, source_target_pairs={{0,12},{1,13},{2,14},{3,15},{4,8},{5,9},{6,10},{7,11},{8,4},{9,5},... | collective-permute-start | bytes 196616 | tf_op jit(solution)/shard_map/ppermute | solution.py:54
  34.1 8.7 %collective-permute-start.7 = (bf16[2,16,8,128]{3,2,1,0:T(8,128)(2,1)S(1)}, bf16[2,16,8,128]{3,2,1,0:T(8,128)(2,1)S(1)}, u32[]{:S(2)}, u32[]{:S(2)}) collective-permute-start(bf16[2,16,8,128]{3,2,1,0:T(8,128)(2,1)S(1)} %get-tuple-element.70), channel_id=1, source_target_pairs={{0,10},{1,11},{2,8},{3,9},{4,14},{5,15},{6,12},{7,13},{8,2},{9,3},... | collective-permute-start | bytes 196616 | tf_op jit(solution)/shard_map/ppermute | solution.py:54
  34.1 10.2 %collective-permute-start.8 = (bf16[2,16,8,128]{3,2,1,0:T(8,128)(2,1)S(1)}, bf16[2,16,8,128]{3,2,1,0:T(8,128)(2,1)S(1)}, u32[]{:S(2)}, u32[]{:S(2)}) collective-permute-start(bf16[2,16,8,128]{3,2,1,0:T(8,128)(2,1)S(1)} %get-tuple-element.69), channel_id=1, source_target_pairs={{0,8},{1,9},{2,10},{3,11},{4,12},{5,13},{6,14},{7,15},{8,0},{9,1},... | collective-permute-start | bytes 196616 | tf_op jit(solution)/shard_map/ppermute | solution.py:54
  37.0 7.3 %collective-permute-start.9 = (bf16[2,16,8,128]{3,2,1,0:T(8,128)(2,1)S(1)}, bf16[2,16,8,128]{3,2,1,0:T(8,128)(2,1)S(1)}, u32[]{:S(2)}, u32[]{:S(2)}) collective-permute-start(bf16[2,16,8,128]{3,2,1,0:T(8,128)(2,1)S(1)} %get-tuple-element.68), channel_id=1, source_target_pairs={{0,6},{1,7},{2,4},{3,5},{4,2},{5,3},{6,0},{7,1},{8,14},{9,15},{10,... | collective-permute-start | bytes 196616 | tf_op jit(solution)/shard_map/ppermute | solution.py:54
  38.9 6.0 %collective-permute-start.10 = (bf16[2,16,8,128]{3,2,1,0:T(8,128)(2,1)S(1)}, bf16[2,16,8,128]{3,2,1,0:T(8,128)(2,1)S(1)}, u32[]{:S(2)}, u32[]{:S(2)}) collective-permute-start(bf16[2,16,8,128]{3,2,1,0:T(8,128)(2,1)S(1)} %get-tuple-element.67), channel_id=1, source_target_pairs={{0,4},{1,5},{2,6},{3,7},{4,0},{5,1},{6,2},{7,3},{8,12},{9,13},{10,... | collective-permute-start | bytes 196616 | tf_op jit(solution)/shard_map/ppermute | solution.py:54
  40.2 4.7 %collective-permute-start.11 = (bf16[2,16,8,128]{3,2,1,0:T(8,128)(2,1)S(1)}, bf16[2,16,8,128]{3,2,1,0:T(8,128)(2,1)S(1)}, u32[]{:S(2)}, u32[]{:S(2)}) collective-permute-start(bf16[2,16,8,128]{3,2,1,0:T(8,128)(2,1)S(1)} %get-tuple-element.66), channel_id=1, source_target_pairs={{0,2},{1,3},{2,0},{3,1},{4,6},{5,7},{6,4},{7,5},{8,10},{9,11},{10,... | collective-permute-start | bytes 196616 | tf_op jit(solution)/shard_map/ppermute | solution.py:54
  45.0 1.6 %collective-permute-start.12 = (bf16[16,8,8,128]{3,2,1,0:T(8,128)(2,1)S(1)}, bf16[16,8,8,128]{3,2,1,0:T(8,128)(2,1)S(1)}, u32[]{:S(2)}, u32[]{:S(2)}) collective-permute-start(bf16[16,8,8,128]{3,2,1,0:T(8,128)(2,1)S(1)} %slice_bitcast_fusion.4), channel_id=1, source_target_pairs={{0,1},{1,0},{2,3},{3,2},{4,5},{5,4},{6,7},{7,6},{8,9},{9,8},{10,11... | collective-permute-start | bytes 786440 | tf_op jit(solution)/shard_map/ppermute | solution.py:62
  47.3 9.1 %collective-permute-start.13 = (bf16[16,8,128]{2,1,0:T(8,128)(2,1)S(1)}, bf16[16,8,128]{2,1,0:T(8,128)(2,1)S(1)}, u32[]{:S(2)}, u32[]{:S(2)}) collective-permute-start(bf16[16,8,128]{2,1,0:T(8,128)(2,1)S(1)} %get-tuple-element.90), channel_id=1, source_target_pairs={{0,14},{1,15},{2,12},{3,13},{4,10},{5,11},{6,8},{7,9},{8,6},{9,7},... | collective-permute-start | bytes 98312 | tf_op jit(solution)/shard_map/ppermute | solution.py:54
  51.0 6.7 %collective-permute-start.14 = (bf16[16,8,128]{2,1,0:T(8,128)(2,1)S(1)}, bf16[16,8,128]{2,1,0:T(8,128)(2,1)S(1)}, u32[]{:S(2)}, u32[]{:S(2)}) collective-permute-start(bf16[16,8,128]{2,1,0:T(8,128)(2,1)S(1)} %get-tuple-element.89), channel_id=1, source_target_pairs={{0,12},{1,13},{2,14},{3,15},{4,8},{5,9},{6,10},{7,11},{8,4},{9,5},... | collective-permute-start | bytes 98312 | tf_op jit(solution)/shard_map/ppermute | solution.py:54
  51.8 6.9 %collective-permute-start.15 = (bf16[16,8,128]{2,1,0:T(8,128)(2,1)S(1)}, bf16[16,8,128]{2,1,0:T(8,128)(2,1)S(1)}, u32[]{:S(2)}, u32[]{:S(2)}) collective-permute-start(bf16[16,8,128]{2,1,0:T(8,128)(2,1)S(1)} %get-tuple-element.88), channel_id=1, source_target_pairs={{0,10},{1,11},{2,8},{3,9},{4,14},{5,15},{6,12},{7,13},{8,2},{9,3},... | collective-permute-start | bytes 98312 | tf_op jit(solution)/shard_map/ppermute | solution.py:54
  51.8 6.9 %collective-permute-start.16 = (bf16[16,8,128]{2,1,0:T(8,128)(2,1)S(1)}, bf16[16,8,128]{2,1,0:T(8,128)(2,1)S(1)}, u32[]{:S(2)}, u32[]{:S(2)}) collective-permute-start(bf16[16,8,128]{2,1,0:T(8,128)(2,1)S(1)} %get-tuple-element.87), channel_id=1, source_target_pairs={{0,8},{1,9},{2,10},{3,11},{4,12},{5,13},{6,14},{7,15},{8,0},{9,1},... | collective-permute-start | bytes 98312 | tf_op jit(solution)/shard_map/ppermute | solution.py:54
  55.1 4.8 %collective-permute-start.17 = (bf16[16,8,128]{2,1,0:T(8,128)(2,1)S(1)}, bf16[16,8,128]{2,1,0:T(8,128)(2,1)S(1)}, u32[]{:S(2)}, u32[]{:S(2)}) collective-permute-start(bf16[16,8,128]{2,1,0:T(8,128)(2,1)S(1)} %get-tuple-element.86), channel_id=1, source_target_pairs={{0,6},{1,7},{2,4},{3,5},{4,2},{5,3},{6,0},{7,1},{8,14},{9,15},{10,... | collective-permute-start | bytes 98312 | tf_op jit(solution)/shard_map/ppermute | solution.py:54
  56.3 3.9 %collective-permute-start.18 = (bf16[16,8,128]{2,1,0:T(8,128)(2,1)S(1)}, bf16[16,8,128]{2,1,0:T(8,128)(2,1)S(1)}, u32[]{:S(2)}, u32[]{:S(2)}) collective-permute-start(bf16[16,8,128]{2,1,0:T(8,128)(2,1)S(1)} %get-tuple-element.85), channel_id=1, source_target_pairs={{0,4},{1,5},{2,6},{3,7},{4,0},{5,1},{6,2},{7,3},{8,12},{9,13},{10,... | collective-permute-start | bytes 98312 | tf_op jit(solution)/shard_map/ppermute | solution.py:54
  57.7 4.0 %collective-permute-start.19 = (bf16[16,8,128]{2,1,0:T(8,128)(2,1)S(1)}, bf16[16,8,128]{2,1,0:T(8,128)(2,1)S(1)}, u32[]{:S(2)}, u32[]{:S(2)}) collective-permute-start(bf16[16,8,128]{2,1,0:T(8,128)(2,1)S(1)} %get-tuple-element.84), channel_id=1, source_target_pairs={{0,2},{1,3},{2,0},{3,1},{4,6},{5,7},{6,4},{7,5},{8,10},{9,11},{10,... | collective-permute-start | bytes 98312 | tf_op jit(solution)/shard_map/ppermute | solution.py:54
  62.0 0.8 copy-start.5
  64.9 9.2 %collective-permute-start.20 = (bf16[2,16,8,128]{3,2,1,0:T(8,128)(2,1)S(1)}, bf16[2,16,8,128]{3,2,1,0:T(8,128)(2,1)S(1)}, u32[]{:S(2)}, u32[]{:S(2)}) collective-permute-start(bf16[2,16,8,128]{3,2,1,0:T(8,128)(2,1)S(1)} %get-tuple-element.65), channel_id=1, source_target_pairs={{0,14},{1,15},{2,12},{3,13},{4,10},{5,11},{6,8},{7,9},{8,6},{9,7},... | collective-permute-start | bytes 196616 | tf_op jit(solution)/shard_map/ppermute | solution.py:54
  68.7 6.6 %collective-permute-start.21 = (bf16[2,16,8,128]{3,2,1,0:T(8,128)(2,1)S(1)}, bf16[2,16,8,128]{3,2,1,0:T(8,128)(2,1)S(1)}, u32[]{:S(2)}, u32[]{:S(2)}) collective-permute-start(bf16[2,16,8,128]{3,2,1,0:T(8,128)(2,1)S(1)} %get-tuple-element.64), channel_id=1, source_target_pairs={{0,12},{1,13},{2,14},{3,15},{4,8},{5,9},{6,10},{7,11},{8,4},{9,5},... | collective-permute-start | bytes 196616 | tf_op jit(solution)/shard_map/ppermute | solution.py:54
  69.2 8.2 %collective-permute-start.22 = (bf16[2,16,8,128]{3,2,1,0:T(8,128)(2,1)S(1)}, bf16[2,16,8,128]{3,2,1,0:T(8,128)(2,1)S(1)}, u32[]{:S(2)}, u32[]{:S(2)}) collective-permute-start(bf16[2,16,8,128]{3,2,1,0:T(8,128)(2,1)S(1)} %get-tuple-element.63), channel_id=1, source_target_pairs={{0,10},{1,11},{2,8},{3,9},{4,14},{5,15},{6,12},{7,13},{8,2},{9,3},... | collective-permute-start | bytes 196616 | tf_op jit(solution)/shard_map/ppermute | solution.py:54
  69.5 9.1 %collective-permute-start.23 = (bf16[2,16,8,128]{3,2,1,0:T(8,128)(2,1)S(1)}, bf16[2,16,8,128]{3,2,1,0:T(8,128)(2,1)S(1)}, u32[]{:S(2)}, u32[]{:S(2)}) collective-permute-start(bf16[2,16,8,128]{3,2,1,0:T(8,128)(2,1)S(1)} %get-tuple-element.62), channel_id=1, source_target_pairs={{0,8},{1,9},{2,10},{3,11},{4,12},{5,13},{6,14},{7,15},{8,0},{9,1},... | collective-permute-start | bytes 196616 | tf_op jit(solution)/shard_map/ppermute | solution.py:54
  72.6 6.1 %collective-permute-start.24 = (bf16[2,16,8,128]{3,2,1,0:T(8,128)(2,1)S(1)}, bf16[2,16,8,128]{3,2,1,0:T(8,128)(2,1)S(1)}, u32[]{:S(2)}, u32[]{:S(2)}) collective-permute-start(bf16[2,16,8,128]{3,2,1,0:T(8,128)(2,1)S(1)} %get-tuple-element.61), channel_id=1, source_target_pairs={{0,6},{1,7},{2,4},{3,5},{4,2},{5,3},{6,0},{7,1},{8,14},{9,15},{10,... | collective-permute-start | bytes 196616 | tf_op jit(solution)/shard_map/ppermute | solution.py:54
  74.2 5.0 %collective-permute-start.25 = (bf16[2,16,8,128]{3,2,1,0:T(8,128)(2,1)S(1)}, bf16[2,16,8,128]{3,2,1,0:T(8,128)(2,1)S(1)}, u32[]{:S(2)}, u32[]{:S(2)}) collective-permute-start(bf16[2,16,8,128]{3,2,1,0:T(8,128)(2,1)S(1)} %get-tuple-element.60), channel_id=1, source_target_pairs={{0,4},{1,5},{2,6},{3,7},{4,0},{5,1},{6,2},{7,3},{8,12},{9,13},{10,... | collective-permute-start | bytes 196616 | tf_op jit(solution)/shard_map/ppermute | solution.py:54
  75.3 4.3 %collective-permute-start.26 = (bf16[2,16,8,128]{3,2,1,0:T(8,128)(2,1)S(1)}, bf16[2,16,8,128]{3,2,1,0:T(8,128)(2,1)S(1)}, u32[]{:S(2)}, u32[]{:S(2)}) collective-permute-start(bf16[2,16,8,128]{3,2,1,0:T(8,128)(2,1)S(1)} %get-tuple-element.59), channel_id=1, source_target_pairs={{0,2},{1,3},{2,0},{3,1},{4,6},{5,7},{6,4},{7,5},{8,10},{9,11},{10,... | collective-permute-start | bytes 196616 | tf_op jit(solution)/shard_map/ppermute | solution.py:54
  80.2 2.0 %collective-permute-start.27 = (f32[16,8,8,128]{3,2,0,1:T(8,128)S(1)}, f32[16,8,8,128]{3,2,0,1:T(8,128)S(1)}, u32[]{:S(2)}, u32[]{:S(2)}) collective-permute-start(f32[16,8,8,128]{3,2,0,1:T(8,128)S(1)} %select_bitcast_fusion), channel_id=1, source_target_pairs={{0,1},{1,0},{2,3},{3,2},{4,5},{5,4},{6,7},{7,6},{8,9},{9,8},{10,11... | collective-permute-start | bytes 1572872 | tf_op jit(solution)/shard_map/ppermute | solution.py:62
  82.3 9.1 %collective-permute-start.28 = (bf16[16,8,128]{2,1,0:T(8,128)(2,1)S(1)}, bf16[16,8,128]{2,1,0:T(8,128)(2,1)S(1)}, u32[]{:S(2)}, u32[]{:S(2)}) collective-permute-start(bf16[16,8,128]{2,1,0:T(8,128)(2,1)S(1)} %get-tuple-element.83), channel_id=1, source_target_pairs={{0,14},{1,15},{2,12},{3,13},{4,10},{5,11},{6,8},{7,9},{8,6},{9,7},... | collective-permute-start | bytes 98312 | tf_op jit(solution)/shard_map/ppermute | solution.py:54
  86.0 6.7 %collective-permute-start.29 = (bf16[16,8,128]{2,1,0:T(8,128)(2,1)S(1)}, bf16[16,8,128]{2,1,0:T(8,128)(2,1)S(1)}, u32[]{:S(2)}, u32[]{:S(2)}) collective-permute-start(bf16[16,8,128]{2,1,0:T(8,128)(2,1)S(1)} %get-tuple-element.82), channel_id=1, source_target_pairs={{0,12},{1,13},{2,14},{3,15},{4,8},{5,9},{6,10},{7,11},{8,4},{9,5},... | collective-permute-start | bytes 98312 | tf_op jit(solution)/shard_map/ppermute | solution.py:54
  86.8 6.9 %collective-permute-start.30 = (bf16[16,8,128]{2,1,0:T(8,128)(2,1)S(1)}, bf16[16,8,128]{2,1,0:T(8,128)(2,1)S(1)}, u32[]{:S(2)}, u32[]{:S(2)}) collective-permute-start(bf16[16,8,128]{2,1,0:T(8,128)(2,1)S(1)} %get-tuple-element.81), channel_id=1, source_target_pairs={{0,10},{1,11},{2,8},{3,9},{4,14},{5,15},{6,12},{7,13},{8,2},{9,3},... | collective-permute-start | bytes 98312 | tf_op jit(solution)/shard_map/ppermute | solution.py:54
  87.3 6.4 %collective-permute-start.31 = (bf16[16,8,128]{2,1,0:T(8,128)(2,1)S(1)}, bf16[16,8,128]{2,1,0:T(8,128)(2,1)S(1)}, u32[]{:S(2)}, u32[]{:S(2)}) collective-permute-start(bf16[16,8,128]{2,1,0:T(8,128)(2,1)S(1)} %get-tuple-element.80), channel_id=1, source_target_pairs={{0,8},{1,9},{2,10},{3,11},{4,12},{5,13},{6,14},{7,15},{8,0},{9,1},... | collective-permute-start | bytes 98312 | tf_op jit(solution)/shard_map/ppermute | solution.py:54
  90.2 4.8 %collective-permute-start.32 = (bf16[16,8,128]{2,1,0:T(8,128)(2,1)S(1)}, bf16[16,8,128]{2,1,0:T(8,128)(2,1)S(1)}, u32[]{:S(2)}, u32[]{:S(2)}) collective-permute-start(bf16[16,8,128]{2,1,0:T(8,128)(2,1)S(1)} %get-tuple-element.79), channel_id=1, source_target_pairs={{0,6},{1,7},{2,4},{3,5},{4,2},{5,3},{6,0},{7,1},{8,14},{9,15},{10,... | collective-permute-start | bytes 98312 | tf_op jit(solution)/shard_map/ppermute | solution.py:54
  91.4 3.9 %collective-permute-start.33 = (bf16[16,8,128]{2,1,0:T(8,128)(2,1)S(1)}, bf16[16,8,128]{2,1,0:T(8,128)(2,1)S(1)}, u32[]{:S(2)}, u32[]{:S(2)}) collective-permute-start(bf16[16,8,128]{2,1,0:T(8,128)(2,1)S(1)} %get-tuple-element.78), channel_id=1, source_target_pairs={{0,4},{1,5},{2,6},{3,7},{4,0},{5,1},{6,2},{7,3},{8,12},{9,13},{10,... | collective-permute-start | bytes 98312 | tf_op jit(solution)/shard_map/ppermute | solution.py:54
  92.7 4.0 %collective-permute-start.34 = (bf16[16,8,128]{2,1,0:T(8,128)(2,1)S(1)}, bf16[16,8,128]{2,1,0:T(8,128)(2,1)S(1)}, u32[]{:S(2)}, u32[]{:S(2)}) collective-permute-start(bf16[16,8,128]{2,1,0:T(8,128)(2,1)S(1)} %get-tuple-element.77), channel_id=1, source_target_pairs={{0,2},{1,3},{2,0},{3,1},{4,6},{5,7},{6,4},{7,5},{8,10},{9,11},{10,... | collective-permute-start | bytes 98312 | tf_op jit(solution)/shard_map/ppermute | solution.py:54

commit v3 on v2

--- a/solution.py
+++ b/solution.py
@@ -41,20 +41,9 @@
 
 
 def chip_exchange(blocks):
-    chips = blocks.shape[0]
     count = lax.axis_size("wide")
-    here = lax.axis_index("wide") // 2
-    held = lax.dynamic_update_index_in_dim(
-        jnp.zeros_like(blocks), lax.dynamic_index_in_dim(blocks, here, 0, False), here, 0
-    )
-    arrived = []
-    for step in range(chips - 1, 0, -1):
-        piece = lax.dynamic_index_in_dim(blocks, here ^ step, 0, False)
-        pairs = [(w, w ^ (2 * step)) for w in range(count)]
-        arrived.append((step, lax.ppermute(piece, "wide", pairs)))
-    for step, piece in arrived:
-        held = lax.dynamic_update_index_in_dim(held, piece, here ^ step, 0)
-    return held
+    groups = [list(range(core, count, 2)) for core in range(2)]
+    return lax.all_to_all(blocks, "wide", 0, 0, axis_index_groups=groups, tiled=True)
 
 
 def core_swap(block):

time: 98.5 us -> 104 us (1.056)
  starting transfers between devices: 54 us -> 16 us
  blocking collectives: 0 us -> 37.5 us
  waiting for transfers between devices: 21.7 us -> 27.4 us
    ppermute x28 -> x0, starting transfers between devices: 45.3 us -> none  [chip_exchange(): arrived.append((step, lax.ppermute(piece, 'wide', pairs)))]
    all_to_all x0 -> x2, blocking collectives: none -> 37.5 us  [chip_exchange(): lax.all_to_all(blocks, 'wide', 0, 0, axis_index_groups=groups, tiled=True)]
    all_to_all x0 -> x2, waiting for transfers between devices: none -> 17.8 us  [chip_exchange(): lax.all_to_all(blocks, 'wide', 0, 0, axis_index_groups=groups, tiled=True)]
    ppermute x28 -> x0, waiting for transfers between devices: 12.8 us -> none  [chip_exchange(): arrived.append((step, lax.ppermute(piece, 'wide', pairs)))]
    all_to_all x0 -> x2, starting transfers between devices: none -> 7.27 us  [chip_exchange(): lax.all_to_all(blocks, 'wide', 0, 0, axis_index_groups=groups, tiled=True)]
    unnamed x22 -> x20, local copies, waits for them, and re-layouts: 3.36 us -> 3.05 us
  transfers between devices with their start and end apart: 35 -> 9, of which waited for: 20 -> 8; matrix products, arithmetic and copies ran while one was open for 2% -> 1% of each run, Pallas kernels for 0% -> 0%
where the time goes in v3:
time: 104 us; the launch traced here: 103 us
  blocking collectives  37.5 us (36%)
  waiting for transfers between devices  27.4 us (26%)
  starting transfers between devices  16 us (15%)
  matrix products  8.95 us (9%)
  local copies, waits for them, and re-layouts  7.22 us (7%)
  other arithmetic  5.23 us (5%)
    all_to_all x2, blocking collectives, chip_exchange(): lax.all_to_all(blocks, 'wide', 0, 0, axis_index_groups=groups, tiled=True)  37.5 us
    all_to_all x2, waiting for transfers between devices, chip_exchange(): lax.all_to_all(blocks, 'wide', 0, 0, axis_index_groups=groups, tiled=True)  17.8 us
    all_to_all x2, starting transfers between devices, chip_exchange(): lax.all_to_all(blocks, 'wide', 0, 0, axis_index_groups=groups, tiled=True)  7.27 us
    ppermute x3, starting transfers between devices, gather_wide(): arrived.append(lax.ppermute(block, 'wide', perm))  7.01 us
    ppermute x1, waiting for transfers between devices, gather_wide(): other = lax.ppermute(held, 'wide', [(w, w ^ 2) for w in range(n)])  3.49 us
    ppermute x2, waiting for transfers between devices, core_swap(): return lax.ppermute(block, 'wide', [(w, w ^ 1) for w in range(count)])  3.42 us
    unnamed x20, local copies, waits for them, and re-layouts  3.05 us
    ppermute x3, waiting for transfers between devices, gather_wide(): arrived.append(lax.ppermute(block, 'wide', perm))  2.38 us
  transfers between devices with their start and end apart: 9, of which 8 were waited for; matrix products, arithmetic and copies ran while one was open for 1% of the time, Pallas kernels for 0%

profile of v3, /device:TPU:0, one launch (start us, length us, event | category | flops | bytes accessed | tf_op | source)
XLA Modules:
  0.0 103.1 jit_solution(8514439036172086509)
XLA Ops:
  0.0 0.7 convert_element_type.89
  0.8 0.8 convert_bitcast_fusion
  1.6 1.1 %convert_reduce_fusion.2 = f32[64,8]{1,0:T(8,128)S(1)} fusion(bf16[64,8,256]{2,1,0:T(8,128)(2,1)} %param.13), kind=kLoop, calls=%fused_computation.60 | loop fusion | flops 261632 | bytes 264192 | tf_op jit(solution)/shard_map/reduce_sum | solution.py:13
  2.7 0.2 fusion.47
  3.0 0.3 fusion.36
  3.5 0.2 reshape.178
  3.7 3.1 %collective-permute-start = (bf16[8,2112]{1,0:T(8,128)(2,1)S(1)}, bf16[8,2112]{1,0:T(8,128)(2,1)S(1)}, u32[]{:S(2)}, u32[]{:S(2)}) collective-permute-start(bf16[8,2112]{1,0:T(8,128)(2,1)S(1)} %pad_maximum_fusion.5), channel_id=1, source_target_pairs={{0,4},{1,5},{2,6},{3,7},{4,8},{5,9},{6,10},{7,11},{8,12},{9,13},{1... | collective-permute-start | bytes 101384 | tf_op jit(solution)/shard_map/ppermute | solution.py:28
  6.7 2.6 %collective-permute-start.1 = (bf16[8,2112]{1,0:T(8,128)(2,1)S(1)}, bf16[8,2112]{1,0:T(8,128)(2,1)S(1)}, u32[]{:S(2)}, u32[]{:S(2)}) collective-permute-start(bf16[8,2112]{1,0:T(8,128)(2,1)S(1)} %pad_maximum_fusion.5), channel_id=1, source_target_pairs={{0,8},{1,9},{2,10},{3,11},{4,12},{5,13},{6,14},{7,15},{8,0},{9,1},... | collective-permute-start | bytes 101384 | tf_op jit(solution)/shard_map/ppermute | solution.py:28
  9.3 1.3 %collective-permute-start.2 = (bf16[8,2112]{1,0:T(8,128)(2,1)S(1)}, bf16[8,2112]{1,0:T(8,128)(2,1)S(1)}, u32[]{:S(2)}, u32[]{:S(2)}) collective-permute-start(bf16[8,2112]{1,0:T(8,128)(2,1)S(1)} %pad_maximum_fusion.5), channel_id=1, source_target_pairs={{0,12},{1,13},{2,14},{3,15},{4,0},{5,1},{6,2},{7,3},{8,4},{9,5},{1... | collective-permute-start | bytes 101384 | tf_op jit(solution)/shard_map/ppermute | solution.py:28
  10.9 1.1 %collective-permute-done.1 = bf16[8,2112]{1,0:T(8,128)(2,1)S(1)} collective-permute-done((bf16[8,2112]{1,0:T(8,128)(2,1)S(1)}, bf16[8,2112]{1,0:T(8,128)(2,1)S(1)}, u32[]{:S(2)}, u32[]{:S(2)}) %collective-permute-start.1) | collective-permute-done | bytes 33824 | tf_op jit(solution)/shard_map/ppermute | solution.py:28
  12.0 1.3 %collective-permute-done.2 = bf16[8,2112]{1,0:T(8,128)(2,1)S(1)} collective-permute-done((bf16[8,2112]{1,0:T(8,128)(2,1)S(1)}, bf16[8,2112]{1,0:T(8,128)(2,1)S(1)}, u32[]{:S(2)}, u32[]{:S(2)}) %collective-permute-start.2) | collective-permute-done | bytes 33824 | tf_op jit(solution)/shard_map/ppermute | solution.py:28
  13.3 1.5 %collective-permute-start.3 = (bf16[4,8,2112]{2,1,0:T(8,128)(2,1)S(1)}, bf16[4,8,2112]{2,1,0:T(8,128)(2,1)S(1)}, u32[]{:S(2)}, u32[]{:S(2)}) collective-permute-start(bf16[4,8,2112]{2,1,0:T(8,128)(2,1)S(1)} %bitcast_dynamic-update-slice_fusion), channel_id=1, source_target_pairs={{0,2},{1,3},{2,0},{3,1},{4,6},{5,7},{6,4},{7,5},{8,10},{9,11},{10,... | collective-permute-start | bytes 405512 | tf_op jit(solution)/shard_map/ppermute | solution.py:32
  14.8 3.5 %collective-permute-done.3 = bf16[4,8,2112]{2,1,0:T(8,128)(2,1)S(1)} collective-permute-done((bf16[4,8,2112]{2,1,0:T(8,128)(2,1)S(1)}, bf16[4,8,2112]{2,1,0:T(8,128)(2,1)S(1)}, u32[]{:S(2)}, u32[]{:S(2)}) %collective-permute-start.3) | collective-permute-done | bytes 135200 | tf_op jit(solution)/shard_map/ppermute | solution.py:32
  18.7 0.5 copy-done.7
  19.3 0.2 copy.83
  19.8 0.3 collective-permute-done.4
  20.3 0.6 copy-done.6
  21.0 0.3 copy.88
  21.4 0.2 copy.90
  21.6 0.7 copy-done.1
  22.3 5.0 %while.10 = (s32[]{:T(128)}, f32[8,128,128]{1,2,0:T(8,128)S(1)}, bf16[8,64,32]{1,2,0:T(8,128)(2,1)S(1)}, bf16[64,128,32]{1,0,2:T(8,128)(2,1)S(1)}, bf16[1024,128]{1,0:T(8,128)(2,1)S(1)}, /*index=5*/s32[]{:T(128)}) while((s32[]{:T(128)}, f32[8,128,128]{1,2,0:T(8,128)S(1)}, bf16[8,64,32]{1,2,0:T(8,128)(2,1)S(1)}, ...), condition=%wide.region_3.4_spmd, body=%wide.region_2.3_spmd.sunk | while | flops 50462720 | bytes 1908813 | solution.py:194
  22.3 0.2 fusion.101
  22.6 0.3 fusion.102
  22.9 0.2 fusion.101
  23.3 0.3 fusion.102
  23.6 0.2 fusion.101
  23.9 0.3 fusion.102
  24.2 0.2 fusion.101
  24.5 0.3 fusion.102
  24.8 0.2 fusion.101
  25.2 0.3 fusion.102
  25.5 0.2 fusion.101
  25.8 0.3 fusion.102
  26.1 0.2 fusion.101
  26.4 0.3 fusion.102
  26.7 0.2 fusion.101
  27.1 0.3 fusion.102
  27.4 0.3 fusion.75
  27.8 0.3 fusion.10
  28.1 0.3 fusion.7
  28.4 0.2 fusion.31
  28.6 0.2 fusion.30
  29.0 19.9 %all_to_all.20 = bf16[8,2,16,8,128]{4,2,3,1,0:T(8,128)(2,1)S(1)} all-to-all(bf16[8,2,16,8,128]{4,2,3,1,0:T(8,128)(2,1)S(1)} %copy.140), channel_id=1, replica_groups={{0,2,4,6,8,10,12,14},{1,3,5,7,9,11,13,15},{16,18,20,22,24,26,28,30},{17..., dimensions={0} | all-to-all | bytes 1048576 | tf_op jit(solution)/shard_map/all_to_all | solution.py:46
  49.0 1.5 %collective-permute-done.5 = bf16[16,8,8,128]{3,0,2,1:T(8,128)(2,1)S(1)} collective-permute-done((bf16[16,8,8,128]{3,0,2,1:T(8,128)(2,1)S(1)}, bf16[16,8,8,128]{3,0,2,1:T(8,128)(2,1)S(1)}, u32[]{:S(2)}, u32[]{:S(2)}) %collective-permute-start.5) | collective-permute-done | bytes 262176 | tf_op jit(solution)/shard_map/ppermute | solution.py:51
  50.8 0.5 fusion.35
  51.3 0.8 copy.189
  52.1 3.6 %all-to-all-start.1 = ((bf16[8,16,8,128]{3,2,1,0:T(8,128)(2,1)}), bf16[8,16,8,128]{3,2,1,0:T(8,128)(2,1)S(1)}, u32[]{:S(2)}, u32[]{:S(2)}) async-start(bf16[8,16,8,128]{3,2,1,0:T(8,128)(2,1)} %bitcast.159), calls=%async_computation.1 | async-start | bytes 524288 | tf_op jit(solution)/shard_map/all_to_all | solution.py:46
  55.7 0.3 fusion.13
  56.0 8.9 %all-to-all-done.1 = bf16[8,16,8,128]{3,2,1,0:T(8,128)(2,1)S(1)} async-done(((bf16[8,16,8,128]{3,2,1,0:T(8,128)(2,1)}), bf16[8,16,8,128]{3,2,1,0:T(8,128)(2,1)S(1)}, u32[]{:S(2)}, u32[]{:S(2)}) %all-to-all-start.1) | async-done | bytes 262176 | tf_op jit(solution)/shard_map/all_to_all | solution.py:46
  65.3 0.8 copy-done.5
  66.1 0.3 fusion.76
  66.5 0.3 fusion.19
  66.8 0.3 fusion.16
  67.2 0.3 fusion.34
  67.5 0.3 fusion.33
  67.8 17.5 %all_to_all.21 = bf16[8,2,16,8,128]{4,2,3,1,0:T(8,128)(2,1)S(1)} all-to-all(bf16[8,2,16,8,128]{4,2,3,1,0:T(8,128)(2,1)S(1)} %copy.145), channel_id=1, replica_groups={{0,2,4,6,8,10,12,14},{1,3,5,7,9,11,13,15},{16,18,20,22,24,26,28,30},{17..., dimensions={0} | all-to-all | bytes 1048576 | tf_op jit(solution)/shard_map/all_to_all | solution.py:46
  85.4 0.4 fusion.52
  86.1 1.9 %collective-permute-done.6 = f32[16,8,8,128]{3,2,0,1:T(8,128)S(1)} collective-permute-done((f32[16,8,8,128]{3,2,0,1:T(8,128)S(1)}, f32[16,8,8,128]{3,2,0,1:T(8,128)S(1)}, u32[]{:S(2)}, u32[]{:S(2)}) %collective-permute-start.6) | collective-permute-done | bytes 524320 | tf_op jit(solution)/shard_map/ppermute | solution.py:51
  88.0 0.8 fusion.50
  88.7 3.6 %all-to-all-start.3 = ((bf16[8,16,8,128]{3,2,1,0:T(8,128)(2,1)}), bf16[8,16,8,128]{3,2,1,0:T(8,128)(2,1)S(1)}, u32[]{:S(2)}, u32[]{:S(2)}) async-start(bf16[8,16,8,128]{3,2,1,0:T(8,128)(2,1)} %fusion.50), calls=%async_computation.3 | async-start | bytes 524288 | tf_op jit(solution)/shard_map/all_to_all | solution.py:46
  92.4 0.3 fusion.22
  92.7 8.9 %all-to-all-done.3 = bf16[8,16,8,128]{3,2,1,0:T(8,128)(2,1)S(1)} async-done(((bf16[8,16,8,128]{3,2,1,0:T(8,128)(2,1)}), bf16[8,16,8,128]{3,2,1,0:T(8,128)(2,1)S(1)}, u32[]{:S(2)}, u32[]{:S(2)}) %all-to-all-start.3) | async-done | bytes 262176 | tf_op jit(solution)/shard_map/all_to_all | solution.py:46
  102.0 0.3 fusion.32
  102.2 0.9 copy.123
  (81 shorter events, 4.2 us)
Async XLA Ops:
  0.0 3.0 %copy-start = (bf16[256,64]{0,1:T(8,128)(2,1)S(1)}, bf16[256,64]{0,1:T(8,128)(2,1)}, u32[]{:S(2)}) copy-start(bf16[256,64]{0,1:T(8,128)(2,1)} %param.18) | copy-start | bytes 98308
  0.0 2.7 %copy-start.2 = (bf16[64,8,256]{2,1,0:T(8,128)(2,1)S(1)}, bf16[64,8,256]{2,1,0:T(8,128)(2,1)}, u32[]{:S(2)}) copy-start(bf16[64,8,256]{2,1,0:T(8,128)(2,1)} %param.13) | copy-start | bytes 786436
  3.4 7.3 %copy-start.3 = (bf16[2,128,640]{2,1,0:T(8,128)(2,1)S(1)}, bf16[2,128,640]{2,1,0:T(8,128)(2,1)}, u32[]{:S(2)}) copy-start(bf16[2,128,640]{2,1,0:T(8,128)(2,1)} %param.20) | copy-start | bytes 983044
  3.7 7.2 %collective-permute-start = (bf16[8,2112]{1,0:T(8,128)(2,1)S(1)}, bf16[8,2112]{1,0:T(8,128)(2,1)S(1)}, u32[]{:S(2)}, u32[]{:S(2)}) collective-permute-start(bf16[8,2112]{1,0:T(8,128)(2,1)S(1)} %pad_maximum_fusion.5), channel_id=1, source_target_pairs={{0,4},{1,5},{2,6},{3,7},{4,8},{5,9},{6,10},{7,11},{8,12},{9,13},{1... | collective-permute-start | bytes 101384 | tf_op jit(solution)/shard_map/ppermute | solution.py:28
  6.7 5.2 %collective-permute-start.1 = (bf16[8,2112]{1,0:T(8,128)(2,1)S(1)}, bf16[8,2112]{1,0:T(8,128)(2,1)S(1)}, u32[]{:S(2)}, u32[]{:S(2)}) collective-permute-start(bf16[8,2112]{1,0:T(8,128)(2,1)S(1)} %pad_maximum_fusion.5), channel_id=1, source_target_pairs={{0,8},{1,9},{2,10},{3,11},{4,12},{5,13},{6,14},{7,15},{8,0},{9,1},... | collective-permute-start | bytes 101384 | tf_op jit(solution)/shard_map/ppermute | solution.py:28
  9.3 3.9 %collective-permute-start.2 = (bf16[8,2112]{1,0:T(8,128)(2,1)S(1)}, bf16[8,2112]{1,0:T(8,128)(2,1)S(1)}, u32[]{:S(2)}, u32[]{:S(2)}) collective-permute-start(bf16[8,2112]{1,0:T(8,128)(2,1)S(1)} %pad_maximum_fusion.5), channel_id=1, source_target_pairs={{0,12},{1,13},{2,14},{3,15},{4,0},{5,1},{6,2},{7,3},{8,4},{9,5},{1... | collective-permute-start | bytes 101384 | tf_op jit(solution)/shard_map/ppermute | solution.py:28
  13.3 5.1 %collective-permute-start.3 = (bf16[4,8,2112]{2,1,0:T(8,128)(2,1)S(1)}, bf16[4,8,2112]{2,1,0:T(8,128)(2,1)S(1)}, u32[]{:S(2)}, u32[]{:S(2)}) collective-permute-start(bf16[4,8,2112]{2,1,0:T(8,128)(2,1)S(1)} %bitcast_dynamic-update-slice_fusion), channel_id=1, source_target_pairs={{0,2},{1,3},{2,0},{3,1},{4,6},{5,7},{6,4},{7,5},{8,10},{9,11},{10,... | collective-permute-start | bytes 405512 | tf_op jit(solution)/shard_map/ppermute | solution.py:32
  18.4 1.0 copy-start.4
  18.4 1.6 %collective-permute-start.4 = (bf16[4,2,8,2112]{3,2,1,0:T(8,128)(2,1)S(1)}, bf16[4,2,8,2112]{3,2,1,0:T(8,128)(2,1)S(1)}, u32[]{:S(2)}, u32[]{:S(2)}) collective-permute-start(bf16[4,2,8,2112]{3,2,1,0:T(8,128)(2,1)S(1)} %pad_maximum_fusion.4), channel_id=1, source_target_pairs={{0,1},{1,0},{2,3},{3,2},{4,5},{5,4},{6,7},{7,6},{8,9},{9,8},{10,11... | collective-permute-start | bytes 811016 | tf_op jit(solution)/shard_map/ppermute | solution.py:36
  18.5 0.7 copy-start.7
  20.2 0.7 copy-start.6
  21.3 1.0 copy-start.1
  22.3 5.1 %copy-start.8 = (bf16[66,128]{1,0:T(8,128)(2,1)S(1)}, bf16[66,128]{1,0:T(8,128)(2,1)}, u32[]{:S(2)}) copy-start(bf16[66,128]{1,0:T(8,128)(2,1)} %param.17) | copy-start | bytes 50692
  49.0 1.6 %collective-permute-start.5 = (bf16[16,8,8,128]{3,0,2,1:T(8,128)(2,1)S(1)}, bf16[16,8,8,128]{3,0,2,1:T(8,128)(2,1)S(1)}, u32[]{:S(2)}, u32[]{:S(2)}) collective-permute-start(bf16[16,8,8,128]{3,0,2,1:T(8,128)(2,1)S(1)} %get-tuple-element.67), channel_id=1, source_target_pairs={{0,1},{1,0},{2,3},{3,2},{4,5},{5,4},{6,7},{7,6},{8,9},{9,8},{10,11... | collective-permute-start | bytes 786440 | tf_op jit(solution)/shard_map/ppermute | solution.py:51
  52.1 12.9 %all-to-all-start.1 = ((bf16[8,16,8,128]{3,2,1,0:T(8,128)(2,1)}), bf16[8,16,8,128]{3,2,1,0:T(8,128)(2,1)S(1)}, u32[]{:S(2)}, u32[]{:S(2)}) async-start(bf16[8,16,8,128]{3,2,1,0:T(8,128)(2,1)} %bitcast.159), calls=%async_computation.1 | async-start | bytes 524288 | tf_op jit(solution)/shard_map/all_to_all | solution.py:46
  65.2 0.8 copy-start.5
  86.0 2.0 %collective-permute-start.6 = (f32[16,8,8,128]{3,2,0,1:T(8,128)S(1)}, f32[16,8,8,128]{3,2,0,1:T(8,128)S(1)}, u32[]{:S(2)}, u32[]{:S(2)}) collective-permute-start(f32[16,8,8,128]{3,2,0,1:T(8,128)S(1)} %select_bitcast_fusion), channel_id=1, source_target_pairs={{0,1},{1,0},{2,3},{3,2},{4,5},{5,4},{6,7},{7,6},{8,9},{9,8},{10,11... | collective-permute-start | bytes 1572872 | tf_op jit(solution)/shard_map/ppermute | solution.py:51
  88.7 12.9 %all-to-all-start.3 = ((bf16[8,16,8,128]{3,2,1,0:T(8,128)(2,1)}), bf16[8,16,8,128]{3,2,1,0:T(8,128)(2,1)S(1)}, u32[]{:S(2)}, u32[]{:S(2)}) async-start(bf16[8,16,8,128]{3,2,1,0:T(8,128)(2,1)} %fusion.50), calls=%async_computation.3 | async-start | bytes 524288 | tf_op jit(solution)/shard_map/all_to_all | solution.py:46

commit v4 on v1

--- a/solution.py
+++ b/solution.py
@@ -1,12 +1,17 @@
+import functools
+
 import jax
 import jax.numpy as jnp
 from jax import lax
+from jax.experimental import pallas as pl
+from jax.experimental.pallas import tpu as pltpu
 from jax.sharding import PartitionSpec as P
 
 RELMAX = 32
-
-
 EPSILON = 1e-05
+LANES = 128
+F32 = jnp.float32
+BF16 = jnp.bfloat16
 
 
 def apply_layer_norm(values, axis_dim):
@@ -95,7 +100,7 @@
     return stream + gate * update
 
 
-def per_device(
+def per_device_general(
     pairwise_state,
     homolog_features,
     residue_chain_index,
@@ -173,7 +178,402 @@
     return stream.astype(jnp.bfloat16)
 
 
+def nn(a, b):
+    return lax.dot_general(a, b, (((1,), (0,)), ((), ())), preferred_element_type=F32)
+
+
+def nt(a, b):
+    return lax.dot_general(a, b, (((1,), (1,)), ((), ())), preferred_element_type=F32)
+
+
+def tn(a, b):
+    return lax.dot_general(a, b, (((0,), (0,)), ((), ())), preferred_element_type=F32)
+
+
+def identity(size):
+    rows = lax.broadcasted_iota(jnp.int32, (size, size), 0)
+    cols = lax.broadcasted_iota(jnp.int32, (size, size), 1)
+    return (rows == cols).astype(F32).astype(BF16)
+
+
+def flip(block):
+    return nt(identity(block.shape[1]), block)
+
+
+def norm_rows(values):
+    scale = 1.0 / values.shape[0]
+    center = values - jnp.sum(values, axis=0, keepdims=True) * scale
+    spread = jnp.sum(center * center, axis=0, keepdims=True) * scale
+    return (center * lax.rsqrt(spread + EPSILON)).astype(BF16)
+
+
+def run(kernel, outs, *args, smem=(), scratch=(), flops=10**7):
+    vmem = pl.BlockSpec(memory_space=pltpu.VMEM)
+    in_specs = [
+        pl.BlockSpec(memory_space=pltpu.SMEM) if at in smem else vmem for at in range(len(args))
+    ]
+    moved = sum(a.size * a.dtype.itemsize for a in args)
+    return pl.pallas_call(
+        kernel,
+        out_shape=[jax.ShapeDtypeStruct(shape, kind) for shape, kind in outs],
+        in_specs=in_specs,
+        out_specs=[vmem] * len(outs),
+        scratch_shapes=[pltpu.VMEM(shape, kind) for shape, kind in scratch],
+        compiler_params=pltpu.CompilerParams(vmem_limit_bytes=VMEM_LIMIT),
+        cost_estimate=pl.CostEstimate(flops=flops, bytes_accessed=moved, transcendentals=0),
+    )(*args)
+
+
+VMEM_LIMIT = 20 * 1024 * 1024
+
+
+def project_kernel(where_ref, feat_ref, weight_ref, mask_ref, present_ref, pay_ref, left_ref, live_ref, turned, packed):
+    homologs, rows, _ = feat_ref.shape
+    half = weight_ref.shape[1] // 2
+    quarter = half // 2
+    values = feat_ref[...].astype(F32).reshape(homologs * rows, feat_ref.shape[2])
+    center = values - jnp.mean(values, axis=1, keepdims=True)
+    spread = jnp.mean(center * center, axis=1, keepdims=True)
+    normed = (center * lax.rsqrt(spread + EPSILON)).astype(BF16)
+    total = homologs * rows
+    out_row = lax.broadcasted_iota(jnp.int32, (total, total), 0)
+    in_row = lax.broadcasted_iota(jnp.int32, (total, total), 1)
+    order = in_row == (out_row & (homologs - 1)) * rows + out_row // homologs
+    normed = nn(order.astype(F32).astype(BF16), normed).astype(BF16)
+    seq = lax.broadcasted_iota(jnp.int32, (homologs, 2 * homologs), 0)
+    lane = lax.broadcasted_iota(jnp.int32, (homologs, 2 * homologs), 1)
+    twice = (seq == (lane & (homologs - 1))).astype(F32).astype(BF16)
+    live = tn(mask_ref[...], twice)
+    cols = present_ref.shape[1]
+    here = lax.broadcasted_iota(jnp.int32, (rows, cols), 1) == (
+        lax.broadcasted_iota(jnp.int32, (rows, cols), 0) + where_ref[0]
+    )
+    present = jnp.sum(jnp.where(here, present_ref[...].astype(F32), 0.0), axis=1, keepdims=True)
+    live = live * present
+    weight = flip(weight_ref[...]).astype(BF16)
+    blank = jnp.zeros((homologs, normed.shape[1]), BF16)
+    for row in range(rows):
+        mine = normed[row * homologs : (row + 1) * homologs]
+        low = nt(weight, jnp.concatenate([mine, blank], axis=0)) * live[row : row + 1]
+        high = nt(weight, jnp.concatenate([blank, mine], axis=0)) * live[row : row + 1]
+        left_ref[row * half : (row + 1) * half] = low[:half].astype(BF16)
+        left_ref[(rows + row) * half : (rows + row + 1) * half] = high[:half].astype(BF16)
+        turned[row] = low[half : half + quarter] + high[half + quarter :]
+    for pair in range(quarter):
+        packed[pair * rows : (pair + 1) * rows] = turned[:, pair, :]
+    packed[quarter * rows : (quarter + 1) * rows] = live
+    packed[(quarter + 1) * rows :] = jnp.zeros((rows, 2 * homologs), F32)
+    pay_ref[...] = packed[...].astype(BF16)
+    live_ref[...] = jnp.where(lax.broadcasted_iota(jnp.int32, live.shape, 1) < homologs, live, 0.0)
+
+
+def prep_kernel(
+    where_ref, chain_ref, chains_ref, pair_ref, table_ref, outer_ref, proj_ref, out_ref,
+    base_ref, outer_t_ref, proj_t_ref, out_t_ref, table_pad, outer_pad,
+):
+    rows, cols, width = pair_ref.shape
+    bins = table_ref.shape[0]
+    table_pad[...] = jnp.zeros_like(table_pad)
+    table_pad[0:bins, :] = table_ref[...].astype(F32)
+    table = flip(table_pad[...].astype(BF16)).astype(BF16)
+    chains = chains_ref[...]
+    col = lax.broadcasted_iota(jnp.int32, (1, cols), 1)
+    slot = lax.broadcasted_iota(jnp.int32, (table_pad.shape[0], cols), 0)
+    for row in range(rows):
+        place = where_ref[0] + row
+        offset = jnp.clip(place - col, -RELMAX, RELMAX) + RELMAX
+        bin_index = jnp.where(chains == chain_ref[place], offset, 2 * RELMAX + 1)
+        hot = (slot == bin_index).astype(F32).astype(BF16)
+        base_ref[row] = flip(pair_ref[row]) + nn(table, hot)
+    half = outer_pad.shape[0]
+    outer_pad[...] = outer_ref[...].astype(F32).reshape(outer_pad.shape)
+    for d in range(half):
+        outer_t_ref[:, d * half : (d + 1) * half] = flip(outer_pad[:, d, :].astype(BF16)).astype(BF16)
+    for turn in range(2):
+        proj_t_ref[turn] = tn(proj_ref[turn], identity(width)).astype(BF16)
+        out_t_ref[turn] = flip(out_ref[turn]).astype(BF16)
+
+
+def sides(normed, weight, live):
+    width = normed.shape[0]
+    made = nn(weight, normed)
+    part = [made[at * width : (at + 1) * width] for at in range(5)]
+    left = jax.nn.sigmoid(part[0]) * part[1] * live
+    right = jax.nn.sigmoid(part[2]) * part[3] * live
+    return left, right, jax.nn.sigmoid(part[4])
+
+
+def outer_kernel(
+    where_ref, flag_ref, own_ref, other_ref, left_ref, live_ref, base_ref, outer_t_ref, proj_ref, present_ref,
+    stream_ref, gate_ref, both0, both1, both2, both3, far0, far1, far2, far3, came, outer, lefts, rights,
+):
+    rows, width, cols = base_ref.shape
+    chip, core = where_ref[1], where_ref[2]
+    per = own_ref.shape[1]
+    chips = own_ref.shape[0]
+    for at in range(chips):
+        chip_at = chip ^ ((at % 4) * 2 + at // 4)
+        came[chip_at * 2 + core] = own_ref[at].astype(F32)
+        came[chip_at * 2 + (1 - core)] = other_ref[at].astype(F32)
+    half = left_ref.shape[0] // (2 * rows)
+    quarter = half // 2
+    live_all = came[:, quarter * rows : (quarter + 1) * rows, :].reshape(cols, per_lane(came)).astype(BF16)
+    counts = nt(live_ref[...].astype(BF16), live_all)
+    share = 1.0 / jnp.maximum(counts, 1.0)
+    left_all = left_ref[...]
+    for pair in range(quarter):
+        right = came[:, pair * rows : (pair + 1) * rows, :].reshape(cols, per_lane(came)).astype(BF16)
+        made = nt(left_all, right).astype(BF16)
+        for part in range(2):
+            d = part * quarter + pair
+            for row in range(rows):
+                first = (part * rows + row) * half
+                outer[row, d * half : (d + 1) * half, :] = made[first : first + half]
+    present = present_ref[...].astype(F32)
+    for row in range(rows):
+        stream = base_ref[row] + nn(outer_t_ref[...], outer[row]) * share[row : row + 1]
+        stream_ref[row] = stream
+        live = present * flag_ref[where_ref[0] + row].astype(F32)
+        left, right, gate = sides(norm_rows(stream), proj_ref[0], live)
+        gate_ref[row] = gate
+        lefts[:, row, :] = left
+        rights[:, row, :] = right
+    groups = 4
+    size = width // groups
+    for step, (near, far) in enumerate(((both0, far0), (both1, far1), (both2, far2), (both3, far3))):
+        group = (chip & (groups - 1)) ^ step
+        block = rights[pl.ds(group * size, size)].reshape(size * rows, cols).astype(BF16)
+        far[...] = block
+        near[size * rows :] = block
+        near[0 : size * rows] = lefts[pl.ds(group * size, size)].reshape(size * rows, cols).astype(BF16)
+
+
+def per_lane(ref):
+    return ref.shape[-1]
+
+
+def mix_rows_kernel(
+    where_ref, both0, both1, both2, both3, far4, far5, far6, far7, other_ref,
+    out0, out1, out2, out3, lefts, rights, mixed,
+):
+    chip, core = where_ref[1], where_ref[2]
+    count, rows, cols = lefts.shape[1:]
+    block = count * rows
+    nears = (both0, both1, both2, both3)
+    fars = (far4, far5, far6, far7)
+    for step in range(8):
+        mine = (nears[step][block:] if step < 4 else fars[step - 4][...]).astype(F32)
+        rights[(chip ^ step) * 2 + core] = mine.reshape(count, rows, cols)
+        rights[(chip ^ step) * 2 + (1 - core)] = other_ref[step].astype(F32).reshape(count, rows, cols)
+        if step < 4:
+            lefts[step] = nears[step][0:block].astype(F32).reshape(count, rows, cols)
+    for c in range(count):
+        left = lefts[:, c].reshape(4 * rows, cols).astype(BF16)
+        right = rights[:, c].reshape(16 * rows, cols).astype(BF16)
+        mixed[:, c, :] = nt(left, right)
+    for step, out in enumerate((out0, out1, out2, out3)):
+        out[...] = mixed[step * rows : (step + 1) * rows].reshape(block, cols).astype(BF16)
+
+
+def update(came, row, stream, gate, out_weight):
+    mixed = came[row]
+    mixed = mixed.reshape(mixed.shape[0] * mixed.shape[1], mixed.shape[2])
+    return stream + gate * nn(out_weight, norm_rows(mixed))
+
+
+def between_kernel(
+    where_ref, flag_ref, in0, in1, in2, in3, stream_ref, gate_ref, out_weight_ref, proj_ref, present_ref,
+    next_ref, next_gate_ref, b0, b1, b2, b3, b4, b5, b6, b7, came, lefts, rights,
+):
+    rows, width, cols = stream_ref.shape
+    chip = where_ref[1]
+    groups = 4
+    for step, block in enumerate((in0, in1, in2, in3)):
+        came[:, (chip & (groups - 1)) ^ step] = block[...].astype(F32).reshape(rows, width // groups, cols)
+    present = present_ref[...].astype(F32)
+    for row in range(rows):
+        stream = update(came, row, stream_ref[row], gate_ref[row], out_weight_ref[0])
+        next_ref[row] = stream
+        live = present * flag_ref[where_ref[0] + row].astype(F32)
+        left, right, gate = sides(norm_rows(stream), proj_ref[1], live)
+        next_gate_ref[row] = gate
+        lefts[:, row, :] = left
+        rights[:, row, :] = right
+    outs = (b0, b1, b2, b3, b4, b5, b6, b7)
+    size = width // len(outs)
+    for step, out in enumerate(outs):
+        first = (chip ^ step) * size
+        out[0 : size * rows] = lefts[pl.ds(first, size)].reshape(size * rows, cols).astype(BF16)
+        out[size * rows :] = rights[pl.ds(first, size)].reshape(size * rows, cols).astype(BF16)
+
+
+def mix_cols_kernel(where_ref, b0, b1, b2, b3, b4, b5, b6, b7, mine_ref, theirs_ref, lefts, rights, partial):
+    chip, core = where_ref[1], where_ref[2]
+    chips, count, rows, cols = lefts.shape
+    block = count * rows
+    for step, came in enumerate((b0, b1, b2, b3, b4, b5, b6, b7)):
+        lefts[step] = came[0:block].astype(F32).reshape(count, rows, cols)
+        rights[step] = came[block:].astype(F32).reshape(count, rows, cols)
+    for c in range(count):
+        left = lefts[:, c].reshape(chips * rows, cols).astype(BF16)
+        right = rights[:, c].reshape(chips * rows, cols).astype(BF16)
+        partial[:, c, :] = tn(left, right)
+    for step in range(chips):
+        at = (chip ^ step) * 2
+        mine_ref[step] = partial[pl.ds((at + core) * rows, rows)].reshape(block, cols)
+        theirs_ref[step] = partial[pl.ds((at + 1 - core) * rows, rows)].reshape(block, cols)
+
+
+def sum_kernel(mine_ref, got_ref, *outs):
+    for step, out in enumerate(outs):
+        out[...] = (mine_ref[step] + got_ref[step]).astype(BF16)
+
+
+def final_kernel(
+    where_ref, b0, b1, b2, b3, b4, b5, b6, b7, stream_ref, gate_ref, out_weight_ref, out_ref, came
+):
+    rows, width, cols = stream_ref.shape
+    chip = where_ref[1]
+    blocks = (b0, b1, b2, b3, b4, b5, b6, b7)
+    for step, block in enumerate(blocks):
+        came[:, chip ^ step] = block[...].astype(F32).reshape(rows, width // len(blocks), cols)
+    for row in range(rows):
+        stream = update(came, row, stream_ref[row], gate_ref[row], out_weight_ref[1])
+        out_ref[row] = flip_out(stream)
+
+
+def flip_out(stream):
+    return nt(identity(stream.shape[1]), stream.astype(BF16)).astype(BF16)
+
+
+def chip_permute(block, step):
+    count = lax.axis_size("wide")
+    return lax.ppermute(block, "wide", [(w, w ^ (2 * step)) for w in range(count)])
+
+
+def core_permute(block):
+    count = lax.axis_size("wide")
+    return lax.ppermute(block, "wide", [(w, w ^ 1) for w in range(count)])
+
+
+def per_device_chips(
+    pairwise_state,
+    homolog_features,
+    residue_chain_index,
+    resolved_residue_mask,
+    alignment_mask,
+    relative_offset_table,
+    homolog_to_sides_matrix,
+    outer_mean_output_weight,
+    triangle_projection_weight,
+    triangle_output_weight,
+):
+    rows, cols, width = pairwise_state.shape
+    homologs = homolog_features.shape[0]
+    half = homolog_to_sides_matrix.shape[1] // 2
+    device = lax.axis_index("wide")
+    chip, core = device // 2, device % 2
+    where = jnp.stack([device * rows, chip, core]).astype(jnp.int32)
+    present = resolved_residue_mask.reshape(1, cols)
+    pay_rows = (half // 2 + 2) * rows
+    pay, left, live = run(
+        project_kernel,
+        [((pay_rows, LANES), BF16), ((2 * rows * half, LANES), BF16), ((rows, LANES), F32)],
+        where, homolog_features, homolog_to_sides_matrix, alignment_mask, present,
+        smem=(0,),
+        scratch=[((rows, half // 2, LANES), F32), ((pay_rows, LANES), F32)],
+    )
+    along_z = [chip_permute(pay, 2 * z) for z in (2, 3, 1)]
+    base, outer_t, proj_t, out_t = run(
+        prep_kernel,
+        [
+            ((rows, width, cols), F32),
+            ((width, half * half), BF16),
+            ((2, triangle_projection_weight.shape[2], width), BF16),
+            ((2, width, width), BF16),
+        ],
+        where, residue_chain_index, residue_chain_index.reshape(1, cols), pairwise_state,
+        relative_offset_table, outer_mean_output_weight, triangle_projection_weight, triangle_output_weight,
+        smem=(0, 1),
+        scratch=[((LANES, width), F32), ((half, half, width), F32)],
+    )
+    along_z = jnp.stack([pay, along_z[2], along_z[0], along_z[1]])
+    own = jnp.concatenate([along_z, chip_permute(along_z, 1)], axis=0)
+    other = core_permute(own)
+    tall = width * rows
+    made = run(
+        outer_kernel,
+        [((rows, width, cols), F32)] * 2
+        + [((tall // 2, cols), BF16)] * 4
+        + [((tall // 4, cols), BF16)] * 4,
+        where, resolved_residue_mask, own, other, left, live, base, outer_t, proj_t, present,
+        smem=(0, 1),
+        scratch=[
+            ((16, pay_rows, LANES), F32),
+            ((rows, half * half, cols), BF16),
+            ((width, rows, cols), F32),
+            ((width, rows, cols), F32),
+        ],
+        flops=4 * 10**8,
+    )
+    stream, gate, both, far = made[0], made[1], made[2:6], made[6:10]
+    far = [chip_permute(far[step], step + 4) for step in (3, 2, 1, 0)][::-1]
+    near = [chip_permute(both[step], step) for step in (3, 2, 1)][::-1]
+    rights = jnp.stack([b[tall // 4 :] for b in [both[0]] + near] + far)
+    rights = core_permute(rights)
+    mixed = run(
+        mix_rows_kernel,
+        [((tall // 4, cols), BF16)] * 4,
+        where, both[0], *near, *far, rights,
+        smem=(0,),
+        scratch=[
+            ((4, width // 4, rows, cols), F32),
+            ((16, width // 4, rows, cols), F32),
+            ((4 * rows, width // 4, cols), F32),
+        ],
+    )
+    mixed = [mixed[0]] + [chip_permute(mixed[step], step) for step in (3, 2, 1)][::-1]
+    made = run(
+        between_kernel,
+        [((rows, width, cols), F32)] * 2 + [((tall // 4, cols), BF16)] * 8,
+        where, resolved_residue_mask, *mixed, stream, gate, out_t, proj_t, present,
+        smem=(0, 1),
+        scratch=[
+            ((rows, 4, width // 4, cols), F32),
+            ((width, rows, cols), F32),
+            ((width, rows, cols), F32),
+        ],
+    )
+    stream, gate, both = made[0], made[1], made[2:]
+    came = [both[0]] + [chip_permute(both[step], step) for step in range(7, 0, -1)][::-1]
+    mine, theirs = run(
+        mix_cols_kernel,
+        [((8, tall // 8, cols), F32)] * 2,
+        where, *came,
+        smem=(0,),
+        scratch=[
+            ((8, width // 8, rows, cols), F32),
+            ((8, width // 8, rows, cols), F32),
+            ((16 * rows, width // 8, cols), F32),
+        ],
+    )
+    mixed = run(sum_kernel, [((tall // 8, cols), BF16)] * 8, mine, core_permute(theirs))
+    mixed = [mixed[0]] + [chip_permute(mixed[step], step) for step in range(7, 0, -1)][::-1]
+    return run(
+        final_kernel,
+        [((rows, cols, width), BF16)],
+        where, *mixed, stream, gate, out_t,
+        smem=(0,),
+        scratch=[((rows, 8, width // 8, cols), F32)],
+    )[0]
+
+
+def fits_chips(mesh):
+    return mesh.shape["narrow"] == 1 and mesh.shape["wide"] == 16
+
+
 def solution(mesh):
+    per_device = per_device_chips if fits_chips(mesh) else per_device_general
     return jax.shard_map(
         per_device,
         mesh=mesh,

time: 103 us -> 101 us (0.981)
  blocking collectives: 37 us -> 0 us
  starting transfers between devices: 16.8 us -> 42.8 us
  Pallas kernels: 0 us -> 15.1 us
  waiting for transfers between devices: 25.6 us -> 39.6 us
  matrix products: 8.71 us -> 0 us
  local copies, waits for them, and re-layouts: 9.25 us -> 3.21 us
  other arithmetic: 3.95 us -> 0.1 us
    all_to_all x2 -> x0, blocking collectives: 37 us -> none  [triangle(): lax.all_to_all(both, ('wide', 'narrow'), split_axis=0, concat_axis=0, til...]
    ppermute x5 -> x31, starting transfers between devices: 8.58 us -> 42.8 us  [the longest x28 42.6 us: chip_permute(): lax.ppermute(block, 'wide', [(w, w ^ 2 * step) for w in range(count)])]
    ppermute x5 -> x31, waiting for transfers between devices: 6.17 us -> 39.6 us  [the longest x28 35.8 us: chip_permute(): lax.ppermute(block, 'wide', [(w, w ^ 2 * step) for w in range(count)])]
    all_to_all x2 -> x0, waiting for transfers between devices: 19.4 us -> none  [triangle(): lax.all_to_all(spread_out, ('wide', 'narrow'), split_axis=0, concat_axis=...]
    pallas_call x0 -> x8, Pallas kernels: none -> 15.1 us  [run(): pl.pallas_call(kernel, out_shape=[jax.ShapeDtypeStruct(shape, kind) for s...]
    dot_general x33 -> x0, matrix products: 8.71 us -> none  [the longest x8 2.27 us: opm_row(): jnp.dot(outer, outer_mean_output_weight, preferred_element_type=jnp.float32)]
    all_to_all x2 -> x0, starting transfers between devices: 8.19 us -> none  [triangle(): lax.all_to_all(spread_out, ('wide', 'narrow'), split_axis=0, concat_axis=...]
    convert_element_type x13 -> x0, local copies, waits for them, and re-layouts: 2.39 us -> none  [the longest x1 0.85 us: per_device(): return stream.astype(jnp.bfloat16)]
  transfers between devices with their start and end apart: 7 -> 31, of which waited for: 6 -> 17; matrix products, arithmetic and copies ran while one was open for 1% -> 0% of each run, Pallas kernels for 0% -> 2%
where the time goes in v4:
time: 101 us
  starting transfers between devices  42.8 us (42%)
  waiting for transfers between devices  39.6 us (39%)
  Pallas kernels  15.1 us (15%)
  local copies, waits for them, and re-layouts  3.21 us (3%)
    ppermute x28, starting transfers between devices, chip_permute(): lax.ppermute(block, 'wide', [(w, w ^ 2 * step) for w in range(count)])  42.6 us
    ppermute x28, waiting for transfers between devices, chip_permute(): lax.ppermute(block, 'wide', [(w, w ^ 2 * step) for w in range(count)])  35.8 us
    pallas_call x8, Pallas kernels, run(): pl.pallas_call(kernel, out_shape=[jax.ShapeDtypeStruct(shape, kind) for s...  15.1 us
    ppermute x3, waiting for transfers between devices, core_permute(): return lax.ppermute(block, 'wide', [(w, w ^ 1) for w in range(count)])  3.8 us
    unnamed x33, local copies, waits for them, and re-layouts  3.18 us
  transfers between devices with their start and end apart: 31, of which 17 were waited for; matrix products, arithmetic and copies ran while one was open for 0% of the time, Pallas kernels for 2%

profile of v4, /device:TPU:0, one launch (start us, length us, event | category | flops | bytes accessed | tf_op | source)
XLA Modules:
  0.0 101.2 jit_solution(12467460173611272446)
XLA Ops:
  0.0 0.7 copy-done.9
  0.7 0.1 copy.12.mask_ref
  0.8 0.1 copy.11.weight_ref
  0.9 0.1 pad_add_fusion.where_ref
  1.0 0.7 copy-done.6
  1.7 0.9 copy-done.1
  2.6 1.5 %shard_map.100 = (bf16[144,128]{1,0:T(8,128)(2,1)S(1)}, bf16[512,128]{1,0:T(8,128)(2,1)S(1)}, f32[8,128]{1,0:T(8,128)S(1)}) custom-call(s32[3]{0:T(128)S(1)} %pad_add_fusion.where_ref, bf16[64,8,256]{2,1,0:T(8,128)(2,1)S(1)} %copy-done.1, bf16[256,64]{1,0:T(8,128)(2,1)S(1)} %copy.11.weight_ref, bf16[64,8]{1,0:T(8,128)(2,1)S(1)} %copy.12.mask_ref, ...), custom_call_target="tpu_custom_call" | custom-call | flops 10000000 | bytes 296460 | tf_op jit(solution)/shard_map/pallas_call | solution.py:216
  4.1 5.1 %collective-permute-start.2 = (bf16[144,128]{1,0:T(8,128)(2,1)S(1)}, bf16[144,128]{1,0:T(8,128)(2,1)S(1)}, u32[]{:S(2)}, u32[]{:S(2)}) collective-permute-start(bf16[144,128]{1,0:T(8,128)(2,1)S(1)} %get-tuple-element.46), channel_id=1, source_target_pairs={{0,12},{1,13},{2,14},{3,15},{4,8},{5,9},{6,10},{7,11},{8,4},{9,5},... | collective-permute-start | bytes 110600 | tf_op jit(solution)/shard_map/ppermute | solution.py:451
  9.3 0.6 collective-permute-start
  9.9 1.3 %collective-permute-done.2 = bf16[144,128]{1,0:T(8,128)(2,1)S(1)} collective-permute-done((bf16[144,128]{1,0:T(8,128)(2,1)S(1)}, bf16[144,128]{1,0:T(8,128)(2,1)S(1)}, u32[]{:S(2)}, u32[]{:S(2)}) %collective-permute-start.2) | collective-permute-done | bytes 36896 | tf_op jit(solution)/shard_map/ppermute | solution.py:451
  11.2 2.9 %collective-permute-done.1 = bf16[144,128]{1,0:T(8,128)(2,1)S(1)} collective-permute-done((bf16[144,128]{1,0:T(8,128)(2,1)S(1)}, bf16[144,128]{1,0:T(8,128)(2,1)S(1)}, u32[]{:S(2)}, u32[]{:S(2)}) %collective-permute-start.1) | collective-permute-done | bytes 36896 | tf_op jit(solution)/shard_map/ppermute | solution.py:451
  14.1 0.0 copy-start
  14.2 1.6 %collective-permute-start.3 = (bf16[4,144,128]{2,1,0:T(8,128)(2,1)S(1)}, bf16[4,144,128]{2,1,0:T(8,128)(2,1)S(1)}, u32[]{:S(2)}, u32[]{:S(2)}) collective-permute-start(bf16[4,144,128]{2,1,0:T(8,128)(2,1)S(1)} %pad_maximum_fusion), channel_id=1, source_target_pairs={{0,2},{1,3},{2,0},{3,1},{4,6},{5,7},{6,4},{7,5},{8,10},{9,11},{10,... | collective-permute-start | bytes 442376 | tf_op jit(solution)/shard_map/ppermute | solution.py:451
  15.8 0.0 copy-start.5
  15.8 3.6 %collective-permute-done.3 = bf16[4,144,128]{2,1,0:T(8,128)(2,1)S(1)} collective-permute-done((bf16[4,144,128]{2,1,0:T(8,128)(2,1)S(1)}, bf16[4,144,128]{2,1,0:T(8,128)(2,1)S(1)}, u32[]{:S(2)}, u32[]{:S(2)}) %collective-permute-start.3) | collective-permute-done | bytes 147488 | tf_op jit(solution)/shard_map/ppermute | solution.py:451
  19.4 0.0 copy-start.7
  19.4 0.1 collective-permute-start.4
  19.5 0.5 copy-done.7
  20.1 2.0 %shard_map.101 = (f32[8,128,128]{2,1,0:T(8,128)S(1)}, bf16[128,1024]{1,0:T(8,128)(2,1)S(1)}, bf16[2,640,128]{2,1,0:T(8,128)(2,1)S(1)}, bf16[2,128,128]{2,1,0:T(8,128)(2,1)S(1)}) custom-call(s32[3]{0:T(128)S(1)} %pad_add_fusion.where_ref, s32[128]{0:T(128)S(1)} %copy-done.7, s32[1,128]{1,0:T(1,128)S(1)} %bitcast.39, bf16[8,128,128]{2,1,0:T(8,128)(2,1)S(1)} %copy-done.2, ...), custom_call_target="tpu_custom_call" | custom-call | flops 10000000 | bytes 935436 | tf_op jit(solution)/shard_map/pallas_call | solution.py:216
  22.1 4.0 %shard_map.102 = (f32[8,128,128]{2,1,0:T(8,128)S(1)}, f32[8,128,128]{2,1,0:T(8,128)S(1)}, bf16[512,128]{1,0:T(8,128)(2,1)S(1)}, bf16[512,128]{1,0:T(8,128)(2,1)S...) custom-call(s32[3]{0:T(128)S(1)} %pad_add_fusion.where_ref, ...), custom_call_target="tpu_custom_call" | custom-call | flops 400000000 | bytes 1840140 | tf_op jit(solution)/shard_map/pallas_call | solution.py:216
  26.1 2.1 %collective-permute-start.8 = (bf16[256,128]{1,0:T(8,128)(2,1)S(1)}, bf16[256,128]{1,0:T(8,128)(2,1)S(1)}, u32[]{:S(2)}, u32[]{:S(2)}) collective-permute-start(bf16[256,128]{1,0:T(8,128)(2,1)S(1)} %get-tuple-element.56), channel_id=1, source_target_pairs={{0,8},{1,9},{2,10},{3,11},{4,12},{5,13},{6,14},{7,15},{8,0},{9,1},... | collective-permute-start | bytes 196616 | tf_op jit(solution)/shard_map/ppermute | solution.py:451
  28.2 1.8 %collective-permute-start.9 = (bf16[256,128]{1,0:T(8,128)(2,1)S(1)}, bf16[256,128]{1,0:T(8,128)(2,1)S(1)}, u32[]{:S(2)}, u32[]{:S(2)}) collective-permute-start(bf16[256,128]{1,0:T(8,128)(2,1)S(1)} %get-tuple-element.57), channel_id=1, source_target_pairs={{0,10},{1,11},{2,8},{3,9},{4,14},{5,15},{6,12},{7,13},{8,2},{9,3},... | collective-permute-start | bytes 196616 | tf_op jit(solution)/shard_map/ppermute | solution.py:451
  30.1 1.5 %collective-permute-start.10 = (bf16[256,128]{1,0:T(8,128)(2,1)S(1)}, bf16[256,128]{1,0:T(8,128)(2,1)S(1)}, u32[]{:S(2)}, u32[]{:S(2)}) collective-permute-start(bf16[256,128]{1,0:T(8,128)(2,1)S(1)} %get-tuple-element.58), channel_id=1, source_target_pairs={{0,12},{1,13},{2,14},{3,15},{4,8},{5,9},{6,10},{7,11},{8,4},{9,5},... | collective-permute-start | bytes 196616 | tf_op jit(solution)/shard_map/ppermute | solution.py:451
  31.5 2.3 %collective-permute-start.11 = (bf16[256,128]{1,0:T(8,128)(2,1)S(1)}, bf16[256,128]{1,0:T(8,128)(2,1)S(1)}, u32[]{:S(2)}, u32[]{:S(2)}) collective-permute-start(bf16[256,128]{1,0:T(8,128)(2,1)S(1)} %get-tuple-element.59), channel_id=1, source_target_pairs={{0,14},{1,15},{2,12},{3,13},{4,10},{5,11},{6,8},{7,9},{8,6},{9,7},... | collective-permute-start | bytes 196616 | tf_op jit(solution)/shard_map/ppermute | solution.py:451
  33.8 1.5 %collective-permute-start.5 = (bf16[512,128]{1,0:T(8,128)(2,1)S(1)}, bf16[512,128]{1,0:T(8,128)(2,1)S(1)}, u32[]{:S(2)}, u32[]{:S(2)}) collective-permute-start(bf16[512,128]{1,0:T(8,128)(2,1)S(1)} %get-tuple-element.53), channel_id=1, source_target_pairs={{0,2},{1,3},{2,0},{3,1},{4,6},{5,7},{6,4},{7,5},{8,10},{9,11},{10,... | collective-permute-start | bytes 393224 | tf_op jit(solution)/shard_map/ppermute | solution.py:451
  35.3 5.1 %collective-permute-done.5.both1 = bf16[512,128]{1,0:T(8,128)(2,1)S(1)} collective-permute-done((bf16[512,128]{1,0:T(8,128)(2,1)S(1)}, bf16[512,128]{1,0:T(8,128)(2,1)S(1)}, u32[]{:S(2)}, u32[]{:S(2)}) %collective-permute-start.5) | collective-permute-done | bytes 131104 | tf_op jit(solution)/shard_map/ppermute | solution.py:451
  40.5 5.0 %collective-permute-done.6.both2 = bf16[512,128]{1,0:T(8,128)(2,1)S(1)} collective-permute-done((bf16[512,128]{1,0:T(8,128)(2,1)S(1)}, bf16[512,128]{1,0:T(8,128)(2,1)S(1)}, u32[]{:S(2)}, u32[]{:S(2)}) %collective-permute-start.6) | collective-permute-done | bytes 131104 | tf_op jit(solution)/shard_map/ppermute | solution.py:451
  45.5 0.1 collective-permute-start.7
  45.6 5.7 %collective-permute-done.7.both3 = bf16[512,128]{1,0:T(8,128)(2,1)S(1)} collective-permute-done((bf16[512,128]{1,0:T(8,128)(2,1)S(1)}, bf16[512,128]{1,0:T(8,128)(2,1)S(1)}, u32[]{:S(2)}, u32[]{:S(2)}) %collective-permute-start.7) | collective-permute-done | bytes 131104 | tf_op jit(solution)/shard_map/ppermute | solution.py:451
  51.5 0.1 collective-permute-start.12
  51.5 1.9 %collective-permute-done.12.other_ref = bf16[8,256,128]{2,1,0:T(8,128)(2,1)S(1)} collective-permute-done((bf16[8,256,128]{2,1,0:T(8,128)(2,1)S(1)}, bf16[8,256,128]{2,1,0:T(8,128)(2,1)S(1)}, u32[]{:S(2)}, u32[]{:S(2)}) %collective-permute-start.12) | collective-permute-done | bytes 524320 | tf_op jit(solution)/shard_map/ppermute | solution.py:456
  53.4 1.4 %shard_map.103 = (bf16[256,128]{1,0:T(8,128)(2,1)S(1)}, bf16[256,128]{1,0:T(8,128)(2,1)S(1)}, bf16[256,128]{1,0:T(8,128)(2,1)S(1)}, bf16[256,128]{1,0:T(8,128)(2,1)S(1)}) custom-call(s32[3]{0:T(128)S(1)} %pad_add_fusion.where_ref, bf16[512,128]{1,0:T(8,128)(2,1)S(1)} %get-tuple-element.52.both0, bf16[512,128]{1,0:T(8,128)(2,1)S(1)} %collective-permute-done.5.both1, ...), custom_call_target="tpu_custom_call" | custom-call | flops 10000000 | bytes 1310732 | tf_op jit(solution)/shard_map/pallas_call | solution.py:216
  54.9 0.8 collective-permute-start.13
  55.6 0.0 collective-permute-start.14
  55.6 2.8 %collective-permute-start.15 = (bf16[256,128]{1,0:T(8,128)(2,1)S(1)}, bf16[256,128]{1,0:T(8,128)(2,1)S(1)}, u32[]{:S(2)}, u32[]{:S(2)}) collective-permute-start(bf16[256,128]{1,0:T(8,128)(2,1)S(1)} %get-tuple-element.63), channel_id=1, source_target_pairs={{0,6},{1,7},{2,4},{3,5},{4,2},{5,3},{6,0},{7,1},{8,14},{9,15},{10,... | collective-permute-start | bytes 196616 | tf_op jit(solution)/shard_map/ppermute | solution.py:451
  58.4 0.8 collective-permute-done.13.in1
  59.2 1.1 %collective-permute-done.14.in2 = bf16[256,128]{1,0:T(8,128)(2,1)S(1)} collective-permute-done((bf16[256,128]{1,0:T(8,128)(2,1)S(1)}, bf16[256,128]{1,0:T(8,128)(2,1)S(1)}, u32[]{:S(2)}, u32[]{:S(2)}) %collective-permute-start.14) | collective-permute-done | bytes 65568 | tf_op jit(solution)/shard_map/ppermute | solution.py:451
  60.3 1.4 %collective-permute-done.15.in3 = bf16[256,128]{1,0:T(8,128)(2,1)S(1)} collective-permute-done((bf16[256,128]{1,0:T(8,128)(2,1)S(1)}, bf16[256,128]{1,0:T(8,128)(2,1)S(1)}, u32[]{:S(2)}, u32[]{:S(2)}) %collective-permute-start.15) | collective-permute-done | bytes 65568 | tf_op jit(solution)/shard_map/ppermute | solution.py:451
  61.7 2.5 %shard_map.104 = (f32[8,128,128]{2,1,0:T(8,128)S(1)}, f32[8,128,128]{2,1,0:T(8,128)S(1)}, bf16[256,128]{1,0:T(8,128)(2,1)S(1)}, bf16[256,128]{1,0:T(8,128)(2,1)S...) custom-call(s32[3]{0:T(128)S(1)} %pad_add_fusion.where_ref, ...), custom_call_target="tpu_custom_call" | custom-call | flops 10000000 | bytes 1704972 | tf_op jit(solution)/shard_map/pallas_call | solution.py:216
  64.1 0.8 collective-permute-start.16
  65.0 1.7 %collective-permute-start.17 = (bf16[256,128]{1,0:T(8,128)(2,1)S(1)}, bf16[256,128]{1,0:T(8,128)(2,1)S(1)}, u32[]{:S(2)}, u32[]{:S(2)}) collective-permute-start(bf16[256,128]{1,0:T(8,128)(2,1)S(1)} %get-tuple-element.69), channel_id=1, source_target_pairs={{0,4},{1,5},{2,6},{3,7},{4,0},{5,1},{6,2},{7,3},{8,12},{9,13},{10,... | collective-permute-start | bytes 196616 | tf_op jit(solution)/shard_map/ppermute | solution.py:451
  66.7 1.0 collective-permute-start.18
  67.7 2.2 %collective-permute-start.19 = (bf16[256,128]{1,0:T(8,128)(2,1)S(1)}, bf16[256,128]{1,0:T(8,128)(2,1)S(1)}, u32[]{:S(2)}, u32[]{:S(2)}) collective-permute-start(bf16[256,128]{1,0:T(8,128)(2,1)S(1)} %get-tuple-element.71), channel_id=1, source_target_pairs={{0,8},{1,9},{2,10},{3,11},{4,12},{5,13},{6,14},{7,15},{8,0},{9,1},... | collective-permute-start | bytes 196616 | tf_op jit(solution)/shard_map/ppermute | solution.py:451
  69.9 0.9 collective-permute-start.20
  70.8 2.4 %collective-permute-start.21 = (bf16[256,128]{1,0:T(8,128)(2,1)S(1)}, bf16[256,128]{1,0:T(8,128)(2,1)S(1)}, u32[]{:S(2)}, u32[]{:S(2)}) collective-permute-start(bf16[256,128]{1,0:T(8,128)(2,1)S(1)} %get-tuple-element.73), channel_id=1, source_target_pairs={{0,12},{1,13},{2,14},{3,15},{4,8},{5,9},{6,10},{7,11},{8,4},{9,5},... | collective-permute-start | bytes 196616 | tf_op jit(solution)/shard_map/ppermute | solution.py:451
  73.2 2.1 %collective-permute-start.22 = (bf16[256,128]{1,0:T(8,128)(2,1)S(1)}, bf16[256,128]{1,0:T(8,128)(2,1)S(1)}, u32[]{:S(2)}, u32[]{:S(2)}) collective-permute-start(bf16[256,128]{1,0:T(8,128)(2,1)S(1)} %get-tuple-element.74), channel_id=1, source_target_pairs={{0,14},{1,15},{2,12},{3,13},{4,10},{5,11},{6,8},{7,9},{8,6},{9,7},... | collective-permute-start | bytes 196616 | tf_op jit(solution)/shard_map/ppermute | solution.py:451
  75.3 2.1 %collective-permute-done.19.b4 = bf16[256,128]{1,0:T(8,128)(2,1)S(1)} collective-permute-done((bf16[256,128]{1,0:T(8,128)(2,1)S(1)}, bf16[256,128]{1,0:T(8,128)(2,1)S(1)}, u32[]{:S(2)}, u32[]{:S(2)}) %collective-permute-start.19) | collective-permute-done | bytes 65568 | tf_op jit(solution)/shard_map/ppermute | solution.py:451
  77.4 1.9 %collective-permute-done.20.b5 = bf16[256,128]{1,0:T(8,128)(2,1)S(1)} collective-permute-done((bf16[256,128]{1,0:T(8,128)(2,1)S(1)}, bf16[256,128]{1,0:T(8,128)(2,1)S(1)}, u32[]{:S(2)}, u32[]{:S(2)}) %collective-permute-start.20) | collective-permute-done | bytes 65568 | tf_op jit(solution)/shard_map/ppermute | solution.py:451
  79.3 1.0 collective-permute-done.22.b7
  80.3 1.4 %shard_map.105 = (f32[8,128,128]{2,1,0:T(8,128)S(1)}, f32[8,128,128]{2,1,0:T(8,128)S(1)}) custom-call(s32[3]{0:T(128)S(1)} %pad_add_fusion.where_ref, bf16[256,128]{1,0:T(8,128)(2,1)S(1)} %get-tuple-element.67.b0, bf16[256,128]{1,0:T(8,128)(2,1)S(1)} %collective-permute-done.16.b1, bf16[256,128]{1,0:T(8,128)(2,1)S(1)} %collective-permute-done.17.b2, ...), custom_call_target="tpu_custom_call" | custom-call | flops 10000000 | bytes 524300 | tf_op jit(solution)/shard_map/pallas_call | solution.py:216
  81.7 0.1 collective-permute-start.23
  81.8 1.9 %collective-permute-done.23.got_ref = f32[8,128,128]{2,1,0:T(8,128)S(1)} collective-permute-done((f32[8,128,128]{2,1,0:T(8,128)S(1)}, f32[8,128,128]{2,1,0:T(8,128)S(1)}, u32[]{:S(2)}, u32[]{:S(2)}) %collective-permute-start.23) | collective-permute-done | bytes 524320 | tf_op jit(solution)/shard_map/ppermute | solution.py:456
  83.7 0.1 shard_map.106
  83.8 0.7 collective-permute-start.24
  84.5 1.9 %collective-permute-start.25 = (bf16[128,128]{1,0:T(8,128)(2,1)S(1)}, bf16[128,128]{1,0:T(8,128)(2,1)S(1)}, u32[]{:S(2)}, u32[]{:S(2)}) collective-permute-start(bf16[128,128]{1,0:T(8,128)(2,1)S(1)} %get-tuple-element.79), channel_id=1, source_target_pairs={{0,4},{1,5},{2,6},{3,7},{4,0},{5,1},{6,2},{7,3},{8,12},{9,13},{10,... | collective-permute-start | bytes 98312 | tf_op jit(solution)/shard_map/ppermute | solution.py:451
  86.4 0.9 collective-permute-start.26
  87.3 1.8 %collective-permute-start.27 = (bf16[128,128]{1,0:T(8,128)(2,1)S(1)}, bf16[128,128]{1,0:T(8,128)(2,1)S(1)}, u32[]{:S(2)}, u32[]{:S(2)}) collective-permute-start(bf16[128,128]{1,0:T(8,128)(2,1)S(1)} %get-tuple-element.81), channel_id=1, source_target_pairs={{0,8},{1,9},{2,10},{3,11},{4,12},{5,13},{6,14},{7,15},{8,0},{9,1},... | collective-permute-start | bytes 98312 | tf_op jit(solution)/shard_map/ppermute | solution.py:451
  89.1 1.2 %collective-permute-start.28 = (bf16[128,128]{1,0:T(8,128)(2,1)S(1)}, bf16[128,128]{1,0:T(8,128)(2,1)S(1)}, u32[]{:S(2)}, u32[]{:S(2)}) collective-permute-start(bf16[128,128]{1,0:T(8,128)(2,1)S(1)} %get-tuple-element.82), channel_id=1, source_target_pairs={{0,10},{1,11},{2,8},{3,9},{4,14},{5,15},{6,12},{7,13},{8,2},{9,3},... | collective-permute-start | bytes 98312 | tf_op jit(solution)/shard_map/ppermute | solution.py:451
  90.3 2.0 %collective-permute-start.29 = (bf16[128,128]{1,0:T(8,128)(2,1)S(1)}, bf16[128,128]{1,0:T(8,128)(2,1)S(1)}, u32[]{:S(2)}, u32[]{:S(2)}) collective-permute-start(bf16[128,128]{1,0:T(8,128)(2,1)S(1)} %get-tuple-element.83), channel_id=1, source_target_pairs={{0,12},{1,13},{2,14},{3,15},{4,8},{5,9},{6,10},{7,11},{8,4},{9,5},... | collective-permute-start | bytes 98312 | tf_op jit(solution)/shard_map/ppermute | solution.py:451
  92.3 2.6 %collective-permute-start.30 = (bf16[128,128]{1,0:T(8,128)(2,1)S(1)}, bf16[128,128]{1,0:T(8,128)(2,1)S(1)}, u32[]{:S(2)}, u32[]{:S(2)}) collective-permute-start(bf16[128,128]{1,0:T(8,128)(2,1)S(1)} %get-tuple-element.84), channel_id=1, source_target_pairs={{0,14},{1,15},{2,12},{3,13},{4,10},{5,11},{6,8},{7,9},{8,6},{9,7},... | collective-permute-start | bytes 98312 | tf_op jit(solution)/shard_map/ppermute | solution.py:451
  95.0 0.5 collective-permute-done.28.b5
  95.5 0.9 collective-permute-done.29.b6
  96.3 2.7 %collective-permute-done.30.b7 = bf16[128,128]{1,0:T(8,128)(2,1)S(1)} collective-permute-done((bf16[128,128]{1,0:T(8,128)(2,1)S(1)}, bf16[128,128]{1,0:T(8,128)(2,1)S(1)}, u32[]{:S(2)}, u32[]{:S(2)}) %collective-permute-start.30) | collective-permute-done | bytes 32800 | tf_op jit(solution)/shard_map/ppermute | solution.py:451
  99.0 2.2 %shard_map.107 = bf16[8,128,128]{2,1,0:T(8,128)(2,1)} custom-call(s32[3]{0:T(128)S(1)} %pad_add_fusion.where_ref, bf16[128,128]{1,0:T(8,128)(2,1)S(1)} %get-tuple-element.77.b0, bf16[128,128]{1,0:T(8,128)(2,1)S(1)} %collective-permute-done.24.b1, bf16[128,128]{1,0:T(8,128)(2,1)S(1)} %collective-permute-done.25.b2, ...), custom_call_target="tpu_custom_call" | custom-call | flops 10000000 | bytes 1376268 | tf_op jit(solution)/shard_map/pallas_call | solution.py:216
  (43 shorter events, 0.2 us)
Async XLA Ops:
  0.0 0.8 copy-start.8
  0.0 0.7 copy-start.9
  1.0 0.7 copy-start.6
  1.7 0.9 copy-start.1
  2.6 16.9 %copy-start.4 = (bf16[2,128,128]{2,1,0:T(8,128)(2,1)S(1)}, bf16[2,128,128]{2,1,0:T(8,128)(2,1)}, u32[]{:S(2)}) copy-start(bf16[2,128,128]{2,1,0:T(8,128)(2,1)} %out_ref.1) | copy-start | bytes 196612
  4.1 7.0 %collective-permute-start.2 = (bf16[144,128]{1,0:T(8,128)(2,1)S(1)}, bf16[144,128]{1,0:T(8,128)(2,1)S(1)}, u32[]{:S(2)}, u32[]{:S(2)}) collective-permute-start(bf16[144,128]{1,0:T(8,128)(2,1)S(1)} %get-tuple-element.46), channel_id=1, source_target_pairs={{0,12},{1,13},{2,14},{3,15},{4,8},{5,9},{6,10},{7,11},{8,4},{9,5},... | collective-permute-start | bytes 110600 | tf_op jit(solution)/shard_map/ppermute | solution.py:451
  9.3 4.9 %collective-permute-start.1 = (bf16[144,128]{1,0:T(8,128)(2,1)S(1)}, bf16[144,128]{1,0:T(8,128)(2,1)S(1)}, u32[]{:S(2)}, u32[]{:S(2)}) collective-permute-start(bf16[144,128]{1,0:T(8,128)(2,1)S(1)} %get-tuple-element.46), channel_id=1, source_target_pairs={{0,8},{1,9},{2,10},{3,11},{4,12},{5,13},{6,14},{7,15},{8,0},{9,1},... | collective-permute-start | bytes 110600 | tf_op jit(solution)/shard_map/ppermute | solution.py:451
  9.3 4.9 %collective-permute-start = (bf16[144,128]{1,0:T(8,128)(2,1)S(1)}, bf16[144,128]{1,0:T(8,128)(2,1)S(1)}, u32[]{:S(2)}, u32[]{:S(2)}) collective-permute-start(bf16[144,128]{1,0:T(8,128)(2,1)S(1)} %get-tuple-element.46), channel_id=1, source_target_pairs={{0,4},{1,5},{2,6},{3,7},{4,0},{5,1},{6,2},{7,3},{8,12},{9,13},{10,... | collective-permute-start | bytes 110600 | tf_op jit(solution)/shard_map/ppermute | solution.py:451
  9.9 9.6 %copy-start.3 = (bf16[1024,128]{1,0:T(8,128)(2,1)S(1)}, bf16[1024,128]{1,0:T(8,128)(2,1)}, u32[]{:S(2)}) copy-start(bf16[1024,128]{1,0:T(8,128)(2,1)} %outer_ref.1) | copy-start | bytes 786436
  14.1 5.4 %copy-start.2 = (bf16[8,128,128]{2,1,0:T(8,128)(2,1)S(1)}, bf16[8,128,128]{2,1,0:T(8,128)(2,1)}, u32[]{:S(2)}) copy-start(bf16[8,128,128]{2,1,0:T(8,128)(2,1)} %pair_ref.1) | copy-start | bytes 786436
  14.1 5.4 %copy-start = (bf16[2,128,640]{2,1,0:T(8,128)(2,1)S(1)}, bf16[2,128,640]{2,1,0:T(8,128)(2,1)}, u32[]{:S(2)}) copy-start(bf16[2,128,640]{2,1,0:T(8,128)(2,1)} %proj_ref.1) | copy-start | bytes 983044
  14.2 5.2 %collective-permute-start.3 = (bf16[4,144,128]{2,1,0:T(8,128)(2,1)S(1)}, bf16[4,144,128]{2,1,0:T(8,128)(2,1)S(1)}, u32[]{:S(2)}, u32[]{:S(2)}) collective-permute-start(bf16[4,144,128]{2,1,0:T(8,128)(2,1)S(1)} %pad_maximum_fusion), channel_id=1, source_target_pairs={{0,2},{1,3},{2,0},{3,1},{4,6},{5,7},{6,4},{7,5},{8,10},{9,11},{10,... | collective-permute-start | bytes 442376 | tf_op jit(solution)/shard_map/ppermute | solution.py:451
  15.8 3.8 %copy-start.5 = (bf16[66,128]{1,0:T(8,128)(2,1)S(1)}, bf16[66,128]{1,0:T(8,128)(2,1)}, u32[]{:S(2)}) copy-start(bf16[66,128]{1,0:T(8,128)(2,1)} %table_ref.1) | copy-start | bytes 50692
  19.4 0.7 copy-start.7
  19.4 2.7 %collective-permute-start.4 = (bf16[8,144,128]{2,1,0:T(8,128)(2,1)S(1)}, bf16[8,144,128]{2,1,0:T(8,128)(2,1)S(1)}, u32[]{:S(2)}, u32[]{:S(2)}) collective-permute-start(bf16[8,144,128]{2,1,0:T(8,128)(2,1)S(1)} %constant_dynamic-update-slice_fusion.own_ref), channel_id=1, source_target_pairs={{0,1},{1,0},{2,3},{3,2},{4,5},{5,4},{6,7},{7,6},{8,9},{9,8},{10,11... | collective-permute-start | bytes 884744 | tf_op jit(solution)/shard_map/ppermute | solution.py:456
  26.1 25.2 %collective-permute-start.8 = (bf16[256,128]{1,0:T(8,128)(2,1)S(1)}, bf16[256,128]{1,0:T(8,128)(2,1)S(1)}, u32[]{:S(2)}, u32[]{:S(2)}) collective-permute-start(bf16[256,128]{1,0:T(8,128)(2,1)S(1)} %get-tuple-element.56), channel_id=1, source_target_pairs={{0,8},{1,9},{2,10},{3,11},{4,12},{5,13},{6,14},{7,15},{8,0},{9,1},... | collective-permute-start | bytes 196616 | tf_op jit(solution)/shard_map/ppermute | solution.py:451
  28.2 23.2 %collective-permute-start.9 = (bf16[256,128]{1,0:T(8,128)(2,1)S(1)}, bf16[256,128]{1,0:T(8,128)(2,1)S(1)}, u32[]{:S(2)}, u32[]{:S(2)}) collective-permute-start(bf16[256,128]{1,0:T(8,128)(2,1)S(1)} %get-tuple-element.57), channel_id=1, source_target_pairs={{0,10},{1,11},{2,8},{3,9},{4,14},{5,15},{6,12},{7,13},{8,2},{9,3},... | collective-permute-start | bytes 196616 | tf_op jit(solution)/shard_map/ppermute | solution.py:451
  30.1 21.3 %collective-permute-start.10 = (bf16[256,128]{1,0:T(8,128)(2,1)S(1)}, bf16[256,128]{1,0:T(8,128)(2,1)S(1)}, u32[]{:S(2)}, u32[]{:S(2)}) collective-permute-start(bf16[256,128]{1,0:T(8,128)(2,1)S(1)} %get-tuple-element.58), channel_id=1, source_target_pairs={{0,12},{1,13},{2,14},{3,15},{4,8},{5,9},{6,10},{7,11},{8,4},{9,5},... | collective-permute-start | bytes 196616 | tf_op jit(solution)/shard_map/ppermute | solution.py:451
  31.5 19.9 %collective-permute-start.11 = (bf16[256,128]{1,0:T(8,128)(2,1)S(1)}, bf16[256,128]{1,0:T(8,128)(2,1)S(1)}, u32[]{:S(2)}, u32[]{:S(2)}) collective-permute-start(bf16[256,128]{1,0:T(8,128)(2,1)S(1)} %get-tuple-element.59), channel_id=1, source_target_pairs={{0,14},{1,15},{2,12},{3,13},{4,10},{5,11},{6,8},{7,9},{8,6},{9,7},... | collective-permute-start | bytes 196616 | tf_op jit(solution)/shard_map/ppermute | solution.py:451
  33.8 6.6 %collective-permute-start.5 = (bf16[512,128]{1,0:T(8,128)(2,1)S(1)}, bf16[512,128]{1,0:T(8,128)(2,1)S(1)}, u32[]{:S(2)}, u32[]{:S(2)}) collective-permute-start(bf16[512,128]{1,0:T(8,128)(2,1)S(1)} %get-tuple-element.53), channel_id=1, source_target_pairs={{0,2},{1,3},{2,0},{3,1},{4,6},{5,7},{6,4},{7,5},{8,10},{9,11},{10,... | collective-permute-start | bytes 393224 | tf_op jit(solution)/shard_map/ppermute | solution.py:451
  40.5 5.0 %collective-permute-start.6 = (bf16[512,128]{1,0:T(8,128)(2,1)S(1)}, bf16[512,128]{1,0:T(8,128)(2,1)S(1)}, u32[]{:S(2)}, u32[]{:S(2)}) collective-permute-start(bf16[512,128]{1,0:T(8,128)(2,1)S(1)} %get-tuple-element.54), channel_id=1, source_target_pairs={{0,4},{1,5},{2,6},{3,7},{4,0},{5,1},{6,2},{7,3},{8,12},{9,13},{10,... | collective-permute-start | bytes 393224 | tf_op jit(solution)/shard_map/ppermute | solution.py:451
  45.5 5.9 %collective-permute-start.7 = (bf16[512,128]{1,0:T(8,128)(2,1)S(1)}, bf16[512,128]{1,0:T(8,128)(2,1)S(1)}, u32[]{:S(2)}, u32[]{:S(2)}) collective-permute-start(bf16[512,128]{1,0:T(8,128)(2,1)S(1)} %get-tuple-element.55), channel_id=1, source_target_pairs={{0,6},{1,7},{2,4},{3,5},{4,2},{5,3},{6,0},{7,1},{8,14},{9,15},{10,... | collective-permute-start | bytes 393224 | tf_op jit(solution)/shard_map/ppermute | solution.py:451
  51.5 2.0 %collective-permute-start.12 = (bf16[8,256,128]{2,1,0:T(8,128)(2,1)S(1)}, bf16[8,256,128]{2,1,0:T(8,128)(2,1)S(1)}, u32[]{:S(2)}, u32[]{:S(2)}) collective-permute-start(bf16[8,256,128]{2,1,0:T(8,128)(2,1)S(1)} %bitcast_dynamic-update-slice_fusion), channel_id=1, source_target_pairs={{0,1},{1,0},{2,3},{3,2},{4,5},{5,4},{6,7},{7,6},{8,9},{9,8},{10,11... | collective-permute-start | bytes 1572872 | tf_op jit(solution)/shard_map/ppermute | solution.py:456
  54.9 4.3 %collective-permute-start.13 = (bf16[256,128]{1,0:T(8,128)(2,1)S(1)}, bf16[256,128]{1,0:T(8,128)(2,1)S(1)}, u32[]{:S(2)}, u32[]{:S(2)}) collective-permute-start(bf16[256,128]{1,0:T(8,128)(2,1)S(1)} %get-tuple-element.61), channel_id=1, source_target_pairs={{0,2},{1,3},{2,0},{3,1},{4,6},{5,7},{6,4},{7,5},{8,10},{9,11},{10,... | collective-permute-start | bytes 196616 | tf_op jit(solution)/shard_map/ppermute | solution.py:451
  55.6 4.6 %collective-permute-start.14 = (bf16[256,128]{1,0:T(8,128)(2,1)S(1)}, bf16[256,128]{1,0:T(8,128)(2,1)S(1)}, u32[]{:S(2)}, u32[]{:S(2)}) collective-permute-start(bf16[256,128]{1,0:T(8,128)(2,1)S(1)} %get-tuple-element.62), channel_id=1, source_target_pairs={{0,4},{1,5},{2,6},{3,7},{4,0},{5,1},{6,2},{7,3},{8,12},{9,13},{10,... | collective-permute-start | bytes 196616 | tf_op jit(solution)/shard_map/ppermute | solution.py:451
  55.6 6.0 %collective-permute-start.15 = (bf16[256,128]{1,0:T(8,128)(2,1)S(1)}, bf16[256,128]{1,0:T(8,128)(2,1)S(1)}, u32[]{:S(2)}, u32[]{:S(2)}) collective-permute-start(bf16[256,128]{1,0:T(8,128)(2,1)S(1)} %get-tuple-element.63), channel_id=1, source_target_pairs={{0,6},{1,7},{2,4},{3,5},{4,2},{5,3},{6,0},{7,1},{8,14},{9,15},{10,... | collective-permute-start | bytes 196616 | tf_op jit(solution)/shard_map/ppermute | solution.py:451
  64.1 6.7 %collective-permute-start.16 = (bf16[256,128]{1,0:T(8,128)(2,1)S(1)}, bf16[256,128]{1,0:T(8,128)(2,1)S(1)}, u32[]{:S(2)}, u32[]{:S(2)}) collective-permute-start(bf16[256,128]{1,0:T(8,128)(2,1)S(1)} %get-tuple-element.68), channel_id=1, source_target_pairs={{0,2},{1,3},{2,0},{3,1},{4,6},{5,7},{6,4},{7,5},{8,10},{9,11},{10,... | collective-permute-start | bytes 196616 | tf_op jit(solution)/shard_map/ppermute | solution.py:451
  65.0 8.3 %collective-permute-start.17 = (bf16[256,128]{1,0:T(8,128)(2,1)S(1)}, bf16[256,128]{1,0:T(8,128)(2,1)S(1)}, u32[]{:S(2)}, u32[]{:S(2)}) collective-permute-start(bf16[256,128]{1,0:T(8,128)(2,1)S(1)} %get-tuple-element.69), channel_id=1, source_target_pairs={{0,4},{1,5},{2,6},{3,7},{4,0},{5,1},{6,2},{7,3},{8,12},{9,13},{10,... | collective-permute-start | bytes 196616 | tf_op jit(solution)/shard_map/ppermute | solution.py:451
  66.7 8.7 %collective-permute-start.18 = (bf16[256,128]{1,0:T(8,128)(2,1)S(1)}, bf16[256,128]{1,0:T(8,128)(2,1)S(1)}, u32[]{:S(2)}, u32[]{:S(2)}) collective-permute-start(bf16[256,128]{1,0:T(8,128)(2,1)S(1)} %get-tuple-element.70), channel_id=1, source_target_pairs={{0,6},{1,7},{2,4},{3,5},{4,2},{5,3},{6,0},{7,1},{8,14},{9,15},{10,... | collective-permute-start | bytes 196616 | tf_op jit(solution)/shard_map/ppermute | solution.py:451
  67.7 9.7 %collective-permute-start.19 = (bf16[256,128]{1,0:T(8,128)(2,1)S(1)}, bf16[256,128]{1,0:T(8,128)(2,1)S(1)}, u32[]{:S(2)}, u32[]{:S(2)}) collective-permute-start(bf16[256,128]{1,0:T(8,128)(2,1)S(1)} %get-tuple-element.71), channel_id=1, source_target_pairs={{0,8},{1,9},{2,10},{3,11},{4,12},{5,13},{6,14},{7,15},{8,0},{9,1},... | collective-permute-start | bytes 196616 | tf_op jit(solution)/shard_map/ppermute | solution.py:451
  69.9 9.4 %collective-permute-start.20 = (bf16[256,128]{1,0:T(8,128)(2,1)S(1)}, bf16[256,128]{1,0:T(8,128)(2,1)S(1)}, u32[]{:S(2)}, u32[]{:S(2)}) collective-permute-start(bf16[256,128]{1,0:T(8,128)(2,1)S(1)} %get-tuple-element.72), channel_id=1, source_target_pairs={{0,10},{1,11},{2,8},{3,9},{4,14},{5,15},{6,12},{7,13},{8,2},{9,3},... | collective-permute-start | bytes 196616 | tf_op jit(solution)/shard_map/ppermute | solution.py:451
  70.8 8.5 %collective-permute-start.21 = (bf16[256,128]{1,0:T(8,128)(2,1)S(1)}, bf16[256,128]{1,0:T(8,128)(2,1)S(1)}, u32[]{:S(2)}, u32[]{:S(2)}) collective-permute-start(bf16[256,128]{1,0:T(8,128)(2,1)S(1)} %get-tuple-element.73), channel_id=1, source_target_pairs={{0,12},{1,13},{2,14},{3,15},{4,8},{5,9},{6,10},{7,11},{8,4},{9,5},... | collective-permute-start | bytes 196616 | tf_op jit(solution)/shard_map/ppermute | solution.py:451
  73.2 7.1 %collective-permute-start.22 = (bf16[256,128]{1,0:T(8,128)(2,1)S(1)}, bf16[256,128]{1,0:T(8,128)(2,1)S(1)}, u32[]{:S(2)}, u32[]{:S(2)}) collective-permute-start(bf16[256,128]{1,0:T(8,128)(2,1)S(1)} %get-tuple-element.74), channel_id=1, source_target_pairs={{0,14},{1,15},{2,12},{3,13},{4,10},{5,11},{6,8},{7,9},{8,6},{9,7},... | collective-permute-start | bytes 196616 | tf_op jit(solution)/shard_map/ppermute | solution.py:451
  81.7 2.0 %collective-permute-start.23 = (f32[8,128,128]{2,1,0:T(8,128)S(1)}, f32[8,128,128]{2,1,0:T(8,128)S(1)}, u32[]{:S(2)}, u32[]{:S(2)}) collective-permute-start(f32[8,128,128]{2,1,0:T(8,128)S(1)} %get-tuple-element.76), channel_id=1, source_target_pairs={{0,1},{1,0},{2,3},{3,2},{4,5},{5,4},{6,7},{7,6},{8,9},{9,8},{10,11... | collective-permute-start | bytes 1572872 | tf_op jit(solution)/shard_map/ppermute | solution.py:456
  83.8 6.6 %collective-permute-start.24 = (bf16[128,128]{1,0:T(8,128)(2,1)S(1)}, bf16[128,128]{1,0:T(8,128)(2,1)S(1)}, u32[]{:S(2)}, u32[]{:S(2)}) collective-permute-start(bf16[128,128]{1,0:T(8,128)(2,1)S(1)} %get-tuple-element.78), channel_id=1, source_target_pairs={{0,2},{1,3},{2,0},{3,1},{4,6},{5,7},{6,4},{7,5},{8,10},{9,11},{10,... | collective-permute-start | bytes 98312 | tf_op jit(solution)/shard_map/ppermute | solution.py:451
  84.5 7.9 %collective-permute-start.25 = (bf16[128,128]{1,0:T(8,128)(2,1)S(1)}, bf16[128,128]{1,0:T(8,128)(2,1)S(1)}, u32[]{:S(2)}, u32[]{:S(2)}) collective-permute-start(bf16[128,128]{1,0:T(8,128)(2,1)S(1)} %get-tuple-element.79), channel_id=1, source_target_pairs={{0,4},{1,5},{2,6},{3,7},{4,0},{5,1},{6,2},{7,3},{8,12},{9,13},{10,... | collective-permute-start | bytes 98312 | tf_op jit(solution)/shard_map/ppermute | solution.py:451
  86.4 8.6 %collective-permute-start.26 = (bf16[128,128]{1,0:T(8,128)(2,1)S(1)}, bf16[128,128]{1,0:T(8,128)(2,1)S(1)}, u32[]{:S(2)}, u32[]{:S(2)}) collective-permute-start(bf16[128,128]{1,0:T(8,128)(2,1)S(1)} %get-tuple-element.80), channel_id=1, source_target_pairs={{0,6},{1,7},{2,4},{3,5},{4,2},{5,3},{6,0},{7,1},{8,14},{9,15},{10,... | collective-permute-start | bytes 98312 | tf_op jit(solution)/shard_map/ppermute | solution.py:451
  87.3 7.7 %collective-permute-start.27 = (bf16[128,128]{1,0:T(8,128)(2,1)S(1)}, bf16[128,128]{1,0:T(8,128)(2,1)S(1)}, u32[]{:S(2)}, u32[]{:S(2)}) collective-permute-start(bf16[128,128]{1,0:T(8,128)(2,1)S(1)} %get-tuple-element.81), channel_id=1, source_target_pairs={{0,8},{1,9},{2,10},{3,11},{4,12},{5,13},{6,14},{7,15},{8,0},{9,1},... | collective-permute-start | bytes 98312 | tf_op jit(solution)/shard_map/ppermute | solution.py:451
  89.1 6.3 %collective-permute-start.28 = (bf16[128,128]{1,0:T(8,128)(2,1)S(1)}, bf16[128,128]{1,0:T(8,128)(2,1)S(1)}, u32[]{:S(2)}, u32[]{:S(2)}) collective-permute-start(bf16[128,128]{1,0:T(8,128)(2,1)S(1)} %get-tuple-element.82), channel_id=1, source_target_pairs={{0,10},{1,11},{2,8},{3,9},{4,14},{5,15},{6,12},{7,13},{8,2},{9,3},... | collective-permute-start | bytes 98312 | tf_op jit(solution)/shard_map/ppermute | solution.py:451
  90.3 6.0 %collective-permute-start.29 = (bf16[128,128]{1,0:T(8,128)(2,1)S(1)}, bf16[128,128]{1,0:T(8,128)(2,1)S(1)}, u32[]{:S(2)}, u32[]{:S(2)}) collective-permute-start(bf16[128,128]{1,0:T(8,128)(2,1)S(1)} %get-tuple-element.83), channel_id=1, source_target_pairs={{0,12},{1,13},{2,14},{3,15},{4,8},{5,9},{6,10},{7,11},{8,4},{9,5},... | collective-permute-start | bytes 98312 | tf_op jit(solution)/shard_map/ppermute | solution.py:451
  92.3 6.6 %collective-permute-start.30 = (bf16[128,128]{1,0:T(8,128)(2,1)S(1)}, bf16[128,128]{1,0:T(8,128)(2,1)S(1)}, u32[]{:S(2)}, u32[]{:S(2)}) collective-permute-start(bf16[128,128]{1,0:T(8,128)(2,1)S(1)} %get-tuple-element.84), channel_id=1, source_target_pairs={{0,14},{1,15},{2,12},{3,13},{4,10},{5,11},{6,8},{7,9},{8,6},{9,7},... | collective-permute-start | bytes 98312 | tf_op jit(solution)/shard_map/ppermute | solution.py:451

commit v5 on v4

--- a/solution.py
+++ b/solution.py
@@ -207,19 +207,21 @@
     return (center * lax.rsqrt(spread + EPSILON)).astype(BF16)
 
 
-def run(kernel, outs, *args, smem=(), scratch=(), flops=10**7):
+def run(kernel, outs, *args, smem=(), hbm=(), scratch=(), flops=10**7, sems=0, limit=None):
     vmem = pl.BlockSpec(memory_space=pltpu.VMEM)
     in_specs = [
-        pl.BlockSpec(memory_space=pltpu.SMEM) if at in smem else vmem for at in range(len(args))
+        pl.BlockSpec(memory_space=pltpu.SMEM if at in smem else pltpu.HBM if at in hbm else pltpu.VMEM)
+        for at in range(len(args))
     ]
+    semaphores = [pltpu.SemaphoreType.DMA((sems,))] if sems else []
     moved = sum(a.size * a.dtype.itemsize for a in args)
     return pl.pallas_call(
         kernel,
         out_shape=[jax.ShapeDtypeStruct(shape, kind) for shape, kind in outs],
         in_specs=in_specs,
         out_specs=[vmem] * len(outs),
-        scratch_shapes=[pltpu.VMEM(shape, kind) for shape, kind in scratch],
-        compiler_params=pltpu.CompilerParams(vmem_limit_bytes=VMEM_LIMIT),
+        scratch_shapes=[pltpu.VMEM(shape, kind) for shape, kind in scratch] + semaphores,
+        compiler_params=pltpu.CompilerParams(vmem_limit_bytes=limit or VMEM_LIMIT),
         cost_estimate=pl.CostEstimate(flops=flops, bytes_accessed=moved, transcendentals=0),
     )(*args)
 
@@ -227,9 +229,18 @@
 VMEM_LIMIT = 20 * 1024 * 1024
 
 
-def project_kernel(where_ref, feat_ref, weight_ref, mask_ref, present_ref, pay_ref, left_ref, live_ref, turned, packed):
+def project_kernel(
+    where_ref, feat_hbm, weight_hbm, mask_hbm, present_hbm, pay_ref, left_ref, live_ref,
+    turned, packed, feat_ref, weight_ref, mask_ref, present_ref, sems,
+):
+    pairs = ((feat_hbm, feat_ref), (weight_hbm, weight_ref), (mask_hbm, mask_ref), (present_hbm, present_ref))
+    copies = [pltpu.make_async_copy(a, b, sems.at[at]) for at, (a, b) in enumerate(pairs)]
+    for copy in copies:
+        copy.start()
+    for copy in copies:
+        copy.wait()
     homologs, rows, _ = feat_ref.shape
-    half = weight_ref.shape[1] // 2
+    half = weight_ref.shape[0] // 2
     quarter = half // 2
     values = feat_ref[...].astype(F32).reshape(homologs * rows, feat_ref.shape[2])
     center = values - jnp.mean(values, axis=1, keepdims=True)
@@ -243,14 +254,14 @@
     seq = lax.broadcasted_iota(jnp.int32, (homologs, 2 * homologs), 0)
     lane = lax.broadcasted_iota(jnp.int32, (homologs, 2 * homologs), 1)
     twice = (seq == (lane & (homologs - 1))).astype(F32).astype(BF16)
-    live = tn(mask_ref[...], twice)
+    live = nn(mask_ref[...], twice)
     cols = present_ref.shape[1]
     here = lax.broadcasted_iota(jnp.int32, (rows, cols), 1) == (
         lax.broadcasted_iota(jnp.int32, (rows, cols), 0) + where_ref[0]
     )
     present = jnp.sum(jnp.where(here, present_ref[...].astype(F32), 0.0), axis=1, keepdims=True)
     live = live * present
-    weight = flip(weight_ref[...]).astype(BF16)
+    weight = weight_ref[...]
     blank = jnp.zeros((homologs, normed.shape[1]), BF16)
     for row in range(rows):
         mine = normed[row * homologs : (row + 1) * homologs]
@@ -312,7 +323,7 @@
     per = own_ref.shape[1]
     chips = own_ref.shape[0]
     for at in range(chips):
-        chip_at = chip ^ ((at % 4) * 2 + at // 4)
+        chip_at = chip ^ ((3 - at % 4) * 2 + at // 4)
         came[chip_at * 2 + core] = own_ref[at].astype(F32)
         came[chip_at * 2 + (1 - core)] = other_ref[at].astype(F32)
     half = left_ref.shape[0] // (2 * rows)
@@ -353,7 +364,7 @@
 
 
 def mix_rows_kernel(
-    where_ref, both0, both1, both2, both3, far4, far5, far6, far7, other_ref,
+    where_ref, far7, far6, far5, far4, both3, both2, both1, both0, other_ref,
     out0, out1, out2, out3, lefts, rights, mixed,
 ):
     chip, core = where_ref[1], where_ref[2]
@@ -364,7 +375,7 @@
     for step in range(8):
         mine = (nears[step][block:] if step < 4 else fars[step - 4][...]).astype(F32)
         rights[(chip ^ step) * 2 + core] = mine.reshape(count, rows, cols)
-        rights[(chip ^ step) * 2 + (1 - core)] = other_ref[step].astype(F32).reshape(count, rows, cols)
+        rights[(chip ^ step) * 2 + (1 - core)] = other_ref[7 - step].astype(F32).reshape(count, rows, cols)
         if step < 4:
             lefts[step] = nears[step][0:block].astype(F32).reshape(count, rows, cols)
     for c in range(count):
@@ -382,7 +393,7 @@
 
 
 def between_kernel(
-    where_ref, flag_ref, in0, in1, in2, in3, stream_ref, gate_ref, out_weight_ref, proj_ref, present_ref,
+    where_ref, flag_ref, in3, in2, in1, in0, stream_ref, gate_ref, out_weight_ref, proj_ref, present_ref,
     next_ref, next_gate_ref, b0, b1, b2, b3, b4, b5, b6, b7, came, lefts, rights,
 ):
     rows, width, cols = stream_ref.shape
@@ -407,7 +418,7 @@
         out[size * rows :] = rights[pl.ds(first, size)].reshape(size * rows, cols).astype(BF16)
 
 
-def mix_cols_kernel(where_ref, b0, b1, b2, b3, b4, b5, b6, b7, mine_ref, theirs_ref, lefts, rights, partial):
+def mix_cols_kernel(where_ref, b7, b6, b5, b4, b3, b2, b1, b0, mine_ref, theirs_ref, lefts, rights, partial):
     chip, core = where_ref[1], where_ref[2]
     chips, count, rows, cols = lefts.shape
     block = count * rows
@@ -430,7 +441,7 @@
 
 
 def final_kernel(
-    where_ref, b0, b1, b2, b3, b4, b5, b6, b7, stream_ref, gate_ref, out_weight_ref, out_ref, came
+    where_ref, b7, b6, b5, b4, b3, b2, b1, b0, stream_ref, gate_ref, out_weight_ref, out_ref, came
 ):
     rows, width, cols = stream_ref.shape
     chip = where_ref[1]
@@ -479,9 +490,19 @@
     pay, left, live = run(
         project_kernel,
         [((pay_rows, LANES), BF16), ((2 * rows * half, LANES), BF16), ((rows, LANES), F32)],
-        where, homolog_features, homolog_to_sides_matrix, alignment_mask, present,
+        where, homolog_features, homolog_to_sides_matrix.T, alignment_mask.T, present,
         smem=(0,),
-        scratch=[((rows, half // 2, LANES), F32), ((pay_rows, LANES), F32)],
+        hbm=(1, 2, 3, 4),
+        scratch=[
+            ((rows, half // 2, LANES), F32),
+            ((pay_rows, LANES), F32),
+            (homolog_features.shape, BF16),
+            (homolog_to_sides_matrix.shape[::-1], BF16),
+            (alignment_mask.shape[::-1], BF16),
+            ((1, cols), jnp.int32),
+        ],
+        sems=4,
+        limit=60 * 1024 * 1024,
     )
     along_z = [chip_permute(pay, 2 * z) for z in (2, 3, 1)]
     base, outer_t, proj_t, out_t = run(
@@ -497,7 +518,8 @@
         smem=(0, 1),
         scratch=[((LANES, width), F32), ((half, half, width), F32)],
     )
-    along_z = jnp.stack([pay, along_z[2], along_z[0], along_z[1]])
+    along_z = jnp.stack([along_z[1], along_z[0], along_z[2], pay])
+    along_z, base, outer_t, proj_t, out_t = lax.optimization_barrier((along_z, base, outer_t, proj_t, out_t))
     own = jnp.concatenate([along_z, chip_permute(along_z, 1)], axis=0)
     other = core_permute(own)
     tall = width * rows
@@ -519,12 +541,12 @@
     stream, gate, both, far = made[0], made[1], made[2:6], made[6:10]
     far = [chip_permute(far[step], step + 4) for step in (3, 2, 1, 0)][::-1]
     near = [chip_permute(both[step], step) for step in (3, 2, 1)][::-1]
-    rights = jnp.stack([b[tall // 4 :] for b in [both[0]] + near] + far)
+    rights = jnp.stack(far[::-1] + [b[tall // 4 :] for b in near[::-1] + [both[0]]])
     rights = core_permute(rights)
     mixed = run(
         mix_rows_kernel,
         [((tall // 4, cols), BF16)] * 4,
-        where, both[0], *near, *far, rights,
+        where, *far[::-1], *near[::-1], both[0], rights,
         smem=(0,),
         scratch=[
             ((4, width // 4, rows, cols), F32),
@@ -536,7 +558,7 @@
     made = run(
         between_kernel,
         [((rows, width, cols), F32)] * 2 + [((tall // 4, cols), BF16)] * 8,
-        where, resolved_residue_mask, *mixed, stream, gate, out_t, proj_t, present,
+        where, resolved_residue_mask, *mixed[::-1], stream, gate, out_t, proj_t, present,
         smem=(0, 1),
         scratch=[
             ((rows, 4, width // 4, cols), F32),
@@ -549,7 +571,7 @@
     mine, theirs = run(
         mix_cols_kernel,
         [((8, tall // 8, cols), F32)] * 2,
-        where, *came,
+        where, *came[::-1],
         smem=(0,),
         scratch=[
             ((8, width // 8, rows, cols), F32),
@@ -562,7 +584,7 @@
     return run(
         final_kernel,
         [((rows, cols, width), BF16)],
-        where, *mixed, stream, gate, out_t,
+        where, *mixed[::-1], stream, gate, out_t,
         smem=(0,),
         scratch=[((rows, 8, width // 8, cols), F32)],
     )[0]

time: 101 us -> 92.8 us (0.919)
  waiting for transfers between devices: 39.6 us -> 26.5 us
  starting transfers between devices: 42.8 us -> 44.7 us
  Pallas kernels: 15.1 us -> 17 us
    ppermute x28, waiting for transfers between devices: 35.8 us -> 21.1 us  [chip_permute(): lax.ppermute(block, 'wide', [(w, w ^ 2 * step) for w in range(count)])]
    pallas_call x8, Pallas kernels: 15.1 us -> 17 us  [run(): pl.pallas_call(kernel, out_shape=[jax.ShapeDtypeStruct(shape, kind) for s...]
    ppermute x28, starting transfers between devices: 42.6 us -> 44.5 us  [chip_permute(): lax.ppermute(block, 'wide', [(w, w ^ 2 * step) for w in range(count)])]
    ppermute x3, waiting for transfers between devices: 3.8 us -> 5.36 us  [core_permute(): return lax.ppermute(block, 'wide', [(w, w ^ 1) for w in range(count)])]
    unnamed x33 -> x30, local copies, waits for them, and re-layouts: 3.18 us -> 3.51 us
where the time goes in v5:
time: 92.8 us; the launch traced here: 92.5 us
  starting transfers between devices  44.7 us (48%)
  waiting for transfers between devices  26.5 us (29%)
  Pallas kernels  17 us (18%)
  local copies, waits for them, and re-layouts  3.54 us (4%)
    ppermute x28, starting transfers between devices, chip_permute(): lax.ppermute(block, 'wide', [(w, w ^ 2 * step) for w in range(count)])  44.5 us
    ppermute x28, waiting for transfers between devices, chip_permute(): lax.ppermute(block, 'wide', [(w, w ^ 2 * step) for w in range(count)])  21.1 us
    pallas_call x8, Pallas kernels, run(): pl.pallas_call(kernel, out_shape=[jax.ShapeDtypeStruct(shape, kind) for s...  17 us
    ppermute x3, waiting for transfers between devices, core_permute(): return lax.ppermute(block, 'wide', [(w, w ^ 1) for w in range(count)])  5.36 us
    unnamed x30, local copies, waits for them, and re-layouts  3.51 us
  transfers between devices with their start and end apart: 31, of which 17 were waited for; matrix products, arithmetic and copies ran while one was open for 0% of the time, Pallas kernels for 2%

profile of v5, /device:TPU:0, one launch (start us, length us, event | category | flops | bytes accessed | tf_op | source)
XLA Modules:
  0.0 92.5 jit_solution(11750846869063157306)
XLA Ops:
  0.0 0.6 pad_add_fusion.where_ref
  0.6 3.4 %shard_map.100 = (bf16[144,128]{1,0:T(8,128)(2,1)}, bf16[512,128]{1,0:T(8,128)(2,1)}, f32[8,128]{1,0:T(8,128)}) custom-call(s32[3]{0:T(128)} %pad_add_fusion.where_ref, bf16[64,8,256]{2,1,0:T(8,128)(2,1)} %feat_hbm.1, bf16[64,256]{1,0:T(8,128)(2,1)} %bitcast.41, bf16[8,64]{1,0:T(8,128)(2,1)} %bitcast.42, s32[1,128]{1,0:T(1,128)} %bitcast.33), custom_call_target="tpu_custom_call" | custom-call | flops 10000000 | bytes 296460 | tf_op jit(solution)/shard_map/pallas_call | solution.py:218
  4.0 0.0 copy-start.9
  4.1 3.1 %collective-permute-start.2 = (bf16[144,128]{1,0:T(8,128)(2,1)}, bf16[144,128]{1,0:T(8,128)(2,1)S(1)}, u32[]{:S(2)}, u32[]{:S(2)}) collective-permute-start(bf16[144,128]{1,0:T(8,128)(2,1)} %get-tuple-element.51), channel_id=1, source_target_pairs={{0,4},{1,5},{2,6},{3,7},{4,0},{5,1},{6,2},{7,3},{8,12},{9,13},{10,... | collective-permute-start | bytes 110600 | tf_op jit(solution)/shard_map/ppermute | solution.py:462
  7.2 2.6 %collective-permute-start.1 = (bf16[144,128]{1,0:T(8,128)(2,1)}, bf16[144,128]{1,0:T(8,128)(2,1)S(1)}, u32[]{:S(2)}, u32[]{:S(2)}) collective-permute-start(bf16[144,128]{1,0:T(8,128)(2,1)} %get-tuple-element.51), channel_id=1, source_target_pairs={{0,8},{1,9},{2,10},{3,11},{4,12},{5,13},{6,14},{7,15},{8,0},{9,1},... | collective-permute-start | bytes 110600 | tf_op jit(solution)/shard_map/ppermute | solution.py:462
  9.7 0.0 collective-permute-start
  9.8 0.0 copy-start.1
  9.8 0.9 %copy-done.1 = bf16[8,128,128]{2,1,0:T(8,128)(2,1)S(1)} copy-done((bf16[8,128,128]{2,1,0:T(8,128)(2,1)S(1)}, bf16[8,128,128]{2,1,0:T(8,128)(2,1)}, u32[]{:S(2)}) %copy-start.1) | copy-done | bytes 262168
  10.7 0.9 %copy-done.2 = bf16[1024,128]{1,0:T(8,128)(2,1)S(1)} copy-done((bf16[1024,128]{1,0:T(8,128)(2,1)S(1)}, bf16[1024,128]{1,0:T(8,128)(2,1)}, u32[]{:S(2)}) %copy-start.2) | copy-done | bytes 262168
  11.7 0.8 copy-done.4
  12.5 2.0 %shard_map.101 = (f32[8,128,128]{2,1,0:T(8,128)S(1)}, bf16[128,1024]{1,0:T(8,128)(2,1)S(1)}, bf16[2,640,128]{2,1,0:T(8,128)(2,1)S(1)}, bf16[2,128,128]{2,1,0:T(8,128)(2,1)S(1)}) custom-call(s32[3]{0:T(128)S(1)} %copy-done.5, s32[128]{0:T(128)S(1)} %copy-done.9, s32[1,128]{1,0:T(1,128)S(1)} %bitcast.36, bf16[8,128,128]{2,1,0:T(8,128)(2,1)S(1)} %copy-done.1, ...), custom_call_target="tpu_custom_call" | custom-call | flops 10000000 | bytes 935436 | tf_op jit(solution)/shard_map/pallas_call | solution.py:218
  14.5 0.0 collective-permute-done.2
  14.6 1.1 %collective-permute-done = bf16[144,128]{1,0:T(8,128)(2,1)S(1)} collective-permute-done((bf16[144,128]{1,0:T(8,128)(2,1)}, bf16[144,128]{1,0:T(8,128)(2,1)S(1)}, u32[]{:S(2)}, u32[]{:S(2)}) %collective-permute-start) | collective-permute-done | bytes 36896 | tf_op jit(solution)/shard_map/ppermute | solution.py:462
  15.7 1.6 %collective-permute-start.3 = (bf16[4,144,128]{2,1,0:T(8,128)(2,1)S(1)}, bf16[4,144,128]{2,1,0:T(8,128)(2,1)S(1)}, u32[]{:S(2)}, u32[]{:S(2)}) collective-permute-start(bf16[4,144,128]{2,1,0:T(8,128)(2,1)S(1)} %pad_maximum_fusion), channel_id=1, source_target_pairs={{0,2},{1,3},{2,0},{3,1},{4,6},{5,7},{6,4},{7,5},{8,10},{9,11},{10,... | collective-permute-start | bytes 442376 | tf_op jit(solution)/shard_map/ppermute | solution.py:462
  17.3 0.0 copy-start.3
  17.3 3.6 %collective-permute-done.3 = bf16[4,144,128]{2,1,0:T(8,128)(2,1)S(1)} collective-permute-done((bf16[4,144,128]{2,1,0:T(8,128)(2,1)S(1)}, bf16[4,144,128]{2,1,0:T(8,128)(2,1)S(1)}, u32[]{:S(2)}, u32[]{:S(2)}) %collective-permute-start.3) | collective-permute-done | bytes 147488 | tf_op jit(solution)/shard_map/ppermute | solution.py:462
  21.0 0.1 collective-permute-start.4
  21.1 1.6 %collective-permute-done.4.other_ref = bf16[8,144,128]{2,1,0:T(8,128)(2,1)S(1)} collective-permute-done((bf16[8,144,128]{2,1,0:T(8,128)(2,1)S(1)}, bf16[8,144,128]{2,1,0:T(8,128)(2,1)S(1)}, u32[]{:S(2)}, u32[]{:S(2)}) %collective-permute-start.4) | collective-permute-done | bytes 294944 | tf_op jit(solution)/shard_map/ppermute | solution.py:467
  22.6 0.6 copy-done.7
  23.3 4.0 %shard_map.102 = (f32[8,128,128]{2,1,0:T(8,128)S(1)}, f32[8,128,128]{2,1,0:T(8,128)S(1)}, bf16[512,128]{1,0:T(8,128)(2,1)S(1)}, bf16[512,128]{1,0:T(8,128)(2,1)S...) custom-call(s32[3]{0:T(128)S(1)} %copy-done.5, ...), custom_call_target="tpu_custom_call" | custom-call | flops 400000000 | bytes 1840140 | tf_op jit(solution)/shard_map/pallas_call | solution.py:218
  27.3 3.7 %collective-permute-start.5 = (bf16[256,128]{1,0:T(8,128)(2,1)S(1)}, bf16[256,128]{1,0:T(8,128)(2,1)S(1)}, u32[]{:S(2)}, u32[]{:S(2)}) collective-permute-start(bf16[256,128]{1,0:T(8,128)(2,1)S(1)} %get-tuple-element.62), channel_id=1, source_target_pairs={{0,14},{1,15},{2,12},{3,13},{4,10},{5,11},{6,8},{7,9},{8,6},{9,7},... | collective-permute-start | bytes 196616 | tf_op jit(solution)/shard_map/ppermute | solution.py:462
  31.0 1.1 %collective-permute-start.6 = (bf16[256,128]{1,0:T(8,128)(2,1)S(1)}, bf16[256,128]{1,0:T(8,128)(2,1)S(1)}, u32[]{:S(2)}, u32[]{:S(2)}) collective-permute-start(bf16[256,128]{1,0:T(8,128)(2,1)S(1)} %get-tuple-element.63), channel_id=1, source_target_pairs={{0,12},{1,13},{2,14},{3,15},{4,8},{5,9},{6,10},{7,11},{8,4},{9,5},... | collective-permute-start | bytes 196616 | tf_op jit(solution)/shard_map/ppermute | solution.py:462
  32.1 2.9 %collective-permute-start.8 = (bf16[256,128]{1,0:T(8,128)(2,1)S(1)}, bf16[256,128]{1,0:T(8,128)(2,1)S(1)}, u32[]{:S(2)}, u32[]{:S(2)}) collective-permute-start(bf16[256,128]{1,0:T(8,128)(2,1)S(1)} %get-tuple-element.65), channel_id=1, source_target_pairs={{0,8},{1,9},{2,10},{3,11},{4,12},{5,13},{6,14},{7,15},{8,0},{9,1},... | collective-permute-start | bytes 196616 | tf_op jit(solution)/shard_map/ppermute | solution.py:462
  35.0 1.3 %collective-permute-start.9 = (bf16[512,128]{1,0:T(8,128)(2,1)S(1)}, bf16[512,128]{1,0:T(8,128)(2,1)S(1)}, u32[]{:S(2)}, u32[]{:S(2)}) collective-permute-start(bf16[512,128]{1,0:T(8,128)(2,1)S(1)} %get-tuple-element.66), channel_id=1, source_target_pairs={{0,6},{1,7},{2,4},{3,5},{4,2},{5,3},{6,0},{7,1},{8,14},{9,15},{10,... | collective-permute-start | bytes 393224 | tf_op jit(solution)/shard_map/ppermute | solution.py:462
  36.3 1.7 %collective-permute-start.10 = (bf16[512,128]{1,0:T(8,128)(2,1)S(1)}, bf16[512,128]{1,0:T(8,128)(2,1)S(1)}, u32[]{:S(2)}, u32[]{:S(2)}) collective-permute-start(bf16[512,128]{1,0:T(8,128)(2,1)S(1)} %get-tuple-element.67), channel_id=1, source_target_pairs={{0,4},{1,5},{2,6},{3,7},{4,0},{5,1},{6,2},{7,3},{8,12},{9,13},{10,... | collective-permute-start | bytes 393224 | tf_op jit(solution)/shard_map/ppermute | solution.py:462
  38.0 0.0 collective-permute-done.6.far6
  38.0 0.6 collective-permute-start.11
  38.6 1.7 %collective-permute-done.7.far5 = bf16[256,128]{1,0:T(8,128)(2,1)S(1)} collective-permute-done((bf16[256,128]{1,0:T(8,128)(2,1)S(1)}, bf16[256,128]{1,0:T(8,128)(2,1)S(1)}, u32[]{:S(2)}, u32[]{:S(2)}) %collective-permute-start.7) | collective-permute-done | bytes 65568 | tf_op jit(solution)/shard_map/ppermute | solution.py:462
  40.3 1.8 %collective-permute-done.8.far4 = bf16[256,128]{1,0:T(8,128)(2,1)S(1)} collective-permute-done((bf16[256,128]{1,0:T(8,128)(2,1)S(1)}, bf16[256,128]{1,0:T(8,128)(2,1)S(1)}, u32[]{:S(2)}, u32[]{:S(2)}) %collective-permute-start.8) | collective-permute-done | bytes 65568 | tf_op jit(solution)/shard_map/ppermute | solution.py:462
  42.2 2.3 %collective-permute-done.9.both3 = bf16[512,128]{1,0:T(8,128)(2,1)S(1)} collective-permute-done((bf16[512,128]{1,0:T(8,128)(2,1)S(1)}, bf16[512,128]{1,0:T(8,128)(2,1)S(1)}, u32[]{:S(2)}, u32[]{:S(2)}) %collective-permute-start.9) | collective-permute-done | bytes 131104 | tf_op jit(solution)/shard_map/ppermute | solution.py:462
  44.5 1.3 %collective-permute-done.10.both2 = bf16[512,128]{1,0:T(8,128)(2,1)S(1)} collective-permute-done((bf16[512,128]{1,0:T(8,128)(2,1)S(1)}, bf16[512,128]{1,0:T(8,128)(2,1)S(1)}, u32[]{:S(2)}, u32[]{:S(2)}) %collective-permute-start.10) | collective-permute-done | bytes 131104 | tf_op jit(solution)/shard_map/ppermute | solution.py:462
  45.9 0.1 collective-permute-start.12
  45.9 1.9 %collective-permute-done.12.other_ref = bf16[8,256,128]{2,1,0:T(8,128)(2,1)S(1)} collective-permute-done((bf16[8,256,128]{2,1,0:T(8,128)(2,1)S(1)}, bf16[8,256,128]{2,1,0:T(8,128)(2,1)S(1)}, u32[]{:S(2)}, u32[]{:S(2)}) %collective-permute-start.12) | collective-permute-done | bytes 524320 | tf_op jit(solution)/shard_map/ppermute | solution.py:467
  47.8 1.4 %shard_map.103 = (bf16[256,128]{1,0:T(8,128)(2,1)S(1)}, bf16[256,128]{1,0:T(8,128)(2,1)S(1)}, bf16[256,128]{1,0:T(8,128)(2,1)S(1)}, bf16[256,128]{1,0:T(8,128)(2,1)S(1)}) custom-call(s32[3]{0:T(128)S(1)} %copy-done.5, bf16[256,128]{1,0:T(8,128)(2,1)S(1)} %collective-permute-done.5.far7, bf16[256,128]{1,0:T(8,128)(2,1)S(1)} %collective-permute-done.6.far6, ...), custom_call_target="tpu_custom_call" | custom-call | flops 10000000 | bytes 1310732 | tf_op jit(solution)/shard_map/pallas_call | solution.py:218
  49.3 0.1 collective-permute-start.13
  49.4 2.1 %collective-permute-start.14 = (bf16[256,128]{1,0:T(8,128)(2,1)S(1)}, bf16[256,128]{1,0:T(8,128)(2,1)S(1)}, u32[]{:S(2)}, u32[]{:S(2)}) collective-permute-start(bf16[256,128]{1,0:T(8,128)(2,1)S(1)} %get-tuple-element.71), channel_id=1, source_target_pairs={{0,4},{1,5},{2,6},{3,7},{4,0},{5,1},{6,2},{7,3},{8,12},{9,13},{10,... | collective-permute-start | bytes 196616 | tf_op jit(solution)/shard_map/ppermute | solution.py:462
  51.4 1.4 %collective-permute-start.15 = (bf16[256,128]{1,0:T(8,128)(2,1)S(1)}, bf16[256,128]{1,0:T(8,128)(2,1)S(1)}, u32[]{:S(2)}, u32[]{:S(2)}) collective-permute-start(bf16[256,128]{1,0:T(8,128)(2,1)S(1)} %get-tuple-element.72), channel_id=1, source_target_pairs={{0,2},{1,3},{2,0},{3,1},{4,6},{5,7},{6,4},{7,5},{8,10},{9,11},{10,... | collective-permute-start | bytes 196616 | tf_op jit(solution)/shard_map/ppermute | solution.py:462
  52.8 2.3 %collective-permute-done.13.in3 = bf16[256,128]{1,0:T(8,128)(2,1)S(1)} collective-permute-done((bf16[256,128]{1,0:T(8,128)(2,1)S(1)}, bf16[256,128]{1,0:T(8,128)(2,1)S(1)}, u32[]{:S(2)}, u32[]{:S(2)}) %collective-permute-start.13) | collective-permute-done | bytes 65568 | tf_op jit(solution)/shard_map/ppermute | solution.py:462
  55.1 0.7 collective-permute-done.15.in1
  55.8 2.5 %shard_map.104 = (f32[8,128,128]{2,1,0:T(8,128)S(1)}, f32[8,128,128]{2,1,0:T(8,128)S(1)}, bf16[256,128]{1,0:T(8,128)(2,1)S(1)}, bf16[256,128]{1,0:T(8,128)(2,1)S...) custom-call(s32[3]{0:T(128)S(1)} %copy-done.5, ...), custom_call_target="tpu_custom_call" | custom-call | flops 10000000 | bytes 1704972 | tf_op jit(solution)/shard_map/pallas_call | solution.py:218
  58.3 3.6 %collective-permute-start.16 = (bf16[256,128]{1,0:T(8,128)(2,1)S(1)}, bf16[256,128]{1,0:T(8,128)(2,1)S(1)}, u32[]{:S(2)}, u32[]{:S(2)}) collective-permute-start(bf16[256,128]{1,0:T(8,128)(2,1)S(1)} %get-tuple-element.77), channel_id=1, source_target_pairs={{0,14},{1,15},{2,12},{3,13},{4,10},{5,11},{6,8},{7,9},{8,6},{9,7},... | collective-permute-start | bytes 196616 | tf_op jit(solution)/shard_map/ppermute | solution.py:462
  61.9 1.0 %collective-permute-start.17 = (bf16[256,128]{1,0:T(8,128)(2,1)S(1)}, bf16[256,128]{1,0:T(8,128)(2,1)S(1)}, u32[]{:S(2)}, u32[]{:S(2)}) collective-permute-start(bf16[256,128]{1,0:T(8,128)(2,1)S(1)} %get-tuple-element.78), channel_id=1, source_target_pairs={{0,12},{1,13},{2,14},{3,15},{4,8},{5,9},{6,10},{7,11},{8,4},{9,5},... | collective-permute-start | bytes 196616 | tf_op jit(solution)/shard_map/ppermute | solution.py:462
  62.9 3.1 %collective-permute-start.19 = (bf16[256,128]{1,0:T(8,128)(2,1)S(1)}, bf16[256,128]{1,0:T(8,128)(2,1)S(1)}, u32[]{:S(2)}, u32[]{:S(2)}) collective-permute-start(bf16[256,128]{1,0:T(8,128)(2,1)S(1)} %get-tuple-element.80), channel_id=1, source_target_pairs={{0,8},{1,9},{2,10},{3,11},{4,12},{5,13},{6,14},{7,15},{8,0},{9,1},... | collective-permute-start | bytes 196616 | tf_op jit(solution)/shard_map/ppermute | solution.py:462
  66.0 1.2 %collective-permute-start.20 = (bf16[256,128]{1,0:T(8,128)(2,1)S(1)}, bf16[256,128]{1,0:T(8,128)(2,1)S(1)}, u32[]{:S(2)}, u32[]{:S(2)}) collective-permute-start(bf16[256,128]{1,0:T(8,128)(2,1)S(1)} %get-tuple-element.81), channel_id=1, source_target_pairs={{0,6},{1,7},{2,4},{3,5},{4,2},{5,3},{6,0},{7,1},{8,14},{9,15},{10,... | collective-permute-start | bytes 196616 | tf_op jit(solution)/shard_map/ppermute | solution.py:462
  67.2 1.6 %collective-permute-start.21 = (bf16[256,128]{1,0:T(8,128)(2,1)S(1)}, bf16[256,128]{1,0:T(8,128)(2,1)S(1)}, u32[]{:S(2)}, u32[]{:S(2)}) collective-permute-start(bf16[256,128]{1,0:T(8,128)(2,1)S(1)} %get-tuple-element.82), channel_id=1, source_target_pairs={{0,4},{1,5},{2,6},{3,7},{4,0},{5,1},{6,2},{7,3},{8,12},{9,13},{10,... | collective-permute-start | bytes 196616 | tf_op jit(solution)/shard_map/ppermute | solution.py:462
  68.7 0.7 collective-permute-start.22
  69.5 1.7 %collective-permute-done.18.b5 = bf16[256,128]{1,0:T(8,128)(2,1)S(1)} collective-permute-done((bf16[256,128]{1,0:T(8,128)(2,1)S(1)}, bf16[256,128]{1,0:T(8,128)(2,1)S(1)}, u32[]{:S(2)}, u32[]{:S(2)}) %collective-permute-start.18) | collective-permute-done | bytes 65568 | tf_op jit(solution)/shard_map/ppermute | solution.py:462
  71.1 1.3 %collective-permute-done.19.b4 = bf16[256,128]{1,0:T(8,128)(2,1)S(1)} collective-permute-done((bf16[256,128]{1,0:T(8,128)(2,1)S(1)}, bf16[256,128]{1,0:T(8,128)(2,1)S(1)}, u32[]{:S(2)}, u32[]{:S(2)}) %collective-permute-start.19) | collective-permute-done | bytes 65568 | tf_op jit(solution)/shard_map/ppermute | solution.py:462
  72.5 0.6 collective-permute-done.21.b2
  73.1 1.4 %shard_map.105 = (f32[8,128,128]{2,1,0:T(8,128)S(1)}, f32[8,128,128]{2,1,0:T(8,128)S(1)}) custom-call(s32[3]{0:T(128)S(1)} %copy-done.5, bf16[256,128]{1,0:T(8,128)(2,1)S(1)} %collective-permute-done.16.b7, bf16[256,128]{1,0:T(8,128)(2,1)S(1)} %collective-permute-done.17.b6, bf16[256,128]{1,0:T(8,128)(2,1)S(1)} %collective-permute-done.18.b5, ...), custom_call_target="tpu_custom_call" | custom-call | flops 10000000 | bytes 524300 | tf_op jit(solution)/shard_map/pallas_call | solution.py:218
  74.5 0.1 collective-permute-start.23
  74.6 1.9 %collective-permute-done.23.got_ref = f32[8,128,128]{2,1,0:T(8,128)S(1)} collective-permute-done((f32[8,128,128]{2,1,0:T(8,128)S(1)}, f32[8,128,128]{2,1,0:T(8,128)S(1)}, u32[]{:S(2)}, u32[]{:S(2)}) %collective-permute-start.23) | collective-permute-done | bytes 524320 | tf_op jit(solution)/shard_map/ppermute | solution.py:467
  76.5 0.1 shard_map.106
  76.6 3.9 %collective-permute-start.24 = (bf16[128,128]{1,0:T(8,128)(2,1)S(1)}, bf16[128,128]{1,0:T(8,128)(2,1)S(1)}, u32[]{:S(2)}, u32[]{:S(2)}) collective-permute-start(bf16[128,128]{1,0:T(8,128)(2,1)S(1)} %get-tuple-element.87), channel_id=1, source_target_pairs={{0,14},{1,15},{2,12},{3,13},{4,10},{5,11},{6,8},{7,9},{8,6},{9,7},... | collective-permute-start | bytes 98312 | tf_op jit(solution)/shard_map/ppermute | solution.py:462
  80.4 0.1 collective-permute-start.25
  80.6 2.0 %collective-permute-start.26 = (bf16[128,128]{1,0:T(8,128)(2,1)S(1)}, bf16[128,128]{1,0:T(8,128)(2,1)S(1)}, u32[]{:S(2)}, u32[]{:S(2)}) collective-permute-start(bf16[128,128]{1,0:T(8,128)(2,1)S(1)} %get-tuple-element.89), channel_id=1, source_target_pairs={{0,10},{1,11},{2,8},{3,9},{4,14},{5,15},{6,12},{7,13},{8,2},{9,3},... | collective-permute-start | bytes 98312 | tf_op jit(solution)/shard_map/ppermute | solution.py:462
  82.5 1.8 %collective-permute-start.27 = (bf16[128,128]{1,0:T(8,128)(2,1)S(1)}, bf16[128,128]{1,0:T(8,128)(2,1)S(1)}, u32[]{:S(2)}, u32[]{:S(2)}) collective-permute-start(bf16[128,128]{1,0:T(8,128)(2,1)S(1)} %get-tuple-element.90), channel_id=1, source_target_pairs={{0,8},{1,9},{2,10},{3,11},{4,12},{5,13},{6,14},{7,15},{8,0},{9,1},... | collective-permute-start | bytes 98312 | tf_op jit(solution)/shard_map/ppermute | solution.py:462
  84.3 1.5 %collective-permute-start.28 = (bf16[128,128]{1,0:T(8,128)(2,1)S(1)}, bf16[128,128]{1,0:T(8,128)(2,1)S(1)}, u32[]{:S(2)}, u32[]{:S(2)}) collective-permute-start(bf16[128,128]{1,0:T(8,128)(2,1)S(1)} %get-tuple-element.91), channel_id=1, source_target_pairs={{0,6},{1,7},{2,4},{3,5},{4,2},{5,3},{6,0},{7,1},{8,14},{9,15},{10,... | collective-permute-start | bytes 98312 | tf_op jit(solution)/shard_map/ppermute | solution.py:462
  85.7 0.7 collective-permute-start.29
  86.4 1.4 %collective-permute-start.30 = (bf16[128,128]{1,0:T(8,128)(2,1)S(1)}, bf16[128,128]{1,0:T(8,128)(2,1)S(1)}, u32[]{:S(2)}, u32[]{:S(2)}) collective-permute-start(bf16[128,128]{1,0:T(8,128)(2,1)S(1)} %get-tuple-element.93), channel_id=1, source_target_pairs={{0,2},{1,3},{2,0},{3,1},{4,6},{5,7},{6,4},{7,5},{8,10},{9,11},{10,... | collective-permute-start | bytes 98312 | tf_op jit(solution)/shard_map/ppermute | solution.py:462
  87.8 1.3 %collective-permute-done.28.b3 = bf16[128,128]{1,0:T(8,128)(2,1)S(1)} collective-permute-done((bf16[128,128]{1,0:T(8,128)(2,1)S(1)}, bf16[128,128]{1,0:T(8,128)(2,1)S(1)}, u32[]{:S(2)}, u32[]{:S(2)}) %collective-permute-start.28) | collective-permute-done | bytes 32800 | tf_op jit(solution)/shard_map/ppermute | solution.py:462
  89.1 0.6 collective-permute-done.29.b2
  89.7 0.7 collective-permute-done.30.b1
  90.3 2.2 %shard_map.107 = bf16[8,128,128]{2,1,0:T(8,128)(2,1)} custom-call(s32[3]{0:T(128)S(1)} %copy-done.5, bf16[128,128]{1,0:T(8,128)(2,1)S(1)} %collective-permute-done.24.b7, bf16[128,128]{1,0:T(8,128)(2,1)S(1)} %collective-permute-done.25.b6, bf16[128,128]{1,0:T(8,128)(2,1)S(1)} %collective-permute-done.26.b5, bf16[128,128]{1,0:T(8,128)(2,1)S(1)} %collective-permute-done.27.b4, ...), custom_call_target="tpu_custom_call" | custom-call | flops 10000000 | bytes 1376268 | tf_op jit(solution)/shard_map/pallas_call | solution.py:218
  (40 shorter events, 0.2 us)
Async XLA Ops:
  0.0 9.7 %copy-start = (bf16[2,128,640]{2,1,0:T(8,128)(2,1)S(1)}, bf16[2,128,640]{2,1,0:T(8,128)(2,1)}, u32[]{:S(2)}) copy-start(bf16[2,128,640]{2,1,0:T(8,128)(2,1)} %proj_ref.1) | copy-start | bytes 983044
  0.6 9.1 %copy-start.6 = (bf16[66,128]{1,0:T(8,128)(2,1)S(1)}, bf16[66,128]{1,0:T(8,128)(2,1)}, u32[]{:S(2)}) copy-start(bf16[66,128]{1,0:T(8,128)(2,1)} %table_ref.1) | copy-start | bytes 50692
  4.0 5.7 %copy-start.5 = (s32[3]{0:T(128)S(1)}, s32[3]{0:T(128)}, u32[]{:S(2)}) copy-start(s32[3]{0:T(128)} %pad_add_fusion.where_ref) | copy-start | bytes 40
  4.0 5.7 %copy-start.9 = (s32[128]{0:T(128)S(1)}, s32[128]{0:T(128)}, u32[]{:S(2)}) copy-start(s32[128]{0:T(128)} %chain_ref.1) | copy-start | bytes 1540
  4.1 10.5 %collective-permute-start.2 = (bf16[144,128]{1,0:T(8,128)(2,1)}, bf16[144,128]{1,0:T(8,128)(2,1)S(1)}, u32[]{:S(2)}, u32[]{:S(2)}) collective-permute-start(bf16[144,128]{1,0:T(8,128)(2,1)} %get-tuple-element.51), channel_id=1, source_target_pairs={{0,4},{1,5},{2,6},{3,7},{4,0},{5,1},{6,2},{7,3},{8,12},{9,13},{10,... | collective-permute-start | bytes 110600 | tf_op jit(solution)/shard_map/ppermute | solution.py:462
  7.2 7.4 %collective-permute-start.1 = (bf16[144,128]{1,0:T(8,128)(2,1)}, bf16[144,128]{1,0:T(8,128)(2,1)S(1)}, u32[]{:S(2)}, u32[]{:S(2)}) collective-permute-start(bf16[144,128]{1,0:T(8,128)(2,1)} %get-tuple-element.51), channel_id=1, source_target_pairs={{0,8},{1,9},{2,10},{3,11},{4,12},{5,13},{6,14},{7,15},{8,0},{9,1},... | collective-permute-start | bytes 110600 | tf_op jit(solution)/shard_map/ppermute | solution.py:462
  9.7 6.0 %collective-permute-start = (bf16[144,128]{1,0:T(8,128)(2,1)}, bf16[144,128]{1,0:T(8,128)(2,1)S(1)}, u32[]{:S(2)}, u32[]{:S(2)}) collective-permute-start(bf16[144,128]{1,0:T(8,128)(2,1)} %get-tuple-element.51), channel_id=1, source_target_pairs={{0,12},{1,13},{2,14},{3,15},{4,8},{5,9},{6,10},{7,11},{8,4},{9,5},... | collective-permute-start | bytes 110600 | tf_op jit(solution)/shard_map/ppermute | solution.py:462
  9.8 1.0 %copy-start.1 = (bf16[8,128,128]{2,1,0:T(8,128)(2,1)S(1)}, bf16[8,128,128]{2,1,0:T(8,128)(2,1)}, u32[]{:S(2)}) copy-start(bf16[8,128,128]{2,1,0:T(8,128)(2,1)} %pair_ref.1) | copy-start | bytes 786436
  10.7 0.9 %copy-start.2 = (bf16[1024,128]{1,0:T(8,128)(2,1)S(1)}, bf16[1024,128]{1,0:T(8,128)(2,1)}, u32[]{:S(2)}) copy-start(bf16[1024,128]{1,0:T(8,128)(2,1)} %outer_ref.1) | copy-start | bytes 786436
  11.7 0.8 copy-start.4
  12.5 3.2 %copy-start.10 = (bf16[144,128]{1,0:T(8,128)(2,1)S(1)}, bf16[144,128]{1,0:T(8,128)(2,1)}, u32[]{:S(2)}) copy-start(bf16[144,128]{1,0:T(8,128)(2,1)} %get-tuple-element.51) | copy-start | bytes 110596
  15.7 5.2 %collective-permute-start.3 = (bf16[4,144,128]{2,1,0:T(8,128)(2,1)S(1)}, bf16[4,144,128]{2,1,0:T(8,128)(2,1)S(1)}, u32[]{:S(2)}, u32[]{:S(2)}) collective-permute-start(bf16[4,144,128]{2,1,0:T(8,128)(2,1)S(1)} %pad_maximum_fusion), channel_id=1, source_target_pairs={{0,2},{1,3},{2,0},{3,1},{4,6},{5,7},{6,4},{7,5},{8,10},{9,11},{10,... | collective-permute-start | bytes 442376 | tf_op jit(solution)/shard_map/ppermute | solution.py:462
  17.3 5.3 %copy-start.3 = (bf16[512,128]{1,0:T(8,128)(2,1)S(1)}, bf16[512,128]{1,0:T(8,128)(2,1)}, u32[]{:S(2)}) copy-start(bf16[512,128]{1,0:T(8,128)(2,1)} %get-tuple-element.57.left_ref) | copy-start | bytes 393220
  20.9 1.7 %copy-start.8 = (f32[8,128]{1,0:T(8,128)S(1)}, f32[8,128]{1,0:T(8,128)}, u32[]{:S(2)}) copy-start(f32[8,128]{1,0:T(8,128)} %get-tuple-element.58.live_ref) | copy-start | bytes 12292
  21.0 1.6 %collective-permute-start.4 = (bf16[8,144,128]{2,1,0:T(8,128)(2,1)S(1)}, bf16[8,144,128]{2,1,0:T(8,128)(2,1)S(1)}, u32[]{:S(2)}, u32[]{:S(2)}) collective-permute-start(bf16[8,144,128]{2,1,0:T(8,128)(2,1)S(1)} %constant_dynamic-update-slice_fusion.own_ref), channel_id=1, source_target_pairs={{0,1},{1,0},{2,3},{3,2},{4,5},{5,4},{6,7},{7,6},{8,9},{9,8},{10,11... | collective-permute-start | bytes 884744 | tf_op jit(solution)/shard_map/ppermute | solution.py:467
  22.6 0.7 copy-start.7
  27.3 9.0 %collective-permute-start.5 = (bf16[256,128]{1,0:T(8,128)(2,1)S(1)}, bf16[256,128]{1,0:T(8,128)(2,1)S(1)}, u32[]{:S(2)}, u32[]{:S(2)}) collective-permute-start(bf16[256,128]{1,0:T(8,128)(2,1)S(1)} %get-tuple-element.62), channel_id=1, source_target_pairs={{0,14},{1,15},{2,12},{3,13},{4,10},{5,11},{6,8},{7,9},{8,6},{9,7},... | collective-permute-start | bytes 196616 | tf_op jit(solution)/shard_map/ppermute | solution.py:462
  31.0 7.0 %collective-permute-start.6 = (bf16[256,128]{1,0:T(8,128)(2,1)S(1)}, bf16[256,128]{1,0:T(8,128)(2,1)S(1)}, u32[]{:S(2)}, u32[]{:S(2)}) collective-permute-start(bf16[256,128]{1,0:T(8,128)(2,1)S(1)} %get-tuple-element.63), channel_id=1, source_target_pairs={{0,12},{1,13},{2,14},{3,15},{4,8},{5,9},{6,10},{7,11},{8,4},{9,5},... | collective-permute-start | bytes 196616 | tf_op jit(solution)/shard_map/ppermute | solution.py:462
  32.1 8.2 %collective-permute-start.7 = (bf16[256,128]{1,0:T(8,128)(2,1)S(1)}, bf16[256,128]{1,0:T(8,128)(2,1)S(1)}, u32[]{:S(2)}, u32[]{:S(2)}) collective-permute-start(bf16[256,128]{1,0:T(8,128)(2,1)S(1)} %get-tuple-element.64), channel_id=1, source_target_pairs={{0,10},{1,11},{2,8},{3,9},{4,14},{5,15},{6,12},{7,13},{8,2},{9,3},... | collective-permute-start | bytes 196616 | tf_op jit(solution)/shard_map/ppermute | solution.py:462
  32.1 10.1 %collective-permute-start.8 = (bf16[256,128]{1,0:T(8,128)(2,1)S(1)}, bf16[256,128]{1,0:T(8,128)(2,1)S(1)}, u32[]{:S(2)}, u32[]{:S(2)}) collective-permute-start(bf16[256,128]{1,0:T(8,128)(2,1)S(1)} %get-tuple-element.65), channel_id=1, source_target_pairs={{0,8},{1,9},{2,10},{3,11},{4,12},{5,13},{6,14},{7,15},{8,0},{9,1},... | collective-permute-start | bytes 196616 | tf_op jit(solution)/shard_map/ppermute | solution.py:462
  35.0 9.4 %collective-permute-start.9 = (bf16[512,128]{1,0:T(8,128)(2,1)S(1)}, bf16[512,128]{1,0:T(8,128)(2,1)S(1)}, u32[]{:S(2)}, u32[]{:S(2)}) collective-permute-start(bf16[512,128]{1,0:T(8,128)(2,1)S(1)} %get-tuple-element.66), channel_id=1, source_target_pairs={{0,6},{1,7},{2,4},{3,5},{4,2},{5,3},{6,0},{7,1},{8,14},{9,15},{10,... | collective-permute-start | bytes 393224 | tf_op jit(solution)/shard_map/ppermute | solution.py:462
  36.3 9.5 %collective-permute-start.10 = (bf16[512,128]{1,0:T(8,128)(2,1)S(1)}, bf16[512,128]{1,0:T(8,128)(2,1)S(1)}, u32[]{:S(2)}, u32[]{:S(2)}) collective-permute-start(bf16[512,128]{1,0:T(8,128)(2,1)S(1)} %get-tuple-element.67), channel_id=1, source_target_pairs={{0,4},{1,5},{2,6},{3,7},{4,0},{5,1},{6,2},{7,3},{8,12},{9,13},{10,... | collective-permute-start | bytes 393224 | tf_op jit(solution)/shard_map/ppermute | solution.py:462
  38.0 7.8 %collective-permute-start.11 = (bf16[512,128]{1,0:T(8,128)(2,1)S(1)}, bf16[512,128]{1,0:T(8,128)(2,1)S(1)}, u32[]{:S(2)}, u32[]{:S(2)}) collective-permute-start(bf16[512,128]{1,0:T(8,128)(2,1)S(1)} %get-tuple-element.68), channel_id=1, source_target_pairs={{0,2},{1,3},{2,0},{3,1},{4,6},{5,7},{6,4},{7,5},{8,10},{9,11},{10,... | collective-permute-start | bytes 393224 | tf_op jit(solution)/shard_map/ppermute | solution.py:462
  45.9 2.0 %collective-permute-start.12 = (bf16[8,256,128]{2,1,0:T(8,128)(2,1)S(1)}, bf16[8,256,128]{2,1,0:T(8,128)(2,1)S(1)}, u32[]{:S(2)}, u32[]{:S(2)}) collective-permute-start(bf16[8,256,128]{2,1,0:T(8,128)(2,1)S(1)} %bitcast_dynamic-update-slice_fusion), channel_id=1, source_target_pairs={{0,1},{1,0},{2,3},{3,2},{4,5},{5,4},{6,7},{7,6},{8,9},{9,8},{10,11... | collective-permute-start | bytes 1572872 | tf_op jit(solution)/shard_map/ppermute | solution.py:467
  49.3 5.8 %collective-permute-start.13 = (bf16[256,128]{1,0:T(8,128)(2,1)S(1)}, bf16[256,128]{1,0:T(8,128)(2,1)S(1)}, u32[]{:S(2)}, u32[]{:S(2)}) collective-permute-start(bf16[256,128]{1,0:T(8,128)(2,1)S(1)} %get-tuple-element.70), channel_id=1, source_target_pairs={{0,6},{1,7},{2,4},{3,5},{4,2},{5,3},{6,0},{7,1},{8,14},{9,15},{10,... | collective-permute-start | bytes 196616 | tf_op jit(solution)/shard_map/ppermute | solution.py:462
  49.4 5.7 %collective-permute-start.14 = (bf16[256,128]{1,0:T(8,128)(2,1)S(1)}, bf16[256,128]{1,0:T(8,128)(2,1)S(1)}, u32[]{:S(2)}, u32[]{:S(2)}) collective-permute-start(bf16[256,128]{1,0:T(8,128)(2,1)S(1)} %get-tuple-element.71), channel_id=1, source_target_pairs={{0,4},{1,5},{2,6},{3,7},{4,0},{5,1},{6,2},{7,3},{8,12},{9,13},{10,... | collective-permute-start | bytes 196616 | tf_op jit(solution)/shard_map/ppermute | solution.py:462
  51.4 4.4 %collective-permute-start.15 = (bf16[256,128]{1,0:T(8,128)(2,1)S(1)}, bf16[256,128]{1,0:T(8,128)(2,1)S(1)}, u32[]{:S(2)}, u32[]{:S(2)}) collective-permute-start(bf16[256,128]{1,0:T(8,128)(2,1)S(1)} %get-tuple-element.72), channel_id=1, source_target_pairs={{0,2},{1,3},{2,0},{3,1},{4,6},{5,7},{6,4},{7,5},{8,10},{9,11},{10,... | collective-permute-start | bytes 196616 | tf_op jit(solution)/shard_map/ppermute | solution.py:462
  58.3 8.9 %collective-permute-start.16 = (bf16[256,128]{1,0:T(8,128)(2,1)S(1)}, bf16[256,128]{1,0:T(8,128)(2,1)S(1)}, u32[]{:S(2)}, u32[]{:S(2)}) collective-permute-start(bf16[256,128]{1,0:T(8,128)(2,1)S(1)} %get-tuple-element.77), channel_id=1, source_target_pairs={{0,14},{1,15},{2,12},{3,13},{4,10},{5,11},{6,8},{7,9},{8,6},{9,7},... | collective-permute-start | bytes 196616 | tf_op jit(solution)/shard_map/ppermute | solution.py:462
  61.9 6.9 %collective-permute-start.17 = (bf16[256,128]{1,0:T(8,128)(2,1)S(1)}, bf16[256,128]{1,0:T(8,128)(2,1)S(1)}, u32[]{:S(2)}, u32[]{:S(2)}) collective-permute-start(bf16[256,128]{1,0:T(8,128)(2,1)S(1)} %get-tuple-element.78), channel_id=1, source_target_pairs={{0,12},{1,13},{2,14},{3,15},{4,8},{5,9},{6,10},{7,11},{8,4},{9,5},... | collective-permute-start | bytes 196616 | tf_op jit(solution)/shard_map/ppermute | solution.py:462
  62.9 8.2 %collective-permute-start.18 = (bf16[256,128]{1,0:T(8,128)(2,1)S(1)}, bf16[256,128]{1,0:T(8,128)(2,1)S(1)}, u32[]{:S(2)}, u32[]{:S(2)}) collective-permute-start(bf16[256,128]{1,0:T(8,128)(2,1)S(1)} %get-tuple-element.79), channel_id=1, source_target_pairs={{0,10},{1,11},{2,8},{3,9},{4,14},{5,15},{6,12},{7,13},{8,2},{9,3},... | collective-permute-start | bytes 196616 | tf_op jit(solution)/shard_map/ppermute | solution.py:462
  62.9 9.6 %collective-permute-start.19 = (bf16[256,128]{1,0:T(8,128)(2,1)S(1)}, bf16[256,128]{1,0:T(8,128)(2,1)S(1)}, u32[]{:S(2)}, u32[]{:S(2)}) collective-permute-start(bf16[256,128]{1,0:T(8,128)(2,1)S(1)} %get-tuple-element.80), channel_id=1, source_target_pairs={{0,8},{1,9},{2,10},{3,11},{4,12},{5,13},{6,14},{7,15},{8,0},{9,1},... | collective-permute-start | bytes 196616 | tf_op jit(solution)/shard_map/ppermute | solution.py:462
  66.0 6.5 %collective-permute-start.20 = (bf16[256,128]{1,0:T(8,128)(2,1)S(1)}, bf16[256,128]{1,0:T(8,128)(2,1)S(1)}, u32[]{:S(2)}, u32[]{:S(2)}) collective-permute-start(bf16[256,128]{1,0:T(8,128)(2,1)S(1)} %get-tuple-element.81), channel_id=1, source_target_pairs={{0,6},{1,7},{2,4},{3,5},{4,2},{5,3},{6,0},{7,1},{8,14},{9,15},{10,... | collective-permute-start | bytes 196616 | tf_op jit(solution)/shard_map/ppermute | solution.py:462
  67.2 5.9 %collective-permute-start.21 = (bf16[256,128]{1,0:T(8,128)(2,1)S(1)}, bf16[256,128]{1,0:T(8,128)(2,1)S(1)}, u32[]{:S(2)}, u32[]{:S(2)}) collective-permute-start(bf16[256,128]{1,0:T(8,128)(2,1)S(1)} %get-tuple-element.82), channel_id=1, source_target_pairs={{0,4},{1,5},{2,6},{3,7},{4,0},{5,1},{6,2},{7,3},{8,12},{9,13},{10,... | collective-permute-start | bytes 196616 | tf_op jit(solution)/shard_map/ppermute | solution.py:462
  68.7 4.4 %collective-permute-start.22 = (bf16[256,128]{1,0:T(8,128)(2,1)S(1)}, bf16[256,128]{1,0:T(8,128)(2,1)S(1)}, u32[]{:S(2)}, u32[]{:S(2)}) collective-permute-start(bf16[256,128]{1,0:T(8,128)(2,1)S(1)} %get-tuple-element.83), channel_id=1, source_target_pairs={{0,2},{1,3},{2,0},{3,1},{4,6},{5,7},{6,4},{7,5},{8,10},{9,11},{10,... | collective-permute-start | bytes 196616 | tf_op jit(solution)/shard_map/ppermute | solution.py:462
  74.5 2.0 %collective-permute-start.23 = (f32[8,128,128]{2,1,0:T(8,128)S(1)}, f32[8,128,128]{2,1,0:T(8,128)S(1)}, u32[]{:S(2)}, u32[]{:S(2)}) collective-permute-start(f32[8,128,128]{2,1,0:T(8,128)S(1)} %get-tuple-element.86), channel_id=1, source_target_pairs={{0,1},{1,0},{2,3},{3,2},{4,5},{5,4},{6,7},{7,6},{8,9},{9,8},{10,11... | collective-permute-start | bytes 1572872 | tf_op jit(solution)/shard_map/ppermute | solution.py:467
  76.6 9.2 %collective-permute-start.24 = (bf16[128,128]{1,0:T(8,128)(2,1)S(1)}, bf16[128,128]{1,0:T(8,128)(2,1)S(1)}, u32[]{:S(2)}, u32[]{:S(2)}) collective-permute-start(bf16[128,128]{1,0:T(8,128)(2,1)S(1)} %get-tuple-element.87), channel_id=1, source_target_pairs={{0,14},{1,15},{2,12},{3,13},{4,10},{5,11},{6,8},{7,9},{8,6},{9,7},... | collective-permute-start | bytes 98312 | tf_op jit(solution)/shard_map/ppermute | solution.py:462
  80.4 6.0 %collective-permute-start.25 = (bf16[128,128]{1,0:T(8,128)(2,1)S(1)}, bf16[128,128]{1,0:T(8,128)(2,1)S(1)}, u32[]{:S(2)}, u32[]{:S(2)}) collective-permute-start(bf16[128,128]{1,0:T(8,128)(2,1)S(1)} %get-tuple-element.88), channel_id=1, source_target_pairs={{0,12},{1,13},{2,14},{3,15},{4,8},{5,9},{6,10},{7,11},{8,4},{9,5},... | collective-permute-start | bytes 98312 | tf_op jit(solution)/shard_map/ppermute | solution.py:462
  80.6 7.2 %collective-permute-start.26 = (bf16[128,128]{1,0:T(8,128)(2,1)S(1)}, bf16[128,128]{1,0:T(8,128)(2,1)S(1)}, u32[]{:S(2)}, u32[]{:S(2)}) collective-permute-start(bf16[128,128]{1,0:T(8,128)(2,1)S(1)} %get-tuple-element.89), channel_id=1, source_target_pairs={{0,10},{1,11},{2,8},{3,9},{4,14},{5,15},{6,12},{7,13},{8,2},{9,3},... | collective-permute-start | bytes 98312 | tf_op jit(solution)/shard_map/ppermute | solution.py:462
  82.5 5.3 %collective-permute-start.27 = (bf16[128,128]{1,0:T(8,128)(2,1)S(1)}, bf16[128,128]{1,0:T(8,128)(2,1)S(1)}, u32[]{:S(2)}, u32[]{:S(2)}) collective-permute-start(bf16[128,128]{1,0:T(8,128)(2,1)S(1)} %get-tuple-element.90), channel_id=1, source_target_pairs={{0,8},{1,9},{2,10},{3,11},{4,12},{5,13},{6,14},{7,15},{8,0},{9,1},... | collective-permute-start | bytes 98312 | tf_op jit(solution)/shard_map/ppermute | solution.py:462
  84.3 4.8 %collective-permute-start.28 = (bf16[128,128]{1,0:T(8,128)(2,1)S(1)}, bf16[128,128]{1,0:T(8,128)(2,1)S(1)}, u32[]{:S(2)}, u32[]{:S(2)}) collective-permute-start(bf16[128,128]{1,0:T(8,128)(2,1)S(1)} %get-tuple-element.91), channel_id=1, source_target_pairs={{0,6},{1,7},{2,4},{3,5},{4,2},{5,3},{6,0},{7,1},{8,14},{9,15},{10,... | collective-permute-start | bytes 98312 | tf_op jit(solution)/shard_map/ppermute | solution.py:462
  85.7 3.9 %collective-permute-start.29 = (bf16[128,128]{1,0:T(8,128)(2,1)S(1)}, bf16[128,128]{1,0:T(8,128)(2,1)S(1)}, u32[]{:S(2)}, u32[]{:S(2)}) collective-permute-start(bf16[128,128]{1,0:T(8,128)(2,1)S(1)} %get-tuple-element.92), channel_id=1, source_target_pairs={{0,4},{1,5},{2,6},{3,7},{4,0},{5,1},{6,2},{7,3},{8,12},{9,13},{10,... | collective-permute-start | bytes 98312 | tf_op jit(solution)/shard_map/ppermute | solution.py:462
  86.4 3.9 %collective-permute-start.30 = (bf16[128,128]{1,0:T(8,128)(2,1)S(1)}, bf16[128,128]{1,0:T(8,128)(2,1)S(1)}, u32[]{:S(2)}, u32[]{:S(2)}) collective-permute-start(bf16[128,128]{1,0:T(8,128)(2,1)S(1)} %get-tuple-element.93), channel_id=1, source_target_pairs={{0,2},{1,3},{2,0},{3,1},{4,6},{5,7},{6,4},{7,5},{8,10},{9,11},{10,... | collective-permute-start | bytes 98312 | tf_op jit(solution)/shard_map/ppermute | solution.py:462

commit v6 on v4

--- a/solution.py
+++ b/solution.py
@@ -207,10 +207,10 @@
     return (center * lax.rsqrt(spread + EPSILON)).astype(BF16)
 
 
-def run(kernel, outs, *args, smem=(), scratch=(), flops=10**7):
+def run(kernel, outs, *args, smem=(), scratch=(), flops=15 * 10**8):
     vmem = pl.BlockSpec(memory_space=pltpu.VMEM)
     in_specs = [
-        pl.BlockSpec(memory_space=pltpu.SMEM) if at in smem else vmem for at in range(len(args))
+        pl.BlockSpec(memory_space=pltpu.SMEM if at in smem else pltpu.VMEM) for at in range(len(args))
     ]
     moved = sum(a.size * a.dtype.itemsize for a in args)
     return pl.pallas_call(
@@ -225,11 +225,13 @@
 
 
 VMEM_LIMIT = 20 * 1024 * 1024
-
-
-def project_kernel(where_ref, feat_ref, weight_ref, mask_ref, present_ref, pay_ref, left_ref, live_ref, turned, packed):
+ALL_STEPS = (7, 3, 1, 6, 2, 5, 4, 0)
+NEAR_STEPS = (3, 1, 2, 0)
+
+
+def project_kernel(feat_ref, weight_ref, live_in_ref, pay_ref, left_ref, live_ref, turned, packed):
     homologs, rows, _ = feat_ref.shape
-    half = weight_ref.shape[1] // 2
+    half = weight_ref.shape[0] // 2
     quarter = half // 2
     values = feat_ref[...].astype(F32).reshape(homologs * rows, feat_ref.shape[2])
     center = values - jnp.mean(values, axis=1, keepdims=True)
@@ -240,17 +242,8 @@
     in_row = lax.broadcasted_iota(jnp.int32, (total, total), 1)
     order = in_row == (out_row & (homologs - 1)) * rows + out_row // homologs
     normed = nn(order.astype(F32).astype(BF16), normed).astype(BF16)
-    seq = lax.broadcasted_iota(jnp.int32, (homologs, 2 * homologs), 0)
-    lane = lax.broadcasted_iota(jnp.int32, (homologs, 2 * homologs), 1)
-    twice = (seq == (lane & (homologs - 1))).astype(F32).astype(BF16)
-    live = tn(mask_ref[...], twice)
-    cols = present_ref.shape[1]
-    here = lax.broadcasted_iota(jnp.int32, (rows, cols), 1) == (
-        lax.broadcasted_iota(jnp.int32, (rows, cols), 0) + where_ref[0]
-    )
-    present = jnp.sum(jnp.where(here, present_ref[...].astype(F32), 0.0), axis=1, keepdims=True)
-    live = live * present
-    weight = flip(weight_ref[...]).astype(BF16)
+    live = live_in_ref[...]
+    weight = weight_ref[...]
     blank = jnp.zeros((homologs, normed.shape[1]), BF16)
     for row in range(rows):
         mine = normed[row * homologs : (row + 1) * homologs]
@@ -312,7 +305,7 @@
     per = own_ref.shape[1]
     chips = own_ref.shape[0]
     for at in range(chips):
-        chip_at = chip ^ ((at % 4) * 2 + at // 4)
+        chip_at = chip ^ ((3 - at % 4) * 2 + at // 4)
         came[chip_at * 2 + core] = own_ref[at].astype(F32)
         came[chip_at * 2 + (1 - core)] = other_ref[at].astype(F32)
     half = left_ref.shape[0] // (2 * rows)
@@ -353,20 +346,18 @@
 
 
 def mix_rows_kernel(
-    where_ref, both0, both1, both2, both3, far4, far5, far6, far7, other_ref,
-    out0, out1, out2, out3, lefts, rights, mixed,
-):
+    where_ref, *refs,
+):
+    came, (other_ref, out0, out1, out2, out3, lefts, rights, mixed) = refs[:8], refs[8:]
     chip, core = where_ref[1], where_ref[2]
     count, rows, cols = lefts.shape[1:]
     block = count * rows
-    nears = (both0, both1, both2, both3)
-    fars = (far4, far5, far6, far7)
-    for step in range(8):
-        mine = (nears[step][block:] if step < 4 else fars[step - 4][...]).astype(F32)
+    for at, step in enumerate(ALL_STEPS):
+        mine = came[at][came[at].shape[0] - block :].astype(F32)
         rights[(chip ^ step) * 2 + core] = mine.reshape(count, rows, cols)
-        rights[(chip ^ step) * 2 + (1 - core)] = other_ref[step].astype(F32).reshape(count, rows, cols)
+        rights[(chip ^ step) * 2 + (1 - core)] = other_ref[at].astype(F32).reshape(count, rows, cols)
         if step < 4:
-            lefts[step] = nears[step][0:block].astype(F32).reshape(count, rows, cols)
+            lefts[step] = came[at][0:block].astype(F32).reshape(count, rows, cols)
     for c in range(count):
         left = lefts[:, c].reshape(4 * rows, cols).astype(BF16)
         right = rights[:, c].reshape(16 * rows, cols).astype(BF16)
@@ -388,7 +379,7 @@
     rows, width, cols = stream_ref.shape
     chip = where_ref[1]
     groups = 4
-    for step, block in enumerate((in0, in1, in2, in3)):
+    for step, block in zip(NEAR_STEPS, (in0, in1, in2, in3)):
         came[:, (chip & (groups - 1)) ^ step] = block[...].astype(F32).reshape(rows, width // groups, cols)
     present = present_ref[...].astype(F32)
     for row in range(rows):
@@ -435,7 +426,7 @@
     rows, width, cols = stream_ref.shape
     chip = where_ref[1]
     blocks = (b0, b1, b2, b3, b4, b5, b6, b7)
-    for step, block in enumerate(blocks):
+    for step, block in zip(ALL_STEPS, blocks):
         came[:, chip ^ step] = block[...].astype(F32).reshape(rows, width // len(blocks), cols)
     for row in range(rows):
         stream = update(came, row, stream_ref[row], gate_ref[row], out_weight_ref[1])
@@ -449,6 +440,10 @@
 def chip_permute(block, step):
     count = lax.axis_size("wide")
     return lax.ppermute(block, "wide", [(w, w ^ (2 * step)) for w in range(count)])
+
+
+def exchange(blocks, steps):
+    return [chip_permute(blocks[step], step) if step else blocks[0] for step in steps]
 
 
 def core_permute(block):
@@ -476,11 +471,13 @@
     where = jnp.stack([device * rows, chip, core]).astype(jnp.int32)
     present = resolved_residue_mask.reshape(1, cols)
     pay_rows = (half // 2 + 2) * rows
+    row_present = lax.dynamic_slice_in_dim(resolved_residue_mask, device * rows, rows).astype(F32)
+    live = alignment_mask.T.astype(F32) * row_present[:, None]
+    live = jnp.concatenate([live, live], axis=1)
     pay, left, live = run(
         project_kernel,
         [((pay_rows, LANES), BF16), ((2 * rows * half, LANES), BF16), ((rows, LANES), F32)],
-        where, homolog_features, homolog_to_sides_matrix, alignment_mask, present,
-        smem=(0,),
+        homolog_features, homolog_to_sides_matrix.T, live,
         scratch=[((rows, half // 2, LANES), F32), ((pay_rows, LANES), F32)],
     )
     along_z = [chip_permute(pay, 2 * z) for z in (2, 3, 1)]
@@ -497,7 +494,8 @@
         smem=(0, 1),
         scratch=[((LANES, width), F32), ((half, half, width), F32)],
     )
-    along_z = jnp.stack([pay, along_z[2], along_z[0], along_z[1]])
+    along_z = jnp.stack([along_z[1], along_z[0], along_z[2], pay])
+    along_z, base, outer_t, proj_t, out_t = lax.optimization_barrier((along_z, base, outer_t, proj_t, out_t))
     own = jnp.concatenate([along_z, chip_permute(along_z, 1)], axis=0)
     other = core_permute(own)
     tall = width * rows
@@ -514,17 +512,15 @@
             ((width, rows, cols), F32),
             ((width, rows, cols), F32),
         ],
-        flops=4 * 10**8,
+        flops=4 * 10**9,
     )
     stream, gate, both, far = made[0], made[1], made[2:6], made[6:10]
-    far = [chip_permute(far[step], step + 4) for step in (3, 2, 1, 0)][::-1]
-    near = [chip_permute(both[step], step) for step in (3, 2, 1)][::-1]
-    rights = jnp.stack([b[tall // 4 :] for b in [both[0]] + near] + far)
-    rights = core_permute(rights)
+    came = exchange(list(both) + list(far), ALL_STEPS)
+    rights = core_permute(jnp.stack([block[block.shape[0] - tall // 4 :] for block in came]))
     mixed = run(
         mix_rows_kernel,
         [((tall // 4, cols), BF16)] * 4,
-        where, both[0], *near, *far, rights,
+        where, *came, rights,
         smem=(0,),
         scratch=[
             ((4, width // 4, rows, cols), F32),
@@ -532,7 +528,7 @@
             ((4 * rows, width // 4, cols), F32),
         ],
     )
-    mixed = [mixed[0]] + [chip_permute(mixed[step], step) for step in (3, 2, 1)][::-1]
+    mixed = exchange(mixed, NEAR_STEPS)
     made = run(
         between_kernel,
         [((rows, width, cols), F32)] * 2 + [((tall // 4, cols), BF16)] * 8,
@@ -545,7 +541,7 @@
         ],
     )
     stream, gate, both = made[0], made[1], made[2:]
-    came = [both[0]] + [chip_permute(both[step], step) for step in range(7, 0, -1)][::-1]
+    came = exchange(both, ALL_STEPS)
     mine, theirs = run(
         mix_cols_kernel,
         [((8, tall // 8, cols), F32)] * 2,
@@ -558,7 +554,7 @@
         ],
     )
     mixed = run(sum_kernel, [((tall // 8, cols), BF16)] * 8, mine, core_permute(theirs))
-    mixed = [mixed[0]] + [chip_permute(mixed[step], step) for step in range(7, 0, -1)][::-1]
+    mixed = exchange(mixed, ALL_STEPS)
     return run(
         final_kernel,
         [((rows, cols, width), BF16)],

time: 101 us -> 94.1 us (0.932)
  waiting for transfers between devices: 39.6 us -> 36 us
  starting transfers between devices: 42.8 us -> 39.6 us
    ppermute x28, waiting for transfers between devices: 35.8 us -> 30.6 us  [chip_permute(): lax.ppermute(block, 'wide', [(w, w ^ 2 * step) for w in range(count)])]
    ppermute x28, starting transfers between devices: 42.6 us -> 39.4 us  [chip_permute(): lax.ppermute(block, 'wide', [(w, w ^ 2 * step) for w in range(count)])]
    ppermute x3, waiting for transfers between devices: 3.8 us -> 5.36 us  [core_permute(): return lax.ppermute(block, 'wide', [(w, w ^ 1) for w in range(count)])]
    unnamed x33 -> x28, local copies, waits for them, and re-layouts: 3.18 us -> 3.1 us
  transfers between devices with their start and end apart: 31 -> 31, of which waited for: 17 -> 18; matrix products, arithmetic and copies ran while one was open for 0% -> 0% of each run, Pallas kernels for 2% -> 2%
where the time goes in v6:
time: 94.1 us; the launch traced here: 93.8 us
  starting transfers between devices  39.6 us (42%)
  waiting for transfers between devices  36 us (38%)
  Pallas kernels  14.6 us (16%)
  local copies, waits for them, and re-layouts  3.14 us (3%)
    ppermute x28, starting transfers between devices, chip_permute(): lax.ppermute(block, 'wide', [(w, w ^ 2 * step) for w in range(count)])  39.4 us
    ppermute x28, waiting for transfers between devices, chip_permute(): lax.ppermute(block, 'wide', [(w, w ^ 2 * step) for w in range(count)])  30.6 us
    pallas_call x8, Pallas kernels, run(): pl.pallas_call(kernel, out_shape=[jax.ShapeDtypeStruct(shape, kind) for s...  14.6 us
    ppermute x3, waiting for transfers between devices, core_permute(): return lax.ppermute(block, 'wide', [(w, w ^ 1) for w in range(count)])  5.36 us
    unnamed x28, local copies, waits for them, and re-layouts  3.1 us
  transfers between devices with their start and end apart: 31, of which 18 were waited for; matrix products, arithmetic and copies ran while one was open for 0% of the time, Pallas kernels for 2%

profile of v6, /device:TPU:0, one launch (start us, length us, event | category | flops | bytes accessed | tf_op | source)
XLA Modules:
  0.0 93.8 jit_solution(12725715120545450921)
XLA Ops:
  0.0 0.7 copy-done.8
  0.7 0.1 dynamic-slice_convert_fusion
  0.7 0.1 multiply_bitcast_fusion
  0.8 0.1 pad_maximum_fusion.1.live_in_ref
  0.9 0.9 %copy-done.1 = bf16[64,8,256]{2,1,0:T(8,128)(2,1)S(1)} copy-done((bf16[64,8,256]{2,1,0:T(8,128)(2,1)S(1)}, bf16[64,8,256]{2,1,0:T(8,128)(2,1)}, u32[]{:S(2)}) %copy-start.1) | copy-done | bytes 262168
  1.8 0.8 copy-done.5
  2.6 1.0 %shard_map.100 = (bf16[144,128]{1,0:T(8,128)(2,1)S(1)}, bf16[512,128]{1,0:T(8,128)(2,1)S(1)}, f32[8,128]{1,0:T(8,128)S(1)}) custom-call(bf16[64,8,256]{2,1,0:T(8,128)(2,1)S(1)} %copy-done.1, bf16[64,256]{1,0:T(8,128)(2,1)S(1)} %bitcast.35, f32[8,128]{1,0:T(8,128)S(1)} %pad_maximum_fusion.1.live_in_ref), custom_call_target="tpu_custom_call" | custom-call | flops 1500000000 | bytes 299008 | tf_op jit(solution)/shard_map/pallas_call | solution.py:216
  3.6 3.1 %collective-permute-start.2 = (bf16[144,128]{1,0:T(8,128)(2,1)S(1)}, bf16[144,128]{1,0:T(8,128)(2,1)S(1)}, u32[]{:S(2)}, u32[]{:S(2)}) collective-permute-start(bf16[144,128]{1,0:T(8,128)(2,1)S(1)} %get-tuple-element.51), channel_id=1, source_target_pairs={{0,4},{1,5},{2,6},{3,7},{4,0},{5,1},{6,2},{7,3},{8,12},{9,13},{10,... | collective-permute-start | bytes 110600 | tf_op jit(solution)/shard_map/ppermute | solution.py:442
  6.7 2.6 %collective-permute-start.1 = (bf16[144,128]{1,0:T(8,128)(2,1)S(1)}, bf16[144,128]{1,0:T(8,128)(2,1)S(1)}, u32[]{:S(2)}, u32[]{:S(2)}) collective-permute-start(bf16[144,128]{1,0:T(8,128)(2,1)S(1)} %get-tuple-element.51), channel_id=1, source_target_pairs={{0,8},{1,9},{2,10},{3,11},{4,12},{5,13},{6,14},{7,15},{8,0},{9,1},... | collective-permute-start | bytes 110600 | tf_op jit(solution)/shard_map/ppermute | solution.py:442
  9.3 0.1 pad_add_fusion.where_ref
  9.4 0.6 copy-done.6
  10.0 0.0 copy-done.7
  10.0 2.0 %shard_map.101 = (f32[8,128,128]{2,1,0:T(8,128)S(1)}, bf16[128,1024]{1,0:T(8,128)(2,1)S(1)}, bf16[2,640,128]{2,1,0:T(8,128)(2,1)S(1)}, bf16[2,128,128]{2,1,0:T(8,128)(2,1)S(1)}) custom-call(s32[3]{0:T(128)S(1)} %pad_add_fusion.where_ref, s32[128]{0:T(128)S(1)} %copy-done.7, s32[1,128]{1,0:T(1,128)S(1)} %bitcast.36, bf16[8,128,128]{2,1,0:T(8,128)(2,1)S(1)} %copy-done.2, ...), custom_call_target="tpu_custom_call" | custom-call | flops 1500000000 | bytes 935436 | tf_op jit(solution)/shard_map/pallas_call | solution.py:216
  12.0 0.0 collective-permute-done.2
  12.0 0.2 collective-permute-done.1
  12.2 2.8 %collective-permute-done = bf16[144,128]{1,0:T(8,128)(2,1)S(1)} collective-permute-done((bf16[144,128]{1,0:T(8,128)(2,1)S(1)}, bf16[144,128]{1,0:T(8,128)(2,1)S(1)}, u32[]{:S(2)}, u32[]{:S(2)}) %collective-permute-start) | collective-permute-done | bytes 36896 | tf_op jit(solution)/shard_map/ppermute | solution.py:442
  15.0 1.6 %collective-permute-start.3 = (bf16[4,144,128]{2,1,0:T(8,128)(2,1)S(1)}, bf16[4,144,128]{2,1,0:T(8,128)(2,1)S(1)}, u32[]{:S(2)}, u32[]{:S(2)}) collective-permute-start(bf16[4,144,128]{2,1,0:T(8,128)(2,1)S(1)} %pad_maximum_fusion), channel_id=1, source_target_pairs={{0,2},{1,3},{2,0},{3,1},{4,6},{5,7},{6,4},{7,5},{8,10},{9,11},{10,... | collective-permute-start | bytes 442376 | tf_op jit(solution)/shard_map/ppermute | solution.py:442
  16.6 3.6 %collective-permute-done.3 = bf16[4,144,128]{2,1,0:T(8,128)(2,1)S(1)} collective-permute-done((bf16[4,144,128]{2,1,0:T(8,128)(2,1)S(1)}, bf16[4,144,128]{2,1,0:T(8,128)(2,1)S(1)}, u32[]{:S(2)}, u32[]{:S(2)}) %collective-permute-start.3) | collective-permute-done | bytes 147488 | tf_op jit(solution)/shard_map/ppermute | solution.py:442
  20.3 0.1 collective-permute-start.4
  20.3 1.6 %collective-permute-done.4.other_ref = bf16[8,144,128]{2,1,0:T(8,128)(2,1)S(1)} collective-permute-done((bf16[8,144,128]{2,1,0:T(8,128)(2,1)S(1)}, bf16[8,144,128]{2,1,0:T(8,128)(2,1)S(1)}, u32[]{:S(2)}, u32[]{:S(2)}) %collective-permute-start.4) | collective-permute-done | bytes 294944 | tf_op jit(solution)/shard_map/ppermute | solution.py:451
  21.9 4.0 %shard_map.102 = (f32[8,128,128]{2,1,0:T(8,128)S(1)}, f32[8,128,128]{2,1,0:T(8,128)S(1)}, bf16[512,128]{1,0:T(8,128)(2,1)S(1)}, bf16[512,128]{1,0:T(8,128)(2,1)S...) custom-call(s32[3]{0:T(128)S(1)} %pad_add_fusion.where_ref, ...), custom_call_target="tpu_custom_call" | custom-call | flops 4000000000 | bytes 1840140 | tf_op jit(solution)/shard_map/pallas_call | solution.py:216
  25.9 1.9 %collective-permute-start.5 = (bf16[256,128]{1,0:T(8,128)(2,1)S(1)}, bf16[256,128]{1,0:T(8,128)(2,1)S(1)}, u32[]{:S(2)}, u32[]{:S(2)}) collective-permute-start(bf16[256,128]{1,0:T(8,128)(2,1)S(1)} %get-tuple-element.62), channel_id=1, source_target_pairs={{0,14},{1,15},{2,12},{3,13},{4,10},{5,11},{6,8},{7,9},{8,6},{9,7},... | collective-permute-start | bytes 196616 | tf_op jit(solution)/shard_map/ppermute | solution.py:442
  27.8 3.0 %collective-permute-start.8 = (bf16[256,128]{1,0:T(8,128)(2,1)S(1)}, bf16[256,128]{1,0:T(8,128)(2,1)S(1)}, u32[]{:S(2)}, u32[]{:S(2)}) collective-permute-start(bf16[256,128]{1,0:T(8,128)(2,1)S(1)} %get-tuple-element.65), channel_id=1, source_target_pairs={{0,12},{1,13},{2,14},{3,15},{4,8},{5,9},{6,10},{7,11},{8,4},{9,5},... | collective-permute-start | bytes 196616 | tf_op jit(solution)/shard_map/ppermute | solution.py:442
  30.8 2.9 %collective-permute-start.11 = (bf16[256,128]{1,0:T(8,128)(2,1)S(1)}, bf16[256,128]{1,0:T(8,128)(2,1)S(1)}, u32[]{:S(2)}, u32[]{:S(2)}) collective-permute-start(bf16[256,128]{1,0:T(8,128)(2,1)S(1)} %get-tuple-element.68), channel_id=1, source_target_pairs={{0,8},{1,9},{2,10},{3,11},{4,12},{5,13},{6,14},{7,15},{8,0},{9,1},... | collective-permute-start | bytes 196616 | tf_op jit(solution)/shard_map/ppermute | solution.py:442
  33.6 0.0 collective-permute-start.6
  33.7 0.0 collective-permute-done.5.refs_0_
  33.7 1.5 %collective-permute-start.7 = (bf16[512,128]{1,0:T(8,128)(2,1)S(1)}, bf16[512,128]{1,0:T(8,128)(2,1)S(1)}, u32[]{:S(2)}, u32[]{:S(2)}) collective-permute-start(bf16[512,128]{1,0:T(8,128)(2,1)S(1)} %get-tuple-element.64), channel_id=1, source_target_pairs={{0,2},{1,3},{2,0},{3,1},{4,6},{5,7},{6,4},{7,5},{8,10},{9,11},{10,... | collective-permute-start | bytes 393224 | tf_op jit(solution)/shard_map/ppermute | solution.py:442
  35.2 6.7 %collective-permute-done.6.refs_1_ = bf16[512,128]{1,0:T(8,128)(2,1)S(1)} collective-permute-done((bf16[512,128]{1,0:T(8,128)(2,1)S(1)}, bf16[512,128]{1,0:T(8,128)(2,1)S(1)}, u32[]{:S(2)}, u32[]{:S(2)}) %collective-permute-start.6) | collective-permute-done | bytes 131104 | tf_op jit(solution)/shard_map/ppermute | solution.py:442
  41.8 0.4 collective-permute-done.7.refs_2_
  42.2 0.0 collective-permute-done.8.refs_3_
  42.3 4.5 %collective-permute-done.9.refs_4_ = bf16[512,128]{1,0:T(8,128)(2,1)S(1)} collective-permute-done((bf16[512,128]{1,0:T(8,128)(2,1)S(1)}, bf16[512,128]{1,0:T(8,128)(2,1)S(1)}, u32[]{:S(2)}, u32[]{:S(2)}) %collective-permute-start.9) | collective-permute-done | bytes 131104 | tf_op jit(solution)/shard_map/ppermute | solution.py:442
  46.9 0.1 collective-permute-start.12
  47.0 1.9 %collective-permute-done.12.refs_8_ = bf16[8,256,128]{2,1,0:T(8,128)(2,1)S(1)} collective-permute-done((bf16[8,256,128]{2,1,0:T(8,128)(2,1)S(1)}, bf16[8,256,128]{2,1,0:T(8,128)(2,1)S(1)}, u32[]{:S(2)}, u32[]{:S(2)}) %collective-permute-start.12) | collective-permute-done | bytes 524320 | tf_op jit(solution)/shard_map/ppermute | solution.py:451
  48.9 1.4 %shard_map.103 = (bf16[256,128]{1,0:T(8,128)(2,1)S(1)}, bf16[256,128]{1,0:T(8,128)(2,1)S(1)}, bf16[256,128]{1,0:T(8,128)(2,1)S(1)}, bf16[256,128]{1,0:T(8,128)(2,1)S(1)}) custom-call(s32[3]{0:T(128)S(1)} %pad_add_fusion.where_ref, bf16[256,128]{1,0:T(8,128)(2,1)S(1)} %collective-permute-done.5.refs_0_, bf16[512,128]{1,0:T(8,128)(2,1)S(1)} %collective-permute-done.6.refs_1_, ...), custom_call_target="tpu_custom_call" | custom-call | flops 1500000000 | bytes 1310732 | tf_op jit(solution)/shard_map/pallas_call | solution.py:216
  50.3 1.0 %collective-permute-start.13 = (bf16[256,128]{1,0:T(8,128)(2,1)S(1)}, bf16[256,128]{1,0:T(8,128)(2,1)S(1)}, u32[]{:S(2)}, u32[]{:S(2)}) collective-permute-start(bf16[256,128]{1,0:T(8,128)(2,1)S(1)} %get-tuple-element.70), channel_id=1, source_target_pairs={{0,6},{1,7},{2,4},{3,5},{4,2},{5,3},{6,0},{7,1},{8,14},{9,15},{10,... | collective-permute-start | bytes 196616 | tf_op jit(solution)/shard_map/ppermute | solution.py:442
  51.3 0.6 collective-permute-start.14
  51.9 1.9 %collective-permute-start.15 = (bf16[256,128]{1,0:T(8,128)(2,1)S(1)}, bf16[256,128]{1,0:T(8,128)(2,1)S(1)}, u32[]{:S(2)}, u32[]{:S(2)}) collective-permute-start(bf16[256,128]{1,0:T(8,128)(2,1)S(1)} %get-tuple-element.72), channel_id=1, source_target_pairs={{0,4},{1,5},{2,6},{3,7},{4,0},{5,1},{6,2},{7,3},{8,12},{9,13},{10,... | collective-permute-start | bytes 196616 | tf_op jit(solution)/shard_map/ppermute | solution.py:442
  53.9 2.1 %collective-permute-done.13.in0 = bf16[256,128]{1,0:T(8,128)(2,1)S(1)} collective-permute-done((bf16[256,128]{1,0:T(8,128)(2,1)S(1)}, bf16[256,128]{1,0:T(8,128)(2,1)S(1)}, u32[]{:S(2)}, u32[]{:S(2)}) %collective-permute-start.13) | collective-permute-done | bytes 65568 | tf_op jit(solution)/shard_map/ppermute | solution.py:442
  55.9 0.6 collective-permute-done.14.in1
  56.6 0.3 collective-permute-done.15.in2
  56.8 2.5 %shard_map.104 = (f32[8,128,128]{2,1,0:T(8,128)S(1)}, f32[8,128,128]{2,1,0:T(8,128)S(1)}, bf16[256,128]{1,0:T(8,128)(2,1)S(1)}, bf16[256,128]{1,0:T(8,128)(2,1)S...) custom-call(s32[3]{0:T(128)S(1)} %pad_add_fusion.where_ref, ...), custom_call_target="tpu_custom_call" | custom-call | flops 1500000000 | bytes 1704972 | tf_op jit(solution)/shard_map/pallas_call | solution.py:216
  59.3 1.5 %collective-permute-start.16 = (bf16[256,128]{1,0:T(8,128)(2,1)S(1)}, bf16[256,128]{1,0:T(8,128)(2,1)S(1)}, u32[]{:S(2)}, u32[]{:S(2)}) collective-permute-start(bf16[256,128]{1,0:T(8,128)(2,1)S(1)} %get-tuple-element.77), channel_id=1, source_target_pairs={{0,14},{1,15},{2,12},{3,13},{4,10},{5,11},{6,8},{7,9},{8,6},{9,7},... | collective-permute-start | bytes 196616 | tf_op jit(solution)/shard_map/ppermute | solution.py:442
  60.9 0.8 collective-permute-start.17
  61.7 1.7 %collective-permute-start.18 = (bf16[256,128]{1,0:T(8,128)(2,1)S(1)}, bf16[256,128]{1,0:T(8,128)(2,1)S(1)}, u32[]{:S(2)}, u32[]{:S(2)}) collective-permute-start(bf16[256,128]{1,0:T(8,128)(2,1)S(1)} %get-tuple-element.79), channel_id=1, source_target_pairs={{0,2},{1,3},{2,0},{3,1},{4,6},{5,7},{6,4},{7,5},{8,10},{9,11},{10,... | collective-permute-start | bytes 196616 | tf_op jit(solution)/shard_map/ppermute | solution.py:442
  63.4 2.6 %collective-permute-start.19 = (bf16[256,128]{1,0:T(8,128)(2,1)S(1)}, bf16[256,128]{1,0:T(8,128)(2,1)S(1)}, u32[]{:S(2)}, u32[]{:S(2)}) collective-permute-start(bf16[256,128]{1,0:T(8,128)(2,1)S(1)} %get-tuple-element.80), channel_id=1, source_target_pairs={{0,12},{1,13},{2,14},{3,15},{4,8},{5,9},{6,10},{7,11},{8,4},{9,5},... | collective-permute-start | bytes 196616 | tf_op jit(solution)/shard_map/ppermute | solution.py:442
  66.0 0.0 collective-permute-start.20
  66.0 1.1 %collective-permute-done.16.b0 = bf16[256,128]{1,0:T(8,128)(2,1)S(1)} collective-permute-done((bf16[256,128]{1,0:T(8,128)(2,1)S(1)}, bf16[256,128]{1,0:T(8,128)(2,1)S(1)}, u32[]{:S(2)}, u32[]{:S(2)}) %collective-permute-start.16) | collective-permute-done | bytes 65568 | tf_op jit(solution)/shard_map/ppermute | solution.py:442
  67.1 0.4 collective-permute-start.21
  67.6 0.2 collective-permute-done.17.b1
  67.7 2.0 %collective-permute-start.22 = (bf16[256,128]{1,0:T(8,128)(2,1)S(1)}, bf16[256,128]{1,0:T(8,128)(2,1)S(1)}, u32[]{:S(2)}, u32[]{:S(2)}) collective-permute-start(bf16[256,128]{1,0:T(8,128)(2,1)S(1)} %get-tuple-element.83), channel_id=1, source_target_pairs={{0,8},{1,9},{2,10},{3,11},{4,12},{5,13},{6,14},{7,15},{8,0},{9,1},... | collective-permute-start | bytes 196616 | tf_op jit(solution)/shard_map/ppermute | solution.py:442
  69.7 1.2 %collective-permute-done.20.b4 = bf16[256,128]{1,0:T(8,128)(2,1)S(1)} collective-permute-done((bf16[256,128]{1,0:T(8,128)(2,1)S(1)}, bf16[256,128]{1,0:T(8,128)(2,1)S(1)}, u32[]{:S(2)}, u32[]{:S(2)}) %collective-permute-start.20) | collective-permute-done | bytes 65568 | tf_op jit(solution)/shard_map/ppermute | solution.py:442
  70.9 3.7 %collective-permute-done.21.b5 = bf16[256,128]{1,0:T(8,128)(2,1)S(1)} collective-permute-done((bf16[256,128]{1,0:T(8,128)(2,1)S(1)}, bf16[256,128]{1,0:T(8,128)(2,1)S(1)}, u32[]{:S(2)}, u32[]{:S(2)}) %collective-permute-start.21) | collective-permute-done | bytes 65568 | tf_op jit(solution)/shard_map/ppermute | solution.py:442
  74.6 1.4 %shard_map.105 = (f32[8,128,128]{2,1,0:T(8,128)S(1)}, f32[8,128,128]{2,1,0:T(8,128)S(1)}) custom-call(s32[3]{0:T(128)S(1)} %pad_add_fusion.where_ref, bf16[256,128]{1,0:T(8,128)(2,1)S(1)} %collective-permute-done.16.b0, bf16[256,128]{1,0:T(8,128)(2,1)S(1)} %collective-permute-done.17.b1, bf16[256,128]{1,0:T(8,128)(2,1)S(1)} %collective-permute-done.18.b2, ...), custom_call_target="tpu_custom_call" | custom-call | flops 1500000000 | bytes 524300 | tf_op jit(solution)/shard_map/pallas_call | solution.py:216
  76.0 0.1 collective-permute-start.23
  76.1 1.9 %collective-permute-done.23.got_ref = f32[8,128,128]{2,1,0:T(8,128)S(1)} collective-permute-done((f32[8,128,128]{2,1,0:T(8,128)S(1)}, f32[8,128,128]{2,1,0:T(8,128)S(1)}, u32[]{:S(2)}, u32[]{:S(2)}) %collective-permute-start.23) | collective-permute-done | bytes 524320 | tf_op jit(solution)/shard_map/ppermute | solution.py:451
  78.0 2.9 %collective-permute-start.24 = (bf16[128,128]{1,0:T(8,128)(2,1)S(1)}, bf16[128,128]{1,0:T(8,128)(2,1)S(1)}, u32[]{:S(2)}, u32[]{:S(2)}) collective-permute-start(bf16[128,128]{1,0:T(8,128)(2,1)S(1)} %get-tuple-element.87), channel_id=1, source_target_pairs={{0,14},{1,15},{2,12},{3,13},{4,10},{5,11},{6,8},{7,9},{8,6},{9,7},... | collective-permute-start | bytes 98312 | tf_op jit(solution)/shard_map/ppermute | solution.py:442
  80.9 0.8 collective-permute-start.26
  81.7 1.6 %collective-permute-start.27 = (bf16[128,128]{1,0:T(8,128)(2,1)S(1)}, bf16[128,128]{1,0:T(8,128)(2,1)S(1)}, u32[]{:S(2)}, u32[]{:S(2)}) collective-permute-start(bf16[128,128]{1,0:T(8,128)(2,1)S(1)} %get-tuple-element.90), channel_id=1, source_target_pairs={{0,12},{1,13},{2,14},{3,15},{4,8},{5,9},{6,10},{7,11},{8,4},{9,5},... | collective-permute-start | bytes 98312 | tf_op jit(solution)/shard_map/ppermute | solution.py:442
  83.4 1.8 %collective-permute-start.28 = (bf16[128,128]{1,0:T(8,128)(2,1)S(1)}, bf16[128,128]{1,0:T(8,128)(2,1)S(1)}, u32[]{:S(2)}, u32[]{:S(2)}) collective-permute-start(bf16[128,128]{1,0:T(8,128)(2,1)S(1)} %get-tuple-element.91), channel_id=1, source_target_pairs={{0,4},{1,5},{2,6},{3,7},{4,0},{5,1},{6,2},{7,3},{8,12},{9,13},{10,... | collective-permute-start | bytes 98312 | tf_op jit(solution)/shard_map/ppermute | solution.py:442
  85.2 1.6 %collective-permute-start.29 = (bf16[128,128]{1,0:T(8,128)(2,1)S(1)}, bf16[128,128]{1,0:T(8,128)(2,1)S(1)}, u32[]{:S(2)}, u32[]{:S(2)}) collective-permute-start(bf16[128,128]{1,0:T(8,128)(2,1)S(1)} %get-tuple-element.92), channel_id=1, source_target_pairs={{0,10},{1,11},{2,8},{3,9},{4,14},{5,15},{6,12},{7,13},{8,2},{9,3},... | collective-permute-start | bytes 98312 | tf_op jit(solution)/shard_map/ppermute | solution.py:442
  86.8 1.6 %collective-permute-start.30 = (bf16[128,128]{1,0:T(8,128)(2,1)S(1)}, bf16[128,128]{1,0:T(8,128)(2,1)S(1)}, u32[]{:S(2)}, u32[]{:S(2)}) collective-permute-start(bf16[128,128]{1,0:T(8,128)(2,1)S(1)} %get-tuple-element.93), channel_id=1, source_target_pairs={{0,8},{1,9},{2,10},{3,11},{4,12},{5,13},{6,14},{7,15},{8,0},{9,1},... | collective-permute-start | bytes 98312 | tf_op jit(solution)/shard_map/ppermute | solution.py:442
  88.4 2.9 %collective-permute-done.29.b5 = bf16[128,128]{1,0:T(8,128)(2,1)S(1)} collective-permute-done((bf16[128,128]{1,0:T(8,128)(2,1)S(1)}, bf16[128,128]{1,0:T(8,128)(2,1)S(1)}, u32[]{:S(2)}, u32[]{:S(2)}) %collective-permute-start.29) | collective-permute-done | bytes 32800 | tf_op jit(solution)/shard_map/ppermute | solution.py:442
  91.2 0.4 collective-permute-done.30.b6
  91.6 2.2 %shard_map.107 = bf16[8,128,128]{2,1,0:T(8,128)(2,1)} custom-call(s32[3]{0:T(128)S(1)} %pad_add_fusion.where_ref, bf16[128,128]{1,0:T(8,128)(2,1)S(1)} %collective-permute-done.24.b0, bf16[128,128]{1,0:T(8,128)(2,1)S(1)} %collective-permute-done.25.b1, bf16[128,128]{1,0:T(8,128)(2,1)S(1)} %collective-permute-done.26.b2, ...), custom_call_target="tpu_custom_call" | custom-call | flops 1500000000 | bytes 1376268 | tf_op jit(solution)/shard_map/pallas_call | solution.py:216
  (41 shorter events, 0.3 us)
Async XLA Ops:
  0.0 0.7 copy-start.8
  0.0 0.7 copy-start.9
  0.9 0.9 %copy-start.1 = (bf16[64,8,256]{2,1,0:T(8,128)(2,1)S(1)}, bf16[64,8,256]{2,1,0:T(8,128)(2,1)}, u32[]{:S(2)}) copy-start(bf16[64,8,256]{2,1,0:T(8,128)(2,1)} %feat_ref.1) | copy-start | bytes 786436
  1.8 0.8 copy-start.5
  2.6 6.7 %copy-start = (bf16[2,128,640]{2,1,0:T(8,128)(2,1)S(1)}, bf16[2,128,640]{2,1,0:T(8,128)(2,1)}, u32[]{:S(2)}) copy-start(bf16[2,128,640]{2,1,0:T(8,128)(2,1)} %proj_ref.1) | copy-start | bytes 983044
  2.6 6.7 %copy-start.2 = (bf16[8,128,128]{2,1,0:T(8,128)(2,1)S(1)}, bf16[8,128,128]{2,1,0:T(8,128)(2,1)}, u32[]{:S(2)}) copy-start(bf16[8,128,128]{2,1,0:T(8,128)(2,1)} %pair_ref.1) | copy-start | bytes 786436
  2.6 6.8 %copy-start.3 = (bf16[1024,128]{1,0:T(8,128)(2,1)S(1)}, bf16[1024,128]{1,0:T(8,128)(2,1)}, u32[]{:S(2)}) copy-start(bf16[1024,128]{1,0:T(8,128)(2,1)} %outer_ref.1) | copy-start | bytes 786436
  2.6 6.8 %copy-start.4 = (bf16[2,128,128]{2,1,0:T(8,128)(2,1)S(1)}, bf16[2,128,128]{2,1,0:T(8,128)(2,1)}, u32[]{:S(2)}) copy-start(bf16[2,128,128]{2,1,0:T(8,128)(2,1)} %out_ref.1) | copy-start | bytes 196612
  3.6 8.5 %collective-permute-start.2 = (bf16[144,128]{1,0:T(8,128)(2,1)S(1)}, bf16[144,128]{1,0:T(8,128)(2,1)S(1)}, u32[]{:S(2)}, u32[]{:S(2)}) collective-permute-start(bf16[144,128]{1,0:T(8,128)(2,1)S(1)} %get-tuple-element.51), channel_id=1, source_target_pairs={{0,4},{1,5},{2,6},{3,7},{4,0},{5,1},{6,2},{7,3},{8,12},{9,13},{10,... | collective-permute-start | bytes 110600 | tf_op jit(solution)/shard_map/ppermute | solution.py:442
  6.7 5.5 %collective-permute-start.1 = (bf16[144,128]{1,0:T(8,128)(2,1)S(1)}, bf16[144,128]{1,0:T(8,128)(2,1)S(1)}, u32[]{:S(2)}, u32[]{:S(2)}) collective-permute-start(bf16[144,128]{1,0:T(8,128)(2,1)S(1)} %get-tuple-element.51), channel_id=1, source_target_pairs={{0,8},{1,9},{2,10},{3,11},{4,12},{5,13},{6,14},{7,15},{8,0},{9,1},... | collective-permute-start | bytes 110600 | tf_op jit(solution)/shard_map/ppermute | solution.py:442
  9.3 5.8 %collective-permute-start = (bf16[144,128]{1,0:T(8,128)(2,1)S(1)}, bf16[144,128]{1,0:T(8,128)(2,1)S(1)}, u32[]{:S(2)}, u32[]{:S(2)}) collective-permute-start(bf16[144,128]{1,0:T(8,128)(2,1)S(1)} %get-tuple-element.51), channel_id=1, source_target_pairs={{0,12},{1,13},{2,14},{3,15},{4,8},{5,9},{6,10},{7,11},{8,4},{9,5},... | collective-permute-start | bytes 110600 | tf_op jit(solution)/shard_map/ppermute | solution.py:442
  9.3 0.7 copy-start.6
  9.3 0.7 copy-start.7
  15.0 5.2 %collective-permute-start.3 = (bf16[4,144,128]{2,1,0:T(8,128)(2,1)S(1)}, bf16[4,144,128]{2,1,0:T(8,128)(2,1)S(1)}, u32[]{:S(2)}, u32[]{:S(2)}) collective-permute-start(bf16[4,144,128]{2,1,0:T(8,128)(2,1)S(1)} %pad_maximum_fusion), channel_id=1, source_target_pairs={{0,2},{1,3},{2,0},{3,1},{4,6},{5,7},{6,4},{7,5},{8,10},{9,11},{10,... | collective-permute-start | bytes 442376 | tf_op jit(solution)/shard_map/ppermute | solution.py:442
  20.3 1.6 %collective-permute-start.4 = (bf16[8,144,128]{2,1,0:T(8,128)(2,1)S(1)}, bf16[8,144,128]{2,1,0:T(8,128)(2,1)S(1)}, u32[]{:S(2)}, u32[]{:S(2)}) collective-permute-start(bf16[8,144,128]{2,1,0:T(8,128)(2,1)S(1)} %constant_dynamic-update-slice_fusion.own_ref), channel_id=1, source_target_pairs={{0,1},{1,0},{2,3},{3,2},{4,5},{5,4},{6,7},{7,6},{8,9},{9,8},{10,11... | collective-permute-start | bytes 884744 | tf_op jit(solution)/shard_map/ppermute | solution.py:451
  25.9 7.7 %collective-permute-start.5 = (bf16[256,128]{1,0:T(8,128)(2,1)S(1)}, bf16[256,128]{1,0:T(8,128)(2,1)S(1)}, u32[]{:S(2)}, u32[]{:S(2)}) collective-permute-start(bf16[256,128]{1,0:T(8,128)(2,1)S(1)} %get-tuple-element.62), channel_id=1, source_target_pairs={{0,14},{1,15},{2,12},{3,13},{4,10},{5,11},{6,8},{7,9},{8,6},{9,7},... | collective-permute-start | bytes 196616 | tf_op jit(solution)/shard_map/ppermute | solution.py:442
  27.8 14.5 %collective-permute-start.8 = (bf16[256,128]{1,0:T(8,128)(2,1)S(1)}, bf16[256,128]{1,0:T(8,128)(2,1)S(1)}, u32[]{:S(2)}, u32[]{:S(2)}) collective-permute-start(bf16[256,128]{1,0:T(8,128)(2,1)S(1)} %get-tuple-element.65), channel_id=1, source_target_pairs={{0,12},{1,13},{2,14},{3,15},{4,8},{5,9},{6,10},{7,11},{8,4},{9,5},... | collective-permute-start | bytes 196616 | tf_op jit(solution)/shard_map/ppermute | solution.py:442
  30.8 16.1 %collective-permute-start.10 = (bf16[256,128]{1,0:T(8,128)(2,1)S(1)}, bf16[256,128]{1,0:T(8,128)(2,1)S(1)}, u32[]{:S(2)}, u32[]{:S(2)}) collective-permute-start(bf16[256,128]{1,0:T(8,128)(2,1)S(1)} %get-tuple-element.67), channel_id=1, source_target_pairs={{0,10},{1,11},{2,8},{3,9},{4,14},{5,15},{6,12},{7,13},{8,2},{9,3},... | collective-permute-start | bytes 196616 | tf_op jit(solution)/shard_map/ppermute | solution.py:442
  30.8 16.1 %collective-permute-start.11 = (bf16[256,128]{1,0:T(8,128)(2,1)S(1)}, bf16[256,128]{1,0:T(8,128)(2,1)S(1)}, u32[]{:S(2)}, u32[]{:S(2)}) collective-permute-start(bf16[256,128]{1,0:T(8,128)(2,1)S(1)} %get-tuple-element.68), channel_id=1, source_target_pairs={{0,8},{1,9},{2,10},{3,11},{4,12},{5,13},{6,14},{7,15},{8,0},{9,1},... | collective-permute-start | bytes 196616 | tf_op jit(solution)/shard_map/ppermute | solution.py:442
  33.6 8.2 %collective-permute-start.6 = (bf16[512,128]{1,0:T(8,128)(2,1)S(1)}, bf16[512,128]{1,0:T(8,128)(2,1)S(1)}, u32[]{:S(2)}, u32[]{:S(2)}) collective-permute-start(bf16[512,128]{1,0:T(8,128)(2,1)S(1)} %get-tuple-element.63), channel_id=1, source_target_pairs={{0,6},{1,7},{2,4},{3,5},{4,2},{5,3},{6,0},{7,1},{8,14},{9,15},{10,... | collective-permute-start | bytes 393224 | tf_op jit(solution)/shard_map/ppermute | solution.py:442
  33.7 8.6 %collective-permute-start.7 = (bf16[512,128]{1,0:T(8,128)(2,1)S(1)}, bf16[512,128]{1,0:T(8,128)(2,1)S(1)}, u32[]{:S(2)}, u32[]{:S(2)}) collective-permute-start(bf16[512,128]{1,0:T(8,128)(2,1)S(1)} %get-tuple-element.64), channel_id=1, source_target_pairs={{0,2},{1,3},{2,0},{3,1},{4,6},{5,7},{6,4},{7,5},{8,10},{9,11},{10,... | collective-permute-start | bytes 393224 | tf_op jit(solution)/shard_map/ppermute | solution.py:442
  41.8 5.0 %collective-permute-start.9 = (bf16[512,128]{1,0:T(8,128)(2,1)S(1)}, bf16[512,128]{1,0:T(8,128)(2,1)S(1)}, u32[]{:S(2)}, u32[]{:S(2)}) collective-permute-start(bf16[512,128]{1,0:T(8,128)(2,1)S(1)} %get-tuple-element.66), channel_id=1, source_target_pairs={{0,4},{1,5},{2,6},{3,7},{4,0},{5,1},{6,2},{7,3},{8,12},{9,13},{10,... | collective-permute-start | bytes 393224 | tf_op jit(solution)/shard_map/ppermute | solution.py:442
  46.9 2.0 %collective-permute-start.12 = (bf16[8,256,128]{2,1,0:T(8,128)(2,1)S(1)}, bf16[8,256,128]{2,1,0:T(8,128)(2,1)S(1)}, u32[]{:S(2)}, u32[]{:S(2)}) collective-permute-start(bf16[8,256,128]{2,1,0:T(8,128)(2,1)S(1)} %bitcast_dynamic-update-slice_fusion), channel_id=1, source_target_pairs={{0,1},{1,0},{2,3},{3,2},{4,5},{5,4},{6,7},{7,6},{8,9},{9,8},{10,11... | collective-permute-start | bytes 1572872 | tf_op jit(solution)/shard_map/ppermute | solution.py:451
  50.3 5.6 %collective-permute-start.13 = (bf16[256,128]{1,0:T(8,128)(2,1)S(1)}, bf16[256,128]{1,0:T(8,128)(2,1)S(1)}, u32[]{:S(2)}, u32[]{:S(2)}) collective-permute-start(bf16[256,128]{1,0:T(8,128)(2,1)S(1)} %get-tuple-element.70), channel_id=1, source_target_pairs={{0,6},{1,7},{2,4},{3,5},{4,2},{5,3},{6,0},{7,1},{8,14},{9,15},{10,... | collective-permute-start | bytes 196616 | tf_op jit(solution)/shard_map/ppermute | solution.py:442
  51.3 5.3 %collective-permute-start.14 = (bf16[256,128]{1,0:T(8,128)(2,1)S(1)}, bf16[256,128]{1,0:T(8,128)(2,1)S(1)}, u32[]{:S(2)}, u32[]{:S(2)}) collective-permute-start(bf16[256,128]{1,0:T(8,128)(2,1)S(1)} %get-tuple-element.71), channel_id=1, source_target_pairs={{0,2},{1,3},{2,0},{3,1},{4,6},{5,7},{6,4},{7,5},{8,10},{9,11},{10,... | collective-permute-start | bytes 196616 | tf_op jit(solution)/shard_map/ppermute | solution.py:442
  51.9 4.9 %collective-permute-start.15 = (bf16[256,128]{1,0:T(8,128)(2,1)S(1)}, bf16[256,128]{1,0:T(8,128)(2,1)S(1)}, u32[]{:S(2)}, u32[]{:S(2)}) collective-permute-start(bf16[256,128]{1,0:T(8,128)(2,1)S(1)} %get-tuple-element.72), channel_id=1, source_target_pairs={{0,4},{1,5},{2,6},{3,7},{4,0},{5,1},{6,2},{7,3},{8,12},{9,13},{10,... | collective-permute-start | bytes 196616 | tf_op jit(solution)/shard_map/ppermute | solution.py:442
  59.3 7.8 %collective-permute-start.16 = (bf16[256,128]{1,0:T(8,128)(2,1)S(1)}, bf16[256,128]{1,0:T(8,128)(2,1)S(1)}, u32[]{:S(2)}, u32[]{:S(2)}) collective-permute-start(bf16[256,128]{1,0:T(8,128)(2,1)S(1)} %get-tuple-element.77), channel_id=1, source_target_pairs={{0,14},{1,15},{2,12},{3,13},{4,10},{5,11},{6,8},{7,9},{8,6},{9,7},... | collective-permute-start | bytes 196616 | tf_op jit(solution)/shard_map/ppermute | solution.py:442
  60.9 6.9 %collective-permute-start.17 = (bf16[256,128]{1,0:T(8,128)(2,1)S(1)}, bf16[256,128]{1,0:T(8,128)(2,1)S(1)}, u32[]{:S(2)}, u32[]{:S(2)}) collective-permute-start(bf16[256,128]{1,0:T(8,128)(2,1)S(1)} %get-tuple-element.78), channel_id=1, source_target_pairs={{0,6},{1,7},{2,4},{3,5},{4,2},{5,3},{6,0},{7,1},{8,14},{9,15},{10,... | collective-permute-start | bytes 196616 | tf_op jit(solution)/shard_map/ppermute | solution.py:442
  61.7 8.0 %collective-permute-start.18 = (bf16[256,128]{1,0:T(8,128)(2,1)S(1)}, bf16[256,128]{1,0:T(8,128)(2,1)S(1)}, u32[]{:S(2)}, u32[]{:S(2)}) collective-permute-start(bf16[256,128]{1,0:T(8,128)(2,1)S(1)} %get-tuple-element.79), channel_id=1, source_target_pairs={{0,2},{1,3},{2,0},{3,1},{4,6},{5,7},{6,4},{7,5},{8,10},{9,11},{10,... | collective-permute-start | bytes 196616 | tf_op jit(solution)/shard_map/ppermute | solution.py:442
  63.4 6.3 %collective-permute-start.19 = (bf16[256,128]{1,0:T(8,128)(2,1)S(1)}, bf16[256,128]{1,0:T(8,128)(2,1)S(1)}, u32[]{:S(2)}, u32[]{:S(2)}) collective-permute-start(bf16[256,128]{1,0:T(8,128)(2,1)S(1)} %get-tuple-element.80), channel_id=1, source_target_pairs={{0,12},{1,13},{2,14},{3,15},{4,8},{5,9},{6,10},{7,11},{8,4},{9,5},... | collective-permute-start | bytes 196616 | tf_op jit(solution)/shard_map/ppermute | solution.py:442
  66.0 4.9 %collective-permute-start.20 = (bf16[256,128]{1,0:T(8,128)(2,1)S(1)}, bf16[256,128]{1,0:T(8,128)(2,1)S(1)}, u32[]{:S(2)}, u32[]{:S(2)}) collective-permute-start(bf16[256,128]{1,0:T(8,128)(2,1)S(1)} %get-tuple-element.81), channel_id=1, source_target_pairs={{0,4},{1,5},{2,6},{3,7},{4,0},{5,1},{6,2},{7,3},{8,12},{9,13},{10,... | collective-permute-start | bytes 196616 | tf_op jit(solution)/shard_map/ppermute | solution.py:442
  67.1 7.5 %collective-permute-start.21 = (bf16[256,128]{1,0:T(8,128)(2,1)S(1)}, bf16[256,128]{1,0:T(8,128)(2,1)S(1)}, u32[]{:S(2)}, u32[]{:S(2)}) collective-permute-start(bf16[256,128]{1,0:T(8,128)(2,1)S(1)} %get-tuple-element.82), channel_id=1, source_target_pairs={{0,10},{1,11},{2,8},{3,9},{4,14},{5,15},{6,12},{7,13},{8,2},{9,3},... | collective-permute-start | bytes 196616 | tf_op jit(solution)/shard_map/ppermute | solution.py:442
  67.7 6.9 %collective-permute-start.22 = (bf16[256,128]{1,0:T(8,128)(2,1)S(1)}, bf16[256,128]{1,0:T(8,128)(2,1)S(1)}, u32[]{:S(2)}, u32[]{:S(2)}) collective-permute-start(bf16[256,128]{1,0:T(8,128)(2,1)S(1)} %get-tuple-element.83), channel_id=1, source_target_pairs={{0,8},{1,9},{2,10},{3,11},{4,12},{5,13},{6,14},{7,15},{8,0},{9,1},... | collective-permute-start | bytes 196616 | tf_op jit(solution)/shard_map/ppermute | solution.py:442
  76.0 2.0 %collective-permute-start.23 = (f32[8,128,128]{2,1,0:T(8,128)S(1)}, f32[8,128,128]{2,1,0:T(8,128)S(1)}, u32[]{:S(2)}, u32[]{:S(2)}) collective-permute-start(f32[8,128,128]{2,1,0:T(8,128)S(1)} %get-tuple-element.86), channel_id=1, source_target_pairs={{0,1},{1,0},{2,3},{3,2},{4,5},{5,4},{6,7},{7,6},{8,9},{9,8},{10,11... | collective-permute-start | bytes 1572872 | tf_op jit(solution)/shard_map/ppermute | solution.py:451
  78.0 7.2 %collective-permute-start.24 = (bf16[128,128]{1,0:T(8,128)(2,1)S(1)}, bf16[128,128]{1,0:T(8,128)(2,1)S(1)}, u32[]{:S(2)}, u32[]{:S(2)}) collective-permute-start(bf16[128,128]{1,0:T(8,128)(2,1)S(1)} %get-tuple-element.87), channel_id=1, source_target_pairs={{0,14},{1,15},{2,12},{3,13},{4,10},{5,11},{6,8},{7,9},{8,6},{9,7},... | collective-permute-start | bytes 98312 | tf_op jit(solution)/shard_map/ppermute | solution.py:442
  80.9 5.9 %collective-permute-start.25 = (bf16[128,128]{1,0:T(8,128)(2,1)S(1)}, bf16[128,128]{1,0:T(8,128)(2,1)S(1)}, u32[]{:S(2)}, u32[]{:S(2)}) collective-permute-start(bf16[128,128]{1,0:T(8,128)(2,1)S(1)} %get-tuple-element.88), channel_id=1, source_target_pairs={{0,6},{1,7},{2,4},{3,5},{4,2},{5,3},{6,0},{7,1},{8,14},{9,15},{10,... | collective-permute-start | bytes 98312 | tf_op jit(solution)/shard_map/ppermute | solution.py:442
  80.9 7.4 %collective-permute-start.26 = (bf16[128,128]{1,0:T(8,128)(2,1)S(1)}, bf16[128,128]{1,0:T(8,128)(2,1)S(1)}, u32[]{:S(2)}, u32[]{:S(2)}) collective-permute-start(bf16[128,128]{1,0:T(8,128)(2,1)S(1)} %get-tuple-element.89), channel_id=1, source_target_pairs={{0,2},{1,3},{2,0},{3,1},{4,6},{5,7},{6,4},{7,5},{8,10},{9,11},{10,... | collective-permute-start | bytes 98312 | tf_op jit(solution)/shard_map/ppermute | solution.py:442
  81.7 6.6 %collective-permute-start.27 = (bf16[128,128]{1,0:T(8,128)(2,1)S(1)}, bf16[128,128]{1,0:T(8,128)(2,1)S(1)}, u32[]{:S(2)}, u32[]{:S(2)}) collective-permute-start(bf16[128,128]{1,0:T(8,128)(2,1)S(1)} %get-tuple-element.90), channel_id=1, source_target_pairs={{0,12},{1,13},{2,14},{3,15},{4,8},{5,9},{6,10},{7,11},{8,4},{9,5},... | collective-permute-start | bytes 98312 | tf_op jit(solution)/shard_map/ppermute | solution.py:442
  83.4 5.0 %collective-permute-start.28 = (bf16[128,128]{1,0:T(8,128)(2,1)S(1)}, bf16[128,128]{1,0:T(8,128)(2,1)S(1)}, u32[]{:S(2)}, u32[]{:S(2)}) collective-permute-start(bf16[128,128]{1,0:T(8,128)(2,1)S(1)} %get-tuple-element.91), channel_id=1, source_target_pairs={{0,4},{1,5},{2,6},{3,7},{4,0},{5,1},{6,2},{7,3},{8,12},{9,13},{10,... | collective-permute-start | bytes 98312 | tf_op jit(solution)/shard_map/ppermute | solution.py:442
  85.2 6.1 %collective-permute-start.29 = (bf16[128,128]{1,0:T(8,128)(2,1)S(1)}, bf16[128,128]{1,0:T(8,128)(2,1)S(1)}, u32[]{:S(2)}, u32[]{:S(2)}) collective-permute-start(bf16[128,128]{1,0:T(8,128)(2,1)S(1)} %get-tuple-element.92), channel_id=1, source_target_pairs={{0,10},{1,11},{2,8},{3,9},{4,14},{5,15},{6,12},{7,13},{8,2},{9,3},... | collective-permute-start | bytes 98312 | tf_op jit(solution)/shard_map/ppermute | solution.py:442
  86.8 4.8 %collective-permute-start.30 = (bf16[128,128]{1,0:T(8,128)(2,1)S(1)}, bf16[128,128]{1,0:T(8,128)(2,1)S(1)}, u32[]{:S(2)}, u32[]{:S(2)}) collective-permute-start(bf16[128,128]{1,0:T(8,128)(2,1)S(1)} %get-tuple-element.93), channel_id=1, source_target_pairs={{0,8},{1,9},{2,10},{3,11},{4,12},{5,13},{6,14},{7,15},{8,0},{9,1},... | collective-permute-start | bytes 98312 | tf_op jit(solution)/shard_map/ppermute | solution.py:442

commit v7 on v6

--- a/solution.py
+++ b/solution.py
@@ -225,8 +225,13 @@
 
 
 VMEM_LIMIT = 20 * 1024 * 1024
-ALL_STEPS = (7, 3, 1, 6, 2, 5, 4, 0)
-NEAR_STEPS = (3, 1, 2, 0)
+SPLIT = ((7, 5), (6, 4), (3, 2), (1, 0))
+OPS = len(SPLIT)
+NEAR = 4
+
+
+def partner_chip(chip, core, op):
+    return chip ^ jnp.where(core == 0, SPLIT[op][0], SPLIT[op][1])
 
 
 def project_kernel(feat_ref, weight_ref, live_in_ref, pay_ref, left_ref, live_ref, turned, packed):
@@ -287,18 +292,29 @@
         out_t_ref[turn] = flip(out_ref[turn]).astype(BF16)
 
 
-def sides(normed, weight, live):
-    width = normed.shape[0]
-    made = nn(weight, normed)
-    part = [made[at * width : (at + 1) * width] for at in range(5)]
-    left = jax.nn.sigmoid(part[0]) * part[1] * live
-    right = jax.nn.sigmoid(part[2]) * part[3] * live
-    return left, right, jax.nn.sigmoid(part[4])
+def sigmoid(values):
+    return 0.5 * jnp.tanh(0.5 * values) + 0.5
+
+
+def sides(streams, weight, lives, gate_ref, lefts, rights, row):
+    width, cols = streams[0].shape
+    made = nn(weight, jnp.concatenate([norm_rows(stream) for stream in streams], axis=1))
+    for at, live in enumerate(lives):
+        part = [
+            made[block * width : (block + 1) * width, at * cols : (at + 1) * cols] for block in range(5)
+        ]
+        lefts[:, row + at, :] = sigmoid(part[0]) * part[1] * live
+        rights[:, row + at, :] = sigmoid(part[2]) * part[3] * live
+        gate_ref[row + at] = sigmoid(part[4])
+
+
+def flat(block):
+    return block.reshape(block.shape[0] * block.shape[1], block.shape[2])
 
 
 def outer_kernel(
     where_ref, flag_ref, own_ref, other_ref, left_ref, live_ref, base_ref, outer_t_ref, proj_ref, present_ref,
-    stream_ref, gate_ref, both0, both1, both2, both3, far0, far1, far2, far3, came, outer, lefts, rights,
+    stream_ref, gate_ref, mine0, mine1, mine2, mine3, theirs_ref, came, outer, lefts, rights,
 ):
     rows, width, cols = base_ref.shape
     chip, core = where_ref[1], where_ref[2]
@@ -321,116 +337,145 @@
             d = part * quarter + pair
             for row in range(rows):
                 first = (part * rows + row) * half
-                outer[row, d * half : (d + 1) * half, :] = made[first : first + half]
+                lane = (row % 2) * cols
+                outer[row // 2, d * half : (d + 1) * half, lane : lane + cols] = made[first : first + half]
     present = present_ref[...].astype(F32)
-    for row in range(rows):
-        stream = base_ref[row] + nn(outer_t_ref[...], outer[row]) * share[row : row + 1]
-        stream_ref[row] = stream
-        live = present * flag_ref[where_ref[0] + row].astype(F32)
-        left, right, gate = sides(norm_rows(stream), proj_ref[0], live)
-        gate_ref[row] = gate
-        lefts[:, row, :] = left
-        rights[:, row, :] = right
-    groups = 4
-    size = width // groups
-    for step, (near, far) in enumerate(((both0, far0), (both1, far1), (both2, far2), (both3, far3))):
-        group = (chip & (groups - 1)) ^ step
-        block = rights[pl.ds(group * size, size)].reshape(size * rows, cols).astype(BF16)
-        far[...] = block
-        near[size * rows :] = block
-        near[0 : size * rows] = lefts[pl.ds(group * size, size)].reshape(size * rows, cols).astype(BF16)
+    for row in range(0, rows, 2):
+        product = nn(outer_t_ref[...], outer[row // 2])
+        streams, lives = [], []
+        for at in range(2):
+            streams.append(
+                base_ref[row + at] + product[:, at * cols : (at + 1) * cols] * share[row + at : row + at + 1]
+            )
+            stream_ref[row + at] = streams[at]
+            lives.append(present * flag_ref[where_ref[0] + row + at].astype(F32))
+        sides(streams, proj_ref[0], lives, gate_ref, lefts, rights, row)
+    size = width // NEAR
+    block = size * rows
+    place = 0
+    for op, mine in enumerate((mine0, mine1, mine2, mine3)):
+        for theirs in range(2):
+            to = partner_chip(chip, core ^ theirs, op)
+            first = pl.multiple_of((to & (NEAR - 1)) * size, size)
+            sent = [rights] if op < OPS // 2 else [lefts, rights]
+            for at, side in enumerate(sent):
+                made = flat(side[pl.ds(first, size)]).astype(BF16)
+                if theirs:
+                    theirs_ref[place : place + block] = made
+                    place += block
+                else:
+                    mine[at * block : (at + 1) * block] = made
 
 
 def per_lane(ref):
     return ref.shape[-1]
 
 
-def mix_rows_kernel(
-    where_ref, *refs,
-):
-    came, (other_ref, out0, out1, out2, out3, lefts, rights, mixed) = refs[:8], refs[8:]
+def mix_rows_kernel(where_ref, came0, came1, came2, came3, other_ref, out0, out1, lefts, rights, mixed):
     chip, core = where_ref[1], where_ref[2]
     count, rows, cols = lefts.shape[1:]
     block = count * rows
-    for at, step in enumerate(ALL_STEPS):
-        mine = came[at][came[at].shape[0] - block :].astype(F32)
-        rights[(chip ^ step) * 2 + core] = mine.reshape(count, rows, cols)
-        rights[(chip ^ step) * 2 + (1 - core)] = other_ref[at].astype(F32).reshape(count, rows, cols)
-        if step < 4:
-            lefts[step] = came[at][0:block].astype(F32).reshape(count, rows, cols)
+    for op, came in enumerate((came0, came1, came2, came3)):
+        sent = came.shape[0] // 2
+        for half in range(2):
+            mine = came[(half + 1) * sent - block : (half + 1) * sent].astype(F32)
+            at = partner_chip(chip, core, op) * 2 + (core ^ half)
+            rights[at] = mine.reshape(count, rows, cols)
+            at = partner_chip(chip, 1 - core, op) * 2 + ((1 - core) ^ half)
+            rights[at] = other_ref[op * 2 + half].astype(F32).reshape(count, rows, cols)
+            if op >= OPS // 2:
+                left = came[half * sent : half * sent + block].astype(F32)
+                lefts[(op - OPS // 2) * 2 + half] = left.reshape(count, rows, cols)
     for c in range(count):
-        left = lefts[:, c].reshape(4 * rows, cols).astype(BF16)
-        right = rights[:, c].reshape(16 * rows, cols).astype(BF16)
+        left = flat(lefts[:, c]).astype(BF16)
+        right = flat(rights[:, c]).astype(BF16)
         mixed[:, c, :] = nt(left, right)
-    for step, out in enumerate((out0, out1, out2, out3)):
-        out[...] = mixed[step * rows : (step + 1) * rows].reshape(block, cols).astype(BF16)
-
-
-def update(came, row, stream, gate, out_weight):
-    mixed = came[row]
-    mixed = mixed.reshape(mixed.shape[0] * mixed.shape[1], mixed.shape[2])
-    return stream + gate * nn(out_weight, norm_rows(mixed))
+    for at, out in enumerate((out0, out1)):
+        out[...] = flat(mixed[at * 2 * rows : (at + 1) * 2 * rows]).astype(BF16)
+
+
+def update(came, row, stream_ref, gate_ref, out_weight):
+    normed = jnp.concatenate([norm_rows(flat(came[row + at])) for at in range(2)], axis=1)
+    made = nn(out_weight, normed)
+    cols = made.shape[1] // 2
+    return [
+        stream_ref[row + at] + gate_ref[row + at] * made[:, at * cols : (at + 1) * cols] for at in range(2)
+    ]
 
 
 def between_kernel(
-    where_ref, flag_ref, in0, in1, in2, in3, stream_ref, gate_ref, out_weight_ref, proj_ref, present_ref,
-    next_ref, next_gate_ref, b0, b1, b2, b3, b4, b5, b6, b7, came, lefts, rights,
+    where_ref, flag_ref, in0, in1, other_ref, stream_ref, gate_ref, out_weight_ref, proj_ref, present_ref,
+    next_ref, next_gate_ref, mine0, mine1, mine2, mine3, theirs_ref, came, lefts, rights,
 ):
     rows, width, cols = stream_ref.shape
-    chip = where_ref[1]
-    groups = 4
-    for step, block in zip(NEAR_STEPS, (in0, in1, in2, in3)):
-        came[:, (chip & (groups - 1)) ^ step] = block[...].astype(F32).reshape(rows, width // groups, cols)
+    chip, core = where_ref[1], where_ref[2]
+    size = width // NEAR
+    for at, block in enumerate((in0, in1)):
+        op = OPS // 2 + at
+        group = partner_chip(chip, core, op) & (NEAR - 1)
+        came[:, group] = block[0 : size * rows].astype(F32).reshape(rows, size, cols)
+        group = partner_chip(chip, 1 - core, op) & (NEAR - 1)
+        block = other_ref[at * size * rows : (at + 1) * size * rows]
+        came[:, group] = block.astype(F32).reshape(rows, size, cols)
     present = present_ref[...].astype(F32)
-    for row in range(rows):
-        stream = update(came, row, stream_ref[row], gate_ref[row], out_weight_ref[0])
-        next_ref[row] = stream
-        live = present * flag_ref[where_ref[0] + row].astype(F32)
-        left, right, gate = sides(norm_rows(stream), proj_ref[1], live)
-        next_gate_ref[row] = gate
-        lefts[:, row, :] = left
-        rights[:, row, :] = right
-    outs = (b0, b1, b2, b3, b4, b5, b6, b7)
-    size = width // len(outs)
-    for step, out in enumerate(outs):
-        first = (chip ^ step) * size
-        out[0 : size * rows] = lefts[pl.ds(first, size)].reshape(size * rows, cols).astype(BF16)
-        out[size * rows :] = rights[pl.ds(first, size)].reshape(size * rows, cols).astype(BF16)
-
-
-def mix_cols_kernel(where_ref, b0, b1, b2, b3, b4, b5, b6, b7, mine_ref, theirs_ref, lefts, rights, partial):
+    for row in range(0, rows, 2):
+        streams = update(came, row, stream_ref, gate_ref, out_weight_ref[0])
+        lives = []
+        for at in range(2):
+            next_ref[row + at] = streams[at]
+            lives.append(present * flag_ref[where_ref[0] + row + at].astype(F32))
+        sides(streams, proj_ref[1], lives, next_gate_ref, lefts, rights, row)
+    size = width // (2 * OPS)
+    block = size * rows
+    for op, mine in enumerate((mine0, mine1, mine2, mine3)):
+        for at, side in enumerate((lefts, rights)):
+            first = pl.multiple_of(partner_chip(chip, core, op) * size, size)
+            mine[at * block : (at + 1) * block] = flat(side[pl.ds(first, size)]).astype(BF16)
+            first = pl.multiple_of(partner_chip(chip, 1 - core, op) * size, size)
+            place = (op * 2 + at) * block
+            theirs_ref[place : place + block] = flat(side[pl.ds(first, size)]).astype(BF16)
+
+
+def mix_cols_kernel(where_ref, came0, came1, came2, came3, mine_ref, theirs_ref, lefts, rights, partial):
     chip, core = where_ref[1], where_ref[2]
-    chips, count, rows, cols = lefts.shape
+    count, rows, cols = lefts.shape[1:]
     block = count * rows
-    for step, came in enumerate((b0, b1, b2, b3, b4, b5, b6, b7)):
-        lefts[step] = came[0:block].astype(F32).reshape(count, rows, cols)
-        rights[step] = came[block:].astype(F32).reshape(count, rows, cols)
+    for op, came in enumerate((came0, came1, came2, came3)):
+        for half in range(2):
+            for at, side in enumerate((lefts, rights)):
+                place = (half * 2 + at) * block
+                side[op * 2 + half] = came[place : place + block].astype(F32).reshape(count, rows, cols)
     for c in range(count):
-        left = lefts[:, c].reshape(chips * rows, cols).astype(BF16)
-        right = rights[:, c].reshape(chips * rows, cols).astype(BF16)
+        left = flat(lefts[:, c]).astype(BF16)
+        right = flat(rights[:, c]).astype(BF16)
         partial[:, c, :] = tn(left, right)
-    for step in range(chips):
-        at = (chip ^ step) * 2
-        mine_ref[step] = partial[pl.ds((at + core) * rows, rows)].reshape(block, cols)
-        theirs_ref[step] = partial[pl.ds((at + 1 - core) * rows, rows)].reshape(block, cols)
+    for op in range(OPS):
+        for half in range(2):
+            to = (partner_chip(chip, core, op) * 2 + (core ^ half)) * rows
+            mine_ref[op, half * block : (half + 1) * block] = flat(partial[pl.ds(to, rows)])
+            to = (partner_chip(chip, 1 - core, op) * 2 + ((1 - core) ^ half)) * rows
+            theirs_ref[op, half * block : (half + 1) * block] = flat(partial[pl.ds(to, rows)])
 
 
 def sum_kernel(mine_ref, got_ref, *outs):
-    for step, out in enumerate(outs):
-        out[...] = (mine_ref[step] + got_ref[step]).astype(BF16)
+    for op, out in enumerate(outs):
+        out[...] = (mine_ref[op] + got_ref[op]).astype(BF16)
 
 
 def final_kernel(
-    where_ref, b0, b1, b2, b3, b4, b5, b6, b7, stream_ref, gate_ref, out_weight_ref, out_ref, came
+    where_ref, came0, came1, came2, came3, other_ref, stream_ref, gate_ref, out_weight_ref, out_ref, came
 ):
     rows, width, cols = stream_ref.shape
-    chip = where_ref[1]
-    blocks = (b0, b1, b2, b3, b4, b5, b6, b7)
-    for step, block in zip(ALL_STEPS, blocks):
-        came[:, chip ^ step] = block[...].astype(F32).reshape(rows, width // len(blocks), cols)
-    for row in range(rows):
-        stream = update(came, row, stream_ref[row], gate_ref[row], out_weight_ref[1])
-        out_ref[row] = flip_out(stream)
+    chip, core = where_ref[1], where_ref[2]
+    size = width // (2 * OPS)
+    block = size * rows
+    for op, mine in enumerate((came0, came1, came2, came3)):
+        came[:, partner_chip(chip, core, op)] = mine[0:block].astype(F32).reshape(rows, size, cols)
+        theirs = other_ref[op * block : (op + 1) * block]
+        came[:, partner_chip(chip, 1 - core, op)] = theirs.astype(F32).reshape(rows, size, cols)
+    for row in range(0, rows, 2):
+        for at, stream in enumerate(update(came, row, stream_ref, gate_ref, out_weight_ref[1])):
+            out_ref[row + at] = flip_out(stream)
 
 
 def flip_out(stream):
@@ -442,8 +487,17 @@
     return lax.ppermute(block, "wide", [(w, w ^ (2 * step)) for w in range(count)])
 
 
-def exchange(blocks, steps):
-    return [chip_permute(blocks[step], step) if step else blocks[0] for step in steps]
+def split_permute(block, op):
+    count = lax.axis_size("wide")
+    return lax.ppermute(block, "wide", [(w, w ^ (2 * SPLIT[op][w % 2])) for w in range(count)])
+
+
+def with_partner(mine, theirs):
+    got, messages, place = core_permute(theirs), [], 0
+    for block in mine:
+        messages.append(jnp.concatenate([block, got[place : place + block.shape[0]]], axis=0))
+        place += block.shape[0]
+    return messages
 
 
 def core_permute(block):
@@ -499,68 +553,76 @@
     own = jnp.concatenate([along_z, chip_permute(along_z, 1)], axis=0)
     other = core_permute(own)
     tall = width * rows
+    near, all_ = tall // NEAR, tall // (2 * OPS)
     made = run(
         outer_kernel,
         [((rows, width, cols), F32)] * 2
-        + [((tall // 2, cols), BF16)] * 4
-        + [((tall // 4, cols), BF16)] * 4,
+        + [((near, cols), BF16)] * 2
+        + [((2 * near, cols), BF16)] * 2
+        + [((6 * near, cols), BF16)],
         where, resolved_residue_mask, own, other, left, live, base, outer_t, proj_t, present,
         smem=(0, 1),
         scratch=[
             ((16, pay_rows, LANES), F32),
-            ((rows, half * half, cols), BF16),
+            ((rows // 2, half * half, 2 * cols), BF16),
             ((width, rows, cols), F32),
             ((width, rows, cols), F32),
         ],
         flops=4 * 10**9,
     )
-    stream, gate, both, far = made[0], made[1], made[2:6], made[6:10]
-    came = exchange(list(both) + list(far), ALL_STEPS)
-    rights = core_permute(jnp.stack([block[block.shape[0] - tall // 4 :] for block in came]))
+    stream, gate, theirs = made[0], made[1], made[6]
+    came = [split_permute(block, op) for op, block in enumerate(with_partner(made[2:6], theirs))]
+    rights = []
+    for block in came:
+        for part in range(2):
+            end = (part + 1) * block.shape[0] // 2
+            rights.append(block[end - near : end])
     mixed = run(
         mix_rows_kernel,
-        [((tall // 4, cols), BF16)] * 4,
-        where, *came, rights,
+        [((2 * near, cols), BF16)] * 2,
+        where, *came, core_permute(jnp.stack(rights)),
         smem=(0,),
         scratch=[
-            ((4, width // 4, rows, cols), F32),
-            ((16, width // 4, rows, cols), F32),
-            ((4 * rows, width // 4, cols), F32),
+            ((4, width // NEAR, rows, cols), F32),
+            ((16, width // NEAR, rows, cols), F32),
+            ((4 * rows, width // NEAR, cols), F32),
         ],
     )
-    mixed = exchange(mixed, NEAR_STEPS)
+    mixed = [split_permute(block, OPS // 2 + at) for at, block in enumerate(mixed)]
+    other = core_permute(jnp.concatenate([block[near:] for block in mixed], axis=0))
     made = run(
         between_kernel,
-        [((rows, width, cols), F32)] * 2 + [((tall // 4, cols), BF16)] * 8,
-        where, resolved_residue_mask, *mixed, stream, gate, out_t, proj_t, present,
+        [((rows, width, cols), F32)] * 2 + [((2 * all_, cols), BF16)] * OPS + [((2 * OPS * all_, cols), BF16)],
+        where, resolved_residue_mask, *mixed, other, stream, gate, out_t, proj_t, present,
         smem=(0, 1),
         scratch=[
-            ((rows, 4, width // 4, cols), F32),
+            ((rows, NEAR, width // NEAR, cols), F32),
             ((width, rows, cols), F32),
             ((width, rows, cols), F32),
         ],
     )
-    stream, gate, both = made[0], made[1], made[2:]
-    came = exchange(both, ALL_STEPS)
+    stream, gate, theirs = made[0], made[1], made[6]
+    came = [split_permute(block, op) for op, block in enumerate(with_partner(made[2:6], theirs))]
     mine, theirs = run(
         mix_cols_kernel,
-        [((8, tall // 8, cols), F32)] * 2,
+        [((OPS, 2 * all_, cols), F32)] * 2,
         where, *came,
         smem=(0,),
         scratch=[
-            ((8, width // 8, rows, cols), F32),
-            ((8, width // 8, rows, cols), F32),
-            ((16 * rows, width // 8, cols), F32),
+            ((2 * OPS, width // (2 * OPS), rows, cols), F32),
+            ((2 * OPS, width // (2 * OPS), rows, cols), F32),
+            ((16 * rows, width // (2 * OPS), cols), F32),
         ],
     )
-    mixed = run(sum_kernel, [((tall // 8, cols), BF16)] * 8, mine, core_permute(theirs))
-    mixed = exchange(mixed, ALL_STEPS)
+    mixed = run(sum_kernel, [((2 * all_, cols), BF16)] * OPS, mine, core_permute(theirs))
+    mixed = [split_permute(block, op) for op, block in enumerate(mixed)]
+    other = core_permute(jnp.concatenate([block[all_:] for block in mixed], axis=0))
     return run(
         final_kernel,
         [((rows, cols, width), BF16)],
-        where, *mixed, stream, gate, out_t,
+        where, *mixed, other, stream, gate, out_t,
         smem=(0,),
-        scratch=[((rows, 8, width // 8, cols), F32)],
+        scratch=[((rows, 2 * OPS, width // (2 * OPS), cols), F32)],
     )[0]
 
 

time: 94.1 us -> 94.5 us (level)
  starting transfers between devices: 39.6 us -> 36.4 us
  local copies, waits for them, and re-layouts: 3.14 us -> 5.96 us
  waiting for transfers between devices: 36 us -> 37.5 us
  Pallas kernels: 14.6 us -> 13.4 us
    ppermute x28 -> x4, starting transfers between devices: 39.4 us -> 7.24 us  [chip_permute(): lax.ppermute(block, 'wide', [(w, w ^ 2 * step) for w in range(count)])]
    ppermute x0 -> x14, starting transfers between devices: none -> 26.9 us  [split_permute(): lax.ppermute(block, 'wide', [(w, w ^ 2 * SPLIT[op][w % 2]) for w in range...]
    ppermute x28 -> x4, waiting for transfers between devices: 30.6 us -> 6.61 us  [chip_permute(): lax.ppermute(block, 'wide', [(w, w ^ 2 * step) for w in range(count)])]
    ppermute x0 -> x14, waiting for transfers between devices: none -> 20.5 us  [split_permute(): lax.ppermute(block, 'wide', [(w, w ^ 2 * SPLIT[op][w % 2]) for w in range...]
    ppermute x3 -> x7, waiting for transfers between devices: 5.36 us -> 10.4 us  [core_permute(): return lax.ppermute(block, 'wide', [(w, w ^ 1) for w in range(count)])]
    ppermute x3 -> x7, starting transfers between devices: 0.21 us -> 2.23 us  [core_permute(): return lax.ppermute(block, 'wide', [(w, w ^ 1) for w in range(count)])]
    unnamed x28 -> x40, local copies, waits for them, and re-layouts: 3.1 us -> 5.03 us
    pallas_call x8, Pallas kernels: 14.6 us -> 13.4 us  [run(): pl.pallas_call(kernel, out_shape=[jax.ShapeDtypeStruct(shape, kind) for s...]
  transfers between devices with their start and end apart: 31 -> 25, of which waited for: 18 -> 22; matrix products, arithmetic and copies ran while one was open for 0% -> 0% of each run, Pallas kernels for 2% -> 2%
where the time goes in v7:
time: 94.5 us; the launch traced here: 94 us
  waiting for transfers between devices  37.5 us (40%)
  starting transfers between devices  36.4 us (39%)
  Pallas kernels  13.4 us (14%)
  local copies, waits for them, and re-layouts  5.96 us (6%)
    ppermute x14, starting transfers between devices, split_permute(): lax.ppermute(block, 'wide', [(w, w ^ 2 * SPLIT[op][w % 2]) for w in range...  26.9 us
    ppermute x14, waiting for transfers between devices, split_permute(): lax.ppermute(block, 'wide', [(w, w ^ 2 * SPLIT[op][w % 2]) for w in range...  20.5 us
    pallas_call x8, Pallas kernels, run(): pl.pallas_call(kernel, out_shape=[jax.ShapeDtypeStruct(shape, kind) for s...  13.4 us
    ppermute x7, waiting for transfers between devices, core_permute(): return lax.ppermute(block, 'wide', [(w, w ^ 1) for w in range(count)])  10.4 us
    ppermute x4, starting transfers between devices, chip_permute(): lax.ppermute(block, 'wide', [(w, w ^ 2 * step) for w in range(count)])  7.24 us
    ppermute x4, waiting for transfers between devices, chip_permute(): lax.ppermute(block, 'wide', [(w, w ^ 2 * step) for w in range(count)])  6.61 us
    unnamed x40, local copies, waits for them, and re-layouts  5.03 us
    ppermute x7, starting transfers between devices, core_permute(): return lax.ppermute(block, 'wide', [(w, w ^ 1) for w in range(count)])  2.23 us
  transfers between devices with their start and end apart: 25, of which 22 were waited for; matrix products, arithmetic and copies ran while one was open for 0% of the time, Pallas kernels for 2%

profile of v7, /device:TPU:0, one launch (start us, length us, event | category | flops | bytes accessed | tf_op | source)
XLA Modules:
  0.0 94.0 jit_solution(11635871661721569969)
XLA Ops:
  0.0 0.7 copy-done.14
  0.7 0.1 dynamic-slice_convert_fusion
  0.7 0.1 multiply_bitcast_fusion
  0.8 0.1 pad_maximum_fusion.11.live_in_ref
  0.9 0.9 %copy-done.7 = bf16[64,8,256]{2,1,0:T(8,128)(2,1)S(1)} copy-done((bf16[64,8,256]{2,1,0:T(8,128)(2,1)S(1)}, bf16[64,8,256]{2,1,0:T(8,128)(2,1)}, u32[]{:S(2)}) %copy-start.7) | copy-done | bytes 262168
  1.8 0.8 copy-done.11
  2.6 1.0 %shard_map.100 = (bf16[144,128]{1,0:T(8,128)(2,1)S(1)}, bf16[512,128]{1,0:T(8,128)(2,1)S(1)}, f32[8,128]{1,0:T(8,128)S(1)}) custom-call(bf16[64,8,256]{2,1,0:T(8,128)(2,1)S(1)} %copy-done.7, bf16[64,256]{1,0:T(8,128)(2,1)S(1)} %bitcast.45, f32[8,128]{1,0:T(8,128)S(1)} %pad_maximum_fusion.11.live_in_ref), custom_call_target="tpu_custom_call" | custom-call | flops 1500000000 | bytes 299008 | tf_op jit(solution)/shard_map/pallas_call | solution.py:216
  3.6 3.1 %collective-permute-start.2 = (bf16[144,128]{1,0:T(8,128)(2,1)S(1)}, bf16[144,128]{1,0:T(8,128)(2,1)S(1)}, u32[]{:S(2)}, u32[]{:S(2)}) collective-permute-start(bf16[144,128]{1,0:T(8,128)(2,1)S(1)} %get-tuple-element.39), channel_id=1, source_target_pairs={{0,4},{1,5},{2,6},{3,7},{4,0},{5,1},{6,2},{7,3},{8,12},{9,13},{10,... | collective-permute-start | bytes 110600 | tf_op jit(solution)/shard_map/ppermute | solution.py:487
  6.7 2.6 %collective-permute-start.1 = (bf16[144,128]{1,0:T(8,128)(2,1)S(1)}, bf16[144,128]{1,0:T(8,128)(2,1)S(1)}, u32[]{:S(2)}, u32[]{:S(2)}) collective-permute-start(bf16[144,128]{1,0:T(8,128)(2,1)S(1)} %get-tuple-element.39), channel_id=1, source_target_pairs={{0,8},{1,9},{2,10},{3,11},{4,12},{5,13},{6,14},{7,15},{8,0},{9,1},... | collective-permute-start | bytes 110600 | tf_op jit(solution)/shard_map/ppermute | solution.py:487
  9.3 0.1 pad_add_fusion.where_ref
  9.4 0.6 copy-done.12
  10.0 2.0 %shard_map.101 = (f32[8,128,128]{2,1,0:T(8,128)S(1)}, bf16[128,1024]{1,0:T(8,128)(2,1)S(1)}, bf16[2,640,128]{2,1,0:T(8,128)(2,1)S(1)}, bf16[2,128,128]{2,1,0:T(8,128)(2,1)S(1)}) custom-call(s32[3]{0:T(128)S(1)} %pad_add_fusion.where_ref, s32[128]{0:T(128)S(1)} %copy-done.13, s32[1,128]{1,0:T(1,128)S(1)} %bitcast.46, bf16[8,128,128]{2,1,0:T(8,128)(2,1)S(1)} %copy-done.8, ...), custom_call_target="tpu_custom_call" | custom-call | flops 1500000000 | bytes 935436 | tf_op jit(solution)/shard_map/pallas_call | solution.py:216
  12.0 0.2 collective-permute-done.1
  12.2 2.8 %collective-permute-done = bf16[144,128]{1,0:T(8,128)(2,1)S(1)} collective-permute-done((bf16[144,128]{1,0:T(8,128)(2,1)S(1)}, bf16[144,128]{1,0:T(8,128)(2,1)S(1)}, u32[]{:S(2)}, u32[]{:S(2)}) %collective-permute-start) | collective-permute-done | bytes 36896 | tf_op jit(solution)/shard_map/ppermute | solution.py:487
  15.0 1.6 %collective-permute-start.3 = (bf16[4,144,128]{2,1,0:T(8,128)(2,1)S(1)}, bf16[4,144,128]{2,1,0:T(8,128)(2,1)S(1)}, u32[]{:S(2)}, u32[]{:S(2)}) collective-permute-start(bf16[4,144,128]{2,1,0:T(8,128)(2,1)S(1)} %pad_maximum_fusion.2), channel_id=1, source_target_pairs={{0,2},{1,3},{2,0},{3,1},{4,6},{5,7},{6,4},{7,5},{8,10},{9,11},{10,... | collective-permute-start | bytes 442376 | tf_op jit(solution)/shard_map/ppermute | solution.py:487
  16.6 3.6 %collective-permute-done.3 = bf16[4,144,128]{2,1,0:T(8,128)(2,1)S(1)} collective-permute-done((bf16[4,144,128]{2,1,0:T(8,128)(2,1)S(1)}, bf16[4,144,128]{2,1,0:T(8,128)(2,1)S(1)}, u32[]{:S(2)}, u32[]{:S(2)}) %collective-permute-start.3) | collective-permute-done | bytes 147488 | tf_op jit(solution)/shard_map/ppermute | solution.py:487
  20.3 0.1 collective-permute-start.4
  20.3 1.6 %collective-permute-done.4.other_ref = bf16[8,144,128]{2,1,0:T(8,128)(2,1)S(1)} collective-permute-done((bf16[8,144,128]{2,1,0:T(8,128)(2,1)S(1)}, bf16[8,144,128]{2,1,0:T(8,128)(2,1)S(1)}, u32[]{:S(2)}, u32[]{:S(2)}) %collective-permute-start.4) | collective-permute-done | bytes 294944 | tf_op jit(solution)/shard_map/ppermute | solution.py:505
  21.9 3.1 %shard_map.102 = (f32[8,128,128]{2,1,0:T(8,128)S(1)}, f32[8,128,128]{2,1,0:T(8,128)S(1)}, bf16[256,128]{1,0:T(8,128)(2,1)S(1)}, bf16[256,128]{1,0:T(8,128)(2,1)S...) custom-call(s32[3]{0:T(128)S(1)} %pad_add_fusion.where_ref, ...), custom_call_target="tpu_custom_call" | custom-call | flops 4000000000 | bytes 1840140 | tf_op jit(solution)/shard_map/pallas_call | solution.py:216
  25.1 0.2 collective-permute-start.5
  25.3 1.6 %collective-permute-done.5 = bf16[1536,128]{1,0:T(8,128)(2,1)S(1)} collective-permute-done((bf16[1536,128]{1,0:T(8,128)(2,1)S(1)}, bf16[1536,128]{1,0:T(8,128)(2,1)S(1)}, u32[]{:S(2)}, u32[]{:S(2)}) %collective-permute-start.5) | collective-permute-done | bytes 393248 | tf_op jit(solution)/shard_map/ppermute | solution.py:505
  26.9 1.9 %collective-permute-start.6 = (bf16[512,128]{1,0:T(8,128)(2,1)S(1)}, bf16[512,128]{1,0:T(8,128)(2,1)S(1)}, u32[]{:S(2)}, u32[]{:S(2)}) collective-permute-start(bf16[512,128]{1,0:T(8,128)(2,1)S(1)} %pad_maximum_fusion.3), channel_id=1, source_target_pairs={{0,14},{1,11},{2,12},{3,9},{4,10},{5,15},{6,8},{7,13},{8,6},{9,3},... | collective-permute-start | bytes 393224 | tf_op jit(solution)/shard_map/ppermute | solution.py:492
  28.8 3.0 %collective-permute-start.7 = (bf16[512,128]{1,0:T(8,128)(2,1)S(1)}, bf16[512,128]{1,0:T(8,128)(2,1)S(1)}, u32[]{:S(2)}, u32[]{:S(2)}) collective-permute-start(bf16[512,128]{1,0:T(8,128)(2,1)S(1)} %pad_maximum_fusion.4), channel_id=1, source_target_pairs={{0,12},{1,9},{2,14},{3,11},{4,8},{5,13},{6,10},{7,15},{8,4},{9,1},... | collective-permute-start | bytes 393224 | tf_op jit(solution)/shard_map/ppermute | solution.py:492
  31.9 2.4 %collective-permute-start.9 = (bf16[1024,128]{1,0:T(8,128)(2,1)S(1)}, bf16[1024,128]{1,0:T(8,128)(2,1)S(1)}, u32[]{:S(2)}, u32[]{:S(2)}) collective-permute-start(bf16[1024,128]{1,0:T(8,128)(2,1)S(1)} %pad_maximum_fusion.1), channel_id=1, source_target_pairs={{0,2},{1,1},{2,0},{3,3},{4,6},{5,5},{6,4},{7,7},{8,10},{9,9},{10,8... | collective-permute-start | bytes 786440 | tf_op jit(solution)/shard_map/ppermute | solution.py:492
  34.4 1.6 %collective-permute-done.6.came0 = bf16[512,128]{1,0:T(8,128)(2,1)S(1)} collective-permute-done((bf16[512,128]{1,0:T(8,128)(2,1)S(1)}, bf16[512,128]{1,0:T(8,128)(2,1)S(1)}, u32[]{:S(2)}, u32[]{:S(2)}) %collective-permute-start.6) | collective-permute-done | bytes 131104 | tf_op jit(solution)/shard_map/ppermute | solution.py:492
  36.1 2.8 %collective-permute-done.7.came1 = bf16[512,128]{1,0:T(8,128)(2,1)S(1)} collective-permute-done((bf16[512,128]{1,0:T(8,128)(2,1)S(1)}, bf16[512,128]{1,0:T(8,128)(2,1)S(1)}, u32[]{:S(2)}, u32[]{:S(2)}) %collective-permute-start.7) | collective-permute-done | bytes 131104 | tf_op jit(solution)/shard_map/ppermute | solution.py:492
  38.9 5.1 %collective-permute-done.8.came2 = bf16[1024,128]{1,0:T(8,128)(2,1)S(1)} collective-permute-done((bf16[1024,128]{1,0:T(8,128)(2,1)S(1)}, bf16[1024,128]{1,0:T(8,128)(2,1)S(1)}, u32[]{:S(2)}, u32[]{:S(2)}) %collective-permute-start.8) | collective-permute-done | bytes 262176 | tf_op jit(solution)/shard_map/ppermute | solution.py:492
  44.1 0.1 collective-permute-start.10
  44.2 1.9 %collective-permute-done.10.other_ref = bf16[8,256,128]{2,1,0:T(8,128)(2,1)S(1)} collective-permute-done((bf16[8,256,128]{2,1,0:T(8,128)(2,1)S(1)}, bf16[8,256,128]{2,1,0:T(8,128)(2,1)S(1)}, u32[]{:S(2)}, u32[]{:S(2)}) %collective-permute-start.10) | collective-permute-done | bytes 524320 | tf_op jit(solution)/shard_map/ppermute | solution.py:505
  46.1 1.4 %shard_map.103 = (bf16[512,128]{1,0:T(8,128)(2,1)S(1)}, bf16[512,128]{1,0:T(8,128)(2,1)S(1)}) custom-call(s32[3]{0:T(128)S(1)} %pad_add_fusion.where_ref, bf16[512,128]{1,0:T(8,128)(2,1)S(1)} %collective-permute-done.6.came0, bf16[512,128]{1,0:T(8,128)(2,1)S(1)} %collective-permute-done.7.came1, bf16[1024,128]{1,0:T(8,128)(2,1)S(1)} %collective-permute-done.8.came2, ...), custom_call_target="tpu_custom_call" | custom-call | flops 1500000000 | bytes 1310732 | tf_op jit(solution)/shard_map/pallas_call | solution.py:216
  47.5 1.4 %collective-permute-start.11 = (bf16[512,128]{1,0:T(8,128)(2,1)S(1)}, bf16[512,128]{1,0:T(8,128)(2,1)S(1)}, u32[]{:S(2)}, u32[]{:S(2)}) collective-permute-start(bf16[512,128]{1,0:T(8,128)(2,1)S(1)} %get-tuple-element.55), channel_id=1, source_target_pairs={{0,6},{1,5},{2,4},{3,7},{4,2},{5,1},{6,0},{7,3},{8,14},{9,13},{10,... | collective-permute-start | bytes 393224 | tf_op jit(solution)/shard_map/ppermute | solution.py:492
  48.9 2.4 %collective-permute-start.12 = (bf16[512,128]{1,0:T(8,128)(2,1)S(1)}, bf16[512,128]{1,0:T(8,128)(2,1)S(1)}, u32[]{:S(2)}, u32[]{:S(2)}) collective-permute-start(bf16[512,128]{1,0:T(8,128)(2,1)S(1)} %get-tuple-element.56), channel_id=1, source_target_pairs={{0,2},{1,1},{2,0},{3,3},{4,6},{5,5},{6,4},{7,7},{8,10},{9,9},{10,8... | collective-permute-start | bytes 393224 | tf_op jit(solution)/shard_map/ppermute | solution.py:492
  51.3 2.7 %collective-permute-done.11.in0 = bf16[512,128]{1,0:T(8,128)(2,1)S(1)} collective-permute-done((bf16[512,128]{1,0:T(8,128)(2,1)S(1)}, bf16[512,128]{1,0:T(8,128)(2,1)S(1)}, u32[]{:S(2)}, u32[]{:S(2)}) %collective-permute-start.11) | collective-permute-done | bytes 131104 | tf_op jit(solution)/shard_map/ppermute | solution.py:492
  54.0 0.7 copy-done
  54.7 1.0 %collective-permute-done.12.in1 = bf16[512,128]{1,0:T(8,128)(2,1)S(1)} collective-permute-done((bf16[512,128]{1,0:T(8,128)(2,1)S(1)}, bf16[512,128]{1,0:T(8,128)(2,1)S(1)}, u32[]{:S(2)}, u32[]{:S(2)}) %collective-permute-start.12) | collective-permute-done | bytes 131104 | tf_op jit(solution)/shard_map/ppermute | solution.py:492
  55.7 0.8 slice-done
  56.6 0.1 collective-permute-start.13
  56.6 1.3 %collective-permute-done.13.other_ref = bf16[512,128]{1,0:T(8,128)(2,1)S(1)} collective-permute-done((bf16[512,128]{1,0:T(8,128)(2,1)S(1)}, bf16[512,128]{1,0:T(8,128)(2,1)S(1)}, u32[]{:S(2)}, u32[]{:S(2)}) %collective-permute-start.13) | collective-permute-done | bytes 131104 | tf_op jit(solution)/shard_map/ppermute | solution.py:505
  58.0 2.2 %shard_map.104 = (f32[8,128,128]{2,1,0:T(8,128)S(1)}, f32[8,128,128]{2,1,0:T(8,128)S(1)}, bf16[256,128]{1,0:T(8,128)(2,1)S(1)}, bf16[256,128]{1,0:T(8,128)(2,1)S...) custom-call(s32[3]{0:T(128)S(1)} %pad_add_fusion.where_ref, ...), custom_call_target="tpu_custom_call" | custom-call | flops 1500000000 | bytes 1836044 | tf_op jit(solution)/shard_map/pallas_call | solution.py:216
  60.2 0.2 collective-permute-start.14
  60.4 1.4 %collective-permute-done.14 = bf16[1024,128]{1,0:T(8,128)(2,1)S(1)} collective-permute-done((bf16[1024,128]{1,0:T(8,128)(2,1)S(1)}, bf16[1024,128]{1,0:T(8,128)(2,1)S(1)}, u32[]{:S(2)}, u32[]{:S(2)}) %collective-permute-start.14) | collective-permute-done | bytes 262176 | tf_op jit(solution)/shard_map/ppermute | solution.py:505
  61.9 1.6 %collective-permute-start.15 = (bf16[512,128]{1,0:T(8,128)(2,1)S(1)}, bf16[512,128]{1,0:T(8,128)(2,1)S(1)}, u32[]{:S(2)}, u32[]{:S(2)}) collective-permute-start(bf16[512,128]{1,0:T(8,128)(2,1)S(1)} %pad_maximum_fusion.6), channel_id=1, source_target_pairs={{0,14},{1,11},{2,12},{3,9},{4,10},{5,15},{6,8},{7,13},{8,6},{9,3},... | collective-permute-start | bytes 393224 | tf_op jit(solution)/shard_map/ppermute | solution.py:492
  63.5 2.4 %collective-permute-start.16 = (bf16[512,128]{1,0:T(8,128)(2,1)S(1)}, bf16[512,128]{1,0:T(8,128)(2,1)S(1)}, u32[]{:S(2)}, u32[]{:S(2)}) collective-permute-start(bf16[512,128]{1,0:T(8,128)(2,1)S(1)} %pad_maximum_fusion.7), channel_id=1, source_target_pairs={{0,12},{1,9},{2,14},{3,11},{4,8},{5,13},{6,10},{7,15},{8,4},{9,1},... | collective-permute-start | bytes 393224 | tf_op jit(solution)/shard_map/ppermute | solution.py:492
  65.9 0.8 collective-permute-start.17
  66.7 2.6 %collective-permute-start.18 = (bf16[512,128]{1,0:T(8,128)(2,1)S(1)}, bf16[512,128]{1,0:T(8,128)(2,1)S(1)}, u32[]{:S(2)}, u32[]{:S(2)}) collective-permute-start(bf16[512,128]{1,0:T(8,128)(2,1)S(1)} %pad_maximum_fusion.9), channel_id=1, source_target_pairs={{0,2},{1,1},{2,0},{3,3},{4,6},{5,5},{6,4},{7,7},{8,10},{9,9},{10,8... | collective-permute-start | bytes 393224 | tf_op jit(solution)/shard_map/ppermute | solution.py:492
  69.3 1.7 %collective-permute-done.15.came0 = bf16[512,128]{1,0:T(8,128)(2,1)S(1)} collective-permute-done((bf16[512,128]{1,0:T(8,128)(2,1)S(1)}, bf16[512,128]{1,0:T(8,128)(2,1)S(1)}, u32[]{:S(2)}, u32[]{:S(2)}) %collective-permute-start.15) | collective-permute-done | bytes 131104 | tf_op jit(solution)/shard_map/ppermute | solution.py:492
  71.0 1.9 %collective-permute-done.16.came1 = bf16[512,128]{1,0:T(8,128)(2,1)S(1)} collective-permute-done((bf16[512,128]{1,0:T(8,128)(2,1)S(1)}, bf16[512,128]{1,0:T(8,128)(2,1)S(1)}, u32[]{:S(2)}, u32[]{:S(2)}) %collective-permute-start.16) | collective-permute-done | bytes 131104 | tf_op jit(solution)/shard_map/ppermute | solution.py:492
  73.0 1.1 %collective-permute-done.17.came2 = bf16[512,128]{1,0:T(8,128)(2,1)S(1)} collective-permute-done((bf16[512,128]{1,0:T(8,128)(2,1)S(1)}, bf16[512,128]{1,0:T(8,128)(2,1)S(1)}, u32[]{:S(2)}, u32[]{:S(2)}) %collective-permute-start.17) | collective-permute-done | bytes 131104 | tf_op jit(solution)/shard_map/ppermute | solution.py:492
  74.1 0.4 collective-permute-done.18.came3
  74.5 1.4 %shard_map.105 = (f32[4,256,128]{2,1,0:T(8,128)S(1)}, f32[4,256,128]{2,1,0:T(8,128)S(1)}) custom-call(s32[3]{0:T(128)S(1)} %pad_add_fusion.where_ref, bf16[512,128]{1,0:T(8,128)(2,1)S(1)} %collective-permute-done.15.came0, bf16[512,128]{1,0:T(8,128)(2,1)S(1)} %collective-permute-done.16.came1, bf16[512,128]{1,0:T(8,128)(2,1)S(1)} %collective-permute-done.17.came2, ...), custom_call_target="tpu_custom_call" | custom-call | flops 1500000000 | bytes 524300 | tf_op jit(solution)/shard_map/pallas_call | solution.py:216
  75.9 1.3 %collective-permute-start.19 = (f32[4,256,128]{2,1,0:T(8,128)S(1)}, f32[4,256,128]{2,1,0:T(8,128)S(1)}, u32[]{:S(2)}, u32[]{:S(2)}) collective-permute-start(f32[4,256,128]{2,1,0:T(8,128)S(1)} %get-tuple-element.66), channel_id=1, source_target_pairs={{0,1},{1,0},{2,3},{3,2},{4,5},{5,4},{6,7},{7,6},{8,9},{9,8},{10,11... | collective-permute-start | bytes 1572872 | tf_op jit(solution)/shard_map/ppermute | solution.py:505
  77.2 1.5 %collective-permute-done.19.got_ref = f32[4,256,128]{2,1,0:T(8,128)S(1)} collective-permute-done((f32[4,256,128]{2,1,0:T(8,128)S(1)}, f32[4,256,128]{2,1,0:T(8,128)S(1)}, u32[]{:S(2)}, u32[]{:S(2)}) %collective-permute-start.19) | collective-permute-done | bytes 524320 | tf_op jit(solution)/shard_map/ppermute | solution.py:505
  78.8 3.2 %collective-permute-start.20 = (bf16[256,128]{1,0:T(8,128)(2,1)S(1)}, bf16[256,128]{1,0:T(8,128)(2,1)S(1)}, u32[]{:S(2)}, u32[]{:S(2)}) collective-permute-start(bf16[256,128]{1,0:T(8,128)(2,1)S(1)} %get-tuple-element.67), channel_id=1, source_target_pairs={{0,14},{1,11},{2,12},{3,9},{4,10},{5,15},{6,8},{7,13},{8,6},{9,3},... | collective-permute-start | bytes 196616 | tf_op jit(solution)/shard_map/ppermute | solution.py:492
  82.0 1.4 %collective-permute-start.21 = (bf16[256,128]{1,0:T(8,128)(2,1)S(1)}, bf16[256,128]{1,0:T(8,128)(2,1)S(1)}, u32[]{:S(2)}, u32[]{:S(2)}) collective-permute-start(bf16[256,128]{1,0:T(8,128)(2,1)S(1)} %get-tuple-element.68), channel_id=1, source_target_pairs={{0,12},{1,9},{2,14},{3,11},{4,8},{5,13},{6,10},{7,15},{8,4},{9,1},... | collective-permute-start | bytes 196616 | tf_op jit(solution)/shard_map/ppermute | solution.py:492
  83.4 0.8 collective-permute-start.22
  84.2 2.9 %collective-permute-start.23 = (bf16[256,128]{1,0:T(8,128)(2,1)S(1)}, bf16[256,128]{1,0:T(8,128)(2,1)S(1)}, u32[]{:S(2)}, u32[]{:S(2)}) collective-permute-start(bf16[256,128]{1,0:T(8,128)(2,1)S(1)} %get-tuple-element.70), channel_id=1, source_target_pairs={{0,2},{1,1},{2,0},{3,3},{4,6},{5,5},{6,4},{7,7},{8,10},{9,9},{10,8... | collective-permute-start | bytes 196616 | tf_op jit(solution)/shard_map/ppermute | solution.py:492
  87.2 0.6 copy-done.2
  87.8 0.6 collective-permute-done.21.came1
  88.4 0.6 copy-done.4
  89.0 0.5 collective-permute-done.22.came2
  89.5 0.8 collective-permute-done.23.came3
  90.4 0.3 collective-permute-start.24
  90.7 1.1 %collective-permute-done.24.other_ref = bf16[512,128]{1,0:T(8,128)(2,1)S(1)} collective-permute-done((bf16[512,128]{1,0:T(8,128)(2,1)S(1)}, bf16[512,128]{1,0:T(8,128)(2,1)S(1)}, u32[]{:S(2)}, u32[]{:S(2)}) %collective-permute-start.24) | collective-permute-done | bytes 131104 | tf_op jit(solution)/shard_map/ppermute | solution.py:505
  91.8 2.2 %shard_map.107 = bf16[8,128,128]{2,1,0:T(8,128)(2,1)} custom-call(s32[3]{0:T(128)S(1)} %pad_add_fusion.where_ref, bf16[256,128]{1,0:T(8,128)(2,1)S(1)} %copy-done.3, bf16[256,128]{1,0:T(8,128)(2,1)S(1)} %copy-done.5, bf16[256,128]{1,0:T(8,128)(2,1)S(1)} %collective-permute-done.22.came2, bf16[256,128]{1,0:T(8,128)(2,1)S(1)} %collective-permute-done.23.came3, ...), custom_call_target="tpu_custom_call" | custom-call | flops 1500000000 | bytes 1507340 | tf_op jit(solution)/shard_map/pallas_call | solution.py:216
  (63 shorter events, 0.5 us)
Async XLA Ops:
  0.0 0.7 copy-start.14
  0.0 0.7 copy-start.15
  0.9 0.9 %copy-start.7 = (bf16[64,8,256]{2,1,0:T(8,128)(2,1)S(1)}, bf16[64,8,256]{2,1,0:T(8,128)(2,1)}, u32[]{:S(2)}) copy-start(bf16[64,8,256]{2,1,0:T(8,128)(2,1)} %feat_ref.1) | copy-start | bytes 786436
  1.8 0.8 copy-start.11
  2.6 6.7 %copy-start.6 = (bf16[2,128,640]{2,1,0:T(8,128)(2,1)S(1)}, bf16[2,128,640]{2,1,0:T(8,128)(2,1)}, u32[]{:S(2)}) copy-start(bf16[2,128,640]{2,1,0:T(8,128)(2,1)} %proj_ref.1) | copy-start | bytes 983044
  2.6 6.7 %copy-start.8 = (bf16[8,128,128]{2,1,0:T(8,128)(2,1)S(1)}, bf16[8,128,128]{2,1,0:T(8,128)(2,1)}, u32[]{:S(2)}) copy-start(bf16[8,128,128]{2,1,0:T(8,128)(2,1)} %pair_ref.1) | copy-start | bytes 786436
  2.6 6.8 %copy-start.9 = (bf16[1024,128]{1,0:T(8,128)(2,1)S(1)}, bf16[1024,128]{1,0:T(8,128)(2,1)}, u32[]{:S(2)}) copy-start(bf16[1024,128]{1,0:T(8,128)(2,1)} %outer_ref.1) | copy-start | bytes 786436
  2.6 6.8 %copy-start.10 = (bf16[2,128,128]{2,1,0:T(8,128)(2,1)S(1)}, bf16[2,128,128]{2,1,0:T(8,128)(2,1)}, u32[]{:S(2)}) copy-start(bf16[2,128,128]{2,1,0:T(8,128)(2,1)} %out_ref.1) | copy-start | bytes 196612
  3.6 8.5 %collective-permute-start.2 = (bf16[144,128]{1,0:T(8,128)(2,1)S(1)}, bf16[144,128]{1,0:T(8,128)(2,1)S(1)}, u32[]{:S(2)}, u32[]{:S(2)}) collective-permute-start(bf16[144,128]{1,0:T(8,128)(2,1)S(1)} %get-tuple-element.39), channel_id=1, source_target_pairs={{0,4},{1,5},{2,6},{3,7},{4,0},{5,1},{6,2},{7,3},{8,12},{9,13},{10,... | collective-permute-start | bytes 110600 | tf_op jit(solution)/shard_map/ppermute | solution.py:487
  6.7 5.5 %collective-permute-start.1 = (bf16[144,128]{1,0:T(8,128)(2,1)S(1)}, bf16[144,128]{1,0:T(8,128)(2,1)S(1)}, u32[]{:S(2)}, u32[]{:S(2)}) collective-permute-start(bf16[144,128]{1,0:T(8,128)(2,1)S(1)} %get-tuple-element.39), channel_id=1, source_target_pairs={{0,8},{1,9},{2,10},{3,11},{4,12},{5,13},{6,14},{7,15},{8,0},{9,1},... | collective-permute-start | bytes 110600 | tf_op jit(solution)/shard_map/ppermute | solution.py:487
  9.3 5.8 %collective-permute-start = (bf16[144,128]{1,0:T(8,128)(2,1)S(1)}, bf16[144,128]{1,0:T(8,128)(2,1)S(1)}, u32[]{:S(2)}, u32[]{:S(2)}) collective-permute-start(bf16[144,128]{1,0:T(8,128)(2,1)S(1)} %get-tuple-element.39), channel_id=1, source_target_pairs={{0,12},{1,13},{2,14},{3,15},{4,8},{5,9},{6,10},{7,11},{8,4},{9,5},... | collective-permute-start | bytes 110600 | tf_op jit(solution)/shard_map/ppermute | solution.py:487
  9.3 0.7 copy-start.12
  9.3 0.7 copy-start.13
  15.0 5.2 %collective-permute-start.3 = (bf16[4,144,128]{2,1,0:T(8,128)(2,1)S(1)}, bf16[4,144,128]{2,1,0:T(8,128)(2,1)S(1)}, u32[]{:S(2)}, u32[]{:S(2)}) collective-permute-start(bf16[4,144,128]{2,1,0:T(8,128)(2,1)S(1)} %pad_maximum_fusion.2), channel_id=1, source_target_pairs={{0,2},{1,3},{2,0},{3,1},{4,6},{5,7},{6,4},{7,5},{8,10},{9,11},{10,... | collective-permute-start | bytes 442376 | tf_op jit(solution)/shard_map/ppermute | solution.py:487
  20.3 1.6 %collective-permute-start.4 = (bf16[8,144,128]{2,1,0:T(8,128)(2,1)S(1)}, bf16[8,144,128]{2,1,0:T(8,128)(2,1)S(1)}, u32[]{:S(2)}, u32[]{:S(2)}) collective-permute-start(bf16[8,144,128]{2,1,0:T(8,128)(2,1)S(1)} %constant_dynamic-update-slice_fusion.own_ref), channel_id=1, source_target_pairs={{0,1},{1,0},{2,3},{3,2},{4,5},{5,4},{6,7},{7,6},{8,9},{9,8},{10,11... | collective-permute-start | bytes 884744 | tf_op jit(solution)/shard_map/ppermute | solution.py:505
  25.1 1.8 %collective-permute-start.5 = (bf16[1536,128]{1,0:T(8,128)(2,1)S(1)}, bf16[1536,128]{1,0:T(8,128)(2,1)S(1)}, u32[]{:S(2)}, u32[]{:S(2)}) collective-permute-start(bf16[1536,128]{1,0:T(8,128)(2,1)S(1)} %get-tuple-element.51), channel_id=1, source_target_pairs={{0,1},{1,0},{2,3},{3,2},{4,5},{5,4},{6,7},{7,6},{8,9},{9,8},{10,11... | collective-permute-start | bytes 1179656 | tf_op jit(solution)/shard_map/ppermute | solution.py:505
  26.9 9.1 %collective-permute-start.6 = (bf16[512,128]{1,0:T(8,128)(2,1)S(1)}, bf16[512,128]{1,0:T(8,128)(2,1)S(1)}, u32[]{:S(2)}, u32[]{:S(2)}) collective-permute-start(bf16[512,128]{1,0:T(8,128)(2,1)S(1)} %pad_maximum_fusion.3), channel_id=1, source_target_pairs={{0,14},{1,11},{2,12},{3,9},{4,10},{5,15},{6,8},{7,13},{8,6},{9,3},... | collective-permute-start | bytes 393224 | tf_op jit(solution)/shard_map/ppermute | solution.py:492
  28.8 10.1 %collective-permute-start.7 = (bf16[512,128]{1,0:T(8,128)(2,1)S(1)}, bf16[512,128]{1,0:T(8,128)(2,1)S(1)}, u32[]{:S(2)}, u32[]{:S(2)}) collective-permute-start(bf16[512,128]{1,0:T(8,128)(2,1)S(1)} %pad_maximum_fusion.4), channel_id=1, source_target_pairs={{0,12},{1,9},{2,14},{3,11},{4,8},{5,13},{6,10},{7,15},{8,4},{9,1},... | collective-permute-start | bytes 393224 | tf_op jit(solution)/shard_map/ppermute | solution.py:492
  31.8 12.2 %collective-permute-start.8 = (bf16[1024,128]{1,0:T(8,128)(2,1)S(1)}, bf16[1024,128]{1,0:T(8,128)(2,1)S(1)}, u32[]{:S(2)}, u32[]{:S(2)}) collective-permute-start(bf16[1024,128]{1,0:T(8,128)(2,1)S(1)} %pad_maximum_fusion), channel_id=1, source_target_pairs={{0,6},{1,5},{2,4},{3,7},{4,2},{5,1},{6,0},{7,3},{8,14},{9,13},{10,... | collective-permute-start | bytes 786440 | tf_op jit(solution)/shard_map/ppermute | solution.py:492
  31.9 12.1 %collective-permute-start.9 = (bf16[1024,128]{1,0:T(8,128)(2,1)S(1)}, bf16[1024,128]{1,0:T(8,128)(2,1)S(1)}, u32[]{:S(2)}, u32[]{:S(2)}) collective-permute-start(bf16[1024,128]{1,0:T(8,128)(2,1)S(1)} %pad_maximum_fusion.1), channel_id=1, source_target_pairs={{0,2},{1,1},{2,0},{3,3},{4,6},{5,5},{6,4},{7,7},{8,10},{9,9},{10,8... | collective-permute-start | bytes 786440 | tf_op jit(solution)/shard_map/ppermute | solution.py:492
  44.1 2.0 %collective-permute-start.10 = (bf16[8,256,128]{2,1,0:T(8,128)(2,1)S(1)}, bf16[8,256,128]{2,1,0:T(8,128)(2,1)S(1)}, u32[]{:S(2)}, u32[]{:S(2)}) collective-permute-start(bf16[8,256,128]{2,1,0:T(8,128)(2,1)S(1)} %fusion), channel_id=1, source_target_pairs={{0,1},{1,0},{2,3},{3,2},{4,5},{5,4},{6,7},{7,6},{8,9},{9,8},{10,11... | collective-permute-start | bytes 1572872 | tf_op jit(solution)/shard_map/ppermute | solution.py:505
  47.5 6.5 %collective-permute-start.11 = (bf16[512,128]{1,0:T(8,128)(2,1)S(1)}, bf16[512,128]{1,0:T(8,128)(2,1)S(1)}, u32[]{:S(2)}, u32[]{:S(2)}) collective-permute-start(bf16[512,128]{1,0:T(8,128)(2,1)S(1)} %get-tuple-element.55), channel_id=1, source_target_pairs={{0,6},{1,5},{2,4},{3,7},{4,2},{5,1},{6,0},{7,3},{8,14},{9,13},{10,... | collective-permute-start | bytes 393224 | tf_op jit(solution)/shard_map/ppermute | solution.py:492
  48.9 6.8 %collective-permute-start.12 = (bf16[512,128]{1,0:T(8,128)(2,1)S(1)}, bf16[512,128]{1,0:T(8,128)(2,1)S(1)}, u32[]{:S(2)}, u32[]{:S(2)}) collective-permute-start(bf16[512,128]{1,0:T(8,128)(2,1)S(1)} %get-tuple-element.56), channel_id=1, source_target_pairs={{0,2},{1,1},{2,0},{3,3},{4,6},{5,5},{6,4},{7,7},{8,10},{9,9},{10,8... | collective-permute-start | bytes 393224 | tf_op jit(solution)/shard_map/ppermute | solution.py:492
  54.0 0.7 copy-start
  55.7 0.8 slice-start
  56.5 1.4 %copy-start.1 = (bf16[512,128]{1,0:T(8,128)(2,1)S(1)}, bf16[512,128]{1,0:T(8,128)(2,1)}, u32[]{:S(2)}) copy-start(bf16[512,128]{1,0:T(8,128)(2,1)} %copy-done) | copy-start | bytes 393220
  56.6 1.4 %collective-permute-start.13 = (bf16[512,128]{1,0:T(8,128)(2,1)S(1)}, bf16[512,128]{1,0:T(8,128)(2,1)S(1)}, u32[]{:S(2)}, u32[]{:S(2)}) collective-permute-start(bf16[512,128]{1,0:T(8,128)(2,1)S(1)} %pad_maximum_fusion.5), channel_id=1, source_target_pairs={{0,1},{1,0},{2,3},{3,2},{4,5},{5,4},{6,7},{7,6},{8,9},{9,8},{10,11... | collective-permute-start | bytes 393224 | tf_op jit(solution)/shard_map/ppermute | solution.py:505
  60.2 1.6 %collective-permute-start.14 = (bf16[1024,128]{1,0:T(8,128)(2,1)S(1)}, bf16[1024,128]{1,0:T(8,128)(2,1)S(1)}, u32[]{:S(2)}, u32[]{:S(2)}) collective-permute-start(bf16[1024,128]{1,0:T(8,128)(2,1)S(1)} %get-tuple-element.61), channel_id=1, source_target_pairs={{0,1},{1,0},{2,3},{3,2},{4,5},{5,4},{6,7},{7,6},{8,9},{9,8},{10,11... | collective-permute-start | bytes 786440 | tf_op jit(solution)/shard_map/ppermute | solution.py:505
  61.9 9.2 %collective-permute-start.15 = (bf16[512,128]{1,0:T(8,128)(2,1)S(1)}, bf16[512,128]{1,0:T(8,128)(2,1)S(1)}, u32[]{:S(2)}, u32[]{:S(2)}) collective-permute-start(bf16[512,128]{1,0:T(8,128)(2,1)S(1)} %pad_maximum_fusion.6), channel_id=1, source_target_pairs={{0,14},{1,11},{2,12},{3,9},{4,10},{5,15},{6,8},{7,13},{8,6},{9,3},... | collective-permute-start | bytes 393224 | tf_op jit(solution)/shard_map/ppermute | solution.py:492
  63.5 9.5 %collective-permute-start.16 = (bf16[512,128]{1,0:T(8,128)(2,1)S(1)}, bf16[512,128]{1,0:T(8,128)(2,1)S(1)}, u32[]{:S(2)}, u32[]{:S(2)}) collective-permute-start(bf16[512,128]{1,0:T(8,128)(2,1)S(1)} %pad_maximum_fusion.7), channel_id=1, source_target_pairs={{0,12},{1,9},{2,14},{3,11},{4,8},{5,13},{6,10},{7,15},{8,4},{9,1},... | collective-permute-start | bytes 393224 | tf_op jit(solution)/shard_map/ppermute | solution.py:492
  65.9 8.2 %collective-permute-start.17 = (bf16[512,128]{1,0:T(8,128)(2,1)S(1)}, bf16[512,128]{1,0:T(8,128)(2,1)S(1)}, u32[]{:S(2)}, u32[]{:S(2)}) collective-permute-start(bf16[512,128]{1,0:T(8,128)(2,1)S(1)} %pad_maximum_fusion.8), channel_id=1, source_target_pairs={{0,6},{1,5},{2,4},{3,7},{4,2},{5,1},{6,0},{7,3},{8,14},{9,13},{10,... | collective-permute-start | bytes 393224 | tf_op jit(solution)/shard_map/ppermute | solution.py:492
  66.7 7.9 %collective-permute-start.18 = (bf16[512,128]{1,0:T(8,128)(2,1)S(1)}, bf16[512,128]{1,0:T(8,128)(2,1)S(1)}, u32[]{:S(2)}, u32[]{:S(2)}) collective-permute-start(bf16[512,128]{1,0:T(8,128)(2,1)S(1)} %pad_maximum_fusion.9), channel_id=1, source_target_pairs={{0,2},{1,1},{2,0},{3,3},{4,6},{5,5},{6,4},{7,7},{8,10},{9,9},{10,8... | collective-permute-start | bytes 393224 | tf_op jit(solution)/shard_map/ppermute | solution.py:492
  75.9 2.8 %collective-permute-start.19 = (f32[4,256,128]{2,1,0:T(8,128)S(1)}, f32[4,256,128]{2,1,0:T(8,128)S(1)}, u32[]{:S(2)}, u32[]{:S(2)}) collective-permute-start(f32[4,256,128]{2,1,0:T(8,128)S(1)} %get-tuple-element.66), channel_id=1, source_target_pairs={{0,1},{1,0},{2,3},{3,2},{4,5},{5,4},{6,7},{7,6},{8,9},{9,8},{10,11... | collective-permute-start | bytes 1572872 | tf_op jit(solution)/shard_map/ppermute | solution.py:505
  78.8 8.3 %collective-permute-start.20 = (bf16[256,128]{1,0:T(8,128)(2,1)S(1)}, bf16[256,128]{1,0:T(8,128)(2,1)S(1)}, u32[]{:S(2)}, u32[]{:S(2)}) collective-permute-start(bf16[256,128]{1,0:T(8,128)(2,1)S(1)} %get-tuple-element.67), channel_id=1, source_target_pairs={{0,14},{1,11},{2,12},{3,9},{4,10},{5,15},{6,8},{7,13},{8,6},{9,3},... | collective-permute-start | bytes 196616 | tf_op jit(solution)/shard_map/ppermute | solution.py:492
  82.0 6.4 %collective-permute-start.21 = (bf16[256,128]{1,0:T(8,128)(2,1)S(1)}, bf16[256,128]{1,0:T(8,128)(2,1)S(1)}, u32[]{:S(2)}, u32[]{:S(2)}) collective-permute-start(bf16[256,128]{1,0:T(8,128)(2,1)S(1)} %get-tuple-element.68), channel_id=1, source_target_pairs={{0,12},{1,9},{2,14},{3,11},{4,8},{5,13},{6,10},{7,15},{8,4},{9,1},... | collective-permute-start | bytes 196616 | tf_op jit(solution)/shard_map/ppermute | solution.py:492
  83.4 6.1 %collective-permute-start.22 = (bf16[256,128]{1,0:T(8,128)(2,1)S(1)}, bf16[256,128]{1,0:T(8,128)(2,1)S(1)}, u32[]{:S(2)}, u32[]{:S(2)}) collective-permute-start(bf16[256,128]{1,0:T(8,128)(2,1)S(1)} %get-tuple-element.69), channel_id=1, source_target_pairs={{0,6},{1,5},{2,4},{3,7},{4,2},{5,1},{6,0},{7,3},{8,14},{9,13},{10,... | collective-permute-start | bytes 196616 | tf_op jit(solution)/shard_map/ppermute | solution.py:492
  84.2 6.1 %collective-permute-start.23 = (bf16[256,128]{1,0:T(8,128)(2,1)S(1)}, bf16[256,128]{1,0:T(8,128)(2,1)S(1)}, u32[]{:S(2)}, u32[]{:S(2)}) collective-permute-start(bf16[256,128]{1,0:T(8,128)(2,1)S(1)} %get-tuple-element.70), channel_id=1, source_target_pairs={{0,2},{1,1},{2,0},{3,3},{4,6},{5,5},{6,4},{7,7},{8,10},{9,9},{10,8... | collective-permute-start | bytes 196616 | tf_op jit(solution)/shard_map/ppermute | solution.py:492
  87.1 0.6 copy-start.2
  88.4 0.6 copy-start.4
  89.5 0.8 slice-start.1
  89.5 0.8 slice-start.2
  90.4 1.5 %copy-start.3 = (bf16[256,128]{1,0:T(8,128)(2,1)S(1)}, bf16[256,128]{1,0:T(8,128)(2,1)}, u32[]{:S(2)}) copy-start(bf16[256,128]{1,0:T(8,128)(2,1)} %copy-done.2) | copy-start | bytes 196612
  90.4 1.4 %copy-start.5 = (bf16[256,128]{1,0:T(8,128)(2,1)S(1)}, bf16[256,128]{1,0:T(8,128)(2,1)}, u32[]{:S(2)}) copy-start(bf16[256,128]{1,0:T(8,128)(2,1)} %copy-done.4) | copy-start | bytes 196612
  90.4 1.4 %collective-permute-start.24 = (bf16[512,128]{1,0:T(8,128)(2,1)S(1)}, bf16[512,128]{1,0:T(8,128)(2,1)S(1)}, u32[]{:S(2)}, u32[]{:S(2)}) collective-permute-start(bf16[512,128]{1,0:T(8,128)(2,1)S(1)} %pad_maximum_fusion.10), channel_id=1, source_target_pairs={{0,1},{1,0},{2,3},{3,2},{4,5},{5,4},{6,7},{7,6},{8,9},{9,8},{10,11... | collective-permute-start | bytes 393224 | tf_op jit(solution)/shard_map/ppermute | solution.py:505

commit v8 on v7

--- a/solution.py
+++ b/solution.py
@@ -228,6 +228,7 @@
 SPLIT = ((7, 5), (6, 4), (3, 2), (1, 0))
 OPS = len(SPLIT)
 NEAR = 4
+NEAR_STEPS = (3, 2, 1, 0)
 
 
 def partner_chip(chip, core, op):
@@ -238,7 +239,7 @@
     homologs, rows, _ = feat_ref.shape
     half = weight_ref.shape[0] // 2
     quarter = half // 2
-    values = feat_ref[...].astype(F32).reshape(homologs * rows, feat_ref.shape[2])
+    values = feat_ref[...].reshape(homologs * rows, feat_ref.shape[2])
     center = values - jnp.mean(values, axis=1, keepdims=True)
     spread = jnp.mean(center * center, axis=1, keepdims=True)
     normed = (center * lax.rsqrt(spread + EPSILON)).astype(BF16)
@@ -314,14 +315,14 @@
 
 def outer_kernel(
     where_ref, flag_ref, own_ref, other_ref, left_ref, live_ref, base_ref, outer_t_ref, proj_ref, present_ref,
-    stream_ref, gate_ref, mine0, mine1, mine2, mine3, theirs_ref, came, outer, lefts, rights,
+    stream_ref, gate_ref, far0, far1, theirs_ref, near0, near1, near2, near3, came, outer, lefts, rights,
 ):
     rows, width, cols = base_ref.shape
     chip, core = where_ref[1], where_ref[2]
     per = own_ref.shape[1]
     chips = own_ref.shape[0]
     for at in range(chips):
-        chip_at = chip ^ ((3 - at % 4) * 2 + at // 4)
+        chip_at = chip ^ (at % 2 * 4 + at // 2 % 2 * 2 + at // 4)
         came[chip_at * 2 + core] = own_ref[at].astype(F32)
         came[chip_at * 2 + (1 - core)] = other_ref[at].astype(F32)
     half = left_ref.shape[0] // (2 * rows)
@@ -352,46 +353,55 @@
         sides(streams, proj_ref[0], lives, gate_ref, lefts, rights, row)
     size = width // NEAR
     block = size * rows
-    place = 0
-    for op, mine in enumerate((mine0, mine1, mine2, mine3)):
-        for theirs in range(2):
-            to = partner_chip(chip, core ^ theirs, op)
-            first = pl.multiple_of((to & (NEAR - 1)) * size, size)
-            sent = [rights] if op < OPS // 2 else [lefts, rights]
-            for at, side in enumerate(sent):
-                made = flat(side[pl.ds(first, size)]).astype(BF16)
-                if theirs:
-                    theirs_ref[place : place + block] = made
-                    place += block
-                else:
-                    mine[at * block : (at + 1) * block] = made
+
+    def group(side, to):
+        first = pl.multiple_of((to & (NEAR - 1)) * size, size)
+        return flat(side[pl.ds(first, size)]).astype(BF16)
+
+    for op, far in enumerate((far0, far1)):
+        far[...] = group(rights, partner_chip(chip, core, op))
+        theirs_ref[op * block : (op + 1) * block] = group(rights, partner_chip(chip, 1 - core, op))
+    for step, near in enumerate((near0, near1, near2, near3)):
+        near[0:block] = group(lefts, chip ^ step)
+        near[block:] = group(rights, chip ^ step)
 
 
 def per_lane(ref):
     return ref.shape[-1]
 
 
-def mix_rows_kernel(where_ref, came0, came1, came2, came3, other_ref, out0, out1, lefts, rights, mixed):
+def mix_rows_kernel(
+    where_ref, near0, near1, near2, near3, far0, far1, other_ref,
+    out0, out1, out2, out3, lefts, rights, mixed,
+):
     chip, core = where_ref[1], where_ref[2]
     count, rows, cols = lefts.shape[1:]
     block = count * rows
-    for op, came in enumerate((came0, came1, came2, came3)):
-        sent = came.shape[0] // 2
+    for at, (step, near) in enumerate(zip(NEAR_STEPS, (near0, near1, near2, near3))):
+        lefts[step] = near[0:block].astype(F32).reshape(count, rows, cols)
+        rights[(chip ^ step) * 2 + core] = near[block:].astype(F32).reshape(count, rows, cols)
+        theirs = other_ref[at * block : (at + 1) * block]
+        rights[(chip ^ step) * 2 + (1 - core)] = theirs.astype(F32).reshape(count, rows, cols)
+    for op, far in enumerate((far0, far1)):
         for half in range(2):
-            mine = came[(half + 1) * sent - block : (half + 1) * sent].astype(F32)
             at = partner_chip(chip, core, op) * 2 + (core ^ half)
-            rights[at] = mine.reshape(count, rows, cols)
+            rights[at] = far[half * block : (half + 1) * block].astype(F32).reshape(count, rows, cols)
             at = partner_chip(chip, 1 - core, op) * 2 + ((1 - core) ^ half)
-            rights[at] = other_ref[op * 2 + half].astype(F32).reshape(count, rows, cols)
-            if op >= OPS // 2:
-                left = came[half * sent : half * sent + block].astype(F32)
-                lefts[(op - OPS // 2) * 2 + half] = left.reshape(count, rows, cols)
+            place = (NEAR + op * 2 + half) * block
+            rights[at] = other_ref[place : place + block].astype(F32).reshape(count, rows, cols)
     for c in range(count):
         left = flat(lefts[:, c]).astype(BF16)
         right = flat(rights[:, c]).astype(BF16)
         mixed[:, c, :] = nt(left, right)
-    for at, out in enumerate((out0, out1)):
-        out[...] = flat(mixed[at * 2 * rows : (at + 1) * 2 * rows]).astype(BF16)
+    for step, out in enumerate((out0, out1, out2, out3)):
+        out[...] = flat(mixed[step * rows : (step + 1) * rows]).astype(BF16)
+
+
+def pick_kernel(*refs):
+    blocks, out_ref = refs[:-1], refs[-1]
+    for at, block in enumerate(blocks):
+        half = block.shape[0] // 2
+        out_ref[at * half : (at + 1) * half] = block[half:]
 
 
 def update(came, row, stream_ref, gate_ref, out_weight):
@@ -404,19 +414,14 @@
 
 
 def between_kernel(
-    where_ref, flag_ref, in0, in1, other_ref, stream_ref, gate_ref, out_weight_ref, proj_ref, present_ref,
+    where_ref, flag_ref, in0, in1, in2, in3, stream_ref, gate_ref, out_weight_ref, proj_ref, present_ref,
     next_ref, next_gate_ref, mine0, mine1, mine2, mine3, theirs_ref, came, lefts, rights,
 ):
     rows, width, cols = stream_ref.shape
     chip, core = where_ref[1], where_ref[2]
     size = width // NEAR
-    for at, block in enumerate((in0, in1)):
-        op = OPS // 2 + at
-        group = partner_chip(chip, core, op) & (NEAR - 1)
-        came[:, group] = block[0 : size * rows].astype(F32).reshape(rows, size, cols)
-        group = partner_chip(chip, 1 - core, op) & (NEAR - 1)
-        block = other_ref[at * size * rows : (at + 1) * size * rows]
-        came[:, group] = block.astype(F32).reshape(rows, size, cols)
+    for step, block in zip(NEAR_STEPS, (in0, in1, in2, in3)):
+        came[:, (chip ^ step) & (NEAR - 1)] = block[...].astype(F32).reshape(rows, size, cols)
     present = present_ref[...].astype(F32)
     for row in range(0, rows, 2):
         streams = update(came, row, stream_ref, gate_ref, out_weight_ref[0])
@@ -485,6 +490,10 @@
 def chip_permute(block, step):
     count = lax.axis_size("wide")
     return lax.ppermute(block, "wide", [(w, w ^ (2 * step)) for w in range(count)])
+
+
+def exchange(blocks, steps):
+    return [chip_permute(blocks[step], step) if step else blocks[0] for step in steps]
 
 
 def split_permute(block, op):
@@ -531,10 +540,10 @@
     pay, left, live = run(
         project_kernel,
         [((pay_rows, LANES), BF16), ((2 * rows * half, LANES), BF16), ((rows, LANES), F32)],
-        homolog_features, homolog_to_sides_matrix.T, live,
+        homolog_features.astype(F32), homolog_to_sides_matrix.T, live,
         scratch=[((rows, half // 2, LANES), F32), ((pay_rows, LANES), F32)],
     )
-    along_z = [chip_permute(pay, 2 * z) for z in (2, 3, 1)]
+    far_z = chip_permute(pay, 4)
     base, outer_t, proj_t, out_t = run(
         prep_kernel,
         [
@@ -548,8 +557,9 @@
         smem=(0, 1),
         scratch=[((LANES, width), F32), ((half, half, width), F32)],
     )
-    along_z = jnp.stack([along_z[1], along_z[0], along_z[2], pay])
+    along_z = jnp.stack([pay, far_z])
     along_z, base, outer_t, proj_t, out_t = lax.optimization_barrier((along_z, base, outer_t, proj_t, out_t))
+    along_z = jnp.concatenate([along_z, chip_permute(along_z, 2)], axis=0)
     own = jnp.concatenate([along_z, chip_permute(along_z, 1)], axis=0)
     other = core_permute(own)
     tall = width * rows
@@ -558,8 +568,7 @@
         outer_kernel,
         [((rows, width, cols), F32)] * 2
         + [((near, cols), BF16)] * 2
-        + [((2 * near, cols), BF16)] * 2
-        + [((6 * near, cols), BF16)],
+        + [((2 * near, cols), BF16)] * (1 + NEAR),
         where, resolved_residue_mask, own, other, left, live, base, outer_t, proj_t, present,
         smem=(0, 1),
         scratch=[
@@ -570,30 +579,26 @@
         ],
         flops=4 * 10**9,
     )
-    stream, gate, theirs = made[0], made[1], made[6]
-    came = [split_permute(block, op) for op, block in enumerate(with_partner(made[2:6], theirs))]
-    rights = []
-    for block in came:
-        for part in range(2):
-            end = (part + 1) * block.shape[0] // 2
-            rights.append(block[end - near : end])
+    stream, gate = made[0], made[1]
+    came = exchange(made[5:9], NEAR_STEPS)
+    far = [split_permute(block, op) for op, block in enumerate(with_partner(made[2:4], made[4]))]
+    rights = jnp.concatenate([block[near:] for block in came] + far, axis=0)
     mixed = run(
         mix_rows_kernel,
-        [((2 * near, cols), BF16)] * 2,
-        where, *came, core_permute(jnp.stack(rights)),
+        [((near, cols), BF16)] * NEAR,
+        where, *came, *far, core_permute(rights),
         smem=(0,),
         scratch=[
-            ((4, width // NEAR, rows, cols), F32),
+            ((NEAR, width // NEAR, rows, cols), F32),
             ((16, width // NEAR, rows, cols), F32),
-            ((4 * rows, width // NEAR, cols), F32),
+            ((NEAR * rows, width // NEAR, cols), F32),
         ],
     )
-    mixed = [split_permute(block, OPS // 2 + at) for at, block in enumerate(mixed)]
-    other = core_permute(jnp.concatenate([block[near:] for block in mixed], axis=0))
+    mixed = exchange(mixed, NEAR_STEPS)
     made = run(
         between_kernel,
         [((rows, width, cols), F32)] * 2 + [((2 * all_, cols), BF16)] * OPS + [((2 * OPS * all_, cols), BF16)],
-        where, resolved_residue_mask, *mixed, other, stream, gate, out_t, proj_t, present,
+        where, resolved_residue_mask, *mixed, stream, gate, out_t, proj_t, present,
         smem=(0, 1),
         scratch=[
             ((rows, NEAR, width // NEAR, cols), F32),
@@ -616,7 +621,7 @@
     )
     mixed = run(sum_kernel, [((2 * all_, cols), BF16)] * OPS, mine, core_permute(theirs))
     mixed = [split_permute(block, op) for op, block in enumerate(mixed)]
-    other = core_permute(jnp.concatenate([block[all_:] for block in mixed], axis=0))
+    other = core_permute(run(pick_kernel, [((OPS * all_, cols), BF16)], *mixed)[0])
     return run(
         final_kernel,
         [((rows, cols, width), BF16)],

time: 94.5 us -> 89.8 us (0.950)
  local copies, waits for them, and re-layouts: 5.96 us -> 1.47 us
  waiting for transfers between devices: 37.5 us -> 33.5 us
  starting transfers between devices: 36.4 us -> 39.4 us
    ppermute x14 -> x10, waiting for transfers between devices: 20.5 us -> 13.2 us  [split_permute(): lax.ppermute(block, 'wide', [(w, w ^ 2 * SPLIT[op][w % 2]) for w in range...]
    ppermute x4 -> x9, starting transfers between devices: 7.24 us -> 14.5 us  [chip_permute(): lax.ppermute(block, 'wide', [(w, w ^ 2 * step) for w in range(count)])]
    ppermute x4 -> x9, waiting for transfers between devices: 6.61 us -> 12.9 us  [chip_permute(): lax.ppermute(block, 'wide', [(w, w ^ 2 * step) for w in range(count)])]
    ppermute x14 -> x10, starting transfers between devices: 26.9 us -> 22.1 us  [split_permute(): lax.ppermute(block, 'wide', [(w, w ^ 2 * SPLIT[op][w % 2]) for w in range...]
    unnamed x40 -> x25, local copies, waits for them, and re-layouts: 5.03 us -> 1.4 us
    ppermute x7 -> x6, waiting for transfers between devices: 10.4 us -> 7.5 us  [core_permute(): return lax.ppermute(block, 'wide', [(w, w ^ 1) for w in range(count)])]
    convert_element_type x0 -> x1, other arithmetic: none -> 0.99 us  [per_device_chips(): homolog_features.astype(F32)]
    ppermute x7 -> x6, starting transfers between devices: 2.23 us -> 2.84 us  [core_permute(): return lax.ppermute(block, 'wide', [(w, w ^ 1) for w in range(count)])]
  transfers between devices with their start and end apart: 25 -> 25, of which waited for: 22 -> 20; matrix products, arithmetic and copies ran while one was open for 0% -> 0% of each run, Pallas kernels for 2% -> 2%
where the time goes in v8:
time: 89.8 us; the launch traced here: 89.5 us
  starting transfers between devices  39.4 us (44%)
  waiting for transfers between devices  33.5 us (37%)
  Pallas kernels  13.4 us (15%)
  local copies, waits for them, and re-layouts  1.47 us (2%)
  other arithmetic  1.38 us (2%)
    ppermute x10, starting transfers between devices, split_permute(): lax.ppermute(block, 'wide', [(w, w ^ 2 * SPLIT[op][w % 2]) for w in range...  22.1 us
    ppermute x9, starting transfers between devices, chip_permute(): lax.ppermute(block, 'wide', [(w, w ^ 2 * step) for w in range(count)])  14.5 us
    pallas_call x9, Pallas kernels, run(): pl.pallas_call(kernel, out_shape=[jax.ShapeDtypeStruct(shape, kind) for s...  13.4 us
    ppermute x10, waiting for transfers between devices, split_permute(): lax.ppermute(block, 'wide', [(w, w ^ 2 * SPLIT[op][w % 2]) for w in range...  13.2 us
    ppermute x9, waiting for transfers between devices, chip_permute(): lax.ppermute(block, 'wide', [(w, w ^ 2 * step) for w in range(count)])  12.9 us
    ppermute x6, waiting for transfers between devices, core_permute(): return lax.ppermute(block, 'wide', [(w, w ^ 1) for w in range(count)])  7.5 us
    ppermute x6, starting transfers between devices, core_permute(): return lax.ppermute(block, 'wide', [(w, w ^ 1) for w in range(count)])  2.84 us
  transfers between devices with their start and end apart: 25, of which 20 were waited for; matrix products, arithmetic and copies ran while one was open for 0% of the time, Pallas kernels for 2%

profile of v8, /device:TPU:0, one launch (start us, length us, event | category | flops | bytes accessed | tf_op | source)
XLA Modules:
  0.0 89.5 jit_solution(7299354491986652505)
XLA Ops:
  0.0 0.7 copy-done.7
  0.7 0.1 dynamic-slice_convert_fusion
  0.7 0.1 multiply_bitcast_fusion
  0.8 0.1 pad_maximum_fusion.8.live_in_ref
  0.9 1.0 %convert_element_type.10.feat_ref = f32[64,8,256]{2,1,0:T(8,128)S(1)} convert(bf16[64,8,256]{2,1,0:T(8,128)(2,1)} %param.11) | non-fusion elementwise | flops 131072 | bytes 786432 | tf_op jit(solution)/shard_map/convert_element_type | solution.py:543
  1.9 0.0 copy-start
  1.9 0.0 copy-start.1
  1.9 0.0 copy-start.2
  1.9 0.0 copy-start.3
  1.9 1.0 %shard_map.100 = (bf16[144,128]{1,0:T(8,128)(2,1)S(1)}, bf16[512,128]{1,0:T(8,128)(2,1)S(1)}, f32[8,128]{1,0:T(8,128)S(1)}) custom-call(f32[64,8,256]{2,1,0:T(8,128)S(1)} %convert_element_type.10.feat_ref, bf16[64,256]{1,0:T(8,128)(2,1)S(1)} %bitcast.11, f32[8,128]{1,0:T(8,128)S(1)} %pad_maximum_fusion.8.live_in_ref), custom_call_target="tpu_custom_call" | custom-call | flops 1500000000 | bytes 561152 | tf_op jit(solution)/shard_map/pallas_call | solution.py:216
  2.9 4.1 %collective-permute-start = (bf16[144,128]{1,0:T(8,128)(2,1)S(1)}, bf16[144,128]{1,0:T(8,128)(2,1)S(1)}, u32[]{:S(2)}, u32[]{:S(2)}) collective-permute-start(bf16[144,128]{1,0:T(8,128)(2,1)S(1)} %get-tuple-element.43), channel_id=1, source_target_pairs={{0,8},{1,9},{2,10},{3,11},{4,12},{5,13},{6,14},{7,15},{8,0},{9,1},... | collective-permute-start | bytes 110600 | tf_op jit(solution)/shard_map/ppermute | solution.py:492
  7.0 0.1 pad_add_fusion.where_ref
  7.1 0.6 copy-done.5
  7.7 0.0 copy-done.6
  7.7 2.0 %shard_map.101 = (f32[8,128,128]{2,1,0:T(8,128)S(1)}, bf16[128,1024]{1,0:T(8,128)(2,1)S(1)}, bf16[2,640,128]{2,1,0:T(8,128)(2,1)S(1)}, bf16[2,128,128]{2,1,0:T(8,128)(2,1)S(1)}) custom-call(s32[3]{0:T(128)S(1)} %pad_add_fusion.where_ref, s32[128]{0:T(128)S(1)} %copy-done.6, s32[1,128]{1,0:T(1,128)S(1)} %bitcast.12, bf16[8,128,128]{2,1,0:T(8,128)(2,1)S(1)} %copy-done.1, ...), custom_call_target="tpu_custom_call" | custom-call | flops 1500000000 | bytes 935436 | tf_op jit(solution)/shard_map/pallas_call | solution.py:216
  9.8 1.6 %collective-permute-start.1 = (bf16[2,144,128]{2,1,0:T(8,128)(2,1)S(1)}, bf16[2,144,128]{2,1,0:T(8,128)(2,1)S(1)}, u32[]{:S(2)}, u32[]{:S(2)}) collective-permute-start(bf16[2,144,128]{2,1,0:T(8,128)(2,1)S(1)} %pad_maximum_fusion.7), channel_id=1, source_target_pairs={{0,4},{1,5},{2,6},{3,7},{4,0},{5,1},{6,2},{7,3},{8,12},{9,13},{10,... | collective-permute-start | bytes 221192 | tf_op jit(solution)/shard_map/ppermute | solution.py:492
  11.4 2.8 %collective-permute-done.1 = bf16[2,144,128]{2,1,0:T(8,128)(2,1)S(1)} collective-permute-done((bf16[2,144,128]{2,1,0:T(8,128)(2,1)S(1)}, bf16[2,144,128]{2,1,0:T(8,128)(2,1)S(1)}, u32[]{:S(2)}, u32[]{:S(2)}) %collective-permute-start.1) | collective-permute-done | bytes 73760 | tf_op jit(solution)/shard_map/ppermute | solution.py:492
  14.2 1.6 %collective-permute-start.2 = (bf16[4,144,128]{2,1,0:T(8,128)(2,1)S(1)}, bf16[4,144,128]{2,1,0:T(8,128)(2,1)S(1)}, u32[]{:S(2)}, u32[]{:S(2)}) collective-permute-start(bf16[4,144,128]{2,1,0:T(8,128)(2,1)S(1)} %pad_maximum_fusion), channel_id=1, source_target_pairs={{0,2},{1,3},{2,0},{3,1},{4,6},{5,7},{6,4},{7,5},{8,10},{9,11},{10,... | collective-permute-start | bytes 442376 | tf_op jit(solution)/shard_map/ppermute | solution.py:492
  15.8 3.6 %collective-permute-done.2 = bf16[4,144,128]{2,1,0:T(8,128)(2,1)S(1)} collective-permute-done((bf16[4,144,128]{2,1,0:T(8,128)(2,1)S(1)}, bf16[4,144,128]{2,1,0:T(8,128)(2,1)S(1)}, u32[]{:S(2)}, u32[]{:S(2)}) %collective-permute-start.2) | collective-permute-done | bytes 147488 | tf_op jit(solution)/shard_map/ppermute | solution.py:492
  19.5 0.1 collective-permute-start.3
  19.6 1.6 %collective-permute-done.3.other_ref = bf16[8,144,128]{2,1,0:T(8,128)(2,1)S(1)} collective-permute-done((bf16[8,144,128]{2,1,0:T(8,128)(2,1)S(1)}, bf16[8,144,128]{2,1,0:T(8,128)(2,1)S(1)}, u32[]{:S(2)}, u32[]{:S(2)}) %collective-permute-start.3) | collective-permute-done | bytes 294944 | tf_op jit(solution)/shard_map/ppermute | solution.py:514
  21.1 3.1 %shard_map.102 = (f32[8,128,128]{2,1,0:T(8,128)S(1)}, f32[8,128,128]{2,1,0:T(8,128)S(1)}, bf16[256,128]{1,0:T(8,128)(2,1)S(1)}, bf16[256,128]{1,0:T(8,128)(2,1)S...) custom-call(s32[3]{0:T(128)S(1)} %pad_add_fusion.where_ref, ...), custom_call_target="tpu_custom_call" | custom-call | flops 4000000000 | bytes 1840140 | tf_op jit(solution)/shard_map/pallas_call | solution.py:216
  24.3 0.2 collective-permute-start.7
  24.5 2.5 %collective-permute-start.4 = (bf16[512,128]{1,0:T(8,128)(2,1)S(1)}, bf16[512,128]{1,0:T(8,128)(2,1)S(1)}, u32[]{:S(2)}, u32[]{:S(2)}) collective-permute-start(bf16[512,128]{1,0:T(8,128)(2,1)S(1)} %get-tuple-element.54), channel_id=1, source_target_pairs={{0,6},{1,7},{2,4},{3,5},{4,2},{5,3},{6,0},{7,1},{8,14},{9,15},{10,... | collective-permute-start | bytes 393224 | tf_op jit(solution)/shard_map/ppermute | solution.py:492
  27.0 0.4 collective-permute-start.5
  27.5 0.5 collective-permute-start.6
  28.0 4.4 %collective-permute-start.8 = (bf16[512,128]{1,0:T(8,128)(2,1)S(1)}, bf16[512,128]{1,0:T(8,128)(2,1)S(1)}, u32[]{:S(2)}, u32[]{:S(2)}) collective-permute-start(bf16[512,128]{1,0:T(8,128)(2,1)S(1)} %pad_maximum_fusion.1), channel_id=1, source_target_pairs={{0,14},{1,11},{2,12},{3,9},{4,10},{5,15},{6,8},{7,13},{8,6},{9,3},... | collective-permute-start | bytes 393224 | tf_op jit(solution)/shard_map/ppermute | solution.py:501
  32.4 0.5 collective-permute-start.9
  32.9 3.4 %collective-permute-done.5.near1 = bf16[512,128]{1,0:T(8,128)(2,1)S(1)} collective-permute-done((bf16[512,128]{1,0:T(8,128)(2,1)S(1)}, bf16[512,128]{1,0:T(8,128)(2,1)S(1)}, u32[]{:S(2)}, u32[]{:S(2)}) %collective-permute-start.5) | collective-permute-done | bytes 131104 | tf_op jit(solution)/shard_map/ppermute | solution.py:492
  36.4 2.5 %collective-permute-done.8.far0 = bf16[512,128]{1,0:T(8,128)(2,1)S(1)} collective-permute-done((bf16[512,128]{1,0:T(8,128)(2,1)S(1)}, bf16[512,128]{1,0:T(8,128)(2,1)S(1)}, u32[]{:S(2)}, u32[]{:S(2)}) %collective-permute-start.8) | collective-permute-done | bytes 131104 | tf_op jit(solution)/shard_map/ppermute | solution.py:501
  39.0 2.3 %collective-permute-done.9.far1 = bf16[512,128]{1,0:T(8,128)(2,1)S(1)} collective-permute-done((bf16[512,128]{1,0:T(8,128)(2,1)S(1)}, bf16[512,128]{1,0:T(8,128)(2,1)S(1)}, u32[]{:S(2)}, u32[]{:S(2)}) %collective-permute-start.9) | collective-permute-done | bytes 131104 | tf_op jit(solution)/shard_map/ppermute | solution.py:501
  41.3 1.0 %collective-permute-start.10 = (bf16[2048,128]{1,0:T(8,128)(2,1)S(1)}, bf16[2048,128]{1,0:T(8,128)(2,1)S(1)}, u32[]{:S(2)}, u32[]{:S(2)}) collective-permute-start(bf16[2048,128]{1,0:T(8,128)(2,1)S(1)} %constant_dynamic-update-slice_fusion.3), channel_id=1, source_target_pairs={{0,1},{1,0},{2,3},{3,2},{4,5},{5,4},{6,7},{7,6},{8,9},{9,8},{10,11... | collective-permute-start | bytes 1572872 | tf_op jit(solution)/shard_map/ppermute | solution.py:514
  42.3 1.5 %collective-permute-done.10.other_ref = bf16[2048,128]{1,0:T(8,128)(2,1)S(1)} collective-permute-done((bf16[2048,128]{1,0:T(8,128)(2,1)S(1)}, bf16[2048,128]{1,0:T(8,128)(2,1)S(1)}, u32[]{:S(2)}, u32[]{:S(2)}) %collective-permute-start.10) | collective-permute-done | bytes 524320 | tf_op jit(solution)/shard_map/ppermute | solution.py:514
  43.8 1.4 %shard_map.103 = (bf16[256,128]{1,0:T(8,128)(2,1)S(1)}, bf16[256,128]{1,0:T(8,128)(2,1)S(1)}, bf16[256,128]{1,0:T(8,128)(2,1)S(1)}, bf16[256,128]{1,0:T(8,128)(2,1)S(1)}) custom-call(s32[3]{0:T(128)S(1)} %pad_add_fusion.where_ref, bf16[512,128]{1,0:T(8,128)(2,1)S(1)} %collective-permute-done.4.near0, bf16[512,128]{1,0:T(8,128)(2,1)S(1)} %collective-permute-done.5.near1, ...), custom_call_target="tpu_custom_call" | custom-call | flops 1500000000 | bytes 1310732 | tf_op jit(solution)/shard_map/pallas_call | solution.py:216
  45.2 2.2 %collective-permute-start.11 = (bf16[256,128]{1,0:T(8,128)(2,1)S(1)}, bf16[256,128]{1,0:T(8,128)(2,1)S(1)}, u32[]{:S(2)}, u32[]{:S(2)}) collective-permute-start(bf16[256,128]{1,0:T(8,128)(2,1)S(1)} %get-tuple-element.61), channel_id=1, source_target_pairs={{0,6},{1,7},{2,4},{3,5},{4,2},{5,3},{6,0},{7,1},{8,14},{9,15},{10,... | collective-permute-start | bytes 196616 | tf_op jit(solution)/shard_map/ppermute | solution.py:492
  47.5 0.1 collective-permute-start.12
  47.6 1.4 %collective-permute-start.13 = (bf16[256,128]{1,0:T(8,128)(2,1)S(1)}, bf16[256,128]{1,0:T(8,128)(2,1)S(1)}, u32[]{:S(2)}, u32[]{:S(2)}) collective-permute-start(bf16[256,128]{1,0:T(8,128)(2,1)S(1)} %get-tuple-element.63), channel_id=1, source_target_pairs={{0,2},{1,3},{2,0},{3,1},{4,6},{5,7},{6,4},{7,5},{8,10},{9,11},{10,... | collective-permute-start | bytes 196616 | tf_op jit(solution)/shard_map/ppermute | solution.py:492
  49.0 1.7 %collective-permute-done.11.in0 = bf16[256,128]{1,0:T(8,128)(2,1)S(1)} collective-permute-done((bf16[256,128]{1,0:T(8,128)(2,1)S(1)}, bf16[256,128]{1,0:T(8,128)(2,1)S(1)}, u32[]{:S(2)}, u32[]{:S(2)}) %collective-permute-start.11) | collective-permute-done | bytes 65568 | tf_op jit(solution)/shard_map/ppermute | solution.py:492
  50.6 1.1 %collective-permute-done.12.in1 = bf16[256,128]{1,0:T(8,128)(2,1)S(1)} collective-permute-done((bf16[256,128]{1,0:T(8,128)(2,1)S(1)}, bf16[256,128]{1,0:T(8,128)(2,1)S(1)}, u32[]{:S(2)}, u32[]{:S(2)}) %collective-permute-start.12) | collective-permute-done | bytes 65568 | tf_op jit(solution)/shard_map/ppermute | solution.py:492
  51.7 0.3 collective-permute-done.13.in2
  52.0 2.2 %shard_map.104 = (f32[8,128,128]{2,1,0:T(8,128)S(1)}, f32[8,128,128]{2,1,0:T(8,128)S(1)}, bf16[256,128]{1,0:T(8,128)(2,1)S(1)}, bf16[256,128]{1,0:T(8,128)(2,1)S...) custom-call(s32[3]{0:T(128)S(1)} %pad_add_fusion.where_ref, ...), custom_call_target="tpu_custom_call" | custom-call | flops 1500000000 | bytes 1704972 | tf_op jit(solution)/shard_map/pallas_call | solution.py:216
  54.2 0.1 collective-permute-start.14
  54.3 1.5 %collective-permute-done.14 = bf16[1024,128]{1,0:T(8,128)(2,1)S(1)} collective-permute-done((bf16[1024,128]{1,0:T(8,128)(2,1)S(1)}, bf16[1024,128]{1,0:T(8,128)(2,1)S(1)}, u32[]{:S(2)}, u32[]{:S(2)}) %collective-permute-start.14) | collective-permute-done | bytes 262176 | tf_op jit(solution)/shard_map/ppermute | solution.py:514
  55.9 4.7 %collective-permute-start.15 = (bf16[512,128]{1,0:T(8,128)(2,1)S(1)}, bf16[512,128]{1,0:T(8,128)(2,1)S(1)}, u32[]{:S(2)}, u32[]{:S(2)}) collective-permute-start(bf16[512,128]{1,0:T(8,128)(2,1)S(1)} %pad_maximum_fusion.3), channel_id=1, source_target_pairs={{0,14},{1,11},{2,12},{3,9},{4,10},{5,15},{6,8},{7,13},{8,6},{9,3},... | collective-permute-start | bytes 393224 | tf_op jit(solution)/shard_map/ppermute | solution.py:501
  60.6 0.1 collective-permute-start.16
  60.7 0.6 collective-permute-start.17
  61.3 3.2 %collective-permute-start.18 = (bf16[512,128]{1,0:T(8,128)(2,1)S(1)}, bf16[512,128]{1,0:T(8,128)(2,1)S(1)}, u32[]{:S(2)}, u32[]{:S(2)}) collective-permute-start(bf16[512,128]{1,0:T(8,128)(2,1)S(1)} %pad_maximum_fusion.6), channel_id=1, source_target_pairs={{0,2},{1,1},{2,0},{3,3},{4,6},{5,5},{6,4},{7,7},{8,10},{9,9},{10,8... | collective-permute-start | bytes 393224 | tf_op jit(solution)/shard_map/ppermute | solution.py:501
  64.5 0.5 collective-permute-done.15.came0
  65.0 3.8 %collective-permute-done.16.came1 = bf16[512,128]{1,0:T(8,128)(2,1)S(1)} collective-permute-done((bf16[512,128]{1,0:T(8,128)(2,1)S(1)}, bf16[512,128]{1,0:T(8,128)(2,1)S(1)}, u32[]{:S(2)}, u32[]{:S(2)}) %collective-permute-start.16) | collective-permute-done | bytes 131104 | tf_op jit(solution)/shard_map/ppermute | solution.py:501
  68.8 0.3 collective-permute-done.17.came2
  69.1 0.2 collective-permute-done.18.came3
  69.3 1.4 %shard_map.105 = (f32[4,256,128]{2,1,0:T(8,128)S(1)}, f32[4,256,128]{2,1,0:T(8,128)S(1)}) custom-call(s32[3]{0:T(128)S(1)} %pad_add_fusion.where_ref, bf16[512,128]{1,0:T(8,128)(2,1)S(1)} %collective-permute-done.15.came0, bf16[512,128]{1,0:T(8,128)(2,1)S(1)} %collective-permute-done.16.came1, bf16[512,128]{1,0:T(8,128)(2,1)S(1)} %collective-permute-done.17.came2, ...), custom_call_target="tpu_custom_call" | custom-call | flops 1500000000 | bytes 524300 | tf_op jit(solution)/shard_map/pallas_call | solution.py:216
  70.7 1.4 %collective-permute-start.19 = (f32[4,256,128]{2,1,0:T(8,128)S(1)}, f32[4,256,128]{2,1,0:T(8,128)S(1)}, u32[]{:S(2)}, u32[]{:S(2)}) collective-permute-start(f32[4,256,128]{2,1,0:T(8,128)S(1)} %get-tuple-element.74), channel_id=1, source_target_pairs={{0,1},{1,0},{2,3},{3,2},{4,5},{5,4},{6,7},{7,6},{8,9},{9,8},{10,11... | collective-permute-start | bytes 1572872 | tf_op jit(solution)/shard_map/ppermute | solution.py:514
  72.1 1.5 %collective-permute-done.19.got_ref = f32[4,256,128]{2,1,0:T(8,128)S(1)} collective-permute-done((f32[4,256,128]{2,1,0:T(8,128)S(1)}, f32[4,256,128]{2,1,0:T(8,128)S(1)}, u32[]{:S(2)}, u32[]{:S(2)}) %collective-permute-start.19) | collective-permute-done | bytes 524320 | tf_op jit(solution)/shard_map/ppermute | solution.py:514
  73.7 4.7 %collective-permute-start.20 = (bf16[256,128]{1,0:T(8,128)(2,1)S(1)}, bf16[256,128]{1,0:T(8,128)(2,1)S(1)}, u32[]{:S(2)}, u32[]{:S(2)}) collective-permute-start(bf16[256,128]{1,0:T(8,128)(2,1)S(1)} %get-tuple-element.75), channel_id=1, source_target_pairs={{0,14},{1,11},{2,12},{3,9},{4,10},{5,15},{6,8},{7,13},{8,6},{9,3},... | collective-permute-start | bytes 196616 | tf_op jit(solution)/shard_map/ppermute | solution.py:501
  78.4 0.5 collective-permute-start.21
  78.9 0.6 collective-permute-start.22
  79.5 2.8 %collective-permute-start.23 = (bf16[256,128]{1,0:T(8,128)(2,1)S(1)}, bf16[256,128]{1,0:T(8,128)(2,1)S(1)}, u32[]{:S(2)}, u32[]{:S(2)}) collective-permute-start(bf16[256,128]{1,0:T(8,128)(2,1)S(1)} %get-tuple-element.78), channel_id=1, source_target_pairs={{0,2},{1,1},{2,0},{3,3},{4,6},{5,5},{6,4},{7,7},{8,10},{9,9},{10,8... | collective-permute-start | bytes 196616 | tf_op jit(solution)/shard_map/ppermute | solution.py:501
  82.3 2.2 %collective-permute-done.21.refs_1_.came1 = bf16[256,128]{1,0:T(8,128)(2,1)S(1)} collective-permute-done((bf16[256,128]{1,0:T(8,128)(2,1)S(1)}, bf16[256,128]{1,0:T(8,128)(2,1)S(1)}, u32[]{:S(2)}, u32[]{:S(2)}) %collective-permute-start.21) | collective-permute-done | bytes 65568 | tf_op jit(solution)/shard_map/ppermute | solution.py:501
  84.5 0.8 collective-permute-done.22.refs_2_.came2
  85.3 0.5 collective-permute-done.23.refs_3_.came3
  85.9 0.1 collective-permute-start.24
  86.0 1.3 %collective-permute-done.24.other_ref = bf16[512,128]{1,0:T(8,128)(2,1)S(1)} collective-permute-done((bf16[512,128]{1,0:T(8,128)(2,1)S(1)}, bf16[512,128]{1,0:T(8,128)(2,1)S(1)}, u32[]{:S(2)}, u32[]{:S(2)}) %collective-permute-start.24) | collective-permute-done | bytes 131104 | tf_op jit(solution)/shard_map/ppermute | solution.py:514
  87.3 2.2 %shard_map.108 = bf16[8,128,128]{2,1,0:T(8,128)(2,1)} custom-call(s32[3]{0:T(128)S(1)} %pad_add_fusion.where_ref, bf16[256,128]{1,0:T(8,128)(2,1)S(1)} %collective-permute-done.20.refs_0_.came0, bf16[256,128]{1,0:T(8,128)(2,1)S(1)} %collective-permute-done.21.refs_1_.came1, bf16[256,128]{1,0:T(8,128)(2,1)S(1)} %collective-permute-done.22.refs_2_.came2, ...), custom_call_target="tpu_custom_call" | custom-call | flops 1500000000 | bytes 1507340 | tf_op jit(solution)/shard_map/pallas_call | solution.py:216
  (37 shorter events, 0.3 us)
Async XLA Ops:
  0.0 0.7 copy-start.7
  0.0 0.7 copy-start.8
  0.9 1.0 %copy-start.4 = (bf16[256,64]{0,1:T(8,128)(2,1)S(1)}, bf16[256,64]{0,1:T(8,128)(2,1)}, u32[]{:S(2)}) copy-start(bf16[256,64]{0,1:T(8,128)(2,1)} %param.16) | copy-start | bytes 98308
  1.9 5.2 %copy-start = (bf16[2,128,640]{2,1,0:T(8,128)(2,1)S(1)}, bf16[2,128,640]{2,1,0:T(8,128)(2,1)}, u32[]{:S(2)}) copy-start(bf16[2,128,640]{2,1,0:T(8,128)(2,1)} %proj_ref.1) | copy-start | bytes 983044
  1.9 5.2 %copy-start.1 = (bf16[8,128,128]{2,1,0:T(8,128)(2,1)S(1)}, bf16[8,128,128]{2,1,0:T(8,128)(2,1)}, u32[]{:S(2)}) copy-start(bf16[8,128,128]{2,1,0:T(8,128)(2,1)} %pair_ref.1) | copy-start | bytes 786436
  1.9 5.2 %copy-start.2 = (bf16[1024,128]{1,0:T(8,128)(2,1)S(1)}, bf16[1024,128]{1,0:T(8,128)(2,1)}, u32[]{:S(2)}) copy-start(bf16[1024,128]{1,0:T(8,128)(2,1)} %outer_ref.1) | copy-start | bytes 786436
  1.9 5.2 %copy-start.3 = (bf16[2,128,128]{2,1,0:T(8,128)(2,1)S(1)}, bf16[2,128,128]{2,1,0:T(8,128)(2,1)}, u32[]{:S(2)}) copy-start(bf16[2,128,128]{2,1,0:T(8,128)(2,1)} %out_ref.1) | copy-start | bytes 196612
  2.9 6.9 %collective-permute-start = (bf16[144,128]{1,0:T(8,128)(2,1)S(1)}, bf16[144,128]{1,0:T(8,128)(2,1)S(1)}, u32[]{:S(2)}, u32[]{:S(2)}) collective-permute-start(bf16[144,128]{1,0:T(8,128)(2,1)S(1)} %get-tuple-element.43), channel_id=1, source_target_pairs={{0,8},{1,9},{2,10},{3,11},{4,12},{5,13},{6,14},{7,15},{8,0},{9,1},... | collective-permute-start | bytes 110600 | tf_op jit(solution)/shard_map/ppermute | solution.py:492
  7.0 0.7 copy-start.5
  7.1 0.7 copy-start.6
  9.8 4.4 %collective-permute-start.1 = (bf16[2,144,128]{2,1,0:T(8,128)(2,1)S(1)}, bf16[2,144,128]{2,1,0:T(8,128)(2,1)S(1)}, u32[]{:S(2)}, u32[]{:S(2)}) collective-permute-start(bf16[2,144,128]{2,1,0:T(8,128)(2,1)S(1)} %pad_maximum_fusion.7), channel_id=1, source_target_pairs={{0,4},{1,5},{2,6},{3,7},{4,0},{5,1},{6,2},{7,3},{8,12},{9,13},{10,... | collective-permute-start | bytes 221192 | tf_op jit(solution)/shard_map/ppermute | solution.py:492
  14.2 5.2 %collective-permute-start.2 = (bf16[4,144,128]{2,1,0:T(8,128)(2,1)S(1)}, bf16[4,144,128]{2,1,0:T(8,128)(2,1)S(1)}, u32[]{:S(2)}, u32[]{:S(2)}) collective-permute-start(bf16[4,144,128]{2,1,0:T(8,128)(2,1)S(1)} %pad_maximum_fusion), channel_id=1, source_target_pairs={{0,2},{1,3},{2,0},{3,1},{4,6},{5,7},{6,4},{7,5},{8,10},{9,11},{10,... | collective-permute-start | bytes 442376 | tf_op jit(solution)/shard_map/ppermute | solution.py:492
  19.5 1.6 %collective-permute-start.3 = (bf16[8,144,128]{2,1,0:T(8,128)(2,1)S(1)}, bf16[8,144,128]{2,1,0:T(8,128)(2,1)S(1)}, u32[]{:S(2)}, u32[]{:S(2)}) collective-permute-start(bf16[8,144,128]{2,1,0:T(8,128)(2,1)S(1)} %constant_dynamic-update-slice_fusion.own_ref), channel_id=1, source_target_pairs={{0,1},{1,0},{2,3},{3,2},{4,5},{5,4},{6,7},{7,6},{8,9},{9,8},{10,11... | collective-permute-start | bytes 884744 | tf_op jit(solution)/shard_map/ppermute | solution.py:514
  24.3 3.7 %collective-permute-start.7 = (bf16[512,128]{1,0:T(8,128)(2,1)S(1)}, bf16[512,128]{1,0:T(8,128)(2,1)S(1)}, u32[]{:S(2)}, u32[]{:S(2)}) collective-permute-start(bf16[512,128]{1,0:T(8,128)(2,1)S(1)} %get-tuple-element.59), channel_id=1, source_target_pairs={{0,1},{1,0},{2,3},{3,2},{4,5},{5,4},{6,7},{7,6},{8,9},{9,8},{10,11... | collective-permute-start | bytes 393224 | tf_op jit(solution)/shard_map/ppermute | solution.py:514
  24.5 8.4 %collective-permute-start.4 = (bf16[512,128]{1,0:T(8,128)(2,1)S(1)}, bf16[512,128]{1,0:T(8,128)(2,1)S(1)}, u32[]{:S(2)}, u32[]{:S(2)}) collective-permute-start(bf16[512,128]{1,0:T(8,128)(2,1)S(1)} %get-tuple-element.54), channel_id=1, source_target_pairs={{0,6},{1,7},{2,4},{3,5},{4,2},{5,3},{6,0},{7,1},{8,14},{9,15},{10,... | collective-permute-start | bytes 393224 | tf_op jit(solution)/shard_map/ppermute | solution.py:492
  27.0 9.3 %collective-permute-start.5 = (bf16[512,128]{1,0:T(8,128)(2,1)S(1)}, bf16[512,128]{1,0:T(8,128)(2,1)S(1)}, u32[]{:S(2)}, u32[]{:S(2)}) collective-permute-start(bf16[512,128]{1,0:T(8,128)(2,1)S(1)} %get-tuple-element.55), channel_id=1, source_target_pairs={{0,4},{1,5},{2,6},{3,7},{4,0},{5,1},{6,2},{7,3},{8,12},{9,13},{10,... | collective-permute-start | bytes 393224 | tf_op jit(solution)/shard_map/ppermute | solution.py:492
  27.5 8.9 %collective-permute-start.6 = (bf16[512,128]{1,0:T(8,128)(2,1)S(1)}, bf16[512,128]{1,0:T(8,128)(2,1)S(1)}, u32[]{:S(2)}, u32[]{:S(2)}) collective-permute-start(bf16[512,128]{1,0:T(8,128)(2,1)S(1)} %get-tuple-element.56), channel_id=1, source_target_pairs={{0,2},{1,3},{2,0},{3,1},{4,6},{5,7},{6,4},{7,5},{8,10},{9,11},{10,... | collective-permute-start | bytes 393224 | tf_op jit(solution)/shard_map/ppermute | solution.py:492
  28.0 10.9 %collective-permute-start.8 = (bf16[512,128]{1,0:T(8,128)(2,1)S(1)}, bf16[512,128]{1,0:T(8,128)(2,1)S(1)}, u32[]{:S(2)}, u32[]{:S(2)}) collective-permute-start(bf16[512,128]{1,0:T(8,128)(2,1)S(1)} %pad_maximum_fusion.1), channel_id=1, source_target_pairs={{0,14},{1,11},{2,12},{3,9},{4,10},{5,15},{6,8},{7,13},{8,6},{9,3},... | collective-permute-start | bytes 393224 | tf_op jit(solution)/shard_map/ppermute | solution.py:501
  32.4 8.9 %collective-permute-start.9 = (bf16[512,128]{1,0:T(8,128)(2,1)S(1)}, bf16[512,128]{1,0:T(8,128)(2,1)S(1)}, u32[]{:S(2)}, u32[]{:S(2)}) collective-permute-start(bf16[512,128]{1,0:T(8,128)(2,1)S(1)} %pad_maximum_fusion.2), channel_id=1, source_target_pairs={{0,12},{1,9},{2,14},{3,11},{4,8},{5,13},{6,10},{7,15},{8,4},{9,1},... | collective-permute-start | bytes 393224 | tf_op jit(solution)/shard_map/ppermute | solution.py:501
  41.3 2.5 %collective-permute-start.10 = (bf16[2048,128]{1,0:T(8,128)(2,1)S(1)}, bf16[2048,128]{1,0:T(8,128)(2,1)S(1)}, u32[]{:S(2)}, u32[]{:S(2)}) collective-permute-start(bf16[2048,128]{1,0:T(8,128)(2,1)S(1)} %constant_dynamic-update-slice_fusion.3), channel_id=1, source_target_pairs={{0,1},{1,0},{2,3},{3,2},{4,5},{5,4},{6,7},{7,6},{8,9},{9,8},{10,11... | collective-permute-start | bytes 1572872 | tf_op jit(solution)/shard_map/ppermute | solution.py:514
  45.2 5.4 %collective-permute-start.11 = (bf16[256,128]{1,0:T(8,128)(2,1)S(1)}, bf16[256,128]{1,0:T(8,128)(2,1)S(1)}, u32[]{:S(2)}, u32[]{:S(2)}) collective-permute-start(bf16[256,128]{1,0:T(8,128)(2,1)S(1)} %get-tuple-element.61), channel_id=1, source_target_pairs={{0,6},{1,7},{2,4},{3,5},{4,2},{5,3},{6,0},{7,1},{8,14},{9,15},{10,... | collective-permute-start | bytes 196616 | tf_op jit(solution)/shard_map/ppermute | solution.py:492
  47.5 4.3 %collective-permute-start.12 = (bf16[256,128]{1,0:T(8,128)(2,1)S(1)}, bf16[256,128]{1,0:T(8,128)(2,1)S(1)}, u32[]{:S(2)}, u32[]{:S(2)}) collective-permute-start(bf16[256,128]{1,0:T(8,128)(2,1)S(1)} %get-tuple-element.62), channel_id=1, source_target_pairs={{0,4},{1,5},{2,6},{3,7},{4,0},{5,1},{6,2},{7,3},{8,12},{9,13},{10,... | collective-permute-start | bytes 196616 | tf_op jit(solution)/shard_map/ppermute | solution.py:492
  47.6 4.4 %collective-permute-start.13 = (bf16[256,128]{1,0:T(8,128)(2,1)S(1)}, bf16[256,128]{1,0:T(8,128)(2,1)S(1)}, u32[]{:S(2)}, u32[]{:S(2)}) collective-permute-start(bf16[256,128]{1,0:T(8,128)(2,1)S(1)} %get-tuple-element.63), channel_id=1, source_target_pairs={{0,2},{1,3},{2,0},{3,1},{4,6},{5,7},{6,4},{7,5},{8,10},{9,11},{10,... | collective-permute-start | bytes 196616 | tf_op jit(solution)/shard_map/ppermute | solution.py:492
  54.2 1.6 %collective-permute-start.14 = (bf16[1024,128]{1,0:T(8,128)(2,1)S(1)}, bf16[1024,128]{1,0:T(8,128)(2,1)S(1)}, u32[]{:S(2)}, u32[]{:S(2)}) collective-permute-start(bf16[1024,128]{1,0:T(8,128)(2,1)S(1)} %get-tuple-element.69), channel_id=1, source_target_pairs={{0,1},{1,0},{2,3},{3,2},{4,5},{5,4},{6,7},{7,6},{8,9},{9,8},{10,11... | collective-permute-start | bytes 786440 | tf_op jit(solution)/shard_map/ppermute | solution.py:514
  55.9 9.1 %collective-permute-start.15 = (bf16[512,128]{1,0:T(8,128)(2,1)S(1)}, bf16[512,128]{1,0:T(8,128)(2,1)S(1)}, u32[]{:S(2)}, u32[]{:S(2)}) collective-permute-start(bf16[512,128]{1,0:T(8,128)(2,1)S(1)} %pad_maximum_fusion.3), channel_id=1, source_target_pairs={{0,14},{1,11},{2,12},{3,9},{4,10},{5,15},{6,8},{7,13},{8,6},{9,3},... | collective-permute-start | bytes 393224 | tf_op jit(solution)/shard_map/ppermute | solution.py:501
  60.6 8.2 %collective-permute-start.16 = (bf16[512,128]{1,0:T(8,128)(2,1)S(1)}, bf16[512,128]{1,0:T(8,128)(2,1)S(1)}, u32[]{:S(2)}, u32[]{:S(2)}) collective-permute-start(bf16[512,128]{1,0:T(8,128)(2,1)S(1)} %pad_maximum_fusion.4), channel_id=1, source_target_pairs={{0,12},{1,9},{2,14},{3,11},{4,8},{5,13},{6,10},{7,15},{8,4},{9,1},... | collective-permute-start | bytes 393224 | tf_op jit(solution)/shard_map/ppermute | solution.py:501
  60.7 8.4 %collective-permute-start.17 = (bf16[512,128]{1,0:T(8,128)(2,1)S(1)}, bf16[512,128]{1,0:T(8,128)(2,1)S(1)}, u32[]{:S(2)}, u32[]{:S(2)}) collective-permute-start(bf16[512,128]{1,0:T(8,128)(2,1)S(1)} %pad_maximum_fusion.5), channel_id=1, source_target_pairs={{0,6},{1,5},{2,4},{3,7},{4,2},{5,1},{6,0},{7,3},{8,14},{9,13},{10,... | collective-permute-start | bytes 393224 | tf_op jit(solution)/shard_map/ppermute | solution.py:501
  61.3 8.0 %collective-permute-start.18 = (bf16[512,128]{1,0:T(8,128)(2,1)S(1)}, bf16[512,128]{1,0:T(8,128)(2,1)S(1)}, u32[]{:S(2)}, u32[]{:S(2)}) collective-permute-start(bf16[512,128]{1,0:T(8,128)(2,1)S(1)} %pad_maximum_fusion.6), channel_id=1, source_target_pairs={{0,2},{1,1},{2,0},{3,3},{4,6},{5,5},{6,4},{7,7},{8,10},{9,9},{10,8... | collective-permute-start | bytes 393224 | tf_op jit(solution)/shard_map/ppermute | solution.py:501
  70.7 3.0 %collective-permute-start.19 = (f32[4,256,128]{2,1,0:T(8,128)S(1)}, f32[4,256,128]{2,1,0:T(8,128)S(1)}, u32[]{:S(2)}, u32[]{:S(2)}) collective-permute-start(f32[4,256,128]{2,1,0:T(8,128)S(1)} %get-tuple-element.74), channel_id=1, source_target_pairs={{0,1},{1,0},{2,3},{3,2},{4,5},{5,4},{6,7},{7,6},{8,9},{9,8},{10,11... | collective-permute-start | bytes 1572872 | tf_op jit(solution)/shard_map/ppermute | solution.py:514
  73.7 8.6 %collective-permute-start.20 = (bf16[256,128]{1,0:T(8,128)(2,1)S(1)}, bf16[256,128]{1,0:T(8,128)(2,1)S(1)}, u32[]{:S(2)}, u32[]{:S(2)}) collective-permute-start(bf16[256,128]{1,0:T(8,128)(2,1)S(1)} %get-tuple-element.75), channel_id=1, source_target_pairs={{0,14},{1,11},{2,12},{3,9},{4,10},{5,15},{6,8},{7,13},{8,6},{9,3},... | collective-permute-start | bytes 196616 | tf_op jit(solution)/shard_map/ppermute | solution.py:501
  78.4 6.2 %collective-permute-start.21 = (bf16[256,128]{1,0:T(8,128)(2,1)S(1)}, bf16[256,128]{1,0:T(8,128)(2,1)S(1)}, u32[]{:S(2)}, u32[]{:S(2)}) collective-permute-start(bf16[256,128]{1,0:T(8,128)(2,1)S(1)} %get-tuple-element.76), channel_id=1, source_target_pairs={{0,12},{1,9},{2,14},{3,11},{4,8},{5,13},{6,10},{7,15},{8,4},{9,1},... | collective-permute-start | bytes 196616 | tf_op jit(solution)/shard_map/ppermute | solution.py:501
  78.9 6.5 %collective-permute-start.22 = (bf16[256,128]{1,0:T(8,128)(2,1)S(1)}, bf16[256,128]{1,0:T(8,128)(2,1)S(1)}, u32[]{:S(2)}, u32[]{:S(2)}) collective-permute-start(bf16[256,128]{1,0:T(8,128)(2,1)S(1)} %get-tuple-element.77), channel_id=1, source_target_pairs={{0,6},{1,5},{2,4},{3,7},{4,2},{5,1},{6,0},{7,3},{8,14},{9,13},{10,... | collective-permute-start | bytes 196616 | tf_op jit(solution)/shard_map/ppermute | solution.py:501
  79.5 6.4 %collective-permute-start.23 = (bf16[256,128]{1,0:T(8,128)(2,1)S(1)}, bf16[256,128]{1,0:T(8,128)(2,1)S(1)}, u32[]{:S(2)}, u32[]{:S(2)}) collective-permute-start(bf16[256,128]{1,0:T(8,128)(2,1)S(1)} %get-tuple-element.78), channel_id=1, source_target_pairs={{0,2},{1,1},{2,0},{3,3},{4,6},{5,5},{6,4},{7,7},{8,10},{9,9},{10,8... | collective-permute-start | bytes 196616 | tf_op jit(solution)/shard_map/ppermute | solution.py:501
  85.9 1.4 %collective-permute-start.24 = (bf16[512,128]{1,0:T(8,128)(2,1)S(1)}, bf16[512,128]{1,0:T(8,128)(2,1)S(1)}, u32[]{:S(2)}, u32[]{:S(2)}) collective-permute-start(bf16[512,128]{1,0:T(8,128)(2,1)S(1)} %shard_map.107), channel_id=1, source_target_pairs={{0,1},{1,0},{2,3},{3,2},{4,5},{5,4},{6,7},{7,6},{8,9},{9,8},{10,11... | collective-permute-start | bytes 393224 | tf_op jit(solution)/shard_map/ppermute | solution.py:514

commit v9 on v8

--- a/solution.py
+++ b/solution.py
@@ -225,14 +225,15 @@
 
 
 VMEM_LIMIT = 20 * 1024 * 1024
-SPLIT = ((7, 5), (6, 4), (3, 2), (1, 0))
+SPLIT = ((7, 3), (2, 6), (5, 1), (0, 4))
+FAR_SPLIT = ((7, 5), (6, 4))
 OPS = len(SPLIT)
 NEAR = 4
 NEAR_STEPS = (3, 2, 1, 0)
 
 
-def partner_chip(chip, core, op):
-    return chip ^ jnp.where(core == 0, SPLIT[op][0], SPLIT[op][1])
+def partner_chip(chip, core, op, split=SPLIT):
+    return chip ^ jnp.where(core == 0, split[op][0], split[op][1])
 
 
 def project_kernel(feat_ref, weight_ref, live_in_ref, pay_ref, left_ref, live_ref, turned, packed):
@@ -359,8 +360,8 @@
         return flat(side[pl.ds(first, size)]).astype(BF16)
 
     for op, far in enumerate((far0, far1)):
-        far[...] = group(rights, partner_chip(chip, core, op))
-        theirs_ref[op * block : (op + 1) * block] = group(rights, partner_chip(chip, 1 - core, op))
+        far[...] = group(rights, partner_chip(chip, core, op, FAR_SPLIT))
+        theirs_ref[op * block : (op + 1) * block] = group(rights, partner_chip(chip, 1 - core, op, FAR_SPLIT))
     for step, near in enumerate((near0, near1, near2, near3)):
         near[0:block] = group(lefts, chip ^ step)
         near[block:] = group(rights, chip ^ step)
@@ -384,9 +385,9 @@
         rights[(chip ^ step) * 2 + (1 - core)] = theirs.astype(F32).reshape(count, rows, cols)
     for op, far in enumerate((far0, far1)):
         for half in range(2):
-            at = partner_chip(chip, core, op) * 2 + (core ^ half)
+            at = partner_chip(chip, core, op, FAR_SPLIT) * 2 + (core ^ half)
             rights[at] = far[half * block : (half + 1) * block].astype(F32).reshape(count, rows, cols)
-            at = partner_chip(chip, 1 - core, op) * 2 + ((1 - core) ^ half)
+            at = partner_chip(chip, 1 - core, op, FAR_SPLIT) * 2 + ((1 - core) ^ half)
             place = (NEAR + op * 2 + half) * block
             rights[at] = other_ref[place : place + block].astype(F32).reshape(count, rows, cols)
     for c in range(count):
@@ -496,9 +497,13 @@
     return [chip_permute(blocks[step], step) if step else blocks[0] for step in steps]
 
 
-def split_permute(block, op):
+def split_permute(block, steps):
     count = lax.axis_size("wide")
-    return lax.ppermute(block, "wide", [(w, w ^ (2 * SPLIT[op][w % 2])) for w in range(count)])
+    return lax.ppermute(block, "wide", [(w, w ^ (2 * steps[w % 2])) for w in range(count)])
+
+
+def split_exchange(blocks, split=SPLIT):
+    return [split_permute(block, steps) for block, steps in zip(blocks, split)]
 
 
 def with_partner(mine, theirs):
@@ -581,7 +586,7 @@
     )
     stream, gate = made[0], made[1]
     came = exchange(made[5:9], NEAR_STEPS)
-    far = [split_permute(block, op) for op, block in enumerate(with_partner(made[2:4], made[4]))]
+    far = split_exchange(with_partner(made[2:4], made[4]), FAR_SPLIT)
     rights = jnp.concatenate([block[near:] for block in came] + far, axis=0)
     mixed = run(
         mix_rows_kernel,
@@ -607,7 +612,7 @@
         ],
     )
     stream, gate, theirs = made[0], made[1], made[6]
-    came = [split_permute(block, op) for op, block in enumerate(with_partner(made[2:6], theirs))]
+    came = split_exchange(with_partner(made[2:6], theirs))
     mine, theirs = run(
         mix_cols_kernel,
         [((OPS, 2 * all_, cols), F32)] * 2,
@@ -620,7 +625,7 @@
         ],
     )
     mixed = run(sum_kernel, [((2 * all_, cols), BF16)] * OPS, mine, core_permute(theirs))
-    mixed = [split_permute(block, op) for op, block in enumerate(mixed)]
+    mixed = split_exchange(mixed)
     other = core_permute(run(pick_kernel, [((OPS * all_, cols), BF16)], *mixed)[0])
     return run(
         final_kernel,

time: 89.8 us -> 91.2 us (1.016)
  waiting for transfers between devices: 33.5 us -> 40 us
  starting transfers between devices: 39.4 us -> 34.4 us
    ppermute x10, waiting for transfers between devices: 13.2 us -> 19.7 us  [split_permute(): lax.ppermute(block, 'wide', [(w, w ^ 2 * steps[w % 2]) for w in range(cou...]
    ppermute x10, starting transfers between devices: 22.1 us -> 17 us  [split_permute(): lax.ppermute(block, 'wide', [(w, w ^ 2 * steps[w % 2]) for w in range(cou...]
  transfers between devices with their start and end apart: 25 -> 25, of which waited for: 20 -> 19; matrix products, arithmetic and copies ran while one was open for 0% -> 0% of each run, Pallas kernels for 2% -> 2%
where the time goes in v9:
time: 91.2 us; the launch traced here: 90.9 us
  waiting for transfers between devices  40 us (44%)
  starting transfers between devices  34.4 us (38%)
  Pallas kernels  13.4 us (15%)
  local copies, waits for them, and re-layouts  1.47 us (2%)
  other arithmetic  1.38 us (2%)
    ppermute x10, waiting for transfers between devices, split_permute(): lax.ppermute(block, 'wide', [(w, w ^ 2 * steps[w % 2]) for w in range(cou...  19.7 us
    ppermute x10, starting transfers between devices, split_permute(): lax.ppermute(block, 'wide', [(w, w ^ 2 * steps[w % 2]) for w in range(cou...  17 us
    ppermute x9, starting transfers between devices, chip_permute(): lax.ppermute(block, 'wide', [(w, w ^ 2 * step) for w in range(count)])  14.5 us
    pallas_call x9, Pallas kernels, run(): pl.pallas_call(kernel, out_shape=[jax.ShapeDtypeStruct(shape, kind) for s...  13.4 us
    ppermute x9, waiting for transfers between devices, chip_permute(): lax.ppermute(block, 'wide', [(w, w ^ 2 * step) for w in range(count)])  12.9 us
    ppermute x6, waiting for transfers between devices, core_permute(): return lax.ppermute(block, 'wide', [(w, w ^ 1) for w in range(count)])  7.42 us
    ppermute x6, starting transfers between devices, core_permute(): return lax.ppermute(block, 'wide', [(w, w ^ 1) for w in range(count)])  2.84 us
  transfers between devices with their start and end apart: 25, of which 19 were waited for; matrix products, arithmetic and copies ran while one was open for 0% of the time, Pallas kernels for 2%

profile of v9, /device:TPU:0, one launch (start us, length us, event | category | flops | bytes accessed | tf_op | source)
XLA Modules:
  0.0 90.9 jit_solution(17942148973430460483)
XLA Ops:
  0.0 0.7 copy-done.7
  0.7 0.1 dynamic-slice_convert_fusion
  0.7 0.1 multiply_bitcast_fusion
  0.8 0.1 pad_maximum_fusion.8.live_in_ref
  0.9 1.0 %convert_element_type.10.feat_ref = f32[64,8,256]{2,1,0:T(8,128)S(1)} convert(bf16[64,8,256]{2,1,0:T(8,128)(2,1)} %param.11) | non-fusion elementwise | flops 131072 | bytes 786432 | tf_op jit(solution)/shard_map/convert_element_type | solution.py:548
  1.9 0.0 copy-start
  1.9 0.0 copy-start.1
  1.9 0.0 copy-start.2
  1.9 0.0 copy-start.3
  1.9 1.0 %shard_map.100 = (bf16[144,128]{1,0:T(8,128)(2,1)S(1)}, bf16[512,128]{1,0:T(8,128)(2,1)S(1)}, f32[8,128]{1,0:T(8,128)S(1)}) custom-call(f32[64,8,256]{2,1,0:T(8,128)S(1)} %convert_element_type.10.feat_ref, bf16[64,256]{1,0:T(8,128)(2,1)S(1)} %bitcast.11, f32[8,128]{1,0:T(8,128)S(1)} %pad_maximum_fusion.8.live_in_ref), custom_call_target="tpu_custom_call" | custom-call | flops 1500000000 | bytes 561152 | tf_op jit(solution)/shard_map/pallas_call | solution.py:216
  2.9 4.1 %collective-permute-start = (bf16[144,128]{1,0:T(8,128)(2,1)S(1)}, bf16[144,128]{1,0:T(8,128)(2,1)S(1)}, u32[]{:S(2)}, u32[]{:S(2)}) collective-permute-start(bf16[144,128]{1,0:T(8,128)(2,1)S(1)} %get-tuple-element.43), channel_id=1, source_target_pairs={{0,8},{1,9},{2,10},{3,11},{4,12},{5,13},{6,14},{7,15},{8,0},{9,1},... | collective-permute-start | bytes 110600 | tf_op jit(solution)/shard_map/ppermute | solution.py:493
  7.0 0.1 pad_add_fusion.where_ref
  7.1 0.6 copy-done.5
  7.7 0.0 copy-done.6
  7.7 2.0 %shard_map.101 = (f32[8,128,128]{2,1,0:T(8,128)S(1)}, bf16[128,1024]{1,0:T(8,128)(2,1)S(1)}, bf16[2,640,128]{2,1,0:T(8,128)(2,1)S(1)}, bf16[2,128,128]{2,1,0:T(8,128)(2,1)S(1)}) custom-call(s32[3]{0:T(128)S(1)} %pad_add_fusion.where_ref, s32[128]{0:T(128)S(1)} %copy-done.6, s32[1,128]{1,0:T(1,128)S(1)} %bitcast.12, bf16[8,128,128]{2,1,0:T(8,128)(2,1)S(1)} %copy-done.1, ...), custom_call_target="tpu_custom_call" | custom-call | flops 1500000000 | bytes 935436 | tf_op jit(solution)/shard_map/pallas_call | solution.py:216
  9.8 1.6 %collective-permute-start.1 = (bf16[2,144,128]{2,1,0:T(8,128)(2,1)S(1)}, bf16[2,144,128]{2,1,0:T(8,128)(2,1)S(1)}, u32[]{:S(2)}, u32[]{:S(2)}) collective-permute-start(bf16[2,144,128]{2,1,0:T(8,128)(2,1)S(1)} %pad_maximum_fusion.7), channel_id=1, source_target_pairs={{0,4},{1,5},{2,6},{3,7},{4,0},{5,1},{6,2},{7,3},{8,12},{9,13},{10,... | collective-permute-start | bytes 221192 | tf_op jit(solution)/shard_map/ppermute | solution.py:493
  11.4 2.8 %collective-permute-done.1 = bf16[2,144,128]{2,1,0:T(8,128)(2,1)S(1)} collective-permute-done((bf16[2,144,128]{2,1,0:T(8,128)(2,1)S(1)}, bf16[2,144,128]{2,1,0:T(8,128)(2,1)S(1)}, u32[]{:S(2)}, u32[]{:S(2)}) %collective-permute-start.1) | collective-permute-done | bytes 73760 | tf_op jit(solution)/shard_map/ppermute | solution.py:493
  14.2 1.6 %collective-permute-start.2 = (bf16[4,144,128]{2,1,0:T(8,128)(2,1)S(1)}, bf16[4,144,128]{2,1,0:T(8,128)(2,1)S(1)}, u32[]{:S(2)}, u32[]{:S(2)}) collective-permute-start(bf16[4,144,128]{2,1,0:T(8,128)(2,1)S(1)} %pad_maximum_fusion), channel_id=1, source_target_pairs={{0,2},{1,3},{2,0},{3,1},{4,6},{5,7},{6,4},{7,5},{8,10},{9,11},{10,... | collective-permute-start | bytes 442376 | tf_op jit(solution)/shard_map/ppermute | solution.py:493
  15.8 3.6 %collective-permute-done.2 = bf16[4,144,128]{2,1,0:T(8,128)(2,1)S(1)} collective-permute-done((bf16[4,144,128]{2,1,0:T(8,128)(2,1)S(1)}, bf16[4,144,128]{2,1,0:T(8,128)(2,1)S(1)}, u32[]{:S(2)}, u32[]{:S(2)}) %collective-permute-start.2) | collective-permute-done | bytes 147488 | tf_op jit(solution)/shard_map/ppermute | solution.py:493
  19.5 0.1 collective-permute-start.3
  19.6 1.6 %collective-permute-done.3.other_ref = bf16[8,144,128]{2,1,0:T(8,128)(2,1)S(1)} collective-permute-done((bf16[8,144,128]{2,1,0:T(8,128)(2,1)S(1)}, bf16[8,144,128]{2,1,0:T(8,128)(2,1)S(1)}, u32[]{:S(2)}, u32[]{:S(2)}) %collective-permute-start.3) | collective-permute-done | bytes 294944 | tf_op jit(solution)/shard_map/ppermute | solution.py:519
  21.1 3.1 %shard_map.102 = (f32[8,128,128]{2,1,0:T(8,128)S(1)}, f32[8,128,128]{2,1,0:T(8,128)S(1)}, bf16[256,128]{1,0:T(8,128)(2,1)S(1)}, bf16[256,128]{1,0:T(8,128)(2,1)S...) custom-call(s32[3]{0:T(128)S(1)} %pad_add_fusion.where_ref, ...), custom_call_target="tpu_custom_call" | custom-call | flops 4000000000 | bytes 1840140 | tf_op jit(solution)/shard_map/pallas_call | solution.py:216
  24.3 0.2 collective-permute-start.7
  24.5 2.5 %collective-permute-start.4 = (bf16[512,128]{1,0:T(8,128)(2,1)S(1)}, bf16[512,128]{1,0:T(8,128)(2,1)S(1)}, u32[]{:S(2)}, u32[]{:S(2)}) collective-permute-start(bf16[512,128]{1,0:T(8,128)(2,1)S(1)} %get-tuple-element.54), channel_id=1, source_target_pairs={{0,6},{1,7},{2,4},{3,5},{4,2},{5,3},{6,0},{7,1},{8,14},{9,15},{10,... | collective-permute-start | bytes 393224 | tf_op jit(solution)/shard_map/ppermute | solution.py:493
  27.0 0.4 collective-permute-start.5
  27.5 0.5 collective-permute-start.6
  28.0 0.0 collective-permute-done.7
  28.0 4.4 %collective-permute-start.8 = (bf16[512,128]{1,0:T(8,128)(2,1)S(1)}, bf16[512,128]{1,0:T(8,128)(2,1)S(1)}, u32[]{:S(2)}, u32[]{:S(2)}) collective-permute-start(bf16[512,128]{1,0:T(8,128)(2,1)S(1)} %pad_maximum_fusion.1), channel_id=1, source_target_pairs={{0,14},{1,11},{2,12},{3,9},{4,10},{5,15},{6,8},{7,13},{8,6},{9,3},... | collective-permute-start | bytes 393224 | tf_op jit(solution)/shard_map/ppermute | solution.py:502
  32.4 0.5 collective-permute-start.9
  32.9 3.4 %collective-permute-done.5.near1 = bf16[512,128]{1,0:T(8,128)(2,1)S(1)} collective-permute-done((bf16[512,128]{1,0:T(8,128)(2,1)S(1)}, bf16[512,128]{1,0:T(8,128)(2,1)S(1)}, u32[]{:S(2)}, u32[]{:S(2)}) %collective-permute-start.5) | collective-permute-done | bytes 131104 | tf_op jit(solution)/shard_map/ppermute | solution.py:493
  36.4 0.0 collective-permute-done.6.near2
  36.4 2.5 %collective-permute-done.8.far0 = bf16[512,128]{1,0:T(8,128)(2,1)S(1)} collective-permute-done((bf16[512,128]{1,0:T(8,128)(2,1)S(1)}, bf16[512,128]{1,0:T(8,128)(2,1)S(1)}, u32[]{:S(2)}, u32[]{:S(2)}) %collective-permute-start.8) | collective-permute-done | bytes 131104 | tf_op jit(solution)/shard_map/ppermute | solution.py:502
  39.0 2.3 %collective-permute-done.9.far1 = bf16[512,128]{1,0:T(8,128)(2,1)S(1)} collective-permute-done((bf16[512,128]{1,0:T(8,128)(2,1)S(1)}, bf16[512,128]{1,0:T(8,128)(2,1)S(1)}, u32[]{:S(2)}, u32[]{:S(2)}) %collective-permute-start.9) | collective-permute-done | bytes 131104 | tf_op jit(solution)/shard_map/ppermute | solution.py:502
  41.3 1.0 %collective-permute-start.10 = (bf16[2048,128]{1,0:T(8,128)(2,1)S(1)}, bf16[2048,128]{1,0:T(8,128)(2,1)S(1)}, u32[]{:S(2)}, u32[]{:S(2)}) collective-permute-start(bf16[2048,128]{1,0:T(8,128)(2,1)S(1)} %constant_dynamic-update-slice_fusion.3), channel_id=1, source_target_pairs={{0,1},{1,0},{2,3},{3,2},{4,5},{5,4},{6,7},{7,6},{8,9},{9,8},{10,11... | collective-permute-start | bytes 1572872 | tf_op jit(solution)/shard_map/ppermute | solution.py:519
  42.3 1.5 %collective-permute-done.10.other_ref = bf16[2048,128]{1,0:T(8,128)(2,1)S(1)} collective-permute-done((bf16[2048,128]{1,0:T(8,128)(2,1)S(1)}, bf16[2048,128]{1,0:T(8,128)(2,1)S(1)}, u32[]{:S(2)}, u32[]{:S(2)}) %collective-permute-start.10) | collective-permute-done | bytes 524320 | tf_op jit(solution)/shard_map/ppermute | solution.py:519
  43.8 1.4 %shard_map.103 = (bf16[256,128]{1,0:T(8,128)(2,1)S(1)}, bf16[256,128]{1,0:T(8,128)(2,1)S(1)}, bf16[256,128]{1,0:T(8,128)(2,1)S(1)}, bf16[256,128]{1,0:T(8,128)(2,1)S(1)}) custom-call(s32[3]{0:T(128)S(1)} %pad_add_fusion.where_ref, bf16[512,128]{1,0:T(8,128)(2,1)S(1)} %collective-permute-done.4.near0, bf16[512,128]{1,0:T(8,128)(2,1)S(1)} %collective-permute-done.5.near1, ...), custom_call_target="tpu_custom_call" | custom-call | flops 1500000000 | bytes 1310732 | tf_op jit(solution)/shard_map/pallas_call | solution.py:216
  45.2 2.2 %collective-permute-start.11 = (bf16[256,128]{1,0:T(8,128)(2,1)S(1)}, bf16[256,128]{1,0:T(8,128)(2,1)S(1)}, u32[]{:S(2)}, u32[]{:S(2)}) collective-permute-start(bf16[256,128]{1,0:T(8,128)(2,1)S(1)} %get-tuple-element.61), channel_id=1, source_target_pairs={{0,6},{1,7},{2,4},{3,5},{4,2},{5,3},{6,0},{7,1},{8,14},{9,15},{10,... | collective-permute-start | bytes 196616 | tf_op jit(solution)/shard_map/ppermute | solution.py:493
  47.5 0.1 collective-permute-start.12
  47.6 1.4 %collective-permute-start.13 = (bf16[256,128]{1,0:T(8,128)(2,1)S(1)}, bf16[256,128]{1,0:T(8,128)(2,1)S(1)}, u32[]{:S(2)}, u32[]{:S(2)}) collective-permute-start(bf16[256,128]{1,0:T(8,128)(2,1)S(1)} %get-tuple-element.63), channel_id=1, source_target_pairs={{0,2},{1,3},{2,0},{3,1},{4,6},{5,7},{6,4},{7,5},{8,10},{9,11},{10,... | collective-permute-start | bytes 196616 | tf_op jit(solution)/shard_map/ppermute | solution.py:493
  49.0 1.7 %collective-permute-done.11.in0 = bf16[256,128]{1,0:T(8,128)(2,1)S(1)} collective-permute-done((bf16[256,128]{1,0:T(8,128)(2,1)S(1)}, bf16[256,128]{1,0:T(8,128)(2,1)S(1)}, u32[]{:S(2)}, u32[]{:S(2)}) %collective-permute-start.11) | collective-permute-done | bytes 65568 | tf_op jit(solution)/shard_map/ppermute | solution.py:493
  50.6 1.1 %collective-permute-done.12.in1 = bf16[256,128]{1,0:T(8,128)(2,1)S(1)} collective-permute-done((bf16[256,128]{1,0:T(8,128)(2,1)S(1)}, bf16[256,128]{1,0:T(8,128)(2,1)S(1)}, u32[]{:S(2)}, u32[]{:S(2)}) %collective-permute-start.12) | collective-permute-done | bytes 65568 | tf_op jit(solution)/shard_map/ppermute | solution.py:493
  51.7 0.3 collective-permute-done.13.in2
  52.0 2.2 %shard_map.104 = (f32[8,128,128]{2,1,0:T(8,128)S(1)}, f32[8,128,128]{2,1,0:T(8,128)S(1)}, bf16[256,128]{1,0:T(8,128)(2,1)S(1)}, bf16[256,128]{1,0:T(8,128)(2,1)S...) custom-call(s32[3]{0:T(128)S(1)} %pad_add_fusion.where_ref, ...), custom_call_target="tpu_custom_call" | custom-call | flops 1500000000 | bytes 1704972 | tf_op jit(solution)/shard_map/pallas_call | solution.py:216
  54.2 0.1 collective-permute-start.14
  54.3 1.5 %collective-permute-done.14 = bf16[1024,128]{1,0:T(8,128)(2,1)S(1)} collective-permute-done((bf16[1024,128]{1,0:T(8,128)(2,1)S(1)}, bf16[1024,128]{1,0:T(8,128)(2,1)S(1)}, u32[]{:S(2)}, u32[]{:S(2)}) %collective-permute-start.14) | collective-permute-done | bytes 262176 | tf_op jit(solution)/shard_map/ppermute | solution.py:519
  55.9 4.7 %collective-permute-start.15 = (bf16[512,128]{1,0:T(8,128)(2,1)S(1)}, bf16[512,128]{1,0:T(8,128)(2,1)S(1)}, u32[]{:S(2)}, u32[]{:S(2)}) collective-permute-start(bf16[512,128]{1,0:T(8,128)(2,1)S(1)} %pad_maximum_fusion.3), channel_id=1, source_target_pairs={{0,14},{1,7},{2,12},{3,5},{4,10},{5,3},{6,8},{7,1},{8,6},{9,15},{1... | collective-permute-start | bytes 393224 | tf_op jit(solution)/shard_map/ppermute | solution.py:502
  60.6 0.5 collective-permute-start.16
  61.0 0.3 collective-permute-start.17
  61.4 0.7 collective-permute-start.18
  62.1 2.5 %collective-permute-done.15.came0 = bf16[512,128]{1,0:T(8,128)(2,1)S(1)} collective-permute-done((bf16[512,128]{1,0:T(8,128)(2,1)S(1)}, bf16[512,128]{1,0:T(8,128)(2,1)S(1)}, u32[]{:S(2)}, u32[]{:S(2)}) %collective-permute-start.15) | collective-permute-done | bytes 131104 | tf_op jit(solution)/shard_map/ppermute | solution.py:502
  64.6 2.5 %collective-permute-done.16.came1 = bf16[512,128]{1,0:T(8,128)(2,1)S(1)} collective-permute-done((bf16[512,128]{1,0:T(8,128)(2,1)S(1)}, bf16[512,128]{1,0:T(8,128)(2,1)S(1)}, u32[]{:S(2)}, u32[]{:S(2)}) %collective-permute-start.16) | collective-permute-done | bytes 131104 | tf_op jit(solution)/shard_map/ppermute | solution.py:502
  67.0 5.7 %collective-permute-done.17.came2 = bf16[512,128]{1,0:T(8,128)(2,1)S(1)} collective-permute-done((bf16[512,128]{1,0:T(8,128)(2,1)S(1)}, bf16[512,128]{1,0:T(8,128)(2,1)S(1)}, u32[]{:S(2)}, u32[]{:S(2)}) %collective-permute-start.17) | collective-permute-done | bytes 131104 | tf_op jit(solution)/shard_map/ppermute | solution.py:502
  72.7 1.4 %shard_map.105 = (f32[4,256,128]{2,1,0:T(8,128)S(1)}, f32[4,256,128]{2,1,0:T(8,128)S(1)}) custom-call(s32[3]{0:T(128)S(1)} %pad_add_fusion.where_ref, bf16[512,128]{1,0:T(8,128)(2,1)S(1)} %collective-permute-done.15.came0, bf16[512,128]{1,0:T(8,128)(2,1)S(1)} %collective-permute-done.16.came1, bf16[512,128]{1,0:T(8,128)(2,1)S(1)} %collective-permute-done.17.came2, ...), custom_call_target="tpu_custom_call" | custom-call | flops 1500000000 | bytes 524300 | tf_op jit(solution)/shard_map/pallas_call | solution.py:216
  74.1 0.2 collective-permute-start.19
  74.3 1.8 %collective-permute-done.19.got_ref = f32[4,256,128]{2,1,0:T(8,128)S(1)} collective-permute-done((f32[4,256,128]{2,1,0:T(8,128)S(1)}, f32[4,256,128]{2,1,0:T(8,128)S(1)}, u32[]{:S(2)}, u32[]{:S(2)}) %collective-permute-start.19) | collective-permute-done | bytes 524320 | tf_op jit(solution)/shard_map/ppermute | solution.py:519
  76.1 4.0 %collective-permute-start.20 = (bf16[256,128]{1,0:T(8,128)(2,1)S(1)}, bf16[256,128]{1,0:T(8,128)(2,1)S(1)}, u32[]{:S(2)}, u32[]{:S(2)}) collective-permute-start(bf16[256,128]{1,0:T(8,128)(2,1)S(1)} %get-tuple-element.75), channel_id=1, source_target_pairs={{0,14},{1,7},{2,12},{3,5},{4,10},{5,3},{6,8},{7,1},{8,6},{9,15},{1... | collective-permute-start | bytes 196616 | tf_op jit(solution)/shard_map/ppermute | solution.py:502
  80.2 1.3 %collective-permute-start.22 = (bf16[256,128]{1,0:T(8,128)(2,1)S(1)}, bf16[256,128]{1,0:T(8,128)(2,1)S(1)}, u32[]{:S(2)}, u32[]{:S(2)}) collective-permute-start(bf16[256,128]{1,0:T(8,128)(2,1)S(1)} %get-tuple-element.77), channel_id=1, source_target_pairs={{0,10},{1,3},{2,8},{3,1},{4,14},{5,7},{6,12},{7,5},{8,2},{9,11},{1... | collective-permute-start | bytes 196616 | tf_op jit(solution)/shard_map/ppermute | solution.py:502
  81.5 0.7 collective-permute-start.23
  82.2 1.3 %collective-permute-done.20.refs_0_.came0 = bf16[256,128]{1,0:T(8,128)(2,1)S(1)} collective-permute-done((bf16[256,128]{1,0:T(8,128)(2,1)S(1)}, bf16[256,128]{1,0:T(8,128)(2,1)S(1)}, u32[]{:S(2)}, u32[]{:S(2)}) %collective-permute-start.20) | collective-permute-done | bytes 65568 | tf_op jit(solution)/shard_map/ppermute | solution.py:502
  83.5 1.0 %collective-permute-done.21.refs_1_.came1 = bf16[256,128]{1,0:T(8,128)(2,1)S(1)} collective-permute-done((bf16[256,128]{1,0:T(8,128)(2,1)S(1)}, bf16[256,128]{1,0:T(8,128)(2,1)S(1)}, u32[]{:S(2)}, u32[]{:S(2)}) %collective-permute-start.21) | collective-permute-done | bytes 65568 | tf_op jit(solution)/shard_map/ppermute | solution.py:502
  84.4 2.0 %collective-permute-done.22.refs_2_.came2 = bf16[256,128]{1,0:T(8,128)(2,1)S(1)} collective-permute-done((bf16[256,128]{1,0:T(8,128)(2,1)S(1)}, bf16[256,128]{1,0:T(8,128)(2,1)S(1)}, u32[]{:S(2)}, u32[]{:S(2)}) %collective-permute-start.22) | collective-permute-done | bytes 65568 | tf_op jit(solution)/shard_map/ppermute | solution.py:502
  86.4 1.3 %collective-permute-start.24 = (bf16[512,128]{1,0:T(8,128)(2,1)S(1)}, bf16[512,128]{1,0:T(8,128)(2,1)S(1)}, u32[]{:S(2)}, u32[]{:S(2)}) collective-permute-start(bf16[512,128]{1,0:T(8,128)(2,1)S(1)} %shard_map.107), channel_id=1, source_target_pairs={{0,1},{1,0},{2,3},{3,2},{4,5},{5,4},{6,7},{7,6},{8,9},{9,8},{10,11... | collective-permute-start | bytes 393224 | tf_op jit(solution)/shard_map/ppermute | solution.py:519
  87.8 1.0 %collective-permute-done.24.other_ref = bf16[512,128]{1,0:T(8,128)(2,1)S(1)} collective-permute-done((bf16[512,128]{1,0:T(8,128)(2,1)S(1)}, bf16[512,128]{1,0:T(8,128)(2,1)S(1)}, u32[]{:S(2)}, u32[]{:S(2)}) %collective-permute-start.24) | collective-permute-done | bytes 131104 | tf_op jit(solution)/shard_map/ppermute | solution.py:519
  88.7 2.2 %shard_map.108 = bf16[8,128,128]{2,1,0:T(8,128)(2,1)} custom-call(s32[3]{0:T(128)S(1)} %pad_add_fusion.where_ref, bf16[256,128]{1,0:T(8,128)(2,1)S(1)} %collective-permute-done.20.refs_0_.came0, bf16[256,128]{1,0:T(8,128)(2,1)S(1)} %collective-permute-done.21.refs_1_.came1, bf16[256,128]{1,0:T(8,128)(2,1)S(1)} %collective-permute-done.22.refs_2_.came2, ...), custom_call_target="tpu_custom_call" | custom-call | flops 1500000000 | bytes 1507340 | tf_op jit(solution)/shard_map/pallas_call | solution.py:216
  (37 shorter events, 0.3 us)
Async XLA Ops:
  0.0 0.7 copy-start.7
  0.0 0.7 copy-start.8
  0.9 1.0 %copy-start.4 = (bf16[256,64]{0,1:T(8,128)(2,1)S(1)}, bf16[256,64]{0,1:T(8,128)(2,1)}, u32[]{:S(2)}) copy-start(bf16[256,64]{0,1:T(8,128)(2,1)} %param.16) | copy-start | bytes 98308
  1.9 5.2 %copy-start = (bf16[2,128,640]{2,1,0:T(8,128)(2,1)S(1)}, bf16[2,128,640]{2,1,0:T(8,128)(2,1)}, u32[]{:S(2)}) copy-start(bf16[2,128,640]{2,1,0:T(8,128)(2,1)} %proj_ref.1) | copy-start | bytes 983044
  1.9 5.2 %copy-start.1 = (bf16[8,128,128]{2,1,0:T(8,128)(2,1)S(1)}, bf16[8,128,128]{2,1,0:T(8,128)(2,1)}, u32[]{:S(2)}) copy-start(bf16[8,128,128]{2,1,0:T(8,128)(2,1)} %pair_ref.1) | copy-start | bytes 786436
  1.9 5.2 %copy-start.2 = (bf16[1024,128]{1,0:T(8,128)(2,1)S(1)}, bf16[1024,128]{1,0:T(8,128)(2,1)}, u32[]{:S(2)}) copy-start(bf16[1024,128]{1,0:T(8,128)(2,1)} %outer_ref.1) | copy-start | bytes 786436
  1.9 5.2 %copy-start.3 = (bf16[2,128,128]{2,1,0:T(8,128)(2,1)S(1)}, bf16[2,128,128]{2,1,0:T(8,128)(2,1)}, u32[]{:S(2)}) copy-start(bf16[2,128,128]{2,1,0:T(8,128)(2,1)} %out_ref.1) | copy-start | bytes 196612
  2.9 6.9 %collective-permute-start = (bf16[144,128]{1,0:T(8,128)(2,1)S(1)}, bf16[144,128]{1,0:T(8,128)(2,1)S(1)}, u32[]{:S(2)}, u32[]{:S(2)}) collective-permute-start(bf16[144,128]{1,0:T(8,128)(2,1)S(1)} %get-tuple-element.43), channel_id=1, source_target_pairs={{0,8},{1,9},{2,10},{3,11},{4,12},{5,13},{6,14},{7,15},{8,0},{9,1},... | collective-permute-start | bytes 110600 | tf_op jit(solution)/shard_map/ppermute | solution.py:493
  7.0 0.7 copy-start.5
  7.1 0.7 copy-start.6
  9.8 4.4 %collective-permute-start.1 = (bf16[2,144,128]{2,1,0:T(8,128)(2,1)S(1)}, bf16[2,144,128]{2,1,0:T(8,128)(2,1)S(1)}, u32[]{:S(2)}, u32[]{:S(2)}) collective-permute-start(bf16[2,144,128]{2,1,0:T(8,128)(2,1)S(1)} %pad_maximum_fusion.7), channel_id=1, source_target_pairs={{0,4},{1,5},{2,6},{3,7},{4,0},{5,1},{6,2},{7,3},{8,12},{9,13},{10,... | collective-permute-start | bytes 221192 | tf_op jit(solution)/shard_map/ppermute | solution.py:493
  14.2 5.2 %collective-permute-start.2 = (bf16[4,144,128]{2,1,0:T(8,128)(2,1)S(1)}, bf16[4,144,128]{2,1,0:T(8,128)(2,1)S(1)}, u32[]{:S(2)}, u32[]{:S(2)}) collective-permute-start(bf16[4,144,128]{2,1,0:T(8,128)(2,1)S(1)} %pad_maximum_fusion), channel_id=1, source_target_pairs={{0,2},{1,3},{2,0},{3,1},{4,6},{5,7},{6,4},{7,5},{8,10},{9,11},{10,... | collective-permute-start | bytes 442376 | tf_op jit(solution)/shard_map/ppermute | solution.py:493
  19.5 1.6 %collective-permute-start.3 = (bf16[8,144,128]{2,1,0:T(8,128)(2,1)S(1)}, bf16[8,144,128]{2,1,0:T(8,128)(2,1)S(1)}, u32[]{:S(2)}, u32[]{:S(2)}) collective-permute-start(bf16[8,144,128]{2,1,0:T(8,128)(2,1)S(1)} %constant_dynamic-update-slice_fusion.own_ref), channel_id=1, source_target_pairs={{0,1},{1,0},{2,3},{3,2},{4,5},{5,4},{6,7},{7,6},{8,9},{9,8},{10,11... | collective-permute-start | bytes 884744 | tf_op jit(solution)/shard_map/ppermute | solution.py:519
  24.3 3.7 %collective-permute-start.7 = (bf16[512,128]{1,0:T(8,128)(2,1)S(1)}, bf16[512,128]{1,0:T(8,128)(2,1)S(1)}, u32[]{:S(2)}, u32[]{:S(2)}) collective-permute-start(bf16[512,128]{1,0:T(8,128)(2,1)S(1)} %get-tuple-element.59), channel_id=1, source_target_pairs={{0,1},{1,0},{2,3},{3,2},{4,5},{5,4},{6,7},{7,6},{8,9},{9,8},{10,11... | collective-permute-start | bytes 393224 | tf_op jit(solution)/shard_map/ppermute | solution.py:519
  24.5 8.4 %collective-permute-start.4 = (bf16[512,128]{1,0:T(8,128)(2,1)S(1)}, bf16[512,128]{1,0:T(8,128)(2,1)S(1)}, u32[]{:S(2)}, u32[]{:S(2)}) collective-permute-start(bf16[512,128]{1,0:T(8,128)(2,1)S(1)} %get-tuple-element.54), channel_id=1, source_target_pairs={{0,6},{1,7},{2,4},{3,5},{4,2},{5,3},{6,0},{7,1},{8,14},{9,15},{10,... | collective-permute-start | bytes 393224 | tf_op jit(solution)/shard_map/ppermute | solution.py:493
  27.0 9.3 %collective-permute-start.5 = (bf16[512,128]{1,0:T(8,128)(2,1)S(1)}, bf16[512,128]{1,0:T(8,128)(2,1)S(1)}, u32[]{:S(2)}, u32[]{:S(2)}) collective-permute-start(bf16[512,128]{1,0:T(8,128)(2,1)S(1)} %get-tuple-element.55), channel_id=1, source_target_pairs={{0,4},{1,5},{2,6},{3,7},{4,0},{5,1},{6,2},{7,3},{8,12},{9,13},{10,... | collective-permute-start | bytes 393224 | tf_op jit(solution)/shard_map/ppermute | solution.py:493
  27.5 8.9 %collective-permute-start.6 = (bf16[512,128]{1,0:T(8,128)(2,1)S(1)}, bf16[512,128]{1,0:T(8,128)(2,1)S(1)}, u32[]{:S(2)}, u32[]{:S(2)}) collective-permute-start(bf16[512,128]{1,0:T(8,128)(2,1)S(1)} %get-tuple-element.56), channel_id=1, source_target_pairs={{0,2},{1,3},{2,0},{3,1},{4,6},{5,7},{6,4},{7,5},{8,10},{9,11},{10,... | collective-permute-start | bytes 393224 | tf_op jit(solution)/shard_map/ppermute | solution.py:493
  28.0 10.9 %collective-permute-start.8 = (bf16[512,128]{1,0:T(8,128)(2,1)S(1)}, bf16[512,128]{1,0:T(8,128)(2,1)S(1)}, u32[]{:S(2)}, u32[]{:S(2)}) collective-permute-start(bf16[512,128]{1,0:T(8,128)(2,1)S(1)} %pad_maximum_fusion.1), channel_id=1, source_target_pairs={{0,14},{1,11},{2,12},{3,9},{4,10},{5,15},{6,8},{7,13},{8,6},{9,3},... | collective-permute-start | bytes 393224 | tf_op jit(solution)/shard_map/ppermute | solution.py:502
  32.4 8.9 %collective-permute-start.9 = (bf16[512,128]{1,0:T(8,128)(2,1)S(1)}, bf16[512,128]{1,0:T(8,128)(2,1)S(1)}, u32[]{:S(2)}, u32[]{:S(2)}) collective-permute-start(bf16[512,128]{1,0:T(8,128)(2,1)S(1)} %pad_maximum_fusion.2), channel_id=1, source_target_pairs={{0,12},{1,9},{2,14},{3,11},{4,8},{5,13},{6,10},{7,15},{8,4},{9,1},... | collective-permute-start | bytes 393224 | tf_op jit(solution)/shard_map/ppermute | solution.py:502
  41.3 2.5 %collective-permute-start.10 = (bf16[2048,128]{1,0:T(8,128)(2,1)S(1)}, bf16[2048,128]{1,0:T(8,128)(2,1)S(1)}, u32[]{:S(2)}, u32[]{:S(2)}) collective-permute-start(bf16[2048,128]{1,0:T(8,128)(2,1)S(1)} %constant_dynamic-update-slice_fusion.3), channel_id=1, source_target_pairs={{0,1},{1,0},{2,3},{3,2},{4,5},{5,4},{6,7},{7,6},{8,9},{9,8},{10,11... | collective-permute-start | bytes 1572872 | tf_op jit(solution)/shard_map/ppermute | solution.py:519
  45.2 5.4 %collective-permute-start.11 = (bf16[256,128]{1,0:T(8,128)(2,1)S(1)}, bf16[256,128]{1,0:T(8,128)(2,1)S(1)}, u32[]{:S(2)}, u32[]{:S(2)}) collective-permute-start(bf16[256,128]{1,0:T(8,128)(2,1)S(1)} %get-tuple-element.61), channel_id=1, source_target_pairs={{0,6},{1,7},{2,4},{3,5},{4,2},{5,3},{6,0},{7,1},{8,14},{9,15},{10,... | collective-permute-start | bytes 196616 | tf_op jit(solution)/shard_map/ppermute | solution.py:493
  47.5 4.3 %collective-permute-start.12 = (bf16[256,128]{1,0:T(8,128)(2,1)S(1)}, bf16[256,128]{1,0:T(8,128)(2,1)S(1)}, u32[]{:S(2)}, u32[]{:S(2)}) collective-permute-start(bf16[256,128]{1,0:T(8,128)(2,1)S(1)} %get-tuple-element.62), channel_id=1, source_target_pairs={{0,4},{1,5},{2,6},{3,7},{4,0},{5,1},{6,2},{7,3},{8,12},{9,13},{10,... | collective-permute-start | bytes 196616 | tf_op jit(solution)/shard_map/ppermute | solution.py:493
  47.6 4.4 %collective-permute-start.13 = (bf16[256,128]{1,0:T(8,128)(2,1)S(1)}, bf16[256,128]{1,0:T(8,128)(2,1)S(1)}, u32[]{:S(2)}, u32[]{:S(2)}) collective-permute-start(bf16[256,128]{1,0:T(8,128)(2,1)S(1)} %get-tuple-element.63), channel_id=1, source_target_pairs={{0,2},{1,3},{2,0},{3,1},{4,6},{5,7},{6,4},{7,5},{8,10},{9,11},{10,... | collective-permute-start | bytes 196616 | tf_op jit(solution)/shard_map/ppermute | solution.py:493
  54.2 1.6 %collective-permute-start.14 = (bf16[1024,128]{1,0:T(8,128)(2,1)S(1)}, bf16[1024,128]{1,0:T(8,128)(2,1)S(1)}, u32[]{:S(2)}, u32[]{:S(2)}) collective-permute-start(bf16[1024,128]{1,0:T(8,128)(2,1)S(1)} %get-tuple-element.69), channel_id=1, source_target_pairs={{0,1},{1,0},{2,3},{3,2},{4,5},{5,4},{6,7},{7,6},{8,9},{9,8},{10,11... | collective-permute-start | bytes 786440 | tf_op jit(solution)/shard_map/ppermute | solution.py:519
  55.9 8.7 %collective-permute-start.15 = (bf16[512,128]{1,0:T(8,128)(2,1)S(1)}, bf16[512,128]{1,0:T(8,128)(2,1)S(1)}, u32[]{:S(2)}, u32[]{:S(2)}) collective-permute-start(bf16[512,128]{1,0:T(8,128)(2,1)S(1)} %pad_maximum_fusion.3), channel_id=1, source_target_pairs={{0,14},{1,7},{2,12},{3,5},{4,10},{5,3},{6,8},{7,1},{8,6},{9,15},{1... | collective-permute-start | bytes 393224 | tf_op jit(solution)/shard_map/ppermute | solution.py:502
  60.6 6.5 %collective-permute-start.16 = (bf16[512,128]{1,0:T(8,128)(2,1)S(1)}, bf16[512,128]{1,0:T(8,128)(2,1)S(1)}, u32[]{:S(2)}, u32[]{:S(2)}) collective-permute-start(bf16[512,128]{1,0:T(8,128)(2,1)S(1)} %pad_maximum_fusion.4), channel_id=1, source_target_pairs={{0,4},{1,13},{2,6},{3,15},{4,0},{5,9},{6,2},{7,11},{8,12},{9,5},{1... | collective-permute-start | bytes 393224 | tf_op jit(solution)/shard_map/ppermute | solution.py:502
  61.0 11.7 %collective-permute-start.17 = (bf16[512,128]{1,0:T(8,128)(2,1)S(1)}, bf16[512,128]{1,0:T(8,128)(2,1)S(1)}, u32[]{:S(2)}, u32[]{:S(2)}) collective-permute-start(bf16[512,128]{1,0:T(8,128)(2,1)S(1)} %pad_maximum_fusion.5), channel_id=1, source_target_pairs={{0,10},{1,3},{2,8},{3,1},{4,14},{5,7},{6,12},{7,5},{8,2},{9,11},{1... | collective-permute-start | bytes 393224 | tf_op jit(solution)/shard_map/ppermute | solution.py:502
  61.4 11.3 %collective-permute-start.18 = (bf16[512,128]{1,0:T(8,128)(2,1)S(1)}, bf16[512,128]{1,0:T(8,128)(2,1)S(1)}, u32[]{:S(2)}, u32[]{:S(2)}) collective-permute-start(bf16[512,128]{1,0:T(8,128)(2,1)S(1)} %pad_maximum_fusion.6), channel_id=1, source_target_pairs={{0,0},{1,9},{2,2},{3,11},{4,4},{5,13},{6,6},{7,15},{8,8},{9,1},{10... | collective-permute-start | bytes 393224 | tf_op jit(solution)/shard_map/ppermute | solution.py:502
  74.1 2.0 %collective-permute-start.19 = (f32[4,256,128]{2,1,0:T(8,128)S(1)}, f32[4,256,128]{2,1,0:T(8,128)S(1)}, u32[]{:S(2)}, u32[]{:S(2)}) collective-permute-start(f32[4,256,128]{2,1,0:T(8,128)S(1)} %get-tuple-element.74), channel_id=1, source_target_pairs={{0,1},{1,0},{2,3},{3,2},{4,5},{5,4},{6,7},{7,6},{8,9},{9,8},{10,11... | collective-permute-start | bytes 1572872 | tf_op jit(solution)/shard_map/ppermute | solution.py:519
  76.1 7.3 %collective-permute-start.20 = (bf16[256,128]{1,0:T(8,128)(2,1)S(1)}, bf16[256,128]{1,0:T(8,128)(2,1)S(1)}, u32[]{:S(2)}, u32[]{:S(2)}) collective-permute-start(bf16[256,128]{1,0:T(8,128)(2,1)S(1)} %get-tuple-element.75), channel_id=1, source_target_pairs={{0,14},{1,7},{2,12},{3,5},{4,10},{5,3},{6,8},{7,1},{8,6},{9,15},{1... | collective-permute-start | bytes 196616 | tf_op jit(solution)/shard_map/ppermute | solution.py:502
  80.2 4.3 %collective-permute-start.21 = (bf16[256,128]{1,0:T(8,128)(2,1)S(1)}, bf16[256,128]{1,0:T(8,128)(2,1)S(1)}, u32[]{:S(2)}, u32[]{:S(2)}) collective-permute-start(bf16[256,128]{1,0:T(8,128)(2,1)S(1)} %get-tuple-element.76), channel_id=1, source_target_pairs={{0,4},{1,13},{2,6},{3,15},{4,0},{5,9},{6,2},{7,11},{8,12},{9,5},{1... | collective-permute-start | bytes 196616 | tf_op jit(solution)/shard_map/ppermute | solution.py:502
  80.2 6.2 %collective-permute-start.22 = (bf16[256,128]{1,0:T(8,128)(2,1)S(1)}, bf16[256,128]{1,0:T(8,128)(2,1)S(1)}, u32[]{:S(2)}, u32[]{:S(2)}) collective-permute-start(bf16[256,128]{1,0:T(8,128)(2,1)S(1)} %get-tuple-element.77), channel_id=1, source_target_pairs={{0,10},{1,3},{2,8},{3,1},{4,14},{5,7},{6,12},{7,5},{8,2},{9,11},{1... | collective-permute-start | bytes 196616 | tf_op jit(solution)/shard_map/ppermute | solution.py:502
  81.5 4.9 %collective-permute-start.23 = (bf16[256,128]{1,0:T(8,128)(2,1)S(1)}, bf16[256,128]{1,0:T(8,128)(2,1)S(1)}, u32[]{:S(2)}, u32[]{:S(2)}) collective-permute-start(bf16[256,128]{1,0:T(8,128)(2,1)S(1)} %get-tuple-element.78), channel_id=1, source_target_pairs={{0,0},{1,9},{2,2},{3,11},{4,4},{5,13},{6,6},{7,15},{8,8},{9,1},{10... | collective-permute-start | bytes 196616 | tf_op jit(solution)/shard_map/ppermute | solution.py:502
  86.4 2.3 %collective-permute-start.24 = (bf16[512,128]{1,0:T(8,128)(2,1)S(1)}, bf16[512,128]{1,0:T(8,128)(2,1)S(1)}, u32[]{:S(2)}, u32[]{:S(2)}) collective-permute-start(bf16[512,128]{1,0:T(8,128)(2,1)S(1)} %shard_map.107), channel_id=1, source_target_pairs={{0,1},{1,0},{2,3},{3,2},{4,5},{5,4},{6,7},{7,6},{8,9},{9,8},{10,11... | collective-permute-start | bytes 393224 | tf_op jit(solution)/shard_map/ppermute | solution.py:519

commit v10 on v9

--- a/solution.py
+++ b/solution.py
@@ -225,8 +225,10 @@
 
 
 VMEM_LIMIT = 20 * 1024 * 1024
-SPLIT = ((7, 3), (2, 6), (5, 1), (0, 4))
-FAR_SPLIT = ((7, 5), (6, 4))
+SPLIT = ((7, 5), (6, 4), (3, 2), (1, 0))
+FAR_SPLIT = SPLIT[:2]
+SMALL_SPLIT = ((7, 3), (2, 6), (5, 1), (0, 4))
+SMALL_NEAR = ((3, 1), (1, 2), (2, 3), (0, 0))
 OPS = len(SPLIT)
 NEAR = 4
 NEAR_STEPS = (3, 2, 1, 0)
@@ -394,8 +396,9 @@
         left = flat(lefts[:, c]).astype(BF16)
         right = flat(rights[:, c]).astype(BF16)
         mixed[:, c, :] = nt(left, right)
-    for step, out in enumerate((out0, out1, out2, out3)):
-        out[...] = flat(mixed[step * rows : (step + 1) * rows]).astype(BF16)
+    for op, out in enumerate((out0, out1, out2, out3)):
+        first = pl.multiple_of(partner_chip(0, core, op, SMALL_NEAR) * rows, rows)
+        out[...] = flat(mixed[pl.ds(first, rows)]).astype(BF16)
 
 
 def pick_kernel(*refs):
@@ -421,8 +424,8 @@
     rows, width, cols = stream_ref.shape
     chip, core = where_ref[1], where_ref[2]
     size = width // NEAR
-    for step, block in zip(NEAR_STEPS, (in0, in1, in2, in3)):
-        came[:, (chip ^ step) & (NEAR - 1)] = block[...].astype(F32).reshape(rows, size, cols)
+    for op, block in enumerate((in0, in1, in2, in3)):
+        came[:, partner_chip(chip, core, op, SMALL_NEAR) & (NEAR - 1)] = block[...].astype(F32).reshape(rows, size, cols)
     present = present_ref[...].astype(F32)
     for row in range(0, rows, 2):
         streams = update(came, row, stream_ref, gate_ref, out_weight_ref[0])
@@ -457,9 +460,9 @@
         partial[:, c, :] = tn(left, right)
     for op in range(OPS):
         for half in range(2):
-            to = (partner_chip(chip, core, op) * 2 + (core ^ half)) * rows
+            to = (partner_chip(chip, core, op, SMALL_SPLIT) * 2 + (core ^ half)) * rows
             mine_ref[op, half * block : (half + 1) * block] = flat(partial[pl.ds(to, rows)])
-            to = (partner_chip(chip, 1 - core, op) * 2 + ((1 - core) ^ half)) * rows
+            to = (partner_chip(chip, 1 - core, op, SMALL_SPLIT) * 2 + ((1 - core) ^ half)) * rows
             theirs_ref[op, half * block : (half + 1) * block] = flat(partial[pl.ds(to, rows)])
 
 
@@ -476,9 +479,9 @@
     size = width // (2 * OPS)
     block = size * rows
     for op, mine in enumerate((came0, came1, came2, came3)):
-        came[:, partner_chip(chip, core, op)] = mine[0:block].astype(F32).reshape(rows, size, cols)
+        came[:, partner_chip(chip, core, op, SMALL_SPLIT)] = mine[0:block].astype(F32).reshape(rows, size, cols)
         theirs = other_ref[op * block : (op + 1) * block]
-        came[:, partner_chip(chip, 1 - core, op)] = theirs.astype(F32).reshape(rows, size, cols)
+        came[:, partner_chip(chip, 1 - core, op, SMALL_SPLIT)] = theirs.astype(F32).reshape(rows, size, cols)
     for row in range(0, rows, 2):
         for at, stream in enumerate(update(came, row, stream_ref, gate_ref, out_weight_ref[1])):
             out_ref[row + at] = flip_out(stream)
@@ -599,7 +602,7 @@
             ((NEAR * rows, width // NEAR, cols), F32),
         ],
     )
-    mixed = exchange(mixed, NEAR_STEPS)
+    mixed = split_exchange(mixed[: NEAR - 1], SMALL_NEAR) + [mixed[NEAR - 1]]
     made = run(
         between_kernel,
         [((rows, width, cols), F32)] * 2 + [((2 * all_, cols), BF16)] * OPS + [((2 * OPS * all_, cols), BF16)],
@@ -625,7 +628,7 @@
         ],
     )
     mixed = run(sum_kernel, [((2 * all_, cols), BF16)] * OPS, mine, core_permute(theirs))
-    mixed = split_exchange(mixed)
+    mixed = split_exchange(mixed, SMALL_SPLIT)
     other = core_permute(run(pick_kernel, [((OPS * all_, cols), BF16)], *mixed)[0])
     return run(
         final_kernel,

time: 91.2 us -> 90.4 us (level)
  waiting for transfers between devices: 40 us -> 36.3 us
  starting transfers between devices: 34.4 us -> 37.3 us
    ppermute x10 -> x13, starting transfers between devices: 17 us -> 22 us  [split_permute(): lax.ppermute(block, 'wide', [(w, w ^ 2 * steps[w % 2]) for w in range(cou...]
    ppermute x9 -> x6, starting transfers between devices: 14.5 us -> 10.8 us  [chip_permute(): lax.ppermute(block, 'wide', [(w, w ^ 2 * step) for w in range(count)])]
    ppermute x9 -> x6, waiting for transfers between devices: 12.9 us -> 9.83 us  [chip_permute(): lax.ppermute(block, 'wide', [(w, w ^ 2 * step) for w in range(count)])]
    ppermute x6, starting transfers between devices: 2.84 us -> 4.42 us  [core_permute(): return lax.ppermute(block, 'wide', [(w, w ^ 1) for w in range(count)])]
    ppermute x10 -> x13, waiting for transfers between devices: 19.7 us -> 19.3 us  [split_permute(): lax.ppermute(block, 'wide', [(w, w ^ 2 * steps[w % 2]) for w in range(cou...]
where the time goes in v10:
time: 90.4 us; the launch traced here: 90.1 us
  starting transfers between devices  37.3 us (41%)
  waiting for transfers between devices  36.3 us (40%)
  Pallas kernels  13.5 us (15%)
  local copies, waits for them, and re-layouts  1.47 us (2%)
  other arithmetic  1.38 us (2%)
    ppermute x13, starting transfers between devices, split_permute(): lax.ppermute(block, 'wide', [(w, w ^ 2 * steps[w % 2]) for w in range(cou...  22 us
    ppermute x13, waiting for transfers between devices, split_permute(): lax.ppermute(block, 'wide', [(w, w ^ 2 * steps[w % 2]) for w in range(cou...  19.3 us
    pallas_call x9, Pallas kernels, run(): pl.pallas_call(kernel, out_shape=[jax.ShapeDtypeStruct(shape, kind) for s...  13.5 us
    ppermute x6, starting transfers between devices, chip_permute(): lax.ppermute(block, 'wide', [(w, w ^ 2 * step) for w in range(count)])  10.8 us
    ppermute x6, waiting for transfers between devices, chip_permute(): lax.ppermute(block, 'wide', [(w, w ^ 2 * step) for w in range(count)])  9.83 us
    ppermute x6, waiting for transfers between devices, core_permute(): return lax.ppermute(block, 'wide', [(w, w ^ 1) for w in range(count)])  7.15 us
    ppermute x6, starting transfers between devices, core_permute(): return lax.ppermute(block, 'wide', [(w, w ^ 1) for w in range(count)])  4.42 us
  transfers between devices with their start and end apart: 25, of which 19 were waited for; matrix products, arithmetic and copies ran while one was open for 0% of the time, Pallas kernels for 2%

profile of v10, /device:TPU:0, one launch (start us, length us, event | category | flops | bytes accessed | tf_op | source)
XLA Modules:
  0.0 90.1 jit_solution(12777189241417456399)
XLA Ops:
  0.0 0.7 copy-done.7
  0.7 0.1 dynamic-slice_convert_fusion
  0.7 0.1 multiply_bitcast_fusion
  0.8 0.1 pad_maximum_fusion.8.live_in_ref
  0.9 1.0 %convert_element_type.10.feat_ref = f32[64,8,256]{2,1,0:T(8,128)S(1)} convert(bf16[64,8,256]{2,1,0:T(8,128)(2,1)} %param.11) | non-fusion elementwise | flops 131072 | bytes 786432 | tf_op jit(solution)/shard_map/convert_element_type | solution.py:551
  1.9 0.0 copy-start
  1.9 0.0 copy-start.1
  1.9 0.0 copy-start.2
  1.9 0.0 copy-start.3
  1.9 1.0 %shard_map.100 = (bf16[144,128]{1,0:T(8,128)(2,1)S(1)}, bf16[512,128]{1,0:T(8,128)(2,1)S(1)}, f32[8,128]{1,0:T(8,128)S(1)}) custom-call(f32[64,8,256]{2,1,0:T(8,128)S(1)} %convert_element_type.10.feat_ref, bf16[64,256]{1,0:T(8,128)(2,1)S(1)} %bitcast.11, f32[8,128]{1,0:T(8,128)S(1)} %pad_maximum_fusion.8.live_in_ref), custom_call_target="tpu_custom_call" | custom-call | flops 1500000000 | bytes 561152 | tf_op jit(solution)/shard_map/pallas_call | solution.py:216
  2.9 4.1 %collective-permute-start = (bf16[144,128]{1,0:T(8,128)(2,1)S(1)}, bf16[144,128]{1,0:T(8,128)(2,1)S(1)}, u32[]{:S(2)}, u32[]{:S(2)}) collective-permute-start(bf16[144,128]{1,0:T(8,128)(2,1)S(1)} %get-tuple-element.43), channel_id=1, source_target_pairs={{0,8},{1,9},{2,10},{3,11},{4,12},{5,13},{6,14},{7,15},{8,0},{9,1},... | collective-permute-start | bytes 110600 | tf_op jit(solution)/shard_map/ppermute | solution.py:496
  7.0 0.1 pad_add_fusion.where_ref
  7.1 0.6 copy-done.5
  7.7 0.0 copy-done.6
  7.7 2.0 %shard_map.101 = (f32[8,128,128]{2,1,0:T(8,128)S(1)}, bf16[128,1024]{1,0:T(8,128)(2,1)S(1)}, bf16[2,640,128]{2,1,0:T(8,128)(2,1)S(1)}, bf16[2,128,128]{2,1,0:T(8,128)(2,1)S(1)}) custom-call(s32[3]{0:T(128)S(1)} %pad_add_fusion.where_ref, s32[128]{0:T(128)S(1)} %copy-done.6, s32[1,128]{1,0:T(1,128)S(1)} %bitcast.12, bf16[8,128,128]{2,1,0:T(8,128)(2,1)S(1)} %copy-done.1, ...), custom_call_target="tpu_custom_call" | custom-call | flops 1500000000 | bytes 935436 | tf_op jit(solution)/shard_map/pallas_call | solution.py:216
  9.8 1.6 %collective-permute-start.1 = (bf16[2,144,128]{2,1,0:T(8,128)(2,1)S(1)}, bf16[2,144,128]{2,1,0:T(8,128)(2,1)S(1)}, u32[]{:S(2)}, u32[]{:S(2)}) collective-permute-start(bf16[2,144,128]{2,1,0:T(8,128)(2,1)S(1)} %pad_maximum_fusion.7), channel_id=1, source_target_pairs={{0,4},{1,5},{2,6},{3,7},{4,0},{5,1},{6,2},{7,3},{8,12},{9,13},{10,... | collective-permute-start | bytes 221192 | tf_op jit(solution)/shard_map/ppermute | solution.py:496
  11.4 2.8 %collective-permute-done.1 = bf16[2,144,128]{2,1,0:T(8,128)(2,1)S(1)} collective-permute-done((bf16[2,144,128]{2,1,0:T(8,128)(2,1)S(1)}, bf16[2,144,128]{2,1,0:T(8,128)(2,1)S(1)}, u32[]{:S(2)}, u32[]{:S(2)}) %collective-permute-start.1) | collective-permute-done | bytes 73760 | tf_op jit(solution)/shard_map/ppermute | solution.py:496
  14.2 1.6 %collective-permute-start.2 = (bf16[4,144,128]{2,1,0:T(8,128)(2,1)S(1)}, bf16[4,144,128]{2,1,0:T(8,128)(2,1)S(1)}, u32[]{:S(2)}, u32[]{:S(2)}) collective-permute-start(bf16[4,144,128]{2,1,0:T(8,128)(2,1)S(1)} %pad_maximum_fusion), channel_id=1, source_target_pairs={{0,2},{1,3},{2,0},{3,1},{4,6},{5,7},{6,4},{7,5},{8,10},{9,11},{10,... | collective-permute-start | bytes 442376 | tf_op jit(solution)/shard_map/ppermute | solution.py:496
  15.8 3.6 %collective-permute-done.2 = bf16[4,144,128]{2,1,0:T(8,128)(2,1)S(1)} collective-permute-done((bf16[4,144,128]{2,1,0:T(8,128)(2,1)S(1)}, bf16[4,144,128]{2,1,0:T(8,128)(2,1)S(1)}, u32[]{:S(2)}, u32[]{:S(2)}) %collective-permute-start.2) | collective-permute-done | bytes 147488 | tf_op jit(solution)/shard_map/ppermute | solution.py:496
  19.5 0.1 collective-permute-start.3
  19.6 1.6 %collective-permute-done.3.other_ref = bf16[8,144,128]{2,1,0:T(8,128)(2,1)S(1)} collective-permute-done((bf16[8,144,128]{2,1,0:T(8,128)(2,1)S(1)}, bf16[8,144,128]{2,1,0:T(8,128)(2,1)S(1)}, u32[]{:S(2)}, u32[]{:S(2)}) %collective-permute-start.3) | collective-permute-done | bytes 294944 | tf_op jit(solution)/shard_map/ppermute | solution.py:522
  21.1 3.1 %shard_map.102 = (f32[8,128,128]{2,1,0:T(8,128)S(1)}, f32[8,128,128]{2,1,0:T(8,128)S(1)}, bf16[256,128]{1,0:T(8,128)(2,1)S(1)}, bf16[256,128]{1,0:T(8,128)(2,1)S...) custom-call(s32[3]{0:T(128)S(1)} %pad_add_fusion.where_ref, ...), custom_call_target="tpu_custom_call" | custom-call | flops 4000000000 | bytes 1840140 | tf_op jit(solution)/shard_map/pallas_call | solution.py:216
  24.3 0.2 collective-permute-start.7
  24.5 2.5 %collective-permute-start.4 = (bf16[512,128]{1,0:T(8,128)(2,1)S(1)}, bf16[512,128]{1,0:T(8,128)(2,1)S(1)}, u32[]{:S(2)}, u32[]{:S(2)}) collective-permute-start(bf16[512,128]{1,0:T(8,128)(2,1)S(1)} %get-tuple-element.54), channel_id=1, source_target_pairs={{0,6},{1,7},{2,4},{3,5},{4,2},{5,3},{6,0},{7,1},{8,14},{9,15},{10,... | collective-permute-start | bytes 393224 | tf_op jit(solution)/shard_map/ppermute | solution.py:496
  27.0 0.4 collective-permute-start.5
  27.5 0.5 collective-permute-start.6
  28.0 0.0 collective-permute-done.7
  28.0 4.4 %collective-permute-start.8 = (bf16[512,128]{1,0:T(8,128)(2,1)S(1)}, bf16[512,128]{1,0:T(8,128)(2,1)S(1)}, u32[]{:S(2)}, u32[]{:S(2)}) collective-permute-start(bf16[512,128]{1,0:T(8,128)(2,1)S(1)} %pad_maximum_fusion.1), channel_id=1, source_target_pairs={{0,14},{1,11},{2,12},{3,9},{4,10},{5,15},{6,8},{7,13},{8,6},{9,3},... | collective-permute-start | bytes 393224 | tf_op jit(solution)/shard_map/ppermute | solution.py:505
  32.4 0.5 collective-permute-start.9
  32.9 3.4 %collective-permute-done.5.near1 = bf16[512,128]{1,0:T(8,128)(2,1)S(1)} collective-permute-done((bf16[512,128]{1,0:T(8,128)(2,1)S(1)}, bf16[512,128]{1,0:T(8,128)(2,1)S(1)}, u32[]{:S(2)}, u32[]{:S(2)}) %collective-permute-start.5) | collective-permute-done | bytes 131104 | tf_op jit(solution)/shard_map/ppermute | solution.py:496
  36.4 0.0 collective-permute-done.6.near2
  36.4 2.5 %collective-permute-done.8.far0 = bf16[512,128]{1,0:T(8,128)(2,1)S(1)} collective-permute-done((bf16[512,128]{1,0:T(8,128)(2,1)S(1)}, bf16[512,128]{1,0:T(8,128)(2,1)S(1)}, u32[]{:S(2)}, u32[]{:S(2)}) %collective-permute-start.8) | collective-permute-done | bytes 131104 | tf_op jit(solution)/shard_map/ppermute | solution.py:505
  39.0 2.3 %collective-permute-done.9.far1 = bf16[512,128]{1,0:T(8,128)(2,1)S(1)} collective-permute-done((bf16[512,128]{1,0:T(8,128)(2,1)S(1)}, bf16[512,128]{1,0:T(8,128)(2,1)S(1)}, u32[]{:S(2)}, u32[]{:S(2)}) %collective-permute-start.9) | collective-permute-done | bytes 131104 | tf_op jit(solution)/shard_map/ppermute | solution.py:505
  41.3 1.0 %collective-permute-start.10 = (bf16[2048,128]{1,0:T(8,128)(2,1)S(1)}, bf16[2048,128]{1,0:T(8,128)(2,1)S(1)}, u32[]{:S(2)}, u32[]{:S(2)}) collective-permute-start(bf16[2048,128]{1,0:T(8,128)(2,1)S(1)} %constant_dynamic-update-slice_fusion.3), channel_id=1, source_target_pairs={{0,1},{1,0},{2,3},{3,2},{4,5},{5,4},{6,7},{7,6},{8,9},{9,8},{10,11... | collective-permute-start | bytes 1572872 | tf_op jit(solution)/shard_map/ppermute | solution.py:522
  42.3 1.5 %collective-permute-done.10.other_ref = bf16[2048,128]{1,0:T(8,128)(2,1)S(1)} collective-permute-done((bf16[2048,128]{1,0:T(8,128)(2,1)S(1)}, bf16[2048,128]{1,0:T(8,128)(2,1)S(1)}, u32[]{:S(2)}, u32[]{:S(2)}) %collective-permute-start.10) | collective-permute-done | bytes 524320 | tf_op jit(solution)/shard_map/ppermute | solution.py:522
  43.8 1.5 %shard_map.103 = (bf16[256,128]{1,0:T(8,128)(2,1)S(1)}, bf16[256,128]{1,0:T(8,128)(2,1)S(1)}, bf16[256,128]{1,0:T(8,128)(2,1)S(1)}, bf16[256,128]{1,0:T(8,128)(2,1)S(1)}) custom-call(s32[3]{0:T(128)S(1)} %pad_add_fusion.where_ref, bf16[512,128]{1,0:T(8,128)(2,1)S(1)} %collective-permute-done.4.near0, bf16[512,128]{1,0:T(8,128)(2,1)S(1)} %collective-permute-done.5.near1, ...), custom_call_target="tpu_custom_call" | custom-call | flops 1500000000 | bytes 1310732 | tf_op jit(solution)/shard_map/pallas_call | solution.py:216
  45.3 2.2 %collective-permute-start.11 = (bf16[256,128]{1,0:T(8,128)(2,1)S(1)}, bf16[256,128]{1,0:T(8,128)(2,1)S(1)}, u32[]{:S(2)}, u32[]{:S(2)}) collective-permute-start(bf16[256,128]{1,0:T(8,128)(2,1)S(1)} %get-tuple-element.61), channel_id=1, source_target_pairs={{0,6},{1,3},{2,4},{3,1},{4,2},{5,7},{6,0},{7,5},{8,14},{9,11},{10,... | collective-permute-start | bytes 196616 | tf_op jit(solution)/shard_map/ppermute | solution.py:505
  47.5 1.5 %collective-permute-start.12 = (bf16[256,128]{1,0:T(8,128)(2,1)S(1)}, bf16[256,128]{1,0:T(8,128)(2,1)S(1)}, u32[]{:S(2)}, u32[]{:S(2)}) collective-permute-start(bf16[256,128]{1,0:T(8,128)(2,1)S(1)} %get-tuple-element.62), channel_id=1, source_target_pairs={{0,2},{1,5},{2,0},{3,7},{4,6},{5,1},{6,4},{7,3},{8,10},{9,13},{10,... | collective-permute-start | bytes 196616 | tf_op jit(solution)/shard_map/ppermute | solution.py:505
  49.0 2.1 %collective-permute-done.11.in0 = bf16[256,128]{1,0:T(8,128)(2,1)S(1)} collective-permute-done((bf16[256,128]{1,0:T(8,128)(2,1)S(1)}, bf16[256,128]{1,0:T(8,128)(2,1)S(1)}, u32[]{:S(2)}, u32[]{:S(2)}) %collective-permute-start.11) | collective-permute-done | bytes 65568 | tf_op jit(solution)/shard_map/ppermute | solution.py:505
  51.1 1.4 %collective-permute-done.12.in1 = bf16[256,128]{1,0:T(8,128)(2,1)S(1)} collective-permute-done((bf16[256,128]{1,0:T(8,128)(2,1)S(1)}, bf16[256,128]{1,0:T(8,128)(2,1)S(1)}, u32[]{:S(2)}, u32[]{:S(2)}) %collective-permute-start.12) | collective-permute-done | bytes 65568 | tf_op jit(solution)/shard_map/ppermute | solution.py:505
  52.5 0.8 collective-permute-done.13.in2
  53.3 2.2 %shard_map.104 = (f32[8,128,128]{2,1,0:T(8,128)S(1)}, f32[8,128,128]{2,1,0:T(8,128)S(1)}, bf16[256,128]{1,0:T(8,128)(2,1)S(1)}, bf16[256,128]{1,0:T(8,128)(2,1)S...) custom-call(s32[3]{0:T(128)S(1)} %pad_add_fusion.where_ref, ...), custom_call_target="tpu_custom_call" | custom-call | flops 1500000000 | bytes 1704972 | tf_op jit(solution)/shard_map/pallas_call | solution.py:216
  55.5 0.1 collective-permute-start.14
  55.6 1.5 %collective-permute-done.14 = bf16[1024,128]{1,0:T(8,128)(2,1)S(1)} collective-permute-done((bf16[1024,128]{1,0:T(8,128)(2,1)S(1)}, bf16[1024,128]{1,0:T(8,128)(2,1)S(1)}, u32[]{:S(2)}, u32[]{:S(2)}) %collective-permute-start.14) | collective-permute-done | bytes 262176 | tf_op jit(solution)/shard_map/ppermute | solution.py:522
  57.2 3.4 %collective-permute-start.15 = (bf16[512,128]{1,0:T(8,128)(2,1)S(1)}, bf16[512,128]{1,0:T(8,128)(2,1)S(1)}, u32[]{:S(2)}, u32[]{:S(2)}) collective-permute-start(bf16[512,128]{1,0:T(8,128)(2,1)S(1)} %pad_maximum_fusion.3), channel_id=1, source_target_pairs={{0,14},{1,11},{2,12},{3,9},{4,10},{5,15},{6,8},{7,13},{8,6},{9,3},... | collective-permute-start | bytes 393224 | tf_op jit(solution)/shard_map/ppermute | solution.py:505
  60.6 0.7 collective-permute-start.16
  61.3 0.1 collective-permute-start.17
  61.4 3.2 %collective-permute-start.18 = (bf16[512,128]{1,0:T(8,128)(2,1)S(1)}, bf16[512,128]{1,0:T(8,128)(2,1)S(1)}, u32[]{:S(2)}, u32[]{:S(2)}) collective-permute-start(bf16[512,128]{1,0:T(8,128)(2,1)S(1)} %pad_maximum_fusion.6), channel_id=1, source_target_pairs={{0,2},{1,1},{2,0},{3,3},{4,6},{5,5},{6,4},{7,7},{8,10},{9,9},{10,8... | collective-permute-start | bytes 393224 | tf_op jit(solution)/shard_map/ppermute | solution.py:505
  64.6 0.5 collective-permute-done.15.came0
  65.2 3.3 %collective-permute-done.16.came1 = bf16[512,128]{1,0:T(8,128)(2,1)S(1)} collective-permute-done((bf16[512,128]{1,0:T(8,128)(2,1)S(1)}, bf16[512,128]{1,0:T(8,128)(2,1)S(1)}, u32[]{:S(2)}, u32[]{:S(2)}) %collective-permute-start.16) | collective-permute-done | bytes 131104 | tf_op jit(solution)/shard_map/ppermute | solution.py:505
  68.5 1.9 %collective-permute-done.17.came2 = bf16[512,128]{1,0:T(8,128)(2,1)S(1)} collective-permute-done((bf16[512,128]{1,0:T(8,128)(2,1)S(1)}, bf16[512,128]{1,0:T(8,128)(2,1)S(1)}, u32[]{:S(2)}, u32[]{:S(2)}) %collective-permute-start.17) | collective-permute-done | bytes 131104 | tf_op jit(solution)/shard_map/ppermute | solution.py:505
  70.4 1.4 %shard_map.105 = (f32[4,256,128]{2,1,0:T(8,128)S(1)}, f32[4,256,128]{2,1,0:T(8,128)S(1)}) custom-call(s32[3]{0:T(128)S(1)} %pad_add_fusion.where_ref, bf16[512,128]{1,0:T(8,128)(2,1)S(1)} %collective-permute-done.15.came0, bf16[512,128]{1,0:T(8,128)(2,1)S(1)} %collective-permute-done.16.came1, bf16[512,128]{1,0:T(8,128)(2,1)S(1)} %collective-permute-done.17.came2, ...), custom_call_target="tpu_custom_call" | custom-call | flops 1500000000 | bytes 524300 | tf_op jit(solution)/shard_map/pallas_call | solution.py:216
  71.8 1.6 %collective-permute-start.19 = (f32[4,256,128]{2,1,0:T(8,128)S(1)}, f32[4,256,128]{2,1,0:T(8,128)S(1)}, u32[]{:S(2)}, u32[]{:S(2)}) collective-permute-start(f32[4,256,128]{2,1,0:T(8,128)S(1)} %get-tuple-element.74), channel_id=1, source_target_pairs={{0,1},{1,0},{2,3},{3,2},{4,5},{5,4},{6,7},{7,6},{8,9},{9,8},{10,11... | collective-permute-start | bytes 1572872 | tf_op jit(solution)/shard_map/ppermute | solution.py:522
  73.3 1.5 %collective-permute-done.19.got_ref = f32[4,256,128]{2,1,0:T(8,128)S(1)} collective-permute-done((f32[4,256,128]{2,1,0:T(8,128)S(1)}, f32[4,256,128]{2,1,0:T(8,128)S(1)}, u32[]{:S(2)}, u32[]{:S(2)}) %collective-permute-start.19) | collective-permute-done | bytes 524320 | tf_op jit(solution)/shard_map/ppermute | solution.py:522
  74.9 4.1 %collective-permute-start.20 = (bf16[256,128]{1,0:T(8,128)(2,1)S(1)}, bf16[256,128]{1,0:T(8,128)(2,1)S(1)}, u32[]{:S(2)}, u32[]{:S(2)}) collective-permute-start(bf16[256,128]{1,0:T(8,128)(2,1)S(1)} %get-tuple-element.75), channel_id=1, source_target_pairs={{0,14},{1,7},{2,12},{3,5},{4,10},{5,3},{6,8},{7,1},{8,6},{9,15},{1... | collective-permute-start | bytes 196616 | tf_op jit(solution)/shard_map/ppermute | solution.py:505
  79.0 0.3 collective-permute-start.21
  79.3 1.0 %collective-permute-start.22 = (bf16[256,128]{1,0:T(8,128)(2,1)S(1)}, bf16[256,128]{1,0:T(8,128)(2,1)S(1)}, u32[]{:S(2)}, u32[]{:S(2)}) collective-permute-start(bf16[256,128]{1,0:T(8,128)(2,1)S(1)} %get-tuple-element.77), channel_id=1, source_target_pairs={{0,10},{1,3},{2,8},{3,1},{4,14},{5,7},{6,12},{7,5},{8,2},{9,11},{1... | collective-permute-start | bytes 196616 | tf_op jit(solution)/shard_map/ppermute | solution.py:505
  80.3 0.7 collective-permute-start.23
  80.9 1.7 %collective-permute-done.20.refs_0_.came0 = bf16[256,128]{1,0:T(8,128)(2,1)S(1)} collective-permute-done((bf16[256,128]{1,0:T(8,128)(2,1)S(1)}, bf16[256,128]{1,0:T(8,128)(2,1)S(1)}, u32[]{:S(2)}, u32[]{:S(2)}) %collective-permute-start.20) | collective-permute-done | bytes 65568 | tf_op jit(solution)/shard_map/ppermute | solution.py:505
  82.7 1.1 %collective-permute-done.21.refs_1_.came1 = bf16[256,128]{1,0:T(8,128)(2,1)S(1)} collective-permute-done((bf16[256,128]{1,0:T(8,128)(2,1)S(1)}, bf16[256,128]{1,0:T(8,128)(2,1)S(1)}, u32[]{:S(2)}, u32[]{:S(2)}) %collective-permute-start.21) | collective-permute-done | bytes 65568 | tf_op jit(solution)/shard_map/ppermute | solution.py:505
  83.8 1.6 %collective-permute-done.22.refs_2_.came2 = bf16[256,128]{1,0:T(8,128)(2,1)S(1)} collective-permute-done((bf16[256,128]{1,0:T(8,128)(2,1)S(1)}, bf16[256,128]{1,0:T(8,128)(2,1)S(1)}, u32[]{:S(2)}, u32[]{:S(2)}) %collective-permute-start.22) | collective-permute-done | bytes 65568 | tf_op jit(solution)/shard_map/ppermute | solution.py:505
  85.4 1.5 %collective-permute-start.24 = (bf16[512,128]{1,0:T(8,128)(2,1)S(1)}, bf16[512,128]{1,0:T(8,128)(2,1)S(1)}, u32[]{:S(2)}, u32[]{:S(2)}) collective-permute-start(bf16[512,128]{1,0:T(8,128)(2,1)S(1)} %shard_map.107), channel_id=1, source_target_pairs={{0,1},{1,0},{2,3},{3,2},{4,5},{5,4},{6,7},{7,6},{8,9},{9,8},{10,11... | collective-permute-start | bytes 393224 | tf_op jit(solution)/shard_map/ppermute | solution.py:522
  86.9 1.0 %collective-permute-done.24.other_ref = bf16[512,128]{1,0:T(8,128)(2,1)S(1)} collective-permute-done((bf16[512,128]{1,0:T(8,128)(2,1)S(1)}, bf16[512,128]{1,0:T(8,128)(2,1)S(1)}, u32[]{:S(2)}, u32[]{:S(2)}) %collective-permute-start.24) | collective-permute-done | bytes 131104 | tf_op jit(solution)/shard_map/ppermute | solution.py:522
  87.9 2.2 %shard_map.108 = bf16[8,128,128]{2,1,0:T(8,128)(2,1)} custom-call(s32[3]{0:T(128)S(1)} %pad_add_fusion.where_ref, bf16[256,128]{1,0:T(8,128)(2,1)S(1)} %collective-permute-done.20.refs_0_.came0, bf16[256,128]{1,0:T(8,128)(2,1)S(1)} %collective-permute-done.21.refs_1_.came1, bf16[256,128]{1,0:T(8,128)(2,1)S(1)} %collective-permute-done.22.refs_2_.came2, ...), custom_call_target="tpu_custom_call" | custom-call | flops 1500000000 | bytes 1507340 | tf_op jit(solution)/shard_map/pallas_call | solution.py:216
  (37 shorter events, 0.3 us)
Async XLA Ops:
  0.0 0.7 copy-start.7
  0.0 0.7 copy-start.8
  0.9 1.0 %copy-start.4 = (bf16[256,64]{0,1:T(8,128)(2,1)S(1)}, bf16[256,64]{0,1:T(8,128)(2,1)}, u32[]{:S(2)}) copy-start(bf16[256,64]{0,1:T(8,128)(2,1)} %param.16) | copy-start | bytes 98308
  1.9 5.2 %copy-start = (bf16[2,128,640]{2,1,0:T(8,128)(2,1)S(1)}, bf16[2,128,640]{2,1,0:T(8,128)(2,1)}, u32[]{:S(2)}) copy-start(bf16[2,128,640]{2,1,0:T(8,128)(2,1)} %proj_ref.1) | copy-start | bytes 983044
  1.9 5.2 %copy-start.1 = (bf16[8,128,128]{2,1,0:T(8,128)(2,1)S(1)}, bf16[8,128,128]{2,1,0:T(8,128)(2,1)}, u32[]{:S(2)}) copy-start(bf16[8,128,128]{2,1,0:T(8,128)(2,1)} %pair_ref.1) | copy-start | bytes 786436
  1.9 5.2 %copy-start.2 = (bf16[1024,128]{1,0:T(8,128)(2,1)S(1)}, bf16[1024,128]{1,0:T(8,128)(2,1)}, u32[]{:S(2)}) copy-start(bf16[1024,128]{1,0:T(8,128)(2,1)} %outer_ref.1) | copy-start | bytes 786436
  1.9 5.2 %copy-start.3 = (bf16[2,128,128]{2,1,0:T(8,128)(2,1)S(1)}, bf16[2,128,128]{2,1,0:T(8,128)(2,1)}, u32[]{:S(2)}) copy-start(bf16[2,128,128]{2,1,0:T(8,128)(2,1)} %out_ref.1) | copy-start | bytes 196612
  2.9 6.9 %collective-permute-start = (bf16[144,128]{1,0:T(8,128)(2,1)S(1)}, bf16[144,128]{1,0:T(8,128)(2,1)S(1)}, u32[]{:S(2)}, u32[]{:S(2)}) collective-permute-start(bf16[144,128]{1,0:T(8,128)(2,1)S(1)} %get-tuple-element.43), channel_id=1, source_target_pairs={{0,8},{1,9},{2,10},{3,11},{4,12},{5,13},{6,14},{7,15},{8,0},{9,1},... | collective-permute-start | bytes 110600 | tf_op jit(solution)/shard_map/ppermute | solution.py:496
  7.0 0.7 copy-start.5
  7.1 0.7 copy-start.6
  9.8 4.4 %collective-permute-start.1 = (bf16[2,144,128]{2,1,0:T(8,128)(2,1)S(1)}, bf16[2,144,128]{2,1,0:T(8,128)(2,1)S(1)}, u32[]{:S(2)}, u32[]{:S(2)}) collective-permute-start(bf16[2,144,128]{2,1,0:T(8,128)(2,1)S(1)} %pad_maximum_fusion.7), channel_id=1, source_target_pairs={{0,4},{1,5},{2,6},{3,7},{4,0},{5,1},{6,2},{7,3},{8,12},{9,13},{10,... | collective-permute-start | bytes 221192 | tf_op jit(solution)/shard_map/ppermute | solution.py:496
  14.2 5.2 %collective-permute-start.2 = (bf16[4,144,128]{2,1,0:T(8,128)(2,1)S(1)}, bf16[4,144,128]{2,1,0:T(8,128)(2,1)S(1)}, u32[]{:S(2)}, u32[]{:S(2)}) collective-permute-start(bf16[4,144,128]{2,1,0:T(8,128)(2,1)S(1)} %pad_maximum_fusion), channel_id=1, source_target_pairs={{0,2},{1,3},{2,0},{3,1},{4,6},{5,7},{6,4},{7,5},{8,10},{9,11},{10,... | collective-permute-start | bytes 442376 | tf_op jit(solution)/shard_map/ppermute | solution.py:496
  19.5 1.6 %collective-permute-start.3 = (bf16[8,144,128]{2,1,0:T(8,128)(2,1)S(1)}, bf16[8,144,128]{2,1,0:T(8,128)(2,1)S(1)}, u32[]{:S(2)}, u32[]{:S(2)}) collective-permute-start(bf16[8,144,128]{2,1,0:T(8,128)(2,1)S(1)} %constant_dynamic-update-slice_fusion.own_ref), channel_id=1, source_target_pairs={{0,1},{1,0},{2,3},{3,2},{4,5},{5,4},{6,7},{7,6},{8,9},{9,8},{10,11... | collective-permute-start | bytes 884744 | tf_op jit(solution)/shard_map/ppermute | solution.py:522
  24.3 3.7 %collective-permute-start.7 = (bf16[512,128]{1,0:T(8,128)(2,1)S(1)}, bf16[512,128]{1,0:T(8,128)(2,1)S(1)}, u32[]{:S(2)}, u32[]{:S(2)}) collective-permute-start(bf16[512,128]{1,0:T(8,128)(2,1)S(1)} %get-tuple-element.59), channel_id=1, source_target_pairs={{0,1},{1,0},{2,3},{3,2},{4,5},{5,4},{6,7},{7,6},{8,9},{9,8},{10,11... | collective-permute-start | bytes 393224 | tf_op jit(solution)/shard_map/ppermute | solution.py:522
  24.5 8.4 %collective-permute-start.4 = (bf16[512,128]{1,0:T(8,128)(2,1)S(1)}, bf16[512,128]{1,0:T(8,128)(2,1)S(1)}, u32[]{:S(2)}, u32[]{:S(2)}) collective-permute-start(bf16[512,128]{1,0:T(8,128)(2,1)S(1)} %get-tuple-element.54), channel_id=1, source_target_pairs={{0,6},{1,7},{2,4},{3,5},{4,2},{5,3},{6,0},{7,1},{8,14},{9,15},{10,... | collective-permute-start | bytes 393224 | tf_op jit(solution)/shard_map/ppermute | solution.py:496
  27.0 9.3 %collective-permute-start.5 = (bf16[512,128]{1,0:T(8,128)(2,1)S(1)}, bf16[512,128]{1,0:T(8,128)(2,1)S(1)}, u32[]{:S(2)}, u32[]{:S(2)}) collective-permute-start(bf16[512,128]{1,0:T(8,128)(2,1)S(1)} %get-tuple-element.55), channel_id=1, source_target_pairs={{0,4},{1,5},{2,6},{3,7},{4,0},{5,1},{6,2},{7,3},{8,12},{9,13},{10,... | collective-permute-start | bytes 393224 | tf_op jit(solution)/shard_map/ppermute | solution.py:496
  27.5 8.9 %collective-permute-start.6 = (bf16[512,128]{1,0:T(8,128)(2,1)S(1)}, bf16[512,128]{1,0:T(8,128)(2,1)S(1)}, u32[]{:S(2)}, u32[]{:S(2)}) collective-permute-start(bf16[512,128]{1,0:T(8,128)(2,1)S(1)} %get-tuple-element.56), channel_id=1, source_target_pairs={{0,2},{1,3},{2,0},{3,1},{4,6},{5,7},{6,4},{7,5},{8,10},{9,11},{10,... | collective-permute-start | bytes 393224 | tf_op jit(solution)/shard_map/ppermute | solution.py:496
  28.0 10.9 %collective-permute-start.8 = (bf16[512,128]{1,0:T(8,128)(2,1)S(1)}, bf16[512,128]{1,0:T(8,128)(2,1)S(1)}, u32[]{:S(2)}, u32[]{:S(2)}) collective-permute-start(bf16[512,128]{1,0:T(8,128)(2,1)S(1)} %pad_maximum_fusion.1), channel_id=1, source_target_pairs={{0,14},{1,11},{2,12},{3,9},{4,10},{5,15},{6,8},{7,13},{8,6},{9,3},... | collective-permute-start | bytes 393224 | tf_op jit(solution)/shard_map/ppermute | solution.py:505
  32.4 8.9 %collective-permute-start.9 = (bf16[512,128]{1,0:T(8,128)(2,1)S(1)}, bf16[512,128]{1,0:T(8,128)(2,1)S(1)}, u32[]{:S(2)}, u32[]{:S(2)}) collective-permute-start(bf16[512,128]{1,0:T(8,128)(2,1)S(1)} %pad_maximum_fusion.2), channel_id=1, source_target_pairs={{0,12},{1,9},{2,14},{3,11},{4,8},{5,13},{6,10},{7,15},{8,4},{9,1},... | collective-permute-start | bytes 393224 | tf_op jit(solution)/shard_map/ppermute | solution.py:505
  41.3 2.5 %collective-permute-start.10 = (bf16[2048,128]{1,0:T(8,128)(2,1)S(1)}, bf16[2048,128]{1,0:T(8,128)(2,1)S(1)}, u32[]{:S(2)}, u32[]{:S(2)}) collective-permute-start(bf16[2048,128]{1,0:T(8,128)(2,1)S(1)} %constant_dynamic-update-slice_fusion.3), channel_id=1, source_target_pairs={{0,1},{1,0},{2,3},{3,2},{4,5},{5,4},{6,7},{7,6},{8,9},{9,8},{10,11... | collective-permute-start | bytes 1572872 | tf_op jit(solution)/shard_map/ppermute | solution.py:522
  45.3 5.8 %collective-permute-start.11 = (bf16[256,128]{1,0:T(8,128)(2,1)S(1)}, bf16[256,128]{1,0:T(8,128)(2,1)S(1)}, u32[]{:S(2)}, u32[]{:S(2)}) collective-permute-start(bf16[256,128]{1,0:T(8,128)(2,1)S(1)} %get-tuple-element.61), channel_id=1, source_target_pairs={{0,6},{1,3},{2,4},{3,1},{4,2},{5,7},{6,0},{7,5},{8,14},{9,11},{10,... | collective-permute-start | bytes 196616 | tf_op jit(solution)/shard_map/ppermute | solution.py:505
  47.5 5.0 %collective-permute-start.12 = (bf16[256,128]{1,0:T(8,128)(2,1)S(1)}, bf16[256,128]{1,0:T(8,128)(2,1)S(1)}, u32[]{:S(2)}, u32[]{:S(2)}) collective-permute-start(bf16[256,128]{1,0:T(8,128)(2,1)S(1)} %get-tuple-element.62), channel_id=1, source_target_pairs={{0,2},{1,5},{2,0},{3,7},{4,6},{5,1},{6,4},{7,3},{8,10},{9,13},{10,... | collective-permute-start | bytes 196616 | tf_op jit(solution)/shard_map/ppermute | solution.py:505
  49.0 4.3 %collective-permute-start.13 = (bf16[256,128]{1,0:T(8,128)(2,1)S(1)}, bf16[256,128]{1,0:T(8,128)(2,1)S(1)}, u32[]{:S(2)}, u32[]{:S(2)}) collective-permute-start(bf16[256,128]{1,0:T(8,128)(2,1)S(1)} %get-tuple-element.63), channel_id=1, source_target_pairs={{0,4},{1,7},{2,6},{3,5},{4,0},{5,3},{6,2},{7,1},{8,12},{9,15},{10,... | collective-permute-start | bytes 196616 | tf_op jit(solution)/shard_map/ppermute | solution.py:505
  55.5 1.6 %collective-permute-start.14 = (bf16[1024,128]{1,0:T(8,128)(2,1)S(1)}, bf16[1024,128]{1,0:T(8,128)(2,1)S(1)}, u32[]{:S(2)}, u32[]{:S(2)}) collective-permute-start(bf16[1024,128]{1,0:T(8,128)(2,1)S(1)} %get-tuple-element.69), channel_id=1, source_target_pairs={{0,1},{1,0},{2,3},{3,2},{4,5},{5,4},{6,7},{7,6},{8,9},{9,8},{10,11... | collective-permute-start | bytes 786440 | tf_op jit(solution)/shard_map/ppermute | solution.py:522
  57.2 8.0 %collective-permute-start.15 = (bf16[512,128]{1,0:T(8,128)(2,1)S(1)}, bf16[512,128]{1,0:T(8,128)(2,1)S(1)}, u32[]{:S(2)}, u32[]{:S(2)}) collective-permute-start(bf16[512,128]{1,0:T(8,128)(2,1)S(1)} %pad_maximum_fusion.3), channel_id=1, source_target_pairs={{0,14},{1,11},{2,12},{3,9},{4,10},{5,15},{6,8},{7,13},{8,6},{9,3},... | collective-permute-start | bytes 393224 | tf_op jit(solution)/shard_map/ppermute | solution.py:505
  60.6 8.0 %collective-permute-start.16 = (bf16[512,128]{1,0:T(8,128)(2,1)S(1)}, bf16[512,128]{1,0:T(8,128)(2,1)S(1)}, u32[]{:S(2)}, u32[]{:S(2)}) collective-permute-start(bf16[512,128]{1,0:T(8,128)(2,1)S(1)} %pad_maximum_fusion.4), channel_id=1, source_target_pairs={{0,12},{1,9},{2,14},{3,11},{4,8},{5,13},{6,10},{7,15},{8,4},{9,1},... | collective-permute-start | bytes 393224 | tf_op jit(solution)/shard_map/ppermute | solution.py:505
  61.3 9.1 %collective-permute-start.17 = (bf16[512,128]{1,0:T(8,128)(2,1)S(1)}, bf16[512,128]{1,0:T(8,128)(2,1)S(1)}, u32[]{:S(2)}, u32[]{:S(2)}) collective-permute-start(bf16[512,128]{1,0:T(8,128)(2,1)S(1)} %pad_maximum_fusion.5), channel_id=1, source_target_pairs={{0,6},{1,5},{2,4},{3,7},{4,2},{5,1},{6,0},{7,3},{8,14},{9,13},{10,... | collective-permute-start | bytes 393224 | tf_op jit(solution)/shard_map/ppermute | solution.py:505
  61.4 9.0 %collective-permute-start.18 = (bf16[512,128]{1,0:T(8,128)(2,1)S(1)}, bf16[512,128]{1,0:T(8,128)(2,1)S(1)}, u32[]{:S(2)}, u32[]{:S(2)}) collective-permute-start(bf16[512,128]{1,0:T(8,128)(2,1)S(1)} %pad_maximum_fusion.6), channel_id=1, source_target_pairs={{0,2},{1,1},{2,0},{3,3},{4,6},{5,5},{6,4},{7,7},{8,10},{9,9},{10,8... | collective-permute-start | bytes 393224 | tf_op jit(solution)/shard_map/ppermute | solution.py:505
  71.8 3.1 %collective-permute-start.19 = (f32[4,256,128]{2,1,0:T(8,128)S(1)}, f32[4,256,128]{2,1,0:T(8,128)S(1)}, u32[]{:S(2)}, u32[]{:S(2)}) collective-permute-start(f32[4,256,128]{2,1,0:T(8,128)S(1)} %get-tuple-element.74), channel_id=1, source_target_pairs={{0,1},{1,0},{2,3},{3,2},{4,5},{5,4},{6,7},{7,6},{8,9},{9,8},{10,11... | collective-permute-start | bytes 1572872 | tf_op jit(solution)/shard_map/ppermute | solution.py:522
  74.9 7.7 %collective-permute-start.20 = (bf16[256,128]{1,0:T(8,128)(2,1)S(1)}, bf16[256,128]{1,0:T(8,128)(2,1)S(1)}, u32[]{:S(2)}, u32[]{:S(2)}) collective-permute-start(bf16[256,128]{1,0:T(8,128)(2,1)S(1)} %get-tuple-element.75), channel_id=1, source_target_pairs={{0,14},{1,7},{2,12},{3,5},{4,10},{5,3},{6,8},{7,1},{8,6},{9,15},{1... | collective-permute-start | bytes 196616 | tf_op jit(solution)/shard_map/ppermute | solution.py:505
  79.0 4.8 %collective-permute-start.21 = (bf16[256,128]{1,0:T(8,128)(2,1)S(1)}, bf16[256,128]{1,0:T(8,128)(2,1)S(1)}, u32[]{:S(2)}, u32[]{:S(2)}) collective-permute-start(bf16[256,128]{1,0:T(8,128)(2,1)S(1)} %get-tuple-element.76), channel_id=1, source_target_pairs={{0,4},{1,13},{2,6},{3,15},{4,0},{5,9},{6,2},{7,11},{8,12},{9,5},{1... | collective-permute-start | bytes 196616 | tf_op jit(solution)/shard_map/ppermute | solution.py:505
  79.3 6.1 %collective-permute-start.22 = (bf16[256,128]{1,0:T(8,128)(2,1)S(1)}, bf16[256,128]{1,0:T(8,128)(2,1)S(1)}, u32[]{:S(2)}, u32[]{:S(2)}) collective-permute-start(bf16[256,128]{1,0:T(8,128)(2,1)S(1)} %get-tuple-element.77), channel_id=1, source_target_pairs={{0,10},{1,3},{2,8},{3,1},{4,14},{5,7},{6,12},{7,5},{8,2},{9,11},{1... | collective-permute-start | bytes 196616 | tf_op jit(solution)/shard_map/ppermute | solution.py:505
  80.3 5.1 %collective-permute-start.23 = (bf16[256,128]{1,0:T(8,128)(2,1)S(1)}, bf16[256,128]{1,0:T(8,128)(2,1)S(1)}, u32[]{:S(2)}, u32[]{:S(2)}) collective-permute-start(bf16[256,128]{1,0:T(8,128)(2,1)S(1)} %get-tuple-element.78), channel_id=1, source_target_pairs={{0,0},{1,9},{2,2},{3,11},{4,4},{5,13},{6,6},{7,15},{8,8},{9,1},{10... | collective-permute-start | bytes 196616 | tf_op jit(solution)/shard_map/ppermute | solution.py:505
  85.4 2.5 %collective-permute-start.24 = (bf16[512,128]{1,0:T(8,128)(2,1)S(1)}, bf16[512,128]{1,0:T(8,128)(2,1)S(1)}, u32[]{:S(2)}, u32[]{:S(2)}) collective-permute-start(bf16[512,128]{1,0:T(8,128)(2,1)S(1)} %shard_map.107), channel_id=1, source_target_pairs={{0,1},{1,0},{2,3},{3,2},{4,5},{5,4},{6,7},{7,6},{8,9},{9,8},{10,11... | collective-permute-start | bytes 393224 | tf_op jit(solution)/shard_map/ppermute | solution.py:522

commit v11 on v10

--- a/solution.py
+++ b/solution.py
@@ -228,7 +228,6 @@
 SPLIT = ((7, 5), (6, 4), (3, 2), (1, 0))
 FAR_SPLIT = SPLIT[:2]
 SMALL_SPLIT = ((7, 3), (2, 6), (5, 1), (0, 4))
-SMALL_NEAR = ((3, 1), (1, 2), (2, 3), (0, 0))
 OPS = len(SPLIT)
 NEAR = 4
 NEAR_STEPS = (3, 2, 1, 0)
@@ -260,9 +259,9 @@
         high = nt(weight, jnp.concatenate([blank, mine], axis=0)) * live[row : row + 1]
         left_ref[row * half : (row + 1) * half] = low[:half].astype(BF16)
         left_ref[(rows + row) * half : (rows + row + 1) * half] = high[:half].astype(BF16)
-        turned[row] = low[half : half + quarter] + high[half + quarter :]
+        turned[row * quarter : (row + 1) * quarter] = low[half : half + quarter] + high[half + quarter :]
     for pair in range(quarter):
-        packed[pair * rows : (pair + 1) * rows] = turned[:, pair, :]
+        packed[pair * rows : (pair + 1) * rows] = turned[pl.ds(pair, rows, stride=quarter), :]
     packed[quarter * rows : (quarter + 1) * rows] = live
     packed[(quarter + 1) * rows :] = jnp.zeros((rows, 2 * homologs), F32)
     pay_ref[...] = packed[...].astype(BF16)
@@ -287,10 +286,10 @@
         bin_index = jnp.where(chains == chain_ref[place], offset, 2 * RELMAX + 1)
         hot = (slot == bin_index).astype(F32).astype(BF16)
         base_ref[row] = flip(pair_ref[row]) + nn(table, hot)
-    half = outer_pad.shape[0]
-    outer_pad[...] = outer_ref[...].astype(F32).reshape(outer_pad.shape)
+    half = round(outer_pad.shape[0] ** 0.5)
+    outer_pad[...] = outer_ref[...].astype(F32)
     for d in range(half):
-        outer_t_ref[:, d * half : (d + 1) * half] = flip(outer_pad[:, d, :].astype(BF16)).astype(BF16)
+        outer_t_ref[:, d * half : (d + 1) * half] = flip(outer_pad[pl.ds(d, half, stride=half), :].astype(BF16)).astype(BF16)
     for turn in range(2):
         proj_t_ref[turn] = tn(proj_ref[turn], identity(width)).astype(BF16)
         out_t_ref[turn] = flip(out_ref[turn]).astype(BF16)
@@ -302,13 +301,14 @@
 
 def sides(streams, weight, lives, gate_ref, lefts, rights, row):
     width, cols = streams[0].shape
+    rows = lefts.shape[0] // width
     made = nn(weight, jnp.concatenate([norm_rows(stream) for stream in streams], axis=1))
     for at, live in enumerate(lives):
         part = [
             made[block * width : (block + 1) * width, at * cols : (at + 1) * cols] for block in range(5)
         ]
-        lefts[:, row + at, :] = sigmoid(part[0]) * part[1] * live
-        rights[:, row + at, :] = sigmoid(part[2]) * part[3] * live
+        lefts[pl.ds(row + at, width, stride=rows), :] = sigmoid(part[0]) * part[1] * live
+        rights[pl.ds(row + at, width, stride=rows), :] = sigmoid(part[2]) * part[3] * live
         gate_ref[row + at] = sigmoid(part[4])
 
 
@@ -358,8 +358,8 @@
     block = size * rows
 
     def group(side, to):
-        first = pl.multiple_of((to & (NEAR - 1)) * size, size)
-        return flat(side[pl.ds(first, size)]).astype(BF16)
+        first = pl.multiple_of((to & (NEAR - 1)) * block, block)
+        return side[pl.ds(first, block), :].astype(BF16)
 
     for op, far in enumerate((far0, far1)):
         far[...] = group(rights, partner_chip(chip, core, op, FAR_SPLIT))
@@ -395,10 +395,9 @@
     for c in range(count):
         left = flat(lefts[:, c]).astype(BF16)
         right = flat(rights[:, c]).astype(BF16)
-        mixed[:, c, :] = nt(left, right)
-    for op, out in enumerate((out0, out1, out2, out3)):
-        first = pl.multiple_of(partner_chip(0, core, op, SMALL_NEAR) * rows, rows)
-        out[...] = flat(mixed[pl.ds(first, rows)]).astype(BF16)
+        mixed[pl.ds(c, NEAR * rows, stride=count), :] = nt(left, right)
+    for step, out in enumerate((out0, out1, out2, out3)):
+        out[...] = mixed[step * block : (step + 1) * block].astype(BF16)
 
 
 def pick_kernel(*refs):
@@ -424,8 +423,8 @@
     rows, width, cols = stream_ref.shape
     chip, core = where_ref[1], where_ref[2]
     size = width // NEAR
-    for op, block in enumerate((in0, in1, in2, in3)):
-        came[:, partner_chip(chip, core, op, SMALL_NEAR) & (NEAR - 1)] = block[...].astype(F32).reshape(rows, size, cols)
+    for step, block in zip(NEAR_STEPS, (in0, in1, in2, in3)):
+        came[:, (chip ^ step) & (NEAR - 1)] = block[...].astype(F32).reshape(rows, size, cols)
     present = present_ref[...].astype(F32)
     for row in range(0, rows, 2):
         streams = update(came, row, stream_ref, gate_ref, out_weight_ref[0])
@@ -434,15 +433,14 @@
             next_ref[row + at] = streams[at]
             lives.append(present * flag_ref[where_ref[0] + row + at].astype(F32))
         sides(streams, proj_ref[1], lives, next_gate_ref, lefts, rights, row)
-    size = width // (2 * OPS)
-    block = size * rows
+    block = width // (2 * OPS) * rows
     for op, mine in enumerate((mine0, mine1, mine2, mine3)):
         for at, side in enumerate((lefts, rights)):
-            first = pl.multiple_of(partner_chip(chip, core, op) * size, size)
-            mine[at * block : (at + 1) * block] = flat(side[pl.ds(first, size)]).astype(BF16)
-            first = pl.multiple_of(partner_chip(chip, 1 - core, op) * size, size)
+            first = pl.multiple_of(partner_chip(chip, core, op) * block, block)
+            mine[at * block : (at + 1) * block] = side[pl.ds(first, block), :].astype(BF16)
+            first = pl.multiple_of(partner_chip(chip, 1 - core, op) * block, block)
             place = (op * 2 + at) * block
-            theirs_ref[place : place + block] = flat(side[pl.ds(first, size)]).astype(BF16)
+            theirs_ref[place : place + block] = side[pl.ds(first, block), :].astype(BF16)
 
 
 def mix_cols_kernel(where_ref, came0, came1, came2, came3, mine_ref, theirs_ref, lefts, rights, partial):
@@ -457,13 +455,14 @@
     for c in range(count):
         left = flat(lefts[:, c]).astype(BF16)
         right = flat(rights[:, c]).astype(BF16)
-        partial[:, c, :] = tn(left, right)
+        partial[pl.ds(c, partial.shape[0] // count, stride=count), :] = tn(left, right)
     for op in range(OPS):
         for half in range(2):
-            to = (partner_chip(chip, core, op, SMALL_SPLIT) * 2 + (core ^ half)) * rows
-            mine_ref[op, half * block : (half + 1) * block] = flat(partial[pl.ds(to, rows)])
-            to = (partner_chip(chip, 1 - core, op, SMALL_SPLIT) * 2 + ((1 - core) ^ half)) * rows
-            theirs_ref[op, half * block : (half + 1) * block] = flat(partial[pl.ds(to, rows)])
+            to = pl.multiple_of((partner_chip(chip, core, op, SMALL_SPLIT) * 2 + (core ^ half)) * block, block)
+            mine_ref[op, half * block : (half + 1) * block] = partial[pl.ds(to, block), :]
+            to = partner_chip(chip, 1 - core, op, SMALL_SPLIT) * 2 + ((1 - core) ^ half)
+            to = pl.multiple_of(to * block, block)
+            theirs_ref[op, half * block : (half + 1) * block] = partial[pl.ds(to, block), :]
 
 
 def sum_kernel(mine_ref, got_ref, *outs):
@@ -549,7 +548,7 @@
         project_kernel,
         [((pay_rows, LANES), BF16), ((2 * rows * half, LANES), BF16), ((rows, LANES), F32)],
         homolog_features.astype(F32), homolog_to_sides_matrix.T, live,
-        scratch=[((rows, half // 2, LANES), F32), ((pay_rows, LANES), F32)],
+        scratch=[((rows * half // 2, LANES), F32), ((pay_rows, LANES), F32)],
     )
     far_z = chip_permute(pay, 4)
     base, outer_t, proj_t, out_t = run(
@@ -563,7 +562,7 @@
         where, residue_chain_index, residue_chain_index.reshape(1, cols), pairwise_state,
         relative_offset_table, outer_mean_output_weight, triangle_projection_weight, triangle_output_weight,
         smem=(0, 1),
-        scratch=[((LANES, width), F32), ((half, half, width), F32)],
+        scratch=[((LANES, width), F32), ((half * half, width), F32)],
     )
     along_z = jnp.stack([pay, far_z])
     along_z, base, outer_t, proj_t, out_t = lax.optimization_barrier((along_z, base, outer_t, proj_t, out_t))
@@ -582,8 +581,8 @@
         scratch=[
             ((16, pay_rows, LANES), F32),
             ((rows // 2, half * half, 2 * cols), BF16),
-            ((width, rows, cols), F32),
-            ((width, rows, cols), F32),
+            ((tall, cols), F32),
+            ((tall, cols), F32),
         ],
         flops=4 * 10**9,
     )
@@ -599,10 +598,10 @@
         scratch=[
             ((NEAR, width // NEAR, rows, cols), F32),
             ((16, width // NEAR, rows, cols), F32),
-            ((NEAR * rows, width // NEAR, cols), F32),
+            ((tall, cols), F32),
         ],
     )
-    mixed = split_exchange(mixed[: NEAR - 1], SMALL_NEAR) + [mixed[NEAR - 1]]
+    mixed = exchange(mixed, NEAR_STEPS)
     made = run(
         between_kernel,
         [((rows, width, cols), F32)] * 2 + [((2 * all_, cols), BF16)] * OPS + [((2 * OPS * all_, cols), BF16)],
@@ -610,8 +609,8 @@
         smem=(0, 1),
         scratch=[
             ((rows, NEAR, width // NEAR, cols), F32),
-            ((width, rows, cols), F32),
-            ((width, rows, cols), F32),
+            ((tall, cols), F32),
+            ((tall, cols), F32),
         ],
     )
     stream, gate, theirs = made[0], made[1], made[6]
@@ -624,7 +623,7 @@
         scratch=[
             ((2 * OPS, width // (2 * OPS), rows, cols), F32),
             ((2 * OPS, width // (2 * OPS), rows, cols), F32),
-            ((16 * rows, width // (2 * OPS), cols), F32),
+            ((2 * tall, cols), F32),
         ],
     )
     mixed = run(sum_kernel, [((2 * all_, cols), BF16)] * OPS, mine, core_permute(theirs))

time: 90.4 us -> 88.9 us (0.983)
  Pallas kernels: 13.5 us -> 12 us
  waiting for transfers between devices: 36.3 us -> 35.2 us
  starting transfers between devices: 37.3 us -> 38.3 us
    ppermute x13 -> x10, waiting for transfers between devices: 19.3 us -> 15.3 us  [split_permute(): lax.ppermute(block, 'wide', [(w, w ^ 2 * steps[w % 2]) for w in range(cou...]
    ppermute x6 -> x9, starting transfers between devices: 10.8 us -> 14.4 us  [chip_permute(): lax.ppermute(block, 'wide', [(w, w ^ 2 * step) for w in range(count)])]
    ppermute x6 -> x9, waiting for transfers between devices: 9.83 us -> 12.8 us  [chip_permute(): lax.ppermute(block, 'wide', [(w, w ^ 2 * step) for w in range(count)])]
    ppermute x13 -> x10, starting transfers between devices: 22 us -> 19.5 us  [split_permute(): lax.ppermute(block, 'wide', [(w, w ^ 2 * steps[w % 2]) for w in range(cou...]
    pallas_call x9, Pallas kernels: 13.5 us -> 12 us  [run(): pl.pallas_call(kernel, out_shape=[jax.ShapeDtypeStruct(shape, kind) for s...]
  transfers between devices with their start and end apart: 25 -> 25, of which waited for: 19 -> 20; matrix products, arithmetic and copies ran while one was open for 0% -> 0% of each run, Pallas kernels for 2% -> 2%
where the time goes in v11:
time: 88.9 us; the launch traced here: 88.7 us
  starting transfers between devices  38.3 us (43%)
  waiting for transfers between devices  35.2 us (40%)
  Pallas kernels  12 us (13%)
  local copies, waits for them, and re-layouts  1.47 us (2%)
  other arithmetic  1.38 us (2%)
    ppermute x10, starting transfers between devices, split_permute(): lax.ppermute(block, 'wide', [(w, w ^ 2 * steps[w % 2]) for w in range(cou...  19.5 us
    ppermute x10, waiting for transfers between devices, split_permute(): lax.ppermute(block, 'wide', [(w, w ^ 2 * steps[w % 2]) for w in range(cou...  15.3 us
    ppermute x9, starting transfers between devices, chip_permute(): lax.ppermute(block, 'wide', [(w, w ^ 2 * step) for w in range(count)])  14.4 us
    ppermute x9, waiting for transfers between devices, chip_permute(): lax.ppermute(block, 'wide', [(w, w ^ 2 * step) for w in range(count)])  12.8 us
    pallas_call x9, Pallas kernels, run(): pl.pallas_call(kernel, out_shape=[jax.ShapeDtypeStruct(shape, kind) for s...  12 us
    ppermute x6, waiting for transfers between devices, core_permute(): return lax.ppermute(block, 'wide', [(w, w ^ 1) for w in range(count)])  7.15 us
    ppermute x6, starting transfers between devices, core_permute(): return lax.ppermute(block, 'wide', [(w, w ^ 1) for w in range(count)])  4.44 us
  transfers between devices with their start and end apart: 25, of which 20 were waited for; matrix products, arithmetic and copies ran while one was open for 0% of the time, Pallas kernels for 2%

profile of v11, /device:TPU:0, one launch (start us, length us, event | category | flops | bytes accessed | tf_op | source)
XLA Modules:
  0.0 88.7 jit_solution(6792059311250066552)
XLA Ops:
  0.0 0.7 copy-done.7
  0.7 0.1 dynamic-slice_convert_fusion
  0.7 0.1 multiply_bitcast_fusion
  0.8 0.1 pad_maximum_fusion.8.live_in_ref
  0.9 1.0 %convert_element_type.10.feat_ref = f32[64,8,256]{2,1,0:T(8,128)S(1)} convert(bf16[64,8,256]{2,1,0:T(8,128)(2,1)} %param.11) | non-fusion elementwise | flops 131072 | bytes 786432 | tf_op jit(solution)/shard_map/convert_element_type | solution.py:550
  1.9 0.0 copy-start
  1.9 0.0 copy-start.1
  1.9 0.0 copy-start.2
  1.9 0.0 copy-start.3
  1.9 1.0 %shard_map.100 = (bf16[144,128]{1,0:T(8,128)(2,1)S(1)}, bf16[512,128]{1,0:T(8,128)(2,1)S(1)}, f32[8,128]{1,0:T(8,128)S(1)}) custom-call(f32[64,8,256]{2,1,0:T(8,128)S(1)} %convert_element_type.10.feat_ref, bf16[64,256]{1,0:T(8,128)(2,1)S(1)} %bitcast.11, f32[8,128]{1,0:T(8,128)S(1)} %pad_maximum_fusion.8.live_in_ref), custom_call_target="tpu_custom_call" | custom-call | flops 1500000000 | bytes 561152 | tf_op jit(solution)/shard_map/pallas_call | solution.py:216
  2.9 4.1 %collective-permute-start = (bf16[144,128]{1,0:T(8,128)(2,1)S(1)}, bf16[144,128]{1,0:T(8,128)(2,1)S(1)}, u32[]{:S(2)}, u32[]{:S(2)}) collective-permute-start(bf16[144,128]{1,0:T(8,128)(2,1)S(1)} %get-tuple-element.43), channel_id=1, source_target_pairs={{0,8},{1,9},{2,10},{3,11},{4,12},{5,13},{6,14},{7,15},{8,0},{9,1},... | collective-permute-start | bytes 110600 | tf_op jit(solution)/shard_map/ppermute | solution.py:495
  7.0 0.1 pad_add_fusion.where_ref
  7.1 0.6 copy-done.5
  7.7 0.0 copy-done.6
  7.7 1.7 %shard_map.101 = (f32[8,128,128]{2,1,0:T(8,128)S(1)}, bf16[128,1024]{1,0:T(8,128)(2,1)S(1)}, bf16[2,640,128]{2,1,0:T(8,128)(2,1)S(1)}, bf16[2,128,128]{2,1,0:T(8,128)(2,1)S(1)}) custom-call(s32[3]{0:T(128)S(1)} %pad_add_fusion.where_ref, s32[128]{0:T(128)S(1)} %copy-done.6, s32[1,128]{1,0:T(1,128)S(1)} %bitcast.12, bf16[8,128,128]{2,1,0:T(8,128)(2,1)S(1)} %copy-done.1, ...), custom_call_target="tpu_custom_call" | custom-call | flops 1500000000 | bytes 935436 | tf_op jit(solution)/shard_map/pallas_call | solution.py:216
  9.5 1.6 %collective-permute-start.1 = (bf16[2,144,128]{2,1,0:T(8,128)(2,1)S(1)}, bf16[2,144,128]{2,1,0:T(8,128)(2,1)S(1)}, u32[]{:S(2)}, u32[]{:S(2)}) collective-permute-start(bf16[2,144,128]{2,1,0:T(8,128)(2,1)S(1)} %pad_maximum_fusion.7), channel_id=1, source_target_pairs={{0,4},{1,5},{2,6},{3,7},{4,0},{5,1},{6,2},{7,3},{8,12},{9,13},{10,... | collective-permute-start | bytes 221192 | tf_op jit(solution)/shard_map/ppermute | solution.py:495
  11.1 2.8 %collective-permute-done.1 = bf16[2,144,128]{2,1,0:T(8,128)(2,1)S(1)} collective-permute-done((bf16[2,144,128]{2,1,0:T(8,128)(2,1)S(1)}, bf16[2,144,128]{2,1,0:T(8,128)(2,1)S(1)}, u32[]{:S(2)}, u32[]{:S(2)}) %collective-permute-start.1) | collective-permute-done | bytes 73760 | tf_op jit(solution)/shard_map/ppermute | solution.py:495
  13.9 1.6 %collective-permute-start.2 = (bf16[4,144,128]{2,1,0:T(8,128)(2,1)S(1)}, bf16[4,144,128]{2,1,0:T(8,128)(2,1)S(1)}, u32[]{:S(2)}, u32[]{:S(2)}) collective-permute-start(bf16[4,144,128]{2,1,0:T(8,128)(2,1)S(1)} %pad_maximum_fusion), channel_id=1, source_target_pairs={{0,2},{1,3},{2,0},{3,1},{4,6},{5,7},{6,4},{7,5},{8,10},{9,11},{10,... | collective-permute-start | bytes 442376 | tf_op jit(solution)/shard_map/ppermute | solution.py:495
  15.6 3.6 %collective-permute-done.2 = bf16[4,144,128]{2,1,0:T(8,128)(2,1)S(1)} collective-permute-done((bf16[4,144,128]{2,1,0:T(8,128)(2,1)S(1)}, bf16[4,144,128]{2,1,0:T(8,128)(2,1)S(1)}, u32[]{:S(2)}, u32[]{:S(2)}) %collective-permute-start.2) | collective-permute-done | bytes 147488 | tf_op jit(solution)/shard_map/ppermute | solution.py:495
  19.2 0.1 collective-permute-start.3
  19.2 1.6 %collective-permute-done.3.other_ref = bf16[8,144,128]{2,1,0:T(8,128)(2,1)S(1)} collective-permute-done((bf16[8,144,128]{2,1,0:T(8,128)(2,1)S(1)}, bf16[8,144,128]{2,1,0:T(8,128)(2,1)S(1)}, u32[]{:S(2)}, u32[]{:S(2)}) %collective-permute-start.3) | collective-permute-done | bytes 294944 | tf_op jit(solution)/shard_map/ppermute | solution.py:521
  20.8 2.7 %shard_map.102 = (f32[8,128,128]{2,1,0:T(8,128)S(1)}, f32[8,128,128]{2,1,0:T(8,128)S(1)}, bf16[256,128]{1,0:T(8,128)(2,1)S(1)}, bf16[256,128]{1,0:T(8,128)(2,1)S...) custom-call(s32[3]{0:T(128)S(1)} %pad_add_fusion.where_ref, ...), custom_call_target="tpu_custom_call" | custom-call | flops 4000000000 | bytes 1840140 | tf_op jit(solution)/shard_map/pallas_call | solution.py:216
  23.6 0.2 collective-permute-start.7
  23.8 2.5 %collective-permute-start.4 = (bf16[512,128]{1,0:T(8,128)(2,1)S(1)}, bf16[512,128]{1,0:T(8,128)(2,1)S(1)}, u32[]{:S(2)}, u32[]{:S(2)}) collective-permute-start(bf16[512,128]{1,0:T(8,128)(2,1)S(1)} %get-tuple-element.54), channel_id=1, source_target_pairs={{0,6},{1,7},{2,4},{3,5},{4,2},{5,3},{6,0},{7,1},{8,14},{9,15},{10,... | collective-permute-start | bytes 393224 | tf_op jit(solution)/shard_map/ppermute | solution.py:495
  26.3 0.5 collective-permute-start.5
  26.8 0.5 collective-permute-start.6
  27.3 4.7 %collective-permute-start.8 = (bf16[512,128]{1,0:T(8,128)(2,1)S(1)}, bf16[512,128]{1,0:T(8,128)(2,1)S(1)}, u32[]{:S(2)}, u32[]{:S(2)}) collective-permute-start(bf16[512,128]{1,0:T(8,128)(2,1)S(1)} %pad_maximum_fusion.1), channel_id=1, source_target_pairs={{0,14},{1,11},{2,12},{3,9},{4,10},{5,15},{6,8},{7,13},{8,6},{9,3},... | collective-permute-start | bytes 393224 | tf_op jit(solution)/shard_map/ppermute | solution.py:504
  32.0 0.3 collective-permute-start.9
  32.3 3.2 %collective-permute-done.5.near1 = bf16[512,128]{1,0:T(8,128)(2,1)S(1)} collective-permute-done((bf16[512,128]{1,0:T(8,128)(2,1)S(1)}, bf16[512,128]{1,0:T(8,128)(2,1)S(1)}, u32[]{:S(2)}, u32[]{:S(2)}) %collective-permute-start.5) | collective-permute-done | bytes 131104 | tf_op jit(solution)/shard_map/ppermute | solution.py:495
  35.6 3.0 %collective-permute-done.8.far0 = bf16[512,128]{1,0:T(8,128)(2,1)S(1)} collective-permute-done((bf16[512,128]{1,0:T(8,128)(2,1)S(1)}, bf16[512,128]{1,0:T(8,128)(2,1)S(1)}, u32[]{:S(2)}, u32[]{:S(2)}) %collective-permute-start.8) | collective-permute-done | bytes 131104 | tf_op jit(solution)/shard_map/ppermute | solution.py:504
  38.6 2.3 %collective-permute-done.9.far1 = bf16[512,128]{1,0:T(8,128)(2,1)S(1)} collective-permute-done((bf16[512,128]{1,0:T(8,128)(2,1)S(1)}, bf16[512,128]{1,0:T(8,128)(2,1)S(1)}, u32[]{:S(2)}, u32[]{:S(2)}) %collective-permute-start.9) | collective-permute-done | bytes 131104 | tf_op jit(solution)/shard_map/ppermute | solution.py:504
  40.9 1.0 %collective-permute-start.10 = (bf16[2048,128]{1,0:T(8,128)(2,1)S(1)}, bf16[2048,128]{1,0:T(8,128)(2,1)S(1)}, u32[]{:S(2)}, u32[]{:S(2)}) collective-permute-start(bf16[2048,128]{1,0:T(8,128)(2,1)S(1)} %constant_dynamic-update-slice_fusion.3), channel_id=1, source_target_pairs={{0,1},{1,0},{2,3},{3,2},{4,5},{5,4},{6,7},{7,6},{8,9},{9,8},{10,11... | collective-permute-start | bytes 1572872 | tf_op jit(solution)/shard_map/ppermute | solution.py:521
  41.9 1.5 %collective-permute-done.10.other_ref = bf16[2048,128]{1,0:T(8,128)(2,1)S(1)} collective-permute-done((bf16[2048,128]{1,0:T(8,128)(2,1)S(1)}, bf16[2048,128]{1,0:T(8,128)(2,1)S(1)}, u32[]{:S(2)}, u32[]{:S(2)}) %collective-permute-start.10) | collective-permute-done | bytes 524320 | tf_op jit(solution)/shard_map/ppermute | solution.py:521
  43.4 1.4 %shard_map.103 = (bf16[256,128]{1,0:T(8,128)(2,1)S(1)}, bf16[256,128]{1,0:T(8,128)(2,1)S(1)}, bf16[256,128]{1,0:T(8,128)(2,1)S(1)}, bf16[256,128]{1,0:T(8,128)(2,1)S(1)}) custom-call(s32[3]{0:T(128)S(1)} %pad_add_fusion.where_ref, bf16[512,128]{1,0:T(8,128)(2,1)S(1)} %collective-permute-done.4.near0, bf16[512,128]{1,0:T(8,128)(2,1)S(1)} %collective-permute-done.5.near1, ...), custom_call_target="tpu_custom_call" | custom-call | flops 1500000000 | bytes 1310732 | tf_op jit(solution)/shard_map/pallas_call | solution.py:216
  44.9 2.0 %collective-permute-start.11 = (bf16[256,128]{1,0:T(8,128)(2,1)S(1)}, bf16[256,128]{1,0:T(8,128)(2,1)S(1)}, u32[]{:S(2)}, u32[]{:S(2)}) collective-permute-start(bf16[256,128]{1,0:T(8,128)(2,1)S(1)} %get-tuple-element.61), channel_id=1, source_target_pairs={{0,6},{1,7},{2,4},{3,5},{4,2},{5,3},{6,0},{7,1},{8,14},{9,15},{10,... | collective-permute-start | bytes 196616 | tf_op jit(solution)/shard_map/ppermute | solution.py:495
  46.9 0.1 collective-permute-start.12
  47.0 1.5 %collective-permute-start.13 = (bf16[256,128]{1,0:T(8,128)(2,1)S(1)}, bf16[256,128]{1,0:T(8,128)(2,1)S(1)}, u32[]{:S(2)}, u32[]{:S(2)}) collective-permute-start(bf16[256,128]{1,0:T(8,128)(2,1)S(1)} %get-tuple-element.63), channel_id=1, source_target_pairs={{0,2},{1,3},{2,0},{3,1},{4,6},{5,7},{6,4},{7,5},{8,10},{9,11},{10,... | collective-permute-start | bytes 196616 | tf_op jit(solution)/shard_map/ppermute | solution.py:495
  48.5 1.8 %collective-permute-done.11.in0 = bf16[256,128]{1,0:T(8,128)(2,1)S(1)} collective-permute-done((bf16[256,128]{1,0:T(8,128)(2,1)S(1)}, bf16[256,128]{1,0:T(8,128)(2,1)S(1)}, u32[]{:S(2)}, u32[]{:S(2)}) %collective-permute-start.11) | collective-permute-done | bytes 65568 | tf_op jit(solution)/shard_map/ppermute | solution.py:495
  50.3 0.8 collective-permute-done.12.in1
  51.2 0.5 collective-permute-done.13.in2
  51.6 1.7 %shard_map.104 = (f32[8,128,128]{2,1,0:T(8,128)S(1)}, f32[8,128,128]{2,1,0:T(8,128)S(1)}, bf16[256,128]{1,0:T(8,128)(2,1)S(1)}, bf16[256,128]{1,0:T(8,128)(2,1)S...) custom-call(s32[3]{0:T(128)S(1)} %pad_add_fusion.where_ref, ...), custom_call_target="tpu_custom_call" | custom-call | flops 1500000000 | bytes 1704972 | tf_op jit(solution)/shard_map/pallas_call | solution.py:216
  53.3 0.1 collective-permute-start.14
  53.4 1.5 %collective-permute-done.14 = bf16[1024,128]{1,0:T(8,128)(2,1)S(1)} collective-permute-done((bf16[1024,128]{1,0:T(8,128)(2,1)S(1)}, bf16[1024,128]{1,0:T(8,128)(2,1)S(1)}, u32[]{:S(2)}, u32[]{:S(2)}) %collective-permute-start.14) | collective-permute-done | bytes 262176 | tf_op jit(solution)/shard_map/ppermute | solution.py:521
  55.0 4.6 %collective-permute-start.15 = (bf16[512,128]{1,0:T(8,128)(2,1)S(1)}, bf16[512,128]{1,0:T(8,128)(2,1)S(1)}, u32[]{:S(2)}, u32[]{:S(2)}) collective-permute-start(bf16[512,128]{1,0:T(8,128)(2,1)S(1)} %pad_maximum_fusion.3), channel_id=1, source_target_pairs={{0,14},{1,11},{2,12},{3,9},{4,10},{5,15},{6,8},{7,13},{8,6},{9,3},... | collective-permute-start | bytes 393224 | tf_op jit(solution)/shard_map/ppermute | solution.py:504
  59.6 0.1 collective-permute-start.16
  59.7 0.6 collective-permute-start.17
  60.3 3.2 %collective-permute-start.18 = (bf16[512,128]{1,0:T(8,128)(2,1)S(1)}, bf16[512,128]{1,0:T(8,128)(2,1)S(1)}, u32[]{:S(2)}, u32[]{:S(2)}) collective-permute-start(bf16[512,128]{1,0:T(8,128)(2,1)S(1)} %pad_maximum_fusion.6), channel_id=1, source_target_pairs={{0,2},{1,1},{2,0},{3,3},{4,6},{5,5},{6,4},{7,7},{8,10},{9,9},{10,8... | collective-permute-start | bytes 393224 | tf_op jit(solution)/shard_map/ppermute | solution.py:504
  63.5 0.2 collective-permute-done.15.came0
  63.7 3.9 %collective-permute-done.16.came1 = bf16[512,128]{1,0:T(8,128)(2,1)S(1)} collective-permute-done((bf16[512,128]{1,0:T(8,128)(2,1)S(1)}, bf16[512,128]{1,0:T(8,128)(2,1)S(1)}, u32[]{:S(2)}, u32[]{:S(2)}) %collective-permute-start.16) | collective-permute-done | bytes 131104 | tf_op jit(solution)/shard_map/ppermute | solution.py:504
  67.6 0.7 collective-permute-done.17.came2
  68.3 0.2 collective-permute-done.18.came3
  68.5 1.2 %shard_map.105 = (f32[4,256,128]{2,1,0:T(8,128)S(1)}, f32[4,256,128]{2,1,0:T(8,128)S(1)}) custom-call(s32[3]{0:T(128)S(1)} %pad_add_fusion.where_ref, bf16[512,128]{1,0:T(8,128)(2,1)S(1)} %collective-permute-done.15.came0, bf16[512,128]{1,0:T(8,128)(2,1)S(1)} %collective-permute-done.16.came1, bf16[512,128]{1,0:T(8,128)(2,1)S(1)} %collective-permute-done.17.came2, ...), custom_call_target="tpu_custom_call" | custom-call | flops 1500000000 | bytes 524300 | tf_op jit(solution)/shard_map/pallas_call | solution.py:216
  69.7 1.4 %collective-permute-start.19 = (f32[4,256,128]{2,1,0:T(8,128)S(1)}, f32[4,256,128]{2,1,0:T(8,128)S(1)}, u32[]{:S(2)}, u32[]{:S(2)}) collective-permute-start(f32[4,256,128]{2,1,0:T(8,128)S(1)} %get-tuple-element.74), channel_id=1, source_target_pairs={{0,1},{1,0},{2,3},{3,2},{4,5},{5,4},{6,7},{7,6},{8,9},{9,8},{10,11... | collective-permute-start | bytes 1572872 | tf_op jit(solution)/shard_map/ppermute | solution.py:521
  71.1 1.5 %collective-permute-done.19.got_ref = f32[4,256,128]{2,1,0:T(8,128)S(1)} collective-permute-done((f32[4,256,128]{2,1,0:T(8,128)S(1)}, f32[4,256,128]{2,1,0:T(8,128)S(1)}, u32[]{:S(2)}, u32[]{:S(2)}) %collective-permute-start.19) | collective-permute-done | bytes 524320 | tf_op jit(solution)/shard_map/ppermute | solution.py:521
  72.7 4.5 %collective-permute-start.20 = (bf16[256,128]{1,0:T(8,128)(2,1)S(1)}, bf16[256,128]{1,0:T(8,128)(2,1)S(1)}, u32[]{:S(2)}, u32[]{:S(2)}) collective-permute-start(bf16[256,128]{1,0:T(8,128)(2,1)S(1)} %get-tuple-element.75), channel_id=1, source_target_pairs={{0,14},{1,7},{2,12},{3,5},{4,10},{5,3},{6,8},{7,1},{8,6},{9,15},{1... | collective-permute-start | bytes 196616 | tf_op jit(solution)/shard_map/ppermute | solution.py:504
  77.2 0.6 collective-permute-start.21
  77.8 0.3 collective-permute-start.22
  78.1 0.7 collective-permute-start.23
  78.7 1.1 %collective-permute-done.20.refs_0_.came0 = bf16[256,128]{1,0:T(8,128)(2,1)S(1)} collective-permute-done((bf16[256,128]{1,0:T(8,128)(2,1)S(1)}, bf16[256,128]{1,0:T(8,128)(2,1)S(1)}, u32[]{:S(2)}, u32[]{:S(2)}) %collective-permute-start.20) | collective-permute-done | bytes 65568 | tf_op jit(solution)/shard_map/ppermute | solution.py:504
  79.8 2.3 %collective-permute-done.21.refs_1_.came1 = bf16[256,128]{1,0:T(8,128)(2,1)S(1)} collective-permute-done((bf16[256,128]{1,0:T(8,128)(2,1)S(1)}, bf16[256,128]{1,0:T(8,128)(2,1)S(1)}, u32[]{:S(2)}, u32[]{:S(2)}) %collective-permute-start.21) | collective-permute-done | bytes 65568 | tf_op jit(solution)/shard_map/ppermute | solution.py:504
  82.2 1.7 %collective-permute-done.22.refs_2_.came2 = bf16[256,128]{1,0:T(8,128)(2,1)S(1)} collective-permute-done((bf16[256,128]{1,0:T(8,128)(2,1)S(1)}, bf16[256,128]{1,0:T(8,128)(2,1)S(1)}, u32[]{:S(2)}, u32[]{:S(2)}) %collective-permute-start.22) | collective-permute-done | bytes 65568 | tf_op jit(solution)/shard_map/ppermute | solution.py:504
  83.9 1.6 %collective-permute-start.24 = (bf16[512,128]{1,0:T(8,128)(2,1)S(1)}, bf16[512,128]{1,0:T(8,128)(2,1)S(1)}, u32[]{:S(2)}, u32[]{:S(2)}) collective-permute-start(bf16[512,128]{1,0:T(8,128)(2,1)S(1)} %shard_map.107), channel_id=1, source_target_pairs={{0,1},{1,0},{2,3},{3,2},{4,5},{5,4},{6,7},{7,6},{8,9},{9,8},{10,11... | collective-permute-start | bytes 393224 | tf_op jit(solution)/shard_map/ppermute | solution.py:521
  85.5 1.0 %collective-permute-done.24.other_ref = bf16[512,128]{1,0:T(8,128)(2,1)S(1)} collective-permute-done((bf16[512,128]{1,0:T(8,128)(2,1)S(1)}, bf16[512,128]{1,0:T(8,128)(2,1)S(1)}, u32[]{:S(2)}, u32[]{:S(2)}) %collective-permute-start.24) | collective-permute-done | bytes 131104 | tf_op jit(solution)/shard_map/ppermute | solution.py:521
  86.5 2.2 %shard_map.108 = bf16[8,128,128]{2,1,0:T(8,128)(2,1)} custom-call(s32[3]{0:T(128)S(1)} %pad_add_fusion.where_ref, bf16[256,128]{1,0:T(8,128)(2,1)S(1)} %collective-permute-done.20.refs_0_.came0, bf16[256,128]{1,0:T(8,128)(2,1)S(1)} %collective-permute-done.21.refs_1_.came1, bf16[256,128]{1,0:T(8,128)(2,1)S(1)} %collective-permute-done.22.refs_2_.came2, ...), custom_call_target="tpu_custom_call" | custom-call | flops 1500000000 | bytes 1507340 | tf_op jit(solution)/shard_map/pallas_call | solution.py:216
  (37 shorter events, 0.3 us)
Async XLA Ops:
  0.0 0.7 copy-start.7
  0.0 0.7 copy-start.8
  0.9 1.0 %copy-start.4 = (bf16[256,64]{0,1:T(8,128)(2,1)S(1)}, bf16[256,64]{0,1:T(8,128)(2,1)}, u32[]{:S(2)}) copy-start(bf16[256,64]{0,1:T(8,128)(2,1)} %param.16) | copy-start | bytes 98308
  1.9 5.2 %copy-start = (bf16[2,128,640]{2,1,0:T(8,128)(2,1)S(1)}, bf16[2,128,640]{2,1,0:T(8,128)(2,1)}, u32[]{:S(2)}) copy-start(bf16[2,128,640]{2,1,0:T(8,128)(2,1)} %proj_ref.1) | copy-start | bytes 983044
  1.9 5.2 %copy-start.1 = (bf16[8,128,128]{2,1,0:T(8,128)(2,1)S(1)}, bf16[8,128,128]{2,1,0:T(8,128)(2,1)}, u32[]{:S(2)}) copy-start(bf16[8,128,128]{2,1,0:T(8,128)(2,1)} %pair_ref.1) | copy-start | bytes 786436
  1.9 5.2 %copy-start.2 = (bf16[1024,128]{1,0:T(8,128)(2,1)S(1)}, bf16[1024,128]{1,0:T(8,128)(2,1)}, u32[]{:S(2)}) copy-start(bf16[1024,128]{1,0:T(8,128)(2,1)} %outer_ref.1) | copy-start | bytes 786436
  1.9 5.2 %copy-start.3 = (bf16[2,128,128]{2,1,0:T(8,128)(2,1)S(1)}, bf16[2,128,128]{2,1,0:T(8,128)(2,1)}, u32[]{:S(2)}) copy-start(bf16[2,128,128]{2,1,0:T(8,128)(2,1)} %out_ref.1) | copy-start | bytes 196612
  2.9 6.6 %collective-permute-start = (bf16[144,128]{1,0:T(8,128)(2,1)S(1)}, bf16[144,128]{1,0:T(8,128)(2,1)S(1)}, u32[]{:S(2)}, u32[]{:S(2)}) collective-permute-start(bf16[144,128]{1,0:T(8,128)(2,1)S(1)} %get-tuple-element.43), channel_id=1, source_target_pairs={{0,8},{1,9},{2,10},{3,11},{4,12},{5,13},{6,14},{7,15},{8,0},{9,1},... | collective-permute-start | bytes 110600 | tf_op jit(solution)/shard_map/ppermute | solution.py:495
  7.0 0.7 copy-start.5
  7.1 0.7 copy-start.6
  9.5 4.4 %collective-permute-start.1 = (bf16[2,144,128]{2,1,0:T(8,128)(2,1)S(1)}, bf16[2,144,128]{2,1,0:T(8,128)(2,1)S(1)}, u32[]{:S(2)}, u32[]{:S(2)}) collective-permute-start(bf16[2,144,128]{2,1,0:T(8,128)(2,1)S(1)} %pad_maximum_fusion.7), channel_id=1, source_target_pairs={{0,4},{1,5},{2,6},{3,7},{4,0},{5,1},{6,2},{7,3},{8,12},{9,13},{10,... | collective-permute-start | bytes 221192 | tf_op jit(solution)/shard_map/ppermute | solution.py:495
  13.9 5.2 %collective-permute-start.2 = (bf16[4,144,128]{2,1,0:T(8,128)(2,1)S(1)}, bf16[4,144,128]{2,1,0:T(8,128)(2,1)S(1)}, u32[]{:S(2)}, u32[]{:S(2)}) collective-permute-start(bf16[4,144,128]{2,1,0:T(8,128)(2,1)S(1)} %pad_maximum_fusion), channel_id=1, source_target_pairs={{0,2},{1,3},{2,0},{3,1},{4,6},{5,7},{6,4},{7,5},{8,10},{9,11},{10,... | collective-permute-start | bytes 442376 | tf_op jit(solution)/shard_map/ppermute | solution.py:495
  19.2 1.6 %collective-permute-start.3 = (bf16[8,144,128]{2,1,0:T(8,128)(2,1)S(1)}, bf16[8,144,128]{2,1,0:T(8,128)(2,1)S(1)}, u32[]{:S(2)}, u32[]{:S(2)}) collective-permute-start(bf16[8,144,128]{2,1,0:T(8,128)(2,1)S(1)} %constant_dynamic-update-slice_fusion.own_ref), channel_id=1, source_target_pairs={{0,1},{1,0},{2,3},{3,2},{4,5},{5,4},{6,7},{7,6},{8,9},{9,8},{10,11... | collective-permute-start | bytes 884744 | tf_op jit(solution)/shard_map/ppermute | solution.py:521
  23.6 3.7 %collective-permute-start.7 = (bf16[512,128]{1,0:T(8,128)(2,1)S(1)}, bf16[512,128]{1,0:T(8,128)(2,1)S(1)}, u32[]{:S(2)}, u32[]{:S(2)}) collective-permute-start(bf16[512,128]{1,0:T(8,128)(2,1)S(1)} %get-tuple-element.59), channel_id=1, source_target_pairs={{0,1},{1,0},{2,3},{3,2},{4,5},{5,4},{6,7},{7,6},{8,9},{9,8},{10,11... | collective-permute-start | bytes 393224 | tf_op jit(solution)/shard_map/ppermute | solution.py:521
  23.8 8.5 %collective-permute-start.4 = (bf16[512,128]{1,0:T(8,128)(2,1)S(1)}, bf16[512,128]{1,0:T(8,128)(2,1)S(1)}, u32[]{:S(2)}, u32[]{:S(2)}) collective-permute-start(bf16[512,128]{1,0:T(8,128)(2,1)S(1)} %get-tuple-element.54), channel_id=1, source_target_pairs={{0,6},{1,7},{2,4},{3,5},{4,2},{5,3},{6,0},{7,1},{8,14},{9,15},{10,... | collective-permute-start | bytes 393224 | tf_op jit(solution)/shard_map/ppermute | solution.py:495
  26.3 9.2 %collective-permute-start.5 = (bf16[512,128]{1,0:T(8,128)(2,1)S(1)}, bf16[512,128]{1,0:T(8,128)(2,1)S(1)}, u32[]{:S(2)}, u32[]{:S(2)}) collective-permute-start(bf16[512,128]{1,0:T(8,128)(2,1)S(1)} %get-tuple-element.55), channel_id=1, source_target_pairs={{0,4},{1,5},{2,6},{3,7},{4,0},{5,1},{6,2},{7,3},{8,12},{9,13},{10,... | collective-permute-start | bytes 393224 | tf_op jit(solution)/shard_map/ppermute | solution.py:495
  26.8 8.7 %collective-permute-start.6 = (bf16[512,128]{1,0:T(8,128)(2,1)S(1)}, bf16[512,128]{1,0:T(8,128)(2,1)S(1)}, u32[]{:S(2)}, u32[]{:S(2)}) collective-permute-start(bf16[512,128]{1,0:T(8,128)(2,1)S(1)} %get-tuple-element.56), channel_id=1, source_target_pairs={{0,2},{1,3},{2,0},{3,1},{4,6},{5,7},{6,4},{7,5},{8,10},{9,11},{10,... | collective-permute-start | bytes 393224 | tf_op jit(solution)/shard_map/ppermute | solution.py:495
  27.3 11.2 %collective-permute-start.8 = (bf16[512,128]{1,0:T(8,128)(2,1)S(1)}, bf16[512,128]{1,0:T(8,128)(2,1)S(1)}, u32[]{:S(2)}, u32[]{:S(2)}) collective-permute-start(bf16[512,128]{1,0:T(8,128)(2,1)S(1)} %pad_maximum_fusion.1), channel_id=1, source_target_pairs={{0,14},{1,11},{2,12},{3,9},{4,10},{5,15},{6,8},{7,13},{8,6},{9,3},... | collective-permute-start | bytes 393224 | tf_op jit(solution)/shard_map/ppermute | solution.py:504
  32.0 8.9 %collective-permute-start.9 = (bf16[512,128]{1,0:T(8,128)(2,1)S(1)}, bf16[512,128]{1,0:T(8,128)(2,1)S(1)}, u32[]{:S(2)}, u32[]{:S(2)}) collective-permute-start(bf16[512,128]{1,0:T(8,128)(2,1)S(1)} %pad_maximum_fusion.2), channel_id=1, source_target_pairs={{0,12},{1,9},{2,14},{3,11},{4,8},{5,13},{6,10},{7,15},{8,4},{9,1},... | collective-permute-start | bytes 393224 | tf_op jit(solution)/shard_map/ppermute | solution.py:504
  40.9 2.6 %collective-permute-start.10 = (bf16[2048,128]{1,0:T(8,128)(2,1)S(1)}, bf16[2048,128]{1,0:T(8,128)(2,1)S(1)}, u32[]{:S(2)}, u32[]{:S(2)}) collective-permute-start(bf16[2048,128]{1,0:T(8,128)(2,1)S(1)} %constant_dynamic-update-slice_fusion.3), channel_id=1, source_target_pairs={{0,1},{1,0},{2,3},{3,2},{4,5},{5,4},{6,7},{7,6},{8,9},{9,8},{10,11... | collective-permute-start | bytes 1572872 | tf_op jit(solution)/shard_map/ppermute | solution.py:521
  44.9 5.4 %collective-permute-start.11 = (bf16[256,128]{1,0:T(8,128)(2,1)S(1)}, bf16[256,128]{1,0:T(8,128)(2,1)S(1)}, u32[]{:S(2)}, u32[]{:S(2)}) collective-permute-start(bf16[256,128]{1,0:T(8,128)(2,1)S(1)} %get-tuple-element.61), channel_id=1, source_target_pairs={{0,6},{1,7},{2,4},{3,5},{4,2},{5,3},{6,0},{7,1},{8,14},{9,15},{10,... | collective-permute-start | bytes 196616 | tf_op jit(solution)/shard_map/ppermute | solution.py:495
  46.9 4.3 %collective-permute-start.12 = (bf16[256,128]{1,0:T(8,128)(2,1)S(1)}, bf16[256,128]{1,0:T(8,128)(2,1)S(1)}, u32[]{:S(2)}, u32[]{:S(2)}) collective-permute-start(bf16[256,128]{1,0:T(8,128)(2,1)S(1)} %get-tuple-element.62), channel_id=1, source_target_pairs={{0,4},{1,5},{2,6},{3,7},{4,0},{5,1},{6,2},{7,3},{8,12},{9,13},{10,... | collective-permute-start | bytes 196616 | tf_op jit(solution)/shard_map/ppermute | solution.py:495
  47.0 4.6 %collective-permute-start.13 = (bf16[256,128]{1,0:T(8,128)(2,1)S(1)}, bf16[256,128]{1,0:T(8,128)(2,1)S(1)}, u32[]{:S(2)}, u32[]{:S(2)}) collective-permute-start(bf16[256,128]{1,0:T(8,128)(2,1)S(1)} %get-tuple-element.63), channel_id=1, source_target_pairs={{0,2},{1,3},{2,0},{3,1},{4,6},{5,7},{6,4},{7,5},{8,10},{9,11},{10,... | collective-permute-start | bytes 196616 | tf_op jit(solution)/shard_map/ppermute | solution.py:495
  53.3 1.6 %collective-permute-start.14 = (bf16[1024,128]{1,0:T(8,128)(2,1)S(1)}, bf16[1024,128]{1,0:T(8,128)(2,1)S(1)}, u32[]{:S(2)}, u32[]{:S(2)}) collective-permute-start(bf16[1024,128]{1,0:T(8,128)(2,1)S(1)} %get-tuple-element.69), channel_id=1, source_target_pairs={{0,1},{1,0},{2,3},{3,2},{4,5},{5,4},{6,7},{7,6},{8,9},{9,8},{10,11... | collective-permute-start | bytes 786440 | tf_op jit(solution)/shard_map/ppermute | solution.py:521
  55.0 8.8 %collective-permute-start.15 = (bf16[512,128]{1,0:T(8,128)(2,1)S(1)}, bf16[512,128]{1,0:T(8,128)(2,1)S(1)}, u32[]{:S(2)}, u32[]{:S(2)}) collective-permute-start(bf16[512,128]{1,0:T(8,128)(2,1)S(1)} %pad_maximum_fusion.3), channel_id=1, source_target_pairs={{0,14},{1,11},{2,12},{3,9},{4,10},{5,15},{6,8},{7,13},{8,6},{9,3},... | collective-permute-start | bytes 393224 | tf_op jit(solution)/shard_map/ppermute | solution.py:504
  59.6 8.0 %collective-permute-start.16 = (bf16[512,128]{1,0:T(8,128)(2,1)S(1)}, bf16[512,128]{1,0:T(8,128)(2,1)S(1)}, u32[]{:S(2)}, u32[]{:S(2)}) collective-permute-start(bf16[512,128]{1,0:T(8,128)(2,1)S(1)} %pad_maximum_fusion.4), channel_id=1, source_target_pairs={{0,12},{1,9},{2,14},{3,11},{4,8},{5,13},{6,10},{7,15},{8,4},{9,1},... | collective-permute-start | bytes 393224 | tf_op jit(solution)/shard_map/ppermute | solution.py:504
  59.7 8.6 %collective-permute-start.17 = (bf16[512,128]{1,0:T(8,128)(2,1)S(1)}, bf16[512,128]{1,0:T(8,128)(2,1)S(1)}, u32[]{:S(2)}, u32[]{:S(2)}) collective-permute-start(bf16[512,128]{1,0:T(8,128)(2,1)S(1)} %pad_maximum_fusion.5), channel_id=1, source_target_pairs={{0,6},{1,5},{2,4},{3,7},{4,2},{5,1},{6,0},{7,3},{8,14},{9,13},{10,... | collective-permute-start | bytes 393224 | tf_op jit(solution)/shard_map/ppermute | solution.py:504
  60.3 8.2 %collective-permute-start.18 = (bf16[512,128]{1,0:T(8,128)(2,1)S(1)}, bf16[512,128]{1,0:T(8,128)(2,1)S(1)}, u32[]{:S(2)}, u32[]{:S(2)}) collective-permute-start(bf16[512,128]{1,0:T(8,128)(2,1)S(1)} %pad_maximum_fusion.6), channel_id=1, source_target_pairs={{0,2},{1,1},{2,0},{3,3},{4,6},{5,5},{6,4},{7,7},{8,10},{9,9},{10,8... | collective-permute-start | bytes 393224 | tf_op jit(solution)/shard_map/ppermute | solution.py:504
  69.7 3.0 %collective-permute-start.19 = (f32[4,256,128]{2,1,0:T(8,128)S(1)}, f32[4,256,128]{2,1,0:T(8,128)S(1)}, u32[]{:S(2)}, u32[]{:S(2)}) collective-permute-start(f32[4,256,128]{2,1,0:T(8,128)S(1)} %get-tuple-element.74), channel_id=1, source_target_pairs={{0,1},{1,0},{2,3},{3,2},{4,5},{5,4},{6,7},{7,6},{8,9},{9,8},{10,11... | collective-permute-start | bytes 1572872 | tf_op jit(solution)/shard_map/ppermute | solution.py:521
  72.7 7.1 %collective-permute-start.20 = (bf16[256,128]{1,0:T(8,128)(2,1)S(1)}, bf16[256,128]{1,0:T(8,128)(2,1)S(1)}, u32[]{:S(2)}, u32[]{:S(2)}) collective-permute-start(bf16[256,128]{1,0:T(8,128)(2,1)S(1)} %get-tuple-element.75), channel_id=1, source_target_pairs={{0,14},{1,7},{2,12},{3,5},{4,10},{5,3},{6,8},{7,1},{8,6},{9,15},{1... | collective-permute-start | bytes 196616 | tf_op jit(solution)/shard_map/ppermute | solution.py:504
  77.2 5.0 %collective-permute-start.21 = (bf16[256,128]{1,0:T(8,128)(2,1)S(1)}, bf16[256,128]{1,0:T(8,128)(2,1)S(1)}, u32[]{:S(2)}, u32[]{:S(2)}) collective-permute-start(bf16[256,128]{1,0:T(8,128)(2,1)S(1)} %get-tuple-element.76), channel_id=1, source_target_pairs={{0,4},{1,13},{2,6},{3,15},{4,0},{5,9},{6,2},{7,11},{8,12},{9,5},{1... | collective-permute-start | bytes 196616 | tf_op jit(solution)/shard_map/ppermute | solution.py:504
  77.8 6.1 %collective-permute-start.22 = (bf16[256,128]{1,0:T(8,128)(2,1)S(1)}, bf16[256,128]{1,0:T(8,128)(2,1)S(1)}, u32[]{:S(2)}, u32[]{:S(2)}) collective-permute-start(bf16[256,128]{1,0:T(8,128)(2,1)S(1)} %get-tuple-element.77), channel_id=1, source_target_pairs={{0,10},{1,3},{2,8},{3,1},{4,14},{5,7},{6,12},{7,5},{8,2},{9,11},{1... | collective-permute-start | bytes 196616 | tf_op jit(solution)/shard_map/ppermute | solution.py:504
  78.1 5.8 %collective-permute-start.23 = (bf16[256,128]{1,0:T(8,128)(2,1)S(1)}, bf16[256,128]{1,0:T(8,128)(2,1)S(1)}, u32[]{:S(2)}, u32[]{:S(2)}) collective-permute-start(bf16[256,128]{1,0:T(8,128)(2,1)S(1)} %get-tuple-element.78), channel_id=1, source_target_pairs={{0,0},{1,9},{2,2},{3,11},{4,4},{5,13},{6,6},{7,15},{8,8},{9,1},{10... | collective-permute-start | bytes 196616 | tf_op jit(solution)/shard_map/ppermute | solution.py:504
  83.9 2.6 %collective-permute-start.24 = (bf16[512,128]{1,0:T(8,128)(2,1)S(1)}, bf16[512,128]{1,0:T(8,128)(2,1)S(1)}, u32[]{:S(2)}, u32[]{:S(2)}) collective-permute-start(bf16[512,128]{1,0:T(8,128)(2,1)S(1)} %shard_map.107), channel_id=1, source_target_pairs={{0,1},{1,0},{2,3},{3,2},{4,5},{5,4},{6,7},{7,6},{8,9},{9,8},{10,11... | collective-permute-start | bytes 393224 | tf_op jit(solution)/shard_map/ppermute | solution.py:521

commit v12 on v11

--- a/solution.py
+++ b/solution.py
@@ -462,12 +462,12 @@
             mine_ref[op, half * block : (half + 1) * block] = partial[pl.ds(to, block), :]
             to = partner_chip(chip, 1 - core, op, SMALL_SPLIT) * 2 + ((1 - core) ^ half)
             to = pl.multiple_of(to * block, block)
-            theirs_ref[op, half * block : (half + 1) * block] = partial[pl.ds(to, block), :]
+            theirs_ref[op, half * block : (half + 1) * block] = partial[pl.ds(to, block), :].astype(BF16)
 
 
 def sum_kernel(mine_ref, got_ref, *outs):
     for op, out in enumerate(outs):
-        out[...] = (mine_ref[op] + got_ref[op]).astype(BF16)
+        out[...] = (mine_ref[op] + got_ref[op].astype(F32)).astype(BF16)
 
 
 def final_kernel(
@@ -565,9 +565,9 @@
         scratch=[((LANES, width), F32), ((half * half, width), F32)],
     )
     along_z = jnp.stack([pay, far_z])
-    along_z, base, outer_t, proj_t, out_t = lax.optimization_barrier((along_z, base, outer_t, proj_t, out_t))
     along_z = jnp.concatenate([along_z, chip_permute(along_z, 2)], axis=0)
     own = jnp.concatenate([along_z, chip_permute(along_z, 1)], axis=0)
+    own, base, outer_t, proj_t, out_t = lax.optimization_barrier((own, base, outer_t, proj_t, out_t))
     other = core_permute(own)
     tall = width * rows
     near, all_ = tall // NEAR, tall // (2 * OPS)
@@ -617,7 +617,7 @@
     came = split_exchange(with_partner(made[2:6], theirs))
     mine, theirs = run(
         mix_cols_kernel,
-        [((OPS, 2 * all_, cols), F32)] * 2,
+        [((OPS, 2 * all_, cols), F32), ((OPS, 2 * all_, cols), BF16)],
         where, *came,
         smem=(0,),
         scratch=[

time: 88.9 us -> 88.5 us (level)
  transfers between devices with their start and end apart: 25 -> 25, of which waited for: 20 -> 21; matrix products, arithmetic and copies ran while one was open for 0% -> 0% of each run, Pallas kernels for 2% -> 2%
where the time goes in v12:
time: 88.5 us; the launch traced here: 88.3 us
  starting transfers between devices  38.6 us (44%)
  waiting for transfers between devices  34.7 us (39%)
  Pallas kernels  12 us (14%)
  local copies, waits for them, and re-layouts  1.42 us (2%)
  other arithmetic  1.41 us (2%)
    ppermute x10, starting transfers between devices, split_permute(): lax.ppermute(block, 'wide', [(w, w ^ 2 * steps[w % 2]) for w in range(cou...  19.6 us
    ppermute x10, waiting for transfers between devices, split_permute(): lax.ppermute(block, 'wide', [(w, w ^ 2 * steps[w % 2]) for w in range(cou...  15.3 us
    ppermute x9, starting transfers between devices, chip_permute(): lax.ppermute(block, 'wide', [(w, w ^ 2 * step) for w in range(count)])  14.5 us
    ppermute x9, waiting for transfers between devices, chip_permute(): lax.ppermute(block, 'wide', [(w, w ^ 2 * step) for w in range(count)])  12.6 us
    pallas_call x9, Pallas kernels, run(): pl.pallas_call(kernel, out_shape=[jax.ShapeDtypeStruct(shape, kind) for s...  12 us
    ppermute x6, waiting for transfers between devices, core_permute(): return lax.ppermute(block, 'wide', [(w, w ^ 1) for w in range(count)])  6.78 us
    ppermute x6, starting transfers between devices, core_permute(): return lax.ppermute(block, 'wide', [(w, w ^ 1) for w in range(count)])  4.45 us
  transfers between devices with their start and end apart: 25, of which 21 were waited for; matrix products, arithmetic and copies ran while one was open for 0% of the time, Pallas kernels for 2%

profile of v12, /device:TPU:0, one launch (start us, length us, event | category | flops | bytes accessed | tf_op | source)
XLA Modules:
  0.0 88.3 jit_solution(14651668467833617029)
XLA Ops:
  0.0 0.7 copy-done.7
  0.7 0.1 dynamic-slice_convert_fusion
  0.7 0.1 multiply_bitcast_fusion
  0.8 0.1 pad_maximum_fusion.9.live_in_ref
  0.9 1.0 %convert_element_type.10.feat_ref = f32[64,8,256]{2,1,0:T(8,128)S(1)} convert(bf16[64,8,256]{2,1,0:T(8,128)(2,1)} %param.11) | non-fusion elementwise | flops 131072 | bytes 786432 | tf_op jit(solution)/shard_map/convert_element_type | solution.py:550
  1.9 0.0 copy-start.1
  1.9 0.0 copy-start.2
  1.9 1.0 %shard_map.100 = (bf16[144,128]{1,0:T(8,128)(2,1)S(1)}, bf16[512,128]{1,0:T(8,128)(2,1)S(1)}, f32[8,128]{1,0:T(8,128)S(1)}) custom-call(f32[64,8,256]{2,1,0:T(8,128)S(1)} %convert_element_type.10.feat_ref, bf16[64,256]{1,0:T(8,128)(2,1)S(1)} %bitcast.13, f32[8,128]{1,0:T(8,128)S(1)} %pad_maximum_fusion.9.live_in_ref), custom_call_target="tpu_custom_call" | custom-call | flops 1500000000 | bytes 561152 | tf_op jit(solution)/shard_map/pallas_call | solution.py:216
  2.9 0.0 copy-start
  2.9 4.1 %collective-permute-start = (bf16[144,128]{1,0:T(8,128)(2,1)S(1)}, bf16[144,128]{1,0:T(8,128)(2,1)S(1)}, u32[]{:S(2)}, u32[]{:S(2)}) collective-permute-start(bf16[144,128]{1,0:T(8,128)(2,1)S(1)} %get-tuple-element.43), channel_id=1, source_target_pairs={{0,8},{1,9},{2,10},{3,11},{4,12},{5,13},{6,14},{7,15},{8,0},{9,1},... | collective-permute-start | bytes 110600 | tf_op jit(solution)/shard_map/ppermute | solution.py:495
  7.0 2.3 %collective-permute-done = bf16[144,128]{1,0:T(8,128)(2,1)S(1)} collective-permute-done((bf16[144,128]{1,0:T(8,128)(2,1)S(1)}, bf16[144,128]{1,0:T(8,128)(2,1)S(1)}, u32[]{:S(2)}, u32[]{:S(2)}) %collective-permute-start) | collective-permute-done | bytes 36896 | tf_op jit(solution)/shard_map/ppermute | solution.py:495
  9.3 1.6 %collective-permute-start.1 = (bf16[2,144,128]{2,1,0:T(8,128)(2,1)S(1)}, bf16[2,144,128]{2,1,0:T(8,128)(2,1)S(1)}, u32[]{:S(2)}, u32[]{:S(2)}) collective-permute-start(bf16[2,144,128]{2,1,0:T(8,128)(2,1)S(1)} %pad_maximum_fusion.8), channel_id=1, source_target_pairs={{0,4},{1,5},{2,6},{3,7},{4,0},{5,1},{6,2},{7,3},{8,12},{9,13},{10,... | collective-permute-start | bytes 221192 | tf_op jit(solution)/shard_map/ppermute | solution.py:495
  10.9 2.8 %collective-permute-done.1 = bf16[2,144,128]{2,1,0:T(8,128)(2,1)S(1)} collective-permute-done((bf16[2,144,128]{2,1,0:T(8,128)(2,1)S(1)}, bf16[2,144,128]{2,1,0:T(8,128)(2,1)S(1)}, u32[]{:S(2)}, u32[]{:S(2)}) %collective-permute-start.1) | collective-permute-done | bytes 73760 | tf_op jit(solution)/shard_map/ppermute | solution.py:495
  13.8 1.8 %collective-permute-start.2 = (bf16[4,144,128]{2,1,0:T(8,128)(2,1)S(1)}, bf16[4,144,128]{2,1,0:T(8,128)(2,1)S(1)}, u32[]{:S(2)}, u32[]{:S(2)}) collective-permute-start(bf16[4,144,128]{2,1,0:T(8,128)(2,1)S(1)} %pad_maximum_fusion.1), channel_id=1, source_target_pairs={{0,2},{1,3},{2,0},{3,1},{4,6},{5,7},{6,4},{7,5},{8,10},{9,11},{10,... | collective-permute-start | bytes 442376 | tf_op jit(solution)/shard_map/ppermute | solution.py:495
  15.5 0.1 pad_add_fusion.where_ref
  15.7 0.6 copy-done.6
  16.3 1.7 %shard_map.101 = (f32[8,128,128]{2,1,0:T(8,128)S(1)}, bf16[128,1024]{1,0:T(8,128)(2,1)S(1)}, bf16[2,640,128]{2,1,0:T(8,128)(2,1)S(1)}, bf16[2,128,128]{2,1,0:T(8,128)(2,1)S(1)}) custom-call(s32[3]{0:T(128)S(1)} %pad_add_fusion.where_ref, s32[128]{0:T(128)S(1)} %copy-done.6, s32[1,128]{1,0:T(1,128)S(1)} %bitcast.14, bf16[8,128,128]{2,1,0:T(8,128)(2,1)S(1)} %copy-done.1, ...), custom_call_target="tpu_custom_call" | custom-call | flops 1500000000 | bytes 935436 | tf_op jit(solution)/shard_map/pallas_call | solution.py:216
  18.0 1.0 %collective-permute-done.2 = bf16[4,144,128]{2,1,0:T(8,128)(2,1)S(1)} collective-permute-done((bf16[4,144,128]{2,1,0:T(8,128)(2,1)S(1)}, bf16[4,144,128]{2,1,0:T(8,128)(2,1)S(1)}, u32[]{:S(2)}, u32[]{:S(2)}) %collective-permute-start.2) | collective-permute-done | bytes 147488 | tf_op jit(solution)/shard_map/ppermute | solution.py:495
  19.0 0.1 collective-permute-start.3
  19.1 1.6 %collective-permute-done.3.other_ref = bf16[8,144,128]{2,1,0:T(8,128)(2,1)S(1)} collective-permute-done((bf16[8,144,128]{2,1,0:T(8,128)(2,1)S(1)}, bf16[8,144,128]{2,1,0:T(8,128)(2,1)S(1)}, u32[]{:S(2)}, u32[]{:S(2)}) %collective-permute-start.3) | collective-permute-done | bytes 294944 | tf_op jit(solution)/shard_map/ppermute | solution.py:521
  20.7 2.7 %shard_map.102 = (f32[8,128,128]{2,1,0:T(8,128)S(1)}, f32[8,128,128]{2,1,0:T(8,128)S(1)}, bf16[256,128]{1,0:T(8,128)(2,1)S(1)}, bf16[256,128]{1,0:T(8,128)(2,1)S...) custom-call(s32[3]{0:T(128)S(1)} %pad_add_fusion.where_ref, ...), custom_call_target="tpu_custom_call" | custom-call | flops 4000000000 | bytes 1840140 | tf_op jit(solution)/shard_map/pallas_call | solution.py:216
  23.4 0.2 collective-permute-start.7
  23.6 2.5 %collective-permute-start.4 = (bf16[512,128]{1,0:T(8,128)(2,1)S(1)}, bf16[512,128]{1,0:T(8,128)(2,1)S(1)}, u32[]{:S(2)}, u32[]{:S(2)}) collective-permute-start(bf16[512,128]{1,0:T(8,128)(2,1)S(1)} %get-tuple-element.54), channel_id=1, source_target_pairs={{0,6},{1,7},{2,4},{3,5},{4,2},{5,3},{6,0},{7,1},{8,14},{9,15},{10,... | collective-permute-start | bytes 393224 | tf_op jit(solution)/shard_map/ppermute | solution.py:495
  26.1 0.7 collective-permute-start.5
  26.8 0.3 collective-permute-start.6
  27.2 4.8 %collective-permute-start.8 = (bf16[512,128]{1,0:T(8,128)(2,1)S(1)}, bf16[512,128]{1,0:T(8,128)(2,1)S(1)}, u32[]{:S(2)}, u32[]{:S(2)}) collective-permute-start(bf16[512,128]{1,0:T(8,128)(2,1)S(1)} %pad_maximum_fusion.2), channel_id=1, source_target_pairs={{0,14},{1,11},{2,12},{3,9},{4,10},{5,15},{6,8},{7,13},{8,6},{9,3},... | collective-permute-start | bytes 393224 | tf_op jit(solution)/shard_map/ppermute | solution.py:504
  32.0 0.3 collective-permute-start.9
  32.3 3.2 %collective-permute-done.5.near1 = bf16[512,128]{1,0:T(8,128)(2,1)S(1)} collective-permute-done((bf16[512,128]{1,0:T(8,128)(2,1)S(1)}, bf16[512,128]{1,0:T(8,128)(2,1)S(1)}, u32[]{:S(2)}, u32[]{:S(2)}) %collective-permute-start.5) | collective-permute-done | bytes 131104 | tf_op jit(solution)/shard_map/ppermute | solution.py:495
  35.6 3.0 %collective-permute-done.8.far0 = bf16[512,128]{1,0:T(8,128)(2,1)S(1)} collective-permute-done((bf16[512,128]{1,0:T(8,128)(2,1)S(1)}, bf16[512,128]{1,0:T(8,128)(2,1)S(1)}, u32[]{:S(2)}, u32[]{:S(2)}) %collective-permute-start.8) | collective-permute-done | bytes 131104 | tf_op jit(solution)/shard_map/ppermute | solution.py:504
  38.6 2.3 %collective-permute-done.9.far1 = bf16[512,128]{1,0:T(8,128)(2,1)S(1)} collective-permute-done((bf16[512,128]{1,0:T(8,128)(2,1)S(1)}, bf16[512,128]{1,0:T(8,128)(2,1)S(1)}, u32[]{:S(2)}, u32[]{:S(2)}) %collective-permute-start.9) | collective-permute-done | bytes 131104 | tf_op jit(solution)/shard_map/ppermute | solution.py:504
  40.9 1.0 %collective-permute-start.10 = (bf16[2048,128]{1,0:T(8,128)(2,1)S(1)}, bf16[2048,128]{1,0:T(8,128)(2,1)S(1)}, u32[]{:S(2)}, u32[]{:S(2)}) collective-permute-start(bf16[2048,128]{1,0:T(8,128)(2,1)S(1)} %constant_dynamic-update-slice_fusion), channel_id=1, source_target_pairs={{0,1},{1,0},{2,3},{3,2},{4,5},{5,4},{6,7},{7,6},{8,9},{9,8},{10,11... | collective-permute-start | bytes 1572872 | tf_op jit(solution)/shard_map/ppermute | solution.py:521
  41.9 1.5 %collective-permute-done.10.other_ref = bf16[2048,128]{1,0:T(8,128)(2,1)S(1)} collective-permute-done((bf16[2048,128]{1,0:T(8,128)(2,1)S(1)}, bf16[2048,128]{1,0:T(8,128)(2,1)S(1)}, u32[]{:S(2)}, u32[]{:S(2)}) %collective-permute-start.10) | collective-permute-done | bytes 524320 | tf_op jit(solution)/shard_map/ppermute | solution.py:521
  43.5 1.4 %shard_map.103 = (bf16[256,128]{1,0:T(8,128)(2,1)S(1)}, bf16[256,128]{1,0:T(8,128)(2,1)S(1)}, bf16[256,128]{1,0:T(8,128)(2,1)S(1)}, bf16[256,128]{1,0:T(8,128)(2,1)S(1)}) custom-call(s32[3]{0:T(128)S(1)} %pad_add_fusion.where_ref, bf16[512,128]{1,0:T(8,128)(2,1)S(1)} %collective-permute-done.4.near0, bf16[512,128]{1,0:T(8,128)(2,1)S(1)} %collective-permute-done.5.near1, ...), custom_call_target="tpu_custom_call" | custom-call | flops 1500000000 | bytes 1310732 | tf_op jit(solution)/shard_map/pallas_call | solution.py:216
  44.9 2.0 %collective-permute-start.11 = (bf16[256,128]{1,0:T(8,128)(2,1)S(1)}, bf16[256,128]{1,0:T(8,128)(2,1)S(1)}, u32[]{:S(2)}, u32[]{:S(2)}) collective-permute-start(bf16[256,128]{1,0:T(8,128)(2,1)S(1)} %get-tuple-element.61), channel_id=1, source_target_pairs={{0,6},{1,7},{2,4},{3,5},{4,2},{5,3},{6,0},{7,1},{8,14},{9,15},{10,... | collective-permute-start | bytes 196616 | tf_op jit(solution)/shard_map/ppermute | solution.py:495
  46.9 0.2 collective-permute-start.12
  47.1 1.4 %collective-permute-start.13 = (bf16[256,128]{1,0:T(8,128)(2,1)S(1)}, bf16[256,128]{1,0:T(8,128)(2,1)S(1)}, u32[]{:S(2)}, u32[]{:S(2)}) collective-permute-start(bf16[256,128]{1,0:T(8,128)(2,1)S(1)} %get-tuple-element.63), channel_id=1, source_target_pairs={{0,2},{1,3},{2,0},{3,1},{4,6},{5,7},{6,4},{7,5},{8,10},{9,11},{10,... | collective-permute-start | bytes 196616 | tf_op jit(solution)/shard_map/ppermute | solution.py:495
  48.5 1.8 %collective-permute-done.11.in0 = bf16[256,128]{1,0:T(8,128)(2,1)S(1)} collective-permute-done((bf16[256,128]{1,0:T(8,128)(2,1)S(1)}, bf16[256,128]{1,0:T(8,128)(2,1)S(1)}, u32[]{:S(2)}, u32[]{:S(2)}) %collective-permute-start.11) | collective-permute-done | bytes 65568 | tf_op jit(solution)/shard_map/ppermute | solution.py:495
  50.3 0.8 collective-permute-done.12.in1
  51.2 0.5 collective-permute-done.13.in2
  51.7 1.7 %shard_map.104 = (f32[8,128,128]{2,1,0:T(8,128)S(1)}, f32[8,128,128]{2,1,0:T(8,128)S(1)}, bf16[256,128]{1,0:T(8,128)(2,1)S(1)}, bf16[256,128]{1,0:T(8,128)(2,1)S...) custom-call(s32[3]{0:T(128)S(1)} %pad_add_fusion.where_ref, ...), custom_call_target="tpu_custom_call" | custom-call | flops 1500000000 | bytes 1704972 | tf_op jit(solution)/shard_map/pallas_call | solution.py:216
  53.3 0.1 collective-permute-start.14
  53.4 1.5 %collective-permute-done.14 = bf16[1024,128]{1,0:T(8,128)(2,1)S(1)} collective-permute-done((bf16[1024,128]{1,0:T(8,128)(2,1)S(1)}, bf16[1024,128]{1,0:T(8,128)(2,1)S(1)}, u32[]{:S(2)}, u32[]{:S(2)}) %collective-permute-start.14) | collective-permute-done | bytes 262176 | tf_op jit(solution)/shard_map/ppermute | solution.py:521
  55.0 4.6 %collective-permute-start.15 = (bf16[512,128]{1,0:T(8,128)(2,1)S(1)}, bf16[512,128]{1,0:T(8,128)(2,1)S(1)}, u32[]{:S(2)}, u32[]{:S(2)}) collective-permute-start(bf16[512,128]{1,0:T(8,128)(2,1)S(1)} %pad_maximum_fusion.4), channel_id=1, source_target_pairs={{0,14},{1,11},{2,12},{3,9},{4,10},{5,15},{6,8},{7,13},{8,6},{9,3},... | collective-permute-start | bytes 393224 | tf_op jit(solution)/shard_map/ppermute | solution.py:504
  59.6 0.1 collective-permute-start.16
  59.7 0.6 collective-permute-start.17
  60.3 3.2 %collective-permute-start.18 = (bf16[512,128]{1,0:T(8,128)(2,1)S(1)}, bf16[512,128]{1,0:T(8,128)(2,1)S(1)}, u32[]{:S(2)}, u32[]{:S(2)}) collective-permute-start(bf16[512,128]{1,0:T(8,128)(2,1)S(1)} %pad_maximum_fusion.7), channel_id=1, source_target_pairs={{0,2},{1,1},{2,0},{3,3},{4,6},{5,5},{6,4},{7,7},{8,10},{9,9},{10,8... | collective-permute-start | bytes 393224 | tf_op jit(solution)/shard_map/ppermute | solution.py:504
  63.5 0.2 collective-permute-done.15.came0
  63.7 3.9 %collective-permute-done.16.came1 = bf16[512,128]{1,0:T(8,128)(2,1)S(1)} collective-permute-done((bf16[512,128]{1,0:T(8,128)(2,1)S(1)}, bf16[512,128]{1,0:T(8,128)(2,1)S(1)}, u32[]{:S(2)}, u32[]{:S(2)}) %collective-permute-start.16) | collective-permute-done | bytes 131104 | tf_op jit(solution)/shard_map/ppermute | solution.py:504
  67.6 0.7 collective-permute-done.17.came2
  68.4 0.2 collective-permute-done.18.came3
  68.5 1.2 %shard_map.105 = (f32[4,256,128]{2,1,0:T(8,128)S(1)}, bf16[4,256,128]{2,1,0:T(8,128)(2,1)S(1)}) custom-call(s32[3]{0:T(128)S(1)} %pad_add_fusion.where_ref, bf16[512,128]{1,0:T(8,128)(2,1)S(1)} %collective-permute-done.15.came0, bf16[512,128]{1,0:T(8,128)(2,1)S(1)} %collective-permute-done.16.came1, bf16[512,128]{1,0:T(8,128)(2,1)S(1)} %collective-permute-done.17.came2, ...), custom_call_target="tpu_custom_call" | custom-call | flops 1500000000 | bytes 524300 | tf_op jit(solution)/shard_map/pallas_call | solution.py:216
  69.7 1.4 %collective-permute-start.19 = (bf16[4,256,128]{2,1,0:T(8,128)(2,1)S(1)}, bf16[4,256,128]{2,1,0:T(8,128)(2,1)S(1)}, u32[]{:S(2)}, u32[]{:S(2)}) collective-permute-start(bf16[4,256,128]{2,1,0:T(8,128)(2,1)S(1)} %get-tuple-element.74), channel_id=1, source_target_pairs={{0,1},{1,0},{2,3},{3,2},{4,5},{5,4},{6,7},{7,6},{8,9},{9,8},{10,11... | collective-permute-start | bytes 786440 | tf_op jit(solution)/shard_map/ppermute | solution.py:521
  71.1 1.2 %collective-permute-done.19.got_ref = bf16[4,256,128]{2,1,0:T(8,128)(2,1)S(1)} collective-permute-done((bf16[4,256,128]{2,1,0:T(8,128)(2,1)S(1)}, bf16[4,256,128]{2,1,0:T(8,128)(2,1)S(1)}, u32[]{:S(2)}, u32[]{:S(2)}) %collective-permute-start.19) | collective-permute-done | bytes 262176 | tf_op jit(solution)/shard_map/ppermute | solution.py:521
  72.3 0.1 shard_map.106
  72.4 4.5 %collective-permute-start.20 = (bf16[256,128]{1,0:T(8,128)(2,1)S(1)}, bf16[256,128]{1,0:T(8,128)(2,1)S(1)}, u32[]{:S(2)}, u32[]{:S(2)}) collective-permute-start(bf16[256,128]{1,0:T(8,128)(2,1)S(1)} %get-tuple-element.75), channel_id=1, source_target_pairs={{0,14},{1,7},{2,12},{3,5},{4,10},{5,3},{6,8},{7,1},{8,6},{9,15},{1... | collective-permute-start | bytes 196616 | tf_op jit(solution)/shard_map/ppermute | solution.py:504
  76.8 0.6 collective-permute-start.21
  77.4 0.3 collective-permute-start.22
  77.7 0.7 collective-permute-start.23
  78.4 1.1 %collective-permute-done.20.refs_0_.came0 = bf16[256,128]{1,0:T(8,128)(2,1)S(1)} collective-permute-done((bf16[256,128]{1,0:T(8,128)(2,1)S(1)}, bf16[256,128]{1,0:T(8,128)(2,1)S(1)}, u32[]{:S(2)}, u32[]{:S(2)}) %collective-permute-start.20) | collective-permute-done | bytes 65568 | tf_op jit(solution)/shard_map/ppermute | solution.py:504
  79.5 2.3 %collective-permute-done.21.refs_1_.came1 = bf16[256,128]{1,0:T(8,128)(2,1)S(1)} collective-permute-done((bf16[256,128]{1,0:T(8,128)(2,1)S(1)}, bf16[256,128]{1,0:T(8,128)(2,1)S(1)}, u32[]{:S(2)}, u32[]{:S(2)}) %collective-permute-start.21) | collective-permute-done | bytes 65568 | tf_op jit(solution)/shard_map/ppermute | solution.py:504
  81.8 1.7 %collective-permute-done.22.refs_2_.came2 = bf16[256,128]{1,0:T(8,128)(2,1)S(1)} collective-permute-done((bf16[256,128]{1,0:T(8,128)(2,1)S(1)}, bf16[256,128]{1,0:T(8,128)(2,1)S(1)}, u32[]{:S(2)}, u32[]{:S(2)}) %collective-permute-start.22) | collective-permute-done | bytes 65568 | tf_op jit(solution)/shard_map/ppermute | solution.py:504
  83.5 1.6 %collective-permute-start.24 = (bf16[512,128]{1,0:T(8,128)(2,1)S(1)}, bf16[512,128]{1,0:T(8,128)(2,1)S(1)}, u32[]{:S(2)}, u32[]{:S(2)}) collective-permute-start(bf16[512,128]{1,0:T(8,128)(2,1)S(1)} %shard_map.107), channel_id=1, source_target_pairs={{0,1},{1,0},{2,3},{3,2},{4,5},{5,4},{6,7},{7,6},{8,9},{9,8},{10,11... | collective-permute-start | bytes 393224 | tf_op jit(solution)/shard_map/ppermute | solution.py:521
  85.1 1.0 %collective-permute-done.24.other_ref = bf16[512,128]{1,0:T(8,128)(2,1)S(1)} collective-permute-done((bf16[512,128]{1,0:T(8,128)(2,1)S(1)}, bf16[512,128]{1,0:T(8,128)(2,1)S(1)}, u32[]{:S(2)}, u32[]{:S(2)}) %collective-permute-start.24) | collective-permute-done | bytes 131104 | tf_op jit(solution)/shard_map/ppermute | solution.py:521
  86.1 2.2 %shard_map.108 = bf16[8,128,128]{2,1,0:T(8,128)(2,1)} custom-call(s32[3]{0:T(128)S(1)} %pad_add_fusion.where_ref, bf16[256,128]{1,0:T(8,128)(2,1)S(1)} %collective-permute-done.20.refs_0_.came0, bf16[256,128]{1,0:T(8,128)(2,1)S(1)} %collective-permute-done.21.refs_1_.came1, bf16[256,128]{1,0:T(8,128)(2,1)S(1)} %collective-permute-done.22.refs_2_.came2, ...), custom_call_target="tpu_custom_call" | custom-call | flops 1500000000 | bytes 1507340 | tf_op jit(solution)/shard_map/pallas_call | solution.py:216
  (35 shorter events, 0.3 us)
Async XLA Ops:
  0.0 0.7 copy-start.7
  0.0 0.7 copy-start.8
  0.9 1.0 %copy-start.4 = (bf16[256,64]{0,1:T(8,128)(2,1)S(1)}, bf16[256,64]{0,1:T(8,128)(2,1)}, u32[]{:S(2)}) copy-start(bf16[256,64]{0,1:T(8,128)(2,1)} %param.16) | copy-start | bytes 98308
  1.9 13.7 %copy-start.1 = (bf16[8,128,128]{2,1,0:T(8,128)(2,1)S(1)}, bf16[8,128,128]{2,1,0:T(8,128)(2,1)}, u32[]{:S(2)}) copy-start(bf16[8,128,128]{2,1,0:T(8,128)(2,1)} %pair_ref.1) | copy-start | bytes 786436
  1.9 13.7 %copy-start.2 = (bf16[1024,128]{1,0:T(8,128)(2,1)S(1)}, bf16[1024,128]{1,0:T(8,128)(2,1)}, u32[]{:S(2)}) copy-start(bf16[1024,128]{1,0:T(8,128)(2,1)} %outer_ref.1) | copy-start | bytes 786436
  2.9 12.8 %copy-start = (bf16[2,128,640]{2,1,0:T(8,128)(2,1)S(1)}, bf16[2,128,640]{2,1,0:T(8,128)(2,1)}, u32[]{:S(2)}) copy-start(bf16[2,128,640]{2,1,0:T(8,128)(2,1)} %proj_ref.1) | copy-start | bytes 983044
  2.9 6.4 %collective-permute-start = (bf16[144,128]{1,0:T(8,128)(2,1)S(1)}, bf16[144,128]{1,0:T(8,128)(2,1)S(1)}, u32[]{:S(2)}, u32[]{:S(2)}) collective-permute-start(bf16[144,128]{1,0:T(8,128)(2,1)S(1)} %get-tuple-element.43), channel_id=1, source_target_pairs={{0,8},{1,9},{2,10},{3,11},{4,12},{5,13},{6,14},{7,15},{8,0},{9,1},... | collective-permute-start | bytes 110600 | tf_op jit(solution)/shard_map/ppermute | solution.py:495
  9.3 4.4 %collective-permute-start.1 = (bf16[2,144,128]{2,1,0:T(8,128)(2,1)S(1)}, bf16[2,144,128]{2,1,0:T(8,128)(2,1)S(1)}, u32[]{:S(2)}, u32[]{:S(2)}) collective-permute-start(bf16[2,144,128]{2,1,0:T(8,128)(2,1)S(1)} %pad_maximum_fusion.8), channel_id=1, source_target_pairs={{0,4},{1,5},{2,6},{3,7},{4,0},{5,1},{6,2},{7,3},{8,12},{9,13},{10,... | collective-permute-start | bytes 221192 | tf_op jit(solution)/shard_map/ppermute | solution.py:495
  10.9 4.7 %copy-start.3 = (bf16[2,128,128]{2,1,0:T(8,128)(2,1)S(1)}, bf16[2,128,128]{2,1,0:T(8,128)(2,1)}, u32[]{:S(2)}) copy-start(bf16[2,128,128]{2,1,0:T(8,128)(2,1)} %out_ref.1) | copy-start | bytes 196612
  10.9 4.7 %copy-start.5 = (bf16[66,128]{1,0:T(8,128)(2,1)S(1)}, bf16[66,128]{1,0:T(8,128)(2,1)}, u32[]{:S(2)}) copy-start(bf16[66,128]{1,0:T(8,128)(2,1)} %table_ref.1) | copy-start | bytes 50692
  13.8 5.2 %collective-permute-start.2 = (bf16[4,144,128]{2,1,0:T(8,128)(2,1)S(1)}, bf16[4,144,128]{2,1,0:T(8,128)(2,1)S(1)}, u32[]{:S(2)}, u32[]{:S(2)}) collective-permute-start(bf16[4,144,128]{2,1,0:T(8,128)(2,1)S(1)} %pad_maximum_fusion.1), channel_id=1, source_target_pairs={{0,2},{1,3},{2,0},{3,1},{4,6},{5,7},{6,4},{7,5},{8,10},{9,11},{10,... | collective-permute-start | bytes 442376 | tf_op jit(solution)/shard_map/ppermute | solution.py:495
  15.6 0.7 copy-start.6
  19.0 1.6 %collective-permute-start.3 = (bf16[8,144,128]{2,1,0:T(8,128)(2,1)S(1)}, bf16[8,144,128]{2,1,0:T(8,128)(2,1)S(1)}, u32[]{:S(2)}, u32[]{:S(2)}) collective-permute-start(bf16[8,144,128]{2,1,0:T(8,128)(2,1)S(1)} %pad_maximum_fusion.own_ref), channel_id=1, source_target_pairs={{0,1},{1,0},{2,3},{3,2},{4,5},{5,4},{6,7},{7,6},{8,9},{9,8},{10,11... | collective-permute-start | bytes 884744 | tf_op jit(solution)/shard_map/ppermute | solution.py:521
  23.4 3.7 %collective-permute-start.7 = (bf16[512,128]{1,0:T(8,128)(2,1)S(1)}, bf16[512,128]{1,0:T(8,128)(2,1)S(1)}, u32[]{:S(2)}, u32[]{:S(2)}) collective-permute-start(bf16[512,128]{1,0:T(8,128)(2,1)S(1)} %get-tuple-element.59), channel_id=1, source_target_pairs={{0,1},{1,0},{2,3},{3,2},{4,5},{5,4},{6,7},{7,6},{8,9},{9,8},{10,11... | collective-permute-start | bytes 393224 | tf_op jit(solution)/shard_map/ppermute | solution.py:521
  23.6 8.6 %collective-permute-start.4 = (bf16[512,128]{1,0:T(8,128)(2,1)S(1)}, bf16[512,128]{1,0:T(8,128)(2,1)S(1)}, u32[]{:S(2)}, u32[]{:S(2)}) collective-permute-start(bf16[512,128]{1,0:T(8,128)(2,1)S(1)} %get-tuple-element.54), channel_id=1, source_target_pairs={{0,6},{1,7},{2,4},{3,5},{4,2},{5,3},{6,0},{7,1},{8,14},{9,15},{10,... | collective-permute-start | bytes 393224 | tf_op jit(solution)/shard_map/ppermute | solution.py:495
  26.1 9.4 %collective-permute-start.5 = (bf16[512,128]{1,0:T(8,128)(2,1)S(1)}, bf16[512,128]{1,0:T(8,128)(2,1)S(1)}, u32[]{:S(2)}, u32[]{:S(2)}) collective-permute-start(bf16[512,128]{1,0:T(8,128)(2,1)S(1)} %get-tuple-element.55), channel_id=1, source_target_pairs={{0,4},{1,5},{2,6},{3,7},{4,0},{5,1},{6,2},{7,3},{8,12},{9,13},{10,... | collective-permute-start | bytes 393224 | tf_op jit(solution)/shard_map/ppermute | solution.py:495
  26.8 8.7 %collective-permute-start.6 = (bf16[512,128]{1,0:T(8,128)(2,1)S(1)}, bf16[512,128]{1,0:T(8,128)(2,1)S(1)}, u32[]{:S(2)}, u32[]{:S(2)}) collective-permute-start(bf16[512,128]{1,0:T(8,128)(2,1)S(1)} %get-tuple-element.56), channel_id=1, source_target_pairs={{0,2},{1,3},{2,0},{3,1},{4,6},{5,7},{6,4},{7,5},{8,10},{9,11},{10,... | collective-permute-start | bytes 393224 | tf_op jit(solution)/shard_map/ppermute | solution.py:495
  27.2 11.4 %collective-permute-start.8 = (bf16[512,128]{1,0:T(8,128)(2,1)S(1)}, bf16[512,128]{1,0:T(8,128)(2,1)S(1)}, u32[]{:S(2)}, u32[]{:S(2)}) collective-permute-start(bf16[512,128]{1,0:T(8,128)(2,1)S(1)} %pad_maximum_fusion.2), channel_id=1, source_target_pairs={{0,14},{1,11},{2,12},{3,9},{4,10},{5,15},{6,8},{7,13},{8,6},{9,3},... | collective-permute-start | bytes 393224 | tf_op jit(solution)/shard_map/ppermute | solution.py:504
  32.0 8.9 %collective-permute-start.9 = (bf16[512,128]{1,0:T(8,128)(2,1)S(1)}, bf16[512,128]{1,0:T(8,128)(2,1)S(1)}, u32[]{:S(2)}, u32[]{:S(2)}) collective-permute-start(bf16[512,128]{1,0:T(8,128)(2,1)S(1)} %pad_maximum_fusion.3), channel_id=1, source_target_pairs={{0,12},{1,9},{2,14},{3,11},{4,8},{5,13},{6,10},{7,15},{8,4},{9,1},... | collective-permute-start | bytes 393224 | tf_op jit(solution)/shard_map/ppermute | solution.py:504
  40.9 2.6 %collective-permute-start.10 = (bf16[2048,128]{1,0:T(8,128)(2,1)S(1)}, bf16[2048,128]{1,0:T(8,128)(2,1)S(1)}, u32[]{:S(2)}, u32[]{:S(2)}) collective-permute-start(bf16[2048,128]{1,0:T(8,128)(2,1)S(1)} %constant_dynamic-update-slice_fusion), channel_id=1, source_target_pairs={{0,1},{1,0},{2,3},{3,2},{4,5},{5,4},{6,7},{7,6},{8,9},{9,8},{10,11... | collective-permute-start | bytes 1572872 | tf_op jit(solution)/shard_map/ppermute | solution.py:521
  44.9 5.4 %collective-permute-start.11 = (bf16[256,128]{1,0:T(8,128)(2,1)S(1)}, bf16[256,128]{1,0:T(8,128)(2,1)S(1)}, u32[]{:S(2)}, u32[]{:S(2)}) collective-permute-start(bf16[256,128]{1,0:T(8,128)(2,1)S(1)} %get-tuple-element.61), channel_id=1, source_target_pairs={{0,6},{1,7},{2,4},{3,5},{4,2},{5,3},{6,0},{7,1},{8,14},{9,15},{10,... | collective-permute-start | bytes 196616 | tf_op jit(solution)/shard_map/ppermute | solution.py:495
  46.9 4.3 %collective-permute-start.12 = (bf16[256,128]{1,0:T(8,128)(2,1)S(1)}, bf16[256,128]{1,0:T(8,128)(2,1)S(1)}, u32[]{:S(2)}, u32[]{:S(2)}) collective-permute-start(bf16[256,128]{1,0:T(8,128)(2,1)S(1)} %get-tuple-element.62), channel_id=1, source_target_pairs={{0,4},{1,5},{2,6},{3,7},{4,0},{5,1},{6,2},{7,3},{8,12},{9,13},{10,... | collective-permute-start | bytes 196616 | tf_op jit(solution)/shard_map/ppermute | solution.py:495
  47.1 4.6 %collective-permute-start.13 = (bf16[256,128]{1,0:T(8,128)(2,1)S(1)}, bf16[256,128]{1,0:T(8,128)(2,1)S(1)}, u32[]{:S(2)}, u32[]{:S(2)}) collective-permute-start(bf16[256,128]{1,0:T(8,128)(2,1)S(1)} %get-tuple-element.63), channel_id=1, source_target_pairs={{0,2},{1,3},{2,0},{3,1},{4,6},{5,7},{6,4},{7,5},{8,10},{9,11},{10,... | collective-permute-start | bytes 196616 | tf_op jit(solution)/shard_map/ppermute | solution.py:495
  53.3 1.6 %collective-permute-start.14 = (bf16[1024,128]{1,0:T(8,128)(2,1)S(1)}, bf16[1024,128]{1,0:T(8,128)(2,1)S(1)}, u32[]{:S(2)}, u32[]{:S(2)}) collective-permute-start(bf16[1024,128]{1,0:T(8,128)(2,1)S(1)} %get-tuple-element.69), channel_id=1, source_target_pairs={{0,1},{1,0},{2,3},{3,2},{4,5},{5,4},{6,7},{7,6},{8,9},{9,8},{10,11... | collective-permute-start | bytes 786440 | tf_op jit(solution)/shard_map/ppermute | solution.py:521
  55.0 8.7 %collective-permute-start.15 = (bf16[512,128]{1,0:T(8,128)(2,1)S(1)}, bf16[512,128]{1,0:T(8,128)(2,1)S(1)}, u32[]{:S(2)}, u32[]{:S(2)}) collective-permute-start(bf16[512,128]{1,0:T(8,128)(2,1)S(1)} %pad_maximum_fusion.4), channel_id=1, source_target_pairs={{0,14},{1,11},{2,12},{3,9},{4,10},{5,15},{6,8},{7,13},{8,6},{9,3},... | collective-permute-start | bytes 393224 | tf_op jit(solution)/shard_map/ppermute | solution.py:504
  59.6 8.0 %collective-permute-start.16 = (bf16[512,128]{1,0:T(8,128)(2,1)S(1)}, bf16[512,128]{1,0:T(8,128)(2,1)S(1)}, u32[]{:S(2)}, u32[]{:S(2)}) collective-permute-start(bf16[512,128]{1,0:T(8,128)(2,1)S(1)} %pad_maximum_fusion.5), channel_id=1, source_target_pairs={{0,12},{1,9},{2,14},{3,11},{4,8},{5,13},{6,10},{7,15},{8,4},{9,1},... | collective-permute-start | bytes 393224 | tf_op jit(solution)/shard_map/ppermute | solution.py:504
  59.7 8.7 %collective-permute-start.17 = (bf16[512,128]{1,0:T(8,128)(2,1)S(1)}, bf16[512,128]{1,0:T(8,128)(2,1)S(1)}, u32[]{:S(2)}, u32[]{:S(2)}) collective-permute-start(bf16[512,128]{1,0:T(8,128)(2,1)S(1)} %pad_maximum_fusion.6), channel_id=1, source_target_pairs={{0,6},{1,5},{2,4},{3,7},{4,2},{5,1},{6,0},{7,3},{8,14},{9,13},{10,... | collective-permute-start | bytes 393224 | tf_op jit(solution)/shard_map/ppermute | solution.py:504
  60.3 8.2 %collective-permute-start.18 = (bf16[512,128]{1,0:T(8,128)(2,1)S(1)}, bf16[512,128]{1,0:T(8,128)(2,1)S(1)}, u32[]{:S(2)}, u32[]{:S(2)}) collective-permute-start(bf16[512,128]{1,0:T(8,128)(2,1)S(1)} %pad_maximum_fusion.7), channel_id=1, source_target_pairs={{0,2},{1,1},{2,0},{3,3},{4,6},{5,5},{6,4},{7,7},{8,10},{9,9},{10,8... | collective-permute-start | bytes 393224 | tf_op jit(solution)/shard_map/ppermute | solution.py:504
  69.7 2.6 %collective-permute-start.19 = (bf16[4,256,128]{2,1,0:T(8,128)(2,1)S(1)}, bf16[4,256,128]{2,1,0:T(8,128)(2,1)S(1)}, u32[]{:S(2)}, u32[]{:S(2)}) collective-permute-start(bf16[4,256,128]{2,1,0:T(8,128)(2,1)S(1)} %get-tuple-element.74), channel_id=1, source_target_pairs={{0,1},{1,0},{2,3},{3,2},{4,5},{5,4},{6,7},{7,6},{8,9},{9,8},{10,11... | collective-permute-start | bytes 786440 | tf_op jit(solution)/shard_map/ppermute | solution.py:521
  72.4 7.1 %collective-permute-start.20 = (bf16[256,128]{1,0:T(8,128)(2,1)S(1)}, bf16[256,128]{1,0:T(8,128)(2,1)S(1)}, u32[]{:S(2)}, u32[]{:S(2)}) collective-permute-start(bf16[256,128]{1,0:T(8,128)(2,1)S(1)} %get-tuple-element.75), channel_id=1, source_target_pairs={{0,14},{1,7},{2,12},{3,5},{4,10},{5,3},{6,8},{7,1},{8,6},{9,15},{1... | collective-permute-start | bytes 196616 | tf_op jit(solution)/shard_map/ppermute | solution.py:504
  76.8 5.0 %collective-permute-start.21 = (bf16[256,128]{1,0:T(8,128)(2,1)S(1)}, bf16[256,128]{1,0:T(8,128)(2,1)S(1)}, u32[]{:S(2)}, u32[]{:S(2)}) collective-permute-start(bf16[256,128]{1,0:T(8,128)(2,1)S(1)} %get-tuple-element.76), channel_id=1, source_target_pairs={{0,4},{1,13},{2,6},{3,15},{4,0},{5,9},{6,2},{7,11},{8,12},{9,5},{1... | collective-permute-start | bytes 196616 | tf_op jit(solution)/shard_map/ppermute | solution.py:504
  77.4 6.1 %collective-permute-start.22 = (bf16[256,128]{1,0:T(8,128)(2,1)S(1)}, bf16[256,128]{1,0:T(8,128)(2,1)S(1)}, u32[]{:S(2)}, u32[]{:S(2)}) collective-permute-start(bf16[256,128]{1,0:T(8,128)(2,1)S(1)} %get-tuple-element.77), channel_id=1, source_target_pairs={{0,10},{1,3},{2,8},{3,1},{4,14},{5,7},{6,12},{7,5},{8,2},{9,11},{1... | collective-permute-start | bytes 196616 | tf_op jit(solution)/shard_map/ppermute | solution.py:504
  77.7 5.8 %collective-permute-start.23 = (bf16[256,128]{1,0:T(8,128)(2,1)S(1)}, bf16[256,128]{1,0:T(8,128)(2,1)S(1)}, u32[]{:S(2)}, u32[]{:S(2)}) collective-permute-start(bf16[256,128]{1,0:T(8,128)(2,1)S(1)} %get-tuple-element.78), channel_id=1, source_target_pairs={{0,0},{1,9},{2,2},{3,11},{4,4},{5,13},{6,6},{7,15},{8,8},{9,1},{10... | collective-permute-start | bytes 196616 | tf_op jit(solution)/shard_map/ppermute | solution.py:504
  83.5 2.6 %collective-permute-start.24 = (bf16[512,128]{1,0:T(8,128)(2,1)S(1)}, bf16[512,128]{1,0:T(8,128)(2,1)S(1)}, u32[]{:S(2)}, u32[]{:S(2)}) collective-permute-start(bf16[512,128]{1,0:T(8,128)(2,1)S(1)} %shard_map.107), channel_id=1, source_target_pairs={{0,1},{1,0},{2,3},{3,2},{4,5},{5,4},{6,7},{7,6},{8,9},{9,8},{10,11... | collective-permute-start | bytes 393224 | tf_op jit(solution)/shard_map/ppermute | solution.py:521

commit v13 on v12

--- a/solution.py
+++ b/solution.py
@@ -237,7 +237,9 @@
     return chip ^ jnp.where(core == 0, split[op][0], split[op][1])
 
 
-def project_kernel(feat_ref, weight_ref, live_in_ref, pay_ref, left_ref, live_ref, turned, packed):
+def project_kernel(
+    where_ref, feat_ref, weight_ref, mask_ref, present_ref, pay_ref, left_ref, live_ref, turned, packed
+):
     homologs, rows, _ = feat_ref.shape
     half = weight_ref.shape[0] // 2
     quarter = half // 2
@@ -250,7 +252,15 @@
     in_row = lax.broadcasted_iota(jnp.int32, (total, total), 1)
     order = in_row == (out_row & (homologs - 1)) * rows + out_row // homologs
     normed = nn(order.astype(F32).astype(BF16), normed).astype(BF16)
-    live = live_in_ref[...]
+    seq = lax.broadcasted_iota(jnp.int32, (homologs, 2 * homologs), 0)
+    lane = lax.broadcasted_iota(jnp.int32, (homologs, 2 * homologs), 1)
+    twice = (seq == (lane & (homologs - 1))).astype(F32).astype(BF16)
+    cols = present_ref.shape[1]
+    here = lax.broadcasted_iota(jnp.int32, (rows, cols), 1) == (
+        lax.broadcasted_iota(jnp.int32, (rows, cols), 0) + where_ref[0]
+    )
+    present = jnp.sum(jnp.where(here, present_ref[...].astype(F32), 0.0), axis=1, keepdims=True)
+    live = nn(mask_ref[...], twice) * present
     weight = weight_ref[...]
     blank = jnp.zeros((homologs, normed.shape[1]), BF16)
     for row in range(rows):
@@ -374,24 +384,27 @@
 
 
 def mix_rows_kernel(
-    where_ref, near0, near1, near2, near3, far0, far1, other_ref,
-    out0, out1, out2, out3, lefts, rights, mixed,
+    where_ref, near3, far0, near2, near1, near0, far1, other_ref, out0, out1, out2, out3, lefts, rights, mixed
 ):
     chip, core = where_ref[1], where_ref[2]
     count, rows, cols = lefts.shape[1:]
     block = count * rows
-    for at, (step, near) in enumerate(zip(NEAR_STEPS, (near0, near1, near2, near3))):
-        lefts[step] = near[0:block].astype(F32).reshape(count, rows, cols)
-        rights[(chip ^ step) * 2 + core] = near[block:].astype(F32).reshape(count, rows, cols)
-        theirs = other_ref[at * block : (at + 1) * block]
-        rights[(chip ^ step) * 2 + (1 - core)] = theirs.astype(F32).reshape(count, rows, cols)
-    for op, far in enumerate((far0, far1)):
-        for half in range(2):
-            at = partner_chip(chip, core, op, FAR_SPLIT) * 2 + (core ^ half)
-            rights[at] = far[half * block : (half + 1) * block].astype(F32).reshape(count, rows, cols)
-            at = partner_chip(chip, 1 - core, op, FAR_SPLIT) * 2 + ((1 - core) ^ half)
-            place = (NEAR + op * 2 + half) * block
-            rights[at] = other_ref[place : place + block].astype(F32).reshape(count, rows, cols)
+    place = 0
+    for step, near in ((3, near3), (None, far0), (2, near2), (1, near1), (0, near0), (None, far1)):
+        if step is None:
+            op = 0 if near is far0 else 1
+            for half in range(2):
+                at = partner_chip(chip, core, op, FAR_SPLIT) * 2 + (core ^ half)
+                rights[at] = near[half * block : (half + 1) * block].astype(F32).reshape(count, rows, cols)
+                at = partner_chip(chip, 1 - core, op, FAR_SPLIT) * 2 + ((1 - core) ^ half)
+                rights[at] = other_ref[place : place + block].astype(F32).reshape(count, rows, cols)
+                place += block
+        else:
+            lefts[step] = near[0:block].astype(F32).reshape(count, rows, cols)
+            rights[(chip ^ step) * 2 + core] = near[block:].astype(F32).reshape(count, rows, cols)
+            theirs = other_ref[place : place + block]
+            rights[(chip ^ step) * 2 + (1 - core)] = theirs.astype(F32).reshape(count, rows, cols)
+            place += block
     for c in range(count):
         left = flat(lefts[:, c]).astype(BF16)
         right = flat(rights[:, c]).astype(BF16)
@@ -541,13 +554,11 @@
     where = jnp.stack([device * rows, chip, core]).astype(jnp.int32)
     present = resolved_residue_mask.reshape(1, cols)
     pay_rows = (half // 2 + 2) * rows
-    row_present = lax.dynamic_slice_in_dim(resolved_residue_mask, device * rows, rows).astype(F32)
-    live = alignment_mask.T.astype(F32) * row_present[:, None]
-    live = jnp.concatenate([live, live], axis=1)
     pay, left, live = run(
         project_kernel,
         [((pay_rows, LANES), BF16), ((2 * rows * half, LANES), BF16), ((rows, LANES), F32)],
-        homolog_features.astype(F32), homolog_to_sides_matrix.T, live,
+        where, homolog_features.astype(F32), homolog_to_sides_matrix.T, alignment_mask.T, present,
+        smem=(0,),
         scratch=[((rows * half // 2, LANES), F32), ((pay_rows, LANES), F32)],
     )
     far_z = chip_permute(pay, 4)
@@ -587,13 +598,17 @@
         flops=4 * 10**9,
     )
     stream, gate = made[0], made[1]
-    came = exchange(made[5:9], NEAR_STEPS)
-    far = split_exchange(with_partner(made[2:4], made[4]), FAR_SPLIT)
-    rights = jnp.concatenate([block[near:] for block in came] + far, axis=0)
+    first = chip_permute(made[8], 3)
+    far, later = lax.optimization_barrier((with_partner(made[2:4], made[4]), list(made[5:8])))
+    far = split_exchange(far, FAR_SPLIT)
+    came = [first] + exchange(later, NEAR_STEPS[1:])
+    came = [came[0], far[0], came[1], came[2], came[3], far[1]]
+    rights = [block if at in (1, 5) else block[near:] for at, block in enumerate(came)]
+    rights = jnp.concatenate(rights, axis=0)
     mixed = run(
         mix_rows_kernel,
         [((near, cols), BF16)] * NEAR,
-        where, *came, *far, core_permute(rights),
+        where, *came, core_permute(rights),
         smem=(0,),
         scratch=[
             ((NEAR, width // NEAR, rows, cols), F32),

time: 88.5 us -> 87.4 us (0.988)
  starting transfers between devices: 38.6 us -> 36.5 us
  waiting for transfers between devices: 34.7 us -> 36 us
    ppermute x10, starting transfers between devices: 19.6 us -> 17.5 us  [split_permute(): lax.ppermute(block, 'wide', [(w, w ^ 2 * steps[w % 2]) for w in range(cou...]
    ppermute x10, waiting for transfers between devices: 15.3 us -> 17.3 us  [split_permute(): lax.ppermute(block, 'wide', [(w, w ^ 2 * steps[w % 2]) for w in range(cou...]
    ppermute x9, waiting for transfers between devices: 12.6 us -> 11.6 us  [chip_permute(): lax.ppermute(block, 'wide', [(w, w ^ 2 * step) for w in range(count)])]
  transfers between devices with their start and end apart: 25 -> 25, of which waited for: 21 -> 22; matrix products, arithmetic and copies ran while one was open for 0% -> 0% of each run, Pallas kernels for 2% -> 2%
where the time goes in v13:
time: 87.4 us; the launch traced here: 87.2 us
  starting transfers between devices  36.5 us (42%)
  waiting for transfers between devices  36 us (41%)
  Pallas kernels  12.5 us (14%)
  other arithmetic  1.19 us (1%)
    ppermute x10, starting transfers between devices, split_permute(): lax.ppermute(block, 'wide', [(w, w ^ 2 * steps[w % 2]) for w in range(cou...  17.5 us
    ppermute x10, waiting for transfers between devices, split_permute(): lax.ppermute(block, 'wide', [(w, w ^ 2 * steps[w % 2]) for w in range(cou...  17.3 us
    ppermute x9, starting transfers between devices, chip_permute(): lax.ppermute(block, 'wide', [(w, w ^ 2 * step) for w in range(count)])  14.8 us
    pallas_call x9, Pallas kernels, run(): pl.pallas_call(kernel, out_shape=[jax.ShapeDtypeStruct(shape, kind) for s...  12.5 us
    ppermute x9, waiting for transfers between devices, chip_permute(): lax.ppermute(block, 'wide', [(w, w ^ 2 * step) for w in range(count)])  11.6 us
    ppermute x6, waiting for transfers between devices, core_permute(): return lax.ppermute(block, 'wide', [(w, w ^ 1) for w in range(count)])  7.09 us
    ppermute x6, starting transfers between devices, core_permute(): return lax.ppermute(block, 'wide', [(w, w ^ 1) for w in range(count)])  4.14 us
  transfers between devices with their start and end apart: 25, of which 22 were waited for; matrix products, arithmetic and copies ran while one was open for 0% of the time, Pallas kernels for 2%

profile of v13, /device:TPU:0, one launch (start us, length us, event | category | flops | bytes accessed | tf_op | source)
XLA Modules:
  0.0 87.2 jit_solution(8268761391402065053)
XLA Ops:
  0.0 1.0 %convert_element_type.3.feat_ref = f32[64,8,256]{2,1,0:T(8,128)S(1)} convert(bf16[64,8,256]{2,1,0:T(8,128)(2,1)} %param.11) | non-fusion elementwise | flops 131072 | bytes 786432 | tf_op jit(solution)/shard_map/convert_element_type | solution.py:560
  1.0 0.1 pad_add_fusion.where_ref
  1.1 0.7 copy-done.6
  1.8 1.5 %shard_map.100 = (bf16[144,128]{1,0:T(8,128)(2,1)S(1)}, bf16[512,128]{1,0:T(8,128)(2,1)S(1)}, f32[8,128]{1,0:T(8,128)S(1)}) custom-call(s32[3]{0:T(128)S(1)} %pad_add_fusion.where_ref, f32[64,8,256]{2,1,0:T(8,128)S(1)} %convert_element_type.3.feat_ref, bf16[64,256]{1,0:T(8,128)(2,1)S(1)} %bitcast.12, bf16[8,64]{1,0:T(8,128)(2,1)S(1)} %bitcast.13, ...), custom_call_target="tpu_custom_call" | custom-call | flops 1500000000 | bytes 558604 | tf_op jit(solution)/shard_map/pallas_call | solution.py:216
  3.3 0.0 copy-start
  3.3 4.1 %collective-permute-start = (bf16[144,128]{1,0:T(8,128)(2,1)S(1)}, bf16[144,128]{1,0:T(8,128)(2,1)S(1)}, u32[]{:S(2)}, u32[]{:S(2)}) collective-permute-start(bf16[144,128]{1,0:T(8,128)(2,1)S(1)} %get-tuple-element.48), channel_id=1, source_target_pairs={{0,8},{1,9},{2,10},{3,11},{4,12},{5,13},{6,14},{7,15},{8,0},{9,1},... | collective-permute-start | bytes 110600 | tf_op jit(solution)/shard_map/ppermute | solution.py:508
  7.4 2.3 %collective-permute-done = bf16[144,128]{1,0:T(8,128)(2,1)S(1)} collective-permute-done((bf16[144,128]{1,0:T(8,128)(2,1)S(1)}, bf16[144,128]{1,0:T(8,128)(2,1)S(1)}, u32[]{:S(2)}, u32[]{:S(2)}) %collective-permute-start) | collective-permute-done | bytes 36896 | tf_op jit(solution)/shard_map/ppermute | solution.py:508
  9.7 0.0 copy-start.3
  9.8 0.0 copy-start.5
  9.8 1.6 %collective-permute-start.1 = (bf16[2,144,128]{2,1,0:T(8,128)(2,1)S(1)}, bf16[2,144,128]{2,1,0:T(8,128)(2,1)S(1)}, u32[]{:S(2)}, u32[]{:S(2)}) collective-permute-start(bf16[2,144,128]{2,1,0:T(8,128)(2,1)S(1)} %pad_maximum_fusion.8), channel_id=1, source_target_pairs={{0,4},{1,5},{2,6},{3,7},{4,0},{5,1},{6,2},{7,3},{8,12},{9,13},{10,... | collective-permute-start | bytes 221192 | tf_op jit(solution)/shard_map/ppermute | solution.py:508
  11.3 2.8 %collective-permute-done.1 = bf16[2,144,128]{2,1,0:T(8,128)(2,1)S(1)} collective-permute-done((bf16[2,144,128]{2,1,0:T(8,128)(2,1)S(1)}, bf16[2,144,128]{2,1,0:T(8,128)(2,1)S(1)}, u32[]{:S(2)}, u32[]{:S(2)}) %collective-permute-start.1) | collective-permute-done | bytes 73760 | tf_op jit(solution)/shard_map/ppermute | solution.py:508
  14.2 0.0 copy-start.7
  14.2 1.8 %collective-permute-start.2 = (bf16[4,144,128]{2,1,0:T(8,128)(2,1)S(1)}, bf16[4,144,128]{2,1,0:T(8,128)(2,1)S(1)}, u32[]{:S(2)}, u32[]{:S(2)}) collective-permute-start(bf16[4,144,128]{2,1,0:T(8,128)(2,1)S(1)} %pad_maximum_fusion.1), channel_id=1, source_target_pairs={{0,2},{1,3},{2,0},{3,1},{4,6},{5,7},{6,4},{7,5},{8,10},{9,11},{10,... | collective-permute-start | bytes 442376 | tf_op jit(solution)/shard_map/ppermute | solution.py:508
  16.0 1.7 %shard_map.101 = (f32[8,128,128]{2,1,0:T(8,128)S(1)}, bf16[128,1024]{1,0:T(8,128)(2,1)S(1)}, bf16[2,640,128]{2,1,0:T(8,128)(2,1)S(1)}, bf16[2,128,128]{2,1,0:T(8,128)(2,1)S(1)}) custom-call(s32[3]{0:T(128)S(1)} %pad_add_fusion.where_ref, s32[128]{0:T(128)S(1)} %copy-done.7, s32[1,128]{1,0:T(1,128)S(1)} %bitcast.14, bf16[8,128,128]{2,1,0:T(8,128)(2,1)S(1)} %copy-done.1, ...), custom_call_target="tpu_custom_call" | custom-call | flops 1500000000 | bytes 935436 | tf_op jit(solution)/shard_map/pallas_call | solution.py:216
  17.7 1.7 %collective-permute-done.2 = bf16[4,144,128]{2,1,0:T(8,128)(2,1)S(1)} collective-permute-done((bf16[4,144,128]{2,1,0:T(8,128)(2,1)S(1)}, bf16[4,144,128]{2,1,0:T(8,128)(2,1)S(1)}, u32[]{:S(2)}, u32[]{:S(2)}) %collective-permute-start.2) | collective-permute-done | bytes 147488 | tf_op jit(solution)/shard_map/ppermute | solution.py:508
  19.5 0.1 collective-permute-start.3
  19.5 1.6 %collective-permute-done.3.other_ref = bf16[8,144,128]{2,1,0:T(8,128)(2,1)S(1)} collective-permute-done((bf16[8,144,128]{2,1,0:T(8,128)(2,1)S(1)}, bf16[8,144,128]{2,1,0:T(8,128)(2,1)S(1)}, u32[]{:S(2)}, u32[]{:S(2)}) %collective-permute-start.3) | collective-permute-done | bytes 294944 | tf_op jit(solution)/shard_map/ppermute | solution.py:534
  21.1 2.7 %shard_map.102 = (f32[8,128,128]{2,1,0:T(8,128)S(1)}, f32[8,128,128]{2,1,0:T(8,128)S(1)}, bf16[256,128]{1,0:T(8,128)(2,1)S(1)}, bf16[256,128]{1,0:T(8,128)(2,1)S...) custom-call(s32[3]{0:T(128)S(1)} %pad_add_fusion.where_ref, ...), custom_call_target="tpu_custom_call" | custom-call | flops 4000000000 | bytes 1840140 | tf_op jit(solution)/shard_map/pallas_call | solution.py:216
  23.8 0.2 collective-permute-start.5
  24.1 2.4 %collective-permute-start.4 = (bf16[512,128]{1,0:T(8,128)(2,1)S(1)}, bf16[512,128]{1,0:T(8,128)(2,1)S(1)}, u32[]{:S(2)}, u32[]{:S(2)}) collective-permute-start(bf16[512,128]{1,0:T(8,128)(2,1)S(1)} %get-tuple-element.59), channel_id=1, source_target_pairs={{0,6},{1,7},{2,4},{3,5},{4,2},{5,3},{6,0},{7,1},{8,14},{9,15},{10,... | collective-permute-start | bytes 393224 | tf_op jit(solution)/shard_map/ppermute | solution.py:508
  26.5 0.0 collective-permute-done.5
  26.5 3.6 %collective-permute-start.6 = (bf16[512,128]{1,0:T(8,128)(2,1)S(1)}, bf16[512,128]{1,0:T(8,128)(2,1)S(1)}, u32[]{:S(2)}, u32[]{:S(2)}) collective-permute-start(bf16[512,128]{1,0:T(8,128)(2,1)S(1)} %get-tuple-element.66), channel_id=1, source_target_pairs={{0,14},{1,11},{2,12},{3,9},{4,10},{5,15},{6,8},{7,13},{8,6},{9,3},... | collective-permute-start | bytes 393224 | tf_op jit(solution)/shard_map/ppermute | solution.py:517
  30.1 0.0 collective-permute-start.7
  30.1 1.4 %collective-permute-start.8 = (bf16[512,128]{1,0:T(8,128)(2,1)S(1)}, bf16[512,128]{1,0:T(8,128)(2,1)S(1)}, u32[]{:S(2)}, u32[]{:S(2)}) collective-permute-start(bf16[512,128]{1,0:T(8,128)(2,1)S(1)} %get-tuple-element.68), channel_id=1, source_target_pairs={{0,2},{1,3},{2,0},{3,1},{4,6},{5,7},{6,4},{7,5},{8,10},{9,11},{10,... | collective-permute-start | bytes 393224 | tf_op jit(solution)/shard_map/ppermute | solution.py:508
  31.5 0.4 collective-permute-start.9
  31.9 0.0 collective-permute-done.4.near3
  31.9 4.2 %collective-permute-done.6.far0 = bf16[512,128]{1,0:T(8,128)(2,1)S(1)} collective-permute-done((bf16[512,128]{1,0:T(8,128)(2,1)S(1)}, bf16[512,128]{1,0:T(8,128)(2,1)S(1)}, u32[]{:S(2)}, u32[]{:S(2)}) %collective-permute-start.6) | collective-permute-done | bytes 131104 | tf_op jit(solution)/shard_map/ppermute | solution.py:517
  36.1 1.3 %collective-permute-done.7.near2 = bf16[512,128]{1,0:T(8,128)(2,1)S(1)} collective-permute-done((bf16[512,128]{1,0:T(8,128)(2,1)S(1)}, bf16[512,128]{1,0:T(8,128)(2,1)S(1)}, u32[]{:S(2)}, u32[]{:S(2)}) %collective-permute-start.7) | collective-permute-done | bytes 131104 | tf_op jit(solution)/shard_map/ppermute | solution.py:508
  37.4 0.2 collective-permute-done.8.near1
  37.7 3.7 %collective-permute-done.9.far1 = bf16[512,128]{1,0:T(8,128)(2,1)S(1)} collective-permute-done((bf16[512,128]{1,0:T(8,128)(2,1)S(1)}, bf16[512,128]{1,0:T(8,128)(2,1)S(1)}, u32[]{:S(2)}, u32[]{:S(2)}) %collective-permute-start.9) | collective-permute-done | bytes 131104 | tf_op jit(solution)/shard_map/ppermute | solution.py:517
  41.3 0.1 collective-permute-start.10
  41.5 1.9 %collective-permute-done.10.other_ref = bf16[2048,128]{1,0:T(8,128)(2,1)S(1)} collective-permute-done((bf16[2048,128]{1,0:T(8,128)(2,1)S(1)}, bf16[2048,128]{1,0:T(8,128)(2,1)S(1)}, u32[]{:S(2)}, u32[]{:S(2)}) %collective-permute-start.10) | collective-permute-done | bytes 524320 | tf_op jit(solution)/shard_map/ppermute | solution.py:534
  43.3 1.4 %shard_map.103 = (bf16[256,128]{1,0:T(8,128)(2,1)S(1)}, bf16[256,128]{1,0:T(8,128)(2,1)S(1)}, bf16[256,128]{1,0:T(8,128)(2,1)S(1)}, bf16[256,128]{1,0:T(8,128)(2,1)S(1)}) custom-call(s32[3]{0:T(128)S(1)} %pad_add_fusion.where_ref, bf16[512,128]{1,0:T(8,128)(2,1)S(1)} %collective-permute-done.4.near3, bf16[512,128]{1,0:T(8,128)(2,1)S(1)} %collective-permute-done.6.far0, ...), custom_call_target="tpu_custom_call" | custom-call | flops 1500000000 | bytes 1310732 | tf_op jit(solution)/shard_map/pallas_call | solution.py:216
  44.8 1.6 %collective-permute-start.11 = (bf16[256,128]{1,0:T(8,128)(2,1)S(1)}, bf16[256,128]{1,0:T(8,128)(2,1)S(1)}, u32[]{:S(2)}, u32[]{:S(2)}) collective-permute-start(bf16[256,128]{1,0:T(8,128)(2,1)S(1)} %get-tuple-element.71), channel_id=1, source_target_pairs={{0,6},{1,7},{2,4},{3,5},{4,2},{5,3},{6,0},{7,1},{8,14},{9,15},{10,... | collective-permute-start | bytes 196616 | tf_op jit(solution)/shard_map/ppermute | solution.py:508
  46.4 0.8 collective-permute-start.12
  47.2 1.2 %collective-permute-start.13 = (bf16[256,128]{1,0:T(8,128)(2,1)S(1)}, bf16[256,128]{1,0:T(8,128)(2,1)S(1)}, u32[]{:S(2)}, u32[]{:S(2)}) collective-permute-start(bf16[256,128]{1,0:T(8,128)(2,1)S(1)} %get-tuple-element.73), channel_id=1, source_target_pairs={{0,2},{1,3},{2,0},{3,1},{4,6},{5,7},{6,4},{7,5},{8,10},{9,11},{10,... | collective-permute-start | bytes 196616 | tf_op jit(solution)/shard_map/ppermute | solution.py:508
  48.3 2.4 %collective-permute-done.11.in0 = bf16[256,128]{1,0:T(8,128)(2,1)S(1)} collective-permute-done((bf16[256,128]{1,0:T(8,128)(2,1)S(1)}, bf16[256,128]{1,0:T(8,128)(2,1)S(1)}, u32[]{:S(2)}, u32[]{:S(2)}) %collective-permute-start.11) | collective-permute-done | bytes 65568 | tf_op jit(solution)/shard_map/ppermute | solution.py:508
  50.7 0.2 collective-permute-done.12.in1
  50.9 0.6 collective-permute-done.13.in2
  51.5 1.7 %shard_map.104 = (f32[8,128,128]{2,1,0:T(8,128)S(1)}, f32[8,128,128]{2,1,0:T(8,128)S(1)}, bf16[256,128]{1,0:T(8,128)(2,1)S(1)}, bf16[256,128]{1,0:T(8,128)(2,1)S...) custom-call(s32[3]{0:T(128)S(1)} %pad_add_fusion.where_ref, ...), custom_call_target="tpu_custom_call" | custom-call | flops 1500000000 | bytes 1704972 | tf_op jit(solution)/shard_map/pallas_call | solution.py:216
  53.2 0.1 collective-permute-start.14
  53.3 1.5 %collective-permute-done.14 = bf16[1024,128]{1,0:T(8,128)(2,1)S(1)} collective-permute-done((bf16[1024,128]{1,0:T(8,128)(2,1)S(1)}, bf16[1024,128]{1,0:T(8,128)(2,1)S(1)}, u32[]{:S(2)}, u32[]{:S(2)}) %collective-permute-start.14) | collective-permute-done | bytes 262176 | tf_op jit(solution)/shard_map/ppermute | solution.py:534
  54.9 3.7 %collective-permute-start.15 = (bf16[512,128]{1,0:T(8,128)(2,1)S(1)}, bf16[512,128]{1,0:T(8,128)(2,1)S(1)}, u32[]{:S(2)}, u32[]{:S(2)}) collective-permute-start(bf16[512,128]{1,0:T(8,128)(2,1)S(1)} %pad_maximum_fusion.4), channel_id=1, source_target_pairs={{0,14},{1,11},{2,12},{3,9},{4,10},{5,15},{6,8},{7,13},{8,6},{9,3},... | collective-permute-start | bytes 393224 | tf_op jit(solution)/shard_map/ppermute | solution.py:517
  58.6 0.8 collective-permute-start.16
  59.3 0.1 collective-permute-start.17
  59.4 3.0 %collective-permute-start.18 = (bf16[512,128]{1,0:T(8,128)(2,1)S(1)}, bf16[512,128]{1,0:T(8,128)(2,1)S(1)}, u32[]{:S(2)}, u32[]{:S(2)}) collective-permute-start(bf16[512,128]{1,0:T(8,128)(2,1)S(1)} %pad_maximum_fusion.7), channel_id=1, source_target_pairs={{0,2},{1,1},{2,0},{3,3},{4,6},{5,5},{6,4},{7,7},{8,10},{9,9},{10,8... | collective-permute-start | bytes 393224 | tf_op jit(solution)/shard_map/ppermute | solution.py:517
  62.5 1.0 %collective-permute-done.15.came0 = bf16[512,128]{1,0:T(8,128)(2,1)S(1)} collective-permute-done((bf16[512,128]{1,0:T(8,128)(2,1)S(1)}, bf16[512,128]{1,0:T(8,128)(2,1)S(1)}, u32[]{:S(2)}, u32[]{:S(2)}) %collective-permute-start.15) | collective-permute-done | bytes 131104 | tf_op jit(solution)/shard_map/ppermute | solution.py:517
  63.5 3.1 %collective-permute-done.16.came1 = bf16[512,128]{1,0:T(8,128)(2,1)S(1)} collective-permute-done((bf16[512,128]{1,0:T(8,128)(2,1)S(1)}, bf16[512,128]{1,0:T(8,128)(2,1)S(1)}, u32[]{:S(2)}, u32[]{:S(2)}) %collective-permute-start.16) | collective-permute-done | bytes 131104 | tf_op jit(solution)/shard_map/ppermute | solution.py:517
  66.6 1.1 %collective-permute-done.17.came2 = bf16[512,128]{1,0:T(8,128)(2,1)S(1)} collective-permute-done((bf16[512,128]{1,0:T(8,128)(2,1)S(1)}, bf16[512,128]{1,0:T(8,128)(2,1)S(1)}, u32[]{:S(2)}, u32[]{:S(2)}) %collective-permute-start.17) | collective-permute-done | bytes 131104 | tf_op jit(solution)/shard_map/ppermute | solution.py:517
  67.7 0.1 collective-permute-done.18.came3
  67.8 1.2 %shard_map.105 = (f32[4,256,128]{2,1,0:T(8,128)S(1)}, bf16[4,256,128]{2,1,0:T(8,128)(2,1)S(1)}) custom-call(s32[3]{0:T(128)S(1)} %pad_add_fusion.where_ref, bf16[512,128]{1,0:T(8,128)(2,1)S(1)} %collective-permute-done.15.came0, bf16[512,128]{1,0:T(8,128)(2,1)S(1)} %collective-permute-done.16.came1, bf16[512,128]{1,0:T(8,128)(2,1)S(1)} %collective-permute-done.17.came2, ...), custom_call_target="tpu_custom_call" | custom-call | flops 1500000000 | bytes 524300 | tf_op jit(solution)/shard_map/pallas_call | solution.py:216
  69.0 2.1 %collective-permute-start.19 = (bf16[4,256,128]{2,1,0:T(8,128)(2,1)S(1)}, bf16[4,256,128]{2,1,0:T(8,128)(2,1)S(1)}, u32[]{:S(2)}, u32[]{:S(2)}) collective-permute-start(bf16[4,256,128]{2,1,0:T(8,128)(2,1)S(1)} %get-tuple-element.84), channel_id=1, source_target_pairs={{0,1},{1,0},{2,3},{3,2},{4,5},{5,4},{6,7},{7,6},{8,9},{9,8},{10,11... | collective-permute-start | bytes 786440 | tf_op jit(solution)/shard_map/ppermute | solution.py:534
  71.0 1.2 %collective-permute-done.19.got_ref = bf16[4,256,128]{2,1,0:T(8,128)(2,1)S(1)} collective-permute-done((bf16[4,256,128]{2,1,0:T(8,128)(2,1)S(1)}, bf16[4,256,128]{2,1,0:T(8,128)(2,1)S(1)}, u32[]{:S(2)}, u32[]{:S(2)}) %collective-permute-start.19) | collective-permute-done | bytes 262176 | tf_op jit(solution)/shard_map/ppermute | solution.py:534
  72.2 0.1 shard_map.106
  72.3 3.5 %collective-permute-start.20 = (bf16[256,128]{1,0:T(8,128)(2,1)S(1)}, bf16[256,128]{1,0:T(8,128)(2,1)S(1)}, u32[]{:S(2)}, u32[]{:S(2)}) collective-permute-start(bf16[256,128]{1,0:T(8,128)(2,1)S(1)} %get-tuple-element.85), channel_id=1, source_target_pairs={{0,14},{1,7},{2,12},{3,5},{4,10},{5,3},{6,8},{7,1},{8,6},{9,15},{1... | collective-permute-start | bytes 196616 | tf_op jit(solution)/shard_map/ppermute | solution.py:517
  75.8 0.6 collective-permute-start.21
  76.4 1.3 %collective-permute-start.22 = (bf16[256,128]{1,0:T(8,128)(2,1)S(1)}, bf16[256,128]{1,0:T(8,128)(2,1)S(1)}, u32[]{:S(2)}, u32[]{:S(2)}) collective-permute-start(bf16[256,128]{1,0:T(8,128)(2,1)S(1)} %get-tuple-element.87), channel_id=1, source_target_pairs={{0,10},{1,3},{2,8},{3,1},{4,14},{5,7},{6,12},{7,5},{8,2},{9,11},{1... | collective-permute-start | bytes 196616 | tf_op jit(solution)/shard_map/ppermute | solution.py:517
  77.6 0.7 collective-permute-start.23
  78.3 1.8 %collective-permute-done.20.refs_0_.came0 = bf16[256,128]{1,0:T(8,128)(2,1)S(1)} collective-permute-done((bf16[256,128]{1,0:T(8,128)(2,1)S(1)}, bf16[256,128]{1,0:T(8,128)(2,1)S(1)}, u32[]{:S(2)}, u32[]{:S(2)}) %collective-permute-start.20) | collective-permute-done | bytes 65568 | tf_op jit(solution)/shard_map/ppermute | solution.py:517
  80.1 0.7 collective-permute-done.21.refs_1_.came1
  80.8 1.7 %collective-permute-done.22.refs_2_.came2 = bf16[256,128]{1,0:T(8,128)(2,1)S(1)} collective-permute-done((bf16[256,128]{1,0:T(8,128)(2,1)S(1)}, bf16[256,128]{1,0:T(8,128)(2,1)S(1)}, u32[]{:S(2)}, u32[]{:S(2)}) %collective-permute-start.22) | collective-permute-done | bytes 65568 | tf_op jit(solution)/shard_map/ppermute | solution.py:517
  82.4 1.6 %collective-permute-start.24 = (bf16[512,128]{1,0:T(8,128)(2,1)S(1)}, bf16[512,128]{1,0:T(8,128)(2,1)S(1)}, u32[]{:S(2)}, u32[]{:S(2)}) collective-permute-start(bf16[512,128]{1,0:T(8,128)(2,1)S(1)} %shard_map.107), channel_id=1, source_target_pairs={{0,1},{1,0},{2,3},{3,2},{4,5},{5,4},{6,7},{7,6},{8,9},{9,8},{10,11... | collective-permute-start | bytes 393224 | tf_op jit(solution)/shard_map/ppermute | solution.py:534
  84.1 1.0 %collective-permute-done.24.other_ref = bf16[512,128]{1,0:T(8,128)(2,1)S(1)} collective-permute-done((bf16[512,128]{1,0:T(8,128)(2,1)S(1)}, bf16[512,128]{1,0:T(8,128)(2,1)S(1)}, u32[]{:S(2)}, u32[]{:S(2)}) %collective-permute-start.24) | collective-permute-done | bytes 131104 | tf_op jit(solution)/shard_map/ppermute | solution.py:534
  85.0 2.2 %shard_map.108 = bf16[8,128,128]{2,1,0:T(8,128)(2,1)} custom-call(s32[3]{0:T(128)S(1)} %pad_add_fusion.where_ref, bf16[256,128]{1,0:T(8,128)(2,1)S(1)} %collective-permute-done.20.refs_0_.came0, bf16[256,128]{1,0:T(8,128)(2,1)S(1)} %collective-permute-done.21.refs_1_.came1, bf16[256,128]{1,0:T(8,128)(2,1)S(1)} %collective-permute-done.22.refs_2_.came2, ...), custom_call_target="tpu_custom_call" | custom-call | flops 1500000000 | bytes 1507340 | tf_op jit(solution)/shard_map/pallas_call | solution.py:216
  (31 shorter events, 0.3 us)
Async XLA Ops:
  0.0 1.1 %copy-start.4 = (bf16[256,64]{0,1:T(8,128)(2,1)S(1)}, bf16[256,64]{0,1:T(8,128)(2,1)}, u32[]{:S(2)}) copy-start(bf16[256,64]{0,1:T(8,128)(2,1)} %param.16) | copy-start | bytes 98308
  1.1 0.7 copy-start.6
  1.1 0.7 copy-start.8
  1.8 14.2 %copy-start.1 = (bf16[8,128,128]{2,1,0:T(8,128)(2,1)S(1)}, bf16[8,128,128]{2,1,0:T(8,128)(2,1)}, u32[]{:S(2)}) copy-start(bf16[8,128,128]{2,1,0:T(8,128)(2,1)} %pair_ref.1) | copy-start | bytes 786436
  1.8 14.2 %copy-start.2 = (bf16[1024,128]{1,0:T(8,128)(2,1)S(1)}, bf16[1024,128]{1,0:T(8,128)(2,1)}, u32[]{:S(2)}) copy-start(bf16[1024,128]{1,0:T(8,128)(2,1)} %outer_ref.1) | copy-start | bytes 786436
  3.3 12.7 %copy-start = (bf16[2,128,640]{2,1,0:T(8,128)(2,1)S(1)}, bf16[2,128,640]{2,1,0:T(8,128)(2,1)}, u32[]{:S(2)}) copy-start(bf16[2,128,640]{2,1,0:T(8,128)(2,1)} %proj_ref.1) | copy-start | bytes 983044
  3.3 6.4 %collective-permute-start = (bf16[144,128]{1,0:T(8,128)(2,1)S(1)}, bf16[144,128]{1,0:T(8,128)(2,1)S(1)}, u32[]{:S(2)}, u32[]{:S(2)}) collective-permute-start(bf16[144,128]{1,0:T(8,128)(2,1)S(1)} %get-tuple-element.48), channel_id=1, source_target_pairs={{0,8},{1,9},{2,10},{3,11},{4,12},{5,13},{6,14},{7,15},{8,0},{9,1},... | collective-permute-start | bytes 110600 | tf_op jit(solution)/shard_map/ppermute | solution.py:508
  9.7 6.3 %copy-start.3 = (bf16[2,128,128]{2,1,0:T(8,128)(2,1)S(1)}, bf16[2,128,128]{2,1,0:T(8,128)(2,1)}, u32[]{:S(2)}) copy-start(bf16[2,128,128]{2,1,0:T(8,128)(2,1)} %out_ref.1) | copy-start | bytes 196612
  9.8 6.2 %copy-start.5 = (bf16[66,128]{1,0:T(8,128)(2,1)S(1)}, bf16[66,128]{1,0:T(8,128)(2,1)}, u32[]{:S(2)}) copy-start(bf16[66,128]{1,0:T(8,128)(2,1)} %table_ref.1) | copy-start | bytes 50692
  9.8 4.4 %collective-permute-start.1 = (bf16[2,144,128]{2,1,0:T(8,128)(2,1)S(1)}, bf16[2,144,128]{2,1,0:T(8,128)(2,1)S(1)}, u32[]{:S(2)}, u32[]{:S(2)}) collective-permute-start(bf16[2,144,128]{2,1,0:T(8,128)(2,1)S(1)} %pad_maximum_fusion.8), channel_id=1, source_target_pairs={{0,4},{1,5},{2,6},{3,7},{4,0},{5,1},{6,2},{7,3},{8,12},{9,13},{10,... | collective-permute-start | bytes 221192 | tf_op jit(solution)/shard_map/ppermute | solution.py:508
  14.2 1.8 %copy-start.7 = (s32[128]{0:T(128)S(1)}, s32[128]{0:T(128)}, u32[]{:S(2)}) copy-start(s32[128]{0:T(128)} %chain_ref.1) | copy-start | bytes 1540
  14.2 5.2 %collective-permute-start.2 = (bf16[4,144,128]{2,1,0:T(8,128)(2,1)S(1)}, bf16[4,144,128]{2,1,0:T(8,128)(2,1)S(1)}, u32[]{:S(2)}, u32[]{:S(2)}) collective-permute-start(bf16[4,144,128]{2,1,0:T(8,128)(2,1)S(1)} %pad_maximum_fusion.1), channel_id=1, source_target_pairs={{0,2},{1,3},{2,0},{3,1},{4,6},{5,7},{6,4},{7,5},{8,10},{9,11},{10,... | collective-permute-start | bytes 442376 | tf_op jit(solution)/shard_map/ppermute | solution.py:508
  19.5 1.6 %collective-permute-start.3 = (bf16[8,144,128]{2,1,0:T(8,128)(2,1)S(1)}, bf16[8,144,128]{2,1,0:T(8,128)(2,1)S(1)}, u32[]{:S(2)}, u32[]{:S(2)}) collective-permute-start(bf16[8,144,128]{2,1,0:T(8,128)(2,1)S(1)} %pad_maximum_fusion.own_ref), channel_id=1, source_target_pairs={{0,1},{1,0},{2,3},{3,2},{4,5},{5,4},{6,7},{7,6},{8,9},{9,8},{10,11... | collective-permute-start | bytes 884744 | tf_op jit(solution)/shard_map/ppermute | solution.py:534
  23.8 2.7 %collective-permute-start.5 = (bf16[512,128]{1,0:T(8,128)(2,1)S(1)}, bf16[512,128]{1,0:T(8,128)(2,1)S(1)}, u32[]{:S(2)}, u32[]{:S(2)}) collective-permute-start(bf16[512,128]{1,0:T(8,128)(2,1)S(1)} %get-tuple-element.61), channel_id=1, source_target_pairs={{0,1},{1,0},{2,3},{3,2},{4,5},{5,4},{6,7},{7,6},{8,9},{9,8},{10,11... | collective-permute-start | bytes 393224 | tf_op jit(solution)/shard_map/ppermute | solution.py:534
  24.1 7.9 %collective-permute-start.4 = (bf16[512,128]{1,0:T(8,128)(2,1)S(1)}, bf16[512,128]{1,0:T(8,128)(2,1)S(1)}, u32[]{:S(2)}, u32[]{:S(2)}) collective-permute-start(bf16[512,128]{1,0:T(8,128)(2,1)S(1)} %get-tuple-element.59), channel_id=1, source_target_pairs={{0,6},{1,7},{2,4},{3,5},{4,2},{5,3},{6,0},{7,1},{8,14},{9,15},{10,... | collective-permute-start | bytes 393224 | tf_op jit(solution)/shard_map/ppermute | solution.py:508
  26.5 9.6 %collective-permute-start.6 = (bf16[512,128]{1,0:T(8,128)(2,1)S(1)}, bf16[512,128]{1,0:T(8,128)(2,1)S(1)}, u32[]{:S(2)}, u32[]{:S(2)}) collective-permute-start(bf16[512,128]{1,0:T(8,128)(2,1)S(1)} %get-tuple-element.66), channel_id=1, source_target_pairs={{0,14},{1,11},{2,12},{3,9},{4,10},{5,15},{6,8},{7,13},{8,6},{9,3},... | collective-permute-start | bytes 393224 | tf_op jit(solution)/shard_map/ppermute | solution.py:517
  30.1 7.3 %collective-permute-start.7 = (bf16[512,128]{1,0:T(8,128)(2,1)S(1)}, bf16[512,128]{1,0:T(8,128)(2,1)S(1)}, u32[]{:S(2)}, u32[]{:S(2)}) collective-permute-start(bf16[512,128]{1,0:T(8,128)(2,1)S(1)} %get-tuple-element.67), channel_id=1, source_target_pairs={{0,4},{1,5},{2,6},{3,7},{4,0},{5,1},{6,2},{7,3},{8,12},{9,13},{10,... | collective-permute-start | bytes 393224 | tf_op jit(solution)/shard_map/ppermute | solution.py:508
  30.1 7.5 %collective-permute-start.8 = (bf16[512,128]{1,0:T(8,128)(2,1)S(1)}, bf16[512,128]{1,0:T(8,128)(2,1)S(1)}, u32[]{:S(2)}, u32[]{:S(2)}) collective-permute-start(bf16[512,128]{1,0:T(8,128)(2,1)S(1)} %get-tuple-element.68), channel_id=1, source_target_pairs={{0,2},{1,3},{2,0},{3,1},{4,6},{5,7},{6,4},{7,5},{8,10},{9,11},{10,... | collective-permute-start | bytes 393224 | tf_op jit(solution)/shard_map/ppermute | solution.py:508
  31.5 9.8 %collective-permute-start.9 = (bf16[512,128]{1,0:T(8,128)(2,1)S(1)}, bf16[512,128]{1,0:T(8,128)(2,1)S(1)}, u32[]{:S(2)}, u32[]{:S(2)}) collective-permute-start(bf16[512,128]{1,0:T(8,128)(2,1)S(1)} %get-tuple-element.70), channel_id=1, source_target_pairs={{0,12},{1,9},{2,14},{3,11},{4,8},{5,13},{6,10},{7,15},{8,4},{9,1},... | collective-permute-start | bytes 393224 | tf_op jit(solution)/shard_map/ppermute | solution.py:517
  41.3 2.0 %collective-permute-start.10 = (bf16[2048,128]{1,0:T(8,128)(2,1)S(1)}, bf16[2048,128]{1,0:T(8,128)(2,1)S(1)}, u32[]{:S(2)}, u32[]{:S(2)}) collective-permute-start(bf16[2048,128]{1,0:T(8,128)(2,1)S(1)} %constant_dynamic-update-slice_fusion), channel_id=1, source_target_pairs={{0,1},{1,0},{2,3},{3,2},{4,5},{5,4},{6,7},{7,6},{8,9},{9,8},{10,11... | collective-permute-start | bytes 1572872 | tf_op jit(solution)/shard_map/ppermute | solution.py:534
  44.8 5.9 %collective-permute-start.11 = (bf16[256,128]{1,0:T(8,128)(2,1)S(1)}, bf16[256,128]{1,0:T(8,128)(2,1)S(1)}, u32[]{:S(2)}, u32[]{:S(2)}) collective-permute-start(bf16[256,128]{1,0:T(8,128)(2,1)S(1)} %get-tuple-element.71), channel_id=1, source_target_pairs={{0,6},{1,7},{2,4},{3,5},{4,2},{5,3},{6,0},{7,1},{8,14},{9,15},{10,... | collective-permute-start | bytes 196616 | tf_op jit(solution)/shard_map/ppermute | solution.py:508
  46.4 4.5 %collective-permute-start.12 = (bf16[256,128]{1,0:T(8,128)(2,1)S(1)}, bf16[256,128]{1,0:T(8,128)(2,1)S(1)}, u32[]{:S(2)}, u32[]{:S(2)}) collective-permute-start(bf16[256,128]{1,0:T(8,128)(2,1)S(1)} %get-tuple-element.72), channel_id=1, source_target_pairs={{0,4},{1,5},{2,6},{3,7},{4,0},{5,1},{6,2},{7,3},{8,12},{9,13},{10,... | collective-permute-start | bytes 196616 | tf_op jit(solution)/shard_map/ppermute | solution.py:508
  47.2 4.4 %collective-permute-start.13 = (bf16[256,128]{1,0:T(8,128)(2,1)S(1)}, bf16[256,128]{1,0:T(8,128)(2,1)S(1)}, u32[]{:S(2)}, u32[]{:S(2)}) collective-permute-start(bf16[256,128]{1,0:T(8,128)(2,1)S(1)} %get-tuple-element.73), channel_id=1, source_target_pairs={{0,2},{1,3},{2,0},{3,1},{4,6},{5,7},{6,4},{7,5},{8,10},{9,11},{10,... | collective-permute-start | bytes 196616 | tf_op jit(solution)/shard_map/ppermute | solution.py:508
  53.2 1.6 %collective-permute-start.14 = (bf16[1024,128]{1,0:T(8,128)(2,1)S(1)}, bf16[1024,128]{1,0:T(8,128)(2,1)S(1)}, u32[]{:S(2)}, u32[]{:S(2)}) collective-permute-start(bf16[1024,128]{1,0:T(8,128)(2,1)S(1)} %get-tuple-element.79), channel_id=1, source_target_pairs={{0,1},{1,0},{2,3},{3,2},{4,5},{5,4},{6,7},{7,6},{8,9},{9,8},{10,11... | collective-permute-start | bytes 786440 | tf_op jit(solution)/shard_map/ppermute | solution.py:534
  54.9 8.6 %collective-permute-start.15 = (bf16[512,128]{1,0:T(8,128)(2,1)S(1)}, bf16[512,128]{1,0:T(8,128)(2,1)S(1)}, u32[]{:S(2)}, u32[]{:S(2)}) collective-permute-start(bf16[512,128]{1,0:T(8,128)(2,1)S(1)} %pad_maximum_fusion.4), channel_id=1, source_target_pairs={{0,14},{1,11},{2,12},{3,9},{4,10},{5,15},{6,8},{7,13},{8,6},{9,3},... | collective-permute-start | bytes 393224 | tf_op jit(solution)/shard_map/ppermute | solution.py:517
  58.6 8.0 %collective-permute-start.16 = (bf16[512,128]{1,0:T(8,128)(2,1)S(1)}, bf16[512,128]{1,0:T(8,128)(2,1)S(1)}, u32[]{:S(2)}, u32[]{:S(2)}) collective-permute-start(bf16[512,128]{1,0:T(8,128)(2,1)S(1)} %pad_maximum_fusion.5), channel_id=1, source_target_pairs={{0,12},{1,9},{2,14},{3,11},{4,8},{5,13},{6,10},{7,15},{8,4},{9,1},... | collective-permute-start | bytes 393224 | tf_op jit(solution)/shard_map/ppermute | solution.py:517
  59.3 8.4 %collective-permute-start.17 = (bf16[512,128]{1,0:T(8,128)(2,1)S(1)}, bf16[512,128]{1,0:T(8,128)(2,1)S(1)}, u32[]{:S(2)}, u32[]{:S(2)}) collective-permute-start(bf16[512,128]{1,0:T(8,128)(2,1)S(1)} %pad_maximum_fusion.6), channel_id=1, source_target_pairs={{0,6},{1,5},{2,4},{3,7},{4,2},{5,1},{6,0},{7,3},{8,14},{9,13},{10,... | collective-permute-start | bytes 393224 | tf_op jit(solution)/shard_map/ppermute | solution.py:517
  59.4 8.4 %collective-permute-start.18 = (bf16[512,128]{1,0:T(8,128)(2,1)S(1)}, bf16[512,128]{1,0:T(8,128)(2,1)S(1)}, u32[]{:S(2)}, u32[]{:S(2)}) collective-permute-start(bf16[512,128]{1,0:T(8,128)(2,1)S(1)} %pad_maximum_fusion.7), channel_id=1, source_target_pairs={{0,2},{1,1},{2,0},{3,3},{4,6},{5,5},{6,4},{7,7},{8,10},{9,9},{10,8... | collective-permute-start | bytes 393224 | tf_op jit(solution)/shard_map/ppermute | solution.py:517
  69.0 3.2 %collective-permute-start.19 = (bf16[4,256,128]{2,1,0:T(8,128)(2,1)S(1)}, bf16[4,256,128]{2,1,0:T(8,128)(2,1)S(1)}, u32[]{:S(2)}, u32[]{:S(2)}) collective-permute-start(bf16[4,256,128]{2,1,0:T(8,128)(2,1)S(1)} %get-tuple-element.84), channel_id=1, source_target_pairs={{0,1},{1,0},{2,3},{3,2},{4,5},{5,4},{6,7},{7,6},{8,9},{9,8},{10,11... | collective-permute-start | bytes 786440 | tf_op jit(solution)/shard_map/ppermute | solution.py:534
  72.3 7.8 %collective-permute-start.20 = (bf16[256,128]{1,0:T(8,128)(2,1)S(1)}, bf16[256,128]{1,0:T(8,128)(2,1)S(1)}, u32[]{:S(2)}, u32[]{:S(2)}) collective-permute-start(bf16[256,128]{1,0:T(8,128)(2,1)S(1)} %get-tuple-element.85), channel_id=1, source_target_pairs={{0,14},{1,7},{2,12},{3,5},{4,10},{5,3},{6,8},{7,1},{8,6},{9,15},{1... | collective-permute-start | bytes 196616 | tf_op jit(solution)/shard_map/ppermute | solution.py:517
  75.8 5.0 %collective-permute-start.21 = (bf16[256,128]{1,0:T(8,128)(2,1)S(1)}, bf16[256,128]{1,0:T(8,128)(2,1)S(1)}, u32[]{:S(2)}, u32[]{:S(2)}) collective-permute-start(bf16[256,128]{1,0:T(8,128)(2,1)S(1)} %get-tuple-element.86), channel_id=1, source_target_pairs={{0,4},{1,13},{2,6},{3,15},{4,0},{5,9},{6,2},{7,11},{8,12},{9,5},{1... | collective-permute-start | bytes 196616 | tf_op jit(solution)/shard_map/ppermute | solution.py:517
  76.4 6.1 %collective-permute-start.22 = (bf16[256,128]{1,0:T(8,128)(2,1)S(1)}, bf16[256,128]{1,0:T(8,128)(2,1)S(1)}, u32[]{:S(2)}, u32[]{:S(2)}) collective-permute-start(bf16[256,128]{1,0:T(8,128)(2,1)S(1)} %get-tuple-element.87), channel_id=1, source_target_pairs={{0,10},{1,3},{2,8},{3,1},{4,14},{5,7},{6,12},{7,5},{8,2},{9,11},{1... | collective-permute-start | bytes 196616 | tf_op jit(solution)/shard_map/ppermute | solution.py:517
  77.6 4.8 %collective-permute-start.23 = (bf16[256,128]{1,0:T(8,128)(2,1)S(1)}, bf16[256,128]{1,0:T(8,128)(2,1)S(1)}, u32[]{:S(2)}, u32[]{:S(2)}) collective-permute-start(bf16[256,128]{1,0:T(8,128)(2,1)S(1)} %get-tuple-element.88), channel_id=1, source_target_pairs={{0,0},{1,9},{2,2},{3,11},{4,4},{5,13},{6,6},{7,15},{8,8},{9,1},{10... | collective-permute-start | bytes 196616 | tf_op jit(solution)/shard_map/ppermute | solution.py:517
  82.4 2.6 %collective-permute-start.24 = (bf16[512,128]{1,0:T(8,128)(2,1)S(1)}, bf16[512,128]{1,0:T(8,128)(2,1)S(1)}, u32[]{:S(2)}, u32[]{:S(2)}) collective-permute-start(bf16[512,128]{1,0:T(8,128)(2,1)S(1)} %shard_map.107), channel_id=1, source_target_pairs={{0,1},{1,0},{2,3},{3,2},{4,5},{5,4},{6,7},{7,6},{8,9},{9,8},{10,11... | collective-permute-start | bytes 393224 | tf_op jit(solution)/shard_map/ppermute | solution.py:534

commit v14 on v13

--- a/solution.py
+++ b/solution.py
@@ -237,9 +237,7 @@
     return chip ^ jnp.where(core == 0, split[op][0], split[op][1])
 
 
-def project_kernel(
-    where_ref, feat_ref, weight_ref, mask_ref, present_ref, pay_ref, left_ref, live_ref, turned, packed
-):
+def project_kernel(feat_ref, weight_ref, live_in_ref, pay_ref, left_ref, live_ref, turned, packed):
     homologs, rows, _ = feat_ref.shape
     half = weight_ref.shape[0] // 2
     quarter = half // 2
@@ -252,15 +250,7 @@
     in_row = lax.broadcasted_iota(jnp.int32, (total, total), 1)
     order = in_row == (out_row & (homologs - 1)) * rows + out_row // homologs
     normed = nn(order.astype(F32).astype(BF16), normed).astype(BF16)
-    seq = lax.broadcasted_iota(jnp.int32, (homologs, 2 * homologs), 0)
-    lane = lax.broadcasted_iota(jnp.int32, (homologs, 2 * homologs), 1)
-    twice = (seq == (lane & (homologs - 1))).astype(F32).astype(BF16)
-    cols = present_ref.shape[1]
-    here = lax.broadcasted_iota(jnp.int32, (rows, cols), 1) == (
-        lax.broadcasted_iota(jnp.int32, (rows, cols), 0) + where_ref[0]
-    )
-    present = jnp.sum(jnp.where(here, present_ref[...].astype(F32), 0.0), axis=1, keepdims=True)
-    live = nn(mask_ref[...], twice) * present
+    live = live_in_ref[...]
     weight = weight_ref[...]
     blank = jnp.zeros((homologs, normed.shape[1]), BF16)
     for row in range(rows):
@@ -384,13 +374,13 @@
 
 
 def mix_rows_kernel(
-    where_ref, near3, far0, near2, near1, near0, far1, other_ref, out0, out1, out2, out3, lefts, rights, mixed
+    where_ref, near3, far0, far1, near2, near1, near0, other_ref, out0, out1, out2, out3, lefts, rights, mixed
 ):
     chip, core = where_ref[1], where_ref[2]
     count, rows, cols = lefts.shape[1:]
     block = count * rows
     place = 0
-    for step, near in ((3, near3), (None, far0), (2, near2), (1, near1), (0, near0), (None, far1)):
+    for step, near in ((3, near3), (None, far0), (None, far1), (2, near2), (1, near1), (0, near0)):
         if step is None:
             op = 0 if near is far0 else 1
             for half in range(2):
@@ -554,11 +544,13 @@
     where = jnp.stack([device * rows, chip, core]).astype(jnp.int32)
     present = resolved_residue_mask.reshape(1, cols)
     pay_rows = (half // 2 + 2) * rows
+    row_present = lax.dynamic_slice_in_dim(resolved_residue_mask, device * rows, rows).astype(F32)
+    live = alignment_mask.T.astype(F32) * row_present[:, None]
+    live = jnp.concatenate([live, live], axis=1)
     pay, left, live = run(
         project_kernel,
         [((pay_rows, LANES), BF16), ((2 * rows * half, LANES), BF16), ((rows, LANES), F32)],
-        where, homolog_features.astype(F32), homolog_to_sides_matrix.T, alignment_mask.T, present,
-        smem=(0,),
+        homolog_features.astype(F32), homolog_to_sides_matrix.T, live,
         scratch=[((rows * half // 2, LANES), F32), ((pay_rows, LANES), F32)],
     )
     far_z = chip_permute(pay, 4)
@@ -602,8 +594,8 @@
     far, later = lax.optimization_barrier((with_partner(made[2:4], made[4]), list(made[5:8])))
     far = split_exchange(far, FAR_SPLIT)
     came = [first] + exchange(later, NEAR_STEPS[1:])
-    came = [came[0], far[0], came[1], came[2], came[3], far[1]]
-    rights = [block if at in (1, 5) else block[near:] for at, block in enumerate(came)]
+    came = [came[0], far[0], far[1], came[1], came[2], came[3]]
+    rights = [block if at in (1, 2) else block[near:] for at, block in enumerate(came)]
     rights = jnp.concatenate(rights, axis=0)
     mixed = run(
         mix_rows_kernel,

time: 87.4 us -> 87.1 us (level)
  waiting for transfers between devices: 36 us -> 33.6 us
  starting transfers between devices: 36.5 us -> 38.2 us
    ppermute x6, starting transfers between devices: 4.14 us -> 5.73 us  [core_permute(): return lax.ppermute(block, 'wide', [(w, w ^ 1) for w in range(count)])]
    ppermute x9, waiting for transfers between devices: 11.6 us -> 10 us  [chip_permute(): lax.ppermute(block, 'wide', [(w, w ^ 2 * step) for w in range(count)])]
  transfers between devices with their start and end apart: 25 -> 25, of which waited for: 22 -> 19; matrix products, arithmetic and copies ran while one was open for 0% -> 0% of each run, Pallas kernels for 2% -> 2%
where the time goes in v14:
time: 87.1 us; the launch traced here: 86.9 us
  starting transfers between devices  38.2 us (44%)
  waiting for transfers between devices  33.6 us (39%)
  Pallas kernels  12 us (14%)
  local copies, waits for them, and re-layouts  1.42 us (2%)
  other arithmetic  1.41 us (2%)
    ppermute x10, starting transfers between devices, split_permute(): lax.ppermute(block, 'wide', [(w, w ^ 2 * steps[w % 2]) for w in range(cou...  17.5 us
    ppermute x10, waiting for transfers between devices, split_permute(): lax.ppermute(block, 'wide', [(w, w ^ 2 * steps[w % 2]) for w in range(cou...  16.8 us
    ppermute x9, starting transfers between devices, chip_permute(): lax.ppermute(block, 'wide', [(w, w ^ 2 * step) for w in range(count)])  15 us
    pallas_call x9, Pallas kernels, run(): pl.pallas_call(kernel, out_shape=[jax.ShapeDtypeStruct(shape, kind) for s...  12 us
    ppermute x9, waiting for transfers between devices, chip_permute(): lax.ppermute(block, 'wide', [(w, w ^ 2 * step) for w in range(count)])  10 us
    ppermute x6, waiting for transfers between devices, core_permute(): return lax.ppermute(block, 'wide', [(w, w ^ 1) for w in range(count)])  6.78 us
    ppermute x6, starting transfers between devices, core_permute(): return lax.ppermute(block, 'wide', [(w, w ^ 1) for w in range(count)])  5.73 us
  transfers between devices with their start and end apart: 25, of which 19 were waited for; matrix products, arithmetic and copies ran while one was open for 0% of the time, Pallas kernels for 2%

profile of v14, /device:TPU:0, one launch (start us, length us, event | category | flops | bytes accessed | tf_op | source)
XLA Modules:
  0.0 86.9 jit_solution(4632328499655002734)
XLA Ops:
  0.0 0.7 copy-done.7
  0.7 0.1 dynamic-slice_convert_fusion
  0.7 0.1 multiply_bitcast_fusion
  0.8 0.1 pad_maximum_fusion.9.live_in_ref
  0.9 1.0 %convert_element_type.10.feat_ref = f32[64,8,256]{2,1,0:T(8,128)S(1)} convert(bf16[64,8,256]{2,1,0:T(8,128)(2,1)} %param.11) | non-fusion elementwise | flops 131072 | bytes 786432 | tf_op jit(solution)/shard_map/convert_element_type | solution.py:553
  1.9 0.0 copy-start.1
  1.9 0.0 copy-start.2
  1.9 1.0 %shard_map.100 = (bf16[144,128]{1,0:T(8,128)(2,1)S(1)}, bf16[512,128]{1,0:T(8,128)(2,1)S(1)}, f32[8,128]{1,0:T(8,128)S(1)}) custom-call(f32[64,8,256]{2,1,0:T(8,128)S(1)} %convert_element_type.10.feat_ref, bf16[64,256]{1,0:T(8,128)(2,1)S(1)} %bitcast.13, f32[8,128]{1,0:T(8,128)S(1)} %pad_maximum_fusion.9.live_in_ref), custom_call_target="tpu_custom_call" | custom-call | flops 1500000000 | bytes 561152 | tf_op jit(solution)/shard_map/pallas_call | solution.py:216
  2.9 0.0 copy-start
  2.9 4.1 %collective-permute-start = (bf16[144,128]{1,0:T(8,128)(2,1)S(1)}, bf16[144,128]{1,0:T(8,128)(2,1)S(1)}, u32[]{:S(2)}, u32[]{:S(2)}) collective-permute-start(bf16[144,128]{1,0:T(8,128)(2,1)S(1)} %get-tuple-element.48), channel_id=1, source_target_pairs={{0,8},{1,9},{2,10},{3,11},{4,12},{5,13},{6,14},{7,15},{8,0},{9,1},... | collective-permute-start | bytes 110600 | tf_op jit(solution)/shard_map/ppermute | solution.py:498
  7.0 2.3 %collective-permute-done = bf16[144,128]{1,0:T(8,128)(2,1)S(1)} collective-permute-done((bf16[144,128]{1,0:T(8,128)(2,1)S(1)}, bf16[144,128]{1,0:T(8,128)(2,1)S(1)}, u32[]{:S(2)}, u32[]{:S(2)}) %collective-permute-start) | collective-permute-done | bytes 36896 | tf_op jit(solution)/shard_map/ppermute | solution.py:498
  9.3 1.6 %collective-permute-start.1 = (bf16[2,144,128]{2,1,0:T(8,128)(2,1)S(1)}, bf16[2,144,128]{2,1,0:T(8,128)(2,1)S(1)}, u32[]{:S(2)}, u32[]{:S(2)}) collective-permute-start(bf16[2,144,128]{2,1,0:T(8,128)(2,1)S(1)} %pad_maximum_fusion.8), channel_id=1, source_target_pairs={{0,4},{1,5},{2,6},{3,7},{4,0},{5,1},{6,2},{7,3},{8,12},{9,13},{10,... | collective-permute-start | bytes 221192 | tf_op jit(solution)/shard_map/ppermute | solution.py:498
  10.9 2.8 %collective-permute-done.1 = bf16[2,144,128]{2,1,0:T(8,128)(2,1)S(1)} collective-permute-done((bf16[2,144,128]{2,1,0:T(8,128)(2,1)S(1)}, bf16[2,144,128]{2,1,0:T(8,128)(2,1)S(1)}, u32[]{:S(2)}, u32[]{:S(2)}) %collective-permute-start.1) | collective-permute-done | bytes 73760 | tf_op jit(solution)/shard_map/ppermute | solution.py:498
  13.8 1.8 %collective-permute-start.2 = (bf16[4,144,128]{2,1,0:T(8,128)(2,1)S(1)}, bf16[4,144,128]{2,1,0:T(8,128)(2,1)S(1)}, u32[]{:S(2)}, u32[]{:S(2)}) collective-permute-start(bf16[4,144,128]{2,1,0:T(8,128)(2,1)S(1)} %pad_maximum_fusion.1), channel_id=1, source_target_pairs={{0,2},{1,3},{2,0},{3,1},{4,6},{5,7},{6,4},{7,5},{8,10},{9,11},{10,... | collective-permute-start | bytes 442376 | tf_op jit(solution)/shard_map/ppermute | solution.py:498
  15.5 0.1 pad_add_fusion.where_ref
  15.7 0.6 copy-done.6
  16.3 1.7 %shard_map.101 = (f32[8,128,128]{2,1,0:T(8,128)S(1)}, bf16[128,1024]{1,0:T(8,128)(2,1)S(1)}, bf16[2,640,128]{2,1,0:T(8,128)(2,1)S(1)}, bf16[2,128,128]{2,1,0:T(8,128)(2,1)S(1)}) custom-call(s32[3]{0:T(128)S(1)} %pad_add_fusion.where_ref, s32[128]{0:T(128)S(1)} %copy-done.6, s32[1,128]{1,0:T(1,128)S(1)} %bitcast.14, bf16[8,128,128]{2,1,0:T(8,128)(2,1)S(1)} %copy-done.1, ...), custom_call_target="tpu_custom_call" | custom-call | flops 1500000000 | bytes 935436 | tf_op jit(solution)/shard_map/pallas_call | solution.py:216
  18.0 1.0 %collective-permute-done.2 = bf16[4,144,128]{2,1,0:T(8,128)(2,1)S(1)} collective-permute-done((bf16[4,144,128]{2,1,0:T(8,128)(2,1)S(1)}, bf16[4,144,128]{2,1,0:T(8,128)(2,1)S(1)}, u32[]{:S(2)}, u32[]{:S(2)}) %collective-permute-start.2) | collective-permute-done | bytes 147488 | tf_op jit(solution)/shard_map/ppermute | solution.py:498
  19.0 0.1 collective-permute-start.3
  19.1 1.6 %collective-permute-done.3.other_ref = bf16[8,144,128]{2,1,0:T(8,128)(2,1)S(1)} collective-permute-done((bf16[8,144,128]{2,1,0:T(8,128)(2,1)S(1)}, bf16[8,144,128]{2,1,0:T(8,128)(2,1)S(1)}, u32[]{:S(2)}, u32[]{:S(2)}) %collective-permute-start.3) | collective-permute-done | bytes 294944 | tf_op jit(solution)/shard_map/ppermute | solution.py:524
  20.7 2.7 %shard_map.102 = (f32[8,128,128]{2,1,0:T(8,128)S(1)}, f32[8,128,128]{2,1,0:T(8,128)S(1)}, bf16[256,128]{1,0:T(8,128)(2,1)S(1)}, bf16[256,128]{1,0:T(8,128)(2,1)S...) custom-call(s32[3]{0:T(128)S(1)} %pad_add_fusion.where_ref, ...), custom_call_target="tpu_custom_call" | custom-call | flops 4000000000 | bytes 1840140 | tf_op jit(solution)/shard_map/pallas_call | solution.py:216
  23.4 0.2 collective-permute-start.5
  23.6 2.5 %collective-permute-start.4 = (bf16[512,128]{1,0:T(8,128)(2,1)S(1)}, bf16[512,128]{1,0:T(8,128)(2,1)S(1)}, u32[]{:S(2)}, u32[]{:S(2)}) collective-permute-start(bf16[512,128]{1,0:T(8,128)(2,1)S(1)} %get-tuple-element.59), channel_id=1, source_target_pairs={{0,6},{1,7},{2,4},{3,5},{4,2},{5,3},{6,0},{7,1},{8,14},{9,15},{10,... | collective-permute-start | bytes 393224 | tf_op jit(solution)/shard_map/ppermute | solution.py:498
  26.1 3.6 %collective-permute-start.6 = (bf16[512,128]{1,0:T(8,128)(2,1)S(1)}, bf16[512,128]{1,0:T(8,128)(2,1)S(1)}, u32[]{:S(2)}, u32[]{:S(2)}) collective-permute-start(bf16[512,128]{1,0:T(8,128)(2,1)S(1)} %get-tuple-element.66), channel_id=1, source_target_pairs={{0,14},{1,11},{2,12},{3,9},{4,10},{5,15},{6,8},{7,13},{8,6},{9,3},... | collective-permute-start | bytes 393224 | tf_op jit(solution)/shard_map/ppermute | solution.py:507
  29.7 0.3 collective-permute-start.7
  30.0 0.0 collective-permute-start.8
  30.0 1.5 %collective-permute-start.9 = (bf16[512,128]{1,0:T(8,128)(2,1)S(1)}, bf16[512,128]{1,0:T(8,128)(2,1)S(1)}, u32[]{:S(2)}, u32[]{:S(2)}) collective-permute-start(bf16[512,128]{1,0:T(8,128)(2,1)S(1)} %get-tuple-element.69), channel_id=1, source_target_pairs={{0,2},{1,3},{2,0},{3,1},{4,6},{5,7},{6,4},{7,5},{8,10},{9,11},{10,... | collective-permute-start | bytes 393224 | tf_op jit(solution)/shard_map/ppermute | solution.py:498
  31.5 0.0 collective-permute-done.4.near3
  31.5 4.3 %collective-permute-done.6.far0 = bf16[512,128]{1,0:T(8,128)(2,1)S(1)} collective-permute-done((bf16[512,128]{1,0:T(8,128)(2,1)S(1)}, bf16[512,128]{1,0:T(8,128)(2,1)S(1)}, u32[]{:S(2)}, u32[]{:S(2)}) %collective-permute-start.6) | collective-permute-done | bytes 131104 | tf_op jit(solution)/shard_map/ppermute | solution.py:507
  35.8 2.8 %collective-permute-done.7.far1 = bf16[512,128]{1,0:T(8,128)(2,1)S(1)} collective-permute-done((bf16[512,128]{1,0:T(8,128)(2,1)S(1)}, bf16[512,128]{1,0:T(8,128)(2,1)S(1)}, u32[]{:S(2)}, u32[]{:S(2)}) %collective-permute-start.7) | collective-permute-done | bytes 131104 | tf_op jit(solution)/shard_map/ppermute | solution.py:507
  38.5 0.0 collective-permute-done.8.near2
  38.6 2.0 %collective-permute-start.10 = (bf16[2048,128]{1,0:T(8,128)(2,1)S(1)}, bf16[2048,128]{1,0:T(8,128)(2,1)S(1)}, u32[]{:S(2)}, u32[]{:S(2)}) collective-permute-start(bf16[2048,128]{1,0:T(8,128)(2,1)S(1)} %slice_dynamic-update-slice_fusion.3), channel_id=1, source_target_pairs={{0,1},{1,0},{2,3},{3,2},{4,5},{5,4},{6,7},{7,6},{8,9},{9,8},{10,11... | collective-permute-start | bytes 1572872 | tf_op jit(solution)/shard_map/ppermute | solution.py:524
  40.6 1.5 %collective-permute-done.10.other_ref = bf16[2048,128]{1,0:T(8,128)(2,1)S(1)} collective-permute-done((bf16[2048,128]{1,0:T(8,128)(2,1)S(1)}, bf16[2048,128]{1,0:T(8,128)(2,1)S(1)}, u32[]{:S(2)}, u32[]{:S(2)}) %collective-permute-start.10) | collective-permute-done | bytes 524320 | tf_op jit(solution)/shard_map/ppermute | solution.py:524
  42.2 1.4 %shard_map.103 = (bf16[256,128]{1,0:T(8,128)(2,1)S(1)}, bf16[256,128]{1,0:T(8,128)(2,1)S(1)}, bf16[256,128]{1,0:T(8,128)(2,1)S(1)}, bf16[256,128]{1,0:T(8,128)(2,1)S(1)}) custom-call(s32[3]{0:T(128)S(1)} %pad_add_fusion.where_ref, bf16[512,128]{1,0:T(8,128)(2,1)S(1)} %collective-permute-done.4.near3, bf16[512,128]{1,0:T(8,128)(2,1)S(1)} %collective-permute-done.6.far0, ...), custom_call_target="tpu_custom_call" | custom-call | flops 1500000000 | bytes 1310732 | tf_op jit(solution)/shard_map/pallas_call | solution.py:216
  43.6 2.4 %collective-permute-start.11 = (bf16[256,128]{1,0:T(8,128)(2,1)S(1)}, bf16[256,128]{1,0:T(8,128)(2,1)S(1)}, u32[]{:S(2)}, u32[]{:S(2)}) collective-permute-start(bf16[256,128]{1,0:T(8,128)(2,1)S(1)} %get-tuple-element.71), channel_id=1, source_target_pairs={{0,6},{1,7},{2,4},{3,5},{4,2},{5,3},{6,0},{7,1},{8,14},{9,15},{10,... | collective-permute-start | bytes 196616 | tf_op jit(solution)/shard_map/ppermute | solution.py:498
  46.0 0.8 collective-permute-start.12
  46.8 0.4 collective-permute-start.13
  47.2 2.0 %collective-permute-done.11.in0 = bf16[256,128]{1,0:T(8,128)(2,1)S(1)} collective-permute-done((bf16[256,128]{1,0:T(8,128)(2,1)S(1)}, bf16[256,128]{1,0:T(8,128)(2,1)S(1)}, u32[]{:S(2)}, u32[]{:S(2)}) %collective-permute-start.11) | collective-permute-done | bytes 65568 | tf_op jit(solution)/shard_map/ppermute | solution.py:498
  49.2 1.4 %collective-permute-done.12.in1 = bf16[256,128]{1,0:T(8,128)(2,1)S(1)} collective-permute-done((bf16[256,128]{1,0:T(8,128)(2,1)S(1)}, bf16[256,128]{1,0:T(8,128)(2,1)S(1)}, u32[]{:S(2)}, u32[]{:S(2)}) %collective-permute-start.12) | collective-permute-done | bytes 65568 | tf_op jit(solution)/shard_map/ppermute | solution.py:498
  50.5 0.5 collective-permute-done.13.in2
  51.1 1.7 %shard_map.104 = (f32[8,128,128]{2,1,0:T(8,128)S(1)}, f32[8,128,128]{2,1,0:T(8,128)S(1)}, bf16[256,128]{1,0:T(8,128)(2,1)S(1)}, bf16[256,128]{1,0:T(8,128)(2,1)S...) custom-call(s32[3]{0:T(128)S(1)} %pad_add_fusion.where_ref, ...), custom_call_target="tpu_custom_call" | custom-call | flops 1500000000 | bytes 1704972 | tf_op jit(solution)/shard_map/pallas_call | solution.py:216
  52.8 0.1 collective-permute-start.14
  52.8 1.5 %collective-permute-done.14 = bf16[1024,128]{1,0:T(8,128)(2,1)S(1)} collective-permute-done((bf16[1024,128]{1,0:T(8,128)(2,1)S(1)}, bf16[1024,128]{1,0:T(8,128)(2,1)S(1)}, u32[]{:S(2)}, u32[]{:S(2)}) %collective-permute-start.14) | collective-permute-done | bytes 262176 | tf_op jit(solution)/shard_map/ppermute | solution.py:524
  54.4 3.8 %collective-permute-start.15 = (bf16[512,128]{1,0:T(8,128)(2,1)S(1)}, bf16[512,128]{1,0:T(8,128)(2,1)S(1)}, u32[]{:S(2)}, u32[]{:S(2)}) collective-permute-start(bf16[512,128]{1,0:T(8,128)(2,1)S(1)} %pad_maximum_fusion.4), channel_id=1, source_target_pairs={{0,14},{1,11},{2,12},{3,9},{4,10},{5,15},{6,8},{7,13},{8,6},{9,3},... | collective-permute-start | bytes 393224 | tf_op jit(solution)/shard_map/ppermute | solution.py:507
  58.2 0.6 collective-permute-start.16
  58.7 0.1 collective-permute-start.17
  58.9 3.2 %collective-permute-start.18 = (bf16[512,128]{1,0:T(8,128)(2,1)S(1)}, bf16[512,128]{1,0:T(8,128)(2,1)S(1)}, u32[]{:S(2)}, u32[]{:S(2)}) collective-permute-start(bf16[512,128]{1,0:T(8,128)(2,1)S(1)} %pad_maximum_fusion.7), channel_id=1, source_target_pairs={{0,2},{1,1},{2,0},{3,3},{4,6},{5,5},{6,4},{7,7},{8,10},{9,9},{10,8... | collective-permute-start | bytes 393224 | tf_op jit(solution)/shard_map/ppermute | solution.py:507
  62.1 1.0 %collective-permute-done.15.came0 = bf16[512,128]{1,0:T(8,128)(2,1)S(1)} collective-permute-done((bf16[512,128]{1,0:T(8,128)(2,1)S(1)}, bf16[512,128]{1,0:T(8,128)(2,1)S(1)}, u32[]{:S(2)}, u32[]{:S(2)}) %collective-permute-start.15) | collective-permute-done | bytes 131104 | tf_op jit(solution)/shard_map/ppermute | solution.py:507
  63.1 3.0 %collective-permute-done.16.came1 = bf16[512,128]{1,0:T(8,128)(2,1)S(1)} collective-permute-done((bf16[512,128]{1,0:T(8,128)(2,1)S(1)}, bf16[512,128]{1,0:T(8,128)(2,1)S(1)}, u32[]{:S(2)}, u32[]{:S(2)}) %collective-permute-start.16) | collective-permute-done | bytes 131104 | tf_op jit(solution)/shard_map/ppermute | solution.py:507
  66.2 1.1 %collective-permute-done.17.came2 = bf16[512,128]{1,0:T(8,128)(2,1)S(1)} collective-permute-done((bf16[512,128]{1,0:T(8,128)(2,1)S(1)}, bf16[512,128]{1,0:T(8,128)(2,1)S(1)}, u32[]{:S(2)}, u32[]{:S(2)}) %collective-permute-start.17) | collective-permute-done | bytes 131104 | tf_op jit(solution)/shard_map/ppermute | solution.py:507
  67.3 1.2 %shard_map.105 = (f32[4,256,128]{2,1,0:T(8,128)S(1)}, bf16[4,256,128]{2,1,0:T(8,128)(2,1)S(1)}) custom-call(s32[3]{0:T(128)S(1)} %pad_add_fusion.where_ref, bf16[512,128]{1,0:T(8,128)(2,1)S(1)} %collective-permute-done.15.came0, bf16[512,128]{1,0:T(8,128)(2,1)S(1)} %collective-permute-done.16.came1, bf16[512,128]{1,0:T(8,128)(2,1)S(1)} %collective-permute-done.17.came2, ...), custom_call_target="tpu_custom_call" | custom-call | flops 1500000000 | bytes 524300 | tf_op jit(solution)/shard_map/pallas_call | solution.py:216
  68.5 1.7 %collective-permute-start.19 = (bf16[4,256,128]{2,1,0:T(8,128)(2,1)S(1)}, bf16[4,256,128]{2,1,0:T(8,128)(2,1)S(1)}, u32[]{:S(2)}, u32[]{:S(2)}) collective-permute-start(bf16[4,256,128]{2,1,0:T(8,128)(2,1)S(1)} %get-tuple-element.84), channel_id=1, source_target_pairs={{0,1},{1,0},{2,3},{3,2},{4,5},{5,4},{6,7},{7,6},{8,9},{9,8},{10,11... | collective-permute-start | bytes 786440 | tf_op jit(solution)/shard_map/ppermute | solution.py:524
  70.2 1.2 %collective-permute-done.19.got_ref = bf16[4,256,128]{2,1,0:T(8,128)(2,1)S(1)} collective-permute-done((bf16[4,256,128]{2,1,0:T(8,128)(2,1)S(1)}, bf16[4,256,128]{2,1,0:T(8,128)(2,1)S(1)}, u32[]{:S(2)}, u32[]{:S(2)}) %collective-permute-start.19) | collective-permute-done | bytes 262176 | tf_op jit(solution)/shard_map/ppermute | solution.py:524
  71.4 0.1 shard_map.106
  71.5 4.0 %collective-permute-start.20 = (bf16[256,128]{1,0:T(8,128)(2,1)S(1)}, bf16[256,128]{1,0:T(8,128)(2,1)S(1)}, u32[]{:S(2)}, u32[]{:S(2)}) collective-permute-start(bf16[256,128]{1,0:T(8,128)(2,1)S(1)} %get-tuple-element.85), channel_id=1, source_target_pairs={{0,14},{1,7},{2,12},{3,5},{4,10},{5,3},{6,8},{7,1},{8,6},{9,15},{1... | collective-permute-start | bytes 196616 | tf_op jit(solution)/shard_map/ppermute | solution.py:507
  75.4 0.6 collective-permute-start.21
  76.0 0.8 collective-permute-start.22
  76.8 0.7 collective-permute-start.23
  77.5 1.4 %collective-permute-done.20.refs_0_.came0 = bf16[256,128]{1,0:T(8,128)(2,1)S(1)} collective-permute-done((bf16[256,128]{1,0:T(8,128)(2,1)S(1)}, bf16[256,128]{1,0:T(8,128)(2,1)S(1)}, u32[]{:S(2)}, u32[]{:S(2)}) %collective-permute-start.20) | collective-permute-done | bytes 65568 | tf_op jit(solution)/shard_map/ppermute | solution.py:507
  78.9 1.5 %collective-permute-done.21.refs_1_.came1 = bf16[256,128]{1,0:T(8,128)(2,1)S(1)} collective-permute-done((bf16[256,128]{1,0:T(8,128)(2,1)S(1)}, bf16[256,128]{1,0:T(8,128)(2,1)S(1)}, u32[]{:S(2)}, u32[]{:S(2)}) %collective-permute-start.21) | collective-permute-done | bytes 65568 | tf_op jit(solution)/shard_map/ppermute | solution.py:507
  80.4 1.7 %collective-permute-done.22.refs_2_.came2 = bf16[256,128]{1,0:T(8,128)(2,1)S(1)} collective-permute-done((bf16[256,128]{1,0:T(8,128)(2,1)S(1)}, bf16[256,128]{1,0:T(8,128)(2,1)S(1)}, u32[]{:S(2)}, u32[]{:S(2)}) %collective-permute-start.22) | collective-permute-done | bytes 65568 | tf_op jit(solution)/shard_map/ppermute | solution.py:507
  82.1 1.6 %collective-permute-start.24 = (bf16[512,128]{1,0:T(8,128)(2,1)S(1)}, bf16[512,128]{1,0:T(8,128)(2,1)S(1)}, u32[]{:S(2)}, u32[]{:S(2)}) collective-permute-start(bf16[512,128]{1,0:T(8,128)(2,1)S(1)} %shard_map.107), channel_id=1, source_target_pairs={{0,1},{1,0},{2,3},{3,2},{4,5},{5,4},{6,7},{7,6},{8,9},{9,8},{10,11... | collective-permute-start | bytes 393224 | tf_op jit(solution)/shard_map/ppermute | solution.py:524
  83.7 1.0 %collective-permute-done.24.other_ref = bf16[512,128]{1,0:T(8,128)(2,1)S(1)} collective-permute-done((bf16[512,128]{1,0:T(8,128)(2,1)S(1)}, bf16[512,128]{1,0:T(8,128)(2,1)S(1)}, u32[]{:S(2)}, u32[]{:S(2)}) %collective-permute-start.24) | collective-permute-done | bytes 131104 | tf_op jit(solution)/shard_map/ppermute | solution.py:524
  84.7 2.2 %shard_map.108 = bf16[8,128,128]{2,1,0:T(8,128)(2,1)} custom-call(s32[3]{0:T(128)S(1)} %pad_add_fusion.where_ref, bf16[256,128]{1,0:T(8,128)(2,1)S(1)} %collective-permute-done.20.refs_0_.came0, bf16[256,128]{1,0:T(8,128)(2,1)S(1)} %collective-permute-done.21.refs_1_.came1, bf16[256,128]{1,0:T(8,128)(2,1)S(1)} %collective-permute-done.22.refs_2_.came2, ...), custom_call_target="tpu_custom_call" | custom-call | flops 1500000000 | bytes 1507340 | tf_op jit(solution)/shard_map/pallas_call | solution.py:216
  (34 shorter events, 0.3 us)
Async XLA Ops:
  0.0 0.7 copy-start.7
  0.0 0.7 copy-start.8
  0.9 1.0 %copy-start.4 = (bf16[256,64]{0,1:T(8,128)(2,1)S(1)}, bf16[256,64]{0,1:T(8,128)(2,1)}, u32[]{:S(2)}) copy-start(bf16[256,64]{0,1:T(8,128)(2,1)} %param.16) | copy-start | bytes 98308
  1.9 13.7 %copy-start.1 = (bf16[8,128,128]{2,1,0:T(8,128)(2,1)S(1)}, bf16[8,128,128]{2,1,0:T(8,128)(2,1)}, u32[]{:S(2)}) copy-start(bf16[8,128,128]{2,1,0:T(8,128)(2,1)} %pair_ref.1) | copy-start | bytes 786436
  1.9 13.7 %copy-start.2 = (bf16[1024,128]{1,0:T(8,128)(2,1)S(1)}, bf16[1024,128]{1,0:T(8,128)(2,1)}, u32[]{:S(2)}) copy-start(bf16[1024,128]{1,0:T(8,128)(2,1)} %outer_ref.1) | copy-start | bytes 786436
  2.9 12.8 %copy-start = (bf16[2,128,640]{2,1,0:T(8,128)(2,1)S(1)}, bf16[2,128,640]{2,1,0:T(8,128)(2,1)}, u32[]{:S(2)}) copy-start(bf16[2,128,640]{2,1,0:T(8,128)(2,1)} %proj_ref.1) | copy-start | bytes 983044
  2.9 6.4 %collective-permute-start = (bf16[144,128]{1,0:T(8,128)(2,1)S(1)}, bf16[144,128]{1,0:T(8,128)(2,1)S(1)}, u32[]{:S(2)}, u32[]{:S(2)}) collective-permute-start(bf16[144,128]{1,0:T(8,128)(2,1)S(1)} %get-tuple-element.48), channel_id=1, source_target_pairs={{0,8},{1,9},{2,10},{3,11},{4,12},{5,13},{6,14},{7,15},{8,0},{9,1},... | collective-permute-start | bytes 110600 | tf_op jit(solution)/shard_map/ppermute | solution.py:498
  9.3 4.4 %collective-permute-start.1 = (bf16[2,144,128]{2,1,0:T(8,128)(2,1)S(1)}, bf16[2,144,128]{2,1,0:T(8,128)(2,1)S(1)}, u32[]{:S(2)}, u32[]{:S(2)}) collective-permute-start(bf16[2,144,128]{2,1,0:T(8,128)(2,1)S(1)} %pad_maximum_fusion.8), channel_id=1, source_target_pairs={{0,4},{1,5},{2,6},{3,7},{4,0},{5,1},{6,2},{7,3},{8,12},{9,13},{10,... | collective-permute-start | bytes 221192 | tf_op jit(solution)/shard_map/ppermute | solution.py:498
  10.9 4.7 %copy-start.3 = (bf16[2,128,128]{2,1,0:T(8,128)(2,1)S(1)}, bf16[2,128,128]{2,1,0:T(8,128)(2,1)}, u32[]{:S(2)}) copy-start(bf16[2,128,128]{2,1,0:T(8,128)(2,1)} %out_ref.1) | copy-start | bytes 196612
  10.9 4.7 %copy-start.5 = (bf16[66,128]{1,0:T(8,128)(2,1)S(1)}, bf16[66,128]{1,0:T(8,128)(2,1)}, u32[]{:S(2)}) copy-start(bf16[66,128]{1,0:T(8,128)(2,1)} %table_ref.1) | copy-start | bytes 50692
  13.8 5.2 %collective-permute-start.2 = (bf16[4,144,128]{2,1,0:T(8,128)(2,1)S(1)}, bf16[4,144,128]{2,1,0:T(8,128)(2,1)S(1)}, u32[]{:S(2)}, u32[]{:S(2)}) collective-permute-start(bf16[4,144,128]{2,1,0:T(8,128)(2,1)S(1)} %pad_maximum_fusion.1), channel_id=1, source_target_pairs={{0,2},{1,3},{2,0},{3,1},{4,6},{5,7},{6,4},{7,5},{8,10},{9,11},{10,... | collective-permute-start | bytes 442376 | tf_op jit(solution)/shard_map/ppermute | solution.py:498
  15.6 0.7 copy-start.6
  19.0 1.6 %collective-permute-start.3 = (bf16[8,144,128]{2,1,0:T(8,128)(2,1)S(1)}, bf16[8,144,128]{2,1,0:T(8,128)(2,1)S(1)}, u32[]{:S(2)}, u32[]{:S(2)}) collective-permute-start(bf16[8,144,128]{2,1,0:T(8,128)(2,1)S(1)} %pad_maximum_fusion.own_ref), channel_id=1, source_target_pairs={{0,1},{1,0},{2,3},{3,2},{4,5},{5,4},{6,7},{7,6},{8,9},{9,8},{10,11... | collective-permute-start | bytes 884744 | tf_op jit(solution)/shard_map/ppermute | solution.py:524
  23.4 2.7 %collective-permute-start.5 = (bf16[512,128]{1,0:T(8,128)(2,1)S(1)}, bf16[512,128]{1,0:T(8,128)(2,1)S(1)}, u32[]{:S(2)}, u32[]{:S(2)}) collective-permute-start(bf16[512,128]{1,0:T(8,128)(2,1)S(1)} %get-tuple-element.61), channel_id=1, source_target_pairs={{0,1},{1,0},{2,3},{3,2},{4,5},{5,4},{6,7},{7,6},{8,9},{9,8},{10,11... | collective-permute-start | bytes 393224 | tf_op jit(solution)/shard_map/ppermute | solution.py:524
  23.6 7.9 %collective-permute-start.4 = (bf16[512,128]{1,0:T(8,128)(2,1)S(1)}, bf16[512,128]{1,0:T(8,128)(2,1)S(1)}, u32[]{:S(2)}, u32[]{:S(2)}) collective-permute-start(bf16[512,128]{1,0:T(8,128)(2,1)S(1)} %get-tuple-element.59), channel_id=1, source_target_pairs={{0,6},{1,7},{2,4},{3,5},{4,2},{5,3},{6,0},{7,1},{8,14},{9,15},{10,... | collective-permute-start | bytes 393224 | tf_op jit(solution)/shard_map/ppermute | solution.py:498
  26.1 9.6 %collective-permute-start.6 = (bf16[512,128]{1,0:T(8,128)(2,1)S(1)}, bf16[512,128]{1,0:T(8,128)(2,1)S(1)}, u32[]{:S(2)}, u32[]{:S(2)}) collective-permute-start(bf16[512,128]{1,0:T(8,128)(2,1)S(1)} %get-tuple-element.66), channel_id=1, source_target_pairs={{0,14},{1,11},{2,12},{3,9},{4,10},{5,15},{6,8},{7,13},{8,6},{9,3},... | collective-permute-start | bytes 393224 | tf_op jit(solution)/shard_map/ppermute | solution.py:507
  29.7 8.8 %collective-permute-start.7 = (bf16[512,128]{1,0:T(8,128)(2,1)S(1)}, bf16[512,128]{1,0:T(8,128)(2,1)S(1)}, u32[]{:S(2)}, u32[]{:S(2)}) collective-permute-start(bf16[512,128]{1,0:T(8,128)(2,1)S(1)} %get-tuple-element.67), channel_id=1, source_target_pairs={{0,12},{1,9},{2,14},{3,11},{4,8},{5,13},{6,10},{7,15},{8,4},{9,1},... | collective-permute-start | bytes 393224 | tf_op jit(solution)/shard_map/ppermute | solution.py:507
  30.0 8.6 %collective-permute-start.8 = (bf16[512,128]{1,0:T(8,128)(2,1)S(1)}, bf16[512,128]{1,0:T(8,128)(2,1)S(1)}, u32[]{:S(2)}, u32[]{:S(2)}) collective-permute-start(bf16[512,128]{1,0:T(8,128)(2,1)S(1)} %get-tuple-element.68), channel_id=1, source_target_pairs={{0,4},{1,5},{2,6},{3,7},{4,0},{5,1},{6,2},{7,3},{8,12},{9,13},{10,... | collective-permute-start | bytes 393224 | tf_op jit(solution)/shard_map/ppermute | solution.py:498
  30.0 8.6 %collective-permute-start.9 = (bf16[512,128]{1,0:T(8,128)(2,1)S(1)}, bf16[512,128]{1,0:T(8,128)(2,1)S(1)}, u32[]{:S(2)}, u32[]{:S(2)}) collective-permute-start(bf16[512,128]{1,0:T(8,128)(2,1)S(1)} %get-tuple-element.69), channel_id=1, source_target_pairs={{0,2},{1,3},{2,0},{3,1},{4,6},{5,7},{6,4},{7,5},{8,10},{9,11},{10,... | collective-permute-start | bytes 393224 | tf_op jit(solution)/shard_map/ppermute | solution.py:498
  38.6 3.6 %collective-permute-start.10 = (bf16[2048,128]{1,0:T(8,128)(2,1)S(1)}, bf16[2048,128]{1,0:T(8,128)(2,1)S(1)}, u32[]{:S(2)}, u32[]{:S(2)}) collective-permute-start(bf16[2048,128]{1,0:T(8,128)(2,1)S(1)} %slice_dynamic-update-slice_fusion.3), channel_id=1, source_target_pairs={{0,1},{1,0},{2,3},{3,2},{4,5},{5,4},{6,7},{7,6},{8,9},{9,8},{10,11... | collective-permute-start | bytes 1572872 | tf_op jit(solution)/shard_map/ppermute | solution.py:524
  43.6 5.5 %collective-permute-start.11 = (bf16[256,128]{1,0:T(8,128)(2,1)S(1)}, bf16[256,128]{1,0:T(8,128)(2,1)S(1)}, u32[]{:S(2)}, u32[]{:S(2)}) collective-permute-start(bf16[256,128]{1,0:T(8,128)(2,1)S(1)} %get-tuple-element.71), channel_id=1, source_target_pairs={{0,6},{1,7},{2,4},{3,5},{4,2},{5,3},{6,0},{7,1},{8,14},{9,15},{10,... | collective-permute-start | bytes 196616 | tf_op jit(solution)/shard_map/ppermute | solution.py:498
  46.0 4.5 %collective-permute-start.12 = (bf16[256,128]{1,0:T(8,128)(2,1)S(1)}, bf16[256,128]{1,0:T(8,128)(2,1)S(1)}, u32[]{:S(2)}, u32[]{:S(2)}) collective-permute-start(bf16[256,128]{1,0:T(8,128)(2,1)S(1)} %get-tuple-element.72), channel_id=1, source_target_pairs={{0,4},{1,5},{2,6},{3,7},{4,0},{5,1},{6,2},{7,3},{8,12},{9,13},{10,... | collective-permute-start | bytes 196616 | tf_op jit(solution)/shard_map/ppermute | solution.py:498
  46.8 4.3 %collective-permute-start.13 = (bf16[256,128]{1,0:T(8,128)(2,1)S(1)}, bf16[256,128]{1,0:T(8,128)(2,1)S(1)}, u32[]{:S(2)}, u32[]{:S(2)}) collective-permute-start(bf16[256,128]{1,0:T(8,128)(2,1)S(1)} %get-tuple-element.73), channel_id=1, source_target_pairs={{0,2},{1,3},{2,0},{3,1},{4,6},{5,7},{6,4},{7,5},{8,10},{9,11},{10,... | collective-permute-start | bytes 196616 | tf_op jit(solution)/shard_map/ppermute | solution.py:498
  52.8 1.6 %collective-permute-start.14 = (bf16[1024,128]{1,0:T(8,128)(2,1)S(1)}, bf16[1024,128]{1,0:T(8,128)(2,1)S(1)}, u32[]{:S(2)}, u32[]{:S(2)}) collective-permute-start(bf16[1024,128]{1,0:T(8,128)(2,1)S(1)} %get-tuple-element.79), channel_id=1, source_target_pairs={{0,1},{1,0},{2,3},{3,2},{4,5},{5,4},{6,7},{7,6},{8,9},{9,8},{10,11... | collective-permute-start | bytes 786440 | tf_op jit(solution)/shard_map/ppermute | solution.py:524
  54.4 8.7 %collective-permute-start.15 = (bf16[512,128]{1,0:T(8,128)(2,1)S(1)}, bf16[512,128]{1,0:T(8,128)(2,1)S(1)}, u32[]{:S(2)}, u32[]{:S(2)}) collective-permute-start(bf16[512,128]{1,0:T(8,128)(2,1)S(1)} %pad_maximum_fusion.4), channel_id=1, source_target_pairs={{0,14},{1,11},{2,12},{3,9},{4,10},{5,15},{6,8},{7,13},{8,6},{9,3},... | collective-permute-start | bytes 393224 | tf_op jit(solution)/shard_map/ppermute | solution.py:507
  58.2 8.0 %collective-permute-start.16 = (bf16[512,128]{1,0:T(8,128)(2,1)S(1)}, bf16[512,128]{1,0:T(8,128)(2,1)S(1)}, u32[]{:S(2)}, u32[]{:S(2)}) collective-permute-start(bf16[512,128]{1,0:T(8,128)(2,1)S(1)} %pad_maximum_fusion.5), channel_id=1, source_target_pairs={{0,12},{1,9},{2,14},{3,11},{4,8},{5,13},{6,10},{7,15},{8,4},{9,1},... | collective-permute-start | bytes 393224 | tf_op jit(solution)/shard_map/ppermute | solution.py:507
  58.7 8.6 %collective-permute-start.17 = (bf16[512,128]{1,0:T(8,128)(2,1)S(1)}, bf16[512,128]{1,0:T(8,128)(2,1)S(1)}, u32[]{:S(2)}, u32[]{:S(2)}) collective-permute-start(bf16[512,128]{1,0:T(8,128)(2,1)S(1)} %pad_maximum_fusion.6), channel_id=1, source_target_pairs={{0,6},{1,5},{2,4},{3,7},{4,2},{5,1},{6,0},{7,3},{8,14},{9,13},{10,... | collective-permute-start | bytes 393224 | tf_op jit(solution)/shard_map/ppermute | solution.py:507
  58.9 8.4 %collective-permute-start.18 = (bf16[512,128]{1,0:T(8,128)(2,1)S(1)}, bf16[512,128]{1,0:T(8,128)(2,1)S(1)}, u32[]{:S(2)}, u32[]{:S(2)}) collective-permute-start(bf16[512,128]{1,0:T(8,128)(2,1)S(1)} %pad_maximum_fusion.7), channel_id=1, source_target_pairs={{0,2},{1,1},{2,0},{3,3},{4,6},{5,5},{6,4},{7,7},{8,10},{9,9},{10,8... | collective-permute-start | bytes 393224 | tf_op jit(solution)/shard_map/ppermute | solution.py:507
  68.5 2.9 %collective-permute-start.19 = (bf16[4,256,128]{2,1,0:T(8,128)(2,1)S(1)}, bf16[4,256,128]{2,1,0:T(8,128)(2,1)S(1)}, u32[]{:S(2)}, u32[]{:S(2)}) collective-permute-start(bf16[4,256,128]{2,1,0:T(8,128)(2,1)S(1)} %get-tuple-element.84), channel_id=1, source_target_pairs={{0,1},{1,0},{2,3},{3,2},{4,5},{5,4},{6,7},{7,6},{8,9},{9,8},{10,11... | collective-permute-start | bytes 786440 | tf_op jit(solution)/shard_map/ppermute | solution.py:524
  71.5 7.4 %collective-permute-start.20 = (bf16[256,128]{1,0:T(8,128)(2,1)S(1)}, bf16[256,128]{1,0:T(8,128)(2,1)S(1)}, u32[]{:S(2)}, u32[]{:S(2)}) collective-permute-start(bf16[256,128]{1,0:T(8,128)(2,1)S(1)} %get-tuple-element.85), channel_id=1, source_target_pairs={{0,14},{1,7},{2,12},{3,5},{4,10},{5,3},{6,8},{7,1},{8,6},{9,15},{1... | collective-permute-start | bytes 196616 | tf_op jit(solution)/shard_map/ppermute | solution.py:507
  75.4 5.0 %collective-permute-start.21 = (bf16[256,128]{1,0:T(8,128)(2,1)S(1)}, bf16[256,128]{1,0:T(8,128)(2,1)S(1)}, u32[]{:S(2)}, u32[]{:S(2)}) collective-permute-start(bf16[256,128]{1,0:T(8,128)(2,1)S(1)} %get-tuple-element.86), channel_id=1, source_target_pairs={{0,4},{1,13},{2,6},{3,15},{4,0},{5,9},{6,2},{7,11},{8,12},{9,5},{1... | collective-permute-start | bytes 196616 | tf_op jit(solution)/shard_map/ppermute | solution.py:507
  76.0 6.1 %collective-permute-start.22 = (bf16[256,128]{1,0:T(8,128)(2,1)S(1)}, bf16[256,128]{1,0:T(8,128)(2,1)S(1)}, u32[]{:S(2)}, u32[]{:S(2)}) collective-permute-start(bf16[256,128]{1,0:T(8,128)(2,1)S(1)} %get-tuple-element.87), channel_id=1, source_target_pairs={{0,10},{1,3},{2,8},{3,1},{4,14},{5,7},{6,12},{7,5},{8,2},{9,11},{1... | collective-permute-start | bytes 196616 | tf_op jit(solution)/shard_map/ppermute | solution.py:507
  76.8 5.2 %collective-permute-start.23 = (bf16[256,128]{1,0:T(8,128)(2,1)S(1)}, bf16[256,128]{1,0:T(8,128)(2,1)S(1)}, u32[]{:S(2)}, u32[]{:S(2)}) collective-permute-start(bf16[256,128]{1,0:T(8,128)(2,1)S(1)} %get-tuple-element.88), channel_id=1, source_target_pairs={{0,0},{1,9},{2,2},{3,11},{4,4},{5,13},{6,6},{7,15},{8,8},{9,1},{10... | collective-permute-start | bytes 196616 | tf_op jit(solution)/shard_map/ppermute | solution.py:507
  82.1 2.6 %collective-permute-start.24 = (bf16[512,128]{1,0:T(8,128)(2,1)S(1)}, bf16[512,128]{1,0:T(8,128)(2,1)S(1)}, u32[]{:S(2)}, u32[]{:S(2)}) collective-permute-start(bf16[512,128]{1,0:T(8,128)(2,1)S(1)} %shard_map.107), channel_id=1, source_target_pairs={{0,1},{1,0},{2,3},{3,2},{4,5},{5,4},{6,7},{7,6},{8,9},{9,8},{10,11... | collective-permute-start | bytes 393224 | tf_op jit(solution)/shard_map/ppermute | solution.py:524

commit v15 on v14

--- a/solution.py
+++ b/solution.py
@@ -225,8 +225,8 @@
 
 
 VMEM_LIMIT = 20 * 1024 * 1024
-SPLIT = ((7, 5), (6, 4), (3, 2), (1, 0))
-FAR_SPLIT = SPLIT[:2]
+SPLIT = ((3, 2), (7, 5), (6, 4), (1, 0))
+FAR_SPLIT = SPLIT[1:3]
 SMALL_SPLIT = ((7, 3), (2, 6), (5, 1), (0, 4))
 OPS = len(SPLIT)
 NEAR = 4

time: 87.1 us -> 88.5 us (1.016)
  starting transfers between devices: 38.2 us -> 40.1 us
    ppermute x10, starting transfers between devices: 17.5 us -> 18.8 us  [split_permute(): lax.ppermute(block, 'wide', [(w, w ^ 2 * steps[w % 2]) for w in range(cou...]
  transfers between devices with their start and end apart: 25 -> 25, of which waited for: 19 -> 18; matrix products, arithmetic and copies ran while one was open for 0% -> 0% of each run, Pallas kernels for 2% -> 2%
where the time goes in v15:
time: 88.5 us; the launch traced here: 88.3 us
  starting transfers between devices  40.1 us (45%)
  waiting for transfers between devices  33.2 us (38%)
  Pallas kernels  12 us (14%)
  local copies, waits for them, and re-layouts  1.42 us (2%)
  other arithmetic  1.41 us (2%)
    ppermute x10, starting transfers between devices, split_permute(): lax.ppermute(block, 'wide', [(w, w ^ 2 * steps[w % 2]) for w in range(cou...  18.8 us
    ppermute x10, waiting for transfers between devices, split_permute(): lax.ppermute(block, 'wide', [(w, w ^ 2 * steps[w % 2]) for w in range(cou...  16.3 us
    ppermute x9, starting transfers between devices, chip_permute(): lax.ppermute(block, 'wide', [(w, w ^ 2 * step) for w in range(count)])  15 us
    pallas_call x9, Pallas kernels, run(): pl.pallas_call(kernel, out_shape=[jax.ShapeDtypeStruct(shape, kind) for s...  12 us
    ppermute x9, waiting for transfers between devices, chip_permute(): lax.ppermute(block, 'wide', [(w, w ^ 2 * step) for w in range(count)])  10 us
    ppermute x6, waiting for transfers between devices, core_permute(): return lax.ppermute(block, 'wide', [(w, w ^ 1) for w in range(count)])  6.78 us
    ppermute x6, starting transfers between devices, core_permute(): return lax.ppermute(block, 'wide', [(w, w ^ 1) for w in range(count)])  6.31 us
  transfers between devices with their start and end apart: 25, of which 18 were waited for; matrix products, arithmetic and copies ran while one was open for 0% of the time, Pallas kernels for 2%

profile of v15, /device:TPU:0, one launch (start us, length us, event | category | flops | bytes accessed | tf_op | source)
XLA Modules:
  0.0 88.3 jit_solution(17098372905528989150)
XLA Ops:
  0.0 0.7 copy-done.7
  0.7 0.1 dynamic-slice_convert_fusion
  0.7 0.1 multiply_bitcast_fusion
  0.8 0.1 pad_maximum_fusion.9.live_in_ref
  0.9 1.0 %convert_element_type.10.feat_ref = f32[64,8,256]{2,1,0:T(8,128)S(1)} convert(bf16[64,8,256]{2,1,0:T(8,128)(2,1)} %param.11) | non-fusion elementwise | flops 131072 | bytes 786432 | tf_op jit(solution)/shard_map/convert_element_type | solution.py:553
  1.9 0.0 copy-start.1
  1.9 0.0 copy-start.2
  1.9 1.0 %shard_map.100 = (bf16[144,128]{1,0:T(8,128)(2,1)S(1)}, bf16[512,128]{1,0:T(8,128)(2,1)S(1)}, f32[8,128]{1,0:T(8,128)S(1)}) custom-call(f32[64,8,256]{2,1,0:T(8,128)S(1)} %convert_element_type.10.feat_ref, bf16[64,256]{1,0:T(8,128)(2,1)S(1)} %bitcast.13, f32[8,128]{1,0:T(8,128)S(1)} %pad_maximum_fusion.9.live_in_ref), custom_call_target="tpu_custom_call" | custom-call | flops 1500000000 | bytes 561152 | tf_op jit(solution)/shard_map/pallas_call | solution.py:216
  2.9 0.0 copy-start
  2.9 4.1 %collective-permute-start = (bf16[144,128]{1,0:T(8,128)(2,1)S(1)}, bf16[144,128]{1,0:T(8,128)(2,1)S(1)}, u32[]{:S(2)}, u32[]{:S(2)}) collective-permute-start(bf16[144,128]{1,0:T(8,128)(2,1)S(1)} %get-tuple-element.48), channel_id=1, source_target_pairs={{0,8},{1,9},{2,10},{3,11},{4,12},{5,13},{6,14},{7,15},{8,0},{9,1},... | collective-permute-start | bytes 110600 | tf_op jit(solution)/shard_map/ppermute | solution.py:498
  7.0 2.3 %collective-permute-done = bf16[144,128]{1,0:T(8,128)(2,1)S(1)} collective-permute-done((bf16[144,128]{1,0:T(8,128)(2,1)S(1)}, bf16[144,128]{1,0:T(8,128)(2,1)S(1)}, u32[]{:S(2)}, u32[]{:S(2)}) %collective-permute-start) | collective-permute-done | bytes 36896 | tf_op jit(solution)/shard_map/ppermute | solution.py:498
  9.3 1.6 %collective-permute-start.1 = (bf16[2,144,128]{2,1,0:T(8,128)(2,1)S(1)}, bf16[2,144,128]{2,1,0:T(8,128)(2,1)S(1)}, u32[]{:S(2)}, u32[]{:S(2)}) collective-permute-start(bf16[2,144,128]{2,1,0:T(8,128)(2,1)S(1)} %pad_maximum_fusion.8), channel_id=1, source_target_pairs={{0,4},{1,5},{2,6},{3,7},{4,0},{5,1},{6,2},{7,3},{8,12},{9,13},{10,... | collective-permute-start | bytes 221192 | tf_op jit(solution)/shard_map/ppermute | solution.py:498
  10.9 2.8 %collective-permute-done.1 = bf16[2,144,128]{2,1,0:T(8,128)(2,1)S(1)} collective-permute-done((bf16[2,144,128]{2,1,0:T(8,128)(2,1)S(1)}, bf16[2,144,128]{2,1,0:T(8,128)(2,1)S(1)}, u32[]{:S(2)}, u32[]{:S(2)}) %collective-permute-start.1) | collective-permute-done | bytes 73760 | tf_op jit(solution)/shard_map/ppermute | solution.py:498
  13.8 1.8 %collective-permute-start.2 = (bf16[4,144,128]{2,1,0:T(8,128)(2,1)S(1)}, bf16[4,144,128]{2,1,0:T(8,128)(2,1)S(1)}, u32[]{:S(2)}, u32[]{:S(2)}) collective-permute-start(bf16[4,144,128]{2,1,0:T(8,128)(2,1)S(1)} %pad_maximum_fusion.1), channel_id=1, source_target_pairs={{0,2},{1,3},{2,0},{3,1},{4,6},{5,7},{6,4},{7,5},{8,10},{9,11},{10,... | collective-permute-start | bytes 442376 | tf_op jit(solution)/shard_map/ppermute | solution.py:498
  15.5 0.1 pad_add_fusion.where_ref
  15.7 0.6 copy-done.6
  16.3 1.7 %shard_map.101 = (f32[8,128,128]{2,1,0:T(8,128)S(1)}, bf16[128,1024]{1,0:T(8,128)(2,1)S(1)}, bf16[2,640,128]{2,1,0:T(8,128)(2,1)S(1)}, bf16[2,128,128]{2,1,0:T(8,128)(2,1)S(1)}) custom-call(s32[3]{0:T(128)S(1)} %pad_add_fusion.where_ref, s32[128]{0:T(128)S(1)} %copy-done.6, s32[1,128]{1,0:T(1,128)S(1)} %bitcast.14, bf16[8,128,128]{2,1,0:T(8,128)(2,1)S(1)} %copy-done.1, ...), custom_call_target="tpu_custom_call" | custom-call | flops 1500000000 | bytes 935436 | tf_op jit(solution)/shard_map/pallas_call | solution.py:216
  18.0 1.0 %collective-permute-done.2 = bf16[4,144,128]{2,1,0:T(8,128)(2,1)S(1)} collective-permute-done((bf16[4,144,128]{2,1,0:T(8,128)(2,1)S(1)}, bf16[4,144,128]{2,1,0:T(8,128)(2,1)S(1)}, u32[]{:S(2)}, u32[]{:S(2)}) %collective-permute-start.2) | collective-permute-done | bytes 147488 | tf_op jit(solution)/shard_map/ppermute | solution.py:498
  19.0 0.1 collective-permute-start.3
  19.1 1.6 %collective-permute-done.3.other_ref = bf16[8,144,128]{2,1,0:T(8,128)(2,1)S(1)} collective-permute-done((bf16[8,144,128]{2,1,0:T(8,128)(2,1)S(1)}, bf16[8,144,128]{2,1,0:T(8,128)(2,1)S(1)}, u32[]{:S(2)}, u32[]{:S(2)}) %collective-permute-start.3) | collective-permute-done | bytes 294944 | tf_op jit(solution)/shard_map/ppermute | solution.py:524
  20.7 2.7 %shard_map.102 = (f32[8,128,128]{2,1,0:T(8,128)S(1)}, f32[8,128,128]{2,1,0:T(8,128)S(1)}, bf16[256,128]{1,0:T(8,128)(2,1)S(1)}, bf16[256,128]{1,0:T(8,128)(2,1)S...) custom-call(s32[3]{0:T(128)S(1)} %pad_add_fusion.where_ref, ...), custom_call_target="tpu_custom_call" | custom-call | flops 4000000000 | bytes 1840140 | tf_op jit(solution)/shard_map/pallas_call | solution.py:216
  23.4 0.2 collective-permute-start.5
  23.6 2.5 %collective-permute-start.4 = (bf16[512,128]{1,0:T(8,128)(2,1)S(1)}, bf16[512,128]{1,0:T(8,128)(2,1)S(1)}, u32[]{:S(2)}, u32[]{:S(2)}) collective-permute-start(bf16[512,128]{1,0:T(8,128)(2,1)S(1)} %get-tuple-element.59), channel_id=1, source_target_pairs={{0,6},{1,7},{2,4},{3,5},{4,2},{5,3},{6,0},{7,1},{8,14},{9,15},{10,... | collective-permute-start | bytes 393224 | tf_op jit(solution)/shard_map/ppermute | solution.py:498
  26.1 3.6 %collective-permute-start.6 = (bf16[512,128]{1,0:T(8,128)(2,1)S(1)}, bf16[512,128]{1,0:T(8,128)(2,1)S(1)}, u32[]{:S(2)}, u32[]{:S(2)}) collective-permute-start(bf16[512,128]{1,0:T(8,128)(2,1)S(1)} %get-tuple-element.66), channel_id=1, source_target_pairs={{0,14},{1,11},{2,12},{3,9},{4,10},{5,15},{6,8},{7,13},{8,6},{9,3},... | collective-permute-start | bytes 393224 | tf_op jit(solution)/shard_map/ppermute | solution.py:507
  29.7 0.3 collective-permute-start.7
  30.0 0.0 collective-permute-start.8
  30.0 1.5 %collective-permute-start.9 = (bf16[512,128]{1,0:T(8,128)(2,1)S(1)}, bf16[512,128]{1,0:T(8,128)(2,1)S(1)}, u32[]{:S(2)}, u32[]{:S(2)}) collective-permute-start(bf16[512,128]{1,0:T(8,128)(2,1)S(1)} %get-tuple-element.69), channel_id=1, source_target_pairs={{0,2},{1,3},{2,0},{3,1},{4,6},{5,7},{6,4},{7,5},{8,10},{9,11},{10,... | collective-permute-start | bytes 393224 | tf_op jit(solution)/shard_map/ppermute | solution.py:498
  31.5 4.3 %collective-permute-done.6.far0 = bf16[512,128]{1,0:T(8,128)(2,1)S(1)} collective-permute-done((bf16[512,128]{1,0:T(8,128)(2,1)S(1)}, bf16[512,128]{1,0:T(8,128)(2,1)S(1)}, u32[]{:S(2)}, u32[]{:S(2)}) %collective-permute-start.6) | collective-permute-done | bytes 131104 | tf_op jit(solution)/shard_map/ppermute | solution.py:507
  35.8 2.8 %collective-permute-done.7.far1 = bf16[512,128]{1,0:T(8,128)(2,1)S(1)} collective-permute-done((bf16[512,128]{1,0:T(8,128)(2,1)S(1)}, bf16[512,128]{1,0:T(8,128)(2,1)S(1)}, u32[]{:S(2)}, u32[]{:S(2)}) %collective-permute-start.7) | collective-permute-done | bytes 131104 | tf_op jit(solution)/shard_map/ppermute | solution.py:507
  38.5 0.0 collective-permute-done.8.near2
  38.6 0.0 collective-permute-done.9.near1
  38.6 2.0 %collective-permute-start.10 = (bf16[2048,128]{1,0:T(8,128)(2,1)S(1)}, bf16[2048,128]{1,0:T(8,128)(2,1)S(1)}, u32[]{:S(2)}, u32[]{:S(2)}) collective-permute-start(bf16[2048,128]{1,0:T(8,128)(2,1)S(1)} %slice_dynamic-update-slice_fusion.3), channel_id=1, source_target_pairs={{0,1},{1,0},{2,3},{3,2},{4,5},{5,4},{6,7},{7,6},{8,9},{9,8},{10,11... | collective-permute-start | bytes 1572872 | tf_op jit(solution)/shard_map/ppermute | solution.py:524
  40.6 1.5 %collective-permute-done.10.other_ref = bf16[2048,128]{1,0:T(8,128)(2,1)S(1)} collective-permute-done((bf16[2048,128]{1,0:T(8,128)(2,1)S(1)}, bf16[2048,128]{1,0:T(8,128)(2,1)S(1)}, u32[]{:S(2)}, u32[]{:S(2)}) %collective-permute-start.10) | collective-permute-done | bytes 524320 | tf_op jit(solution)/shard_map/ppermute | solution.py:524
  42.2 1.4 %shard_map.103 = (bf16[256,128]{1,0:T(8,128)(2,1)S(1)}, bf16[256,128]{1,0:T(8,128)(2,1)S(1)}, bf16[256,128]{1,0:T(8,128)(2,1)S(1)}, bf16[256,128]{1,0:T(8,128)(2,1)S(1)}) custom-call(s32[3]{0:T(128)S(1)} %pad_add_fusion.where_ref, bf16[512,128]{1,0:T(8,128)(2,1)S(1)} %collective-permute-done.4.near3, bf16[512,128]{1,0:T(8,128)(2,1)S(1)} %collective-permute-done.6.far0, ...), custom_call_target="tpu_custom_call" | custom-call | flops 1500000000 | bytes 1310732 | tf_op jit(solution)/shard_map/pallas_call | solution.py:216
  43.6 2.4 %collective-permute-start.11 = (bf16[256,128]{1,0:T(8,128)(2,1)S(1)}, bf16[256,128]{1,0:T(8,128)(2,1)S(1)}, u32[]{:S(2)}, u32[]{:S(2)}) collective-permute-start(bf16[256,128]{1,0:T(8,128)(2,1)S(1)} %get-tuple-element.71), channel_id=1, source_target_pairs={{0,6},{1,7},{2,4},{3,5},{4,2},{5,3},{6,0},{7,1},{8,14},{9,15},{10,... | collective-permute-start | bytes 196616 | tf_op jit(solution)/shard_map/ppermute | solution.py:498
  46.0 0.8 collective-permute-start.12
  46.8 0.4 collective-permute-start.13
  47.2 2.0 %collective-permute-done.11.in0 = bf16[256,128]{1,0:T(8,128)(2,1)S(1)} collective-permute-done((bf16[256,128]{1,0:T(8,128)(2,1)S(1)}, bf16[256,128]{1,0:T(8,128)(2,1)S(1)}, u32[]{:S(2)}, u32[]{:S(2)}) %collective-permute-start.11) | collective-permute-done | bytes 65568 | tf_op jit(solution)/shard_map/ppermute | solution.py:498
  49.2 1.4 %collective-permute-done.12.in1 = bf16[256,128]{1,0:T(8,128)(2,1)S(1)} collective-permute-done((bf16[256,128]{1,0:T(8,128)(2,1)S(1)}, bf16[256,128]{1,0:T(8,128)(2,1)S(1)}, u32[]{:S(2)}, u32[]{:S(2)}) %collective-permute-start.12) | collective-permute-done | bytes 65568 | tf_op jit(solution)/shard_map/ppermute | solution.py:498
  50.5 0.5 collective-permute-done.13.in2
  51.1 1.7 %shard_map.104 = (f32[8,128,128]{2,1,0:T(8,128)S(1)}, f32[8,128,128]{2,1,0:T(8,128)S(1)}, bf16[256,128]{1,0:T(8,128)(2,1)S(1)}, bf16[256,128]{1,0:T(8,128)(2,1)S...) custom-call(s32[3]{0:T(128)S(1)} %pad_add_fusion.where_ref, ...), custom_call_target="tpu_custom_call" | custom-call | flops 1500000000 | bytes 1704972 | tf_op jit(solution)/shard_map/pallas_call | solution.py:216
  52.8 0.1 collective-permute-start.14
  52.8 1.5 %collective-permute-done.14 = bf16[1024,128]{1,0:T(8,128)(2,1)S(1)} collective-permute-done((bf16[1024,128]{1,0:T(8,128)(2,1)S(1)}, bf16[1024,128]{1,0:T(8,128)(2,1)S(1)}, u32[]{:S(2)}, u32[]{:S(2)}) %collective-permute-start.14) | collective-permute-done | bytes 262176 | tf_op jit(solution)/shard_map/ppermute | solution.py:524
  54.4 1.6 %collective-permute-start.15 = (bf16[512,128]{1,0:T(8,128)(2,1)S(1)}, bf16[512,128]{1,0:T(8,128)(2,1)S(1)}, u32[]{:S(2)}, u32[]{:S(2)}) collective-permute-start(bf16[512,128]{1,0:T(8,128)(2,1)S(1)} %pad_maximum_fusion.4), channel_id=1, source_target_pairs={{0,6},{1,5},{2,4},{3,7},{4,2},{5,1},{6,0},{7,3},{8,14},{9,13},{10,... | collective-permute-start | bytes 393224 | tf_op jit(solution)/shard_map/ppermute | solution.py:507
  56.1 3.6 %collective-permute-start.16 = (bf16[512,128]{1,0:T(8,128)(2,1)S(1)}, bf16[512,128]{1,0:T(8,128)(2,1)S(1)}, u32[]{:S(2)}, u32[]{:S(2)}) collective-permute-start(bf16[512,128]{1,0:T(8,128)(2,1)S(1)} %pad_maximum_fusion.5), channel_id=1, source_target_pairs={{0,14},{1,11},{2,12},{3,9},{4,10},{5,15},{6,8},{7,13},{8,6},{9,3},... | collective-permute-start | bytes 393224 | tf_op jit(solution)/shard_map/ppermute | solution.py:507
  59.7 0.9 %collective-permute-start.17 = (bf16[512,128]{1,0:T(8,128)(2,1)S(1)}, bf16[512,128]{1,0:T(8,128)(2,1)S(1)}, u32[]{:S(2)}, u32[]{:S(2)}) collective-permute-start(bf16[512,128]{1,0:T(8,128)(2,1)S(1)} %pad_maximum_fusion.6), channel_id=1, source_target_pairs={{0,12},{1,9},{2,14},{3,11},{4,8},{5,13},{6,10},{7,15},{8,4},{9,1},... | collective-permute-start | bytes 393224 | tf_op jit(solution)/shard_map/ppermute | solution.py:507
  60.6 2.8 %collective-permute-start.18 = (bf16[512,128]{1,0:T(8,128)(2,1)S(1)}, bf16[512,128]{1,0:T(8,128)(2,1)S(1)}, u32[]{:S(2)}, u32[]{:S(2)}) collective-permute-start(bf16[512,128]{1,0:T(8,128)(2,1)S(1)} %pad_maximum_fusion.7), channel_id=1, source_target_pairs={{0,2},{1,1},{2,0},{3,3},{4,6},{5,5},{6,4},{7,7},{8,10},{9,9},{10,8... | collective-permute-start | bytes 393224 | tf_op jit(solution)/shard_map/ppermute | solution.py:507
  63.4 3.4 %collective-permute-done.16.came1 = bf16[512,128]{1,0:T(8,128)(2,1)S(1)} collective-permute-done((bf16[512,128]{1,0:T(8,128)(2,1)S(1)}, bf16[512,128]{1,0:T(8,128)(2,1)S(1)}, u32[]{:S(2)}, u32[]{:S(2)}) %collective-permute-start.16) | collective-permute-done | bytes 131104 | tf_op jit(solution)/shard_map/ppermute | solution.py:507
  66.8 1.0 %collective-permute-done.17.came2 = bf16[512,128]{1,0:T(8,128)(2,1)S(1)} collective-permute-done((bf16[512,128]{1,0:T(8,128)(2,1)S(1)}, bf16[512,128]{1,0:T(8,128)(2,1)S(1)}, u32[]{:S(2)}, u32[]{:S(2)}) %collective-permute-start.17) | collective-permute-done | bytes 131104 | tf_op jit(solution)/shard_map/ppermute | solution.py:507
  67.8 0.0 collective-permute-done.18.came3
  67.9 1.2 %shard_map.105 = (f32[4,256,128]{2,1,0:T(8,128)S(1)}, bf16[4,256,128]{2,1,0:T(8,128)(2,1)S(1)}) custom-call(s32[3]{0:T(128)S(1)} %pad_add_fusion.where_ref, bf16[512,128]{1,0:T(8,128)(2,1)S(1)} %collective-permute-done.15.came0, bf16[512,128]{1,0:T(8,128)(2,1)S(1)} %collective-permute-done.16.came1, bf16[512,128]{1,0:T(8,128)(2,1)S(1)} %collective-permute-done.17.came2, ...), custom_call_target="tpu_custom_call" | custom-call | flops 1500000000 | bytes 524300 | tf_op jit(solution)/shard_map/pallas_call | solution.py:216
  69.0 1.8 %collective-permute-start.19 = (bf16[4,256,128]{2,1,0:T(8,128)(2,1)S(1)}, bf16[4,256,128]{2,1,0:T(8,128)(2,1)S(1)}, u32[]{:S(2)}, u32[]{:S(2)}) collective-permute-start(bf16[4,256,128]{2,1,0:T(8,128)(2,1)S(1)} %get-tuple-element.84), channel_id=1, source_target_pairs={{0,1},{1,0},{2,3},{3,2},{4,5},{5,4},{6,7},{7,6},{8,9},{9,8},{10,11... | collective-permute-start | bytes 786440 | tf_op jit(solution)/shard_map/ppermute | solution.py:524
  70.9 1.2 %collective-permute-done.19.got_ref = bf16[4,256,128]{2,1,0:T(8,128)(2,1)S(1)} collective-permute-done((bf16[4,256,128]{2,1,0:T(8,128)(2,1)S(1)}, bf16[4,256,128]{2,1,0:T(8,128)(2,1)S(1)}, u32[]{:S(2)}, u32[]{:S(2)}) %collective-permute-start.19) | collective-permute-done | bytes 262176 | tf_op jit(solution)/shard_map/ppermute | solution.py:524
  72.0 0.1 shard_map.106
  72.1 4.1 %collective-permute-start.20 = (bf16[256,128]{1,0:T(8,128)(2,1)S(1)}, bf16[256,128]{1,0:T(8,128)(2,1)S(1)}, u32[]{:S(2)}, u32[]{:S(2)}) collective-permute-start(bf16[256,128]{1,0:T(8,128)(2,1)S(1)} %get-tuple-element.85), channel_id=1, source_target_pairs={{0,14},{1,7},{2,12},{3,5},{4,10},{5,3},{6,8},{7,1},{8,6},{9,15},{1... | collective-permute-start | bytes 196616 | tf_op jit(solution)/shard_map/ppermute | solution.py:507
  76.2 0.8 collective-permute-start.21
  76.9 0.5 collective-permute-start.22
  77.4 0.7 collective-permute-start.23
  78.1 1.1 %collective-permute-done.20.refs_0_.came0 = bf16[256,128]{1,0:T(8,128)(2,1)S(1)} collective-permute-done((bf16[256,128]{1,0:T(8,128)(2,1)S(1)}, bf16[256,128]{1,0:T(8,128)(2,1)S(1)}, u32[]{:S(2)}, u32[]{:S(2)}) %collective-permute-start.20) | collective-permute-done | bytes 65568 | tf_op jit(solution)/shard_map/ppermute | solution.py:507
  79.2 1.7 %collective-permute-done.21.refs_1_.came1 = bf16[256,128]{1,0:T(8,128)(2,1)S(1)} collective-permute-done((bf16[256,128]{1,0:T(8,128)(2,1)S(1)}, bf16[256,128]{1,0:T(8,128)(2,1)S(1)}, u32[]{:S(2)}, u32[]{:S(2)}) %collective-permute-start.21) | collective-permute-done | bytes 65568 | tf_op jit(solution)/shard_map/ppermute | solution.py:507
  80.9 2.1 %collective-permute-done.22.refs_2_.came2 = bf16[256,128]{1,0:T(8,128)(2,1)S(1)} collective-permute-done((bf16[256,128]{1,0:T(8,128)(2,1)S(1)}, bf16[256,128]{1,0:T(8,128)(2,1)S(1)}, u32[]{:S(2)}, u32[]{:S(2)}) %collective-permute-start.22) | collective-permute-done | bytes 65568 | tf_op jit(solution)/shard_map/ppermute | solution.py:507
  83.0 2.1 %collective-permute-start.24 = (bf16[512,128]{1,0:T(8,128)(2,1)S(1)}, bf16[512,128]{1,0:T(8,128)(2,1)S(1)}, u32[]{:S(2)}, u32[]{:S(2)}) collective-permute-start(bf16[512,128]{1,0:T(8,128)(2,1)S(1)} %shard_map.107), channel_id=1, source_target_pairs={{0,1},{1,0},{2,3},{3,2},{4,5},{5,4},{6,7},{7,6},{8,9},{9,8},{10,11... | collective-permute-start | bytes 393224 | tf_op jit(solution)/shard_map/ppermute | solution.py:524
  85.1 1.0 %collective-permute-done.24.other_ref = bf16[512,128]{1,0:T(8,128)(2,1)S(1)} collective-permute-done((bf16[512,128]{1,0:T(8,128)(2,1)S(1)}, bf16[512,128]{1,0:T(8,128)(2,1)S(1)}, u32[]{:S(2)}, u32[]{:S(2)}) %collective-permute-start.24) | collective-permute-done | bytes 131104 | tf_op jit(solution)/shard_map/ppermute | solution.py:524
  86.1 2.2 %shard_map.108 = bf16[8,128,128]{2,1,0:T(8,128)(2,1)} custom-call(s32[3]{0:T(128)S(1)} %pad_add_fusion.where_ref, bf16[256,128]{1,0:T(8,128)(2,1)S(1)} %collective-permute-done.20.refs_0_.came0, bf16[256,128]{1,0:T(8,128)(2,1)S(1)} %collective-permute-done.21.refs_1_.came1, bf16[256,128]{1,0:T(8,128)(2,1)S(1)} %collective-permute-done.22.refs_2_.came2, ...), custom_call_target="tpu_custom_call" | custom-call | flops 1500000000 | bytes 1507340 | tf_op jit(solution)/shard_map/pallas_call | solution.py:216
  (34 shorter events, 0.3 us)
Async XLA Ops:
  0.0 0.7 copy-start.7
  0.0 0.7 copy-start.8
  0.9 1.0 %copy-start.4 = (bf16[256,64]{0,1:T(8,128)(2,1)S(1)}, bf16[256,64]{0,1:T(8,128)(2,1)}, u32[]{:S(2)}) copy-start(bf16[256,64]{0,1:T(8,128)(2,1)} %param.16) | copy-start | bytes 98308
  1.9 13.7 %copy-start.1 = (bf16[8,128,128]{2,1,0:T(8,128)(2,1)S(1)}, bf16[8,128,128]{2,1,0:T(8,128)(2,1)}, u32[]{:S(2)}) copy-start(bf16[8,128,128]{2,1,0:T(8,128)(2,1)} %pair_ref.1) | copy-start | bytes 786436
  1.9 13.7 %copy-start.2 = (bf16[1024,128]{1,0:T(8,128)(2,1)S(1)}, bf16[1024,128]{1,0:T(8,128)(2,1)}, u32[]{:S(2)}) copy-start(bf16[1024,128]{1,0:T(8,128)(2,1)} %outer_ref.1) | copy-start | bytes 786436
  2.9 12.8 %copy-start = (bf16[2,128,640]{2,1,0:T(8,128)(2,1)S(1)}, bf16[2,128,640]{2,1,0:T(8,128)(2,1)}, u32[]{:S(2)}) copy-start(bf16[2,128,640]{2,1,0:T(8,128)(2,1)} %proj_ref.1) | copy-start | bytes 983044
  2.9 6.4 %collective-permute-start = (bf16[144,128]{1,0:T(8,128)(2,1)S(1)}, bf16[144,128]{1,0:T(8,128)(2,1)S(1)}, u32[]{:S(2)}, u32[]{:S(2)}) collective-permute-start(bf16[144,128]{1,0:T(8,128)(2,1)S(1)} %get-tuple-element.48), channel_id=1, source_target_pairs={{0,8},{1,9},{2,10},{3,11},{4,12},{5,13},{6,14},{7,15},{8,0},{9,1},... | collective-permute-start | bytes 110600 | tf_op jit(solution)/shard_map/ppermute | solution.py:498
  9.3 4.4 %collective-permute-start.1 = (bf16[2,144,128]{2,1,0:T(8,128)(2,1)S(1)}, bf16[2,144,128]{2,1,0:T(8,128)(2,1)S(1)}, u32[]{:S(2)}, u32[]{:S(2)}) collective-permute-start(bf16[2,144,128]{2,1,0:T(8,128)(2,1)S(1)} %pad_maximum_fusion.8), channel_id=1, source_target_pairs={{0,4},{1,5},{2,6},{3,7},{4,0},{5,1},{6,2},{7,3},{8,12},{9,13},{10,... | collective-permute-start | bytes 221192 | tf_op jit(solution)/shard_map/ppermute | solution.py:498
  10.9 4.7 %copy-start.3 = (bf16[2,128,128]{2,1,0:T(8,128)(2,1)S(1)}, bf16[2,128,128]{2,1,0:T(8,128)(2,1)}, u32[]{:S(2)}) copy-start(bf16[2,128,128]{2,1,0:T(8,128)(2,1)} %out_ref.1) | copy-start | bytes 196612
  10.9 4.7 %copy-start.5 = (bf16[66,128]{1,0:T(8,128)(2,1)S(1)}, bf16[66,128]{1,0:T(8,128)(2,1)}, u32[]{:S(2)}) copy-start(bf16[66,128]{1,0:T(8,128)(2,1)} %table_ref.1) | copy-start | bytes 50692
  13.8 5.2 %collective-permute-start.2 = (bf16[4,144,128]{2,1,0:T(8,128)(2,1)S(1)}, bf16[4,144,128]{2,1,0:T(8,128)(2,1)S(1)}, u32[]{:S(2)}, u32[]{:S(2)}) collective-permute-start(bf16[4,144,128]{2,1,0:T(8,128)(2,1)S(1)} %pad_maximum_fusion.1), channel_id=1, source_target_pairs={{0,2},{1,3},{2,0},{3,1},{4,6},{5,7},{6,4},{7,5},{8,10},{9,11},{10,... | collective-permute-start | bytes 442376 | tf_op jit(solution)/shard_map/ppermute | solution.py:498
  15.6 0.7 copy-start.6
  19.0 1.6 %collective-permute-start.3 = (bf16[8,144,128]{2,1,0:T(8,128)(2,1)S(1)}, bf16[8,144,128]{2,1,0:T(8,128)(2,1)S(1)}, u32[]{:S(2)}, u32[]{:S(2)}) collective-permute-start(bf16[8,144,128]{2,1,0:T(8,128)(2,1)S(1)} %pad_maximum_fusion.own_ref), channel_id=1, source_target_pairs={{0,1},{1,0},{2,3},{3,2},{4,5},{5,4},{6,7},{7,6},{8,9},{9,8},{10,11... | collective-permute-start | bytes 884744 | tf_op jit(solution)/shard_map/ppermute | solution.py:524
  23.4 2.7 %collective-permute-start.5 = (bf16[512,128]{1,0:T(8,128)(2,1)S(1)}, bf16[512,128]{1,0:T(8,128)(2,1)S(1)}, u32[]{:S(2)}, u32[]{:S(2)}) collective-permute-start(bf16[512,128]{1,0:T(8,128)(2,1)S(1)} %get-tuple-element.61), channel_id=1, source_target_pairs={{0,1},{1,0},{2,3},{3,2},{4,5},{5,4},{6,7},{7,6},{8,9},{9,8},{10,11... | collective-permute-start | bytes 393224 | tf_op jit(solution)/shard_map/ppermute | solution.py:524
  23.6 7.9 %collective-permute-start.4 = (bf16[512,128]{1,0:T(8,128)(2,1)S(1)}, bf16[512,128]{1,0:T(8,128)(2,1)S(1)}, u32[]{:S(2)}, u32[]{:S(2)}) collective-permute-start(bf16[512,128]{1,0:T(8,128)(2,1)S(1)} %get-tuple-element.59), channel_id=1, source_target_pairs={{0,6},{1,7},{2,4},{3,5},{4,2},{5,3},{6,0},{7,1},{8,14},{9,15},{10,... | collective-permute-start | bytes 393224 | tf_op jit(solution)/shard_map/ppermute | solution.py:498
  26.1 9.6 %collective-permute-start.6 = (bf16[512,128]{1,0:T(8,128)(2,1)S(1)}, bf16[512,128]{1,0:T(8,128)(2,1)S(1)}, u32[]{:S(2)}, u32[]{:S(2)}) collective-permute-start(bf16[512,128]{1,0:T(8,128)(2,1)S(1)} %get-tuple-element.66), channel_id=1, source_target_pairs={{0,14},{1,11},{2,12},{3,9},{4,10},{5,15},{6,8},{7,13},{8,6},{9,3},... | collective-permute-start | bytes 393224 | tf_op jit(solution)/shard_map/ppermute | solution.py:507
  29.7 8.8 %collective-permute-start.7 = (bf16[512,128]{1,0:T(8,128)(2,1)S(1)}, bf16[512,128]{1,0:T(8,128)(2,1)S(1)}, u32[]{:S(2)}, u32[]{:S(2)}) collective-permute-start(bf16[512,128]{1,0:T(8,128)(2,1)S(1)} %get-tuple-element.67), channel_id=1, source_target_pairs={{0,12},{1,9},{2,14},{3,11},{4,8},{5,13},{6,10},{7,15},{8,4},{9,1},... | collective-permute-start | bytes 393224 | tf_op jit(solution)/shard_map/ppermute | solution.py:507
  30.0 8.6 %collective-permute-start.8 = (bf16[512,128]{1,0:T(8,128)(2,1)S(1)}, bf16[512,128]{1,0:T(8,128)(2,1)S(1)}, u32[]{:S(2)}, u32[]{:S(2)}) collective-permute-start(bf16[512,128]{1,0:T(8,128)(2,1)S(1)} %get-tuple-element.68), channel_id=1, source_target_pairs={{0,4},{1,5},{2,6},{3,7},{4,0},{5,1},{6,2},{7,3},{8,12},{9,13},{10,... | collective-permute-start | bytes 393224 | tf_op jit(solution)/shard_map/ppermute | solution.py:498
  30.0 8.6 %collective-permute-start.9 = (bf16[512,128]{1,0:T(8,128)(2,1)S(1)}, bf16[512,128]{1,0:T(8,128)(2,1)S(1)}, u32[]{:S(2)}, u32[]{:S(2)}) collective-permute-start(bf16[512,128]{1,0:T(8,128)(2,1)S(1)} %get-tuple-element.69), channel_id=1, source_target_pairs={{0,2},{1,3},{2,0},{3,1},{4,6},{5,7},{6,4},{7,5},{8,10},{9,11},{10,... | collective-permute-start | bytes 393224 | tf_op jit(solution)/shard_map/ppermute | solution.py:498
  38.6 3.6 %collective-permute-start.10 = (bf16[2048,128]{1,0:T(8,128)(2,1)S(1)}, bf16[2048,128]{1,0:T(8,128)(2,1)S(1)}, u32[]{:S(2)}, u32[]{:S(2)}) collective-permute-start(bf16[2048,128]{1,0:T(8,128)(2,1)S(1)} %slice_dynamic-update-slice_fusion.3), channel_id=1, source_target_pairs={{0,1},{1,0},{2,3},{3,2},{4,5},{5,4},{6,7},{7,6},{8,9},{9,8},{10,11... | collective-permute-start | bytes 1572872 | tf_op jit(solution)/shard_map/ppermute | solution.py:524
  43.6 5.5 %collective-permute-start.11 = (bf16[256,128]{1,0:T(8,128)(2,1)S(1)}, bf16[256,128]{1,0:T(8,128)(2,1)S(1)}, u32[]{:S(2)}, u32[]{:S(2)}) collective-permute-start(bf16[256,128]{1,0:T(8,128)(2,1)S(1)} %get-tuple-element.71), channel_id=1, source_target_pairs={{0,6},{1,7},{2,4},{3,5},{4,2},{5,3},{6,0},{7,1},{8,14},{9,15},{10,... | collective-permute-start | bytes 196616 | tf_op jit(solution)/shard_map/ppermute | solution.py:498
  46.0 4.5 %collective-permute-start.12 = (bf16[256,128]{1,0:T(8,128)(2,1)S(1)}, bf16[256,128]{1,0:T(8,128)(2,1)S(1)}, u32[]{:S(2)}, u32[]{:S(2)}) collective-permute-start(bf16[256,128]{1,0:T(8,128)(2,1)S(1)} %get-tuple-element.72), channel_id=1, source_target_pairs={{0,4},{1,5},{2,6},{3,7},{4,0},{5,1},{6,2},{7,3},{8,12},{9,13},{10,... | collective-permute-start | bytes 196616 | tf_op jit(solution)/shard_map/ppermute | solution.py:498
  46.8 4.3 %collective-permute-start.13 = (bf16[256,128]{1,0:T(8,128)(2,1)S(1)}, bf16[256,128]{1,0:T(8,128)(2,1)S(1)}, u32[]{:S(2)}, u32[]{:S(2)}) collective-permute-start(bf16[256,128]{1,0:T(8,128)(2,1)S(1)} %get-tuple-element.73), channel_id=1, source_target_pairs={{0,2},{1,3},{2,0},{3,1},{4,6},{5,7},{6,4},{7,5},{8,10},{9,11},{10,... | collective-permute-start | bytes 196616 | tf_op jit(solution)/shard_map/ppermute | solution.py:498
  52.8 1.6 %collective-permute-start.14 = (bf16[1024,128]{1,0:T(8,128)(2,1)S(1)}, bf16[1024,128]{1,0:T(8,128)(2,1)S(1)}, u32[]{:S(2)}, u32[]{:S(2)}) collective-permute-start(bf16[1024,128]{1,0:T(8,128)(2,1)S(1)} %get-tuple-element.79), channel_id=1, source_target_pairs={{0,1},{1,0},{2,3},{3,2},{4,5},{5,4},{6,7},{7,6},{8,9},{9,8},{10,11... | collective-permute-start | bytes 786440 | tf_op jit(solution)/shard_map/ppermute | solution.py:524
  54.4 9.0 %collective-permute-start.15 = (bf16[512,128]{1,0:T(8,128)(2,1)S(1)}, bf16[512,128]{1,0:T(8,128)(2,1)S(1)}, u32[]{:S(2)}, u32[]{:S(2)}) collective-permute-start(bf16[512,128]{1,0:T(8,128)(2,1)S(1)} %pad_maximum_fusion.4), channel_id=1, source_target_pairs={{0,6},{1,5},{2,4},{3,7},{4,2},{5,1},{6,0},{7,3},{8,14},{9,13},{10,... | collective-permute-start | bytes 393224 | tf_op jit(solution)/shard_map/ppermute | solution.py:507
  56.1 10.8 %collective-permute-start.16 = (bf16[512,128]{1,0:T(8,128)(2,1)S(1)}, bf16[512,128]{1,0:T(8,128)(2,1)S(1)}, u32[]{:S(2)}, u32[]{:S(2)}) collective-permute-start(bf16[512,128]{1,0:T(8,128)(2,1)S(1)} %pad_maximum_fusion.5), channel_id=1, source_target_pairs={{0,14},{1,11},{2,12},{3,9},{4,10},{5,15},{6,8},{7,13},{8,6},{9,3},... | collective-permute-start | bytes 393224 | tf_op jit(solution)/shard_map/ppermute | solution.py:507
  59.7 8.1 %collective-permute-start.17 = (bf16[512,128]{1,0:T(8,128)(2,1)S(1)}, bf16[512,128]{1,0:T(8,128)(2,1)S(1)}, u32[]{:S(2)}, u32[]{:S(2)}) collective-permute-start(bf16[512,128]{1,0:T(8,128)(2,1)S(1)} %pad_maximum_fusion.6), channel_id=1, source_target_pairs={{0,12},{1,9},{2,14},{3,11},{4,8},{5,13},{6,10},{7,15},{8,4},{9,1},... | collective-permute-start | bytes 393224 | tf_op jit(solution)/shard_map/ppermute | solution.py:507
  60.6 7.2 %collective-permute-start.18 = (bf16[512,128]{1,0:T(8,128)(2,1)S(1)}, bf16[512,128]{1,0:T(8,128)(2,1)S(1)}, u32[]{:S(2)}, u32[]{:S(2)}) collective-permute-start(bf16[512,128]{1,0:T(8,128)(2,1)S(1)} %pad_maximum_fusion.7), channel_id=1, source_target_pairs={{0,2},{1,1},{2,0},{3,3},{4,6},{5,5},{6,4},{7,7},{8,10},{9,9},{10,8... | collective-permute-start | bytes 393224 | tf_op jit(solution)/shard_map/ppermute | solution.py:507
  69.0 3.0 %collective-permute-start.19 = (bf16[4,256,128]{2,1,0:T(8,128)(2,1)S(1)}, bf16[4,256,128]{2,1,0:T(8,128)(2,1)S(1)}, u32[]{:S(2)}, u32[]{:S(2)}) collective-permute-start(bf16[4,256,128]{2,1,0:T(8,128)(2,1)S(1)} %get-tuple-element.84), channel_id=1, source_target_pairs={{0,1},{1,0},{2,3},{3,2},{4,5},{5,4},{6,7},{7,6},{8,9},{9,8},{10,11... | collective-permute-start | bytes 786440 | tf_op jit(solution)/shard_map/ppermute | solution.py:524
  72.1 7.1 %collective-permute-start.20 = (bf16[256,128]{1,0:T(8,128)(2,1)S(1)}, bf16[256,128]{1,0:T(8,128)(2,1)S(1)}, u32[]{:S(2)}, u32[]{:S(2)}) collective-permute-start(bf16[256,128]{1,0:T(8,128)(2,1)S(1)} %get-tuple-element.85), channel_id=1, source_target_pairs={{0,14},{1,7},{2,12},{3,5},{4,10},{5,3},{6,8},{7,1},{8,6},{9,15},{1... | collective-permute-start | bytes 196616 | tf_op jit(solution)/shard_map/ppermute | solution.py:507
  76.2 4.8 %collective-permute-start.21 = (bf16[256,128]{1,0:T(8,128)(2,1)S(1)}, bf16[256,128]{1,0:T(8,128)(2,1)S(1)}, u32[]{:S(2)}, u32[]{:S(2)}) collective-permute-start(bf16[256,128]{1,0:T(8,128)(2,1)S(1)} %get-tuple-element.86), channel_id=1, source_target_pairs={{0,4},{1,13},{2,6},{3,15},{4,0},{5,9},{6,2},{7,11},{8,12},{9,5},{1... | collective-permute-start | bytes 196616 | tf_op jit(solution)/shard_map/ppermute | solution.py:507
  76.9 6.1 %collective-permute-start.22 = (bf16[256,128]{1,0:T(8,128)(2,1)S(1)}, bf16[256,128]{1,0:T(8,128)(2,1)S(1)}, u32[]{:S(2)}, u32[]{:S(2)}) collective-permute-start(bf16[256,128]{1,0:T(8,128)(2,1)S(1)} %get-tuple-element.87), channel_id=1, source_target_pairs={{0,10},{1,3},{2,8},{3,1},{4,14},{5,7},{6,12},{7,5},{8,2},{9,11},{1... | collective-permute-start | bytes 196616 | tf_op jit(solution)/shard_map/ppermute | solution.py:507
  77.4 5.6 %collective-permute-start.23 = (bf16[256,128]{1,0:T(8,128)(2,1)S(1)}, bf16[256,128]{1,0:T(8,128)(2,1)S(1)}, u32[]{:S(2)}, u32[]{:S(2)}) collective-permute-start(bf16[256,128]{1,0:T(8,128)(2,1)S(1)} %get-tuple-element.88), channel_id=1, source_target_pairs={{0,0},{1,9},{2,2},{3,11},{4,4},{5,13},{6,6},{7,15},{8,8},{9,1},{10... | collective-permute-start | bytes 196616 | tf_op jit(solution)/shard_map/ppermute | solution.py:507
  83.0 3.1 %collective-permute-start.24 = (bf16[512,128]{1,0:T(8,128)(2,1)S(1)}, bf16[512,128]{1,0:T(8,128)(2,1)S(1)}, u32[]{:S(2)}, u32[]{:S(2)}) collective-permute-start(bf16[512,128]{1,0:T(8,128)(2,1)S(1)} %shard_map.107), channel_id=1, source_target_pairs={{0,1},{1,0},{2,3},{3,2},{4,5},{5,4},{6,7},{7,6},{8,9},{9,8},{10,11... | collective-permute-start | bytes 393224 | tf_op jit(solution)/shard_map/ppermute | solution.py:524

commit v16 on v14

--- a/solution.py
+++ b/solution.py
@@ -374,13 +374,13 @@
 
 
 def mix_rows_kernel(
-    where_ref, near3, far0, far1, near2, near1, near0, other_ref, out0, out1, out2, out3, lefts, rights, mixed
+    where_ref, near1, far0, far1, near3, near2, near0, other_ref, out0, out1, out2, out3, lefts, rights, mixed
 ):
     chip, core = where_ref[1], where_ref[2]
     count, rows, cols = lefts.shape[1:]
     block = count * rows
     place = 0
-    for step, near in ((3, near3), (None, far0), (None, far1), (2, near2), (1, near1), (0, near0)):
+    for step, near in ((1, near1), (None, far0), (None, far1), (3, near3), (2, near2), (0, near0)):
         if step is None:
             op = 0 if near is far0 else 1
             for half in range(2):
@@ -590,10 +590,10 @@
         flops=4 * 10**9,
     )
     stream, gate = made[0], made[1]
-    first = chip_permute(made[8], 3)
-    far, later = lax.optimization_barrier((with_partner(made[2:4], made[4]), list(made[5:8])))
+    first = chip_permute(made[6], 1)
+    far, later = lax.optimization_barrier((with_partner(made[2:4], made[4]), [made[5], made[7], made[8]]))
     far = split_exchange(far, FAR_SPLIT)
-    came = [first] + exchange(later, NEAR_STEPS[1:])
+    came = [first, chip_permute(later[2], 3), chip_permute(later[1], 2), later[0]]
     came = [came[0], far[0], far[1], came[1], came[2], came[3]]
     rights = [block if at in (1, 2) else block[near:] for at, block in enumerate(came)]
     rights = jnp.concatenate(rights, axis=0)

time: 87.1 us -> 89.1 us (1.023)
  waiting for transfers between devices: 33.6 us -> 35.8 us
    ppermute x9, waiting for transfers between devices: 10 us -> 13.4 us  [chip_permute(): lax.ppermute(block, 'wide', [(w, w ^ 2 * step) for w in range(count)])]
    ppermute x10, waiting for transfers between devices: 16.8 us -> 15.3 us  [split_permute(): lax.ppermute(block, 'wide', [(w, w ^ 2 * steps[w % 2]) for w in range(cou...]
    ppermute x6, starting transfers between devices: 5.73 us -> 4.56 us  [core_permute(): return lax.ppermute(block, 'wide', [(w, w ^ 1) for w in range(count)])]
    ppermute x10, starting transfers between devices: 17.5 us -> 18.6 us  [split_permute(): lax.ppermute(block, 'wide', [(w, w ^ 2 * steps[w % 2]) for w in range(cou...]
  transfers between devices with their start and end apart: 25 -> 25, of which waited for: 19 -> 21; matrix products, arithmetic and copies ran while one was open for 0% -> 0% of each run, Pallas kernels for 2% -> 2%
where the time goes in v16:
time: 89.1 us; the launch traced here: 88.9 us
  starting transfers between devices  38.1 us (43%)
  waiting for transfers between devices  35.8 us (40%)
  Pallas kernels  12 us (13%)
  local copies, waits for them, and re-layouts  1.41 us (2%)
  other arithmetic  1.41 us (2%)
    ppermute x10, starting transfers between devices, split_permute(): lax.ppermute(block, 'wide', [(w, w ^ 2 * steps[w % 2]) for w in range(cou...  18.6 us
    ppermute x10, waiting for transfers between devices, split_permute(): lax.ppermute(block, 'wide', [(w, w ^ 2 * steps[w % 2]) for w in range(cou...  15.3 us
    ppermute x9, starting transfers between devices, chip_permute(): lax.ppermute(block, 'wide', [(w, w ^ 2 * step) for w in range(count)])  15 us
    ppermute x9, waiting for transfers between devices, chip_permute(): lax.ppermute(block, 'wide', [(w, w ^ 2 * step) for w in range(count)])  13.4 us
    pallas_call x9, Pallas kernels, run(): pl.pallas_call(kernel, out_shape=[jax.ShapeDtypeStruct(shape, kind) for s...  12 us
    ppermute x6, waiting for transfers between devices, core_permute(): return lax.ppermute(block, 'wide', [(w, w ^ 1) for w in range(count)])  7.14 us
    ppermute x6, starting transfers between devices, core_permute(): return lax.ppermute(block, 'wide', [(w, w ^ 1) for w in range(count)])  4.56 us
  transfers between devices with their start and end apart: 25, of which 21 were waited for; matrix products, arithmetic and copies ran while one was open for 0% of the time, Pallas kernels for 2%

profile of v16, /device:TPU:0, one launch (start us, length us, event | category | flops | bytes accessed | tf_op | source)
XLA Modules:
  0.0 88.9 jit_solution(1569550368877557527)
XLA Ops:
  0.0 0.7 copy-done.7
  0.7 0.1 dynamic-slice_convert_fusion
  0.7 0.1 multiply_bitcast_fusion
  0.8 0.1 pad_maximum_fusion.9.live_in_ref
  0.9 1.0 %convert_element_type.10.feat_ref = f32[64,8,256]{2,1,0:T(8,128)S(1)} convert(bf16[64,8,256]{2,1,0:T(8,128)(2,1)} %param.11) | non-fusion elementwise | flops 131072 | bytes 786432 | tf_op jit(solution)/shard_map/convert_element_type | solution.py:553
  1.9 0.0 copy-start.1
  1.9 0.0 copy-start.2
  1.9 1.0 %shard_map.100 = (bf16[144,128]{1,0:T(8,128)(2,1)S(1)}, bf16[512,128]{1,0:T(8,128)(2,1)S(1)}, f32[8,128]{1,0:T(8,128)S(1)}) custom-call(f32[64,8,256]{2,1,0:T(8,128)S(1)} %convert_element_type.10.feat_ref, bf16[64,256]{1,0:T(8,128)(2,1)S(1)} %bitcast.13, f32[8,128]{1,0:T(8,128)S(1)} %pad_maximum_fusion.9.live_in_ref), custom_call_target="tpu_custom_call" | custom-call | flops 1500000000 | bytes 561152 | tf_op jit(solution)/shard_map/pallas_call | solution.py:216
  2.9 0.0 copy-start
  2.9 4.1 %collective-permute-start = (bf16[144,128]{1,0:T(8,128)(2,1)S(1)}, bf16[144,128]{1,0:T(8,128)(2,1)S(1)}, u32[]{:S(2)}, u32[]{:S(2)}) collective-permute-start(bf16[144,128]{1,0:T(8,128)(2,1)S(1)} %get-tuple-element.48), channel_id=1, source_target_pairs={{0,8},{1,9},{2,10},{3,11},{4,12},{5,13},{6,14},{7,15},{8,0},{9,1},... | collective-permute-start | bytes 110600 | tf_op jit(solution)/shard_map/ppermute | solution.py:498
  7.0 2.3 %collective-permute-done = bf16[144,128]{1,0:T(8,128)(2,1)S(1)} collective-permute-done((bf16[144,128]{1,0:T(8,128)(2,1)S(1)}, bf16[144,128]{1,0:T(8,128)(2,1)S(1)}, u32[]{:S(2)}, u32[]{:S(2)}) %collective-permute-start) | collective-permute-done | bytes 36896 | tf_op jit(solution)/shard_map/ppermute | solution.py:498
  9.3 1.6 %collective-permute-start.1 = (bf16[2,144,128]{2,1,0:T(8,128)(2,1)S(1)}, bf16[2,144,128]{2,1,0:T(8,128)(2,1)S(1)}, u32[]{:S(2)}, u32[]{:S(2)}) collective-permute-start(bf16[2,144,128]{2,1,0:T(8,128)(2,1)S(1)} %pad_maximum_fusion.8), channel_id=1, source_target_pairs={{0,4},{1,5},{2,6},{3,7},{4,0},{5,1},{6,2},{7,3},{8,12},{9,13},{10,... | collective-permute-start | bytes 221192 | tf_op jit(solution)/shard_map/ppermute | solution.py:498
  10.9 2.8 %collective-permute-done.1 = bf16[2,144,128]{2,1,0:T(8,128)(2,1)S(1)} collective-permute-done((bf16[2,144,128]{2,1,0:T(8,128)(2,1)S(1)}, bf16[2,144,128]{2,1,0:T(8,128)(2,1)S(1)}, u32[]{:S(2)}, u32[]{:S(2)}) %collective-permute-start.1) | collective-permute-done | bytes 73760 | tf_op jit(solution)/shard_map/ppermute | solution.py:498
  13.8 1.8 %collective-permute-start.2 = (bf16[4,144,128]{2,1,0:T(8,128)(2,1)S(1)}, bf16[4,144,128]{2,1,0:T(8,128)(2,1)S(1)}, u32[]{:S(2)}, u32[]{:S(2)}) collective-permute-start(bf16[4,144,128]{2,1,0:T(8,128)(2,1)S(1)} %pad_maximum_fusion.1), channel_id=1, source_target_pairs={{0,2},{1,3},{2,0},{3,1},{4,6},{5,7},{6,4},{7,5},{8,10},{9,11},{10,... | collective-permute-start | bytes 442376 | tf_op jit(solution)/shard_map/ppermute | solution.py:498
  15.5 0.1 pad_add_fusion.where_ref
  15.7 0.6 copy-done.6
  16.3 1.7 %shard_map.101 = (f32[8,128,128]{2,1,0:T(8,128)S(1)}, bf16[128,1024]{1,0:T(8,128)(2,1)S(1)}, bf16[2,640,128]{2,1,0:T(8,128)(2,1)S(1)}, bf16[2,128,128]{2,1,0:T(8,128)(2,1)S(1)}) custom-call(s32[3]{0:T(128)S(1)} %pad_add_fusion.where_ref, s32[128]{0:T(128)S(1)} %copy-done.6, s32[1,128]{1,0:T(1,128)S(1)} %bitcast.14, bf16[8,128,128]{2,1,0:T(8,128)(2,1)S(1)} %copy-done.1, ...), custom_call_target="tpu_custom_call" | custom-call | flops 1500000000 | bytes 935436 | tf_op jit(solution)/shard_map/pallas_call | solution.py:216
  18.0 1.0 %collective-permute-done.2 = bf16[4,144,128]{2,1,0:T(8,128)(2,1)S(1)} collective-permute-done((bf16[4,144,128]{2,1,0:T(8,128)(2,1)S(1)}, bf16[4,144,128]{2,1,0:T(8,128)(2,1)S(1)}, u32[]{:S(2)}, u32[]{:S(2)}) %collective-permute-start.2) | collective-permute-done | bytes 147488 | tf_op jit(solution)/shard_map/ppermute | solution.py:498
  19.0 0.1 collective-permute-start.3
  19.1 1.6 %collective-permute-done.3.other_ref = bf16[8,144,128]{2,1,0:T(8,128)(2,1)S(1)} collective-permute-done((bf16[8,144,128]{2,1,0:T(8,128)(2,1)S(1)}, bf16[8,144,128]{2,1,0:T(8,128)(2,1)S(1)}, u32[]{:S(2)}, u32[]{:S(2)}) %collective-permute-start.3) | collective-permute-done | bytes 294944 | tf_op jit(solution)/shard_map/ppermute | solution.py:524
  20.7 2.7 %shard_map.102 = (f32[8,128,128]{2,1,0:T(8,128)S(1)}, f32[8,128,128]{2,1,0:T(8,128)S(1)}, bf16[256,128]{1,0:T(8,128)(2,1)S(1)}, bf16[256,128]{1,0:T(8,128)(2,1)S...) custom-call(s32[3]{0:T(128)S(1)} %pad_add_fusion.where_ref, ...), custom_call_target="tpu_custom_call" | custom-call | flops 4000000000 | bytes 1840140 | tf_op jit(solution)/shard_map/pallas_call | solution.py:216
  23.4 0.2 collective-permute-start.5
  23.6 1.7 %collective-permute-start.4 = (bf16[512,128]{1,0:T(8,128)(2,1)S(1)}, bf16[512,128]{1,0:T(8,128)(2,1)S(1)}, u32[]{:S(2)}, u32[]{:S(2)}) collective-permute-start(bf16[512,128]{1,0:T(8,128)(2,1)S(1)} %get-tuple-element.59), channel_id=1, source_target_pairs={{0,2},{1,3},{2,0},{3,1},{4,6},{5,7},{6,4},{7,5},{8,10},{9,11},{10,... | collective-permute-start | bytes 393224 | tf_op jit(solution)/shard_map/ppermute | solution.py:498
  25.3 0.0 collective-permute-done.5
  25.4 4.3 %collective-permute-start.6 = (bf16[512,128]{1,0:T(8,128)(2,1)S(1)}, bf16[512,128]{1,0:T(8,128)(2,1)S(1)}, u32[]{:S(2)}, u32[]{:S(2)}) collective-permute-start(bf16[512,128]{1,0:T(8,128)(2,1)S(1)} %get-tuple-element.66), channel_id=1, source_target_pairs={{0,14},{1,11},{2,12},{3,9},{4,10},{5,15},{6,8},{7,13},{8,6},{9,3},... | collective-permute-start | bytes 393224 | tf_op jit(solution)/shard_map/ppermute | solution.py:507
  29.7 0.2 collective-permute-start.7
  29.9 2.3 %collective-permute-start.9 = (bf16[512,128]{1,0:T(8,128)(2,1)S(1)}, bf16[512,128]{1,0:T(8,128)(2,1)S(1)}, u32[]{:S(2)}, u32[]{:S(2)}) collective-permute-start(bf16[512,128]{1,0:T(8,128)(2,1)S(1)} %get-tuple-element.69), channel_id=1, source_target_pairs={{0,4},{1,5},{2,6},{3,7},{4,0},{5,1},{6,2},{7,3},{8,12},{9,13},{10,... | collective-permute-start | bytes 393224 | tf_op jit(solution)/shard_map/ppermute | solution.py:498
  32.2 1.6 %collective-permute-done.6.far0 = bf16[512,128]{1,0:T(8,128)(2,1)S(1)} collective-permute-done((bf16[512,128]{1,0:T(8,128)(2,1)S(1)}, bf16[512,128]{1,0:T(8,128)(2,1)S(1)}, u32[]{:S(2)}, u32[]{:S(2)}) %collective-permute-start.6) | collective-permute-done | bytes 131104 | tf_op jit(solution)/shard_map/ppermute | solution.py:507
  33.9 4.1 %collective-permute-done.7.far1 = bf16[512,128]{1,0:T(8,128)(2,1)S(1)} collective-permute-done((bf16[512,128]{1,0:T(8,128)(2,1)S(1)}, bf16[512,128]{1,0:T(8,128)(2,1)S(1)}, u32[]{:S(2)}, u32[]{:S(2)}) %collective-permute-start.7) | collective-permute-done | bytes 131104 | tf_op jit(solution)/shard_map/ppermute | solution.py:507
  37.9 2.7 %collective-permute-done.8.near3 = bf16[512,128]{1,0:T(8,128)(2,1)S(1)} collective-permute-done((bf16[512,128]{1,0:T(8,128)(2,1)S(1)}, bf16[512,128]{1,0:T(8,128)(2,1)S(1)}, u32[]{:S(2)}, u32[]{:S(2)}) %collective-permute-start.8) | collective-permute-done | bytes 131104 | tf_op jit(solution)/shard_map/ppermute | solution.py:498
  40.7 1.2 %collective-permute-done.9.near2 = bf16[512,128]{1,0:T(8,128)(2,1)S(1)} collective-permute-done((bf16[512,128]{1,0:T(8,128)(2,1)S(1)}, bf16[512,128]{1,0:T(8,128)(2,1)S(1)}, u32[]{:S(2)}, u32[]{:S(2)}) %collective-permute-start.9) | collective-permute-done | bytes 131104 | tf_op jit(solution)/shard_map/ppermute | solution.py:498
  41.9 0.1 collective-permute-start.10
  42.0 1.9 %collective-permute-done.10.other_ref = bf16[2048,128]{1,0:T(8,128)(2,1)S(1)} collective-permute-done((bf16[2048,128]{1,0:T(8,128)(2,1)S(1)}, bf16[2048,128]{1,0:T(8,128)(2,1)S(1)}, u32[]{:S(2)}, u32[]{:S(2)}) %collective-permute-start.10) | collective-permute-done | bytes 524320 | tf_op jit(solution)/shard_map/ppermute | solution.py:524
  43.9 1.4 %shard_map.103 = (bf16[256,128]{1,0:T(8,128)(2,1)S(1)}, bf16[256,128]{1,0:T(8,128)(2,1)S(1)}, bf16[256,128]{1,0:T(8,128)(2,1)S(1)}, bf16[256,128]{1,0:T(8,128)(2,1)S(1)}) custom-call(s32[3]{0:T(128)S(1)} %pad_add_fusion.where_ref, bf16[512,128]{1,0:T(8,128)(2,1)S(1)} %collective-permute-done.4.near1, bf16[512,128]{1,0:T(8,128)(2,1)S(1)} %collective-permute-done.6.far0, ...), custom_call_target="tpu_custom_call" | custom-call | flops 1500000000 | bytes 1310732 | tf_op jit(solution)/shard_map/pallas_call | solution.py:216
  45.4 0.8 collective-permute-start.11
  46.2 1.8 %collective-permute-start.12 = (bf16[256,128]{1,0:T(8,128)(2,1)S(1)}, bf16[256,128]{1,0:T(8,128)(2,1)S(1)}, u32[]{:S(2)}, u32[]{:S(2)}) collective-permute-start(bf16[256,128]{1,0:T(8,128)(2,1)S(1)} %get-tuple-element.72), channel_id=1, source_target_pairs={{0,4},{1,5},{2,6},{3,7},{4,0},{5,1},{6,2},{7,3},{8,12},{9,13},{10,... | collective-permute-start | bytes 196616 | tf_op jit(solution)/shard_map/ppermute | solution.py:498
  47.9 1.0 %collective-permute-start.13 = (bf16[256,128]{1,0:T(8,128)(2,1)S(1)}, bf16[256,128]{1,0:T(8,128)(2,1)S(1)}, u32[]{:S(2)}, u32[]{:S(2)}) collective-permute-start(bf16[256,128]{1,0:T(8,128)(2,1)S(1)} %get-tuple-element.73), channel_id=1, source_target_pairs={{0,2},{1,3},{2,0},{3,1},{4,6},{5,7},{6,4},{7,5},{8,10},{9,11},{10,... | collective-permute-start | bytes 196616 | tf_op jit(solution)/shard_map/ppermute | solution.py:498
  48.9 2.4 %collective-permute-done.11.in0 = bf16[256,128]{1,0:T(8,128)(2,1)S(1)} collective-permute-done((bf16[256,128]{1,0:T(8,128)(2,1)S(1)}, bf16[256,128]{1,0:T(8,128)(2,1)S(1)}, u32[]{:S(2)}, u32[]{:S(2)}) %collective-permute-start.11) | collective-permute-done | bytes 65568 | tf_op jit(solution)/shard_map/ppermute | solution.py:498
  51.3 0.2 collective-permute-done.12.in1
  51.4 0.8 collective-permute-done.13.in2
  52.2 1.7 %shard_map.104 = (f32[8,128,128]{2,1,0:T(8,128)S(1)}, f32[8,128,128]{2,1,0:T(8,128)S(1)}, bf16[256,128]{1,0:T(8,128)(2,1)S(1)}, bf16[256,128]{1,0:T(8,128)(2,1)S...) custom-call(s32[3]{0:T(128)S(1)} %pad_add_fusion.where_ref, ...), custom_call_target="tpu_custom_call" | custom-call | flops 1500000000 | bytes 1704972 | tf_op jit(solution)/shard_map/pallas_call | solution.py:216
  53.9 0.1 collective-permute-start.14
  53.9 1.5 %collective-permute-done.14 = bf16[1024,128]{1,0:T(8,128)(2,1)S(1)} collective-permute-done((bf16[1024,128]{1,0:T(8,128)(2,1)S(1)}, bf16[1024,128]{1,0:T(8,128)(2,1)S(1)}, u32[]{:S(2)}, u32[]{:S(2)}) %collective-permute-start.14) | collective-permute-done | bytes 262176 | tf_op jit(solution)/shard_map/ppermute | solution.py:524
  55.5 4.8 %collective-permute-start.15 = (bf16[512,128]{1,0:T(8,128)(2,1)S(1)}, bf16[512,128]{1,0:T(8,128)(2,1)S(1)}, u32[]{:S(2)}, u32[]{:S(2)}) collective-permute-start(bf16[512,128]{1,0:T(8,128)(2,1)S(1)} %pad_maximum_fusion.4), channel_id=1, source_target_pairs={{0,14},{1,11},{2,12},{3,9},{4,10},{5,15},{6,8},{7,13},{8,6},{9,3},... | collective-permute-start | bytes 393224 | tf_op jit(solution)/shard_map/ppermute | solution.py:507
  60.3 0.1 collective-permute-start.16
  60.4 0.1 collective-permute-start.17
  60.5 3.0 %collective-permute-start.18 = (bf16[512,128]{1,0:T(8,128)(2,1)S(1)}, bf16[512,128]{1,0:T(8,128)(2,1)S(1)}, u32[]{:S(2)}, u32[]{:S(2)}) collective-permute-start(bf16[512,128]{1,0:T(8,128)(2,1)S(1)} %pad_maximum_fusion.7), channel_id=1, source_target_pairs={{0,2},{1,1},{2,0},{3,3},{4,6},{5,5},{6,4},{7,7},{8,10},{9,9},{10,8... | collective-permute-start | bytes 393224 | tf_op jit(solution)/shard_map/ppermute | solution.py:507
  63.6 0.7 collective-permute-done.15.came0
  64.3 3.8 %collective-permute-done.16.came1 = bf16[512,128]{1,0:T(8,128)(2,1)S(1)} collective-permute-done((bf16[512,128]{1,0:T(8,128)(2,1)S(1)}, bf16[512,128]{1,0:T(8,128)(2,1)S(1)}, u32[]{:S(2)}, u32[]{:S(2)}) %collective-permute-start.16) | collective-permute-done | bytes 131104 | tf_op jit(solution)/shard_map/ppermute | solution.py:507
  68.2 0.2 collective-permute-done.18.came3
  68.3 1.2 %shard_map.105 = (f32[4,256,128]{2,1,0:T(8,128)S(1)}, bf16[4,256,128]{2,1,0:T(8,128)(2,1)S(1)}) custom-call(s32[3]{0:T(128)S(1)} %pad_add_fusion.where_ref, bf16[512,128]{1,0:T(8,128)(2,1)S(1)} %collective-permute-done.15.came0, bf16[512,128]{1,0:T(8,128)(2,1)S(1)} %collective-permute-done.16.came1, bf16[512,128]{1,0:T(8,128)(2,1)S(1)} %collective-permute-done.17.came2, ...), custom_call_target="tpu_custom_call" | custom-call | flops 1500000000 | bytes 524300 | tf_op jit(solution)/shard_map/pallas_call | solution.py:216
  69.5 2.0 %collective-permute-start.19 = (bf16[4,256,128]{2,1,0:T(8,128)(2,1)S(1)}, bf16[4,256,128]{2,1,0:T(8,128)(2,1)S(1)}, u32[]{:S(2)}, u32[]{:S(2)}) collective-permute-start(bf16[4,256,128]{2,1,0:T(8,128)(2,1)S(1)} %get-tuple-element.84), channel_id=1, source_target_pairs={{0,1},{1,0},{2,3},{3,2},{4,5},{5,4},{6,7},{7,6},{8,9},{9,8},{10,11... | collective-permute-start | bytes 786440 | tf_op jit(solution)/shard_map/ppermute | solution.py:524
  71.5 1.2 %collective-permute-done.19.got_ref = bf16[4,256,128]{2,1,0:T(8,128)(2,1)S(1)} collective-permute-done((bf16[4,256,128]{2,1,0:T(8,128)(2,1)S(1)}, bf16[4,256,128]{2,1,0:T(8,128)(2,1)S(1)}, u32[]{:S(2)}, u32[]{:S(2)}) %collective-permute-start.19) | collective-permute-done | bytes 262176 | tf_op jit(solution)/shard_map/ppermute | solution.py:524
  72.7 0.1 shard_map.106
  72.8 4.7 %collective-permute-start.20 = (bf16[256,128]{1,0:T(8,128)(2,1)S(1)}, bf16[256,128]{1,0:T(8,128)(2,1)S(1)}, u32[]{:S(2)}, u32[]{:S(2)}) collective-permute-start(bf16[256,128]{1,0:T(8,128)(2,1)S(1)} %get-tuple-element.85), channel_id=1, source_target_pairs={{0,14},{1,7},{2,12},{3,5},{4,10},{5,3},{6,8},{7,1},{8,6},{9,15},{1... | collective-permute-start | bytes 196616 | tf_op jit(solution)/shard_map/ppermute | solution.py:507
  77.5 0.0 collective-permute-start.21
  77.6 0.6 collective-permute-start.22
  78.1 0.7 collective-permute-start.23
  78.8 1.4 %collective-permute-done.20.refs_0_.came0 = bf16[256,128]{1,0:T(8,128)(2,1)S(1)} collective-permute-done((bf16[256,128]{1,0:T(8,128)(2,1)S(1)}, bf16[256,128]{1,0:T(8,128)(2,1)S(1)}, u32[]{:S(2)}, u32[]{:S(2)}) %collective-permute-start.20) | collective-permute-done | bytes 65568 | tf_op jit(solution)/shard_map/ppermute | solution.py:507
  80.2 2.0 %collective-permute-done.21.refs_1_.came1 = bf16[256,128]{1,0:T(8,128)(2,1)S(1)} collective-permute-done((bf16[256,128]{1,0:T(8,128)(2,1)S(1)}, bf16[256,128]{1,0:T(8,128)(2,1)S(1)}, u32[]{:S(2)}, u32[]{:S(2)}) %collective-permute-start.21) | collective-permute-done | bytes 65568 | tf_op jit(solution)/shard_map/ppermute | solution.py:507
  82.2 1.4 %collective-permute-done.22.refs_2_.came2 = bf16[256,128]{1,0:T(8,128)(2,1)S(1)} collective-permute-done((bf16[256,128]{1,0:T(8,128)(2,1)S(1)}, bf16[256,128]{1,0:T(8,128)(2,1)S(1)}, u32[]{:S(2)}, u32[]{:S(2)}) %collective-permute-start.22) | collective-permute-done | bytes 65568 | tf_op jit(solution)/shard_map/ppermute | solution.py:507
  83.6 2.1 %collective-permute-start.24 = (bf16[512,128]{1,0:T(8,128)(2,1)S(1)}, bf16[512,128]{1,0:T(8,128)(2,1)S(1)}, u32[]{:S(2)}, u32[]{:S(2)}) collective-permute-start(bf16[512,128]{1,0:T(8,128)(2,1)S(1)} %shard_map.107), channel_id=1, source_target_pairs={{0,1},{1,0},{2,3},{3,2},{4,5},{5,4},{6,7},{7,6},{8,9},{9,8},{10,11... | collective-permute-start | bytes 393224 | tf_op jit(solution)/shard_map/ppermute | solution.py:524
  85.8 1.0 %collective-permute-done.24.other_ref = bf16[512,128]{1,0:T(8,128)(2,1)S(1)} collective-permute-done((bf16[512,128]{1,0:T(8,128)(2,1)S(1)}, bf16[512,128]{1,0:T(8,128)(2,1)S(1)}, u32[]{:S(2)}, u32[]{:S(2)}) %collective-permute-start.24) | collective-permute-done | bytes 131104 | tf_op jit(solution)/shard_map/ppermute | solution.py:524
  86.7 2.2 %shard_map.108 = bf16[8,128,128]{2,1,0:T(8,128)(2,1)} custom-call(s32[3]{0:T(128)S(1)} %pad_add_fusion.where_ref, bf16[256,128]{1,0:T(8,128)(2,1)S(1)} %collective-permute-done.20.refs_0_.came0, bf16[256,128]{1,0:T(8,128)(2,1)S(1)} %collective-permute-done.21.refs_1_.came1, bf16[256,128]{1,0:T(8,128)(2,1)S(1)} %collective-permute-done.22.refs_2_.came2, ...), custom_call_target="tpu_custom_call" | custom-call | flops 1500000000 | bytes 1507340 | tf_op jit(solution)/shard_map/pallas_call | solution.py:216
  (34 shorter events, 0.3 us)
Async XLA Ops:
  0.0 0.7 copy-start.7
  0.0 0.7 copy-start.8
  0.9 1.0 %copy-start.4 = (bf16[256,64]{0,1:T(8,128)(2,1)S(1)}, bf16[256,64]{0,1:T(8,128)(2,1)}, u32[]{:S(2)}) copy-start(bf16[256,64]{0,1:T(8,128)(2,1)} %param.16) | copy-start | bytes 98308
  1.9 13.7 %copy-start.1 = (bf16[8,128,128]{2,1,0:T(8,128)(2,1)S(1)}, bf16[8,128,128]{2,1,0:T(8,128)(2,1)}, u32[]{:S(2)}) copy-start(bf16[8,128,128]{2,1,0:T(8,128)(2,1)} %pair_ref.1) | copy-start | bytes 786436
  1.9 13.7 %copy-start.2 = (bf16[1024,128]{1,0:T(8,128)(2,1)S(1)}, bf16[1024,128]{1,0:T(8,128)(2,1)}, u32[]{:S(2)}) copy-start(bf16[1024,128]{1,0:T(8,128)(2,1)} %outer_ref.1) | copy-start | bytes 786436
  2.9 12.8 %copy-start = (bf16[2,128,640]{2,1,0:T(8,128)(2,1)S(1)}, bf16[2,128,640]{2,1,0:T(8,128)(2,1)}, u32[]{:S(2)}) copy-start(bf16[2,128,640]{2,1,0:T(8,128)(2,1)} %proj_ref.1) | copy-start | bytes 983044
  2.9 6.4 %collective-permute-start = (bf16[144,128]{1,0:T(8,128)(2,1)S(1)}, bf16[144,128]{1,0:T(8,128)(2,1)S(1)}, u32[]{:S(2)}, u32[]{:S(2)}) collective-permute-start(bf16[144,128]{1,0:T(8,128)(2,1)S(1)} %get-tuple-element.48), channel_id=1, source_target_pairs={{0,8},{1,9},{2,10},{3,11},{4,12},{5,13},{6,14},{7,15},{8,0},{9,1},... | collective-permute-start | bytes 110600 | tf_op jit(solution)/shard_map/ppermute | solution.py:498
  9.3 4.4 %collective-permute-start.1 = (bf16[2,144,128]{2,1,0:T(8,128)(2,1)S(1)}, bf16[2,144,128]{2,1,0:T(8,128)(2,1)S(1)}, u32[]{:S(2)}, u32[]{:S(2)}) collective-permute-start(bf16[2,144,128]{2,1,0:T(8,128)(2,1)S(1)} %pad_maximum_fusion.8), channel_id=1, source_target_pairs={{0,4},{1,5},{2,6},{3,7},{4,0},{5,1},{6,2},{7,3},{8,12},{9,13},{10,... | collective-permute-start | bytes 221192 | tf_op jit(solution)/shard_map/ppermute | solution.py:498
  10.9 4.7 %copy-start.3 = (bf16[2,128,128]{2,1,0:T(8,128)(2,1)S(1)}, bf16[2,128,128]{2,1,0:T(8,128)(2,1)}, u32[]{:S(2)}) copy-start(bf16[2,128,128]{2,1,0:T(8,128)(2,1)} %out_ref.1) | copy-start | bytes 196612
  10.9 4.7 %copy-start.5 = (bf16[66,128]{1,0:T(8,128)(2,1)S(1)}, bf16[66,128]{1,0:T(8,128)(2,1)}, u32[]{:S(2)}) copy-start(bf16[66,128]{1,0:T(8,128)(2,1)} %table_ref.1) | copy-start | bytes 50692
  13.8 5.2 %collective-permute-start.2 = (bf16[4,144,128]{2,1,0:T(8,128)(2,1)S(1)}, bf16[4,144,128]{2,1,0:T(8,128)(2,1)S(1)}, u32[]{:S(2)}, u32[]{:S(2)}) collective-permute-start(bf16[4,144,128]{2,1,0:T(8,128)(2,1)S(1)} %pad_maximum_fusion.1), channel_id=1, source_target_pairs={{0,2},{1,3},{2,0},{3,1},{4,6},{5,7},{6,4},{7,5},{8,10},{9,11},{10,... | collective-permute-start | bytes 442376 | tf_op jit(solution)/shard_map/ppermute | solution.py:498
  15.6 0.7 copy-start.6
  19.0 1.6 %collective-permute-start.3 = (bf16[8,144,128]{2,1,0:T(8,128)(2,1)S(1)}, bf16[8,144,128]{2,1,0:T(8,128)(2,1)S(1)}, u32[]{:S(2)}, u32[]{:S(2)}) collective-permute-start(bf16[8,144,128]{2,1,0:T(8,128)(2,1)S(1)} %pad_maximum_fusion.own_ref), channel_id=1, source_target_pairs={{0,1},{1,0},{2,3},{3,2},{4,5},{5,4},{6,7},{7,6},{8,9},{9,8},{10,11... | collective-permute-start | bytes 884744 | tf_op jit(solution)/shard_map/ppermute | solution.py:524
  23.4 1.9 %collective-permute-start.5 = (bf16[512,128]{1,0:T(8,128)(2,1)S(1)}, bf16[512,128]{1,0:T(8,128)(2,1)S(1)}, u32[]{:S(2)}, u32[]{:S(2)}) collective-permute-start(bf16[512,128]{1,0:T(8,128)(2,1)S(1)} %get-tuple-element.61), channel_id=1, source_target_pairs={{0,1},{1,0},{2,3},{3,2},{4,5},{5,4},{6,7},{7,6},{8,9},{9,8},{10,11... | collective-permute-start | bytes 393224 | tf_op jit(solution)/shard_map/ppermute | solution.py:524
  23.6 8.6 %collective-permute-start.4 = (bf16[512,128]{1,0:T(8,128)(2,1)S(1)}, bf16[512,128]{1,0:T(8,128)(2,1)S(1)}, u32[]{:S(2)}, u32[]{:S(2)}) collective-permute-start(bf16[512,128]{1,0:T(8,128)(2,1)S(1)} %get-tuple-element.59), channel_id=1, source_target_pairs={{0,2},{1,3},{2,0},{3,1},{4,6},{5,7},{6,4},{7,5},{8,10},{9,11},{10,... | collective-permute-start | bytes 393224 | tf_op jit(solution)/shard_map/ppermute | solution.py:498
  25.4 8.5 %collective-permute-start.6 = (bf16[512,128]{1,0:T(8,128)(2,1)S(1)}, bf16[512,128]{1,0:T(8,128)(2,1)S(1)}, u32[]{:S(2)}, u32[]{:S(2)}) collective-permute-start(bf16[512,128]{1,0:T(8,128)(2,1)S(1)} %get-tuple-element.66), channel_id=1, source_target_pairs={{0,14},{1,11},{2,12},{3,9},{4,10},{5,15},{6,8},{7,13},{8,6},{9,3},... | collective-permute-start | bytes 393224 | tf_op jit(solution)/shard_map/ppermute | solution.py:507
  29.7 8.2 %collective-permute-start.7 = (bf16[512,128]{1,0:T(8,128)(2,1)S(1)}, bf16[512,128]{1,0:T(8,128)(2,1)S(1)}, u32[]{:S(2)}, u32[]{:S(2)}) collective-permute-start(bf16[512,128]{1,0:T(8,128)(2,1)S(1)} %get-tuple-element.67), channel_id=1, source_target_pairs={{0,12},{1,9},{2,14},{3,11},{4,8},{5,13},{6,10},{7,15},{8,4},{9,1},... | collective-permute-start | bytes 393224 | tf_op jit(solution)/shard_map/ppermute | solution.py:507
  29.9 10.8 %collective-permute-start.8 = (bf16[512,128]{1,0:T(8,128)(2,1)S(1)}, bf16[512,128]{1,0:T(8,128)(2,1)S(1)}, u32[]{:S(2)}, u32[]{:S(2)}) collective-permute-start(bf16[512,128]{1,0:T(8,128)(2,1)S(1)} %get-tuple-element.68), channel_id=1, source_target_pairs={{0,6},{1,7},{2,4},{3,5},{4,2},{5,3},{6,0},{7,1},{8,14},{9,15},{10,... | collective-permute-start | bytes 393224 | tf_op jit(solution)/shard_map/ppermute | solution.py:498
  29.9 12.0 %collective-permute-start.9 = (bf16[512,128]{1,0:T(8,128)(2,1)S(1)}, bf16[512,128]{1,0:T(8,128)(2,1)S(1)}, u32[]{:S(2)}, u32[]{:S(2)}) collective-permute-start(bf16[512,128]{1,0:T(8,128)(2,1)S(1)} %get-tuple-element.69), channel_id=1, source_target_pairs={{0,4},{1,5},{2,6},{3,7},{4,0},{5,1},{6,2},{7,3},{8,12},{9,13},{10,... | collective-permute-start | bytes 393224 | tf_op jit(solution)/shard_map/ppermute | solution.py:498
  41.9 2.0 %collective-permute-start.10 = (bf16[2048,128]{1,0:T(8,128)(2,1)S(1)}, bf16[2048,128]{1,0:T(8,128)(2,1)S(1)}, u32[]{:S(2)}, u32[]{:S(2)}) collective-permute-start(bf16[2048,128]{1,0:T(8,128)(2,1)S(1)} %slice_dynamic-update-slice_fusion.3), channel_id=1, source_target_pairs={{0,1},{1,0},{2,3},{3,2},{4,5},{5,4},{6,7},{7,6},{8,9},{9,8},{10,11... | collective-permute-start | bytes 1572872 | tf_op jit(solution)/shard_map/ppermute | solution.py:524
  45.4 5.9 %collective-permute-start.11 = (bf16[256,128]{1,0:T(8,128)(2,1)S(1)}, bf16[256,128]{1,0:T(8,128)(2,1)S(1)}, u32[]{:S(2)}, u32[]{:S(2)}) collective-permute-start(bf16[256,128]{1,0:T(8,128)(2,1)S(1)} %get-tuple-element.71), channel_id=1, source_target_pairs={{0,6},{1,7},{2,4},{3,5},{4,2},{5,3},{6,0},{7,1},{8,14},{9,15},{10,... | collective-permute-start | bytes 196616 | tf_op jit(solution)/shard_map/ppermute | solution.py:498
  46.2 5.3 %collective-permute-start.12 = (bf16[256,128]{1,0:T(8,128)(2,1)S(1)}, bf16[256,128]{1,0:T(8,128)(2,1)S(1)}, u32[]{:S(2)}, u32[]{:S(2)}) collective-permute-start(bf16[256,128]{1,0:T(8,128)(2,1)S(1)} %get-tuple-element.72), channel_id=1, source_target_pairs={{0,4},{1,5},{2,6},{3,7},{4,0},{5,1},{6,2},{7,3},{8,12},{9,13},{10,... | collective-permute-start | bytes 196616 | tf_op jit(solution)/shard_map/ppermute | solution.py:498
  47.9 4.3 %collective-permute-start.13 = (bf16[256,128]{1,0:T(8,128)(2,1)S(1)}, bf16[256,128]{1,0:T(8,128)(2,1)S(1)}, u32[]{:S(2)}, u32[]{:S(2)}) collective-permute-start(bf16[256,128]{1,0:T(8,128)(2,1)S(1)} %get-tuple-element.73), channel_id=1, source_target_pairs={{0,2},{1,3},{2,0},{3,1},{4,6},{5,7},{6,4},{7,5},{8,10},{9,11},{10,... | collective-permute-start | bytes 196616 | tf_op jit(solution)/shard_map/ppermute | solution.py:498
  53.9 1.6 %collective-permute-start.14 = (bf16[1024,128]{1,0:T(8,128)(2,1)S(1)}, bf16[1024,128]{1,0:T(8,128)(2,1)S(1)}, u32[]{:S(2)}, u32[]{:S(2)}) collective-permute-start(bf16[1024,128]{1,0:T(8,128)(2,1)S(1)} %get-tuple-element.79), channel_id=1, source_target_pairs={{0,1},{1,0},{2,3},{3,2},{4,5},{5,4},{6,7},{7,6},{8,9},{9,8},{10,11... | collective-permute-start | bytes 786440 | tf_op jit(solution)/shard_map/ppermute | solution.py:524
  55.5 8.8 %collective-permute-start.15 = (bf16[512,128]{1,0:T(8,128)(2,1)S(1)}, bf16[512,128]{1,0:T(8,128)(2,1)S(1)}, u32[]{:S(2)}, u32[]{:S(2)}) collective-permute-start(bf16[512,128]{1,0:T(8,128)(2,1)S(1)} %pad_maximum_fusion.4), channel_id=1, source_target_pairs={{0,14},{1,11},{2,12},{3,9},{4,10},{5,15},{6,8},{7,13},{8,6},{9,3},... | collective-permute-start | bytes 393224 | tf_op jit(solution)/shard_map/ppermute | solution.py:507
  60.3 7.8 %collective-permute-start.16 = (bf16[512,128]{1,0:T(8,128)(2,1)S(1)}, bf16[512,128]{1,0:T(8,128)(2,1)S(1)}, u32[]{:S(2)}, u32[]{:S(2)}) collective-permute-start(bf16[512,128]{1,0:T(8,128)(2,1)S(1)} %pad_maximum_fusion.5), channel_id=1, source_target_pairs={{0,12},{1,9},{2,14},{3,11},{4,8},{5,13},{6,10},{7,15},{8,4},{9,1},... | collective-permute-start | bytes 393224 | tf_op jit(solution)/shard_map/ppermute | solution.py:507
  60.4 7.7 %collective-permute-start.17 = (bf16[512,128]{1,0:T(8,128)(2,1)S(1)}, bf16[512,128]{1,0:T(8,128)(2,1)S(1)}, u32[]{:S(2)}, u32[]{:S(2)}) collective-permute-start(bf16[512,128]{1,0:T(8,128)(2,1)S(1)} %pad_maximum_fusion.6), channel_id=1, source_target_pairs={{0,6},{1,5},{2,4},{3,7},{4,2},{5,1},{6,0},{7,3},{8,14},{9,13},{10,... | collective-permute-start | bytes 393224 | tf_op jit(solution)/shard_map/ppermute | solution.py:507
  60.5 7.8 %collective-permute-start.18 = (bf16[512,128]{1,0:T(8,128)(2,1)S(1)}, bf16[512,128]{1,0:T(8,128)(2,1)S(1)}, u32[]{:S(2)}, u32[]{:S(2)}) collective-permute-start(bf16[512,128]{1,0:T(8,128)(2,1)S(1)} %pad_maximum_fusion.7), channel_id=1, source_target_pairs={{0,2},{1,1},{2,0},{3,3},{4,6},{5,5},{6,4},{7,7},{8,10},{9,9},{10,8... | collective-permute-start | bytes 393224 | tf_op jit(solution)/shard_map/ppermute | solution.py:507
  69.5 3.2 %collective-permute-start.19 = (bf16[4,256,128]{2,1,0:T(8,128)(2,1)S(1)}, bf16[4,256,128]{2,1,0:T(8,128)(2,1)S(1)}, u32[]{:S(2)}, u32[]{:S(2)}) collective-permute-start(bf16[4,256,128]{2,1,0:T(8,128)(2,1)S(1)} %get-tuple-element.84), channel_id=1, source_target_pairs={{0,1},{1,0},{2,3},{3,2},{4,5},{5,4},{6,7},{7,6},{8,9},{9,8},{10,11... | collective-permute-start | bytes 786440 | tf_op jit(solution)/shard_map/ppermute | solution.py:524
  72.8 7.4 %collective-permute-start.20 = (bf16[256,128]{1,0:T(8,128)(2,1)S(1)}, bf16[256,128]{1,0:T(8,128)(2,1)S(1)}, u32[]{:S(2)}, u32[]{:S(2)}) collective-permute-start(bf16[256,128]{1,0:T(8,128)(2,1)S(1)} %get-tuple-element.85), channel_id=1, source_target_pairs={{0,14},{1,7},{2,12},{3,5},{4,10},{5,3},{6,8},{7,1},{8,6},{9,15},{1... | collective-permute-start | bytes 196616 | tf_op jit(solution)/shard_map/ppermute | solution.py:507
  77.5 4.7 %collective-permute-start.21 = (bf16[256,128]{1,0:T(8,128)(2,1)S(1)}, bf16[256,128]{1,0:T(8,128)(2,1)S(1)}, u32[]{:S(2)}, u32[]{:S(2)}) collective-permute-start(bf16[256,128]{1,0:T(8,128)(2,1)S(1)} %get-tuple-element.86), channel_id=1, source_target_pairs={{0,4},{1,13},{2,6},{3,15},{4,0},{5,9},{6,2},{7,11},{8,12},{9,5},{1... | collective-permute-start | bytes 196616 | tf_op jit(solution)/shard_map/ppermute | solution.py:507
  77.6 6.1 %collective-permute-start.22 = (bf16[256,128]{1,0:T(8,128)(2,1)S(1)}, bf16[256,128]{1,0:T(8,128)(2,1)S(1)}, u32[]{:S(2)}, u32[]{:S(2)}) collective-permute-start(bf16[256,128]{1,0:T(8,128)(2,1)S(1)} %get-tuple-element.87), channel_id=1, source_target_pairs={{0,10},{1,3},{2,8},{3,1},{4,14},{5,7},{6,12},{7,5},{8,2},{9,11},{1... | collective-permute-start | bytes 196616 | tf_op jit(solution)/shard_map/ppermute | solution.py:507
  78.1 5.5 %collective-permute-start.23 = (bf16[256,128]{1,0:T(8,128)(2,1)S(1)}, bf16[256,128]{1,0:T(8,128)(2,1)S(1)}, u32[]{:S(2)}, u32[]{:S(2)}) collective-permute-start(bf16[256,128]{1,0:T(8,128)(2,1)S(1)} %get-tuple-element.88), channel_id=1, source_target_pairs={{0,0},{1,9},{2,2},{3,11},{4,4},{5,13},{6,6},{7,15},{8,8},{9,1},{10... | collective-permute-start | bytes 196616 | tf_op jit(solution)/shard_map/ppermute | solution.py:507
  83.6 3.1 %collective-permute-start.24 = (bf16[512,128]{1,0:T(8,128)(2,1)S(1)}, bf16[512,128]{1,0:T(8,128)(2,1)S(1)}, u32[]{:S(2)}, u32[]{:S(2)}) collective-permute-start(bf16[512,128]{1,0:T(8,128)(2,1)S(1)} %shard_map.107), channel_id=1, source_target_pairs={{0,1},{1,0},{2,3},{3,2},{4,5},{5,4},{6,7},{7,6},{8,9},{9,8},{10,11... | collective-permute-start | bytes 393224 | tf_op jit(solution)/shard_map/ppermute | solution.py:524
